TPU v7x, 32 devices: a whole 2x2x4 slice. The times are simulated.
32 devices in a mesh: ctx: 4 (over x, core), ch: 8 (over z, y).
Axes of the slice: x: 2, y: 2, z: 4, core: 2. Of those that a mesh axis runs over, the one named last changes fastest.
Arguments:
- out_grad: bfloat16 [1024, 8192], P('ctx', 'ch'), may hold values from -6 to 6
- out_weight: bfloat16 [8192, 8192], P(None, 'ch'), may hold values from -0.09375 to 0.09375
- query_in: bfloat16 [1024, 8192], P('ctx', 'ch'), may hold values from -6 to 6
- conv_out: bfloat16 [1024, 8192], P('ctx', 'ch'), may hold values from -6 to 6
- residues: float32 [8192, 16], P('ch'), may hold values from -0.3 to 0.3
- decay_rates: float32 [8192, 16], P('ch'), may hold values from 0.96 to 1, as said below
Outputs:
- grad_query: bfloat16 [1024, 8192], P('ctx', 'ch')
- grad_input: bfloat16 [1024, 8192], P('ctx', 'ch')
Inputs may be any that keep to these rules, and one draw needn't show every extreme that they name: `decay_rates`: each pole lies strictly below 1.
All inputs are finite; a program needn't handle non-finite values.
Results may differ from a plain program's by a relative error of at most 0.001.
Values may be sent and summed in bfloat16 or wider, within the bound.
No kernel may reach another device: no remote copies, remote signals or barrier semaphores. Data moves between devices by JAX's collectives and lax.ppermute only.
A program may use at most 256 MiB of HBM per device.

v0:
```python
import math

import jax
import jax.numpy as jnp
from jax import lax
from jax.sharding import PartitionSpec as P


def from_behind(shard, axis, by):
    length = lax.axis_size(axis)
    pairs = [(i, i + by) for i in range(length) if 0 <= i + by < length]
    return lax.ppermute(shard, axis, pairs)


def local(out_grad, out_weight, query_in, conv_out, residues, decay_rates):
    tok_rows = out_grad.shape[0]
    width_local = query_in.shape[1]
    highest = lax.Precision.HIGHEST
    grad_mix = lax.psum_scatter(
        lax.dot_general(
            out_weight, out_grad, (((1,), (1,)), ((), ())), preferred_element_type=jnp.float32
        ),
        "ch",
        scatter_dimension=0,
        tiled=True,
    ).T
    grad_query = (grad_mix * conv_out.astype(jnp.float32)).astype(jnp.bfloat16)
    grad_conv = grad_mix * query_in.astype(jnp.float32)
    block_len = math.gcd(tok_rows, 128)
    block_count = tok_rows // block_len
    log_decay = jnp.log(decay_rates)
    offsets = jnp.arange(block_len, dtype=jnp.float32)
    powers = jnp.exp(offsets[:, None, None] * log_decay[None])
    filter_taps = jnp.sum(residues[None] * powers, axis=2)
    lagged = jnp.arange(block_len)[None, :] - jnp.arange(block_len)[:, None]
    toeplitz = jnp.where(
        (lagged >= 0)[:, :, None], jnp.take(filter_taps, jnp.maximum(lagged, 0), axis=0), 0.0
    )
    blocks = grad_conv.reshape(block_count, block_len, width_local)
    inner_part = jnp.einsum("stc,btc->bsc", toeplitz, blocks, precision=highest)
    block_sums = jnp.einsum("btc,tcn->bcn", blocks, powers, precision=highest)
    decay_block = jnp.exp(block_len * log_decay)

    def carry_back(late_state, block_sum):
        return (decay_block * late_state + block_sum, late_state)

    zero_state = jnp.zeros(decay_rates.shape, jnp.float32)
    first_state, ends_local = lax.scan(carry_back, zero_state, block_sums, reverse=True)
    decay_group = jnp.exp(tok_rows * log_decay)

    def hop_once(hop_index, received):
        return from_behind(decay_group * received + first_state, "ctx", -1)

    incoming = lax.fori_loop(0, lax.axis_size("ctx") - 1, hop_once, zero_state)
    remaining = jnp.exp(
        (block_count - 1 - jnp.arange(block_count, dtype=jnp.float32))[:, None, None]
        * block_len
        * log_decay[None]
    )
    block_ends = ends_local + remaining * incoming[None]
    tail_weights = jnp.exp((block_len - offsets)[:, None, None] * log_decay[None]) * residues[None]
    outer_part = jnp.einsum("scn,bcn->bsc", tail_weights, block_ends, precision=highest)
    grad_input = (inner_part + outer_part).reshape(tok_rows, width_local).astype(jnp.bfloat16)
    return (grad_query, grad_input)


def solution(mesh):
    placed = (
        P("ctx", "ch"),
        P(None, "ch"),
        P("ctx", "ch"),
        P("ctx", "ch"),
        P("ch", None),
        P("ch", None),
    )
    return jax.shard_map(
        local,
        mesh=mesh,
        in_specs=placed,
        out_specs=(P("ctx", "ch"), P("ctx", "ch")),
        check_vma=False,
    )
```

profile of v0, /device:TPU:0, one launch (start us, length us, event | category | flops | bytes accessed | tf_op | source)
XLA Modules:
  0.0 343.5 jit_solution(17947327810432909189)
XLA Ops:
  7.2 0.0 copy-start
  7.2 0.0 reduce-scatter.2.cloned.1.call-start
  7.2 1.0 copy-done
  8.2 13.6 %fusion.30 = f32[8192,256]{1,0:T(8,128)} fusion(bf16[8192,1024]{1,0:T(8,128)(2,1)} %param.11, bf16[256,1024]{1,0:T(8,128)(2,1)S(1)} %copy-done), kind=kOutput, calls=%fused_computation.40 | convolution fusion | flops 4294967296 | bytes 25690112 | tf_op jit(solution)/shard_map/dot_general | solution.py:20
  21.8 0.0 copy-start.12
  21.8 0.0 copy-start.13
  21.8 0.0 copy-start.15
  21.8 0.0 copy-start.14
  21.8 0.0 reduce-scatter.2.cloned.1.call-update
  21.8 1.0 copy-done.12
  22.8 1.0 copy.27
  23.8 0.0 copy-done.13
  23.8 1.0 copy.26
  24.8 0.0 copy-done.15
  24.8 0.7 multiply_exponential_fusion.4
  25.5 0.0 copy-start.6
  25.5 0.2 copy.29
  25.7 0.0 copy-done.14
  25.7 0.0 copy-start.8
  25.7 0.2 copy.28
  25.9 0.2 copy-done.6
  26.1 0.4 copy-done.8
  26.5 0.0 copy-start.10
  26.5 11.9 %multiply_reduce_fusion = f32[128,1024]{0,1:T(8,128)S(1)} fusion(f32[1024,16]{1,0:T(8,128)S(1)} %copy.29, f32[1024,16]{1,0:T(8,128)S(1)} %copy.28), kind=kLoop, calls=%fused_computation.15 | loop fusion | flops 6160384 | bytes 655360 | tf_op jit(solution)/shard_map/reduce_sum | solution.py:34
  38.5 0.2 copy.30
  38.7 71.0 %gather_fusion = f32[16384,1024]{1,0:T(8,128)} fusion(f32[128,1024]{1,0:T(8,128)S(1)} %copy.30, s32[16384]{0:T(1024)S(1)} %bitcast_clamp_fusion), kind=kCustom, calls=%fused_computation | custom fusion | bytes 134283264 | tf_op jit(solution)/shard_map/jit(_take)/gather | solution.py:37
  109.7 0.0 copy-done.10
  109.7 0.0 copy-start.4
  109.7 0.0 copy-start.5
  109.7 70.8 %copy.31 = f32[128,128,1024]{1,0,2:T(8,128)} copy(f32[128,128,1024]{2,1,0:T(8,128)} %bitcast.2) | data formatting | bytes 134217728 | tf_op jit(solution)/shard_map/jit(_take)/gather | solution.py:37
  180.5 0.0 copy-start.1
  180.5 0.0 copy-start.3
  180.6 0.0 copy-start.2
  180.6 0.0 reduce-scatter.2.cloned.1.call-done
  180.6 0.0 copy-done.4
  180.7 0.0 copy-done.5
  180.7 1.4 bitcast_multiply_fusion
  182.1 0.0 copy-start.7
  182.1 1.0 copy.34
  183.1 0.5 reshape.65
  183.6 14.8 %fusion.16 = f32[2,1024,16]{2,0,1:T(2,128)S(1)} fusion(f32[2,128,1024]{1,0,2:T(2,128)S(1)} %reshape.65, f32[1024,16]{1,0:T(8,128)} %copy-done.8), kind=kOutput, calls=%fused_computation.22 | convolution fusion | flops 52428800 | bytes 1245184 | tf_op jit(solution)/shard_map/btc,tcn->bcn/dot_general | solution.py:41
  198.5 0.4 copy.32
  198.9 0.0 copy-done.1
  198.9 0.0 copy-done.3
  198.9 0.1 while.28
  199.1 0.0 copy-done.2
  199.1 15.1 %while.27 = (s32[]{:T(128)}, f32[1024,16]{0,1:T(8,128)S(1)}, f32[1024,16]{0,1:T(8,128)S(1)}, f32[1024,16]{0,1:T(8,128)S(1)}, s32[]{:T(128)}) while((s32[]{:T(128)}, f32[1024,16]{0,1:T(8,128)S(1)}, f32[1024,16]{0,1:T(8,128)S(1)}, f32[1024,16]{0,1:T(8,128)S(1)}, s32[]{:T(128)}) %tuple.74), condition=%wide.region_5.6_spmd, body=%wide.region_4.5_spmd.sunk | while | flops 32770 | bytes 524389 | solution.py:54
  199.1 1.3 collective-permute-start
  200.4 1.8 collective-permute-done
  202.3 1.3 collective-permute-start
  203.6 5.0 %collective-permute-done = f32[1024,16]{0,1:T(8,128)S(1)} collective-permute-done((f32[1024,16]{0,1:T(8,128)S(1)}, f32[1024,16]{0,1:T(8,128)S(1)}, u32[]{:S(2)}, u32[]{:S(2)}) %collective-permute-start) | collective-permute-done | bytes 65568 | tf_op jit(solution)/shard_map/while/body/eval_jaxpr/ppermute | solution.py:12
  208.6 1.3 collective-permute-start
  209.9 4.3 %collective-permute-done = f32[1024,16]{0,1:T(8,128)S(1)} collective-permute-done((f32[1024,16]{0,1:T(8,128)S(1)}, f32[1024,16]{0,1:T(8,128)S(1)}, u32[]{:S(2)}, u32[]{:S(2)}) %collective-permute-start) | collective-permute-done | bytes 65568 | tf_op jit(solution)/shard_map/while/body/eval_jaxpr/ppermute | solution.py:12
  214.2 0.0 copy-done.7
  214.2 0.1 multiply_add_fusion.1
  214.3 0.5 copy.33
  214.9 0.0 copy-start.9
  214.9 0.0 copy-start.11
  214.9 109.3 %fusion = f32[1024,2,128]{2,1,0:T(2,128)S(1)} fusion(f32[2,128,1024]{1,0,2:T(2,128)S(1)} %reshape.65, f32[128,128,1024]{1,0,2:T(8,128)} %copy.31, pred[128,128]{1,0:T(8,128)(4,1)S(1)} %get-tuple-element.193, pred[128,128]{1,0:T(8,128)(4,1)S(1)} %get-tuple-element.194), kind=kOutput, calls=%fused_computation.4 | convolution fusion | flops 436207616 | bytes 69238784 | tf_op jit(solution)/shard_map/stc,btc->bsc/dot_general | solution.py:40
  324.1 0.0 copy-done.9
  324.1 0.0 copy-done.11
  324.1 11.4 %fusion.23 = bf16[2,128,1024]{1,0,2:T(2,128)(2,1)S(1)} fusion(f32[1024,2,128]{2,1,0:T(2,128)S(1)} %fusion, f32[2,1024,16]{2,0,1:T(2,128)S(1)} %copy.33, f32[128]{0:T(128)S(1)} %iota_subtract_fusion.1, f32[1024,16]{1,0:T(8,128)S(1)} %copy-done.9, f32[1024,16]{1,0:T(8,128)S(1)} %copy-done.11), kind=kOutput, calls=%fused_computation.25 | convolution fusion | flops 55050240 | bytes 1835520 | tf_op jit(solution)/shard_map/scn,bcn->bsc/dot_general | solution.py:62
  335.6 1.1 copy.36
  (14 shorter events, 0.2 us)
Async XLA Ops:
  7.2 1.0 copy-start
  7.2 173.5 %reduce-scatter.2.cloned.1.call-start = ((), (), s32[]{:S(2)}) async-start(), calls=%async_computation.1 | async-start | bytes 9437184 | tf_op jit(solution)/shard_map/reduce_scatter | solution.py:19
  21.8 1.0 copy-start.12
  21.8 2.0 copy-start.13
  21.8 3.0 copy-start.15
  21.8 3.9 %copy-start.14 = (f32[1024,16]{0,1:T(8,128)S(1)}, f32[1024,16]{0,1:T(8,128)}, u32[]{:S(2)}) copy-start(f32[1024,16]{0,1:T(8,128)} %param.14) | copy-start | bytes 196612
  25.5 0.6 copy-start.6
  25.7 0.8 copy-start.8
  26.5 83.2 %copy-start.10 = (f32[1024,16]{1,0:T(8,128)}, f32[1024,16]{1,0:T(8,128)S(1)}, u32[]{:S(2)}) copy-start(f32[1024,16]{1,0:T(8,128)S(1)} %copy.28) | copy-start | bytes 196612
  109.7 70.9 %copy-start.4 = (bf16[256,1024]{0,1:T(8,128)(2,1)S(1)}, bf16[256,1024]{0,1:T(8,128)(2,1)}, u32[]{:S(2)}) copy-start(bf16[256,1024]{0,1:T(8,128)(2,1)} %copy.27) | copy-start | bytes 1572868
  109.7 70.9 %copy-start.5 = (bf16[256,1024]{0,1:T(8,128)(2,1)S(1)}, bf16[256,1024]{0,1:T(8,128)(2,1)}, u32[]{:S(2)}) copy-start(bf16[256,1024]{0,1:T(8,128)(2,1)} %copy.26) | copy-start | bytes 1572868
  180.5 18.4 %copy-start.1 = (f32[1024,16]{0,1:T(8,128)S(1)}, f32[1024,16]{0,1:T(8,128)}, u32[]{:S(2)}) copy-start(f32[1024,16]{0,1:T(8,128)} %custom-call) | copy-start | bytes 196612
  180.5 18.4 %copy-start.3 = (f32[1024,16]{0,1:T(8,128)S(1)}, f32[1024,16]{0,1:T(8,128)}, u32[]{:S(2)}) copy-start(f32[1024,16]{0,1:T(8,128)} %get-tuple-element.254) | copy-start | bytes 196612
  180.6 18.5 %copy-start.2 = (f32[1024,16]{0,1:T(8,128)S(1)}, f32[1024,16]{0,1:T(8,128)}, u32[]{:S(2)}) copy-start(f32[1024,16]{0,1:T(8,128)} %get-tuple-element.274) | copy-start | bytes 196612
  182.1 32.2 %copy-start.7 = (f32[1024,16]{0,1:T(8,128)S(1)}, f32[1024,16]{0,1:T(8,128)}, u32[]{:S(2)}) copy-start(f32[1024,16]{0,1:T(8,128)} %copy-done.6) | copy-start | bytes 196612
  199.1 3.1 collective-permute-start
  202.3 6.3 %collective-permute-start = (f32[1024,16]{0,1:T(8,128)S(1)}, f32[1024,16]{0,1:T(8,128)S(1)}, u32[]{:S(2)}, u32[]{:S(2)}) collective-permute-start(f32[1024,16]{0,1:T(8,128)S(1)} %multiply_add_fusion.3), channel_id=1, source_target_pairs={{8,0},{16,8},{24,16},{9,1},{17,9},{25,17},{10,2},{18,10},{26,18},{... | collective-permute-start | bytes 196616 | tf_op jit(solution)/shard_map/while/body/eval_jaxpr/ppermute | solution.py:12
  208.6 5.6 %collective-permute-start = (f32[1024,16]{0,1:T(8,128)S(1)}, f32[1024,16]{0,1:T(8,128)S(1)}, u32[]{:S(2)}, u32[]{:S(2)}) collective-permute-start(f32[1024,16]{0,1:T(8,128)S(1)} %multiply_add_fusion.3), channel_id=1, source_target_pairs={{8,0},{16,8},{24,16},{9,1},{17,9},{25,17},{10,2},{18,10},{26,18},{... | collective-permute-start | bytes 196616 | tf_op jit(solution)/shard_map/while/body/eval_jaxpr/ppermute | solution.py:12
  214.9 109.3 %copy-start.9 = (f32[1024,16]{1,0:T(8,128)S(1)}, f32[1024,16]{1,0:T(8,128)}, u32[]{:S(2)}) copy-start(f32[1024,16]{1,0:T(8,128)} %copy-done.8) | copy-start | bytes 196612
  214.9 109.3 %copy-start.11 = (f32[1024,16]{1,0:T(8,128)S(1)}, f32[1024,16]{1,0:T(8,128)}, u32[]{:S(2)}) copy-start(f32[1024,16]{1,0:T(8,128)} %copy-done.10) | copy-start | bytes 196612
Sparse Core Ops, SparseCore 0:
  21.9 151.6 reduce-scatter.1
where the time goes:
time: 347 us; the launch traced here: 344 us
  local copies, waits for them, and re-layouts  151 us (44%)
  matrix products  149 us (43%)
  other arithmetic  14.3 us (4%)
  between operations  14.3 us (4%)
  waiting for transfers between devices  11.2 us (3%)
  starting transfers between devices  3.91 us (1%)
    gather x2, local copies, waits for them, and re-layouts, local(): jnp.take(filter_taps, jnp.maximum(lagged, 0), axis=0)  142 us
    dot_general x1, matrix products, local(): inner_part = jnp.einsum('stc,btc->bsc', toeplitz, blocks, precision=highest)  109 us
    dot_general x1, matrix products, local(): block_sums = jnp.einsum('btc,tcn->bcn', blocks, powers, precision=highest)  14.8 us
    dot_general x1, matrix products, local(): lax.dot_general(out_weight, out_grad, (((1,), (1,)), ((), ())), preferred...  13.6 us
    reduce_sum x1, other arithmetic, local(): filter_taps = jnp.sum(residues[None] * powers, axis=2)  11.9 us
    dot_general x1, matrix products, local(): jnp.einsum('scn,bcn->bsc', tail_weights, block_ends, precision=highest)  11.4 us
    ppermute x3, waiting for transfers between devices, from_behind(): return lax.ppermute(shard, axis, pairs)  11.1 us
    unnamed x38, local copies, waits for them, and re-layouts  7.36 us
  transfers between devices with their start and end apart: 4, of which 3 were waited for; matrix products, arithmetic and copies ran while one was open for 46% of the time, Pallas kernels for 0%

commit v1 on v0

v1 whole, which is shorter than its diff:
```python
import functools
import math

import jax
import jax.numpy as jnp
from jax import lax
from jax.experimental import pallas as pl
from jax.experimental.pallas import tpu as pltpu
from jax.sharding import PartitionSpec as P

GROUPS = 16
SPAN = 251 * math.log(2.0)
SHIFT = 125 * math.log(2.0)
SUBS = 1
VMEM = 24 * 1024 * 1024


def encode(acc, out_ref):
    rows, _ = acc.shape
    part = rows // GROUPS
    peaks = []
    for i in range(GROUPS):
        block = acc[i * part : (i + 1) * part, :]
        size = jnp.abs(block)
        peak = jnp.maximum(jnp.max(size, axis=0, keepdims=True) * 1.01, 1e-30)
        peak = peak.astype(jnp.bfloat16).astype(jnp.float32)
        code = jnp.exp(size * (SPAN / peak) - SHIFT)
        out_ref[i * part : (i + 1) * part, :] = jnp.where(block < 0, -code, code).astype(jnp.bfloat16)
        peaks.append(peak)
    out_ref[rows:, :] = jnp.concatenate(peaks, axis=0).astype(jnp.bfloat16)


def decode(ref, first, count):
    rows = ref.shape[0] - GROUPS
    part = rows // GROUPS
    peaks = ref[rows:, :].astype(jnp.float32) * (1.0 / SPAN)
    blocks = []
    for i in range(first // part, (first + count) // part):
        code = ref[i * part : (i + 1) * part, :].astype(jnp.float32)
        size = (jnp.log(jnp.abs(code)) + SHIFT) * peaks[i : i + 1, :]
        blocks.append(jnp.where(code < 0, -size, size))
    return jnp.concatenate(blocks, axis=0)


def product(w_ref, g_ref):
    return lax.dot_general(
        w_ref[...], g_ref[...], (((1,), (1,)), ((), ())), preferred_element_type=jnp.float32
    )


def first_kernel(_, w_ref, g_ref, out_ref):
    encode(product(w_ref, g_ref), out_ref)


def relay_kernel(_, w_ref, g_ref, near_ref, out_ref):
    rows = w_ref.shape[0]
    encode(product(w_ref, g_ref) + decode(near_ref, 0, rows), out_ref)


def keep_kernel(_, w_ref, g_ref, near_ref, out_ref):
    rows = w_ref.shape[0]
    out_ref[...] = product(w_ref, g_ref) + decode(near_ref, 0, rows)


def on_block(kernel, block, rows, weight, grad, near, coded):
    toks, depth = grad.shape
    whole = lambda shape: pl.BlockSpec(shape, lambda i, at: (0, 0))
    specs = [pl.BlockSpec((rows, depth), lambda i, at: (at[0], 0)), whole((toks, depth))]
    operands = [pltpu.with_memory_space_constraint(weight, pltpu.HBM), grad]
    if near is not None:
        specs.append(whole(near.shape))
        operands.append(near)
    out = (
        jax.ShapeDtypeStruct((rows + GROUPS, toks), jnp.bfloat16)
        if coded
        else jax.ShapeDtypeStruct((rows, toks), jnp.float32)
    )
    return pl.pallas_call(
        kernel,
        grid_spec=pltpu.PrefetchScalarGridSpec(
            num_scalar_prefetch=1, grid=(1,), in_specs=specs, out_specs=whole(out.shape)
        ),
        out_shape=out,
        compiler_params=pltpu.CompilerParams(vmem_limit_bytes=VMEM),
        cost_estimate=pl.CostEstimate(
            flops=2 * rows * depth * toks, bytes_accessed=2 * rows * (depth + toks), transcendentals=2 * rows * toks
        ),
    )(jnp.reshape(block, (1,)).astype(jnp.int32), *operands)


def steps_back(count, body, state, unroll):
    def some(i, state):
        for j in range(unroll):
            state = body(count - 1 - (i * unroll + j), state)
        return state

    return lax.fori_loop(0, count // unroll, some, state)


def gate_kernel(subs, far_count, *refs):
    accs, refs = refs[:subs], refs[subs:]
    fars, refs = refs[: subs * far_count], refs[subs * far_count :]
    query_ref, conv_ref, decay_ref, gq_ref, gc_ref, state_ref = refs
    toks, width = query_ref.shape
    modes, lines, lanes = decay_ref.shape
    rows = width // subs
    for line in range(lines):
        sub, first = divmod(line * lanes, rows)
        mix = accs[sub][first : first + lanes, :]
        for far in range(far_count):
            mix = mix + decode(fars[far * subs + sub], first, lanes)
        mix = mix.T
        at = slice(line * lanes, (line + 1) * lanes)
        gq_ref[:, at] = (mix * conv_ref[:, at].astype(jnp.float32)).astype(jnp.bfloat16)
        gc_ref[line * toks : (line + 1) * toks, :] = mix * query_ref[:, at].astype(jnp.float32)
    decay = [decay_ref[n] for n in range(modes)]

    def step(t, state):
        row = gc_ref[pl.ds(t, lines, stride=toks), :]
        return tuple(decay[n] * state[n] + row for n in range(modes))

    zero = jnp.zeros((lines, lanes), jnp.float32)
    state = steps_back(toks, step, (zero,) * modes, 8)
    for n in range(modes):
        state_ref[n] = state[n]


def gate(accs, fars, query_in, conv_out, decay):
    toks, width = query_in.shape
    modes, lines, lanes = decay.shape
    return pl.pallas_call(
        functools.partial(gate_kernel, len(accs), len(fars) // len(accs)),
        out_shape=(
            jax.ShapeDtypeStruct((toks, width), jnp.bfloat16),
            jax.ShapeDtypeStruct((lines * toks, lanes), jnp.float32),
            jax.ShapeDtypeStruct(decay.shape, jnp.float32),
        ),
        compiler_params=pltpu.CompilerParams(vmem_limit_bytes=VMEM),
        cost_estimate=pl.CostEstimate(
            flops=2 * modes * toks * width, bytes_accessed=16 * toks * width, transcendentals=3 * toks * width
        ),
    )(*accs, *fars, query_in, conv_out, decay)


def power(base, exponent):
    result = None
    while exponent:
        if exponent % 2:
            result = base if result is None else result * base
        base = base * base
        exponent //= 2
    return result


def scan_kernel(hops, gc_ref, *refs):
    laters, (decay_ref, residue_ref, out_ref, rows_ref) = refs[:hops], refs[hops:]
    toks, width = out_ref.shape
    modes, lines, lanes = decay_ref.shape
    decay = [decay_ref[n] for n in range(modes)]
    state = []
    for n in range(modes):
        group = power(decay[n], toks)
        total = laters[-1][n]
        for later in reversed(laters[:-1]):
            total = total * group + later[n]
        state.append(total)

    def step(t, state):
        at = pl.ds(t, lines, stride=toks)
        row = gc_ref[at, :]
        state = tuple(decay[n] * state[n] + row for n in range(modes))
        terms = [residue_ref[n] * state[n] for n in range(modes)]
        while len(terms) > 1:
            terms = [sum(terms[i : i + 2][1:], terms[i]) for i in range(0, len(terms), 2)]
        rows_ref[at, :] = terms[0]
        return state

    steps_back(toks, step, tuple(state), 8)
    for line in range(lines):
        out_ref[:, line * lanes : (line + 1) * lanes] = rows_ref[
            line * toks : (line + 1) * toks, :
        ].astype(jnp.bfloat16)


def scan(grad_conv, laters, decay, residues, toks):
    modes, lines, lanes = decay.shape
    return pl.pallas_call(
        functools.partial(scan_kernel, len(laters)),
        out_shape=jax.ShapeDtypeStruct((toks, lines * lanes), jnp.bfloat16),
        scratch_shapes=[pltpu.VMEM((lines * toks, lanes), jnp.float32)],
        compiler_params=pltpu.CompilerParams(vmem_limit_bytes=VMEM),
        cost_estimate=pl.CostEstimate(
            flops=4 * modes * toks * lines * lanes, bytes_accessed=6 * toks * lines * lanes, transcendentals=0
        ),
    )(grad_conv, *laters, decay, residues)


def local(out_grad, out_weight, query_in, conv_out, residues, decay_rates):
    toks, width = query_in.shape
    modes = decay_rates.shape[1]
    lanes = math.gcd(width, 128)
    by_mode = lambda values: values.T.reshape(modes, width // lanes, lanes)
    decay, residues = by_mode(decay_rates), by_mode(residues)

    pairs = lax.axis_size("ch") // 2
    place = lax.axis_index("ch")
    high, low = place // 2, place % 2
    rows = width // SUBS
    shifts = [pairs // 2] + [k for k in range(1, pairs) if k != pairs // 2] + [0]
    near_pairs = [(i, i ^ 1) for i in range(2 * pairs)]
    chunks = [(k, sub) for k in shifts for sub in range(SUBS)]

    def block_of(shift, sub, side):
        return (((high + shift) % pairs) * 2 + side) * SUBS + sub

    nears = {}
    for k, sub in chunks:
        coded = on_block(first_kernel, block_of(k, sub, 1 - low), rows, out_weight, out_grad, None, True)
        nears[k, sub] = lax.ppermute(coded, "ch", near_pairs)
    fars, accs = [], []
    for k, sub in chunks:
        block = block_of(k, sub, low)
        if k == 0:
            accs.append(on_block(keep_kernel, block, rows, out_weight, out_grad, nears[k, sub], False))
            continue
        coded = on_block(relay_kernel, block, rows, out_weight, out_grad, nears[k, sub], True)
        far_pairs = [(i, (i + 2 * k) % (2 * pairs)) for i in range(2 * pairs)]
        fars.append(lax.ppermute(coded, "ch", far_pairs))
    grad_query, grad_conv, state = gate(accs, fars, query_in, conv_out, decay)

    groups = lax.axis_size("ctx")
    laters = [
        lax.ppermute(state, "ctx", [(i, i - hop) for i in range(hop, groups)]) for hop in range(1, groups)
    ]
    grad_input = scan(grad_conv, laters, decay, residues, toks)
    return grad_query, grad_input


def solution(mesh):
    placed = (
        P("ctx", "ch"),
        P(None, "ch"),
        P("ctx", "ch"),
        P("ctx", "ch"),
        P("ch", None),
        P("ch", None),
    )
    return jax.shard_map(
        local,
        mesh=mesh,
        in_specs=placed,
        out_specs=(P("ctx", "ch"), P("ctx", "ch")),
        check_vma=False,
    )
```

time: 347 us -> 89.4 us (0.26)
  local copies, waits for them, and re-layouts: 151 us -> 1.08 us
  matrix products: 149 us -> 0 us
  Pallas kernels: 0 us -> 33.2 us
  waiting for transfers between devices: 11.2 us -> 35.4 us
  starting transfers between devices: 3.91 us -> 18.5 us
  other arithmetic: 14.3 us -> 0 us
  between operations: 14.3 us -> 0.77 us
    dot_general x4 -> x0, matrix products: 149 us -> none  [the longest x1 109 us: local(): inner_part = jnp.einsum('stc,btc->bsc', toeplitz, blocks, precision=highest)]
    gather x2 -> x0, local copies, waits for them, and re-layouts: 142 us -> none  [local(): jnp.take(filter_taps, jnp.maximum(lagged, 0), axis=0)]
    pallas_call x0 -> x10, Pallas kernels: none -> 33.2 us  [the longest x8 25.1 us: on_block(): pl.pallas_call(kernel, grid_spec=pltpu.PrefetchScalarGridSpec(num_scalar_...]
    ppermute x3 -> x10, waiting for transfers between devices: 11.1 us -> 35.4 us  [the longest x3 15.7 us: local(): fars.append(lax.ppermute(coded, 'ch', far_pairs))]
    ppermute x3 -> x10, starting transfers between devices: 3.88 us -> 18.5 us  [the longest x3 9.45 us: local(): fars.append(lax.ppermute(coded, 'ch', far_pairs))]
    reduce_sum x1 -> x0, other arithmetic: 11.9 us -> none  [local(): filter_taps = jnp.sum(residues[None] * powers, axis=2)]
    unnamed x38 -> x14, local copies, waits for them, and re-layouts: 7.36 us -> 1.08 us
  transfers between devices with their start and end apart: 4 -> 10, of which waited for: 3 -> 8; matrix products, arithmetic and copies ran while one was open for 46% -> 0% of each run, Pallas kernels for 0% -> 25%
where the time goes in v1:
time: 89.4 us; the launch traced here: 88.9 us
  waiting for transfers between devices  35.4 us (40%)
  Pallas kernels  33.2 us (37%)
  starting transfers between devices  18.5 us (21%)
  local copies, waits for them, and re-layouts  1.08 us (1%)
    pallas_call x8, Pallas kernels, on_block(): pl.pallas_call(kernel, grid_spec=pltpu.PrefetchScalarGridSpec(num_scalar_...  25.1 us
    ppermute x3, waiting for transfers between devices, local(): fars.append(lax.ppermute(coded, 'ch', far_pairs))  15.7 us
    ppermute x4, waiting for transfers between devices, local(): nears[k, sub] = lax.ppermute(coded, 'ch', near_pairs)  14.7 us
    ppermute x3, starting transfers between devices, local(): fars.append(lax.ppermute(coded, 'ch', far_pairs))  9.45 us
    ppermute x4, starting transfers between devices, local(): nears[k, sub] = lax.ppermute(coded, 'ch', near_pairs)  5.17 us
    ppermute x3, waiting for transfers between devices, local(): lax.ppermute(state, 'ctx', [(i, i - hop) for i in range(hop, groups)])  4.98 us
    pallas_call x1, Pallas kernels, scan(): pl.pallas_call(functools.partial(scan_kernel, len(laters)), out_shape=jax...  4.42 us
    ppermute x3, starting transfers between devices, local(): lax.ppermute(state, 'ctx', [(i, i - hop) for i in range(hop, groups)])  3.86 us
  transfers between devices with their start and end apart: 10, of which 8 were waited for; matrix products, arithmetic and copies ran while one was open for 0% of the time, Pallas kernels for 25%

profile of v1, /device:TPU:0, one launch (start us, length us, event | category | flops | bytes accessed | tf_op | source)
XLA Modules:
  0.0 88.9 jit_solution(10488915003661638454)
XLA Ops:
  0.7 0.0 copy-start
  0.7 1.0 %copy-done = bf16[256,1024]{1,0:T(8,128)(2,1)S(1)} copy-done((bf16[256,1024]{1,0:T(8,128)(2,1)S(1)}, bf16[256,1024]{1,0:T(8,128)(2,1)}, u32[]{:S(2)}) %copy-start) | copy-done | bytes 524312
  1.7 0.0 copy-start.1
  1.7 2.7 %shard_map.79 = bf16[1040,256]{1,0:T(8,128)(2,1)S(1)} custom-call(s32[1]{0:T(128)} %bitcast.3._, bf16[8192,1024]{1,0:T(8,128)(2,1)} %w_ref.15, bf16[256,1024]{1,0:T(8,128)(2,1)S(1)} %copy-done), custom_call_target="tpu_custom_call" | custom-call | flops 536870912 | bytes 2621440 | tf_op jit(solution)/shard_map/pallas_call | solution.py:78
  4.4 3.0 %collective-permute-start.1 = (bf16[1040,256]{1,0:T(8,128)(2,1)S(1)}, bf16[1040,256]{1,0:T(8,128)(2,1)S(1)}, u32[]{:S(2)}, u32[]{:S(2)}) collective-permute-start(bf16[1040,256]{1,0:T(8,128)(2,1)S(1)} %shard_map.79), channel_id=1, source_target_pairs={{0,1},{1,0},{2,3},{3,2},{4,5},{5,4},{6,7},{7,6},{8,9},{9,8},{10,11... | collective-permute-start | bytes 1597448 | tf_op jit(solution)/shard_map/ppermute | solution.py:219
  7.4 0.0 copy-done.1
  7.4 2.6 %shard_map.81 = bf16[1040,256]{1,0:T(8,128)(2,1)S(1)} custom-call(s32[1]{0:T(128)} %bitcast.5._, bf16[8192,1024]{1,0:T(8,128)(2,1)} %w_ref.15, bf16[256,1024]{1,0:T(8,128)(2,1)S(1)} %copy-done.1), custom_call_target="tpu_custom_call" | custom-call | flops 536870912 | bytes 2621440 | tf_op jit(solution)/shard_map/pallas_call | solution.py:78
  10.0 0.1 collective-permute-start.3
  10.1 3.4 %shard_map.83 = bf16[1040,256]{1,0:T(8,128)(2,1)} custom-call(s32[1]{0:T(128)} %bitcast.7._, bf16[8192,1024]{1,0:T(8,128)(2,1)} %w_ref.15, bf16[256,1024]{1,0:T(8,128)(2,1)S(1)} %copy-done.1), custom_call_target="tpu_custom_call" | custom-call | flops 536870912 | bytes 2621440 | tf_op jit(solution)/shard_map/pallas_call | solution.py:78
  13.6 2.0 %collective-permute-start.5 = (bf16[1040,256]{1,0:T(8,128)(2,1)}, bf16[1040,256]{1,0:T(8,128)(2,1)}, u32[]{:S(2)}, u32[]{:S(2)}) collective-permute-start(bf16[1040,256]{1,0:T(8,128)(2,1)} %shard_map.83), channel_id=1, source_target_pairs={{0,1},{1,0},{2,3},{3,2},{4,5},{5,4},{6,7},{7,6},{8,9},{9,8},{10,11... | collective-permute-start | bytes 1597448 | tf_op jit(solution)/shard_map/ppermute | solution.py:219
  15.6 3.4 %shard_map.77 = bf16[1040,256]{1,0:T(8,128)(2,1)} custom-call(s32[1]{0:T(128)} %bitcast.1._, bf16[8192,1024]{1,0:T(8,128)(2,1)} %w_ref.15, bf16[256,1024]{1,0:T(8,128)(2,1)S(1)} %copy-done.1), custom_call_target="tpu_custom_call" | custom-call | flops 536870912 | bytes 2621440 | tf_op jit(solution)/shard_map/pallas_call | solution.py:78
  19.0 0.1 collective-permute-start
  19.0 1.3 %collective-permute-done.1.near_ref = bf16[1040,256]{1,0:T(8,128)(2,1)S(1)} collective-permute-done((bf16[1040,256]{1,0:T(8,128)(2,1)S(1)}, bf16[1040,256]{1,0:T(8,128)(2,1)S(1)}, u32[]{:S(2)}, u32[]{:S(2)}) %collective-permute-start.1) | collective-permute-done | bytes 532512 | tf_op jit(solution)/shard_map/ppermute | solution.py:219
  20.3 3.7 %shard_map.80 = bf16[1040,256]{1,0:T(8,128)(2,1)} custom-call(s32[1]{0:T(128)} %bitcast.2._, bf16[8192,1024]{1,0:T(8,128)(2,1)} %w_ref.15, bf16[256,1024]{1,0:T(8,128)(2,1)S(1)} %copy-done.1, bf16[1040,256]{1,0:T(8,128)(2,1)S(1)} %collective-permute-done.1.near_ref), custom_call_target="tpu_custom_call" | custom-call | flops 536870912 | bytes 2621440 | tf_op jit(solution)/shard_map/pallas_call | solution.py:78
  24.1 3.1 %collective-permute-start.2 = (bf16[1040,256]{1,0:T(8,128)(2,1)}, bf16[1040,256]{1,0:T(8,128)(2,1)S(1)}, u32[]{:S(2)}, u32[]{:S(2)}) collective-permute-start(bf16[1040,256]{1,0:T(8,128)(2,1)} %shard_map.80), channel_id=1, source_target_pairs={{0,4},{1,5},{2,6},{3,7},{4,0},{5,1},{6,2},{7,3},{8,12},{9,13},{10,... | collective-permute-start | bytes 1597448 | tf_op jit(solution)/shard_map/ppermute | solution.py:228
  27.2 4.5 %collective-permute-done.3.near_ref = bf16[1040,256]{1,0:T(8,128)(2,1)S(1)} collective-permute-done((bf16[1040,256]{1,0:T(8,128)(2,1)S(1)}, bf16[1040,256]{1,0:T(8,128)(2,1)S(1)}, u32[]{:S(2)}, u32[]{:S(2)}) %collective-permute-start.3) | collective-permute-done | bytes 532512 | tf_op jit(solution)/shard_map/ppermute | solution.py:219
  31.8 0.0 copy-start.4
  31.8 3.0 %shard_map.82 = bf16[1040,256]{1,0:T(8,128)(2,1)S(1)} custom-call(s32[1]{0:T(128)} %bitcast.4._, bf16[8192,1024]{1,0:T(8,128)(2,1)} %w_ref.15, bf16[256,1024]{1,0:T(8,128)(2,1)S(1)} %copy-done.1, bf16[1040,256]{1,0:T(8,128)(2,1)S(1)} %collective-permute-done.3.near_ref), custom_call_target="tpu_custom_call" | custom-call | flops 536870912 | bytes 2621440 | tf_op jit(solution)/shard_map/pallas_call | solution.py:78
  34.7 2.2 %collective-permute-start.4 = (bf16[1040,256]{1,0:T(8,128)(2,1)S(1)}, bf16[1040,256]{1,0:T(8,128)(2,1)S(1)}, u32[]{:S(2)}, u32[]{:S(2)}) collective-permute-start(bf16[1040,256]{1,0:T(8,128)(2,1)S(1)} %shard_map.82), channel_id=1, source_target_pairs={{0,2},{1,3},{2,4},{3,5},{4,6},{5,7},{6,0},{7,1},{8,10},{9,11},{10,... | collective-permute-start | bytes 1597448 | tf_op jit(solution)/shard_map/ppermute | solution.py:228
  36.9 6.4 %collective-permute-done.5.near_ref = bf16[1040,256]{1,0:T(8,128)(2,1)} collective-permute-done((bf16[1040,256]{1,0:T(8,128)(2,1)}, bf16[1040,256]{1,0:T(8,128)(2,1)}, u32[]{:S(2)}, u32[]{:S(2)}) %collective-permute-start.5) | collective-permute-done | bytes 532512 | tf_op jit(solution)/shard_map/ppermute | solution.py:219
  43.3 0.0 copy-start.5
  43.3 3.9 %shard_map.84 = bf16[1040,256]{1,0:T(8,128)(2,1)} custom-call(s32[1]{0:T(128)} %bitcast.6._, bf16[8192,1024]{1,0:T(8,128)(2,1)} %w_ref.15, bf16[256,1024]{1,0:T(8,128)(2,1)S(1)} %copy-done.1, bf16[1040,256]{1,0:T(8,128)(2,1)} %collective-permute-done.5.near_ref), custom_call_target="tpu_custom_call" | custom-call | flops 536870912 | bytes 2621440 | tf_op jit(solution)/shard_map/pallas_call | solution.py:78
  47.2 4.1 %collective-permute-start.6 = (bf16[1040,256]{1,0:T(8,128)(2,1)}, bf16[1040,256]{1,0:T(8,128)(2,1)S(1)}, u32[]{:S(2)}, u32[]{:S(2)}) collective-permute-start(bf16[1040,256]{1,0:T(8,128)(2,1)} %shard_map.84), channel_id=1, source_target_pairs={{0,6},{1,7},{2,0},{3,1},{4,2},{5,3},{6,4},{7,5},{8,14},{9,15},{10,... | collective-permute-start | bytes 1597448 | tf_op jit(solution)/shard_map/ppermute | solution.py:228
  51.3 0.0 copy-start.2
  51.3 0.0 copy-start.3
  51.3 0.0 copy-done.4
  51.3 2.4 %collective-permute-done.near_ref = bf16[1040,256]{1,0:T(8,128)(2,1)S(1)} collective-permute-done((bf16[1040,256]{1,0:T(8,128)(2,1)}, bf16[1040,256]{1,0:T(8,128)(2,1)S(1)}, u32[]{:S(2)}, u32[]{:S(2)}) %collective-permute-start) | collective-permute-done | bytes 532512 | tf_op jit(solution)/shard_map/ppermute | solution.py:219
  53.8 2.4 %shard_map.78.refs_0_ = f32[1024,256]{1,0:T(8,128)S(1)} custom-call(s32[1]{0:T(128)} %bitcast._, bf16[8192,1024]{1,0:T(8,128)(2,1)} %w_ref.15, bf16[256,1024]{1,0:T(8,128)(2,1)S(1)} %copy-done.1, bf16[1040,256]{1,0:T(8,128)(2,1)S(1)} %collective-permute-done.near_ref), custom_call_target="tpu_custom_call" | custom-call | flops 536870912 | bytes 2621440 | tf_op jit(solution)/shard_map/pallas_call | solution.py:78
  56.2 5.4 %collective-permute-done.2.refs_1_ = bf16[1040,256]{1,0:T(8,128)(2,1)S(1)} collective-permute-done((bf16[1040,256]{1,0:T(8,128)(2,1)}, bf16[1040,256]{1,0:T(8,128)(2,1)S(1)}, u32[]{:S(2)}, u32[]{:S(2)}) %collective-permute-start.2) | collective-permute-done | bytes 532512 | tf_op jit(solution)/shard_map/ppermute | solution.py:228
  61.6 0.0 collective-permute-done.4.refs_2_
  61.6 10.3 %collective-permute-done.6.refs_3_ = bf16[1040,256]{1,0:T(8,128)(2,1)S(1)} collective-permute-done((bf16[1040,256]{1,0:T(8,128)(2,1)}, bf16[1040,256]{1,0:T(8,128)(2,1)S(1)}, u32[]{:S(2)}, u32[]{:S(2)}) %collective-permute-start.6) | collective-permute-done | bytes 532512 | tf_op jit(solution)/shard_map/ppermute | solution.py:228
  71.9 0.0 copy-done.2
  71.9 0.0 copy-done.3
  71.9 3.7 %shard_map.85 = (bf16[256,1024]{1,0:T(8,128)(2,1)}, f32[2048,128]{1,0:T(8,128)S(1)}, f32[16,8,128]{2,1,0:T(8,128)S(1)}) custom-call(f32[1024,256]{1,0:T(8,128)S(1)} %shard_map.78.refs_0_, bf16[1040,256]{1,0:T(8,128)(2,1)S(1)} %collective-permute-done.2.refs_1_, bf16[1040,256]{1,0:T(8,128)(2,1)S(1)} %collective-permute-done.4.refs_2_, ...), custom_call_target="tpu_custom_call" | custom-call | flops 8388608 | bytes 4194304 | tf_op jit(solution)/shard_map/pallas_call | solution.py:131
  75.6 1.3 %collective-permute-start.7 = (f32[16,8,128]{2,1,0:T(8,128)S(1)}, f32[16,8,128]{2,1,0:T(8,128)S(1)}, u32[]{:S(2)}, u32[]{:S(2)}) collective-permute-start(f32[16,8,128]{2,1,0:T(8,128)S(1)} %get-tuple-element.7), channel_id=1, source_target_pairs={{8,0},{16,8},{24,16},{9,1},{17,9},{25,17},{10,2},{18,10},{26,18},{... | collective-permute-start | bytes 196616 | tf_op jit(solution)/shard_map/ppermute | solution.py:233
  76.9 1.3 %collective-permute-start.8 = (f32[16,8,128]{2,1,0:T(8,128)S(1)}, f32[16,8,128]{2,1,0:T(8,128)S(1)}, u32[]{:S(2)}, u32[]{:S(2)}) collective-permute-start(f32[16,8,128]{2,1,0:T(8,128)S(1)} %get-tuple-element.7), channel_id=1, source_target_pairs={{16,0},{24,8},{17,1},{25,9},{18,2},{26,10},{19,3},{27,11},{20,4},{... | collective-permute-start | bytes 196616 | tf_op jit(solution)/shard_map/ppermute | solution.py:233
  78.2 1.3 %collective-permute-start.9 = (f32[16,8,128]{2,1,0:T(8,128)S(1)}, f32[16,8,128]{2,1,0:T(8,128)S(1)}, u32[]{:S(2)}, u32[]{:S(2)}) collective-permute-start(f32[16,8,128]{2,1,0:T(8,128)S(1)} %get-tuple-element.7), channel_id=1, source_target_pairs={{24,0},{25,1},{26,2},{27,3},{28,4},{29,5},{30,6},{31,7}} | collective-permute-start | bytes 196616 | tf_op jit(solution)/shard_map/ppermute | solution.py:233
  79.5 0.0 copy-done.5
  79.5 0.0 collective-permute-done.7.refs_0_
  79.5 4.1 %collective-permute-done.8.refs_1_ = f32[16,8,128]{2,1,0:T(8,128)S(1)} collective-permute-done((f32[16,8,128]{2,1,0:T(8,128)S(1)}, f32[16,8,128]{2,1,0:T(8,128)S(1)}, u32[]{:S(2)}, u32[]{:S(2)}) %collective-permute-start.8) | collective-permute-done | bytes 65568 | tf_op jit(solution)/shard_map/ppermute | solution.py:233
  83.6 0.9 %collective-permute-done.9.refs_2_ = f32[16,8,128]{2,1,0:T(8,128)S(1)} collective-permute-done((f32[16,8,128]{2,1,0:T(8,128)S(1)}, f32[16,8,128]{2,1,0:T(8,128)S(1)}, u32[]{:S(2)}, u32[]{:S(2)}) %collective-permute-start.9) | collective-permute-done | bytes 65568 | tf_op jit(solution)/shard_map/ppermute | solution.py:233
  84.5 4.4 %shard_map.86 = bf16[256,1024]{1,0:T(8,128)(2,1)} custom-call(f32[2048,128]{1,0:T(8,128)S(1)} %get-tuple-element.6.gc_ref, f32[16,8,128]{2,1,0:T(8,128)S(1)} %collective-permute-done.7.refs_0_, f32[16,8,128]{2,1,0:T(8,128)S(1)} %collective-permute-done.8.refs_1_, f32[16,8,128]{2,1,0:T(8,128)S(1)} %collective-permute-done.9.refs_2_, ...), custom_call_target="tpu_custom_call" | custom-call | flops 16777216 | bytes 1572864 | tf_op jit(solution)/shard_map/pallas_call | solution.py:187
  (2 shorter events, 0.0 us)
Async XLA Ops:
  0.7 1.0 %copy-start = (bf16[256,1024]{1,0:T(8,128)(2,1)S(1)}, bf16[256,1024]{1,0:T(8,128)(2,1)}, u32[]{:S(2)}) copy-start(bf16[256,1024]{1,0:T(8,128)(2,1)} %g_ref.15) | copy-start | bytes 1572868
  1.7 5.7 %copy-start.1 = (bf16[256,1024]{1,0:T(8,128)(2,1)S(1)}, bf16[256,1024]{1,0:T(8,128)(2,1)}, u32[]{:S(2)}) copy-start(bf16[256,1024]{1,0:T(8,128)(2,1)} %g_ref.15) | copy-start | bytes 1572868
  4.4 16.0 %collective-permute-start.1 = (bf16[1040,256]{1,0:T(8,128)(2,1)S(1)}, bf16[1040,256]{1,0:T(8,128)(2,1)S(1)}, u32[]{:S(2)}, u32[]{:S(2)}) collective-permute-start(bf16[1040,256]{1,0:T(8,128)(2,1)S(1)} %shard_map.79), channel_id=1, source_target_pairs={{0,1},{1,0},{2,3},{3,2},{4,5},{5,4},{6,7},{7,6},{8,9},{9,8},{10,11... | collective-permute-start | bytes 1597448 | tf_op jit(solution)/shard_map/ppermute | solution.py:219
  10.0 21.7 %collective-permute-start.3 = (bf16[1040,256]{1,0:T(8,128)(2,1)S(1)}, bf16[1040,256]{1,0:T(8,128)(2,1)S(1)}, u32[]{:S(2)}, u32[]{:S(2)}) collective-permute-start(bf16[1040,256]{1,0:T(8,128)(2,1)S(1)} %shard_map.81), channel_id=1, source_target_pairs={{0,1},{1,0},{2,3},{3,2},{4,5},{5,4},{6,7},{7,6},{8,9},{9,8},{10,11... | collective-permute-start | bytes 1597448 | tf_op jit(solution)/shard_map/ppermute | solution.py:219
  13.6 29.7 %collective-permute-start.5 = (bf16[1040,256]{1,0:T(8,128)(2,1)}, bf16[1040,256]{1,0:T(8,128)(2,1)}, u32[]{:S(2)}, u32[]{:S(2)}) collective-permute-start(bf16[1040,256]{1,0:T(8,128)(2,1)} %shard_map.83), channel_id=1, source_target_pairs={{0,1},{1,0},{2,3},{3,2},{4,5},{5,4},{6,7},{7,6},{8,9},{9,8},{10,11... | collective-permute-start | bytes 1597448 | tf_op jit(solution)/shard_map/ppermute | solution.py:219
  19.0 34.8 %collective-permute-start = (bf16[1040,256]{1,0:T(8,128)(2,1)}, bf16[1040,256]{1,0:T(8,128)(2,1)S(1)}, u32[]{:S(2)}, u32[]{:S(2)}) collective-permute-start(bf16[1040,256]{1,0:T(8,128)(2,1)} %shard_map.77), channel_id=1, source_target_pairs={{0,1},{1,0},{2,3},{3,2},{4,5},{5,4},{6,7},{7,6},{8,9},{9,8},{10,11... | collective-permute-start | bytes 1597448 | tf_op jit(solution)/shard_map/ppermute | solution.py:219
  24.1 37.5 %collective-permute-start.2 = (bf16[1040,256]{1,0:T(8,128)(2,1)}, bf16[1040,256]{1,0:T(8,128)(2,1)S(1)}, u32[]{:S(2)}, u32[]{:S(2)}) collective-permute-start(bf16[1040,256]{1,0:T(8,128)(2,1)} %shard_map.80), channel_id=1, source_target_pairs={{0,4},{1,5},{2,6},{3,7},{4,0},{5,1},{6,2},{7,3},{8,12},{9,13},{10,... | collective-permute-start | bytes 1597448 | tf_op jit(solution)/shard_map/ppermute | solution.py:228
  31.8 19.5 %copy-start.4 = (f32[1024,16]{0,1:T(8,128)S(1)}, f32[1024,16]{0,1:T(8,128)}, u32[]{:S(2)}) copy-start(f32[1024,16]{0,1:T(8,128)} %param.11) | copy-start | bytes 196612
  34.7 26.9 %collective-permute-start.4 = (bf16[1040,256]{1,0:T(8,128)(2,1)S(1)}, bf16[1040,256]{1,0:T(8,128)(2,1)S(1)}, u32[]{:S(2)}, u32[]{:S(2)}) collective-permute-start(bf16[1040,256]{1,0:T(8,128)(2,1)S(1)} %shard_map.82), channel_id=1, source_target_pairs={{0,2},{1,3},{2,4},{3,5},{4,6},{5,7},{6,0},{7,1},{8,10},{9,11},{10,... | collective-permute-start | bytes 1597448 | tf_op jit(solution)/shard_map/ppermute | solution.py:228
  43.3 36.2 %copy-start.5 = (f32[1024,16]{0,1:T(8,128)S(1)}, f32[1024,16]{0,1:T(8,128)}, u32[]{:S(2)}) copy-start(f32[1024,16]{0,1:T(8,128)} %param.10) | copy-start | bytes 196612
  47.2 24.7 %collective-permute-start.6 = (bf16[1040,256]{1,0:T(8,128)(2,1)}, bf16[1040,256]{1,0:T(8,128)(2,1)S(1)}, u32[]{:S(2)}, u32[]{:S(2)}) collective-permute-start(bf16[1040,256]{1,0:T(8,128)(2,1)} %shard_map.84), channel_id=1, source_target_pairs={{0,6},{1,7},{2,0},{3,1},{4,2},{5,3},{6,4},{7,5},{8,14},{9,15},{10,... | collective-permute-start | bytes 1597448 | tf_op jit(solution)/shard_map/ppermute | solution.py:228
  51.3 20.6 %copy-start.2 = (bf16[256,1024]{1,0:T(8,128)(2,1)S(1)}, bf16[256,1024]{1,0:T(8,128)(2,1)}, u32[]{:S(2)}) copy-start(bf16[256,1024]{1,0:T(8,128)(2,1)} %refs_4_.1) | copy-start | bytes 1572868
  51.3 20.6 %copy-start.3 = (bf16[256,1024]{1,0:T(8,128)(2,1)S(1)}, bf16[256,1024]{1,0:T(8,128)(2,1)}, u32[]{:S(2)}) copy-start(bf16[256,1024]{1,0:T(8,128)(2,1)} %refs_5_.1) | copy-start | bytes 1572868
  75.6 3.9 %collective-permute-start.7 = (f32[16,8,128]{2,1,0:T(8,128)S(1)}, f32[16,8,128]{2,1,0:T(8,128)S(1)}, u32[]{:S(2)}, u32[]{:S(2)}) collective-permute-start(f32[16,8,128]{2,1,0:T(8,128)S(1)} %get-tuple-element.7), channel_id=1, source_target_pairs={{8,0},{16,8},{24,16},{9,1},{17,9},{25,17},{10,2},{18,10},{26,18},{... | collective-permute-start | bytes 196616 | tf_op jit(solution)/shard_map/ppermute | solution.py:233
  76.9 6.7 %collective-permute-start.8 = (f32[16,8,128]{2,1,0:T(8,128)S(1)}, f32[16,8,128]{2,1,0:T(8,128)S(1)}, u32[]{:S(2)}, u32[]{:S(2)}) collective-permute-start(f32[16,8,128]{2,1,0:T(8,128)S(1)} %get-tuple-element.7), channel_id=1, source_target_pairs={{16,0},{24,8},{17,1},{25,9},{18,2},{26,10},{19,3},{27,11},{20,4},{... | collective-permute-start | bytes 196616 | tf_op jit(solution)/shard_map/ppermute | solution.py:233
  78.2 6.3 %collective-permute-start.9 = (f32[16,8,128]{2,1,0:T(8,128)S(1)}, f32[16,8,128]{2,1,0:T(8,128)S(1)}, u32[]{:S(2)}, u32[]{:S(2)}) collective-permute-start(f32[16,8,128]{2,1,0:T(8,128)S(1)} %get-tuple-element.7), channel_id=1, source_target_pairs={{24,0},{25,1},{26,2},{27,3},{28,4},{29,5},{30,6},{31,7}} | collective-permute-start | bytes 196616 | tf_op jit(solution)/shard_map/ppermute | solution.py:233

commit v2 on v0

v2 whole, which is shorter than its diff:
```python
import functools
import math

import jax
import jax.numpy as jnp
from jax import lax
from jax.experimental import pallas as pl
from jax.experimental.pallas import tpu as pltpu
from jax.sharding import PartitionSpec as P

PEAKS = 16
SPAN = 251 * math.log(2.0)
SHIFT = 125 * math.log(2.0)
STEP = 256
VMEM = 24 * 1024 * 1024
QUICK = pl.CostEstimate(flops=0, bytes_accessed=1024, transcendentals=0)

ORDER = (
    (0, 0, 6), (1, 0, 6), (0, 0, 4), (0, 1, 4), (0, 0, 2), (1, 1, 4), (1, 0, 4), (0, 2, 0), (0, 1, 0),
    (1, 0, 2), (1, 2, 0), (0, 0, 0), (1, 1, 0), (1, 0, 0),
)


def part_of(rows):
    return max(rows // PEAKS, min(rows, 16))


def encode(block, part):
    codes, peaks = [], []
    for i in range(block.shape[0] // part):
        piece = block[i * part : (i + 1) * part, :]
        size = jnp.abs(piece)
        peak = jnp.maximum(jnp.max(size, axis=0, keepdims=True) * 1.01, 1e-30)
        peak = peak.astype(jnp.bfloat16).astype(jnp.float32)
        code = jnp.exp(size * (SPAN / peak) - SHIFT)
        codes.append(jnp.where(piece < 0, -code, code))
        peaks.append(peak)
    return jnp.concatenate(codes, axis=0).astype(jnp.bfloat16), peaks


def decode(ref, base, rows, first, count):
    part = part_of(rows)
    peaks = ref[base + rows : base + rows + PEAKS, :].astype(jnp.float32) * (1.0 / SPAN)
    blocks = []
    for i in range(first // part, (first + count) // part):
        code = ref[base + i * part : base + (i + 1) * part, :].astype(jnp.float32)
        size = (jnp.log(jnp.abs(code)) + SHIFT) * peaks[i : i + 1, :]
        blocks.append(jnp.where(code < 0, -size, size))
    return jnp.concatenate(blocks, axis=0)


def pinned(array):
    return pltpu.with_memory_space_constraint(array, pltpu.HBM)


def send_kernel(rows, starts, sources, coded, near, place_ref, w_ref, g_ref, *refs):
    near_refs, (out_ref, w_buf, g_buf, sems) = refs[:near], refs[near:]
    step = min(rows, STEP)
    place = place_ref[0]
    grad = pltpu.make_async_copy(g_ref, g_buf, sems.at[0])
    grad.start()
    copies = []
    for i, (block, offset, width) in enumerate(starts):
        first = pl.multiple_of((place ^ block) * width + offset, 16)
        for at in range(0, rows, step):
            copy = pltpu.make_async_copy(
                w_ref.at[pl.ds(first + at, step), :],
                w_buf.at[pl.ds(i * rows + at, step), :],
                sems.at[1 + len(copies)],
            )
            copy.start()
            copies.append(copy)
    grad.wait()
    part = part_of(rows)
    stride = rows + PEAKS if coded else rows
    copies = iter(copies)
    for i in range(len(starts)):
        peaks = []
        for at in range(0, rows, step):
            next(copies).wait()
            block = lax.dot_general(
                w_buf[i * rows + at : i * rows + at + step, :],
                g_buf[...],
                (((1,), (1,)), ((), ())),
                preferred_element_type=jnp.float32,
            )
            for source, base in sources[i]:
                block = block + decode(near_refs[source], base, rows, at, step)
            if coded:
                block, more = encode(block, part)
                peaks += more
            out_ref[i * stride + at : i * stride + at + step, :] = block
        if coded:
            toks = block.shape[1]
            if len(peaks) < PEAKS:
                peaks.append(jnp.zeros((PEAKS - len(peaks), toks), jnp.float32))
            out_ref[i * stride + rows : (i + 1) * stride, :] = jnp.concatenate(peaks, axis=0).astype(jnp.bfloat16)


def send(rows, starts, sources, coded, place, weight, grad, nears):
    toks, depth = grad.shape
    vmem = pl.BlockSpec(memory_space=pltpu.VMEM)
    high = pl.BlockSpec(memory_space=pltpu.HBM)
    count = len(starts) * (rows + PEAKS if coded else rows)
    steps = len(starts) * (rows // min(rows, STEP))
    work = len(starts) * rows
    return pl.pallas_call(
        functools.partial(send_kernel, rows, starts, sources, coded, len(nears)),
        in_specs=[pl.BlockSpec(memory_space=pltpu.SMEM), high, high] + [vmem] * len(nears),
        out_specs=vmem,
        out_shape=jax.ShapeDtypeStruct((count, toks), jnp.bfloat16 if coded else jnp.float32),
        scratch_shapes=[
            pltpu.VMEM((work, depth), jnp.bfloat16),
            pltpu.VMEM((toks, depth), jnp.bfloat16),
            pltpu.SemaphoreType.DMA((steps + 1,)),
        ],
        compiler_params=pltpu.CompilerParams(vmem_limit_bytes=VMEM),
        cost_estimate=QUICK,
    )(place, pinned(weight), pinned(grad), *nears)


def steps_back(count, body, state, unroll):
    def some(i, state):
        for j in range(unroll):
            state = body(count - 1 - (i * unroll + j), state)
        return state

    return lax.fori_loop(0, count // unroll, some, state)


def power(base, exponent):
    result = None
    while exponent:
        if exponent % 2:
            result = base if result is None else result * base
        base = base * base
        exponent //= 2
    return result


def segment_of(shape, segments):
    return lax.rem(lax.broadcasted_iota(jnp.int32, shape, 0), segments)


def rolled(value, by):
    by %= value.shape[0]
    return pltpu.roll(value, by, 0) if by else value


def gate_kernel(portion, rows, segments, fars, acc_ref, *refs):
    far_refs, refs = refs[: len(fars)], refs[len(fars) :]
    query_hbm, conv_hbm, decay_ref = refs[:3]
    out_hbm, gc_ref, state_ref, pack_ref, query_ref, conv_ref, gq_ref, sems = refs[-8:]
    columns = pl.ds(portion * rows, rows)
    loads = [
        pltpu.make_async_copy(query_hbm.at[:, columns], query_ref, sems.at[0]),
        pltpu.make_async_copy(conv_hbm.at[:, columns], conv_ref, sems.at[1]),
    ]
    for load in loads:
        load.start()
    toks = query_ref.shape[0]
    modes, sublanes, lanes = state_ref.shape
    mine = slice(portion * sublanes, (portion + 1) * sublanes)
    for line in range(rows // lanes):
        mix = acc_ref[line * lanes : (line + 1) * lanes, :]
        for ref, base in zip(far_refs, fars):
            mix = mix + decode(ref, base, rows, line * lanes, lanes)
        mix = mix.T
        if line == 0:
            for load in loads:
                load.wait()
        at = slice(line * lanes, (line + 1) * lanes)
        gq_ref[:, at] = (mix * conv_ref[:, at].astype(jnp.float32)).astype(jnp.bfloat16)
        gc_ref[line * toks : (line + 1) * toks, :] = mix * query_ref[:, at].astype(jnp.float32)
    store = pltpu.make_async_copy(gq_ref, out_hbm.at[:, columns], sems.at[2])
    store.start()
    decay = [decay_ref[n, mine] for n in range(modes)]
    span = toks // segments

    def step(t, state):
        row = gc_ref[pl.ds(t, sublanes, stride=span), :]
        return tuple(decay[n] * state[n] + row for n in range(modes))

    zero = jnp.zeros((sublanes, lanes), jnp.float32)
    state = steps_back(span, step, (zero,) * modes, 8)
    segment = segment_of((sublanes, lanes), segments)
    whole = []
    for n in range(modes):
        state_ref[n] = state[n]
        total = state[n]
        if segments > 1:
            factor = jnp.where(segment < segments - 1, power(decay[n], span), 0.0)
            for _ in range(segments - 1):
                total = state[n] + factor * rolled(total, -1)
        whole.append(total)
    for m in range(modes // segments):
        packed = whole[m * segments]
        for j in range(1, segments):
            packed = jnp.where(segment == j, rolled(whole[m * segments + j], j), packed)
        pack_ref[m] = packed
    store.wait()


def gate(portion, rows, segments, acc, fars, query_in, conv_out, decay, partial):
    toks, width = query_in.shape
    modes, sublanes, lanes = decay.shape
    sublanes = rows // lanes * segments
    vmem = pl.BlockSpec(memory_space=pltpu.VMEM)
    high = pl.BlockSpec(memory_space=pltpu.HBM)
    more = [] if partial is None else [partial]
    return pl.pallas_call(
        functools.partial(gate_kernel, portion, rows, segments, (0,) * len(fars)),
        in_specs=[vmem] * (1 + len(fars)) + [high, high, vmem] + [high] * len(more),
        out_specs=(high, vmem, vmem, vmem),
        out_shape=(
            jax.ShapeDtypeStruct((toks, width), jnp.bfloat16),
            jax.ShapeDtypeStruct((rows // lanes * toks, lanes), jnp.float32),
            jax.ShapeDtypeStruct((modes, sublanes, lanes), jnp.float32),
            jax.ShapeDtypeStruct((modes // segments, sublanes, lanes), jnp.float32),
        ),
        scratch_shapes=[pltpu.VMEM((toks, rows), jnp.bfloat16)] * 3 + [pltpu.SemaphoreType.DMA((3,))],
        input_output_aliases={4 + len(fars): 0} if more else {},
        compiler_params=pltpu.CompilerParams(vmem_limit_bytes=VMEM),
        cost_estimate=QUICK,
    )(acc, *fars, pinned(query_in), pinned(conv_out), decay, *more)


def scan_kernel(portion, segments, hops, gc_ref, state_ref, *refs):
    later_refs, refs = refs[:hops], refs[hops:]
    decay_ref, residue_ref = refs[:2]
    out_hbm, rows_ref, out_ref, sem = refs[-4:]
    toks, rows = out_ref.shape
    modes, sublanes, lanes = state_ref.shape
    mine = slice(portion * sublanes, (portion + 1) * sublanes)
    span = toks // segments
    segment = segment_of((sublanes, lanes), segments)
    decay = [decay_ref[n, mine] for n in range(modes)]
    start = []
    for n in range(modes):
        group = power(decay[n], span)
        whole = power(group, segments)
        m, j = divmod(n, segments)
        total = later_refs[-1][m]
        for ref in reversed(later_refs[:-1]):
            total = total * whole + ref[m]
        total = rolled(total, segments - 1 - j)
        for k in range(segments - 2, -1, -1):
            total = jnp.where(segment == k, rolled(state_ref[n] + group * total, -1), total)
        start.append(total)

    def step(t, state):
        at = pl.ds(t, sublanes, stride=span)
        row = gc_ref[at, :]
        state = tuple(decay[n] * state[n] + row for n in range(modes))
        terms = [residue_ref[n, mine] * state[n] for n in range(modes)]
        while len(terms) > 1:
            terms = [terms[i] + terms[i + 1] for i in range(0, len(terms), 2)]
        rows_ref[at, :] = terms[0]
        return state

    steps_back(span, step, tuple(start), 8)
    for line in range(rows // lanes):
        out_ref[:, line * lanes : (line + 1) * lanes] = rows_ref[
            line * toks : (line + 1) * toks, :
        ].astype(jnp.bfloat16)
    store = pltpu.make_async_copy(out_ref, out_hbm.at[:, pl.ds(portion * rows, rows)], sem)
    store.start()
    store.wait()


def scan(portion, rows, segments, grad_conv, state, laters, decay, residues, toks, width, partial):
    vmem = pl.BlockSpec(memory_space=pltpu.VMEM)
    high = pl.BlockSpec(memory_space=pltpu.HBM)
    more = [] if partial is None else [partial]
    return pl.pallas_call(
        functools.partial(scan_kernel, portion, segments, len(laters)),
        in_specs=[vmem] * (4 + len(laters)) + [high] * len(more),
        out_specs=high,
        out_shape=jax.ShapeDtypeStruct((toks, width), jnp.bfloat16),
        scratch_shapes=[
            pltpu.VMEM(grad_conv.shape, jnp.float32),
            pltpu.VMEM((toks, rows), jnp.bfloat16),
            pltpu.SemaphoreType.DMA,
        ],
        input_output_aliases={4 + len(laters): 0} if more else {},
        compiler_params=pltpu.CompilerParams(vmem_limit_bytes=VMEM),
        cost_estimate=QUICK,
    )(grad_conv, state, *laters, decay, residues, *more)


def local(out_grad, out_weight, query_in, conv_out, residues, decay_rates):
    toks, width = query_in.shape
    modes = decay_rates.shape[1]
    lanes = math.gcd(width, 128)
    size = lax.axis_size("ch")
    bits = [1 << i for i in range(size.bit_length() - 1)]
    place = jnp.reshape(lax.axis_index("ch"), (1,)).astype(jnp.int32)
    rows = width // 2
    lines = rows // lanes
    segments = 8 // lines
    by_mode = lambda values: jnp.repeat(values.T.reshape(modes, width // lanes, lanes), segments, axis=1)
    decay, residue = by_mode(decay_rates), by_mode(residues)

    order = ORDER
    if size != 8:
        order = [
            (p, s, block)
            for p in range(2)
            for s, bit in enumerate(bits)
            for block in sorted(range(0, size, 2 * bit), reverse=True)
        ]
    received = {}
    groups = lax.axis_size("ctx")
    last = None

    def after(value):
        return value if last is None else lax.optimization_barrier((value, last))[0]

    for p, s, block in order:
        bit = bits[s]
        nears = [received[p, i, block ^ bit] for i in range(s)]
        last = send(
            rows,
            ((block ^ bit, p * rows, width),),
            (tuple((i, 0) for i in range(s)),),
            True,
            after(place),
            out_weight,
            out_grad,
            nears,
        )
        received[p, s, block] = lax.ppermute(last, "ch", [(i, i ^ bit) for i in range(size)])

    states = []
    grad_query = grad_input = None
    for p in range(2):
        acc = send(
            rows, ((0, p * rows, width),), (((0, 0),),), False, after(place), out_weight, out_grad, [received[p, 0, 0]]
        )
        fars = [received[p, s, 0] for s in range(1, len(bits))]
        grad_query, grad_conv, state, packed = gate(
            p, rows, segments, acc, fars, query_in, conv_out, decay, grad_query
        )
        last = packed
        laters = [
            lax.ppermute(packed, "ctx", [(i, i - hop) for i in range(hop, groups)]) for hop in range(1, groups)
        ]
        states.append((grad_conv, state, laters))
    for p, (grad_conv, state, laters) in enumerate(states):
        grad_input = scan(
            p, rows, segments, grad_conv, state, laters, decay, residue, toks, width, grad_input
        )
    return grad_query, grad_input


def solution(mesh):
    placed = (
        P("ctx", "ch"),
        P(None, "ch"),
        P("ctx", "ch"),
        P("ctx", "ch"),
        P("ch", None),
        P("ch", None),
    )
    return jax.shard_map(
        local,
        mesh=mesh,
        in_specs=placed,
        out_specs=(P("ctx", "ch"), P("ctx", "ch")),
        check_vma=False,
    )
```

time: 347 us -> 86 us (0.25)
  the two profiles are of different devices: /device:TPU:0 before, /device:TPU:27 now
where the time goes in v2:
time: 86 us; the launch traced here: 85.3 us
  Pallas kernels  46.8 us (54%)
  starting transfers between devices  34.3 us (40%)
  waiting for transfers between devices  2.96 us (3%)
  between operations  1.12 us (1%)
    pallas_call x16, Pallas kernels, send(): pl.pallas_call(functools.partial(send_kernel, rows, starts, sources, code...  36.9 us
    ppermute x6, starting transfers between devices, local(): lax.ppermute(packed, 'ctx', [(i, i - hop) for i in range(hop, groups)])  21.5 us
    ppermute x14, starting transfers between devices, local(): lax.ppermute(last, 'ch', [(i, i ^ bit) for i in range(size)])  12.8 us
    pallas_call x2, Pallas kernels, scan(): pl.pallas_call(functools.partial(scan_kernel, portion, segments, len(late...  5.05 us
    pallas_call x2, Pallas kernels, gate(): pl.pallas_call(functools.partial(gate_kernel, portion, rows, segments, (0...  4.86 us
    ppermute x14, waiting for transfers between devices, local(): lax.ppermute(last, 'ch', [(i, i ^ bit) for i in range(size)])  2.94 us
  transfers between devices with their start and end apart: 20, of which 2 were waited for; matrix products, arithmetic and copies ran while one was open for 0% of the time, Pallas kernels for 49%

profile of v2, /device:TPU:27, one launch (start us, length us, event | category | flops | bytes accessed | tf_op | source)
XLA Modules:
  0.0 85.3 jit_solution(11005807589730589841)
XLA Ops:
  0.6 2.3 %shard_map.77 = bf16[528,256]{1,0:T(8,128)(2,1)S(1)} custom-call(s32[1]{0:T(128)} %bitcast.place_ref, bf16[8192,1024]{1,0:T(8,128)(2,1)} %w_ref.31, bf16[256,1024]{1,0:T(8,128)(2,1)} %g_ref.31), custom_call_target="tpu_custom_call" | custom-call | bytes 1024 | tf_op jit(solution)/shard_map/pallas_call | solution.py:107
  2.9 1.3 %collective-permute-start = (bf16[528,256]{1,0:T(8,128)(2,1)S(1)}, bf16[528,256]{1,0:T(8,128)(2,1)S(1)}, u32[]{:S(2)}, u32[]{:S(2)}) collective-permute-start(bf16[528,256]{1,0:T(8,128)(2,1)S(1)} %shard_map.77), channel_id=1, source_target_pairs={{0,1},{1,0},{2,3},{3,2},{4,5},{5,4},{6,7},{7,6},{8,9},{9,8},{10,11... | collective-permute-start | bytes 811016 | tf_op jit(solution)/shard_map/ppermute | solution.py:332
  4.2 2.3 %shard_map.78 = bf16[528,256]{1,0:T(8,128)(2,1)S(1)} custom-call(s32[1]{0:T(128)} %bitcast.place_ref, bf16[8192,1024]{1,0:T(8,128)(2,1)} %w_ref.31, bf16[256,1024]{1,0:T(8,128)(2,1)} %g_ref.31), custom_call_target="tpu_custom_call" | custom-call | bytes 1024 | tf_op jit(solution)/shard_map/pallas_call | solution.py:107
  6.5 0.3 collective-permute-start.1
  6.8 2.3 %shard_map.79 = bf16[528,256]{1,0:T(8,128)(2,1)S(1)} custom-call(s32[1]{0:T(128)} %bitcast.place_ref, bf16[8192,1024]{1,0:T(8,128)(2,1)} %w_ref.31, bf16[256,1024]{1,0:T(8,128)(2,1)} %g_ref.31), custom_call_target="tpu_custom_call" | custom-call | bytes 1024 | tf_op jit(solution)/shard_map/pallas_call | solution.py:107
  9.1 1.3 %collective-permute-start.2 = (bf16[528,256]{1,0:T(8,128)(2,1)S(1)}, bf16[528,256]{1,0:T(8,128)(2,1)S(1)}, u32[]{:S(2)}, u32[]{:S(2)}) collective-permute-start(bf16[528,256]{1,0:T(8,128)(2,1)S(1)} %shard_map.79), channel_id=1, source_target_pairs={{0,1},{1,0},{2,3},{3,2},{4,5},{5,4},{6,7},{7,6},{8,9},{9,8},{10,11... | collective-permute-start | bytes 811016 | tf_op jit(solution)/shard_map/ppermute | solution.py:332
  10.4 0.0 collective-permute-done.refs_0_
  10.4 2.3 %shard_map.80 = bf16[528,256]{1,0:T(8,128)(2,1)S(1)} custom-call(s32[1]{0:T(128)} %bitcast.place_ref, bf16[8192,1024]{1,0:T(8,128)(2,1)} %w_ref.31, bf16[256,1024]{1,0:T(8,128)(2,1)} %g_ref.31, bf16[528,256]{1,0:T(8,128)(2,1)S(1)} %collective-permute-done.refs_0_), custom_call_target="tpu_custom_call" | custom-call | bytes 1024 | tf_op jit(solution)/shard_map/pallas_call | solution.py:107
  12.8 0.2 collective-permute-start.3
  13.0 2.3 %shard_map.81 = bf16[528,256]{1,0:T(8,128)(2,1)S(1)} custom-call(s32[1]{0:T(128)} %bitcast.place_ref, bf16[8192,1024]{1,0:T(8,128)(2,1)} %w_ref.31, bf16[256,1024]{1,0:T(8,128)(2,1)} %g_ref.31), custom_call_target="tpu_custom_call" | custom-call | bytes 1024 | tf_op jit(solution)/shard_map/pallas_call | solution.py:107
  15.3 1.2 %collective-permute-start.4 = (bf16[528,256]{1,0:T(8,128)(2,1)S(1)}, bf16[528,256]{1,0:T(8,128)(2,1)S(1)}, u32[]{:S(2)}, u32[]{:S(2)}) collective-permute-start(bf16[528,256]{1,0:T(8,128)(2,1)S(1)} %shard_map.81), channel_id=1, source_target_pairs={{0,1},{1,0},{2,3},{3,2},{4,5},{5,4},{6,7},{7,6},{8,9},{9,8},{10,11... | collective-permute-start | bytes 811016 | tf_op jit(solution)/shard_map/ppermute | solution.py:332
  16.5 0.0 collective-permute-done.1.refs_0_
  16.5 2.3 %shard_map.82 = bf16[528,256]{1,0:T(8,128)(2,1)S(1)} custom-call(s32[1]{0:T(128)} %bitcast.place_ref, bf16[8192,1024]{1,0:T(8,128)(2,1)} %w_ref.31, bf16[256,1024]{1,0:T(8,128)(2,1)} %g_ref.31, bf16[528,256]{1,0:T(8,128)(2,1)S(1)} %collective-permute-done.1.refs_0_), custom_call_target="tpu_custom_call" | custom-call | bytes 1024 | tf_op jit(solution)/shard_map/pallas_call | solution.py:107
  18.9 2.3 %shard_map.83 = bf16[528,256]{1,0:T(8,128)(2,1)S(1)} custom-call(s32[1]{0:T(128)} %bitcast.place_ref, bf16[8192,1024]{1,0:T(8,128)(2,1)} %w_ref.31, bf16[256,1024]{1,0:T(8,128)(2,1)} %g_ref.31), custom_call_target="tpu_custom_call" | custom-call | bytes 1024 | tf_op jit(solution)/shard_map/pallas_call | solution.py:107
  21.2 0.9 %collective-permute-start.5 = (bf16[528,256]{1,0:T(8,128)(2,1)S(1)}, bf16[528,256]{1,0:T(8,128)(2,1)S(1)}, u32[]{:S(2)}, u32[]{:S(2)}) collective-permute-start(bf16[528,256]{1,0:T(8,128)(2,1)S(1)} %shard_map.83), channel_id=1, source_target_pairs={{0,1},{1,0},{2,3},{3,2},{4,5},{5,4},{6,7},{7,6},{8,9},{9,8},{10,11... | collective-permute-start | bytes 811016 | tf_op jit(solution)/shard_map/ppermute | solution.py:332
  22.1 0.7 collective-permute-start.6
  22.8 0.0 collective-permute-done.2.refs_0_
  22.8 0.0 collective-permute-done.3.refs_1_
  22.8 2.5 %shard_map.84 = bf16[528,256]{1,0:T(8,128)(2,1)S(1)} custom-call(s32[1]{0:T(128)} %bitcast.place_ref, bf16[8192,1024]{1,0:T(8,128)(2,1)} %w_ref.31, bf16[256,1024]{1,0:T(8,128)(2,1)} %g_ref.31, bf16[528,256]{1,0:T(8,128)(2,1)S(1)} %collective-permute-done.2.refs_0_, bf16[528,256]{1,0:T(8,128)(2,1)S(1)} %collective-permute-done.3.refs_1_), custom_call_target="tpu_custom_call" | custom-call | bytes 1024 | tf_op jit(solution)/shard_map/pallas_call | solution.py:107
  25.3 2.4 %collective-permute-done.4.refs_0_ = bf16[528,256]{1,0:T(8,128)(2,1)S(1)} collective-permute-done((bf16[528,256]{1,0:T(8,128)(2,1)S(1)}, bf16[528,256]{1,0:T(8,128)(2,1)S(1)}, u32[]{:S(2)}, u32[]{:S(2)}) %collective-permute-start.4) | collective-permute-done | bytes 270368 | tf_op jit(solution)/shard_map/ppermute | solution.py:332
  27.7 2.3 %shard_map.85 = bf16[528,256]{1,0:T(8,128)(2,1)S(1)} custom-call(s32[1]{0:T(128)} %bitcast.place_ref, bf16[8192,1024]{1,0:T(8,128)(2,1)} %w_ref.31, bf16[256,1024]{1,0:T(8,128)(2,1)} %g_ref.31, bf16[528,256]{1,0:T(8,128)(2,1)S(1)} %collective-permute-done.4.refs_0_), custom_call_target="tpu_custom_call" | custom-call | bytes 1024 | tf_op jit(solution)/shard_map/pallas_call | solution.py:107
  30.1 2.3 %shard_map.86 = bf16[528,256]{1,0:T(8,128)(2,1)S(1)} custom-call(s32[1]{0:T(128)} %bitcast.place_ref, bf16[8192,1024]{1,0:T(8,128)(2,1)} %w_ref.31, bf16[256,1024]{1,0:T(8,128)(2,1)} %g_ref.31), custom_call_target="tpu_custom_call" | custom-call | bytes 1024 | tf_op jit(solution)/shard_map/pallas_call | solution.py:107
  32.4 1.3 %collective-permute-start.7 = (bf16[528,256]{1,0:T(8,128)(2,1)S(1)}, bf16[528,256]{1,0:T(8,128)(2,1)S(1)}, u32[]{:S(2)}, u32[]{:S(2)}) collective-permute-start(bf16[528,256]{1,0:T(8,128)(2,1)S(1)} %shard_map.86), channel_id=1, source_target_pairs={{0,1},{1,0},{2,3},{3,2},{4,5},{5,4},{6,7},{7,6},{8,9},{9,8},{10,11... | collective-permute-start | bytes 811016 | tf_op jit(solution)/shard_map/ppermute | solution.py:332
  33.7 0.0 collective-permute-done.5.refs_0_
  33.7 0.0 collective-permute-done.6.refs_1_
  33.7 2.5 %shard_map.87 = bf16[528,256]{1,0:T(8,128)(2,1)S(1)} custom-call(s32[1]{0:T(128)} %bitcast.place_ref, bf16[8192,1024]{1,0:T(8,128)(2,1)} %w_ref.31, bf16[256,1024]{1,0:T(8,128)(2,1)} %g_ref.31, bf16[528,256]{1,0:T(8,128)(2,1)S(1)} %collective-permute-done.5.refs_0_, bf16[528,256]{1,0:T(8,128)(2,1)S(1)} %collective-permute-done.6.refs_1_), custom_call_target="tpu_custom_call" | custom-call | bytes 1024 | tf_op jit(solution)/shard_map/pallas_call | solution.py:107
  36.2 2.3 %shard_map.88 = bf16[528,256]{1,0:T(8,128)(2,1)S(1)} custom-call(s32[1]{0:T(128)} %bitcast.place_ref, bf16[8192,1024]{1,0:T(8,128)(2,1)} %w_ref.31, bf16[256,1024]{1,0:T(8,128)(2,1)} %g_ref.31), custom_call_target="tpu_custom_call" | custom-call | bytes 1024 | tf_op jit(solution)/shard_map/pallas_call | solution.py:107
  38.5 0.0 copy-start
  38.5 1.1 %collective-permute-start.8 = (bf16[528,256]{1,0:T(8,128)(2,1)S(1)}, bf16[528,256]{1,0:T(8,128)(2,1)S(1)}, u32[]{:S(2)}, u32[]{:S(2)}) collective-permute-start(bf16[528,256]{1,0:T(8,128)(2,1)S(1)} %shard_map.88), channel_id=1, source_target_pairs={{0,1},{1,0},{2,3},{3,2},{4,5},{5,4},{6,7},{7,6},{8,9},{9,8},{10,11... | collective-permute-start | bytes 811016 | tf_op jit(solution)/shard_map/ppermute | solution.py:332
  39.6 0.2 collective-permute-start.9
  39.8 0.1 collective-permute-start.10
  39.8 0.0 collective-permute-done.7.refs_0_
  39.9 2.3 %shard_map.89 = bf16[528,256]{1,0:T(8,128)(2,1)S(1)} custom-call(s32[1]{0:T(128)} %bitcast.place_ref, bf16[8192,1024]{1,0:T(8,128)(2,1)} %w_ref.31, bf16[256,1024]{1,0:T(8,128)(2,1)} %g_ref.31, bf16[528,256]{1,0:T(8,128)(2,1)S(1)} %collective-permute-done.7.refs_0_), custom_call_target="tpu_custom_call" | custom-call | bytes 1024 | tf_op jit(solution)/shard_map/pallas_call | solution.py:107
  42.2 2.3 %shard_map.90 = bf16[528,256]{1,0:T(8,128)(2,1)S(1)} custom-call(s32[1]{0:T(128)} %bitcast.place_ref, bf16[8192,1024]{1,0:T(8,128)(2,1)} %w_ref.31, bf16[256,1024]{1,0:T(8,128)(2,1)} %g_ref.31), custom_call_target="tpu_custom_call" | custom-call | bytes 1024 | tf_op jit(solution)/shard_map/pallas_call | solution.py:107
  44.5 0.5 collective-permute-start.11
  45.0 2.3 %collective-permute-start.13 = (bf16[528,256]{1,0:T(8,128)(2,1)S(1)}, bf16[528,256]{1,0:T(8,128)(2,1)S(1)}, u32[]{:S(2)}, u32[]{:S(2)}) collective-permute-start(bf16[528,256]{1,0:T(8,128)(2,1)S(1)} %shard_map.87), channel_id=1, source_target_pairs={{0,4},{1,5},{2,6},{3,7},{4,0},{5,1},{6,2},{7,3},{8,12},{9,13},{10,... | collective-permute-start | bytes 811016 | tf_op jit(solution)/shard_map/ppermute | solution.py:332
  47.3 0.0 collective-permute-done.8.refs_0_
  47.3 1.3 %collective-permute-start.12 = (bf16[528,256]{1,0:T(8,128)(2,1)S(1)}, bf16[528,256]{1,0:T(8,128)(2,1)S(1)}, u32[]{:S(2)}, u32[]{:S(2)}) collective-permute-start(bf16[528,256]{1,0:T(8,128)(2,1)S(1)} %shard_map.89), channel_id=1, source_target_pairs={{0,2},{1,3},{2,0},{3,1},{4,6},{5,7},{6,4},{7,5},{8,10},{9,11},{10,... | collective-permute-start | bytes 811016 | tf_op jit(solution)/shard_map/ppermute | solution.py:332
  48.6 0.0 copy-done
  48.6 0.0 copy-start.1
  48.6 2.2 %shard_map.91.acc_ref = f32[512,256]{1,0:T(8,128)S(1)} custom-call(s32[1]{0:T(128)} %bitcast.place_ref, bf16[8192,1024]{1,0:T(8,128)(2,1)} %w_ref.31, bf16[256,1024]{1,0:T(8,128)(2,1)} %g_ref.31, bf16[528,256]{1,0:T(8,128)(2,1)S(1)} %collective-permute-done.8.refs_0_), custom_call_target="tpu_custom_call" | custom-call | bytes 1024 | tf_op jit(solution)/shard_map/pallas_call | solution.py:107
  50.8 0.5 collective-permute-done.9.refs_0_
  51.3 0.0 collective-permute-done.10.refs_1_
  51.4 2.5 %shard_map.92 = (bf16[256,1024]{1,0:T(8,128)(2,1)}, f32[1024,128]{1,0:T(8,128)S(1)}, f32[16,8,128]{2,1,0:T(8,128)S(1)}, f32[8,8,128]{2,1,0:T(8,128)S(1)}) custom-call(f32[512,256]{1,0:T(8,128)S(1)} %shard_map.91.acc_ref, bf16[528,256]{1,0:T(8,128)(2,1)S(1)} %collective-permute-done.9.refs_0_, bf16[528,256]{1,0:T(8,128)(2,1)S(1)} %collective-permute-done.10.refs_1_, ...), custom_call_target="tpu_custom_call" | custom-call | bytes 1024 | tf_op jit(solution)/shard_map/pallas_call | solution.py:211
  53.9 14.2 %collective-permute-start.17 = (f32[8,8,128]{2,1,0:T(8,128)S(1)}, f32[8,8,128]{2,1,0:T(8,128)S(1)}, u32[]{:S(2)}, u32[]{:S(2)}) collective-permute-start(f32[8,8,128]{2,1,0:T(8,128)S(1)} %get-tuple-element.39), channel_id=1, source_target_pairs={{8,0},{16,8},{24,16},{9,1},{17,9},{25,17},{10,2},{18,10},{26,18},{... | collective-permute-start | bytes 98312 | tf_op jit(solution)/shard_map/ppermute | solution.py:346
  68.1 2.2 %collective-permute-start.18 = (f32[8,8,128]{2,1,0:T(8,128)S(1)}, f32[8,8,128]{2,1,0:T(8,128)S(1)}, u32[]{:S(2)}, u32[]{:S(2)}) collective-permute-start(f32[8,8,128]{2,1,0:T(8,128)S(1)} %get-tuple-element.39), channel_id=1, source_target_pairs={{16,0},{24,8},{17,1},{25,9},{18,2},{26,10},{19,3},{27,11},{20,4},{... | collective-permute-start | bytes 98312 | tf_op jit(solution)/shard_map/ppermute | solution.py:346
  70.3 0.0 collective-permute-done.11.refs_0_
  70.3 1.3 %collective-permute-start.19 = (f32[8,8,128]{2,1,0:T(8,128)S(1)}, f32[8,8,128]{2,1,0:T(8,128)S(1)}, u32[]{:S(2)}, u32[]{:S(2)}) collective-permute-start(f32[8,8,128]{2,1,0:T(8,128)S(1)} %get-tuple-element.39), channel_id=1, source_target_pairs={{24,0},{25,1},{26,2},{27,3},{28,4},{29,5},{30,6},{31,7}} | collective-permute-start | bytes 98312 | tf_op jit(solution)/shard_map/ppermute | solution.py:346
  71.6 2.1 %shard_map.93.acc_ref = f32[512,256]{1,0:T(8,128)S(1)} custom-call(s32[1]{0:T(128)} %bitcast.place_ref, bf16[8192,1024]{1,0:T(8,128)(2,1)} %w_ref.31, bf16[256,1024]{1,0:T(8,128)(2,1)} %g_ref.31, bf16[528,256]{1,0:T(8,128)(2,1)S(1)} %collective-permute-done.11.refs_0_), custom_call_target="tpu_custom_call" | custom-call | bytes 1024 | tf_op jit(solution)/shard_map/pallas_call | solution.py:107
  73.7 0.0 collective-permute-done.13.refs_1_
  73.7 0.0 collective-permute-done.12.refs_0_
  73.7 2.3 %shard_map.94 = (bf16[256,1024]{1,0:T(8,128)(2,1)}, f32[1024,128]{1,0:T(8,128)S(1)}, f32[16,8,128]{2,1,0:T(8,128)S(1)}, f32[8,8,128]{2,1,0:T(8,128)S(1)}) custom-call(f32[512,256]{1,0:T(8,128)S(1)} %shard_map.93.acc_ref, bf16[528,256]{1,0:T(8,128)(2,1)S(1)} %collective-permute-done.12.refs_0_, ...), custom_call_target="tpu_custom_call", output_to_operand_aliasing={{0}: (6, {})} | custom-call | bytes 1024 | tf_op jit(solution)/shard_map/pallas_call | solution.py:211
  76.1 1.3 %collective-permute-start.14 = (f32[8,8,128]{2,1,0:T(8,128)S(1)}, f32[8,8,128]{2,1,0:T(8,128)S(1)}, u32[]{:S(2)}, u32[]{:S(2)}) collective-permute-start(f32[8,8,128]{2,1,0:T(8,128)S(1)} %get-tuple-element.45), channel_id=1, source_target_pairs={{8,0},{16,8},{24,16},{9,1},{17,9},{25,17},{10,2},{18,10},{26,18},{... | collective-permute-start | bytes 98312 | tf_op jit(solution)/shard_map/ppermute | solution.py:346
  77.4 1.3 %collective-permute-start.15 = (f32[8,8,128]{2,1,0:T(8,128)S(1)}, f32[8,8,128]{2,1,0:T(8,128)S(1)}, u32[]{:S(2)}, u32[]{:S(2)}) collective-permute-start(f32[8,8,128]{2,1,0:T(8,128)S(1)} %get-tuple-element.45), channel_id=1, source_target_pairs={{16,0},{24,8},{17,1},{25,9},{18,2},{26,10},{19,3},{27,11},{20,4},{... | collective-permute-start | bytes 98312 | tf_op jit(solution)/shard_map/ppermute | solution.py:346
  78.7 0.0 collective-permute-done.17.refs_0_
  78.7 1.3 %collective-permute-start.16 = (f32[8,8,128]{2,1,0:T(8,128)S(1)}, f32[8,8,128]{2,1,0:T(8,128)S(1)}, u32[]{:S(2)}, u32[]{:S(2)}) collective-permute-start(f32[8,8,128]{2,1,0:T(8,128)S(1)} %get-tuple-element.45), channel_id=1, source_target_pairs={{24,0},{25,1},{26,2},{27,3},{28,4},{29,5},{30,6},{31,7}} | collective-permute-start | bytes 98312 | tf_op jit(solution)/shard_map/ppermute | solution.py:346
  80.0 0.0 copy-done.1
  80.0 0.0 collective-permute-done.18.refs_1_
  80.0 0.0 collective-permute-done.19.refs_2_
  80.1 2.5 %shard_map.95.refs_5_ = bf16[256,1024]{1,0:T(8,128)(2,1)} custom-call(f32[1024,128]{1,0:T(8,128)S(1)} %get-tuple-element.46.gc_ref, f32[16,8,128]{2,1,0:T(8,128)S(1)} %get-tuple-element.47.state_ref, f32[8,8,128]{2,1,0:T(8,128)S(1)} %collective-permute-done.17.refs_0_, f32[8,8,128]{2,1,0:T(8,128)S(1)} %collective-permute-done.18.refs_1_, ...), custom_call_target="tpu_custom_call" | custom-call | bytes 1024 | tf_op jit(solution)/shard_map/pallas_call | solution.py:275
  82.6 0.0 collective-permute-done.14.refs_0_
  82.6 0.0 collective-permute-done.15.refs_1_
  82.6 0.0 collective-permute-done.16.refs_2_
  82.7 2.5 %shard_map.96 = bf16[256,1024]{1,0:T(8,128)(2,1)} custom-call(f32[1024,128]{1,0:T(8,128)S(1)} %get-tuple-element.43.gc_ref, f32[16,8,128]{2,1,0:T(8,128)S(1)} %get-tuple-element.44.state_ref, f32[8,8,128]{2,1,0:T(8,128)S(1)} %collective-permute-done.14.refs_0_, f32[8,8,128]{2,1,0:T(8,128)S(1)} %collective-permute-done.15.refs_1_, ...), custom_call_target="tpu_custom_call", output_to_operand_aliasing={{}: (7, {})} | custom-call | bytes 1024 | tf_op jit(solution)/shard_map/pallas_call | solution.py:275
  (4 shorter events, 0.1 us)
Async XLA Ops:
  2.9 7.5 %collective-permute-start = (bf16[528,256]{1,0:T(8,128)(2,1)S(1)}, bf16[528,256]{1,0:T(8,128)(2,1)S(1)}, u32[]{:S(2)}, u32[]{:S(2)}) collective-permute-start(bf16[528,256]{1,0:T(8,128)(2,1)S(1)} %shard_map.77), channel_id=1, source_target_pairs={{0,1},{1,0},{2,3},{3,2},{4,5},{5,4},{6,7},{7,6},{8,9},{9,8},{10,11... | collective-permute-start | bytes 811016 | tf_op jit(solution)/shard_map/ppermute | solution.py:332
  6.5 10.0 %collective-permute-start.1 = (bf16[528,256]{1,0:T(8,128)(2,1)S(1)}, bf16[528,256]{1,0:T(8,128)(2,1)S(1)}, u32[]{:S(2)}, u32[]{:S(2)}) collective-permute-start(bf16[528,256]{1,0:T(8,128)(2,1)S(1)} %shard_map.78), channel_id=1, source_target_pairs={{0,1},{1,0},{2,3},{3,2},{4,5},{5,4},{6,7},{7,6},{8,9},{9,8},{10,11... | collective-permute-start | bytes 811016 | tf_op jit(solution)/shard_map/ppermute | solution.py:332
  9.1 13.7 %collective-permute-start.2 = (bf16[528,256]{1,0:T(8,128)(2,1)S(1)}, bf16[528,256]{1,0:T(8,128)(2,1)S(1)}, u32[]{:S(2)}, u32[]{:S(2)}) collective-permute-start(bf16[528,256]{1,0:T(8,128)(2,1)S(1)} %shard_map.79), channel_id=1, source_target_pairs={{0,1},{1,0},{2,3},{3,2},{4,5},{5,4},{6,7},{7,6},{8,9},{9,8},{10,11... | collective-permute-start | bytes 811016 | tf_op jit(solution)/shard_map/ppermute | solution.py:332
  12.8 10.1 %collective-permute-start.3 = (bf16[528,256]{1,0:T(8,128)(2,1)S(1)}, bf16[528,256]{1,0:T(8,128)(2,1)S(1)}, u32[]{:S(2)}, u32[]{:S(2)}) collective-permute-start(bf16[528,256]{1,0:T(8,128)(2,1)S(1)} %shard_map.80), channel_id=1, source_target_pairs={{0,2},{1,3},{2,0},{3,1},{4,6},{5,7},{6,4},{7,5},{8,10},{9,11},{10,... | collective-permute-start | bytes 811016 | tf_op jit(solution)/shard_map/ppermute | solution.py:332
  15.3 12.4 %collective-permute-start.4 = (bf16[528,256]{1,0:T(8,128)(2,1)S(1)}, bf16[528,256]{1,0:T(8,128)(2,1)S(1)}, u32[]{:S(2)}, u32[]{:S(2)}) collective-permute-start(bf16[528,256]{1,0:T(8,128)(2,1)S(1)} %shard_map.81), channel_id=1, source_target_pairs={{0,1},{1,0},{2,3},{3,2},{4,5},{5,4},{6,7},{7,6},{8,9},{9,8},{10,11... | collective-permute-start | bytes 811016 | tf_op jit(solution)/shard_map/ppermute | solution.py:332
  21.2 12.5 %collective-permute-start.5 = (bf16[528,256]{1,0:T(8,128)(2,1)S(1)}, bf16[528,256]{1,0:T(8,128)(2,1)S(1)}, u32[]{:S(2)}, u32[]{:S(2)}) collective-permute-start(bf16[528,256]{1,0:T(8,128)(2,1)S(1)} %shard_map.83), channel_id=1, source_target_pairs={{0,1},{1,0},{2,3},{3,2},{4,5},{5,4},{6,7},{7,6},{8,9},{9,8},{10,11... | collective-permute-start | bytes 811016 | tf_op jit(solution)/shard_map/ppermute | solution.py:332
  22.1 11.6 %collective-permute-start.6 = (bf16[528,256]{1,0:T(8,128)(2,1)S(1)}, bf16[528,256]{1,0:T(8,128)(2,1)S(1)}, u32[]{:S(2)}, u32[]{:S(2)}) collective-permute-start(bf16[528,256]{1,0:T(8,128)(2,1)S(1)} %shard_map.82), channel_id=1, source_target_pairs={{0,2},{1,3},{2,0},{3,1},{4,6},{5,7},{6,4},{7,5},{8,10},{9,11},{10,... | collective-permute-start | bytes 811016 | tf_op jit(solution)/shard_map/ppermute | solution.py:332
  32.4 7.5 %collective-permute-start.7 = (bf16[528,256]{1,0:T(8,128)(2,1)S(1)}, bf16[528,256]{1,0:T(8,128)(2,1)S(1)}, u32[]{:S(2)}, u32[]{:S(2)}) collective-permute-start(bf16[528,256]{1,0:T(8,128)(2,1)S(1)} %shard_map.86), channel_id=1, source_target_pairs={{0,1},{1,0},{2,3},{3,2},{4,5},{5,4},{6,7},{7,6},{8,9},{9,8},{10,11... | collective-permute-start | bytes 811016 | tf_op jit(solution)/shard_map/ppermute | solution.py:332
  38.5 10.1 %copy-start = (f32[1024,16]{0,1:T(8,128)S(1)}, f32[1024,16]{0,1:T(8,128)}, u32[]{:S(2)}) copy-start(f32[1024,16]{0,1:T(8,128)} %param.11) | copy-start | bytes 196612
  38.5 8.8 %collective-permute-start.8 = (bf16[528,256]{1,0:T(8,128)(2,1)S(1)}, bf16[528,256]{1,0:T(8,128)(2,1)S(1)}, u32[]{:S(2)}, u32[]{:S(2)}) collective-permute-start(bf16[528,256]{1,0:T(8,128)(2,1)S(1)} %shard_map.88), channel_id=1, source_target_pairs={{0,1},{1,0},{2,3},{3,2},{4,5},{5,4},{6,7},{7,6},{8,9},{9,8},{10,11... | collective-permute-start | bytes 811016 | tf_op jit(solution)/shard_map/ppermute | solution.py:332
  39.6 11.7 %collective-permute-start.9 = (bf16[528,256]{1,0:T(8,128)(2,1)S(1)}, bf16[528,256]{1,0:T(8,128)(2,1)S(1)}, u32[]{:S(2)}, u32[]{:S(2)}) collective-permute-start(bf16[528,256]{1,0:T(8,128)(2,1)S(1)} %shard_map.85), channel_id=1, source_target_pairs={{0,2},{1,3},{2,0},{3,1},{4,6},{5,7},{6,4},{7,5},{8,10},{9,11},{10,... | collective-permute-start | bytes 811016 | tf_op jit(solution)/shard_map/ppermute | solution.py:332
  39.8 11.5 %collective-permute-start.10 = (bf16[528,256]{1,0:T(8,128)(2,1)S(1)}, bf16[528,256]{1,0:T(8,128)(2,1)S(1)}, u32[]{:S(2)}, u32[]{:S(2)}) collective-permute-start(bf16[528,256]{1,0:T(8,128)(2,1)S(1)} %shard_map.84), channel_id=1, source_target_pairs={{0,4},{1,5},{2,6},{3,7},{4,0},{5,1},{6,2},{7,3},{8,12},{9,13},{10,... | collective-permute-start | bytes 811016 | tf_op jit(solution)/shard_map/ppermute | solution.py:332
  44.5 25.8 %collective-permute-start.11 = (bf16[528,256]{1,0:T(8,128)(2,1)S(1)}, bf16[528,256]{1,0:T(8,128)(2,1)S(1)}, u32[]{:S(2)}, u32[]{:S(2)}) collective-permute-start(bf16[528,256]{1,0:T(8,128)(2,1)S(1)} %shard_map.90), channel_id=1, source_target_pairs={{0,1},{1,0},{2,3},{3,2},{4,5},{5,4},{6,7},{7,6},{8,9},{9,8},{10,11... | collective-permute-start | bytes 811016 | tf_op jit(solution)/shard_map/ppermute | solution.py:332
  45.0 28.8 %collective-permute-start.13 = (bf16[528,256]{1,0:T(8,128)(2,1)S(1)}, bf16[528,256]{1,0:T(8,128)(2,1)S(1)}, u32[]{:S(2)}, u32[]{:S(2)}) collective-permute-start(bf16[528,256]{1,0:T(8,128)(2,1)S(1)} %shard_map.87), channel_id=1, source_target_pairs={{0,4},{1,5},{2,6},{3,7},{4,0},{5,1},{6,2},{7,3},{8,12},{9,13},{10,... | collective-permute-start | bytes 811016 | tf_op jit(solution)/shard_map/ppermute | solution.py:332
  47.3 26.5 %collective-permute-start.12 = (bf16[528,256]{1,0:T(8,128)(2,1)S(1)}, bf16[528,256]{1,0:T(8,128)(2,1)S(1)}, u32[]{:S(2)}, u32[]{:S(2)}) collective-permute-start(bf16[528,256]{1,0:T(8,128)(2,1)S(1)} %shard_map.89), channel_id=1, source_target_pairs={{0,2},{1,3},{2,0},{3,1},{4,6},{5,7},{6,4},{7,5},{8,10},{9,11},{10,... | collective-permute-start | bytes 811016 | tf_op jit(solution)/shard_map/ppermute | solution.py:332
  48.6 31.4 %copy-start.1 = (f32[1024,16]{0,1:T(8,128)S(1)}, f32[1024,16]{0,1:T(8,128)}, u32[]{:S(2)}) copy-start(f32[1024,16]{0,1:T(8,128)} %param.10) | copy-start | bytes 196612
  53.9 24.8 %collective-permute-start.17 = (f32[8,8,128]{2,1,0:T(8,128)S(1)}, f32[8,8,128]{2,1,0:T(8,128)S(1)}, u32[]{:S(2)}, u32[]{:S(2)}) collective-permute-start(f32[8,8,128]{2,1,0:T(8,128)S(1)} %get-tuple-element.39), channel_id=1, source_target_pairs={{8,0},{16,8},{24,16},{9,1},{17,9},{25,17},{10,2},{18,10},{26,18},{... | collective-permute-start | bytes 98312 | tf_op jit(solution)/shard_map/ppermute | solution.py:346
  68.1 11.9 %collective-permute-start.18 = (f32[8,8,128]{2,1,0:T(8,128)S(1)}, f32[8,8,128]{2,1,0:T(8,128)S(1)}, u32[]{:S(2)}, u32[]{:S(2)}) collective-permute-start(f32[8,8,128]{2,1,0:T(8,128)S(1)} %get-tuple-element.39), channel_id=1, source_target_pairs={{16,0},{24,8},{17,1},{25,9},{18,2},{26,10},{19,3},{27,11},{20,4},{... | collective-permute-start | bytes 98312 | tf_op jit(solution)/shard_map/ppermute | solution.py:346
  70.3 9.8 %collective-permute-start.19 = (f32[8,8,128]{2,1,0:T(8,128)S(1)}, f32[8,8,128]{2,1,0:T(8,128)S(1)}, u32[]{:S(2)}, u32[]{:S(2)}) collective-permute-start(f32[8,8,128]{2,1,0:T(8,128)S(1)} %get-tuple-element.39), channel_id=1, source_target_pairs={{24,0},{25,1},{26,2},{27,3},{28,4},{29,5},{30,6},{31,7}} | collective-permute-start | bytes 98312 | tf_op jit(solution)/shard_map/ppermute | solution.py:346
  76.1 6.5 %collective-permute-start.14 = (f32[8,8,128]{2,1,0:T(8,128)S(1)}, f32[8,8,128]{2,1,0:T(8,128)S(1)}, u32[]{:S(2)}, u32[]{:S(2)}) collective-permute-start(f32[8,8,128]{2,1,0:T(8,128)S(1)} %get-tuple-element.45), channel_id=1, source_target_pairs={{8,0},{16,8},{24,16},{9,1},{17,9},{25,17},{10,2},{18,10},{26,18},{... | collective-permute-start | bytes 98312 | tf_op jit(solution)/shard_map/ppermute | solution.py:346
  77.4 5.3 %collective-permute-start.15 = (f32[8,8,128]{2,1,0:T(8,128)S(1)}, f32[8,8,128]{2,1,0:T(8,128)S(1)}, u32[]{:S(2)}, u32[]{:S(2)}) collective-permute-start(f32[8,8,128]{2,1,0:T(8,128)S(1)} %get-tuple-element.45), channel_id=1, source_target_pairs={{16,0},{24,8},{17,1},{25,9},{18,2},{26,10},{19,3},{27,11},{20,4},{... | collective-permute-start | bytes 98312 | tf_op jit(solution)/shard_map/ppermute | solution.py:346
  78.7 4.0 %collective-permute-start.16 = (f32[8,8,128]{2,1,0:T(8,128)S(1)}, f32[8,8,128]{2,1,0:T(8,128)S(1)}, u32[]{:S(2)}, u32[]{:S(2)}) collective-permute-start(f32[8,8,128]{2,1,0:T(8,128)S(1)} %get-tuple-element.45), channel_id=1, source_target_pairs={{24,0},{25,1},{26,2},{27,3},{28,4},{29,5},{30,6},{31,7}} | collective-permute-start | bytes 98312 | tf_op jit(solution)/shard_map/ppermute | solution.py:346

commit v3 on v2

--- a/solution.py
+++ b/solution.py
@@ -53,70 +53,87 @@
     return pltpu.with_memory_space_constraint(array, pltpu.HBM)
 
 
-def send_kernel(rows, starts, sources, coded, near, place_ref, w_ref, g_ref, *refs):
-    near_refs, (out_ref, w_buf, g_buf, sems) = refs[:near], refs[near:]
+def send_kernel(rows, block, offset, width, sources, coded, place_ref, w_ref, turned_ref, *refs):
+    near_refs, out_ref = refs[:sources], refs[sources]
     step = min(rows, STEP)
-    place = place_ref[0]
-    grad = pltpu.make_async_copy(g_ref, g_buf, sems.at[0])
-    grad.start()
-    copies = []
-    for i, (block, offset, width) in enumerate(starts):
-        first = pl.multiple_of((place ^ block) * width + offset, 16)
-        for at in range(0, rows, step):
-            copy = pltpu.make_async_copy(
-                w_ref.at[pl.ds(first + at, step), :],
-                w_buf.at[pl.ds(i * rows + at, step), :],
-                sems.at[1 + len(copies)],
-            )
-            copy.start()
-            copies.append(copy)
-    grad.wait()
+    first = (place_ref[0] ^ block) * width + offset
     part = part_of(rows)
-    stride = rows + PEAKS if coded else rows
-    copies = iter(copies)
-    for i in range(len(starts)):
-        peaks = []
-        for at in range(0, rows, step):
-            next(copies).wait()
-            block = lax.dot_general(
-                w_buf[i * rows + at : i * rows + at + step, :],
-                g_buf[...],
-                (((1,), (1,)), ((), ())),
-                preferred_element_type=jnp.float32,
-            )
-            for source, base in sources[i]:
-                block = block + decode(near_refs[source], base, rows, at, step)
-            if coded:
-                block, more = encode(block, part)
-                peaks += more
-            out_ref[i * stride + at : i * stride + at + step, :] = block
+    peaks = []
+    for at in range(0, rows, step):
+        total = jnp.dot(
+            w_ref[pl.ds(pl.multiple_of(first + at, 16), step), :], turned_ref[...], preferred_element_type=jnp.float32
+        )
+        for near_ref in near_refs:
+            total = total + decode(near_ref, 0, rows, at, step)
         if coded:
-            toks = block.shape[1]
-            if len(peaks) < PEAKS:
-                peaks.append(jnp.zeros((PEAKS - len(peaks), toks), jnp.float32))
-            out_ref[i * stride + rows : (i + 1) * stride, :] = jnp.concatenate(peaks, axis=0).astype(jnp.bfloat16)
-
-
-def send(rows, starts, sources, coded, place, weight, grad, nears):
+            total, more = encode(total, part)
+            peaks += more
+        out_ref[at : at + step, :] = total
+    if coded:
+        if len(peaks) < PEAKS:
+            peaks.append(jnp.zeros((PEAKS - len(peaks), total.shape[1]), jnp.float32))
+        out_ref[rows:, :] = jnp.concatenate(peaks, axis=0).astype(jnp.bfloat16)
+
+
+def send(rows, block, offset, width, coded, place, weight, turned, nears):
+    toks = turned.shape[1]
+    vmem = pl.BlockSpec(memory_space=pltpu.VMEM)
+    count = rows + PEAKS if coded else rows
+    return pl.pallas_call(
+        functools.partial(send_kernel, rows, block, offset, width, len(nears), coded),
+        in_specs=[pl.BlockSpec(memory_space=pltpu.SMEM)] + [vmem] * (2 + len(nears)),
+        out_specs=vmem,
+        out_shape=jax.ShapeDtypeStruct((count, toks), jnp.bfloat16 if coded else jnp.float32),
+        compiler_params=pltpu.CompilerParams(vmem_limit_bytes=VMEM),
+        cost_estimate=QUICK,
+    )(place, weight, turned, *nears)
+
+
+def first_kernel(rows, block, offset, width, place_ref, w_hbm, g_hbm, out_ref, turned_ref, w_ref, g_ref, sems):
+    step = min(rows, STEP)
+    first = pl.multiple_of((place_ref[0] ^ block) * width + offset, 16)
+    copies = [pltpu.make_async_copy(g_hbm, g_ref, sems.at[0])]
+    for i, at in enumerate(range(0, rows, step)):
+        copies.append(
+            pltpu.make_async_copy(w_hbm.at[pl.ds(first + at, step), :], w_ref.at[pl.ds(at, step), :], sems.at[1 + i])
+        )
+    for copy in copies:
+        copy.start()
+    copies[0].wait()
+    turned_ref[...] = g_ref[...].T
+    part = part_of(rows)
+    peaks = []
+    for i, at in enumerate(range(0, rows, step)):
+        copies[1 + i].wait()
+        total = jnp.dot(w_ref[at : at + step, :], turned_ref[...], preferred_element_type=jnp.float32)
+        total, more = encode(total, part)
+        peaks += more
+        out_ref[at : at + step, :] = total
+    if len(peaks) < PEAKS:
+        peaks.append(jnp.zeros((PEAKS - len(peaks), total.shape[1]), jnp.float32))
+    out_ref[rows:, :] = jnp.concatenate(peaks, axis=0).astype(jnp.bfloat16)
+
+
+def first_send(rows, block, offset, width, place, weight, grad):
     toks, depth = grad.shape
     vmem = pl.BlockSpec(memory_space=pltpu.VMEM)
     high = pl.BlockSpec(memory_space=pltpu.HBM)
-    count = len(starts) * (rows + PEAKS if coded else rows)
-    steps = len(starts) * (rows // min(rows, STEP))
-    work = len(starts) * rows
     return pl.pallas_call(
-        functools.partial(send_kernel, rows, starts, sources, coded, len(nears)),
-        in_specs=[pl.BlockSpec(memory_space=pltpu.SMEM), high, high] + [vmem] * len(nears),
-        out_specs=vmem,
-        out_shape=jax.ShapeDtypeStruct((count, toks), jnp.bfloat16 if coded else jnp.float32),
+        functools.partial(first_kernel, rows, block, offset, width),
+        in_specs=[pl.BlockSpec(memory_space=pltpu.SMEM), high, high],
+        out_specs=(vmem, vmem),
+        out_shape=(
+            jax.ShapeDtypeStruct((rows + PEAKS, toks), jnp.bfloat16),
+            jax.ShapeDtypeStruct((depth, toks), jnp.bfloat16),
+        ),
         scratch_shapes=[
-            pltpu.VMEM((work, depth), jnp.bfloat16),
+            pltpu.VMEM((rows, depth), jnp.bfloat16),
             pltpu.VMEM((toks, depth), jnp.bfloat16),
-            pltpu.SemaphoreType.DMA((steps + 1,)),
+            pltpu.SemaphoreType.DMA((1 + rows // min(rows, STEP),)),
         ],
         compiler_params=pltpu.CompilerParams(vmem_limit_bytes=VMEM),
         cost_estimate=QUICK,
-    )(place, pinned(weight), pinned(grad), *nears)
+    )(place, pinned(weight), pinned(grad))
 
 
 def steps_back(count, body, state, unroll):
@@ -318,25 +335,17 @@
 
     for p, s, block in order:
         bit = bits[s]
-        nears = [received[p, i, block ^ bit] for i in range(s)]
-        last = send(
-            rows,
-            ((block ^ bit, p * rows, width),),
-            (tuple((i, 0) for i in range(s)),),
-            True,
-            after(place),
-            out_weight,
-            out_grad,
-            nears,
-        )
+        if last is None:
+            last, turned = first_send(rows, block ^ bit, p * rows, width, place, out_weight, out_grad)
+        else:
+            nears = [received[p, i, block ^ bit] for i in range(s)]
+            last = send(rows, block ^ bit, p * rows, width, True, after(place), out_weight, turned, nears)
         received[p, s, block] = lax.ppermute(last, "ch", [(i, i ^ bit) for i in range(size)])
 
     states = []
     grad_query = grad_input = None
     for p in range(2):
-        acc = send(
-            rows, ((0, p * rows, width),), (((0, 0),),), False, after(place), out_weight, out_grad, [received[p, 0, 0]]
-        )
+        acc = send(rows, 0, p * rows, width, False, after(place), out_weight, turned, [received[p, 0, 0]])
         fars = [received[p, s, 0] for s in range(1, len(bits))]
         grad_query, grad_conv, state, packed = gate(
             p, rows, segments, acc, fars, query_in, conv_out, decay, grad_query

time: 86 us -> 82.5 us (0.959)
  the two profiles are of different devices: /device:TPU:27 before, /device:TPU:0 now
where the time goes in v3:
time: 82.5 us; the launch traced here: 82.3 us
  starting transfers between devices  34.2 us (41%)
  waiting for transfers between devices  23.8 us (29%)
  Pallas kernels  22.3 us (27%)
  between operations  0.96 us (1%)
  local copies, waits for them, and re-layouts  0.93 us (1%)
    ppermute x14, starting transfers between devices, local(): lax.ppermute(last, 'ch', [(i, i ^ bit) for i in range(size)])  26.5 us
    ppermute x14, waiting for transfers between devices, local(): lax.ppermute(last, 'ch', [(i, i ^ bit) for i in range(size)])  21.8 us
    pallas_call x15, Pallas kernels, send(): pl.pallas_call(functools.partial(send_kernel, rows, block, offset, width,...  10.2 us
    ppermute x6, starting transfers between devices, local(): lax.ppermute(packed, 'ctx', [(i, i - hop) for i in range(hop, groups)])  7.75 us
    pallas_call x2, Pallas kernels, scan(): pl.pallas_call(functools.partial(scan_kernel, portion, segments, len(late...  5.04 us
    pallas_call x2, Pallas kernels, gate(): pl.pallas_call(functools.partial(gate_kernel, portion, rows, segments, (0...  4.69 us
    pallas_call x1, Pallas kernels, first_send(): pl.pallas_call(functools.partial(first_kernel, rows, block, offset, width...  2.4 us
    ppermute x6, waiting for transfers between devices, local(): lax.ppermute(packed, 'ctx', [(i, i - hop) for i in range(hop, groups)])  2.03 us
  transfers between devices with their start and end apart: 20, of which 9 were waited for; matrix products, arithmetic and copies ran while one was open for 0% of the time, Pallas kernels for 21%

profile of v3, /device:TPU:0, one launch (start us, length us, event | category | flops | bytes accessed | tf_op | source)
XLA Modules:
  0.0 82.3 jit_solution(2467563548030634637)
XLA Ops:
  0.6 2.4 %shard_map.77 = (bf16[528,256]{1,0:T(8,128)(2,1)S(1)}, bf16[1024,256]{1,0:T(8,128)(2,1)S(1)}) custom-call(s32[1]{0:T(128)} %bitcast.place_ref, bf16[8192,1024]{1,0:T(8,128)(2,1)} %w_ref.29, bf16[256,1024]{1,0:T(8,128)(2,1)} %g_hbm.1), custom_call_target="tpu_custom_call" | custom-call | bytes 1024 | tf_op jit(solution)/shard_map/pallas_call | solution.py:121
  3.0 3.0 %collective-permute-start = (bf16[528,256]{1,0:T(8,128)(2,1)S(1)}, bf16[528,256]{1,0:T(8,128)(2,1)S(1)}, u32[]{:S(2)}, u32[]{:S(2)}) collective-permute-start(bf16[528,256]{1,0:T(8,128)(2,1)S(1)} %get-tuple-element.27), channel_id=1, source_target_pairs={{0,1},{1,0},{2,3},{3,2},{4,5},{5,4},{6,7},{7,6},{8,9},{9,8},{10,11... | collective-permute-start | bytes 811016 | tf_op jit(solution)/shard_map/ppermute | solution.py:343
  6.1 0.8 copy-done
  6.9 0.6 shard_map.78
  7.5 3.0 %collective-permute-start.1 = (bf16[528,256]{1,0:T(8,128)(2,1)S(1)}, bf16[528,256]{1,0:T(8,128)(2,1)S(1)}, u32[]{:S(2)}, u32[]{:S(2)}) collective-permute-start(bf16[528,256]{1,0:T(8,128)(2,1)S(1)} %shard_map.78), channel_id=1, source_target_pairs={{0,1},{1,0},{2,3},{3,2},{4,5},{5,4},{6,7},{7,6},{8,9},{9,8},{10,11... | collective-permute-start | bytes 811016 | tf_op jit(solution)/shard_map/ppermute | solution.py:343
  10.5 0.6 shard_map.79
  11.2 0.1 collective-permute-start.2
  11.3 2.1 %collective-permute-done.refs_0_ = bf16[528,256]{1,0:T(8,128)(2,1)S(1)} collective-permute-done((bf16[528,256]{1,0:T(8,128)(2,1)S(1)}, bf16[528,256]{1,0:T(8,128)(2,1)S(1)}, u32[]{:S(2)}, u32[]{:S(2)}) %collective-permute-start) | collective-permute-done | bytes 270368 | tf_op jit(solution)/shard_map/ppermute | solution.py:343
  13.4 0.7 shard_map.80
  14.1 2.2 %collective-permute-start.3 = (bf16[528,256]{1,0:T(8,128)(2,1)S(1)}, bf16[528,256]{1,0:T(8,128)(2,1)S(1)}, u32[]{:S(2)}, u32[]{:S(2)}) collective-permute-start(bf16[528,256]{1,0:T(8,128)(2,1)S(1)} %shard_map.80), channel_id=1, source_target_pairs={{0,2},{1,3},{2,0},{3,1},{4,6},{5,7},{6,4},{7,5},{8,10},{9,11},{10,... | collective-permute-start | bytes 811016 | tf_op jit(solution)/shard_map/ppermute | solution.py:343
  16.3 0.6 shard_map.81
  17.0 1.6 %collective-permute-start.4 = (bf16[528,256]{1,0:T(8,128)(2,1)S(1)}, bf16[528,256]{1,0:T(8,128)(2,1)S(1)}, u32[]{:S(2)}, u32[]{:S(2)}) collective-permute-start(bf16[528,256]{1,0:T(8,128)(2,1)S(1)} %shard_map.81), channel_id=1, source_target_pairs={{0,1},{1,0},{2,3},{3,2},{4,5},{5,4},{6,7},{7,6},{8,9},{9,8},{10,11... | collective-permute-start | bytes 811016 | tf_op jit(solution)/shard_map/ppermute | solution.py:343
  18.5 0.6 collective-permute-done.1.refs_0_
  19.2 0.7 shard_map.82
  19.9 0.6 shard_map.83
  20.6 2.1 %collective-permute-start.5 = (bf16[528,256]{1,0:T(8,128)(2,1)S(1)}, bf16[528,256]{1,0:T(8,128)(2,1)S(1)}, u32[]{:S(2)}, u32[]{:S(2)}) collective-permute-start(bf16[528,256]{1,0:T(8,128)(2,1)S(1)} %shard_map.83), channel_id=1, source_target_pairs={{0,1},{1,0},{2,3},{3,2},{4,5},{5,4},{6,7},{7,6},{8,9},{9,8},{10,11... | collective-permute-start | bytes 811016 | tf_op jit(solution)/shard_map/ppermute | solution.py:343
  22.7 1.6 %collective-permute-start.6 = (bf16[528,256]{1,0:T(8,128)(2,1)S(1)}, bf16[528,256]{1,0:T(8,128)(2,1)S(1)}, u32[]{:S(2)}, u32[]{:S(2)}) collective-permute-start(bf16[528,256]{1,0:T(8,128)(2,1)S(1)} %shard_map.82), channel_id=1, source_target_pairs={{0,2},{1,3},{2,0},{3,1},{4,6},{5,7},{6,4},{7,5},{8,10},{9,11},{10,... | collective-permute-start | bytes 811016 | tf_op jit(solution)/shard_map/ppermute | solution.py:343
  24.3 0.7 collective-permute-done.2.refs_0_
  25.0 0.0 collective-permute-done.3.refs_1_
  25.0 0.9 %shard_map.84 = bf16[528,256]{1,0:T(8,128)(2,1)S(1)} custom-call(s32[1]{0:T(128)} %bitcast.place_ref, bf16[8192,1024]{1,0:T(8,128)(2,1)S(1)} %copy-done, bf16[1024,256]{1,0:T(8,128)(2,1)S(1)} %get-tuple-element.29.turned_ref, bf16[528,256]{1,0:T(8,128)(2,1)S(1)} %collective-permute-done.2.refs_0_, bf16[528,256]{1,0:T(8,128)(2,1)S(1)} %collective-permute-done.3.refs_1_), custom_call_target="tpu_custom_call" | custom-call | bytes 1024 | tf_op jit(solution)/shard_map/pallas_call | solution.py:82
  25.9 4.9 %collective-permute-done.4.refs_0_ = bf16[528,256]{1,0:T(8,128)(2,1)S(1)} collective-permute-done((bf16[528,256]{1,0:T(8,128)(2,1)S(1)}, bf16[528,256]{1,0:T(8,128)(2,1)S(1)}, u32[]{:S(2)}, u32[]{:S(2)}) %collective-permute-start.4) | collective-permute-done | bytes 270368 | tf_op jit(solution)/shard_map/ppermute | solution.py:343
  30.8 0.7 shard_map.85
  31.5 0.6 shard_map.86
  32.2 2.1 %collective-permute-start.7 = (bf16[528,256]{1,0:T(8,128)(2,1)S(1)}, bf16[528,256]{1,0:T(8,128)(2,1)S(1)}, u32[]{:S(2)}, u32[]{:S(2)}) collective-permute-start(bf16[528,256]{1,0:T(8,128)(2,1)S(1)} %shard_map.86), channel_id=1, source_target_pairs={{0,1},{1,0},{2,3},{3,2},{4,5},{5,4},{6,7},{7,6},{8,9},{9,8},{10,11... | collective-permute-start | bytes 811016 | tf_op jit(solution)/shard_map/ppermute | solution.py:343
  34.3 2.3 %collective-permute-done.5.refs_0_ = bf16[528,256]{1,0:T(8,128)(2,1)S(1)} collective-permute-done((bf16[528,256]{1,0:T(8,128)(2,1)S(1)}, bf16[528,256]{1,0:T(8,128)(2,1)S(1)}, u32[]{:S(2)}, u32[]{:S(2)}) %collective-permute-start.5) | collective-permute-done | bytes 270368 | tf_op jit(solution)/shard_map/ppermute | solution.py:343
  36.6 0.0 collective-permute-done.6.refs_1_
  36.6 0.9 %shard_map.87 = bf16[528,256]{1,0:T(8,128)(2,1)S(1)} custom-call(s32[1]{0:T(128)} %bitcast.place_ref, bf16[8192,1024]{1,0:T(8,128)(2,1)S(1)} %copy-done, bf16[1024,256]{1,0:T(8,128)(2,1)S(1)} %get-tuple-element.29.turned_ref, bf16[528,256]{1,0:T(8,128)(2,1)S(1)} %collective-permute-done.5.refs_0_, bf16[528,256]{1,0:T(8,128)(2,1)S(1)} %collective-permute-done.6.refs_1_), custom_call_target="tpu_custom_call" | custom-call | bytes 1024 | tf_op jit(solution)/shard_map/pallas_call | solution.py:82
  37.5 0.6 shard_map.88
  38.1 0.0 copy-start.1
  38.1 2.1 %collective-permute-start.8 = (bf16[528,256]{1,0:T(8,128)(2,1)S(1)}, bf16[528,256]{1,0:T(8,128)(2,1)S(1)}, u32[]{:S(2)}, u32[]{:S(2)}) collective-permute-start(bf16[528,256]{1,0:T(8,128)(2,1)S(1)} %shard_map.88), channel_id=1, source_target_pairs={{0,1},{1,0},{2,3},{3,2},{4,5},{5,4},{6,7},{7,6},{8,9},{9,8},{10,11... | collective-permute-start | bytes 811016 | tf_op jit(solution)/shard_map/ppermute | solution.py:343
  40.3 1.6 %collective-permute-start.9 = (bf16[528,256]{1,0:T(8,128)(2,1)S(1)}, bf16[528,256]{1,0:T(8,128)(2,1)S(1)}, u32[]{:S(2)}, u32[]{:S(2)}) collective-permute-start(bf16[528,256]{1,0:T(8,128)(2,1)S(1)} %shard_map.85), channel_id=1, source_target_pairs={{0,2},{1,3},{2,0},{3,1},{4,6},{5,7},{6,4},{7,5},{8,10},{9,11},{10,... | collective-permute-start | bytes 811016 | tf_op jit(solution)/shard_map/ppermute | solution.py:343
  41.9 2.6 %collective-permute-start.10 = (bf16[528,256]{1,0:T(8,128)(2,1)S(1)}, bf16[528,256]{1,0:T(8,128)(2,1)S(1)}, u32[]{:S(2)}, u32[]{:S(2)}) collective-permute-start(bf16[528,256]{1,0:T(8,128)(2,1)S(1)} %shard_map.84), channel_id=1, source_target_pairs={{0,4},{1,5},{2,6},{3,7},{4,0},{5,1},{6,2},{7,3},{8,12},{9,13},{10,... | collective-permute-start | bytes 811016 | tf_op jit(solution)/shard_map/ppermute | solution.py:343
  44.4 0.0 collective-permute-done.7.refs_0_
  44.4 0.7 shard_map.89
  45.2 0.6 shard_map.90
  45.8 0.6 collective-permute-start.11
  46.4 2.1 %collective-permute-start.13 = (bf16[528,256]{1,0:T(8,128)(2,1)S(1)}, bf16[528,256]{1,0:T(8,128)(2,1)S(1)}, u32[]{:S(2)}, u32[]{:S(2)}) collective-permute-start(bf16[528,256]{1,0:T(8,128)(2,1)S(1)} %shard_map.87), channel_id=1, source_target_pairs={{0,4},{1,5},{2,6},{3,7},{4,0},{5,1},{6,2},{7,3},{8,12},{9,13},{10,... | collective-permute-start | bytes 811016 | tf_op jit(solution)/shard_map/ppermute | solution.py:343
  48.5 0.0 collective-permute-done.8.refs_0_
  48.5 1.8 %collective-permute-start.12 = (bf16[528,256]{1,0:T(8,128)(2,1)S(1)}, bf16[528,256]{1,0:T(8,128)(2,1)S(1)}, u32[]{:S(2)}, u32[]{:S(2)}) collective-permute-start(bf16[528,256]{1,0:T(8,128)(2,1)S(1)} %shard_map.89), channel_id=1, source_target_pairs={{0,2},{1,3},{2,0},{3,1},{4,6},{5,7},{6,4},{7,5},{8,10},{9,11},{10,... | collective-permute-start | bytes 811016 | tf_op jit(solution)/shard_map/ppermute | solution.py:343
  50.3 0.0 copy-done.1
  50.3 0.0 copy-start.2
  50.3 0.5 shard_map.91.acc_ref
  50.8 2.2 %collective-permute-done.9.refs_0_ = bf16[528,256]{1,0:T(8,128)(2,1)S(1)} collective-permute-done((bf16[528,256]{1,0:T(8,128)(2,1)S(1)}, bf16[528,256]{1,0:T(8,128)(2,1)S(1)}, u32[]{:S(2)}, u32[]{:S(2)}) %collective-permute-start.9) | collective-permute-done | bytes 270368 | tf_op jit(solution)/shard_map/ppermute | solution.py:343
  53.0 9.0 %collective-permute-done.10.refs_1_ = bf16[528,256]{1,0:T(8,128)(2,1)S(1)} collective-permute-done((bf16[528,256]{1,0:T(8,128)(2,1)S(1)}, bf16[528,256]{1,0:T(8,128)(2,1)S(1)}, u32[]{:S(2)}, u32[]{:S(2)}) %collective-permute-start.10) | collective-permute-done | bytes 270368 | tf_op jit(solution)/shard_map/ppermute | solution.py:343
  62.0 2.3 %shard_map.92 = (bf16[256,1024]{1,0:T(8,128)(2,1)}, f32[1024,128]{1,0:T(8,128)S(1)}, f32[16,8,128]{2,1,0:T(8,128)S(1)}, f32[8,8,128]{2,1,0:T(8,128)S(1)}) custom-call(f32[512,256]{1,0:T(8,128)S(1)} %shard_map.91.acc_ref, bf16[528,256]{1,0:T(8,128)(2,1)S(1)} %collective-permute-done.9.refs_0_, bf16[528,256]{1,0:T(8,128)(2,1)S(1)} %collective-permute-done.10.refs_1_, ...), custom_call_target="tpu_custom_call" | custom-call | bytes 1024 | tf_op jit(solution)/shard_map/pallas_call | solution.py:228
  64.4 1.3 %collective-permute-start.17 = (f32[8,8,128]{2,1,0:T(8,128)S(1)}, f32[8,8,128]{2,1,0:T(8,128)S(1)}, u32[]{:S(2)}, u32[]{:S(2)}) collective-permute-start(f32[8,8,128]{2,1,0:T(8,128)S(1)} %get-tuple-element.43), channel_id=1, source_target_pairs={{8,0},{16,8},{24,16},{9,1},{17,9},{25,17},{10,2},{18,10},{26,18},{... | collective-permute-start | bytes 98312 | tf_op jit(solution)/shard_map/ppermute | solution.py:355
  65.7 1.3 %collective-permute-start.18 = (f32[8,8,128]{2,1,0:T(8,128)S(1)}, f32[8,8,128]{2,1,0:T(8,128)S(1)}, u32[]{:S(2)}, u32[]{:S(2)}) collective-permute-start(f32[8,8,128]{2,1,0:T(8,128)S(1)} %get-tuple-element.43), channel_id=1, source_target_pairs={{16,0},{24,8},{17,1},{25,9},{18,2},{26,10},{19,3},{27,11},{20,4},{... | collective-permute-start | bytes 98312 | tf_op jit(solution)/shard_map/ppermute | solution.py:355
  67.0 0.0 collective-permute-done.11.refs_0_
  67.0 1.3 %collective-permute-start.19 = (f32[8,8,128]{2,1,0:T(8,128)S(1)}, f32[8,8,128]{2,1,0:T(8,128)S(1)}, u32[]{:S(2)}, u32[]{:S(2)}) collective-permute-start(f32[8,8,128]{2,1,0:T(8,128)S(1)} %get-tuple-element.43), channel_id=1, source_target_pairs={{24,0},{25,1},{26,2},{27,3},{28,4},{29,5},{30,6},{31,7}} | collective-permute-start | bytes 98312 | tf_op jit(solution)/shard_map/ppermute | solution.py:355
  68.3 0.5 shard_map.93.acc_ref
  68.8 0.0 collective-permute-done.13.refs_1_
  68.8 0.0 collective-permute-done.12.refs_0_
  68.8 2.3 %shard_map.94 = (bf16[256,1024]{1,0:T(8,128)(2,1)}, f32[1024,128]{1,0:T(8,128)S(1)}, f32[16,8,128]{2,1,0:T(8,128)S(1)}, f32[8,8,128]{2,1,0:T(8,128)S(1)}) custom-call(f32[512,256]{1,0:T(8,128)S(1)} %shard_map.93.acc_ref, bf16[528,256]{1,0:T(8,128)(2,1)S(1)} %collective-permute-done.12.refs_0_, ...), custom_call_target="tpu_custom_call", output_to_operand_aliasing={{0}: (6, {})} | custom-call | bytes 1024 | tf_op jit(solution)/shard_map/pallas_call | solution.py:228
  71.2 1.3 %collective-permute-start.14 = (f32[8,8,128]{2,1,0:T(8,128)S(1)}, f32[8,8,128]{2,1,0:T(8,128)S(1)}, u32[]{:S(2)}, u32[]{:S(2)}) collective-permute-start(f32[8,8,128]{2,1,0:T(8,128)S(1)} %get-tuple-element.49), channel_id=1, source_target_pairs={{8,0},{16,8},{24,16},{9,1},{17,9},{25,17},{10,2},{18,10},{26,18},{... | collective-permute-start | bytes 98312 | tf_op jit(solution)/shard_map/ppermute | solution.py:355
  72.5 1.3 %collective-permute-start.15 = (f32[8,8,128]{2,1,0:T(8,128)S(1)}, f32[8,8,128]{2,1,0:T(8,128)S(1)}, u32[]{:S(2)}, u32[]{:S(2)}) collective-permute-start(f32[8,8,128]{2,1,0:T(8,128)S(1)} %get-tuple-element.49), channel_id=1, source_target_pairs={{16,0},{24,8},{17,1},{25,9},{18,2},{26,10},{19,3},{27,11},{20,4},{... | collective-permute-start | bytes 98312 | tf_op jit(solution)/shard_map/ppermute | solution.py:355
  73.8 0.0 collective-permute-done.17.refs_0_
  73.8 1.3 %collective-permute-start.16 = (f32[8,8,128]{2,1,0:T(8,128)S(1)}, f32[8,8,128]{2,1,0:T(8,128)S(1)}, u32[]{:S(2)}, u32[]{:S(2)}) collective-permute-start(f32[8,8,128]{2,1,0:T(8,128)S(1)} %get-tuple-element.49), channel_id=1, source_target_pairs={{24,0},{25,1},{26,2},{27,3},{28,4},{29,5},{30,6},{31,7}} | collective-permute-start | bytes 98312 | tf_op jit(solution)/shard_map/ppermute | solution.py:355
  75.1 0.0 collective-permute-done.18.refs_1_
  75.1 0.0 collective-permute-done.19.refs_2_
  75.2 2.5 %shard_map.95.refs_5_ = bf16[256,1024]{1,0:T(8,128)(2,1)} custom-call(f32[1024,128]{1,0:T(8,128)S(1)} %get-tuple-element.50.gc_ref, f32[16,8,128]{2,1,0:T(8,128)S(1)} %get-tuple-element.51.state_ref, f32[8,8,128]{2,1,0:T(8,128)S(1)} %collective-permute-done.17.refs_0_, f32[8,8,128]{2,1,0:T(8,128)S(1)} %collective-permute-done.18.refs_1_, ...), custom_call_target="tpu_custom_call" | custom-call | bytes 1024 | tf_op jit(solution)/shard_map/pallas_call | solution.py:292
  77.7 0.0 collective-permute-done.14.refs_0_
  77.7 1.0 %collective-permute-done.15.refs_1_ = f32[8,8,128]{2,1,0:T(8,128)S(1)} collective-permute-done((f32[8,8,128]{2,1,0:T(8,128)S(1)}, f32[8,8,128]{2,1,0:T(8,128)S(1)}, u32[]{:S(2)}, u32[]{:S(2)}) %collective-permute-start.15) | collective-permute-done | bytes 32800 | tf_op jit(solution)/shard_map/ppermute | solution.py:355
  78.7 1.1 %collective-permute-done.16.refs_2_ = f32[8,8,128]{2,1,0:T(8,128)S(1)} collective-permute-done((f32[8,8,128]{2,1,0:T(8,128)S(1)}, f32[8,8,128]{2,1,0:T(8,128)S(1)}, u32[]{:S(2)}, u32[]{:S(2)}) %collective-permute-start.16) | collective-permute-done | bytes 32800 | tf_op jit(solution)/shard_map/ppermute | solution.py:355
  79.7 2.5 %shard_map.96 = bf16[256,1024]{1,0:T(8,128)(2,1)} custom-call(f32[1024,128]{1,0:T(8,128)S(1)} %get-tuple-element.47.gc_ref, f32[16,8,128]{2,1,0:T(8,128)S(1)} %get-tuple-element.48.state_ref, f32[8,8,128]{2,1,0:T(8,128)S(1)} %collective-permute-done.14.refs_0_, f32[8,8,128]{2,1,0:T(8,128)S(1)} %collective-permute-done.15.refs_1_, ...), custom_call_target="tpu_custom_call", output_to_operand_aliasing={{}: (7, {})} | custom-call | bytes 1024 | tf_op jit(solution)/shard_map/pallas_call | solution.py:292
  (6 shorter events, 0.1 us)
Async XLA Ops:
  0.6 6.2 %copy-start = (bf16[8192,1024]{1,0:T(8,128)(2,1)S(1)}, bf16[8192,1024]{1,0:T(8,128)(2,1)}, u32[]{:S(2)}) copy-start(bf16[8192,1024]{1,0:T(8,128)(2,1)} %w_ref.29) | copy-start | bytes 50331652
  3.0 10.3 %collective-permute-start = (bf16[528,256]{1,0:T(8,128)(2,1)S(1)}, bf16[528,256]{1,0:T(8,128)(2,1)S(1)}, u32[]{:S(2)}, u32[]{:S(2)}) collective-permute-start(bf16[528,256]{1,0:T(8,128)(2,1)S(1)} %get-tuple-element.27), channel_id=1, source_target_pairs={{0,1},{1,0},{2,3},{3,2},{4,5},{5,4},{6,7},{7,6},{8,9},{9,8},{10,11... | collective-permute-start | bytes 811016 | tf_op jit(solution)/shard_map/ppermute | solution.py:343
  7.5 11.7 %collective-permute-start.1 = (bf16[528,256]{1,0:T(8,128)(2,1)S(1)}, bf16[528,256]{1,0:T(8,128)(2,1)S(1)}, u32[]{:S(2)}, u32[]{:S(2)}) collective-permute-start(bf16[528,256]{1,0:T(8,128)(2,1)S(1)} %shard_map.78), channel_id=1, source_target_pairs={{0,1},{1,0},{2,3},{3,2},{4,5},{5,4},{6,7},{7,6},{8,9},{9,8},{10,11... | collective-permute-start | bytes 811016 | tf_op jit(solution)/shard_map/ppermute | solution.py:343
  11.2 13.8 %collective-permute-start.2 = (bf16[528,256]{1,0:T(8,128)(2,1)S(1)}, bf16[528,256]{1,0:T(8,128)(2,1)S(1)}, u32[]{:S(2)}, u32[]{:S(2)}) collective-permute-start(bf16[528,256]{1,0:T(8,128)(2,1)S(1)} %shard_map.79), channel_id=1, source_target_pairs={{0,1},{1,0},{2,3},{3,2},{4,5},{5,4},{6,7},{7,6},{8,9},{9,8},{10,11... | collective-permute-start | bytes 811016 | tf_op jit(solution)/shard_map/ppermute | solution.py:343
  14.1 10.8 %collective-permute-start.3 = (bf16[528,256]{1,0:T(8,128)(2,1)S(1)}, bf16[528,256]{1,0:T(8,128)(2,1)S(1)}, u32[]{:S(2)}, u32[]{:S(2)}) collective-permute-start(bf16[528,256]{1,0:T(8,128)(2,1)S(1)} %shard_map.80), channel_id=1, source_target_pairs={{0,2},{1,3},{2,0},{3,1},{4,6},{5,7},{6,4},{7,5},{8,10},{9,11},{10,... | collective-permute-start | bytes 811016 | tf_op jit(solution)/shard_map/ppermute | solution.py:343
  17.0 13.8 %collective-permute-start.4 = (bf16[528,256]{1,0:T(8,128)(2,1)S(1)}, bf16[528,256]{1,0:T(8,128)(2,1)S(1)}, u32[]{:S(2)}, u32[]{:S(2)}) collective-permute-start(bf16[528,256]{1,0:T(8,128)(2,1)S(1)} %shard_map.81), channel_id=1, source_target_pairs={{0,1},{1,0},{2,3},{3,2},{4,5},{5,4},{6,7},{7,6},{8,9},{9,8},{10,11... | collective-permute-start | bytes 811016 | tf_op jit(solution)/shard_map/ppermute | solution.py:343
  20.6 16.0 %collective-permute-start.5 = (bf16[528,256]{1,0:T(8,128)(2,1)S(1)}, bf16[528,256]{1,0:T(8,128)(2,1)S(1)}, u32[]{:S(2)}, u32[]{:S(2)}) collective-permute-start(bf16[528,256]{1,0:T(8,128)(2,1)S(1)} %shard_map.83), channel_id=1, source_target_pairs={{0,1},{1,0},{2,3},{3,2},{4,5},{5,4},{6,7},{7,6},{8,9},{9,8},{10,11... | collective-permute-start | bytes 811016 | tf_op jit(solution)/shard_map/ppermute | solution.py:343
  22.7 13.9 %collective-permute-start.6 = (bf16[528,256]{1,0:T(8,128)(2,1)S(1)}, bf16[528,256]{1,0:T(8,128)(2,1)S(1)}, u32[]{:S(2)}, u32[]{:S(2)}) collective-permute-start(bf16[528,256]{1,0:T(8,128)(2,1)S(1)} %shard_map.82), channel_id=1, source_target_pairs={{0,2},{1,3},{2,0},{3,1},{4,6},{5,7},{6,4},{7,5},{8,10},{9,11},{10,... | collective-permute-start | bytes 811016 | tf_op jit(solution)/shard_map/ppermute | solution.py:343
  32.2 12.3 %collective-permute-start.7 = (bf16[528,256]{1,0:T(8,128)(2,1)S(1)}, bf16[528,256]{1,0:T(8,128)(2,1)S(1)}, u32[]{:S(2)}, u32[]{:S(2)}) collective-permute-start(bf16[528,256]{1,0:T(8,128)(2,1)S(1)} %shard_map.86), channel_id=1, source_target_pairs={{0,1},{1,0},{2,3},{3,2},{4,5},{5,4},{6,7},{7,6},{8,9},{9,8},{10,11... | collective-permute-start | bytes 811016 | tf_op jit(solution)/shard_map/ppermute | solution.py:343
  38.1 12.1 %copy-start.1 = (f32[1024,16]{0,1:T(8,128)S(1)}, f32[1024,16]{0,1:T(8,128)}, u32[]{:S(2)}) copy-start(f32[1024,16]{0,1:T(8,128)} %param.11) | copy-start | bytes 196612
  38.1 10.3 %collective-permute-start.8 = (bf16[528,256]{1,0:T(8,128)(2,1)S(1)}, bf16[528,256]{1,0:T(8,128)(2,1)S(1)}, u32[]{:S(2)}, u32[]{:S(2)}) collective-permute-start(bf16[528,256]{1,0:T(8,128)(2,1)S(1)} %shard_map.88), channel_id=1, source_target_pairs={{0,1},{1,0},{2,3},{3,2},{4,5},{5,4},{6,7},{7,6},{8,9},{9,8},{10,11... | collective-permute-start | bytes 811016 | tf_op jit(solution)/shard_map/ppermute | solution.py:343
  40.3 12.7 %collective-permute-start.9 = (bf16[528,256]{1,0:T(8,128)(2,1)S(1)}, bf16[528,256]{1,0:T(8,128)(2,1)S(1)}, u32[]{:S(2)}, u32[]{:S(2)}) collective-permute-start(bf16[528,256]{1,0:T(8,128)(2,1)S(1)} %shard_map.85), channel_id=1, source_target_pairs={{0,2},{1,3},{2,0},{3,1},{4,6},{5,7},{6,4},{7,5},{8,10},{9,11},{10,... | collective-permute-start | bytes 811016 | tf_op jit(solution)/shard_map/ppermute | solution.py:343
  41.9 20.1 %collective-permute-start.10 = (bf16[528,256]{1,0:T(8,128)(2,1)S(1)}, bf16[528,256]{1,0:T(8,128)(2,1)S(1)}, u32[]{:S(2)}, u32[]{:S(2)}) collective-permute-start(bf16[528,256]{1,0:T(8,128)(2,1)S(1)} %shard_map.84), channel_id=1, source_target_pairs={{0,4},{1,5},{2,6},{3,7},{4,0},{5,1},{6,2},{7,3},{8,12},{9,13},{10,... | collective-permute-start | bytes 811016 | tf_op jit(solution)/shard_map/ppermute | solution.py:343
  45.8 21.2 %collective-permute-start.11 = (bf16[528,256]{1,0:T(8,128)(2,1)S(1)}, bf16[528,256]{1,0:T(8,128)(2,1)S(1)}, u32[]{:S(2)}, u32[]{:S(2)}) collective-permute-start(bf16[528,256]{1,0:T(8,128)(2,1)S(1)} %shard_map.90), channel_id=1, source_target_pairs={{0,1},{1,0},{2,3},{3,2},{4,5},{5,4},{6,7},{7,6},{8,9},{9,8},{10,11... | collective-permute-start | bytes 811016 | tf_op jit(solution)/shard_map/ppermute | solution.py:343
  46.4 22.4 %collective-permute-start.13 = (bf16[528,256]{1,0:T(8,128)(2,1)S(1)}, bf16[528,256]{1,0:T(8,128)(2,1)S(1)}, u32[]{:S(2)}, u32[]{:S(2)}) collective-permute-start(bf16[528,256]{1,0:T(8,128)(2,1)S(1)} %shard_map.87), channel_id=1, source_target_pairs={{0,4},{1,5},{2,6},{3,7},{4,0},{5,1},{6,2},{7,3},{8,12},{9,13},{10,... | collective-permute-start | bytes 811016 | tf_op jit(solution)/shard_map/ppermute | solution.py:343
  48.5 20.3 %collective-permute-start.12 = (bf16[528,256]{1,0:T(8,128)(2,1)S(1)}, bf16[528,256]{1,0:T(8,128)(2,1)S(1)}, u32[]{:S(2)}, u32[]{:S(2)}) collective-permute-start(bf16[528,256]{1,0:T(8,128)(2,1)S(1)} %shard_map.89), channel_id=1, source_target_pairs={{0,2},{1,3},{2,0},{3,1},{4,6},{5,7},{6,4},{7,5},{8,10},{9,11},{10,... | collective-permute-start | bytes 811016 | tf_op jit(solution)/shard_map/ppermute | solution.py:343
  50.3 24.8 %copy-start.2 = (f32[1024,16]{0,1:T(8,128)S(1)}, f32[1024,16]{0,1:T(8,128)}, u32[]{:S(2)}) copy-start(f32[1024,16]{0,1:T(8,128)} %param.10) | copy-start | bytes 196612
  64.4 9.4 %collective-permute-start.17 = (f32[8,8,128]{2,1,0:T(8,128)S(1)}, f32[8,8,128]{2,1,0:T(8,128)S(1)}, u32[]{:S(2)}, u32[]{:S(2)}) collective-permute-start(f32[8,8,128]{2,1,0:T(8,128)S(1)} %get-tuple-element.43), channel_id=1, source_target_pairs={{8,0},{16,8},{24,16},{9,1},{17,9},{25,17},{10,2},{18,10},{26,18},{... | collective-permute-start | bytes 98312 | tf_op jit(solution)/shard_map/ppermute | solution.py:355
  65.7 9.4 %collective-permute-start.18 = (f32[8,8,128]{2,1,0:T(8,128)S(1)}, f32[8,8,128]{2,1,0:T(8,128)S(1)}, u32[]{:S(2)}, u32[]{:S(2)}) collective-permute-start(f32[8,8,128]{2,1,0:T(8,128)S(1)} %get-tuple-element.43), channel_id=1, source_target_pairs={{16,0},{24,8},{17,1},{25,9},{18,2},{26,10},{19,3},{27,11},{20,4},{... | collective-permute-start | bytes 98312 | tf_op jit(solution)/shard_map/ppermute | solution.py:355
  67.0 8.1 %collective-permute-start.19 = (f32[8,8,128]{2,1,0:T(8,128)S(1)}, f32[8,8,128]{2,1,0:T(8,128)S(1)}, u32[]{:S(2)}, u32[]{:S(2)}) collective-permute-start(f32[8,8,128]{2,1,0:T(8,128)S(1)} %get-tuple-element.43), channel_id=1, source_target_pairs={{24,0},{25,1},{26,2},{27,3},{28,4},{29,5},{30,6},{31,7}} | collective-permute-start | bytes 98312 | tf_op jit(solution)/shard_map/ppermute | solution.py:355
  71.2 6.5 %collective-permute-start.14 = (f32[8,8,128]{2,1,0:T(8,128)S(1)}, f32[8,8,128]{2,1,0:T(8,128)S(1)}, u32[]{:S(2)}, u32[]{:S(2)}) collective-permute-start(f32[8,8,128]{2,1,0:T(8,128)S(1)} %get-tuple-element.49), channel_id=1, source_target_pairs={{8,0},{16,8},{24,16},{9,1},{17,9},{25,17},{10,2},{18,10},{26,18},{... | collective-permute-start | bytes 98312 | tf_op jit(solution)/shard_map/ppermute | solution.py:355
  72.5 6.2 %collective-permute-start.15 = (f32[8,8,128]{2,1,0:T(8,128)S(1)}, f32[8,8,128]{2,1,0:T(8,128)S(1)}, u32[]{:S(2)}, u32[]{:S(2)}) collective-permute-start(f32[8,8,128]{2,1,0:T(8,128)S(1)} %get-tuple-element.49), channel_id=1, source_target_pairs={{16,0},{24,8},{17,1},{25,9},{18,2},{26,10},{19,3},{27,11},{20,4},{... | collective-permute-start | bytes 98312 | tf_op jit(solution)/shard_map/ppermute | solution.py:355
  73.8 6.0 %collective-permute-start.16 = (f32[8,8,128]{2,1,0:T(8,128)S(1)}, f32[8,8,128]{2,1,0:T(8,128)S(1)}, u32[]{:S(2)}, u32[]{:S(2)}) collective-permute-start(f32[8,8,128]{2,1,0:T(8,128)S(1)} %get-tuple-element.49), channel_id=1, source_target_pairs={{24,0},{25,1},{26,2},{27,3},{28,4},{29,5},{30,6},{31,7}} | collective-permute-start | bytes 98312 | tf_op jit(solution)/shard_map/ppermute | solution.py:355

commit v4 on v3

--- a/solution.py
+++ b/solution.py
@@ -16,8 +16,9 @@
 QUICK = pl.CostEstimate(flops=0, bytes_accessed=1024, transcendentals=0)
 
 ORDER = (
-    (0, 0, 6), (1, 0, 6), (0, 0, 4), (0, 1, 4), (0, 0, 2), (1, 1, 4), (1, 0, 4), (0, 2, 0), (0, 1, 0),
-    (1, 0, 2), (1, 2, 0), (0, 0, 0), (1, 1, 0), (1, 0, 0),
+    (0, 0, 6), (0, 0, 4), (0, 0, 2), (0, 1, 4), (1, 0, 6), (0, 0, 0), (0, 2, 0), (0, 1, 0), (1, 0, 4), (1, 1, 4),
+    (1, 0, 2), (1, 0, 0), (0, "sum"), (0, "gate"), (0, "scan"), (1, 2, 0), (1, 1, 0), (0, "fix"), (1, "sum"),
+    (1, "gate"), (1, "scan"), (1, "fix"),
 )
 
 
@@ -166,15 +167,8 @@
 
 def gate_kernel(portion, rows, segments, fars, acc_ref, *refs):
     far_refs, refs = refs[: len(fars)], refs[len(fars) :]
-    query_hbm, conv_hbm, decay_ref = refs[:3]
-    out_hbm, gc_ref, state_ref, pack_ref, query_ref, conv_ref, gq_ref, sems = refs[-8:]
-    columns = pl.ds(portion * rows, rows)
-    loads = [
-        pltpu.make_async_copy(query_hbm.at[:, columns], query_ref, sems.at[0]),
-        pltpu.make_async_copy(conv_hbm.at[:, columns], conv_ref, sems.at[1]),
-    ]
-    for load in loads:
-        load.start()
+    query_ref, conv_ref, decay_ref = refs[:3]
+    out_hbm, gc_ref, state_ref, pack_ref, gq_ref, sem = refs[-6:]
     toks = query_ref.shape[0]
     modes, sublanes, lanes = state_ref.shape
     mine = slice(portion * sublanes, (portion + 1) * sublanes)
@@ -183,13 +177,11 @@
         for ref, base in zip(far_refs, fars):
             mix = mix + decode(ref, base, rows, line * lanes, lanes)
         mix = mix.T
-        if line == 0:
-            for load in loads:
-                load.wait()
         at = slice(line * lanes, (line + 1) * lanes)
-        gq_ref[:, at] = (mix * conv_ref[:, at].astype(jnp.float32)).astype(jnp.bfloat16)
-        gc_ref[line * toks : (line + 1) * toks, :] = mix * query_ref[:, at].astype(jnp.float32)
-    store = pltpu.make_async_copy(gq_ref, out_hbm.at[:, columns], sems.at[2])
+        full = slice(portion * rows + line * lanes, portion * rows + (line + 1) * lanes)
+        gq_ref[:, at] = (mix * conv_ref[:, full].astype(jnp.float32)).astype(jnp.bfloat16)
+        gc_ref[line * toks : (line + 1) * toks, :] = mix * query_ref[:, full].astype(jnp.float32)
+    store = pltpu.make_async_copy(gq_ref, out_hbm.at[:, pl.ds(portion * rows, rows)], sem)
     store.start()
     decay = [decay_ref[n, mine] for n in range(modes)]
     span = toks // segments
@@ -227,7 +219,7 @@
     more = [] if partial is None else [partial]
     return pl.pallas_call(
         functools.partial(gate_kernel, portion, rows, segments, (0,) * len(fars)),
-        in_specs=[vmem] * (1 + len(fars)) + [high, high, vmem] + [high] * len(more),
+        in_specs=[vmem] * (4 + len(fars)) + [high] * len(more),
         out_specs=(high, vmem, vmem, vmem),
         out_shape=(
             jax.ShapeDtypeStruct((toks, width), jnp.bfloat16),
@@ -235,19 +227,63 @@
             jax.ShapeDtypeStruct((modes, sublanes, lanes), jnp.float32),
             jax.ShapeDtypeStruct((modes // segments, sublanes, lanes), jnp.float32),
         ),
-        scratch_shapes=[pltpu.VMEM((toks, rows), jnp.bfloat16)] * 3 + [pltpu.SemaphoreType.DMA((3,))],
+        scratch_shapes=[pltpu.VMEM((toks, rows), jnp.bfloat16), pltpu.SemaphoreType.DMA],
         input_output_aliases={4 + len(fars): 0} if more else {},
         compiler_params=pltpu.CompilerParams(vmem_limit_bytes=VMEM),
         cost_estimate=QUICK,
-    )(acc, *fars, pinned(query_in), pinned(conv_out), decay, *more)
-
-
-def scan_kernel(portion, segments, hops, gc_ref, state_ref, *refs):
+    )(acc, *fars, query_in, conv_out, decay, *more)
+
+
+def summed(terms):
+    while len(terms) > 1:
+        terms = [terms[k] + terms[k + 1] if k + 1 < len(terms) else terms[k] for k in range(0, len(terms), 2)]
+    return terms[0]
+
+
+def scan_kernel(portion, segments, gc_ref, state_ref, decay_ref, residue_ref, rows_ref):
+    modes, sublanes, lanes = state_ref.shape
+    mine = slice(portion * sublanes, (portion + 1) * sublanes)
+    span = gc_ref.shape[0] // sublanes
+    segment = segment_of((sublanes, lanes), segments)
+    decay = [decay_ref[n, mine] for n in range(modes)]
+    start = []
+    for n in range(modes):
+        total = jnp.zeros((sublanes, lanes), jnp.float32)
+        if segments > 1:
+            group = power(decay[n], span)
+            for k in range(segments - 2, -1, -1):
+                total = jnp.where(segment == k, rolled(state_ref[n] + group * total, -1), total)
+        start.append(total)
+
+    def step(t, state):
+        at = pl.ds(t, sublanes, stride=span)
+        row = gc_ref[at, :]
+        state = tuple(decay[n] * state[n] + row for n in range(modes))
+        rows_ref[at, :] = summed([residue_ref[n, mine] * state[n] for n in range(modes)])
+        return state
+
+    steps_back(span, step, tuple(start), 8)
+
+
+def scan(portion, segments, grad_conv, state, decay, residues):
+    vmem = pl.BlockSpec(memory_space=pltpu.VMEM)
+    return pl.pallas_call(
+        functools.partial(scan_kernel, portion, segments),
+        in_specs=[vmem] * 4,
+        out_specs=vmem,
+        out_shape=jax.ShapeDtypeStruct(grad_conv.shape, jnp.float32),
+        compiler_params=pltpu.CompilerParams(vmem_limit_bytes=VMEM),
+        cost_estimate=QUICK,
+    )(grad_conv, state, decay, residues)
+
+
+def fix_kernel(portion, segments, hops, rows_in_ref, *refs):
     later_refs, refs = refs[:hops], refs[hops:]
     decay_ref, residue_ref = refs[:2]
     out_hbm, rows_ref, out_ref, sem = refs[-4:]
     toks, rows = out_ref.shape
-    modes, sublanes, lanes = state_ref.shape
+    sublanes, lanes = later_refs[0].shape[1:]
+    modes = decay_ref.shape[0]
     mine = slice(portion * sublanes, (portion + 1) * sublanes)
     span = toks // segments
     segment = segment_of((sublanes, lanes), segments)
@@ -255,24 +291,21 @@
     start = []
     for n in range(modes):
         group = power(decay[n], span)
-        whole = power(group, segments)
         m, j = divmod(n, segments)
         total = later_refs[-1][m]
-        for ref in reversed(later_refs[:-1]):
-            total = total * whole + ref[m]
+        if hops > 1:
+            whole = rolled(power(group, segments), 0)
+            for ref in reversed(later_refs[:-1]):
+                total = total * whole + ref[m]
         total = rolled(total, segments - 1 - j)
         for k in range(segments - 2, -1, -1):
-            total = jnp.where(segment == k, rolled(state_ref[n] + group * total, -1), total)
-        start.append(total)
+            total = jnp.where(segment == k, rolled(group * total, -1), total)
+        start.append(residue_ref[n, mine] * total)
 
     def step(t, state):
         at = pl.ds(t, sublanes, stride=span)
-        row = gc_ref[at, :]
-        state = tuple(decay[n] * state[n] + row for n in range(modes))
-        terms = [residue_ref[n, mine] * state[n] for n in range(modes)]
-        while len(terms) > 1:
-            terms = [terms[i] + terms[i + 1] for i in range(0, len(terms), 2)]
-        rows_ref[at, :] = terms[0]
+        state = tuple(decay[n] * state[n] for n in range(modes))
+        rows_ref[at, :] = rows_in_ref[at, :] + summed(list(state))
         return state
 
     steps_back(span, step, tuple(start), 8)
@@ -285,24 +318,24 @@
     store.wait()
 
 
-def scan(portion, rows, segments, grad_conv, state, laters, decay, residues, toks, width, partial):
+def fix(portion, rows, segments, scanned, laters, decay, residues, toks, width, partial):
     vmem = pl.BlockSpec(memory_space=pltpu.VMEM)
     high = pl.BlockSpec(memory_space=pltpu.HBM)
     more = [] if partial is None else [partial]
     return pl.pallas_call(
-        functools.partial(scan_kernel, portion, segments, len(laters)),
-        in_specs=[vmem] * (4 + len(laters)) + [high] * len(more),
+        functools.partial(fix_kernel, portion, segments, len(laters)),
+        in_specs=[vmem] * (3 + len(laters)) + [high] * len(more),
         out_specs=high,
         out_shape=jax.ShapeDtypeStruct((toks, width), jnp.bfloat16),
         scratch_shapes=[
-            pltpu.VMEM(grad_conv.shape, jnp.float32),
+            pltpu.VMEM(scanned.shape, jnp.float32),
             pltpu.VMEM((toks, rows), jnp.bfloat16),
             pltpu.SemaphoreType.DMA,
         ],
-        input_output_aliases={4 + len(laters): 0} if more else {},
+        input_output_aliases={3 + len(laters): 0} if more else {},
         compiler_params=pltpu.CompilerParams(vmem_limit_bytes=VMEM),
         cost_estimate=QUICK,
-    )(grad_conv, state, *laters, decay, residues, *more)
+    )(scanned, *laters, decay, residues, *more)
 
 
 def local(out_grad, out_weight, query_in, conv_out, residues, decay_rates):
@@ -325,40 +358,40 @@
             for p in range(2)
             for s, bit in enumerate(bits)
             for block in sorted(range(0, size, 2 * bit), reverse=True)
-        ]
-    received = {}
+        ] + [(p, kind) for kind in ("sum", "gate", "scan", "fix") for p in range(2)]
     groups = lax.axis_size("ctx")
-    last = None
+    received, sums, gated, scanned, laters = {}, {}, {}, {}, {}
+    grad_query = grad_input = last = None
 
     def after(value):
         return value if last is None else lax.optimization_barrier((value, last))[0]
 
-    for p, s, block in order:
-        bit = bits[s]
-        if last is None:
-            last, turned = first_send(rows, block ^ bit, p * rows, width, place, out_weight, out_grad)
+    for p, s, *block in order:
+        if s == "sum":
+            last = sums[p] = send(rows, 0, p * rows, width, False, after(place), out_weight, turned, [received[p, 0, 0]])
+        elif s == "gate":
+            fars = [received[p, s, 0] for s in range(1, len(bits))]
+            grad_query, grad_conv, state, packed = gate(
+                p, rows, segments, after(sums[p]), fars, query_in, conv_out, decay, grad_query
+            )
+            last, gated[p] = packed, (grad_conv, state)
+            laters[p] = [
+                lax.ppermute(packed, "ctx", [(i, i - hop) for i in range(hop, groups)]) for hop in range(1, groups)
+            ]
+        elif s == "scan":
+            last = scanned[p] = scan(p, segments, *gated[p], decay, residue)
+        elif s == "fix":
+            grad_input = fix(
+                p, rows, segments, after(scanned[p]), laters[p], decay, residue, toks, width, grad_input
+            )
         else:
-            nears = [received[p, i, block ^ bit] for i in range(s)]
-            last = send(rows, block ^ bit, p * rows, width, True, after(place), out_weight, turned, nears)
-        received[p, s, block] = lax.ppermute(last, "ch", [(i, i ^ bit) for i in range(size)])
-
-    states = []
-    grad_query = grad_input = None
-    for p in range(2):
-        acc = send(rows, 0, p * rows, width, False, after(place), out_weight, turned, [received[p, 0, 0]])
-        fars = [received[p, s, 0] for s in range(1, len(bits))]
-        grad_query, grad_conv, state, packed = gate(
-            p, rows, segments, acc, fars, query_in, conv_out, decay, grad_query
-        )
-        last = packed
-        laters = [
-            lax.ppermute(packed, "ctx", [(i, i - hop) for i in range(hop, groups)]) for hop in range(1, groups)
-        ]
-        states.append((grad_conv, state, laters))
-    for p, (grad_conv, state, laters) in enumerate(states):
-        grad_input = scan(
-            p, rows, segments, grad_conv, state, laters, decay, residue, toks, width, grad_input
-        )
+            (block,), bit = block, bits[s]
+            if last is None:
+                last, turned = first_send(rows, block ^ bit, p * rows, width, place, out_weight, out_grad)
+            else:
+                nears = [received[p, i, block ^ bit] for i in range(s)]
+                last = send(rows, block ^ bit, p * rows, width, True, after(place), out_weight, turned, nears)
+            received[p, s, block] = lax.ppermute(last, "ch", [(i, i ^ bit) for i in range(size)])
     return grad_query, grad_input
 
 

time: 82.5 us -> 75.8 us (0.919)
  waiting for transfers between devices: 23.8 us -> 17.5 us
    ppermute x14, waiting for transfers between devices: 21.8 us -> 16.5 us  [local(): lax.ppermute(last, 'ch', [(i, i ^ bit) for i in range(size)])]
    pallas_call x2 -> x4, Pallas kernels: 5.04 us -> 7.13 us  [the longest x2 3.66 us: fix(): pl.pallas_call(functools.partial(fix_kernel, portion, segments, len(later...]
    pallas_call x2, Pallas kernels: 4.69 us -> 2.77 us  [gate(): pl.pallas_call(functools.partial(gate_kernel, portion, rows, segments, (0...]
    ppermute x6, waiting for transfers between devices: 2.03 us -> 1.06 us  [local(): lax.ppermute(packed, 'ctx', [(i, i - hop) for i in range(hop, groups)])]
  transfers between devices with their start and end apart: 20 -> 20, of which waited for: 9 -> 9; matrix products, arithmetic and copies ran while one was open for 0% -> 0% of each run, Pallas kernels for 21% -> 24%
where the time goes in v4:
time: 75.8 us; the launch traced here: 75.5 us
  starting transfers between devices  33.6 us (44%)
  Pallas kernels  22.5 us (30%)
  waiting for transfers between devices  17.5 us (23%)
  between operations  1.01 us (1%)
  local copies, waits for them, and re-layouts  0.94 us (1%)
    ppermute x14, starting transfers between devices, local(): lax.ppermute(last, 'ch', [(i, i ^ bit) for i in range(size)])  25.8 us
    ppermute x14, waiting for transfers between devices, local(): lax.ppermute(last, 'ch', [(i, i ^ bit) for i in range(size)])  16.5 us
    pallas_call x15, Pallas kernels, send(): pl.pallas_call(functools.partial(send_kernel, rows, block, offset, width,...  10.2 us
    ppermute x6, starting transfers between devices, local(): lax.ppermute(packed, 'ctx', [(i, i - hop) for i in range(hop, groups)])  7.74 us
    pallas_call x2, Pallas kernels, fix(): pl.pallas_call(functools.partial(fix_kernel, portion, segments, len(later...  3.66 us
    pallas_call x2, Pallas kernels, scan(): pl.pallas_call(functools.partial(scan_kernel, portion, segments), in_spec...  3.47 us
    pallas_call x2, Pallas kernels, gate(): pl.pallas_call(functools.partial(gate_kernel, portion, rows, segments, (0...  2.77 us
    pallas_call x1, Pallas kernels, first_send(): pl.pallas_call(functools.partial(first_kernel, rows, block, offset, width...  2.4 us
  transfers between devices with their start and end apart: 20, of which 9 were waited for; matrix products, arithmetic and copies ran while one was open for 0% of the time, Pallas kernels for 24%

profile of v4, /device:TPU:0, one launch (start us, length us, event | category | flops | bytes accessed | tf_op | source)
XLA Modules:
  0.0 75.5 jit_solution(6733295183714597407)
XLA Ops:
  0.6 2.4 %shard_map.77 = (bf16[528,256]{1,0:T(8,128)(2,1)S(1)}, bf16[1024,256]{1,0:T(8,128)(2,1)S(1)}) custom-call(s32[1]{0:T(128)} %bitcast.place_ref, bf16[8192,1024]{1,0:T(8,128)(2,1)} %w_ref.29, bf16[256,1024]{1,0:T(8,128)(2,1)} %g_hbm.1), custom_call_target="tpu_custom_call" | custom-call | bytes 1024 | tf_op jit(solution)/shard_map/pallas_call | solution.py:122
  3.0 3.0 %collective-permute-start = (bf16[528,256]{1,0:T(8,128)(2,1)S(1)}, bf16[528,256]{1,0:T(8,128)(2,1)S(1)}, u32[]{:S(2)}, u32[]{:S(2)}) collective-permute-start(bf16[528,256]{1,0:T(8,128)(2,1)S(1)} %get-tuple-element.28), channel_id=1, source_target_pairs={{0,1},{1,0},{2,3},{3,2},{4,5},{5,4},{6,7},{7,6},{8,9},{9,8},{10,11... | collective-permute-start | bytes 811016 | tf_op jit(solution)/shard_map/ppermute | solution.py:394
  6.1 0.8 %copy-done = bf16[8192,1024]{1,0:T(8,128)(2,1)S(1)} copy-done((bf16[8192,1024]{1,0:T(8,128)(2,1)S(1)}, bf16[8192,1024]{1,0:T(8,128)(2,1)}, u32[]{:S(2)}) %copy-start) | copy-done | bytes 16777240
  6.9 0.6 shard_map.78
  7.5 3.0 %collective-permute-start.1 = (bf16[528,256]{1,0:T(8,128)(2,1)S(1)}, bf16[528,256]{1,0:T(8,128)(2,1)S(1)}, u32[]{:S(2)}, u32[]{:S(2)}) collective-permute-start(bf16[528,256]{1,0:T(8,128)(2,1)S(1)} %shard_map.78), channel_id=1, source_target_pairs={{0,1},{1,0},{2,3},{3,2},{4,5},{5,4},{6,7},{7,6},{8,9},{9,8},{10,11... | collective-permute-start | bytes 811016 | tf_op jit(solution)/shard_map/ppermute | solution.py:394
  10.5 0.6 shard_map.79
  11.2 2.2 %collective-permute-done.refs_0_ = bf16[528,256]{1,0:T(8,128)(2,1)S(1)} collective-permute-done((bf16[528,256]{1,0:T(8,128)(2,1)S(1)}, bf16[528,256]{1,0:T(8,128)(2,1)S(1)}, u32[]{:S(2)}, u32[]{:S(2)}) %collective-permute-start) | collective-permute-done | bytes 270368 | tf_op jit(solution)/shard_map/ppermute | solution.py:394
  13.4 0.7 shard_map.80
  14.1 2.2 %collective-permute-start.2 = (bf16[528,256]{1,0:T(8,128)(2,1)S(1)}, bf16[528,256]{1,0:T(8,128)(2,1)S(1)}, u32[]{:S(2)}, u32[]{:S(2)}) collective-permute-start(bf16[528,256]{1,0:T(8,128)(2,1)S(1)} %shard_map.80), channel_id=1, source_target_pairs={{0,2},{1,3},{2,0},{3,1},{4,6},{5,7},{6,4},{7,5},{8,10},{9,11},{10,... | collective-permute-start | bytes 811016 | tf_op jit(solution)/shard_map/ppermute | solution.py:394
  16.3 1.5 %collective-permute-start.3 = (bf16[528,256]{1,0:T(8,128)(2,1)S(1)}, bf16[528,256]{1,0:T(8,128)(2,1)S(1)}, u32[]{:S(2)}, u32[]{:S(2)}) collective-permute-start(bf16[528,256]{1,0:T(8,128)(2,1)S(1)} %shard_map.79), channel_id=1, source_target_pairs={{0,1},{1,0},{2,3},{3,2},{4,5},{5,4},{6,7},{7,6},{8,9},{9,8},{10,11... | collective-permute-start | bytes 811016 | tf_op jit(solution)/shard_map/ppermute | solution.py:394
  17.9 0.6 shard_map.81
  18.5 0.6 collective-permute-start.4
  19.1 0.6 shard_map.82
  19.7 1.6 %collective-permute-start.5 = (bf16[528,256]{1,0:T(8,128)(2,1)S(1)}, bf16[528,256]{1,0:T(8,128)(2,1)S(1)}, u32[]{:S(2)}, u32[]{:S(2)}) collective-permute-start(bf16[528,256]{1,0:T(8,128)(2,1)S(1)} %shard_map.82), channel_id=1, source_target_pairs={{0,1},{1,0},{2,3},{3,2},{4,5},{5,4},{6,7},{7,6},{8,9},{9,8},{10,11... | collective-permute-start | bytes 811016 | tf_op jit(solution)/shard_map/ppermute | solution.py:394
  21.3 0.0 collective-permute-done.1.refs_0_
  21.3 0.0 collective-permute-done.2.refs_1_
  21.3 0.9 %shard_map.83 = bf16[528,256]{1,0:T(8,128)(2,1)S(1)} custom-call(s32[1]{0:T(128)} %bitcast.place_ref, bf16[8192,1024]{1,0:T(8,128)(2,1)S(1)} %copy-done, bf16[1024,256]{1,0:T(8,128)(2,1)S(1)} %get-tuple-element.30.turned_ref, bf16[528,256]{1,0:T(8,128)(2,1)S(1)} %collective-permute-done.1.refs_0_, bf16[528,256]{1,0:T(8,128)(2,1)S(1)} %collective-permute-done.2.refs_1_), custom_call_target="tpu_custom_call" | custom-call | bytes 1024 | tf_op jit(solution)/shard_map/pallas_call | solution.py:83
  22.2 3.5 %collective-permute-done.3.refs_0_ = bf16[528,256]{1,0:T(8,128)(2,1)S(1)} collective-permute-done((bf16[528,256]{1,0:T(8,128)(2,1)S(1)}, bf16[528,256]{1,0:T(8,128)(2,1)S(1)}, u32[]{:S(2)}, u32[]{:S(2)}) %collective-permute-start.3) | collective-permute-done | bytes 270368 | tf_op jit(solution)/shard_map/ppermute | solution.py:394
  25.8 0.7 shard_map.84
  26.5 1.4 %collective-permute-start.6 = (bf16[528,256]{1,0:T(8,128)(2,1)S(1)}, bf16[528,256]{1,0:T(8,128)(2,1)S(1)}, u32[]{:S(2)}, u32[]{:S(2)}) collective-permute-start(bf16[528,256]{1,0:T(8,128)(2,1)S(1)} %shard_map.84), channel_id=1, source_target_pairs={{0,2},{1,3},{2,0},{3,1},{4,6},{5,7},{6,4},{7,5},{8,10},{9,11},{10,... | collective-permute-start | bytes 811016 | tf_op jit(solution)/shard_map/ppermute | solution.py:394
  27.9 2.6 %collective-permute-start.7 = (bf16[528,256]{1,0:T(8,128)(2,1)S(1)}, bf16[528,256]{1,0:T(8,128)(2,1)S(1)}, u32[]{:S(2)}, u32[]{:S(2)}) collective-permute-start(bf16[528,256]{1,0:T(8,128)(2,1)S(1)} %shard_map.83), channel_id=1, source_target_pairs={{0,4},{1,5},{2,6},{3,7},{4,0},{5,1},{6,2},{7,3},{8,12},{9,13},{10,... | collective-permute-start | bytes 811016 | tf_op jit(solution)/shard_map/ppermute | solution.py:394
  30.5 0.6 shard_map.85
  31.1 0.0 copy-start.3
  31.1 0.0 copy-start.4
  31.2 0.4 collective-permute-done.4.refs_0_
  31.6 0.7 shard_map.86
  32.3 1.4 %collective-permute-start.9 = (bf16[528,256]{1,0:T(8,128)(2,1)S(1)}, bf16[528,256]{1,0:T(8,128)(2,1)S(1)}, u32[]{:S(2)}, u32[]{:S(2)}) collective-permute-start(bf16[528,256]{1,0:T(8,128)(2,1)S(1)} %shard_map.86), channel_id=1, source_target_pairs={{0,2},{1,3},{2,0},{3,1},{4,6},{5,7},{6,4},{7,5},{8,10},{9,11},{10,... | collective-permute-start | bytes 811016 | tf_op jit(solution)/shard_map/ppermute | solution.py:394
  33.7 1.5 %collective-permute-start.8 = (bf16[528,256]{1,0:T(8,128)(2,1)S(1)}, bf16[528,256]{1,0:T(8,128)(2,1)S(1)}, u32[]{:S(2)}, u32[]{:S(2)}) collective-permute-start(bf16[528,256]{1,0:T(8,128)(2,1)S(1)} %shard_map.85), channel_id=1, source_target_pairs={{0,1},{1,0},{2,3},{3,2},{4,5},{5,4},{6,7},{7,6},{8,9},{9,8},{10,11... | collective-permute-start | bytes 811016 | tf_op jit(solution)/shard_map/ppermute | solution.py:394
  35.2 0.6 shard_map.87
  35.9 1.5 %collective-permute-done.5.refs_0_ = bf16[528,256]{1,0:T(8,128)(2,1)S(1)} collective-permute-done((bf16[528,256]{1,0:T(8,128)(2,1)S(1)}, bf16[528,256]{1,0:T(8,128)(2,1)S(1)}, u32[]{:S(2)}, u32[]{:S(2)}) %collective-permute-start.5) | collective-permute-done | bytes 270368 | tf_op jit(solution)/shard_map/ppermute | solution.py:394
  37.4 1.5 %collective-permute-start.10 = (bf16[528,256]{1,0:T(8,128)(2,1)S(1)}, bf16[528,256]{1,0:T(8,128)(2,1)S(1)}, u32[]{:S(2)}, u32[]{:S(2)}) collective-permute-start(bf16[528,256]{1,0:T(8,128)(2,1)S(1)} %shard_map.87), channel_id=1, source_target_pairs={{0,1},{1,0},{2,3},{3,2},{4,5},{5,4},{6,7},{7,6},{8,9},{9,8},{10,11... | collective-permute-start | bytes 811016 | tf_op jit(solution)/shard_map/ppermute | solution.py:394
  38.9 0.0 copy-start.1
  38.9 0.0 copy-start.2
  39.0 0.6 shard_map.88
  39.6 0.5 shard_map.89.acc_ref
  40.1 0.6 collective-permute-done.6.refs_0_
  40.7 1.5 %collective-permute-start.11 = (bf16[528,256]{1,0:T(8,128)(2,1)S(1)}, bf16[528,256]{1,0:T(8,128)(2,1)S(1)}, u32[]{:S(2)}, u32[]{:S(2)}) collective-permute-start(bf16[528,256]{1,0:T(8,128)(2,1)S(1)} %shard_map.88), channel_id=1, source_target_pairs={{0,1},{1,0},{2,3},{3,2},{4,5},{5,4},{6,7},{7,6},{8,9},{9,8},{10,11... | collective-permute-start | bytes 811016 | tf_op jit(solution)/shard_map/ppermute | solution.py:394
  42.2 0.0 collective-permute-done.7.refs_1_
  42.3 1.4 %shard_map.90 = (bf16[256,1024]{1,0:T(8,128)(2,1)}, f32[1024,128]{1,0:T(8,128)S(1)}, f32[16,8,128]{2,1,0:T(8,128)S(1)}, f32[8,8,128]{2,1,0:T(8,128)S(1)}) custom-call(f32[512,256]{1,0:T(8,128)S(1)} %shard_map.89.acc_ref, bf16[528,256]{1,0:T(8,128)(2,1)S(1)} %collective-permute-done.6.refs_0_, bf16[528,256]{1,0:T(8,128)(2,1)S(1)} %collective-permute-done.7.refs_1_, ...), custom_call_target="tpu_custom_call" | custom-call | bytes 1024 | tf_op jit(solution)/shard_map/pallas_call | solution.py:220
  43.7 1.7 %shard_map.91.rows_in_ref = f32[1024,128]{1,0:T(8,128)S(1)} custom-call(f32[1024,128]{1,0:T(8,128)S(1)} %get-tuple-element.42.gc_ref, f32[16,8,128]{2,1,0:T(8,128)S(1)} %get-tuple-element.43.state_ref, f32[16,16,128]{2,1,0:T(8,128)S(1)} %bitcast.10, f32[16,16,128]{2,1,0:T(8,128)S(1)} %bitcast.15), custom_call_target="tpu_custom_call" | custom-call | bytes 1024 | tf_op jit(solution)/shard_map/pallas_call | solution.py:270
  45.5 0.0 collective-permute-done.9.refs_1_
  45.5 0.0 collective-permute-done.8.refs_0_
  45.5 0.9 %shard_map.92 = bf16[528,256]{1,0:T(8,128)(2,1)S(1)} custom-call(s32[1]{0:T(128)} %bitcast.place_ref, bf16[8192,1024]{1,0:T(8,128)(2,1)S(1)} %copy-done, bf16[1024,256]{1,0:T(8,128)(2,1)S(1)} %get-tuple-element.30.turned_ref, bf16[528,256]{1,0:T(8,128)(2,1)S(1)} %collective-permute-done.8.refs_0_, bf16[528,256]{1,0:T(8,128)(2,1)S(1)} %collective-permute-done.9.refs_1_), custom_call_target="tpu_custom_call" | custom-call | bytes 1024 | tf_op jit(solution)/shard_map/pallas_call | solution.py:83
  46.4 2.5 %collective-permute-done.10.refs_0_ = bf16[528,256]{1,0:T(8,128)(2,1)S(1)} collective-permute-done((bf16[528,256]{1,0:T(8,128)(2,1)S(1)}, bf16[528,256]{1,0:T(8,128)(2,1)S(1)}, u32[]{:S(2)}, u32[]{:S(2)}) %collective-permute-start.10) | collective-permute-done | bytes 270368 | tf_op jit(solution)/shard_map/ppermute | solution.py:394
  48.9 0.7 shard_map.93
  49.7 1.4 %collective-permute-start.12 = (bf16[528,256]{1,0:T(8,128)(2,1)S(1)}, bf16[528,256]{1,0:T(8,128)(2,1)S(1)}, u32[]{:S(2)}, u32[]{:S(2)}) collective-permute-start(bf16[528,256]{1,0:T(8,128)(2,1)S(1)} %shard_map.93), channel_id=1, source_target_pairs={{0,2},{1,3},{2,0},{3,1},{4,6},{5,7},{6,4},{7,5},{8,10},{9,11},{10,... | collective-permute-start | bytes 811016 | tf_op jit(solution)/shard_map/ppermute | solution.py:394
  51.1 2.6 %collective-permute-start.13 = (bf16[528,256]{1,0:T(8,128)(2,1)S(1)}, bf16[528,256]{1,0:T(8,128)(2,1)S(1)}, u32[]{:S(2)}, u32[]{:S(2)}) collective-permute-start(bf16[528,256]{1,0:T(8,128)(2,1)S(1)} %shard_map.92), channel_id=1, source_target_pairs={{0,4},{1,5},{2,6},{3,7},{4,0},{5,1},{6,2},{7,3},{8,12},{9,13},{10,... | collective-permute-start | bytes 811016 | tf_op jit(solution)/shard_map/ppermute | solution.py:394
  53.7 1.3 %collective-permute-start.17 = (f32[8,8,128]{2,1,0:T(8,128)S(1)}, f32[8,8,128]{2,1,0:T(8,128)S(1)}, u32[]{:S(2)}, u32[]{:S(2)}) collective-permute-start(f32[8,8,128]{2,1,0:T(8,128)S(1)} %get-tuple-element.53), channel_id=1, source_target_pairs={{8,0},{16,8},{24,16},{9,1},{17,9},{25,17},{10,2},{18,10},{26,18},{... | collective-permute-start | bytes 98312 | tf_op jit(solution)/shard_map/ppermute | solution.py:379
  55.0 1.3 %collective-permute-start.18 = (f32[8,8,128]{2,1,0:T(8,128)S(1)}, f32[8,8,128]{2,1,0:T(8,128)S(1)}, u32[]{:S(2)}, u32[]{:S(2)}) collective-permute-start(f32[8,8,128]{2,1,0:T(8,128)S(1)} %get-tuple-element.53), channel_id=1, source_target_pairs={{16,0},{24,8},{17,1},{25,9},{18,2},{26,10},{19,3},{27,11},{20,4},{... | collective-permute-start | bytes 98312 | tf_op jit(solution)/shard_map/ppermute | solution.py:379
  56.3 0.0 collective-permute-done.11.refs_0_
  56.3 1.3 %collective-permute-start.19 = (f32[8,8,128]{2,1,0:T(8,128)S(1)}, f32[8,8,128]{2,1,0:T(8,128)S(1)}, u32[]{:S(2)}, u32[]{:S(2)}) collective-permute-start(f32[8,8,128]{2,1,0:T(8,128)S(1)} %get-tuple-element.53), channel_id=1, source_target_pairs={{24,0},{25,1},{26,2},{27,3},{28,4},{29,5},{30,6},{31,7}} | collective-permute-start | bytes 98312 | tf_op jit(solution)/shard_map/ppermute | solution.py:379
  57.6 0.5 shard_map.94.acc_ref
  58.1 3.0 %collective-permute-done.12.refs_0_ = bf16[528,256]{1,0:T(8,128)(2,1)S(1)} collective-permute-done((bf16[528,256]{1,0:T(8,128)(2,1)S(1)}, bf16[528,256]{1,0:T(8,128)(2,1)S(1)}, u32[]{:S(2)}, u32[]{:S(2)}) %collective-permute-start.12) | collective-permute-done | bytes 270368 | tf_op jit(solution)/shard_map/ppermute | solution.py:394
  61.1 2.7 %collective-permute-done.13.refs_1_ = bf16[528,256]{1,0:T(8,128)(2,1)S(1)} collective-permute-done((bf16[528,256]{1,0:T(8,128)(2,1)S(1)}, bf16[528,256]{1,0:T(8,128)(2,1)S(1)}, u32[]{:S(2)}, u32[]{:S(2)}) %collective-permute-start.13) | collective-permute-done | bytes 270368 | tf_op jit(solution)/shard_map/ppermute | solution.py:394
  63.7 1.4 %shard_map.95 = (bf16[256,1024]{1,0:T(8,128)(2,1)}, f32[1024,128]{1,0:T(8,128)S(1)}, f32[16,8,128]{2,1,0:T(8,128)S(1)}, f32[8,8,128]{2,1,0:T(8,128)S(1)}) custom-call(f32[512,256]{1,0:T(8,128)S(1)} %shard_map.94.acc_ref, bf16[528,256]{1,0:T(8,128)(2,1)S(1)} %collective-permute-done.12.refs_0_, ...), custom_call_target="tpu_custom_call", output_to_operand_aliasing={{0}: (6, {})} | custom-call | bytes 1024 | tf_op jit(solution)/shard_map/pallas_call | solution.py:220
  65.1 1.3 %collective-permute-start.14 = (f32[8,8,128]{2,1,0:T(8,128)S(1)}, f32[8,8,128]{2,1,0:T(8,128)S(1)}, u32[]{:S(2)}, u32[]{:S(2)}) collective-permute-start(f32[8,8,128]{2,1,0:T(8,128)S(1)} %get-tuple-element.51), channel_id=1, source_target_pairs={{8,0},{16,8},{24,16},{9,1},{17,9},{25,17},{10,2},{18,10},{26,18},{... | collective-permute-start | bytes 98312 | tf_op jit(solution)/shard_map/ppermute | solution.py:379
  66.4 1.3 %collective-permute-start.15 = (f32[8,8,128]{2,1,0:T(8,128)S(1)}, f32[8,8,128]{2,1,0:T(8,128)S(1)}, u32[]{:S(2)}, u32[]{:S(2)}) collective-permute-start(f32[8,8,128]{2,1,0:T(8,128)S(1)} %get-tuple-element.51), channel_id=1, source_target_pairs={{16,0},{24,8},{17,1},{25,9},{18,2},{26,10},{19,3},{27,11},{20,4},{... | collective-permute-start | bytes 98312 | tf_op jit(solution)/shard_map/ppermute | solution.py:379
  67.7 0.0 collective-permute-done.17.refs_0_
  67.7 1.3 %collective-permute-start.16 = (f32[8,8,128]{2,1,0:T(8,128)S(1)}, f32[8,8,128]{2,1,0:T(8,128)S(1)}, u32[]{:S(2)}, u32[]{:S(2)}) collective-permute-start(f32[8,8,128]{2,1,0:T(8,128)S(1)} %get-tuple-element.51), channel_id=1, source_target_pairs={{24,0},{25,1},{26,2},{27,3},{28,4},{29,5},{30,6},{31,7}} | collective-permute-start | bytes 98312 | tf_op jit(solution)/shard_map/ppermute | solution.py:379
  69.1 0.0 collective-permute-done.19.refs_2_
  69.1 1.8 %shard_map.97.refs_5_ = bf16[256,1024]{1,0:T(8,128)(2,1)} custom-call(f32[1024,128]{1,0:T(8,128)S(1)} %shard_map.91.rows_in_ref, f32[8,8,128]{2,1,0:T(8,128)S(1)} %collective-permute-done.17.refs_0_, f32[8,8,128]{2,1,0:T(8,128)S(1)} %collective-permute-done.18.refs_1_, f32[8,8,128]{2,1,0:T(8,128)S(1)} %collective-permute-done.19.refs_2_, ...), custom_call_target="tpu_custom_call" | custom-call | bytes 1024 | tf_op jit(solution)/shard_map/pallas_call | solution.py:325
  70.9 1.7 %shard_map.96.rows_in_ref = f32[1024,128]{1,0:T(8,128)S(1)} custom-call(f32[1024,128]{1,0:T(8,128)S(1)} %get-tuple-element.49.gc_ref, f32[16,8,128]{2,1,0:T(8,128)S(1)} %get-tuple-element.50.state_ref, f32[16,16,128]{2,1,0:T(8,128)S(1)} %bitcast.13, f32[16,16,128]{2,1,0:T(8,128)S(1)} %bitcast.17), custom_call_target="tpu_custom_call" | custom-call | bytes 1024 | tf_op jit(solution)/shard_map/pallas_call | solution.py:270
  72.7 1.0 %collective-permute-done.16.refs_2_ = f32[8,8,128]{2,1,0:T(8,128)S(1)} collective-permute-done((f32[8,8,128]{2,1,0:T(8,128)S(1)}, f32[8,8,128]{2,1,0:T(8,128)S(1)}, u32[]{:S(2)}, u32[]{:S(2)}) %collective-permute-start.16) | collective-permute-done | bytes 32800 | tf_op jit(solution)/shard_map/ppermute | solution.py:379
  73.7 1.8 %shard_map.98 = bf16[256,1024]{1,0:T(8,128)(2,1)} custom-call(f32[1024,128]{1,0:T(8,128)S(1)} %shard_map.96.rows_in_ref, f32[8,8,128]{2,1,0:T(8,128)S(1)} %collective-permute-done.14.refs_0_, f32[8,8,128]{2,1,0:T(8,128)S(1)} %collective-permute-done.15.refs_1_, f32[8,8,128]{2,1,0:T(8,128)S(1)} %collective-permute-done.16.refs_2_, ...), custom_call_target="tpu_custom_call", output_to_operand_aliasing={{}: (6, {})} | custom-call | bytes 1024 | tf_op jit(solution)/shard_map/pallas_call | solution.py:325
  (12 shorter events, 0.1 us)
Async XLA Ops:
  0.6 6.2 %copy-start = (bf16[8192,1024]{1,0:T(8,128)(2,1)S(1)}, bf16[8192,1024]{1,0:T(8,128)(2,1)}, u32[]{:S(2)}) copy-start(bf16[8192,1024]{1,0:T(8,128)(2,1)} %w_ref.29) | copy-start | bytes 50331652
  3.0 10.3 %collective-permute-start = (bf16[528,256]{1,0:T(8,128)(2,1)S(1)}, bf16[528,256]{1,0:T(8,128)(2,1)S(1)}, u32[]{:S(2)}, u32[]{:S(2)}) collective-permute-start(bf16[528,256]{1,0:T(8,128)(2,1)S(1)} %get-tuple-element.28), channel_id=1, source_target_pairs={{0,1},{1,0},{2,3},{3,2},{4,5},{5,4},{6,7},{7,6},{8,9},{9,8},{10,11... | collective-permute-start | bytes 811016 | tf_op jit(solution)/shard_map/ppermute | solution.py:394
  7.5 13.8 %collective-permute-start.1 = (bf16[528,256]{1,0:T(8,128)(2,1)S(1)}, bf16[528,256]{1,0:T(8,128)(2,1)S(1)}, u32[]{:S(2)}, u32[]{:S(2)}) collective-permute-start(bf16[528,256]{1,0:T(8,128)(2,1)S(1)} %shard_map.78), channel_id=1, source_target_pairs={{0,1},{1,0},{2,3},{3,2},{4,5},{5,4},{6,7},{7,6},{8,9},{9,8},{10,11... | collective-permute-start | bytes 811016 | tf_op jit(solution)/shard_map/ppermute | solution.py:394
  14.1 7.2 %collective-permute-start.2 = (bf16[528,256]{1,0:T(8,128)(2,1)S(1)}, bf16[528,256]{1,0:T(8,128)(2,1)S(1)}, u32[]{:S(2)}, u32[]{:S(2)}) collective-permute-start(bf16[528,256]{1,0:T(8,128)(2,1)S(1)} %shard_map.80), channel_id=1, source_target_pairs={{0,2},{1,3},{2,0},{3,1},{4,6},{5,7},{6,4},{7,5},{8,10},{9,11},{10,... | collective-permute-start | bytes 811016 | tf_op jit(solution)/shard_map/ppermute | solution.py:394
  16.3 9.4 %collective-permute-start.3 = (bf16[528,256]{1,0:T(8,128)(2,1)S(1)}, bf16[528,256]{1,0:T(8,128)(2,1)S(1)}, u32[]{:S(2)}, u32[]{:S(2)}) collective-permute-start(bf16[528,256]{1,0:T(8,128)(2,1)S(1)} %shard_map.79), channel_id=1, source_target_pairs={{0,1},{1,0},{2,3},{3,2},{4,5},{5,4},{6,7},{7,6},{8,9},{9,8},{10,11... | collective-permute-start | bytes 811016 | tf_op jit(solution)/shard_map/ppermute | solution.py:394
  18.5 13.1 %collective-permute-start.4 = (bf16[528,256]{1,0:T(8,128)(2,1)S(1)}, bf16[528,256]{1,0:T(8,128)(2,1)S(1)}, u32[]{:S(2)}, u32[]{:S(2)}) collective-permute-start(bf16[528,256]{1,0:T(8,128)(2,1)S(1)} %shard_map.81), channel_id=1, source_target_pairs={{0,1},{1,0},{2,3},{3,2},{4,5},{5,4},{6,7},{7,6},{8,9},{9,8},{10,11... | collective-permute-start | bytes 811016 | tf_op jit(solution)/shard_map/ppermute | solution.py:394
  19.7 17.7 %collective-permute-start.5 = (bf16[528,256]{1,0:T(8,128)(2,1)S(1)}, bf16[528,256]{1,0:T(8,128)(2,1)S(1)}, u32[]{:S(2)}, u32[]{:S(2)}) collective-permute-start(bf16[528,256]{1,0:T(8,128)(2,1)S(1)} %shard_map.82), channel_id=1, source_target_pairs={{0,1},{1,0},{2,3},{3,2},{4,5},{5,4},{6,7},{7,6},{8,9},{9,8},{10,11... | collective-permute-start | bytes 811016 | tf_op jit(solution)/shard_map/ppermute | solution.py:394
  26.5 14.2 %collective-permute-start.6 = (bf16[528,256]{1,0:T(8,128)(2,1)S(1)}, bf16[528,256]{1,0:T(8,128)(2,1)S(1)}, u32[]{:S(2)}, u32[]{:S(2)}) collective-permute-start(bf16[528,256]{1,0:T(8,128)(2,1)S(1)} %shard_map.84), channel_id=1, source_target_pairs={{0,2},{1,3},{2,0},{3,1},{4,6},{5,7},{6,4},{7,5},{8,10},{9,11},{10,... | collective-permute-start | bytes 811016 | tf_op jit(solution)/shard_map/ppermute | solution.py:394
  27.9 14.3 %collective-permute-start.7 = (bf16[528,256]{1,0:T(8,128)(2,1)S(1)}, bf16[528,256]{1,0:T(8,128)(2,1)S(1)}, u32[]{:S(2)}, u32[]{:S(2)}) collective-permute-start(bf16[528,256]{1,0:T(8,128)(2,1)S(1)} %shard_map.83), channel_id=1, source_target_pairs={{0,4},{1,5},{2,6},{3,7},{4,0},{5,1},{6,2},{7,3},{8,12},{9,13},{10,... | collective-permute-start | bytes 811016 | tf_op jit(solution)/shard_map/ppermute | solution.py:394
  31.1 7.8 %copy-start.3 = (f32[1024,16]{0,1:T(8,128)S(1)}, f32[1024,16]{0,1:T(8,128)}, u32[]{:S(2)}) copy-start(f32[1024,16]{0,1:T(8,128)} %param.11) | copy-start | bytes 196612
  31.1 7.8 %copy-start.4 = (f32[1024,16]{0,1:T(8,128)S(1)}, f32[1024,16]{0,1:T(8,128)}, u32[]{:S(2)}) copy-start(f32[1024,16]{0,1:T(8,128)} %param.10) | copy-start | bytes 196612
  32.3 13.2 %collective-permute-start.9 = (bf16[528,256]{1,0:T(8,128)(2,1)S(1)}, bf16[528,256]{1,0:T(8,128)(2,1)S(1)}, u32[]{:S(2)}, u32[]{:S(2)}) collective-permute-start(bf16[528,256]{1,0:T(8,128)(2,1)S(1)} %shard_map.86), channel_id=1, source_target_pairs={{0,2},{1,3},{2,0},{3,1},{4,6},{5,7},{6,4},{7,5},{8,10},{9,11},{10,... | collective-permute-start | bytes 811016 | tf_op jit(solution)/shard_map/ppermute | solution.py:394
  33.7 11.8 %collective-permute-start.8 = (bf16[528,256]{1,0:T(8,128)(2,1)S(1)}, bf16[528,256]{1,0:T(8,128)(2,1)S(1)}, u32[]{:S(2)}, u32[]{:S(2)}) collective-permute-start(bf16[528,256]{1,0:T(8,128)(2,1)S(1)} %shard_map.85), channel_id=1, source_target_pairs={{0,1},{1,0},{2,3},{3,2},{4,5},{5,4},{6,7},{7,6},{8,9},{9,8},{10,11... | collective-permute-start | bytes 811016 | tf_op jit(solution)/shard_map/ppermute | solution.py:394
  37.4 11.6 %collective-permute-start.10 = (bf16[528,256]{1,0:T(8,128)(2,1)S(1)}, bf16[528,256]{1,0:T(8,128)(2,1)S(1)}, u32[]{:S(2)}, u32[]{:S(2)}) collective-permute-start(bf16[528,256]{1,0:T(8,128)(2,1)S(1)} %shard_map.87), channel_id=1, source_target_pairs={{0,1},{1,0},{2,3},{3,2},{4,5},{5,4},{6,7},{7,6},{8,9},{9,8},{10,11... | collective-permute-start | bytes 811016 | tf_op jit(solution)/shard_map/ppermute | solution.py:394
  38.9 3.3 %copy-start.1 = (bf16[256,1024]{1,0:T(8,128)(2,1)S(1)}, bf16[256,1024]{1,0:T(8,128)(2,1)}, u32[]{:S(2)}) copy-start(bf16[256,1024]{1,0:T(8,128)(2,1)} %refs_2_.3) | copy-start | bytes 1572868
  38.9 3.3 %copy-start.2 = (bf16[256,1024]{1,0:T(8,128)(2,1)S(1)}, bf16[256,1024]{1,0:T(8,128)(2,1)}, u32[]{:S(2)}) copy-start(bf16[256,1024]{1,0:T(8,128)(2,1)} %refs_3_.3) | copy-start | bytes 1572868
  40.7 15.6 %collective-permute-start.11 = (bf16[528,256]{1,0:T(8,128)(2,1)S(1)}, bf16[528,256]{1,0:T(8,128)(2,1)S(1)}, u32[]{:S(2)}, u32[]{:S(2)}) collective-permute-start(bf16[528,256]{1,0:T(8,128)(2,1)S(1)} %shard_map.88), channel_id=1, source_target_pairs={{0,1},{1,0},{2,3},{3,2},{4,5},{5,4},{6,7},{7,6},{8,9},{9,8},{10,11... | collective-permute-start | bytes 811016 | tf_op jit(solution)/shard_map/ppermute | solution.py:394
  49.7 11.4 %collective-permute-start.12 = (bf16[528,256]{1,0:T(8,128)(2,1)S(1)}, bf16[528,256]{1,0:T(8,128)(2,1)S(1)}, u32[]{:S(2)}, u32[]{:S(2)}) collective-permute-start(bf16[528,256]{1,0:T(8,128)(2,1)S(1)} %shard_map.93), channel_id=1, source_target_pairs={{0,2},{1,3},{2,0},{3,1},{4,6},{5,7},{6,4},{7,5},{8,10},{9,11},{10,... | collective-permute-start | bytes 811016 | tf_op jit(solution)/shard_map/ppermute | solution.py:394
  51.1 12.7 %collective-permute-start.13 = (bf16[528,256]{1,0:T(8,128)(2,1)S(1)}, bf16[528,256]{1,0:T(8,128)(2,1)S(1)}, u32[]{:S(2)}, u32[]{:S(2)}) collective-permute-start(bf16[528,256]{1,0:T(8,128)(2,1)S(1)} %shard_map.92), channel_id=1, source_target_pairs={{0,4},{1,5},{2,6},{3,7},{4,0},{5,1},{6,2},{7,3},{8,12},{9,13},{10,... | collective-permute-start | bytes 811016 | tf_op jit(solution)/shard_map/ppermute | solution.py:394
  53.7 14.1 %collective-permute-start.17 = (f32[8,8,128]{2,1,0:T(8,128)S(1)}, f32[8,8,128]{2,1,0:T(8,128)S(1)}, u32[]{:S(2)}, u32[]{:S(2)}) collective-permute-start(f32[8,8,128]{2,1,0:T(8,128)S(1)} %get-tuple-element.53), channel_id=1, source_target_pairs={{8,0},{16,8},{24,16},{9,1},{17,9},{25,17},{10,2},{18,10},{26,18},{... | collective-permute-start | bytes 98312 | tf_op jit(solution)/shard_map/ppermute | solution.py:379
  55.0 14.1 %collective-permute-start.18 = (f32[8,8,128]{2,1,0:T(8,128)S(1)}, f32[8,8,128]{2,1,0:T(8,128)S(1)}, u32[]{:S(2)}, u32[]{:S(2)}) collective-permute-start(f32[8,8,128]{2,1,0:T(8,128)S(1)} %get-tuple-element.53), channel_id=1, source_target_pairs={{16,0},{24,8},{17,1},{25,9},{18,2},{26,10},{19,3},{27,11},{20,4},{... | collective-permute-start | bytes 98312 | tf_op jit(solution)/shard_map/ppermute | solution.py:379
  56.3 12.8 %collective-permute-start.19 = (f32[8,8,128]{2,1,0:T(8,128)S(1)}, f32[8,8,128]{2,1,0:T(8,128)S(1)}, u32[]{:S(2)}, u32[]{:S(2)}) collective-permute-start(f32[8,8,128]{2,1,0:T(8,128)S(1)} %get-tuple-element.53), channel_id=1, source_target_pairs={{24,0},{25,1},{26,2},{27,3},{28,4},{29,5},{30,6},{31,7}} | collective-permute-start | bytes 98312 | tf_op jit(solution)/shard_map/ppermute | solution.py:379
  65.1 7.5 %collective-permute-start.14 = (f32[8,8,128]{2,1,0:T(8,128)S(1)}, f32[8,8,128]{2,1,0:T(8,128)S(1)}, u32[]{:S(2)}, u32[]{:S(2)}) collective-permute-start(f32[8,8,128]{2,1,0:T(8,128)S(1)} %get-tuple-element.51), channel_id=1, source_target_pairs={{8,0},{16,8},{24,16},{9,1},{17,9},{25,17},{10,2},{18,10},{26,18},{... | collective-permute-start | bytes 98312 | tf_op jit(solution)/shard_map/ppermute | solution.py:379
  66.4 6.2 %collective-permute-start.15 = (f32[8,8,128]{2,1,0:T(8,128)S(1)}, f32[8,8,128]{2,1,0:T(8,128)S(1)}, u32[]{:S(2)}, u32[]{:S(2)}) collective-permute-start(f32[8,8,128]{2,1,0:T(8,128)S(1)} %get-tuple-element.51), channel_id=1, source_target_pairs={{16,0},{24,8},{17,1},{25,9},{18,2},{26,10},{19,3},{27,11},{20,4},{... | collective-permute-start | bytes 98312 | tf_op jit(solution)/shard_map/ppermute | solution.py:379
  67.7 6.0 %collective-permute-start.16 = (f32[8,8,128]{2,1,0:T(8,128)S(1)}, f32[8,8,128]{2,1,0:T(8,128)S(1)}, u32[]{:S(2)}, u32[]{:S(2)}) collective-permute-start(f32[8,8,128]{2,1,0:T(8,128)S(1)} %get-tuple-element.51), channel_id=1, source_target_pairs={{24,0},{25,1},{26,2},{27,3},{28,4},{29,5},{30,6},{31,7}} | collective-permute-start | bytes 98312 | tf_op jit(solution)/shard_map/ppermute | solution.py:379

commit v5 on v4

--- a/solution.py
+++ b/solution.py
@@ -15,15 +15,21 @@
 VMEM = 24 * 1024 * 1024
 QUICK = pl.CostEstimate(flops=0, bytes_accessed=1024, transcendentals=0)
 
+PORTIONS = (((0, 1, 2), 2, 0), ((0, 1, 2), 2, 1))
 ORDER = (
-    (0, 0, 6), (0, 0, 4), (0, 0, 2), (0, 1, 4), (1, 0, 6), (0, 0, 0), (0, 2, 0), (0, 1, 0), (1, 0, 4), (1, 1, 4),
-    (1, 0, 2), (1, 0, 0), (0, "sum"), (0, "gate"), (0, "scan"), (1, 2, 0), (1, 1, 0), (0, "fix"), (1, "sum"),
-    (1, "gate"), (1, "scan"), (1, "fix"),
+    (0, 0, (6,)), (0, 0, (4,)), (1, 0, (2,)), (0, 0, (2,)), (0, 0, (0,)), (1, 0, (4,)), (1, 0, (6,)), (0, 1, (4,)),
+    (0, 1, (0,)), (1, 0, (0,)), (1, 1, (4,)), (0, 2, (0,)), (1, 1, (0,)), (1, 2, (0,)), (0, "sum"), (0, "gate"),
+    (1, "sum"), (0, "scan"), (1, "gate"), (1, "scan"), (0, "fix"), (1, "fix"),
 )
+GATHERED = (True, False)
 
 
 def part_of(rows):
-    return max(rows // PEAKS, min(rows, 16))
+    return next(part for part in range(16, rows + 1, 16) if rows % part == 0 and rows // part <= PEAKS)
+
+
+def step_of(rows):
+    return next(step for step in (STEP, STEP // 2, rows) if rows % step == 0)
 
 
 def encode(block, part):
@@ -54,34 +60,39 @@
     return pltpu.with_memory_space_constraint(array, pltpu.HBM)
 
 
-def send_kernel(rows, block, offset, width, sources, coded, place_ref, w_ref, turned_ref, *refs):
-    near_refs, out_ref = refs[:sources], refs[sources]
-    step = min(rows, STEP)
-    first = (place_ref[0] ^ block) * width + offset
-    part = part_of(rows)
-    peaks = []
-    for at in range(0, rows, step):
-        total = jnp.dot(
-            w_ref[pl.ds(pl.multiple_of(first + at, 16), step), :], turned_ref[...], preferred_element_type=jnp.float32
-        )
-        for near_ref in near_refs:
-            total = total + decode(near_ref, 0, rows, at, step)
+def send_kernel(items, coded, width, near, place_ref, w_ref, turned_ref, *refs):
+    near_refs, out_ref = refs[:near], refs[near]
+    base = 0
+    for block, offset, rows, sources in items:
+        step, part = step_of(rows), part_of(rows)
+        first = (place_ref[0] ^ block) * width + offset
+        peaks = []
+        for at in range(0, rows, step):
+            total = jnp.dot(
+                w_ref[pl.ds(pl.multiple_of(first + at, 16), step), :],
+                turned_ref[...],
+                preferred_element_type=jnp.float32,
+            )
+            for source, start in sources:
+                total = total + decode(near_refs[source], start, rows, at, step)
+            if coded:
+                total, more = encode(total, part)
+                peaks += more
+            out_ref[base + at : base + at + step, :] = total
+        base += rows
         if coded:
-            total, more = encode(total, part)
-            peaks += more
-        out_ref[at : at + step, :] = total
-    if coded:
-        if len(peaks) < PEAKS:
-            peaks.append(jnp.zeros((PEAKS - len(peaks), total.shape[1]), jnp.float32))
-        out_ref[rows:, :] = jnp.concatenate(peaks, axis=0).astype(jnp.bfloat16)
-
-
-def send(rows, block, offset, width, coded, place, weight, turned, nears):
+            if len(peaks) < PEAKS:
+                peaks.append(jnp.zeros((PEAKS - len(peaks), total.shape[1]), jnp.float32))
+            out_ref[base : base + PEAKS, :] = jnp.concatenate(peaks, axis=0).astype(jnp.bfloat16)
+            base += PEAKS
+
+
+def send(items, coded, width, place, weight, turned, nears):
     toks = turned.shape[1]
     vmem = pl.BlockSpec(memory_space=pltpu.VMEM)
-    count = rows + PEAKS if coded else rows
+    count = sum(rows + PEAKS if coded else rows for _, _, rows, _ in items)
     return pl.pallas_call(
-        functools.partial(send_kernel, rows, block, offset, width, len(nears), coded),
+        functools.partial(send_kernel, items, coded, width, len(nears)),
         in_specs=[pl.BlockSpec(memory_space=pltpu.SMEM)] + [vmem] * (2 + len(nears)),
         out_specs=vmem,
         out_shape=jax.ShapeDtypeStruct((count, toks), jnp.bfloat16 if coded else jnp.float32),
@@ -91,7 +102,7 @@
 
 
 def first_kernel(rows, block, offset, width, place_ref, w_hbm, g_hbm, out_ref, turned_ref, w_ref, g_ref, sems):
-    step = min(rows, STEP)
+    step = step_of(rows)
     first = pl.multiple_of((place_ref[0] ^ block) * width + offset, 16)
     copies = [pltpu.make_async_copy(g_hbm, g_ref, sems.at[0])]
     for i, at in enumerate(range(0, rows, step)):
@@ -130,7 +141,7 @@
         scratch_shapes=[
             pltpu.VMEM((rows, depth), jnp.bfloat16),
             pltpu.VMEM((toks, depth), jnp.bfloat16),
-            pltpu.SemaphoreType.DMA((1 + rows // min(rows, STEP),)),
+            pltpu.SemaphoreType.DMA((1 + rows // step_of(rows),)),
         ],
         compiler_params=pltpu.CompilerParams(vmem_limit_bytes=VMEM),
         cost_estimate=QUICK,
@@ -165,23 +176,24 @@
     return pltpu.roll(value, by, 0) if by else value
 
 
-def gate_kernel(portion, rows, segments, fars, acc_ref, *refs):
-    far_refs, refs = refs[: len(fars)], refs[len(fars) :]
+def gate_kernel(half, rows, segments, pieces, near, acc_ref, *refs):
+    near_refs, refs = refs[:near], refs[near:]
     query_ref, conv_ref, decay_ref = refs[:3]
     out_hbm, gc_ref, state_ref, pack_ref, gq_ref, sem = refs[-6:]
     toks = query_ref.shape[0]
     modes, sublanes, lanes = state_ref.shape
-    mine = slice(portion * sublanes, (portion + 1) * sublanes)
+    mine = slice(half * sublanes, (half + 1) * sublanes)
     for line in range(rows // lanes):
         mix = acc_ref[line * lanes : (line + 1) * lanes, :]
-        for ref, base in zip(far_refs, fars):
-            mix = mix + decode(ref, base, rows, line * lanes, lanes)
+        first, count, sources = next(piece for piece in reversed(pieces) if piece[0] <= line * lanes)
+        for source, start in sources:
+            mix = mix + decode(near_refs[source], start, count, line * lanes - first, lanes)
         mix = mix.T
         at = slice(line * lanes, (line + 1) * lanes)
-        full = slice(portion * rows + line * lanes, portion * rows + (line + 1) * lanes)
+        full = slice(half * rows + line * lanes, half * rows + (line + 1) * lanes)
         gq_ref[:, at] = (mix * conv_ref[:, full].astype(jnp.float32)).astype(jnp.bfloat16)
         gc_ref[line * toks : (line + 1) * toks, :] = mix * query_ref[:, full].astype(jnp.float32)
-    store = pltpu.make_async_copy(gq_ref, out_hbm.at[:, pl.ds(portion * rows, rows)], sem)
+    store = pltpu.make_async_copy(gq_ref, out_hbm.at[:, pl.ds(half * rows, rows)], sem)
     store.start()
     decay = [decay_ref[n, mine] for n in range(modes)]
     span = toks // segments
@@ -206,11 +218,12 @@
         packed = whole[m * segments]
         for j in range(1, segments):
             packed = jnp.where(segment == j, rolled(whole[m * segments + j], j), packed)
-        pack_ref[m] = packed
+        for copy in range(pack_ref.shape[0]):
+            pack_ref[copy, m] = packed
     store.wait()
 
 
-def gate(portion, rows, segments, acc, fars, query_in, conv_out, decay, partial):
+def gate(half, rows, segments, copies, pieces, acc, nears, query_in, conv_out, decay, partial):
     toks, width = query_in.shape
     modes, sublanes, lanes = decay.shape
     sublanes = rows // lanes * segments
@@ -218,20 +231,20 @@
     high = pl.BlockSpec(memory_space=pltpu.HBM)
     more = [] if partial is None else [partial]
     return pl.pallas_call(
-        functools.partial(gate_kernel, portion, rows, segments, (0,) * len(fars)),
-        in_specs=[vmem] * (4 + len(fars)) + [high] * len(more),
+        functools.partial(gate_kernel, half, rows, segments, pieces, len(nears)),
+        in_specs=[vmem] * (4 + len(nears)) + [high] * len(more),
         out_specs=(high, vmem, vmem, vmem),
         out_shape=(
             jax.ShapeDtypeStruct((toks, width), jnp.bfloat16),
             jax.ShapeDtypeStruct((rows // lanes * toks, lanes), jnp.float32),
             jax.ShapeDtypeStruct((modes, sublanes, lanes), jnp.float32),
-            jax.ShapeDtypeStruct((modes // segments, sublanes, lanes), jnp.float32),
+            jax.ShapeDtypeStruct((copies, modes // segments, sublanes, lanes), jnp.float32),
         ),
         scratch_shapes=[pltpu.VMEM((toks, rows), jnp.bfloat16), pltpu.SemaphoreType.DMA],
-        input_output_aliases={4 + len(fars): 0} if more else {},
+        input_output_aliases={4 + len(nears): 0} if more else {},
         compiler_params=pltpu.CompilerParams(vmem_limit_bytes=VMEM),
         cost_estimate=QUICK,
-    )(acc, *fars, query_in, conv_out, decay, *more)
+    )(acc, *nears, query_in, conv_out, decay, *more)
 
 
 def summed(terms):
@@ -240,9 +253,9 @@
     return terms[0]
 
 
-def scan_kernel(portion, segments, gc_ref, state_ref, decay_ref, residue_ref, rows_ref):
+def scan_kernel(half, segments, gc_ref, state_ref, decay_ref, residue_ref, rows_ref):
     modes, sublanes, lanes = state_ref.shape
-    mine = slice(portion * sublanes, (portion + 1) * sublanes)
+    mine = slice(half * sublanes, (half + 1) * sublanes)
     span = gc_ref.shape[0] // sublanes
     segment = segment_of((sublanes, lanes), segments)
     decay = [decay_ref[n, mine] for n in range(modes)]
@@ -265,10 +278,10 @@
     steps_back(span, step, tuple(start), 8)
 
 
-def scan(portion, segments, grad_conv, state, decay, residues):
+def scan(half, segments, grad_conv, state, decay, residues):
     vmem = pl.BlockSpec(memory_space=pltpu.VMEM)
     return pl.pallas_call(
-        functools.partial(scan_kernel, portion, segments),
+        functools.partial(scan_kernel, half, segments),
         in_specs=[vmem] * 4,
         out_specs=vmem,
         out_shape=jax.ShapeDtypeStruct(grad_conv.shape, jnp.float32),
@@ -277,29 +290,26 @@
     )(grad_conv, state, decay, residues)
 
 
-def fix_kernel(portion, segments, hops, rows_in_ref, *refs):
-    later_refs, refs = refs[:hops], refs[hops:]
-    decay_ref, residue_ref = refs[:2]
+def fix_kernel(half, segments, group_ref, rows_in_ref, states_ref, decay_ref, residue_ref, *refs):
     out_hbm, rows_ref, out_ref, sem = refs[-4:]
     toks, rows = out_ref.shape
-    sublanes, lanes = later_refs[0].shape[1:]
+    groups, _, sublanes, lanes = states_ref.shape
     modes = decay_ref.shape[0]
-    mine = slice(portion * sublanes, (portion + 1) * sublanes)
+    mine = slice(half * sublanes, (half + 1) * sublanes)
     span = toks // segments
     segment = segment_of((sublanes, lanes), segments)
     decay = [decay_ref[n, mine] for n in range(modes)]
     start = []
     for n in range(modes):
-        group = power(decay[n], span)
+        lap = power(decay[n], span)
+        whole = power(lap, segments)
         m, j = divmod(n, segments)
-        total = later_refs[-1][m]
-        if hops > 1:
-            whole = rolled(power(group, segments), 0)
-            for ref in reversed(later_refs[:-1]):
-                total = total * whole + ref[m]
-        total = rolled(total, segments - 1 - j)
+        total = jnp.zeros((sublanes, lanes), jnp.float32)
+        for group in range(groups - 1, 0, -1):
+            state = rolled(states_ref[group, m], segments - 1 - j)
+            total = jnp.where(group > group_ref[0], total * whole + state, total)
         for k in range(segments - 2, -1, -1):
-            total = jnp.where(segment == k, rolled(group * total, -1), total)
+            total = jnp.where(segment == k, rolled(lap * total, -1), total)
         start.append(residue_ref[n, mine] * total)
 
     def step(t, state):
@@ -313,18 +323,18 @@
         out_ref[:, line * lanes : (line + 1) * lanes] = rows_ref[
             line * toks : (line + 1) * toks, :
         ].astype(jnp.bfloat16)
-    store = pltpu.make_async_copy(out_ref, out_hbm.at[:, pl.ds(portion * rows, rows)], sem)
+    store = pltpu.make_async_copy(out_ref, out_hbm.at[:, pl.ds(half * rows, rows)], sem)
     store.start()
     store.wait()
 
 
-def fix(portion, rows, segments, scanned, laters, decay, residues, toks, width, partial):
+def fix(half, rows, segments, group, scanned, states, decay, residues, toks, width, partial):
     vmem = pl.BlockSpec(memory_space=pltpu.VMEM)
     high = pl.BlockSpec(memory_space=pltpu.HBM)
     more = [] if partial is None else [partial]
     return pl.pallas_call(
-        functools.partial(fix_kernel, portion, segments, len(laters)),
-        in_specs=[vmem] * (3 + len(laters)) + [high] * len(more),
+        functools.partial(fix_kernel, half, segments),
+        in_specs=[pl.BlockSpec(memory_space=pltpu.SMEM)] + [vmem] * 4 + [high] * len(more),
         out_specs=high,
         out_shape=jax.ShapeDtypeStruct((toks, width), jnp.bfloat16),
         scratch_shapes=[
@@ -332,66 +342,102 @@
             pltpu.VMEM((toks, rows), jnp.bfloat16),
             pltpu.SemaphoreType.DMA,
         ],
-        input_output_aliases={3 + len(laters): 0} if more else {},
+        input_output_aliases={5: 0} if more else {},
         compiler_params=pltpu.CompilerParams(vmem_limit_bytes=VMEM),
         cost_estimate=QUICK,
-    )(scanned, *laters, decay, residues, *more)
+    )(group, scanned, states, decay, residues, *more)
 
 
 def local(out_grad, out_weight, query_in, conv_out, residues, decay_rates):
     toks, width = query_in.shape
     modes = decay_rates.shape[1]
     lanes = math.gcd(width, 128)
-    size = lax.axis_size("ch")
+    size, groups = lax.axis_size("ch"), lax.axis_size("ctx")
     bits = [1 << i for i in range(size.bit_length() - 1)]
     place = jnp.reshape(lax.axis_index("ch"), (1,)).astype(jnp.int32)
-    rows = width // 2
-    lines = rows // lanes
+    group = jnp.reshape(lax.axis_index("ctx"), (1,)).astype(jnp.int32)
+    half_rows = width // 2
+    lines = half_rows // lanes
     segments = 8 // lines
     by_mode = lambda values: jnp.repeat(values.T.reshape(modes, width // lanes, lanes), segments, axis=1)
     decay, residue = by_mode(decay_rates), by_mode(residues)
 
-    order = ORDER
+    portions, order = PORTIONS, ORDER
     if size != 8:
+        portions = ((tuple(range(len(bits))), 2, 0), (tuple(range(len(bits))), 2, 1))
         order = [
-            (p, s, block)
+            (p, s, (block,))
             for p in range(2)
             for s, bit in enumerate(bits)
             for block in sorted(range(0, size, 2 * bit), reverse=True)
         ] + [(p, kind) for kind in ("sum", "gate", "scan", "fix") for p in range(2)]
-    groups = lax.axis_size("ctx")
-    received, sums, gated, scanned, laters = {}, {}, {}, {}, {}
+    offsets = [sum(width // part for _, part, _ in portions[:p]) for p in range(len(portions))]
+
+    received, sums, gated, scanned, states = {}, {}, {}, {}, {}
     grad_query = grad_input = last = None
 
     def after(value):
         return value if last is None else lax.optimization_barrier((value, last))[0]
 
-    for p, s, *block in order:
+    def collect(wanted):
+        arrays, places = [], []
+        for key in wanted:
+            array, start = received[key]
+            index = next((i for i, known in enumerate(arrays) if known is array), len(arrays))
+            if index == len(arrays):
+                arrays.append(array)
+            places.append((index, start))
+        return arrays, places
+
+    for p, s, *blocks in order:
+        inside = [q for q, (_, _, half) in enumerate(portions) if half == p]
         if s == "sum":
-            last = sums[p] = send(rows, 0, p * rows, width, False, after(place), out_weight, turned, [received[p, 0, 0]])
+            arrays, places = collect([(q, 0, 0) for q in inside])
+            items = tuple((0, offsets[q], width // portions[q][1], (at,)) for q, at in zip(inside, places))
+            last = sums[p] = send(items, False, width, after(place), out_weight, turned, arrays)
         elif s == "gate":
-            fars = [received[p, s, 0] for s in range(1, len(bits))]
+            later = range(1, len(bits))
+            arrays, places = collect([(q, i, 0) for q in inside for i in later])
+            pieces = tuple(
+                (
+                    offsets[q] - p * half_rows,
+                    width // portions[q][1],
+                    tuple(places[i * len(later) : (i + 1) * len(later)]),
+                )
+                for i, q in enumerate(inside)
+            )
+            copies = 1 if GATHERED[p] else groups
             grad_query, grad_conv, state, packed = gate(
-                p, rows, segments, after(sums[p]), fars, query_in, conv_out, decay, grad_query
+                p, half_rows, segments, copies, pieces, after(sums[p]), arrays, query_in, conv_out, decay, grad_query
             )
             last, gated[p] = packed, (grad_conv, state)
-            laters[p] = [
-                lax.ppermute(packed, "ctx", [(i, i - hop) for i in range(hop, groups)]) for hop in range(1, groups)
-            ]
+            if GATHERED[p]:
+                states[p] = lax.all_gather(packed, "ctx", tiled=True)
+            else:
+                states[p] = lax.all_to_all(packed, "ctx", 0, 0, tiled=True)
         elif s == "scan":
             last = scanned[p] = scan(p, segments, *gated[p], decay, residue)
         elif s == "fix":
-            grad_input = fix(
-                p, rows, segments, after(scanned[p]), laters[p], decay, residue, toks, width, grad_input
+            last = grad_input = fix(
+                p, half_rows, segments, group, after(scanned[p]), states[p], decay, residue, toks, width, grad_input
             )
         else:
-            (block,), bit = block, bits[s]
+            route, part, _ = portions[p]
+            rows, (blocks,) = width // part, blocks
+            bit = bits[route[s]]
             if last is None:
-                last, turned = first_send(rows, block ^ bit, p * rows, width, place, out_weight, out_grad)
+                last, turned = first_send(rows, blocks[0] ^ bit, offsets[p], width, place, out_weight, out_grad)
             else:
-                nears = [received[p, i, block ^ bit] for i in range(s)]
-                last = send(rows, block ^ bit, p * rows, width, True, after(place), out_weight, turned, nears)
-            received[p, s, block] = lax.ppermute(last, "ch", [(i, i ^ bit) for i in range(size)])
+                wanted = [(p, i, block ^ bit) for block in blocks for i in range(s)]
+                arrays, places = collect(wanted)
+                items = tuple(
+                    (block ^ bit, offsets[p], rows, tuple(places[i * s : (i + 1) * s]))
+                    for i, block in enumerate(blocks)
+                )
+                last = send(items, True, width, after(place), out_weight, turned, arrays)
+            arrived = lax.ppermute(last, "ch", [(i, i ^ bit) for i in range(size)])
+            for i, block in enumerate(blocks):
+                received[p, s, block] = (arrived, i * (rows + PEAKS))
     return grad_query, grad_input
 
 

time: 75.8 us -> 80.9 us (1.067)
  blocking collectives: 0 us -> 5.52 us
  starting transfers between devices: 33.6 us -> 31.5 us
    all_gather x0 -> x1, blocking collectives: none -> 5.52 us  [local(): states[p] = lax.all_gather(packed, 'ctx', tiled=True)]
    ppermute x20 -> x14, starting transfers between devices: 33.6 us -> 28.2 us  [local(): arrived = lax.ppermute(last, 'ch', [(i, i ^ bit) for i in range(size)])]
    all_to_all x0 -> x1, starting transfers between devices: none -> 3.33 us  [local(): states[p] = lax.all_to_all(packed, 'ctx', 0, 0, tiled=True)]
    ppermute x20 -> x14, waiting for transfers between devices: 17.5 us -> 17.8 us  [local(): arrived = lax.ppermute(last, 'ch', [(i, i ^ bit) for i in range(size)])]
  transfers between devices with their start and end apart: 20 -> 15, of which waited for: 9 -> 9; matrix products, arithmetic and copies ran while one was open for 0% -> 0% of each run, Pallas kernels for 24% -> 21%
where the time goes in v5:
time: 80.9 us; the launch traced here: 79.9 us
  starting transfers between devices  31.5 us (39%)
  Pallas kernels  23.2 us (29%)
  waiting for transfers between devices  17.8 us (22%)
  blocking collectives  5.52 us (7%)
  local copies, waits for them, and re-layouts  0.94 us (1%)
  between operations  0.94 us (1%)
    ppermute x14, starting transfers between devices, local(): arrived = lax.ppermute(last, 'ch', [(i, i ^ bit) for i in range(size)])  28.2 us
    ppermute x14, waiting for transfers between devices, local(): arrived = lax.ppermute(last, 'ch', [(i, i ^ bit) for i in range(size)])  17.8 us
    pallas_call x15, Pallas kernels, send(): pl.pallas_call(functools.partial(send_kernel, items, coded, width, len(ne...  10.2 us
    all_gather x1, blocking collectives, local(): states[p] = lax.all_gather(packed, 'ctx', tiled=True)  5.52 us
    pallas_call x2, Pallas kernels, fix(): pl.pallas_call(functools.partial(fix_kernel, half, segments), in_specs=[p...  3.72 us
    pallas_call x2, Pallas kernels, scan(): pl.pallas_call(functools.partial(scan_kernel, half, segments), in_specs=[...  3.47 us
    pallas_call x2, Pallas kernels, gate(): pl.pallas_call(functools.partial(gate_kernel, half, rows, segments, piece...  3.42 us
    all_to_all x1, starting transfers between devices, local(): states[p] = lax.all_to_all(packed, 'ctx', 0, 0, tiled=True)  3.33 us
  transfers between devices with their start and end apart: 15, of which 9 were waited for; matrix products, arithmetic and copies ran while one was open for 0% of the time, Pallas kernels for 21%

profile of v5, /device:TPU:0, one launch (start us, length us, event | category | flops | bytes accessed | tf_op | source)
XLA Modules:
  0.0 79.9 jit_solution(7225113684320821675)
XLA Ops:
  0.6 0.0 copy-start
  0.6 2.4 %shard_map.77 = (bf16[528,256]{1,0:T(8,128)(2,1)S(1)}, bf16[1024,256]{1,0:T(8,128)(2,1)S(1)}) custom-call(s32[1]{0:T(128)} %bitcast.place_ref, bf16[8192,1024]{1,0:T(8,128)(2,1)} %w_ref.29, bf16[256,1024]{1,0:T(8,128)(2,1)} %g_hbm.1), custom_call_target="tpu_custom_call" | custom-call | bytes 1024 | tf_op jit(solution)/shard_map/pallas_call | solution.py:133
  3.1 3.0 %collective-permute-start = (bf16[528,256]{1,0:T(8,128)(2,1)S(1)}, bf16[528,256]{1,0:T(8,128)(2,1)S(1)}, u32[]{:S(2)}, u32[]{:S(2)}) collective-permute-start(bf16[528,256]{1,0:T(8,128)(2,1)S(1)} %get-tuple-element.30), channel_id=1, source_target_pairs={{0,1},{1,0},{2,3},{3,2},{4,5},{5,4},{6,7},{7,6},{8,9},{9,8},{10,11... | collective-permute-start | bytes 811016 | tf_op jit(solution)/shard_map/ppermute | solution.py:438
  6.1 0.8 copy-done
  6.9 0.6 shard_map.78
  7.5 0.6 shard_map.79
  8.1 0.6 shard_map.80
  8.8 3.0 %collective-permute-start.1 = (bf16[528,256]{1,0:T(8,128)(2,1)S(1)}, bf16[528,256]{1,0:T(8,128)(2,1)S(1)}, u32[]{:S(2)}, u32[]{:S(2)}) collective-permute-start(bf16[528,256]{1,0:T(8,128)(2,1)S(1)} %shard_map.80), channel_id=1, source_target_pairs={{0,1},{1,0},{2,3},{3,2},{4,5},{5,4},{6,7},{7,6},{8,9},{9,8},{10,11... | collective-permute-start | bytes 811016 | tf_op jit(solution)/shard_map/ppermute | solution.py:438
  11.8 0.6 shard_map.81
  12.4 0.6 shard_map.82
  13.1 0.6 shard_map.83
  13.7 0.1 collective-permute-start.2
  13.8 2.0 %collective-permute-start.3 = (bf16[528,256]{1,0:T(8,128)(2,1)S(1)}, bf16[528,256]{1,0:T(8,128)(2,1)S(1)}, u32[]{:S(2)}, u32[]{:S(2)}) collective-permute-start(bf16[528,256]{1,0:T(8,128)(2,1)S(1)} %shard_map.78), channel_id=1, source_target_pairs={{0,1},{1,0},{2,3},{3,2},{4,5},{5,4},{6,7},{7,6},{8,9},{9,8},{10,11... | collective-permute-start | bytes 811016 | tf_op jit(solution)/shard_map/ppermute | solution.py:438
  15.8 0.0 collective-permute-done.refs_0_
  15.8 0.7 shard_map.84
  16.6 1.6 %collective-permute-start.4 = (bf16[528,256]{1,0:T(8,128)(2,1)S(1)}, bf16[528,256]{1,0:T(8,128)(2,1)S(1)}, u32[]{:S(2)}, u32[]{:S(2)}) collective-permute-start(bf16[528,256]{1,0:T(8,128)(2,1)S(1)} %shard_map.84), channel_id=1, source_target_pairs={{0,2},{1,3},{2,0},{3,1},{4,6},{5,7},{6,4},{7,5},{8,10},{9,11},{10,... | collective-permute-start | bytes 811016 | tf_op jit(solution)/shard_map/ppermute | solution.py:438
  18.2 0.5 collective-permute-start.5
  18.7 0.4 collective-permute-done.1.refs_0_
  19.1 2.1 %collective-permute-start.6 = (bf16[528,256]{1,0:T(8,128)(2,1)S(1)}, bf16[528,256]{1,0:T(8,128)(2,1)S(1)}, u32[]{:S(2)}, u32[]{:S(2)}) collective-permute-start(bf16[528,256]{1,0:T(8,128)(2,1)S(1)} %shard_map.82), channel_id=1, source_target_pairs={{0,1},{1,0},{2,3},{3,2},{4,5},{5,4},{6,7},{7,6},{8,9},{9,8},{10,11... | collective-permute-start | bytes 811016 | tf_op jit(solution)/shard_map/ppermute | solution.py:438
  21.2 0.7 shard_map.85
  21.9 0.6 shard_map.86
  22.6 2.3 %collective-permute-done.2.refs_0_ = bf16[528,256]{1,0:T(8,128)(2,1)S(1)} collective-permute-done((bf16[528,256]{1,0:T(8,128)(2,1)S(1)}, bf16[528,256]{1,0:T(8,128)(2,1)S(1)}, u32[]{:S(2)}, u32[]{:S(2)}) %collective-permute-start.2) | collective-permute-done | bytes 270368 | tf_op jit(solution)/shard_map/ppermute | solution.py:438
  24.9 0.7 shard_map.87
  25.7 2.2 %collective-permute-start.7 = (bf16[528,256]{1,0:T(8,128)(2,1)S(1)}, bf16[528,256]{1,0:T(8,128)(2,1)S(1)}, u32[]{:S(2)}, u32[]{:S(2)}) collective-permute-start(bf16[528,256]{1,0:T(8,128)(2,1)S(1)} %shard_map.87), channel_id=1, source_target_pairs={{0,2},{1,3},{2,0},{3,1},{4,6},{5,7},{6,4},{7,5},{8,10},{9,11},{10,... | collective-permute-start | bytes 811016 | tf_op jit(solution)/shard_map/ppermute | solution.py:438
  27.9 2.9 %collective-permute-done.3.refs_0_ = bf16[528,256]{1,0:T(8,128)(2,1)S(1)} collective-permute-done((bf16[528,256]{1,0:T(8,128)(2,1)S(1)}, bf16[528,256]{1,0:T(8,128)(2,1)S(1)}, u32[]{:S(2)}, u32[]{:S(2)}) %collective-permute-start.3) | collective-permute-done | bytes 270368 | tf_op jit(solution)/shard_map/ppermute | solution.py:438
  30.7 2.1 %collective-permute-start.8 = (bf16[528,256]{1,0:T(8,128)(2,1)S(1)}, bf16[528,256]{1,0:T(8,128)(2,1)S(1)}, u32[]{:S(2)}, u32[]{:S(2)}) collective-permute-start(bf16[528,256]{1,0:T(8,128)(2,1)S(1)} %shard_map.81), channel_id=1, source_target_pairs={{0,1},{1,0},{2,3},{3,2},{4,5},{5,4},{6,7},{7,6},{8,9},{9,8},{10,11... | collective-permute-start | bytes 811016 | tf_op jit(solution)/shard_map/ppermute | solution.py:438
  32.8 0.0 collective-permute-done.4.refs_1_
  32.8 1.6 %collective-permute-start.9 = (bf16[528,256]{1,0:T(8,128)(2,1)S(1)}, bf16[528,256]{1,0:T(8,128)(2,1)S(1)}, u32[]{:S(2)}, u32[]{:S(2)}) collective-permute-start(bf16[528,256]{1,0:T(8,128)(2,1)S(1)} %shard_map.85), channel_id=1, source_target_pairs={{0,2},{1,3},{2,0},{3,1},{4,6},{5,7},{6,4},{7,5},{8,10},{9,11},{10,... | collective-permute-start | bytes 811016 | tf_op jit(solution)/shard_map/ppermute | solution.py:438
  34.4 0.9 %shard_map.88 = bf16[528,256]{1,0:T(8,128)(2,1)S(1)} custom-call(s32[1]{0:T(128)} %bitcast.place_ref, bf16[8192,1024]{1,0:T(8,128)(2,1)S(1)} %copy-done, bf16[1024,256]{1,0:T(8,128)(2,1)S(1)} %get-tuple-element.32.turned_ref, bf16[528,256]{1,0:T(8,128)(2,1)S(1)} %collective-permute-done.3.refs_0_, bf16[528,256]{1,0:T(8,128)(2,1)S(1)} %collective-permute-done.4.refs_1_), custom_call_target="tpu_custom_call" | custom-call | bytes 1024 | tf_op jit(solution)/shard_map/pallas_call | solution.py:94
  35.3 0.0 copy-start.3
  35.3 0.0 copy-start.4
  35.3 1.2 %collective-permute-done.5.refs_0_ = bf16[528,256]{1,0:T(8,128)(2,1)S(1)} collective-permute-done((bf16[528,256]{1,0:T(8,128)(2,1)S(1)}, bf16[528,256]{1,0:T(8,128)(2,1)S(1)}, u32[]{:S(2)}, u32[]{:S(2)}) %collective-permute-start.5) | collective-permute-done | bytes 270368 | tf_op jit(solution)/shard_map/ppermute | solution.py:438
  36.5 3.1 %collective-permute-start.10 = (bf16[528,256]{1,0:T(8,128)(2,1)S(1)}, bf16[528,256]{1,0:T(8,128)(2,1)S(1)}, u32[]{:S(2)}, u32[]{:S(2)}) collective-permute-start(bf16[528,256]{1,0:T(8,128)(2,1)S(1)} %shard_map.88), channel_id=1, source_target_pairs={{0,4},{1,5},{2,6},{3,7},{4,0},{5,1},{6,2},{7,3},{8,12},{9,13},{10,... | collective-permute-start | bytes 811016 | tf_op jit(solution)/shard_map/ppermute | solution.py:438
  39.6 0.7 shard_map.89
  40.4 0.0 copy-start.1
  40.4 0.0 copy-start.2
  40.4 1.9 %collective-permute-done.6.refs_0_ = bf16[528,256]{1,0:T(8,128)(2,1)S(1)} collective-permute-done((bf16[528,256]{1,0:T(8,128)(2,1)S(1)}, bf16[528,256]{1,0:T(8,128)(2,1)S(1)}, u32[]{:S(2)}, u32[]{:S(2)}) %collective-permute-start.6) | collective-permute-done | bytes 270368 | tf_op jit(solution)/shard_map/ppermute | solution.py:438
  42.3 2.1 %collective-permute-start.11 = (bf16[528,256]{1,0:T(8,128)(2,1)S(1)}, bf16[528,256]{1,0:T(8,128)(2,1)S(1)}, u32[]{:S(2)}, u32[]{:S(2)}) collective-permute-start(bf16[528,256]{1,0:T(8,128)(2,1)S(1)} %shard_map.86), channel_id=1, source_target_pairs={{0,1},{1,0},{2,3},{3,2},{4,5},{5,4},{6,7},{7,6},{8,9},{9,8},{10,11... | collective-permute-start | bytes 811016 | tf_op jit(solution)/shard_map/ppermute | solution.py:438
  44.4 0.0 collective-permute-done.7.refs_1_
  44.4 0.9 %shard_map.90 = bf16[528,256]{1,0:T(8,128)(2,1)S(1)} custom-call(s32[1]{0:T(128)} %bitcast.place_ref, bf16[8192,1024]{1,0:T(8,128)(2,1)S(1)} %copy-done, bf16[1024,256]{1,0:T(8,128)(2,1)S(1)} %get-tuple-element.32.turned_ref, bf16[528,256]{1,0:T(8,128)(2,1)S(1)} %collective-permute-done.6.refs_0_, bf16[528,256]{1,0:T(8,128)(2,1)S(1)} %collective-permute-done.7.refs_1_), custom_call_target="tpu_custom_call" | custom-call | bytes 1024 | tf_op jit(solution)/shard_map/pallas_call | solution.py:94
  45.3 2.7 %collective-permute-start.13 = (bf16[528,256]{1,0:T(8,128)(2,1)S(1)}, bf16[528,256]{1,0:T(8,128)(2,1)S(1)}, u32[]{:S(2)}, u32[]{:S(2)}) collective-permute-start(bf16[528,256]{1,0:T(8,128)(2,1)S(1)} %shard_map.90), channel_id=1, source_target_pairs={{0,4},{1,5},{2,6},{3,7},{4,0},{5,1},{6,2},{7,3},{8,12},{9,13},{10,... | collective-permute-start | bytes 811016 | tf_op jit(solution)/shard_map/ppermute | solution.py:438
  47.9 0.1 collective-permute-done.8.refs_0_
  48.1 2.1 %collective-permute-start.12 = (bf16[528,256]{1,0:T(8,128)(2,1)S(1)}, bf16[528,256]{1,0:T(8,128)(2,1)S(1)}, u32[]{:S(2)}, u32[]{:S(2)}) collective-permute-start(bf16[528,256]{1,0:T(8,128)(2,1)S(1)} %shard_map.89), channel_id=1, source_target_pairs={{0,2},{1,3},{2,0},{3,1},{4,6},{5,7},{6,4},{7,5},{8,10},{9,11},{10,... | collective-permute-start | bytes 811016 | tf_op jit(solution)/shard_map/ppermute | solution.py:438
  50.2 0.0 copy-done.3
  50.2 0.0 copy-done.4
  50.3 0.5 shard_map.91.acc_ref
  50.8 0.0 collective-permute-done.9.refs_0_
  50.8 7.1 %collective-permute-done.10.refs_1_ = bf16[528,256]{1,0:T(8,128)(2,1)S(1)} collective-permute-done((bf16[528,256]{1,0:T(8,128)(2,1)S(1)}, bf16[528,256]{1,0:T(8,128)(2,1)S(1)}, u32[]{:S(2)}, u32[]{:S(2)}) %collective-permute-start.10) | collective-permute-done | bytes 270368 | tf_op jit(solution)/shard_map/ppermute | solution.py:438
  57.9 0.0 copy-done.1
  57.9 0.0 copy-done.2
  57.9 1.4 %shard_map.92 = (bf16[256,1024]{1,0:T(8,128)(2,1)}, f32[1024,128]{1,0:T(8,128)S(1)}, f32[16,8,128]{2,1,0:T(8,128)S(1)}, f32[1,8,8,128]{3,2,1,0:T(8,128)S(1)}) custom-call(f32[512,256]{1,0:T(8,128)S(1)} %shard_map.91.acc_ref, bf16[528,256]{1,0:T(8,128)(2,1)S(1)} %collective-permute-done.9.refs_0_, bf16[528,256]{1,0:T(8,128)(2,1)S(1)} %collective-permute-done.10.refs_1_, ...), custom_call_target="tpu_custom_call" | custom-call | bytes 1024 | tf_op jit(solution)/shard_map/pallas_call | solution.py:233
  59.4 1.7 %shard_map.94.rows_in_ref = f32[1024,128]{1,0:T(8,128)S(1)} custom-call(f32[1024,128]{1,0:T(8,128)S(1)} %get-tuple-element.48.gc_ref, f32[16,8,128]{2,1,0:T(8,128)S(1)} %get-tuple-element.49.state_ref, f32[16,16,128]{2,1,0:T(8,128)S(1)} %bitcast.11, f32[16,16,128]{2,1,0:T(8,128)S(1)} %bitcast.16), custom_call_target="tpu_custom_call" | custom-call | bytes 1024 | tf_op jit(solution)/shard_map/pallas_call | solution.py:283
  61.1 0.0 collective-permute-done.11.refs_0_
  61.1 0.5 shard_map.93.acc_ref
  61.6 0.2 collective-permute-done.13.refs_1_
  61.8 1.7 %collective-permute-done.12.refs_0_ = bf16[528,256]{1,0:T(8,128)(2,1)S(1)} collective-permute-done((bf16[528,256]{1,0:T(8,128)(2,1)S(1)}, bf16[528,256]{1,0:T(8,128)(2,1)S(1)}, u32[]{:S(2)}, u32[]{:S(2)}) %collective-permute-start.12) | collective-permute-done | bytes 270368 | tf_op jit(solution)/shard_map/ppermute | solution.py:438
  63.5 2.0 %shard_map.95 = (bf16[256,1024]{1,0:T(8,128)(2,1)}, f32[1024,128]{1,0:T(8,128)S(1)}, f32[16,8,128]{2,1,0:T(8,128)S(1)}, f32[4,8,8,128]{3,2,1,0:T(8,128)}) custom-call(f32[512,256]{1,0:T(8,128)S(1)} %shard_map.93.acc_ref, bf16[528,256]{1,0:T(8,128)(2,1)S(1)} %collective-permute-done.12.refs_0_, ...), custom_call_target="tpu_custom_call", output_to_operand_aliasing={{0}: (6, {})} | custom-call | bytes 1024 | tf_op jit(solution)/shard_map/pallas_call | solution.py:233
  65.5 3.3 %all-to-all-start = ((f32[4,8,8,128]{3,2,1,0:T(8,128)}), f32[4,8,8,128]{3,2,1,0:T(8,128)S(1)}, u32[]{:S(2)}, u32[]{:S(2)}) async-start(f32[4,8,8,128]{3,2,1,0:T(8,128)} %get-tuple-element.57), calls=%async_computation | async-start | bytes 262144 | tf_op jit(solution)/shard_map/all_to_all | solution.py:417
  68.9 1.7 %shard_map.96.rows_in_ref = f32[1024,128]{1,0:T(8,128)S(1)} custom-call(f32[1024,128]{1,0:T(8,128)S(1)} %get-tuple-element.53.gc_ref, f32[16,8,128]{2,1,0:T(8,128)S(1)} %get-tuple-element.54.state_ref, f32[16,16,128]{2,1,0:T(8,128)S(1)} %bitcast.13, f32[16,16,128]{2,1,0:T(8,128)S(1)} %bitcast.17), custom_call_target="tpu_custom_call" | custom-call | bytes 1024 | tf_op jit(solution)/shard_map/pallas_call | solution.py:283
  70.6 5.5 %all_gather.3.states_ref = f32[4,8,8,128]{3,2,1,0:T(8,128)S(1)} all-gather(f32[1,8,8,128]{3,2,1,0:T(8,128)S(1)} %get-tuple-element.46), channel_id=1, replica_groups=mesh['ctx'=4,'ch'=8] {'ctx'}, dimensions={0}, use_global_device_ids=true | all-gather | bytes 163840 | tf_op jit(solution)/shard_map/all_gather | solution.py:415
  76.1 1.9 %shard_map.97.refs_0_ = bf16[256,1024]{1,0:T(8,128)(2,1)} custom-call(s32[1]{0:T(128)} %bitcast.5.group_ref, f32[1024,128]{1,0:T(8,128)S(1)} %shard_map.94.rows_in_ref, f32[4,8,8,128]{3,2,1,0:T(8,128)S(1)} %all_gather.3.states_ref, f32[16,16,128]{2,1,0:T(8,128)S(1)} %bitcast.14, f32[16,16,128]{2,1,0:T(8,128)S(1)} %bitcast.18), custom_call_target="tpu_custom_call" | custom-call | bytes 1024 | tf_op jit(solution)/shard_map/pallas_call | solution.py:335
  78.0 0.0 all-to-all-done.states_ref
  78.0 1.9 %shard_map.98 = bf16[256,1024]{1,0:T(8,128)(2,1)} custom-call(s32[1]{0:T(128)} %bitcast.5.group_ref, f32[1024,128]{1,0:T(8,128)S(1)} %shard_map.96.rows_in_ref, f32[4,8,8,128]{3,2,1,0:T(8,128)S(1)} %all-to-all-done.states_ref, f32[16,16,128]{2,1,0:T(8,128)S(1)} %bitcast.15, f32[16,16,128]{2,1,0:T(8,128)S(1)} %bitcast.19, ...), custom_call_target="tpu_custom_call", output_to_operand_aliasing={{}: (5, {})} | custom-call | bytes 1024 | tf_op jit(solution)/shard_map/pallas_call | solution.py:335
  (4 shorter events, 0.1 us)
Async XLA Ops:
  0.6 6.2 %copy-start = (bf16[8192,1024]{1,0:T(8,128)(2,1)S(1)}, bf16[8192,1024]{1,0:T(8,128)(2,1)}, u32[]{:S(2)}) copy-start(bf16[8192,1024]{1,0:T(8,128)(2,1)} %w_ref.29) | copy-start | bytes 50331652
  3.1 12.8 %collective-permute-start = (bf16[528,256]{1,0:T(8,128)(2,1)S(1)}, bf16[528,256]{1,0:T(8,128)(2,1)S(1)}, u32[]{:S(2)}, u32[]{:S(2)}) collective-permute-start(bf16[528,256]{1,0:T(8,128)(2,1)S(1)} %get-tuple-element.30), channel_id=1, source_target_pairs={{0,1},{1,0},{2,3},{3,2},{4,5},{5,4},{6,7},{7,6},{8,9},{9,8},{10,11... | collective-permute-start | bytes 811016 | tf_op jit(solution)/shard_map/ppermute | solution.py:438
  8.8 10.3 %collective-permute-start.1 = (bf16[528,256]{1,0:T(8,128)(2,1)S(1)}, bf16[528,256]{1,0:T(8,128)(2,1)S(1)}, u32[]{:S(2)}, u32[]{:S(2)}) collective-permute-start(bf16[528,256]{1,0:T(8,128)(2,1)S(1)} %shard_map.80), channel_id=1, source_target_pairs={{0,1},{1,0},{2,3},{3,2},{4,5},{5,4},{6,7},{7,6},{8,9},{9,8},{10,11... | collective-permute-start | bytes 811016 | tf_op jit(solution)/shard_map/ppermute | solution.py:438
  13.7 11.2 %collective-permute-start.2 = (bf16[528,256]{1,0:T(8,128)(2,1)S(1)}, bf16[528,256]{1,0:T(8,128)(2,1)S(1)}, u32[]{:S(2)}, u32[]{:S(2)}) collective-permute-start(bf16[528,256]{1,0:T(8,128)(2,1)S(1)} %shard_map.83), channel_id=1, source_target_pairs={{0,1},{1,0},{2,3},{3,2},{4,5},{5,4},{6,7},{7,6},{8,9},{9,8},{10,11... | collective-permute-start | bytes 811016 | tf_op jit(solution)/shard_map/ppermute | solution.py:438
  13.8 16.9 %collective-permute-start.3 = (bf16[528,256]{1,0:T(8,128)(2,1)S(1)}, bf16[528,256]{1,0:T(8,128)(2,1)S(1)}, u32[]{:S(2)}, u32[]{:S(2)}) collective-permute-start(bf16[528,256]{1,0:T(8,128)(2,1)S(1)} %shard_map.78), channel_id=1, source_target_pairs={{0,1},{1,0},{2,3},{3,2},{4,5},{5,4},{6,7},{7,6},{8,9},{9,8},{10,11... | collective-permute-start | bytes 811016 | tf_op jit(solution)/shard_map/ppermute | solution.py:438
  16.6 16.2 %collective-permute-start.4 = (bf16[528,256]{1,0:T(8,128)(2,1)S(1)}, bf16[528,256]{1,0:T(8,128)(2,1)S(1)}, u32[]{:S(2)}, u32[]{:S(2)}) collective-permute-start(bf16[528,256]{1,0:T(8,128)(2,1)S(1)} %shard_map.84), channel_id=1, source_target_pairs={{0,2},{1,3},{2,0},{3,1},{4,6},{5,7},{6,4},{7,5},{8,10},{9,11},{10,... | collective-permute-start | bytes 811016 | tf_op jit(solution)/shard_map/ppermute | solution.py:438
  18.2 18.3 %collective-permute-start.5 = (bf16[528,256]{1,0:T(8,128)(2,1)S(1)}, bf16[528,256]{1,0:T(8,128)(2,1)S(1)}, u32[]{:S(2)}, u32[]{:S(2)}) collective-permute-start(bf16[528,256]{1,0:T(8,128)(2,1)S(1)} %shard_map.79), channel_id=1, source_target_pairs={{0,1},{1,0},{2,3},{3,2},{4,5},{5,4},{6,7},{7,6},{8,9},{9,8},{10,11... | collective-permute-start | bytes 811016 | tf_op jit(solution)/shard_map/ppermute | solution.py:438
  19.1 23.2 %collective-permute-start.6 = (bf16[528,256]{1,0:T(8,128)(2,1)S(1)}, bf16[528,256]{1,0:T(8,128)(2,1)S(1)}, u32[]{:S(2)}, u32[]{:S(2)}) collective-permute-start(bf16[528,256]{1,0:T(8,128)(2,1)S(1)} %shard_map.82), channel_id=1, source_target_pairs={{0,1},{1,0},{2,3},{3,2},{4,5},{5,4},{6,7},{7,6},{8,9},{9,8},{10,11... | collective-permute-start | bytes 811016 | tf_op jit(solution)/shard_map/ppermute | solution.py:438
  25.7 18.7 %collective-permute-start.7 = (bf16[528,256]{1,0:T(8,128)(2,1)S(1)}, bf16[528,256]{1,0:T(8,128)(2,1)S(1)}, u32[]{:S(2)}, u32[]{:S(2)}) collective-permute-start(bf16[528,256]{1,0:T(8,128)(2,1)S(1)} %shard_map.87), channel_id=1, source_target_pairs={{0,2},{1,3},{2,0},{3,1},{4,6},{5,7},{6,4},{7,5},{8,10},{9,11},{10,... | collective-permute-start | bytes 811016 | tf_op jit(solution)/shard_map/ppermute | solution.py:438
  30.7 17.4 %collective-permute-start.8 = (bf16[528,256]{1,0:T(8,128)(2,1)S(1)}, bf16[528,256]{1,0:T(8,128)(2,1)S(1)}, u32[]{:S(2)}, u32[]{:S(2)}) collective-permute-start(bf16[528,256]{1,0:T(8,128)(2,1)S(1)} %shard_map.81), channel_id=1, source_target_pairs={{0,1},{1,0},{2,3},{3,2},{4,5},{5,4},{6,7},{7,6},{8,9},{9,8},{10,11... | collective-permute-start | bytes 811016 | tf_op jit(solution)/shard_map/ppermute | solution.py:438
  32.8 18.0 %collective-permute-start.9 = (bf16[528,256]{1,0:T(8,128)(2,1)S(1)}, bf16[528,256]{1,0:T(8,128)(2,1)S(1)}, u32[]{:S(2)}, u32[]{:S(2)}) collective-permute-start(bf16[528,256]{1,0:T(8,128)(2,1)S(1)} %shard_map.85), channel_id=1, source_target_pairs={{0,2},{1,3},{2,0},{3,1},{4,6},{5,7},{6,4},{7,5},{8,10},{9,11},{10,... | collective-permute-start | bytes 811016 | tf_op jit(solution)/shard_map/ppermute | solution.py:438
  35.3 14.9 %copy-start.3 = (f32[1024,16]{0,1:T(8,128)S(1)}, f32[1024,16]{0,1:T(8,128)}, u32[]{:S(2)}) copy-start(f32[1024,16]{0,1:T(8,128)} %param.11) | copy-start | bytes 196612
  35.3 14.9 %copy-start.4 = (f32[1024,16]{0,1:T(8,128)S(1)}, f32[1024,16]{0,1:T(8,128)}, u32[]{:S(2)}) copy-start(f32[1024,16]{0,1:T(8,128)} %param.10) | copy-start | bytes 196612
  36.5 21.3 %collective-permute-start.10 = (bf16[528,256]{1,0:T(8,128)(2,1)S(1)}, bf16[528,256]{1,0:T(8,128)(2,1)S(1)}, u32[]{:S(2)}, u32[]{:S(2)}) collective-permute-start(bf16[528,256]{1,0:T(8,128)(2,1)S(1)} %shard_map.88), channel_id=1, source_target_pairs={{0,4},{1,5},{2,6},{3,7},{4,0},{5,1},{6,2},{7,3},{8,12},{9,13},{10,... | collective-permute-start | bytes 811016 | tf_op jit(solution)/shard_map/ppermute | solution.py:438
  40.4 17.5 %copy-start.1 = (bf16[256,1024]{1,0:T(8,128)(2,1)S(1)}, bf16[256,1024]{1,0:T(8,128)(2,1)}, u32[]{:S(2)}) copy-start(bf16[256,1024]{1,0:T(8,128)(2,1)} %refs_2_.3) | copy-start | bytes 1572868
  40.4 17.5 %copy-start.2 = (bf16[256,1024]{1,0:T(8,128)(2,1)S(1)}, bf16[256,1024]{1,0:T(8,128)(2,1)}, u32[]{:S(2)}) copy-start(bf16[256,1024]{1,0:T(8,128)(2,1)} %refs_3_.3) | copy-start | bytes 1572868
  42.3 18.8 %collective-permute-start.11 = (bf16[528,256]{1,0:T(8,128)(2,1)S(1)}, bf16[528,256]{1,0:T(8,128)(2,1)S(1)}, u32[]{:S(2)}, u32[]{:S(2)}) collective-permute-start(bf16[528,256]{1,0:T(8,128)(2,1)S(1)} %shard_map.86), channel_id=1, source_target_pairs={{0,1},{1,0},{2,3},{3,2},{4,5},{5,4},{6,7},{7,6},{8,9},{9,8},{10,11... | collective-permute-start | bytes 811016 | tf_op jit(solution)/shard_map/ppermute | solution.py:438
  45.3 16.5 %collective-permute-start.13 = (bf16[528,256]{1,0:T(8,128)(2,1)S(1)}, bf16[528,256]{1,0:T(8,128)(2,1)S(1)}, u32[]{:S(2)}, u32[]{:S(2)}) collective-permute-start(bf16[528,256]{1,0:T(8,128)(2,1)S(1)} %shard_map.90), channel_id=1, source_target_pairs={{0,4},{1,5},{2,6},{3,7},{4,0},{5,1},{6,2},{7,3},{8,12},{9,13},{10,... | collective-permute-start | bytes 811016 | tf_op jit(solution)/shard_map/ppermute | solution.py:438
  48.1 15.4 %collective-permute-start.12 = (bf16[528,256]{1,0:T(8,128)(2,1)S(1)}, bf16[528,256]{1,0:T(8,128)(2,1)S(1)}, u32[]{:S(2)}, u32[]{:S(2)}) collective-permute-start(bf16[528,256]{1,0:T(8,128)(2,1)S(1)} %shard_map.89), channel_id=1, source_target_pairs={{0,2},{1,3},{2,0},{3,1},{4,6},{5,7},{6,4},{7,5},{8,10},{9,11},{10,... | collective-permute-start | bytes 811016 | tf_op jit(solution)/shard_map/ppermute | solution.py:438
  65.5 12.5 %all-to-all-start = ((f32[4,8,8,128]{3,2,1,0:T(8,128)}), f32[4,8,8,128]{3,2,1,0:T(8,128)S(1)}, u32[]{:S(2)}, u32[]{:S(2)}) async-start(f32[4,8,8,128]{3,2,1,0:T(8,128)} %get-tuple-element.57), calls=%async_computation | async-start | bytes 262144 | tf_op jit(solution)/shard_map/all_to_all | solution.py:417

commit v6 on v5

--- a/solution.py
+++ b/solution.py
@@ -15,17 +15,16 @@
 VMEM = 24 * 1024 * 1024
 QUICK = pl.CostEstimate(flops=0, bytes_accessed=1024, transcendentals=0)
 
-PORTIONS = (((0, 1, 2), 2, 0), ((0, 1, 2), 2, 1))
+PORTIONS = (((0, 1, 2), 2, 0), ((0, 1, 2), 4, 1), ((1, 0, 2), 4, 1))
 ORDER = (
-    (0, 0, (6,)), (0, 0, (4,)), (1, 0, (2,)), (0, 0, (2,)), (0, 0, (0,)), (1, 0, (4,)), (1, 0, (6,)), (0, 1, (4,)),
-    (0, 1, (0,)), (1, 0, (0,)), (1, 1, (4,)), (0, 2, (0,)), (1, 1, (0,)), (1, 2, (0,)), (0, "sum"), (0, "gate"),
-    (1, "sum"), (0, "scan"), (1, "gate"), (1, "scan"), (0, "fix"), (1, "fix"),
+    (0, 0, (6,)), (1, 0, (4,)), (1, 0, (6,)), (2, 0, (5, 4, 1, 0)), (0, 0, (4, 2)), (0, 1, (4,)), (0, 0, (0,)),
+    (1, 1, (4,)), (1, 0, (2,)), (2, 1, (4, 0)), (0, 1, (0,)), (0, 2, (0,)), (1, 1, (0,)), (0, "sum"), (1, 0, (0,)),
+    (1, 2, (0,)), (0, "gate"), (2, 2, (0,)), (0, "scan"), (1, "sum"), (1, "gate"), (0, "fix"), (1, "scan"), (1, "fix"),
 )
-GATHERED = (True, False)
-
-
-def part_of(rows):
-    return next(part for part in range(16, rows + 1, 16) if rows % part == 0 and rows // part <= PEAKS)
+
+
+def part_of(rows, blocks):
+    return next(part for part in range(16, rows + 1, 16) if rows % part == 0 and rows // part * blocks <= PEAKS)
 
 
 def step_of(rows):
@@ -45,13 +44,20 @@
     return jnp.concatenate(codes, axis=0).astype(jnp.bfloat16), peaks
 
 
-def decode(ref, base, rows, first, count):
-    part = part_of(rows)
-    peaks = ref[base + rows : base + rows + PEAKS, :].astype(jnp.float32) * (1.0 / SPAN)
+def put_peaks(peaks, out_ref):
+    if len(peaks) < PEAKS:
+        peaks = peaks + [jnp.zeros((PEAKS - len(peaks), peaks[0].shape[1]), jnp.float32)]
+    out_ref[out_ref.shape[0] - PEAKS :, :] = jnp.concatenate(peaks, axis=0).astype(jnp.bfloat16)
+
+
+def decode(ref, place, first, count):
+    start, peak, part = place
+    peaks = ref[ref.shape[0] - PEAKS :, :].astype(jnp.float32) * (1.0 / SPAN)
     blocks = []
-    for i in range(first // part, (first + count) // part):
-        code = ref[base + i * part : base + (i + 1) * part, :].astype(jnp.float32)
-        size = (jnp.log(jnp.abs(code)) + SHIFT) * peaks[i : i + 1, :]
+    for i in range(first // part, -(-(first + count) // part)):
+        low, high = max(first, i * part), min(first + count, (i + 1) * part)
+        code = ref[start + low : start + high, :].astype(jnp.float32)
+        size = (jnp.log(jnp.abs(code)) + SHIFT) * peaks[peak + i : peak + i + 1, :]
         blocks.append(jnp.where(code < 0, -size, size))
     return jnp.concatenate(blocks, axis=0)
 
@@ -62,35 +68,31 @@
 
 def send_kernel(items, coded, width, near, place_ref, w_ref, turned_ref, *refs):
     near_refs, out_ref = refs[:near], refs[near]
-    base = 0
+    base, peaks = 0, []
     for block, offset, rows, sources in items:
-        step, part = step_of(rows), part_of(rows)
+        step = step_of(rows)
         first = (place_ref[0] ^ block) * width + offset
-        peaks = []
         for at in range(0, rows, step):
             total = jnp.dot(
                 w_ref[pl.ds(pl.multiple_of(first + at, 16), step), :],
                 turned_ref[...],
                 preferred_element_type=jnp.float32,
             )
-            for source, start in sources:
-                total = total + decode(near_refs[source], start, rows, at, step)
+            for source, place in sources:
+                total = total + decode(near_refs[source], place, at, step)
             if coded:
-                total, more = encode(total, part)
+                total, more = encode(total, part_of(rows, len(items)))
                 peaks += more
             out_ref[base + at : base + at + step, :] = total
         base += rows
-        if coded:
-            if len(peaks) < PEAKS:
-                peaks.append(jnp.zeros((PEAKS - len(peaks), total.shape[1]), jnp.float32))
-            out_ref[base : base + PEAKS, :] = jnp.concatenate(peaks, axis=0).astype(jnp.bfloat16)
-            base += PEAKS
+    if coded:
+        put_peaks(peaks, out_ref)
 
 
 def send(items, coded, width, place, weight, turned, nears):
     toks = turned.shape[1]
     vmem = pl.BlockSpec(memory_space=pltpu.VMEM)
-    count = sum(rows + PEAKS if coded else rows for _, _, rows, _ in items)
+    count = sum(rows for _, _, rows, _ in items) + (PEAKS if coded else 0)
     return pl.pallas_call(
         functools.partial(send_kernel, items, coded, width, len(nears)),
         in_specs=[pl.BlockSpec(memory_space=pltpu.SMEM)] + [vmem] * (2 + len(nears)),
@@ -101,47 +103,54 @@
     )(place, weight, turned, *nears)
 
 
-def first_kernel(rows, block, offset, width, place_ref, w_hbm, g_hbm, out_ref, turned_ref, w_ref, g_ref, sems):
-    step = step_of(rows)
-    first = pl.multiple_of((place_ref[0] ^ block) * width + offset, 16)
+def first_kernel(items, width, place_ref, w_hbm, g_hbm, out_ref, turned_ref, w_ref, g_ref, sems):
     copies = [pltpu.make_async_copy(g_hbm, g_ref, sems.at[0])]
-    for i, at in enumerate(range(0, rows, step)):
-        copies.append(
-            pltpu.make_async_copy(w_hbm.at[pl.ds(first + at, step), :], w_ref.at[pl.ds(at, step), :], sems.at[1 + i])
-        )
+    base = 0
+    for block, offset, rows, _ in items:
+        step = step_of(rows)
+        first = pl.multiple_of((place_ref[0] ^ block) * width + offset, 16)
+        for at in range(0, rows, step):
+            copies.append(
+                pltpu.make_async_copy(
+                    w_hbm.at[pl.ds(first + at, step), :], w_ref.at[pl.ds(base + at, step), :], sems.at[len(copies)]
+                )
+            )
+        base += rows
     for copy in copies:
         copy.start()
     copies[0].wait()
     turned_ref[...] = g_ref[...].T
-    part = part_of(rows)
-    peaks = []
-    for i, at in enumerate(range(0, rows, step)):
-        copies[1 + i].wait()
-        total = jnp.dot(w_ref[at : at + step, :], turned_ref[...], preferred_element_type=jnp.float32)
-        total, more = encode(total, part)
-        peaks += more
-        out_ref[at : at + step, :] = total
-    if len(peaks) < PEAKS:
-        peaks.append(jnp.zeros((PEAKS - len(peaks), total.shape[1]), jnp.float32))
-    out_ref[rows:, :] = jnp.concatenate(peaks, axis=0).astype(jnp.bfloat16)
-
-
-def first_send(rows, block, offset, width, place, weight, grad):
+    base, peaks, waits = 0, [], iter(copies[1:])
+    for _, _, rows, _ in items:
+        step = step_of(rows)
+        for at in range(base, base + rows, step):
+            next(waits).wait()
+            total = jnp.dot(w_ref[at : at + step, :], turned_ref[...], preferred_element_type=jnp.float32)
+            total, more = encode(total, part_of(rows, len(items)))
+            peaks += more
+            out_ref[at : at + step, :] = total
+        base += rows
+    put_peaks(peaks, out_ref)
+
+
+def first_send(items, width, place, weight, grad):
     toks, depth = grad.shape
     vmem = pl.BlockSpec(memory_space=pltpu.VMEM)
     high = pl.BlockSpec(memory_space=pltpu.HBM)
+    count = sum(rows for _, _, rows, _ in items)
+    steps = sum(rows // step_of(rows) for _, _, rows, _ in items)
     return pl.pallas_call(
-        functools.partial(first_kernel, rows, block, offset, width),
+        functools.partial(first_kernel, items, width),
         in_specs=[pl.BlockSpec(memory_space=pltpu.SMEM), high, high],
         out_specs=(vmem, vmem),
         out_shape=(
-            jax.ShapeDtypeStruct((rows + PEAKS, toks), jnp.bfloat16),
+            jax.ShapeDtypeStruct((count + PEAKS, toks), jnp.bfloat16),
             jax.ShapeDtypeStruct((depth, toks), jnp.bfloat16),
         ),
         scratch_shapes=[
-            pltpu.VMEM((rows, depth), jnp.bfloat16),
+            pltpu.VMEM((count, depth), jnp.bfloat16),
             pltpu.VMEM((toks, depth), jnp.bfloat16),
-            pltpu.SemaphoreType.DMA((1 + rows // step_of(rows),)),
+            pltpu.SemaphoreType.DMA((1 + steps,)),
         ],
         compiler_params=pltpu.CompilerParams(vmem_limit_bytes=VMEM),
         cost_estimate=QUICK,
@@ -185,9 +194,9 @@
     mine = slice(half * sublanes, (half + 1) * sublanes)
     for line in range(rows // lanes):
         mix = acc_ref[line * lanes : (line + 1) * lanes, :]
-        first, count, sources = next(piece for piece in reversed(pieces) if piece[0] <= line * lanes)
-        for source, start in sources:
-            mix = mix + decode(near_refs[source], start, count, line * lanes - first, lanes)
+        first, sources = next(piece for piece in reversed(pieces) if piece[0] <= line * lanes)
+        for source, place in sources:
+            mix = mix + decode(near_refs[source], place, line * lanes - first, lanes)
         mix = mix.T
         at = slice(line * lanes, (line + 1) * lanes)
         full = slice(half * rows + line * lanes, half * rows + (line + 1) * lanes)
@@ -382,11 +391,11 @@
     def collect(wanted):
         arrays, places = [], []
         for key in wanted:
-            array, start = received[key]
+            array, *place = received[key]
             index = next((i for i, known in enumerate(arrays) if known is array), len(arrays))
             if index == len(arrays):
                 arrays.append(array)
-            places.append((index, start))
+            places.append((index, tuple(place)))
         return arrays, places
 
     for p, s, *blocks in order:
@@ -401,20 +410,15 @@
             pieces = tuple(
                 (
                     offsets[q] - p * half_rows,
-                    width // portions[q][1],
                     tuple(places[i * len(later) : (i + 1) * len(later)]),
                 )
                 for i, q in enumerate(inside)
             )
-            copies = 1 if GATHERED[p] else groups
             grad_query, grad_conv, state, packed = gate(
-                p, half_rows, segments, copies, pieces, after(sums[p]), arrays, query_in, conv_out, decay, grad_query
+                p, half_rows, segments, groups, pieces, after(sums[p]), arrays, query_in, conv_out, decay, grad_query
             )
             last, gated[p] = packed, (grad_conv, state)
-            if GATHERED[p]:
-                states[p] = lax.all_gather(packed, "ctx", tiled=True)
-            else:
-                states[p] = lax.all_to_all(packed, "ctx", 0, 0, tiled=True)
+            states[p] = lax.all_to_all(packed, "ctx", 0, 0, tiled=True)
         elif s == "scan":
             last = scanned[p] = scan(p, segments, *gated[p], decay, residue)
         elif s == "fix":
@@ -425,19 +429,19 @@
             route, part, _ = portions[p]
             rows, (blocks,) = width // part, blocks
             bit = bits[route[s]]
+            wanted = [(p, i, block ^ bit) for block in blocks for i in range(s)]
+            arrays, places = collect(wanted)
+            items = tuple(
+                (block ^ bit, offsets[p], rows, tuple(places[i * s : (i + 1) * s])) for i, block in enumerate(blocks)
+            )
             if last is None:
-                last, turned = first_send(rows, blocks[0] ^ bit, offsets[p], width, place, out_weight, out_grad)
+                last, turned = first_send(items, width, place, out_weight, out_grad)
             else:
-                wanted = [(p, i, block ^ bit) for block in blocks for i in range(s)]
-                arrays, places = collect(wanted)
-                items = tuple(
-                    (block ^ bit, offsets[p], rows, tuple(places[i * s : (i + 1) * s]))
-                    for i, block in enumerate(blocks)
-                )
                 last = send(items, True, width, after(place), out_weight, turned, arrays)
             arrived = lax.ppermute(last, "ch", [(i, i ^ bit) for i in range(size)])
+            each = part_of(rows, len(blocks))
             for i, block in enumerate(blocks):
-                received[p, s, block] = (arrived, i * (rows + PEAKS))
+                received[p, s, block] = (arrived, i * rows, i * (rows // each), each)
     return grad_query, grad_input
 
 

time: 80.9 us -> 86.4 us (1.068)
  local copies, waits for them, and re-layouts: 0.94 us -> 10.4 us
  blocking collectives: 5.52 us -> 0 us
  Pallas kernels: 23.2 us -> 28.6 us
  waiting for transfers between devices: 17.8 us -> 14.9 us
    unnamed x12 -> x22, local copies, waits for them, and re-layouts: 0.85 us -> 10.3 us
    all_gather x1 -> x0, blocking collectives: 5.52 us -> none  [local(): states[p] = lax.all_gather(packed, 'ctx', tiled=True)]
    pallas_call x15 -> x17, Pallas kernels: 10.2 us -> 14 us  [send(): pl.pallas_call(functools.partial(send_kernel, items, coded, width, len(ne...]
    ppermute x14 -> x16, starting transfers between devices: 28.2 us -> 24.4 us  [local(): arrived = lax.ppermute(last, 'ch', [(i, i ^ bit) for i in range(size)])]
    all_to_all x1 -> x2, starting transfers between devices: 3.33 us -> 6.65 us  [local(): states[p] = lax.all_to_all(packed, 'ctx', 0, 0, tiled=True)]
    ppermute x14 -> x16, waiting for transfers between devices: 17.8 us -> 14.9 us  [local(): arrived = lax.ppermute(last, 'ch', [(i, i ^ bit) for i in range(size)])]
    pallas_call x2, Pallas kernels: 3.42 us -> 5.05 us  [gate(): pl.pallas_call(functools.partial(gate_kernel, half, rows, segments, piece...]
  transfers between devices with their start and end apart: 15 -> 18, of which waited for: 9 -> 3; matrix products, arithmetic and copies ran while one was open for 0% -> 0% of each run, Pallas kernels for 21% -> 28%
where the time goes in v6:
time: 86.4 us; the launch traced here: 85.9 us
  starting transfers between devices  31 us (36%)
  Pallas kernels  28.6 us (33%)
  waiting for transfers between devices  14.9 us (17%)
  local copies, waits for them, and re-layouts  10.4 us (12%)
  between operations  0.99 us (1%)
    ppermute x16, starting transfers between devices, local(): arrived = lax.ppermute(last, 'ch', [(i, i ^ bit) for i in range(size)])  24.4 us
    ppermute x16, waiting for transfers between devices, local(): arrived = lax.ppermute(last, 'ch', [(i, i ^ bit) for i in range(size)])  14.9 us
    pallas_call x17, Pallas kernels, send(): pl.pallas_call(functools.partial(send_kernel, items, coded, width, len(ne...  14 us
    unnamed x22, local copies, waits for them, and re-layouts  10.3 us
    all_to_all x2, starting transfers between devices, local(): states[p] = lax.all_to_all(packed, 'ctx', 0, 0, tiled=True)  6.65 us
    pallas_call x2, Pallas kernels, gate(): pl.pallas_call(functools.partial(gate_kernel, half, rows, segments, piece...  5.05 us
    pallas_call x2, Pallas kernels, fix(): pl.pallas_call(functools.partial(fix_kernel, half, segments), in_specs=[p...  3.72 us
    pallas_call x2, Pallas kernels, scan(): pl.pallas_call(functools.partial(scan_kernel, half, segments), in_specs=[...  3.46 us
  transfers between devices with their start and end apart: 18, of which 3 were waited for; matrix products, arithmetic and copies ran while one was open for 0% of the time, Pallas kernels for 28%

profile of v6, /device:TPU:0, one launch (start us, length us, event | category | flops | bytes accessed | tf_op | source)
XLA Modules:
  0.0 85.9 jit_solution(2408776339878593779)
XLA Ops:
  0.6 0.0 copy-start
  0.6 2.4 %shard_map.77 = (bf16[528,256]{1,0:T(8,128)(2,1)S(1)}, bf16[1024,256]{1,0:T(8,128)(2,1)S(1)}) custom-call(s32[1]{0:T(128)} %bitcast.place_ref, bf16[8192,1024]{1,0:T(8,128)(2,1)} %w_ref.33, bf16[256,1024]{1,0:T(8,128)(2,1)} %g_hbm.1), custom_call_target="tpu_custom_call" | custom-call | bytes 1024 | tf_op jit(solution)/shard_map/pallas_call | solution.py:142
  3.1 3.0 %collective-permute-start = (bf16[528,256]{1,0:T(8,128)(2,1)S(1)}, bf16[528,256]{1,0:T(8,128)(2,1)S(1)}, u32[]{:S(2)}, u32[]{:S(2)}) collective-permute-start(bf16[528,256]{1,0:T(8,128)(2,1)S(1)} %get-tuple-element.31), channel_id=1, source_target_pairs={{0,1},{1,0},{2,3},{3,2},{4,5},{5,4},{6,7},{7,6},{8,9},{9,8},{10,11... | collective-permute-start | bytes 811016 | tf_op jit(solution)/shard_map/ppermute | solution.py:441
  6.1 0.8 copy-done
  6.9 0.4 shard_map.78
  7.3 0.4 shard_map.79
  7.7 1.1 %shard_map.80 = bf16[1040,256]{1,0:T(8,128)(2,1)S(1)} custom-call(s32[1]{0:T(128)} %bitcast.place_ref, bf16[8192,1024]{1,0:T(8,128)(2,1)S(1)} %copy-done, bf16[1024,256]{1,0:T(8,128)(2,1)S(1)} %get-tuple-element.33.turned_ref), custom_call_target="tpu_custom_call" | custom-call | bytes 1024 | tf_op jit(solution)/shard_map/pallas_call | solution.py:96
  8.8 3.1 %collective-permute-start.2 = (bf16[1040,256]{1,0:T(8,128)(2,1)S(1)}, bf16[1040,256]{1,0:T(8,128)(2,1)S(1)}, u32[]{:S(2)}, u32[]{:S(2)}) collective-permute-start(bf16[1040,256]{1,0:T(8,128)(2,1)S(1)} %shard_map.80), channel_id=1, source_target_pairs={{0,2},{1,3},{2,0},{3,1},{4,6},{5,7},{6,4},{7,5},{8,10},{9,11},{10,... | collective-permute-start | bytes 1597448 | tf_op jit(solution)/shard_map/ppermute | solution.py:441
  11.9 1.1 %shard_map.81 = bf16[1040,256]{1,0:T(8,128)(2,1)S(1)} custom-call(s32[1]{0:T(128)} %bitcast.place_ref, bf16[8192,1024]{1,0:T(8,128)(2,1)S(1)} %copy-done, bf16[1024,256]{1,0:T(8,128)(2,1)S(1)} %get-tuple-element.33.turned_ref), custom_call_target="tpu_custom_call" | custom-call | bytes 1024 | tf_op jit(solution)/shard_map/pallas_call | solution.py:96
  12.9 1.6 %collective-permute-start.3 = (bf16[1040,256]{1,0:T(8,128)(2,1)S(1)}, bf16[1040,256]{1,0:T(8,128)(2,1)S(1)}, u32[]{:S(2)}, u32[]{:S(2)}) collective-permute-start(bf16[1040,256]{1,0:T(8,128)(2,1)S(1)} %shard_map.81), channel_id=1, source_target_pairs={{0,1},{1,0},{2,3},{3,2},{4,5},{5,4},{6,7},{7,6},{8,9},{9,8},{10,11... | collective-permute-start | bytes 1597448 | tf_op jit(solution)/shard_map/ppermute | solution.py:441
  14.5 0.0 collective-permute-done.refs_0_
  14.5 0.7 shard_map.82
  15.3 0.5 collective-permute-start.4
  15.8 0.9 %collective-permute-start.1 = (bf16[272,256]{1,0:T(8,128)(2,1)S(1)}, bf16[272,256]{1,0:T(8,128)(2,1)S(1)}, u32[]{:S(2)}, u32[]{:S(2)}) collective-permute-start(bf16[272,256]{1,0:T(8,128)(2,1)S(1)} %shard_map.79), channel_id=1, source_target_pairs={{0,1},{1,0},{2,3},{3,2},{4,5},{5,4},{6,7},{7,6},{8,9},{9,8},{10,11... | collective-permute-start | bytes 417800 | tf_op jit(solution)/shard_map/ppermute | solution.py:441
  16.7 0.6 shard_map.83
  17.3 1.2 %collective-permute-start.6 = (bf16[528,256]{1,0:T(8,128)(2,1)S(1)}, bf16[528,256]{1,0:T(8,128)(2,1)S(1)}, u32[]{:S(2)}, u32[]{:S(2)}) collective-permute-start(bf16[528,256]{1,0:T(8,128)(2,1)S(1)} %shard_map.83), channel_id=1, source_target_pairs={{0,1},{1,0},{2,3},{3,2},{4,5},{5,4},{6,7},{7,6},{8,9},{9,8},{10,11... | collective-permute-start | bytes 811016 | tf_op jit(solution)/shard_map/ppermute | solution.py:441
  18.5 12.5 %collective-permute-done.1.refs_0_ = bf16[272,256]{1,0:T(8,128)(2,1)S(1)} collective-permute-done((bf16[272,256]{1,0:T(8,128)(2,1)S(1)}, bf16[272,256]{1,0:T(8,128)(2,1)S(1)}, u32[]{:S(2)}, u32[]{:S(2)}) %collective-permute-start.1) | collective-permute-done | bytes 139296 | tf_op jit(solution)/shard_map/ppermute | solution.py:441
  31.0 0.5 shard_map.84
  31.5 0.4 shard_map.85
  31.9 1.6 %collective-permute-start.5 = (bf16[272,256]{1,0:T(8,128)(2,1)S(1)}, bf16[272,256]{1,0:T(8,128)(2,1)S(1)}, u32[]{:S(2)}, u32[]{:S(2)}) collective-permute-start(bf16[272,256]{1,0:T(8,128)(2,1)S(1)} %shard_map.85), channel_id=1, source_target_pairs={{0,1},{1,0},{2,3},{3,2},{4,5},{5,4},{6,7},{7,6},{8,9},{9,8},{10,11... | collective-permute-start | bytes 417800 | tf_op jit(solution)/shard_map/ppermute | solution.py:441
  33.5 0.0 collective-permute-done.2.refs_0_.refs_1_
  33.5 0.7 shard_map.86
  34.2 0.0 copy-start.8
  34.2 0.0 collective-permute-done.3.refs_0_
  34.2 0.7 shard_map.87
  35.0 0.5 collective-permute-start.9
  35.5 0.0 collective-permute-done.4.refs_1_
  35.5 0.9 %shard_map.88 = bf16[528,256]{1,0:T(8,128)(2,1)S(1)} custom-call(s32[1]{0:T(128)} %bitcast.place_ref, bf16[8192,1024]{1,0:T(8,128)(2,1)S(1)} %copy-done, bf16[1024,256]{1,0:T(8,128)(2,1)S(1)} %get-tuple-element.33.turned_ref, bf16[1040,256]{1,0:T(8,128)(2,1)S(1)} %collective-permute-done.3.refs_0_, bf16[528,256]{1,0:T(8,128)(2,1)S(1)} %collective-permute-done.4.refs_1_), custom_call_target="tpu_custom_call" | custom-call | bytes 1024 | tf_op jit(solution)/shard_map/pallas_call | solution.py:96
  36.4 2.7 %collective-permute-start.10 = (bf16[528,256]{1,0:T(8,128)(2,1)S(1)}, bf16[528,256]{1,0:T(8,128)(2,1)S(1)}, u32[]{:S(2)}, u32[]{:S(2)}) collective-permute-start(bf16[528,256]{1,0:T(8,128)(2,1)S(1)} %shard_map.88), channel_id=1, source_target_pairs={{0,4},{1,5},{2,6},{3,7},{4,0},{5,1},{6,2},{7,3},{8,12},{9,13},{10,... | collective-permute-start | bytes 811016 | tf_op jit(solution)/shard_map/ppermute | solution.py:441
  39.1 0.5 collective-permute-start.14
  39.6 1.5 %collective-permute-start.7 = (bf16[272,256]{1,0:T(8,128)(2,1)S(1)}, bf16[272,256]{1,0:T(8,128)(2,1)S(1)}, u32[]{:S(2)}, u32[]{:S(2)}) collective-permute-start(bf16[272,256]{1,0:T(8,128)(2,1)S(1)} %shard_map.78), channel_id=1, source_target_pairs={{0,1},{1,0},{2,3},{3,2},{4,5},{5,4},{6,7},{7,6},{8,9},{9,8},{10,11... | collective-permute-start | bytes 417800 | tf_op jit(solution)/shard_map/ppermute | solution.py:441
  41.1 1.6 %collective-permute-start.8 = (bf16[272,256]{1,0:T(8,128)(2,1)S(1)}, bf16[272,256]{1,0:T(8,128)(2,1)S(1)}, u32[]{:S(2)}, u32[]{:S(2)}) collective-permute-start(bf16[272,256]{1,0:T(8,128)(2,1)S(1)} %shard_map.84), channel_id=1, source_target_pairs={{0,2},{1,3},{2,0},{3,1},{4,6},{5,7},{6,4},{7,5},{8,10},{9,11},{10,... | collective-permute-start | bytes 417800 | tf_op jit(solution)/shard_map/ppermute | solution.py:441
  42.7 1.1 %shard_map.89 = bf16[272,256]{1,0:T(8,128)(2,1)} custom-call(s32[1]{0:T(128)} %bitcast.place_ref, bf16[8192,1024]{1,0:T(8,128)(2,1)S(1)} %copy-done, bf16[1024,256]{1,0:T(8,128)(2,1)S(1)} %get-tuple-element.33.turned_ref, bf16[272,256]{1,0:T(8,128)(2,1)S(1)} %collective-permute-done.5.refs_0_), custom_call_target="tpu_custom_call" | custom-call | bytes 1024 | tf_op jit(solution)/shard_map/pallas_call | solution.py:96
  43.9 0.5 shard_map.90.acc_ref
  44.4 0.0 copy-start.2
  44.4 0.0 copy-start.3
  44.4 1.1 %shard_map.91 = bf16[272,256]{1,0:T(8,128)(2,1)} custom-call(s32[1]{0:T(128)} %bitcast.place_ref, bf16[8192,1024]{1,0:T(8,128)(2,1)S(1)} %copy-done, bf16[1024,256]{1,0:T(8,128)(2,1)S(1)} %get-tuple-element.33.turned_ref), custom_call_target="tpu_custom_call" | custom-call | bytes 1024 | tf_op jit(solution)/shard_map/pallas_call | solution.py:96
  45.5 2.3 %collective-permute-done.7.refs_0_ = bf16[272,256]{1,0:T(8,128)(2,1)S(1)} collective-permute-done((bf16[272,256]{1,0:T(8,128)(2,1)S(1)}, bf16[272,256]{1,0:T(8,128)(2,1)S(1)}, u32[]{:S(2)}, u32[]{:S(2)}) %collective-permute-start.7) | collective-permute-done | bytes 139296 | tf_op jit(solution)/shard_map/ppermute | solution.py:441
  47.7 1.3 %collective-permute-start.11 = (bf16[272,256]{1,0:T(8,128)(2,1)}, bf16[272,256]{1,0:T(8,128)(2,1)}, u32[]{:S(2)}, u32[]{:S(2)}) collective-permute-start(bf16[272,256]{1,0:T(8,128)(2,1)} %shard_map.91), channel_id=1, source_target_pairs={{0,1},{1,0},{2,3},{3,2},{4,5},{5,4},{6,7},{7,6},{8,9},{9,8},{10,11... | collective-permute-start | bytes 417800 | tf_op jit(solution)/shard_map/ppermute | solution.py:441
  49.0 0.1 collective-permute-done.8.refs_1_
  49.1 1.2 %shard_map.92 = bf16[272,256]{1,0:T(8,128)(2,1)} custom-call(s32[1]{0:T(128)} %bitcast.place_ref, bf16[8192,1024]{1,0:T(8,128)(2,1)S(1)} %copy-done, bf16[1024,256]{1,0:T(8,128)(2,1)S(1)} %get-tuple-element.33.turned_ref, bf16[272,256]{1,0:T(8,128)(2,1)S(1)} %collective-permute-done.7.refs_0_, bf16[272,256]{1,0:T(8,128)(2,1)S(1)} %collective-permute-done.8.refs_1_), custom_call_target="tpu_custom_call" | custom-call | bytes 1024 | tf_op jit(solution)/shard_map/pallas_call | solution.py:96
  50.3 2.6 %collective-permute-start.13 = (bf16[272,256]{1,0:T(8,128)(2,1)}, bf16[272,256]{1,0:T(8,128)(2,1)S(1)}, u32[]{:S(2)}, u32[]{:S(2)}) collective-permute-start(bf16[272,256]{1,0:T(8,128)(2,1)} %shard_map.92), channel_id=1, source_target_pairs={{0,4},{1,5},{2,6},{3,7},{4,0},{5,1},{6,2},{7,3},{8,12},{9,13},{10,... | collective-permute-start | bytes 417800 | tf_op jit(solution)/shard_map/ppermute | solution.py:441
  52.9 1.5 %collective-permute-start.12 = (bf16[272,256]{1,0:T(8,128)(2,1)}, bf16[272,256]{1,0:T(8,128)(2,1)}, u32[]{:S(2)}, u32[]{:S(2)}) collective-permute-start(bf16[272,256]{1,0:T(8,128)(2,1)} %shard_map.89), channel_id=1, source_target_pairs={{0,2},{1,3},{2,0},{3,1},{4,6},{5,7},{6,4},{7,5},{8,10},{9,11},{10,... | collective-permute-start | bytes 417800 | tf_op jit(solution)/shard_map/ppermute | solution.py:441
  54.5 2.0 %shard_map.93 = (bf16[256,1024]{1,0:T(8,128)(2,1)}, f32[1024,128]{1,0:T(8,128)S(1)}, f32[16,8,128]{2,1,0:T(8,128)S(1)}, f32[4,8,8,128]{3,2,1,0:T(8,128)}) custom-call(f32[512,256]{1,0:T(8,128)S(1)} %shard_map.90.acc_ref, bf16[528,256]{1,0:T(8,128)(2,1)S(1)} %collective-permute-done.9.refs_0_, bf16[528,256]{1,0:T(8,128)(2,1)S(1)} %collective-permute-done.10.refs_1_, ...), custom_call_target="tpu_custom_call" | custom-call | bytes 1024 | tf_op jit(solution)/shard_map/pallas_call | solution.py:242
  56.5 0.0 copy-start.6
  56.5 0.8 copy-done.6
  57.3 1.2 %shard_map.96 = bf16[272,256]{1,0:T(8,128)(2,1)} custom-call(s32[1]{0:T(128)} %bitcast.place_ref, bf16[8192,1024]{1,0:T(8,128)(2,1)S(1)} %copy-done, bf16[1024,256]{1,0:T(8,128)(2,1)S(1)} %get-tuple-element.33.turned_ref, bf16[1040,256]{1,0:T(8,128)(2,1)S(1)} %collective-permute-done.2.refs_0_.refs_1_, ...), custom_call_target="tpu_custom_call" | custom-call | bytes 1024 | tf_op jit(solution)/shard_map/pallas_call | solution.py:96
  58.5 0.3 collective-permute-start.15
  58.8 3.3 %all-to-all-start.1 = ((f32[4,8,8,128]{3,2,1,0:T(8,128)}), f32[4,8,8,128]{3,2,1,0:T(8,128)S(1)}, u32[]{:S(2)}, u32[]{:S(2)}) async-start(f32[4,8,8,128]{3,2,1,0:T(8,128)} %get-tuple-element.52), calls=%async_computation.1 | async-start | bytes 262144 | tf_op jit(solution)/shard_map/all_to_all | solution.py:421
  62.2 0.0 copy-start.7
  62.2 1.0 %copy-done.7 = f32[1024,128]{1,0:T(8,128)S(1)} copy-done((f32[1024,128]{1,0:T(8,128)S(1)}, f32[1024,128]{1,0:T(8,128)}, u32[]{:S(2)}) %copy-start.7) | copy-done | bytes 524312
  63.3 1.7 %shard_map.94.rows_in_ref = f32[1024,128]{1,0:T(8,128)S(1)} custom-call(f32[1024,128]{1,0:T(8,128)S(1)} %copy-done.7, f32[16,8,128]{2,1,0:T(8,128)S(1)} %get-tuple-element.50.state_ref, f32[16,16,128]{2,1,0:T(8,128)S(1)} %bitcast.11, f32[16,16,128]{2,1,0:T(8,128)S(1)} %bitcast.16), custom_call_target="tpu_custom_call" | custom-call | bytes 1024 | tf_op jit(solution)/shard_map/pallas_call | solution.py:292
  65.0 0.0 copy-start.1
  65.1 5.8 %copy-done.1 = bf16[8192,1024]{1,0:T(8,128)(2,1)S(1)} copy-done((bf16[8192,1024]{1,0:T(8,128)(2,1)S(1)}, bf16[8192,1024]{1,0:T(8,128)(2,1)}, u32[]{:S(2)}) %copy-start.1) | copy-done | bytes 16777240
  70.8 1.4 %shard_map.95.acc_ref = f32[512,256]{1,0:T(8,128)S(1)} custom-call(s32[1]{0:T(128)} %bitcast.place_ref, bf16[8192,1024]{1,0:T(8,128)(2,1)S(1)} %copy-done.1, bf16[1024,256]{1,0:T(8,128)(2,1)S(1)} %get-tuple-element.33.turned_ref, bf16[272,256]{1,0:T(8,128)(2,1)} %collective-permute-done.11.refs_0_, bf16[1040,256]{1,0:T(8,128)(2,1)S(1)} %collective-permute-done.2.refs_0_.refs_1_), custom_call_target="tpu_custom_call" | custom-call | bytes 1024 | tf_op jit(solution)/shard_map/pallas_call | solution.py:96
  72.2 3.0 %shard_map.97 = (bf16[256,1024]{1,0:T(8,128)(2,1)}, f32[1024,128]{1,0:T(8,128)S(1)}, f32[16,8,128]{2,1,0:T(8,128)S(1)}, f32[4,8,8,128]{3,2,1,0:T(8,128)}) custom-call(f32[512,256]{1,0:T(8,128)S(1)} %shard_map.95.acc_ref, bf16[272,256]{1,0:T(8,128)(2,1)} %collective-permute-done.12.refs_0_, ...), custom_call_target="tpu_custom_call", output_to_operand_aliasing={{0}: (8, {})} | custom-call | bytes 1024 | tf_op jit(solution)/shard_map/pallas_call | solution.py:242
  75.3 0.0 copy-start.4
  75.3 0.8 copy-done.4
  76.1 3.3 %all-to-all-start = ((f32[4,8,8,128]{3,2,1,0:T(8,128)}), f32[4,8,8,128]{3,2,1,0:T(8,128)S(1)}, u32[]{:S(2)}, u32[]{:S(2)}) async-start(f32[4,8,8,128]{3,2,1,0:T(8,128)} %get-tuple-element.58), calls=%async_computation | async-start | bytes 262144 | tf_op jit(solution)/shard_map/all_to_all | solution.py:421
  79.4 0.0 copy-start.5
  79.4 1.0 %copy-done.5 = f32[1024,128]{1,0:T(8,128)S(1)} copy-done((f32[1024,128]{1,0:T(8,128)S(1)}, f32[1024,128]{1,0:T(8,128)}, u32[]{:S(2)}) %copy-start.5) | copy-done | bytes 524312
  80.5 1.7 %shard_map.98.rows_in_ref = f32[1024,128]{1,0:T(8,128)S(1)} custom-call(f32[1024,128]{1,0:T(8,128)S(1)} %copy-done.5, f32[16,8,128]{2,1,0:T(8,128)S(1)} %get-tuple-element.57.state_ref, f32[16,16,128]{2,1,0:T(8,128)S(1)} %bitcast.13, f32[16,16,128]{2,1,0:T(8,128)S(1)} %bitcast.17), custom_call_target="tpu_custom_call" | custom-call | bytes 1024 | tf_op jit(solution)/shard_map/pallas_call | solution.py:292
  82.2 1.9 %shard_map.99.refs_0_ = bf16[256,1024]{1,0:T(8,128)(2,1)} custom-call(s32[1]{0:T(128)} %bitcast.5.group_ref, f32[1024,128]{1,0:T(8,128)S(1)} %shard_map.94.rows_in_ref, f32[4,8,8,128]{3,2,1,0:T(8,128)S(1)} %all-to-all-done.1.states_ref, f32[16,16,128]{2,1,0:T(8,128)S(1)} %bitcast.14, f32[16,16,128]{2,1,0:T(8,128)S(1)} %bitcast.18), custom_call_target="tpu_custom_call" | custom-call | bytes 1024 | tf_op jit(solution)/shard_map/pallas_call | solution.py:344
  84.1 1.9 %shard_map.100 = bf16[256,1024]{1,0:T(8,128)(2,1)} custom-call(s32[1]{0:T(128)} %bitcast.5.group_ref, f32[1024,128]{1,0:T(8,128)S(1)} %shard_map.98.rows_in_ref, f32[4,8,8,128]{3,2,1,0:T(8,128)S(1)} %all-to-all-done.states_ref, f32[16,16,128]{2,1,0:T(8,128)S(1)} %bitcast.15, f32[16,16,128]{2,1,0:T(8,128)S(1)} %bitcast.19, ...), custom_call_target="tpu_custom_call", output_to_operand_aliasing={{}: (5, {})} | custom-call | bytes 1024 | tf_op jit(solution)/shard_map/pallas_call | solution.py:344
  (20 shorter events, 0.2 us)
Async XLA Ops:
  0.6 6.2 %copy-start = (bf16[8192,1024]{1,0:T(8,128)(2,1)S(1)}, bf16[8192,1024]{1,0:T(8,128)(2,1)}, u32[]{:S(2)}) copy-start(bf16[8192,1024]{1,0:T(8,128)(2,1)} %w_ref.33) | copy-start | bytes 50331652
  3.1 11.5 %collective-permute-start = (bf16[528,256]{1,0:T(8,128)(2,1)S(1)}, bf16[528,256]{1,0:T(8,128)(2,1)S(1)}, u32[]{:S(2)}, u32[]{:S(2)}) collective-permute-start(bf16[528,256]{1,0:T(8,128)(2,1)S(1)} %get-tuple-element.31), channel_id=1, source_target_pairs={{0,1},{1,0},{2,3},{3,2},{4,5},{5,4},{6,7},{7,6},{8,9},{9,8},{10,11... | collective-permute-start | bytes 811016 | tf_op jit(solution)/shard_map/ppermute | solution.py:441
  8.8 24.7 %collective-permute-start.2 = (bf16[1040,256]{1,0:T(8,128)(2,1)S(1)}, bf16[1040,256]{1,0:T(8,128)(2,1)S(1)}, u32[]{:S(2)}, u32[]{:S(2)}) collective-permute-start(bf16[1040,256]{1,0:T(8,128)(2,1)S(1)} %shard_map.80), channel_id=1, source_target_pairs={{0,2},{1,3},{2,0},{3,1},{4,6},{5,7},{6,4},{7,5},{8,10},{9,11},{10,... | collective-permute-start | bytes 1597448 | tf_op jit(solution)/shard_map/ppermute | solution.py:441
  12.9 21.3 %collective-permute-start.3 = (bf16[1040,256]{1,0:T(8,128)(2,1)S(1)}, bf16[1040,256]{1,0:T(8,128)(2,1)S(1)}, u32[]{:S(2)}, u32[]{:S(2)}) collective-permute-start(bf16[1040,256]{1,0:T(8,128)(2,1)S(1)} %shard_map.81), channel_id=1, source_target_pairs={{0,1},{1,0},{2,3},{3,2},{4,5},{5,4},{6,7},{7,6},{8,9},{9,8},{10,11... | collective-permute-start | bytes 1597448 | tf_op jit(solution)/shard_map/ppermute | solution.py:441
  15.3 20.2 %collective-permute-start.4 = (bf16[528,256]{1,0:T(8,128)(2,1)S(1)}, bf16[528,256]{1,0:T(8,128)(2,1)S(1)}, u32[]{:S(2)}, u32[]{:S(2)}) collective-permute-start(bf16[528,256]{1,0:T(8,128)(2,1)S(1)} %shard_map.82), channel_id=1, source_target_pairs={{0,2},{1,3},{2,0},{3,1},{4,6},{5,7},{6,4},{7,5},{8,10},{9,11},{10,... | collective-permute-start | bytes 811016 | tf_op jit(solution)/shard_map/ppermute | solution.py:441
  15.8 15.2 %collective-permute-start.1 = (bf16[272,256]{1,0:T(8,128)(2,1)S(1)}, bf16[272,256]{1,0:T(8,128)(2,1)S(1)}, u32[]{:S(2)}, u32[]{:S(2)}) collective-permute-start(bf16[272,256]{1,0:T(8,128)(2,1)S(1)} %shard_map.79), channel_id=1, source_target_pairs={{0,1},{1,0},{2,3},{3,2},{4,5},{5,4},{6,7},{7,6},{8,9},{9,8},{10,11... | collective-permute-start | bytes 417800 | tf_op jit(solution)/shard_map/ppermute | solution.py:441
  17.3 23.8 %collective-permute-start.6 = (bf16[528,256]{1,0:T(8,128)(2,1)S(1)}, bf16[528,256]{1,0:T(8,128)(2,1)S(1)}, u32[]{:S(2)}, u32[]{:S(2)}) collective-permute-start(bf16[528,256]{1,0:T(8,128)(2,1)S(1)} %shard_map.83), channel_id=1, source_target_pairs={{0,1},{1,0},{2,3},{3,2},{4,5},{5,4},{6,7},{7,6},{8,9},{9,8},{10,11... | collective-permute-start | bytes 811016 | tf_op jit(solution)/shard_map/ppermute | solution.py:441
  31.9 7.7 %collective-permute-start.5 = (bf16[272,256]{1,0:T(8,128)(2,1)S(1)}, bf16[272,256]{1,0:T(8,128)(2,1)S(1)}, u32[]{:S(2)}, u32[]{:S(2)}) collective-permute-start(bf16[272,256]{1,0:T(8,128)(2,1)S(1)} %shard_map.85), channel_id=1, source_target_pairs={{0,1},{1,0},{2,3},{3,2},{4,5},{5,4},{6,7},{7,6},{8,9},{9,8},{10,11... | collective-permute-start | bytes 417800 | tf_op jit(solution)/shard_map/ppermute | solution.py:441
  34.2 8.5 %copy-start.8 = (f32[1024,16]{0,1:T(8,128)S(1)}, f32[1024,16]{0,1:T(8,128)}, u32[]{:S(2)}) copy-start(f32[1024,16]{0,1:T(8,128)} %param.11) | copy-start | bytes 196612
  35.0 17.9 %collective-permute-start.9 = (bf16[528,256]{1,0:T(8,128)(2,1)S(1)}, bf16[528,256]{1,0:T(8,128)(2,1)S(1)}, u32[]{:S(2)}, u32[]{:S(2)}) collective-permute-start(bf16[528,256]{1,0:T(8,128)(2,1)S(1)} %shard_map.87), channel_id=1, source_target_pairs={{0,2},{1,3},{2,0},{3,1},{4,6},{5,7},{6,4},{7,5},{8,10},{9,11},{10,... | collective-permute-start | bytes 811016 | tf_op jit(solution)/shard_map/ppermute | solution.py:441
  36.4 18.0 %collective-permute-start.10 = (bf16[528,256]{1,0:T(8,128)(2,1)S(1)}, bf16[528,256]{1,0:T(8,128)(2,1)S(1)}, u32[]{:S(2)}, u32[]{:S(2)}) collective-permute-start(bf16[528,256]{1,0:T(8,128)(2,1)S(1)} %shard_map.88), channel_id=1, source_target_pairs={{0,4},{1,5},{2,6},{3,7},{4,0},{5,1},{6,2},{7,3},{8,12},{9,13},{10,... | collective-permute-start | bytes 811016 | tf_op jit(solution)/shard_map/ppermute | solution.py:441
  39.1 18.2 %collective-permute-start.14 = (bf16[528,256]{1,0:T(8,128)(2,1)S(1)}, bf16[528,256]{1,0:T(8,128)(2,1)S(1)}, u32[]{:S(2)}, u32[]{:S(2)}) collective-permute-start(bf16[528,256]{1,0:T(8,128)(2,1)S(1)} %shard_map.86), channel_id=1, source_target_pairs={{0,1},{1,0},{2,3},{3,2},{4,5},{5,4},{6,7},{7,6},{8,9},{9,8},{10,11... | collective-permute-start | bytes 811016 | tf_op jit(solution)/shard_map/ppermute | solution.py:441
  39.6 8.1 %collective-permute-start.7 = (bf16[272,256]{1,0:T(8,128)(2,1)S(1)}, bf16[272,256]{1,0:T(8,128)(2,1)S(1)}, u32[]{:S(2)}, u32[]{:S(2)}) collective-permute-start(bf16[272,256]{1,0:T(8,128)(2,1)S(1)} %shard_map.78), channel_id=1, source_target_pairs={{0,1},{1,0},{2,3},{3,2},{4,5},{5,4},{6,7},{7,6},{8,9},{9,8},{10,11... | collective-permute-start | bytes 417800 | tf_op jit(solution)/shard_map/ppermute | solution.py:441
  41.1 8.0 %collective-permute-start.8 = (bf16[272,256]{1,0:T(8,128)(2,1)S(1)}, bf16[272,256]{1,0:T(8,128)(2,1)S(1)}, u32[]{:S(2)}, u32[]{:S(2)}) collective-permute-start(bf16[272,256]{1,0:T(8,128)(2,1)S(1)} %shard_map.84), channel_id=1, source_target_pairs={{0,2},{1,3},{2,0},{3,1},{4,6},{5,7},{6,4},{7,5},{8,10},{9,11},{10,... | collective-permute-start | bytes 417800 | tf_op jit(solution)/shard_map/ppermute | solution.py:441
  44.4 10.1 %copy-start.2 = (bf16[256,1024]{1,0:T(8,128)(2,1)S(1)}, bf16[256,1024]{1,0:T(8,128)(2,1)}, u32[]{:S(2)}) copy-start(bf16[256,1024]{1,0:T(8,128)(2,1)} %refs_4_.1) | copy-start | bytes 1572868
  44.4 10.1 %copy-start.3 = (bf16[256,1024]{1,0:T(8,128)(2,1)S(1)}, bf16[256,1024]{1,0:T(8,128)(2,1)}, u32[]{:S(2)}) copy-start(bf16[256,1024]{1,0:T(8,128)(2,1)} %refs_5_.1) | copy-start | bytes 1572868
  45.5 16.7 %copy-start.9 = (f32[1024,16]{0,1:T(8,128)S(1)}, f32[1024,16]{0,1:T(8,128)}, u32[]{:S(2)}) copy-start(f32[1024,16]{0,1:T(8,128)} %param.10) | copy-start | bytes 196612
  47.7 17.3 %collective-permute-start.11 = (bf16[272,256]{1,0:T(8,128)(2,1)}, bf16[272,256]{1,0:T(8,128)(2,1)}, u32[]{:S(2)}, u32[]{:S(2)}) collective-permute-start(bf16[272,256]{1,0:T(8,128)(2,1)} %shard_map.91), channel_id=1, source_target_pairs={{0,1},{1,0},{2,3},{3,2},{4,5},{5,4},{6,7},{7,6},{8,9},{9,8},{10,11... | collective-permute-start | bytes 417800 | tf_op jit(solution)/shard_map/ppermute | solution.py:441
  50.3 21.9 %collective-permute-start.13 = (bf16[272,256]{1,0:T(8,128)(2,1)}, bf16[272,256]{1,0:T(8,128)(2,1)S(1)}, u32[]{:S(2)}, u32[]{:S(2)}) collective-permute-start(bf16[272,256]{1,0:T(8,128)(2,1)} %shard_map.92), channel_id=1, source_target_pairs={{0,4},{1,5},{2,6},{3,7},{4,0},{5,1},{6,2},{7,3},{8,12},{9,13},{10,... | collective-permute-start | bytes 417800 | tf_op jit(solution)/shard_map/ppermute | solution.py:441
  52.9 19.3 %collective-permute-start.12 = (bf16[272,256]{1,0:T(8,128)(2,1)}, bf16[272,256]{1,0:T(8,128)(2,1)}, u32[]{:S(2)}, u32[]{:S(2)}) collective-permute-start(bf16[272,256]{1,0:T(8,128)(2,1)} %shard_map.89), channel_id=1, source_target_pairs={{0,2},{1,3},{2,0},{3,1},{4,6},{5,7},{6,4},{7,5},{8,10},{9,11},{10,... | collective-permute-start | bytes 417800 | tf_op jit(solution)/shard_map/ppermute | solution.py:441
  56.5 0.8 copy-start.6
  58.5 13.7 %collective-permute-start.15 = (bf16[272,256]{1,0:T(8,128)(2,1)}, bf16[272,256]{1,0:T(8,128)(2,1)}, u32[]{:S(2)}, u32[]{:S(2)}) collective-permute-start(bf16[272,256]{1,0:T(8,128)(2,1)} %shard_map.96), channel_id=1, source_target_pairs={{0,4},{1,5},{2,6},{3,7},{4,0},{5,1},{6,2},{7,3},{8,12},{9,13},{10,... | collective-permute-start | bytes 417800 | tf_op jit(solution)/shard_map/ppermute | solution.py:441
  58.8 17.3 %all-to-all-start.1 = ((f32[4,8,8,128]{3,2,1,0:T(8,128)}), f32[4,8,8,128]{3,2,1,0:T(8,128)S(1)}, u32[]{:S(2)}, u32[]{:S(2)}) async-start(f32[4,8,8,128]{3,2,1,0:T(8,128)} %get-tuple-element.52), calls=%async_computation.1 | async-start | bytes 262144 | tf_op jit(solution)/shard_map/all_to_all | solution.py:421
  62.2 1.0 %copy-start.7 = (f32[1024,128]{1,0:T(8,128)S(1)}, f32[1024,128]{1,0:T(8,128)}, u32[]{:S(2)}) copy-start(f32[1024,128]{1,0:T(8,128)} %copy-done.6) | copy-start | bytes 1572868
  65.0 5.8 %copy-start.1 = (bf16[8192,1024]{1,0:T(8,128)(2,1)S(1)}, bf16[8192,1024]{1,0:T(8,128)(2,1)}, u32[]{:S(2)}) copy-start(bf16[8192,1024]{1,0:T(8,128)(2,1)} %w_ref.33) | copy-start | bytes 50331652
  75.3 0.8 copy-start.4
  76.1 8.0 %all-to-all-start = ((f32[4,8,8,128]{3,2,1,0:T(8,128)}), f32[4,8,8,128]{3,2,1,0:T(8,128)S(1)}, u32[]{:S(2)}, u32[]{:S(2)}) async-start(f32[4,8,8,128]{3,2,1,0:T(8,128)} %get-tuple-element.58), calls=%async_computation | async-start | bytes 262144 | tf_op jit(solution)/shard_map/all_to_all | solution.py:421
  79.4 1.0 %copy-start.5 = (f32[1024,128]{1,0:T(8,128)S(1)}, f32[1024,128]{1,0:T(8,128)}, u32[]{:S(2)}) copy-start(f32[1024,128]{1,0:T(8,128)} %copy-done.4) | copy-start | bytes 1572868

commit v7 on v6

--- a/solution.py
+++ b/solution.py
@@ -12,15 +12,16 @@
 SPAN = 251 * math.log(2.0)
 SHIFT = 125 * math.log(2.0)
 STEP = 256
-VMEM = 24 * 1024 * 1024
+VMEM = 12 * 1024 * 1024
 QUICK = pl.CostEstimate(flops=0, bytes_accessed=1024, transcendentals=0)
 
-PORTIONS = (((0, 1, 2), 2, 0), ((0, 1, 2), 4, 1), ((1, 0, 2), 4, 1))
+PORTIONS = (((0, 1, 2), 2, 0), ((0, 1, 2), 2, 1))
 ORDER = (
-    (0, 0, (6,)), (1, 0, (4,)), (1, 0, (6,)), (2, 0, (5, 4, 1, 0)), (0, 0, (4, 2)), (0, 1, (4,)), (0, 0, (0,)),
-    (1, 1, (4,)), (1, 0, (2,)), (2, 1, (4, 0)), (0, 1, (0,)), (0, 2, (0,)), (1, 1, (0,)), (0, "sum"), (1, 0, (0,)),
-    (1, 2, (0,)), (0, "gate"), (2, 2, (0,)), (0, "scan"), (1, "sum"), (1, "gate"), (0, "fix"), (1, "scan"), (1, "fix"),
+    (0, 0, (6,)), (1, 0, (6,)), (0, 0, (4,)), (1, 0, (4,)), (0, 0, (0,)), (0, 1, (4,)), (0, 0, (2,)), (1, 1, (4,)),
+    (1, 0, (2,)), (0, 2, (0,)), (0, 1, (0,)), (1, 0, (0,)), (1, 2, (0,)), (1, 1, (0,)), (0, "sum"), (0, "gate"),
+    (0, "scan"), (1, "sum"), (1, "gate"), (0, "fix"), (1, "scan"), (1, "fix"),
 )
+WAITS = {(0, "sum"): ((0, 2, 0),), (0, "scan"): ((1, 2, 0),), (1, 0, (0,)): ((1, 1, 4),)}
 
 
 def part_of(rows, blocks):
@@ -371,8 +372,9 @@
     by_mode = lambda values: jnp.repeat(values.T.reshape(modes, width // lanes, lanes), segments, axis=1)
     decay, residue = by_mode(decay_rates), by_mode(residues)
 
-    portions, order = PORTIONS, ORDER
+    portions, order, waits = PORTIONS, ORDER, WAITS
     if size != 8:
+        waits = {}
         portions = ((tuple(range(len(bits))), 2, 0), (tuple(range(len(bits))), 2, 1))
         order = [
             (p, s, (block,))
@@ -386,7 +388,7 @@
     grad_query = grad_input = last = None
 
     def after(value):
-        return value if last is None else lax.optimization_barrier((value, last))[0]
+        return value if last is None else lax.optimization_barrier((value, last, *awaited))[0]
 
     def collect(wanted):
         arrays, places = [], []
@@ -399,6 +401,7 @@
         return arrays, places
 
     for p, s, *blocks in order:
+        awaited = [received[key][0] for key in waits.get((p, s, *blocks), ())]
         inside = [q for q, (_, _, half) in enumerate(portions) if half == p]
         if s == "sum":
             arrays, places = collect([(q, 0, 0) for q in inside])
@@ -420,7 +423,7 @@
             last, gated[p] = packed, (grad_conv, state)
             states[p] = lax.all_to_all(packed, "ctx", 0, 0, tiled=True)
         elif s == "scan":
-            last = scanned[p] = scan(p, segments, *gated[p], decay, residue)
+            last = scanned[p] = scan(p, segments, after(gated[p][0]), gated[p][1], decay, residue)
         elif s == "fix":
             last = grad_input = fix(
                 p, half_rows, segments, group, after(scanned[p]), states[p], decay, residue, toks, width, grad_input

time: 86.4 us -> 77 us (0.89)
  waiting for transfers between devices: 14.9 us -> 4.23 us
  starting transfers between devices: 31 us -> 35.4 us
  Pallas kernels: 28.6 us -> 26.9 us
  local copies, waits for them, and re-layouts: 10.4 us -> 8.99 us
    ppermute x16 -> x14, waiting for transfers between devices: 14.9 us -> 4.07 us  [local(): arrived = lax.ppermute(last, 'ch', [(i, i ^ bit) for i in range(size)])]
    ppermute x16 -> x14, starting transfers between devices: 24.4 us -> 28.8 us  [local(): arrived = lax.ppermute(last, 'ch', [(i, i ^ bit) for i in range(size)])]
    unnamed x22, local copies, waits for them, and re-layouts: 10.3 us -> 8.9 us
    pallas_call x2, Pallas kernels: 5.05 us -> 4.07 us  [gate(): pl.pallas_call(functools.partial(gate_kernel, half, rows, segments, piece...]
    pallas_call x17 -> x15, Pallas kernels: 14 us -> 13.2 us  [send(): pl.pallas_call(functools.partial(send_kernel, items, coded, width, len(ne...]
  transfers between devices with their start and end apart: 18 -> 16, of which waited for: 3 -> 7; matrix products, arithmetic and copies ran while one was open for 0% -> 0% of each run, Pallas kernels for 28% -> 30%
where the time goes in v7:
time: 77 us; the launch traced here: 76.5 us
  starting transfers between devices  35.4 us (46%)
  Pallas kernels  26.9 us (35%)
  local copies, waits for them, and re-layouts  8.99 us (12%)
  waiting for transfers between devices  4.23 us (5%)
  between operations  0.96 us (1%)
    ppermute x14, starting transfers between devices, local(): arrived = lax.ppermute(last, 'ch', [(i, i ^ bit) for i in range(size)])  28.8 us
    pallas_call x15, Pallas kernels, send(): pl.pallas_call(functools.partial(send_kernel, items, coded, width, len(ne...  13.2 us
    unnamed x22, local copies, waits for them, and re-layouts  8.9 us
    all_to_all x2, starting transfers between devices, local(): states[p] = lax.all_to_all(packed, 'ctx', 0, 0, tiled=True)  6.66 us
    ppermute x14, waiting for transfers between devices, local(): arrived = lax.ppermute(last, 'ch', [(i, i ^ bit) for i in range(size)])  4.07 us
    pallas_call x2, Pallas kernels, gate(): pl.pallas_call(functools.partial(gate_kernel, half, rows, segments, piece...  4.07 us
    pallas_call x2, Pallas kernels, fix(): pl.pallas_call(functools.partial(fix_kernel, half, segments), in_specs=[p...  3.71 us
    pallas_call x2, Pallas kernels, scan(): pl.pallas_call(functools.partial(scan_kernel, half, segments), in_specs=[...  3.46 us
  transfers between devices with their start and end apart: 16, of which 7 were waited for; matrix products, arithmetic and copies ran while one was open for 0% of the time, Pallas kernels for 30%

profile of v7, /device:TPU:0, one launch (start us, length us, event | category | flops | bytes accessed | tf_op | source)
XLA Modules:
  0.0 76.5 jit_solution(3696250949095965402)
XLA Ops:
  0.6 0.0 copy-start
  0.6 2.4 %shard_map.77 = (bf16[528,256]{1,0:T(8,128)(2,1)S(1)}, bf16[1024,256]{1,0:T(8,128)(2,1)S(1)}) custom-call(s32[1]{0:T(128)} %bitcast.place_ref, bf16[8192,1024]{1,0:T(8,128)(2,1)} %w_ref.29, bf16[256,1024]{1,0:T(8,128)(2,1)} %g_hbm.1), custom_call_target="tpu_custom_call" | custom-call | bytes 1024 | tf_op jit(solution)/shard_map/pallas_call | solution.py:143
  3.1 3.0 %collective-permute-start = (bf16[528,256]{1,0:T(8,128)(2,1)S(1)}, bf16[528,256]{1,0:T(8,128)(2,1)S(1)}, u32[]{:S(2)}, u32[]{:S(2)}) collective-permute-start(bf16[528,256]{1,0:T(8,128)(2,1)S(1)} %get-tuple-element.30), channel_id=1, source_target_pairs={{0,1},{1,0},{2,3},{3,2},{4,5},{5,4},{6,7},{7,6},{8,9},{9,8},{10,11... | collective-permute-start | bytes 811016 | tf_op jit(solution)/shard_map/ppermute | solution.py:444
  6.1 0.8 %copy-done = bf16[8192,1024]{1,0:T(8,128)(2,1)S(1)} copy-done((bf16[8192,1024]{1,0:T(8,128)(2,1)S(1)}, bf16[8192,1024]{1,0:T(8,128)(2,1)}, u32[]{:S(2)}) %copy-start) | copy-done | bytes 16777240
  6.9 0.6 shard_map.78
  7.5 3.0 %collective-permute-start.1 = (bf16[528,256]{1,0:T(8,128)(2,1)S(1)}, bf16[528,256]{1,0:T(8,128)(2,1)S(1)}, u32[]{:S(2)}, u32[]{:S(2)}) collective-permute-start(bf16[528,256]{1,0:T(8,128)(2,1)S(1)} %shard_map.78), channel_id=1, source_target_pairs={{0,1},{1,0},{2,3},{3,2},{4,5},{5,4},{6,7},{7,6},{8,9},{9,8},{10,11... | collective-permute-start | bytes 811016 | tf_op jit(solution)/shard_map/ppermute | solution.py:444
  10.5 0.6 shard_map.79
  11.2 0.1 collective-permute-start.2
  11.3 0.6 shard_map.80
  11.9 0.6 shard_map.81
  12.5 0.9 %collective-permute-done.refs_0_ = bf16[528,256]{1,0:T(8,128)(2,1)S(1)} collective-permute-done((bf16[528,256]{1,0:T(8,128)(2,1)S(1)}, bf16[528,256]{1,0:T(8,128)(2,1)S(1)}, u32[]{:S(2)}, u32[]{:S(2)}) %collective-permute-start) | collective-permute-done | bytes 270368 | tf_op jit(solution)/shard_map/ppermute | solution.py:444
  13.4 0.7 shard_map.82
  14.1 2.2 %collective-permute-start.3 = (bf16[528,256]{1,0:T(8,128)(2,1)S(1)}, bf16[528,256]{1,0:T(8,128)(2,1)S(1)}, u32[]{:S(2)}, u32[]{:S(2)}) collective-permute-start(bf16[528,256]{1,0:T(8,128)(2,1)S(1)} %shard_map.82), channel_id=1, source_target_pairs={{0,2},{1,3},{2,0},{3,1},{4,6},{5,7},{6,4},{7,5},{8,10},{9,11},{10,... | collective-permute-start | bytes 811016 | tf_op jit(solution)/shard_map/ppermute | solution.py:444
  16.3 0.6 shard_map.83
  17.0 1.6 %collective-permute-start.4 = (bf16[528,256]{1,0:T(8,128)(2,1)S(1)}, bf16[528,256]{1,0:T(8,128)(2,1)S(1)}, u32[]{:S(2)}, u32[]{:S(2)}) collective-permute-start(bf16[528,256]{1,0:T(8,128)(2,1)S(1)} %shard_map.83), channel_id=1, source_target_pairs={{0,1},{1,0},{2,3},{3,2},{4,5},{5,4},{6,7},{7,6},{8,9},{9,8},{10,11... | collective-permute-start | bytes 811016 | tf_op jit(solution)/shard_map/ppermute | solution.py:444
  18.5 0.6 collective-permute-done.1.refs_0_
  19.2 0.7 shard_map.84
  19.9 2.2 %collective-permute-start.5 = (bf16[528,256]{1,0:T(8,128)(2,1)S(1)}, bf16[528,256]{1,0:T(8,128)(2,1)S(1)}, u32[]{:S(2)}, u32[]{:S(2)}) collective-permute-start(bf16[528,256]{1,0:T(8,128)(2,1)S(1)} %shard_map.84), channel_id=1, source_target_pairs={{0,2},{1,3},{2,0},{3,1},{4,6},{5,7},{6,4},{7,5},{8,10},{9,11},{10,... | collective-permute-start | bytes 811016 | tf_op jit(solution)/shard_map/ppermute | solution.py:444
  22.1 1.5 %collective-permute-start.6 = (bf16[528,256]{1,0:T(8,128)(2,1)S(1)}, bf16[528,256]{1,0:T(8,128)(2,1)S(1)}, u32[]{:S(2)}, u32[]{:S(2)}) collective-permute-start(bf16[528,256]{1,0:T(8,128)(2,1)S(1)} %shard_map.80), channel_id=1, source_target_pairs={{0,1},{1,0},{2,3},{3,2},{4,5},{5,4},{6,7},{7,6},{8,9},{9,8},{10,11... | collective-permute-start | bytes 811016 | tf_op jit(solution)/shard_map/ppermute | solution.py:444
  23.6 0.6 shard_map.85
  24.3 0.7 collective-permute-done.2.refs_0_
  25.0 2.1 %collective-permute-start.7 = (bf16[528,256]{1,0:T(8,128)(2,1)S(1)}, bf16[528,256]{1,0:T(8,128)(2,1)S(1)}, u32[]{:S(2)}, u32[]{:S(2)}) collective-permute-start(bf16[528,256]{1,0:T(8,128)(2,1)S(1)} %shard_map.85), channel_id=1, source_target_pairs={{0,1},{1,0},{2,3},{3,2},{4,5},{5,4},{6,7},{7,6},{8,9},{9,8},{10,11... | collective-permute-start | bytes 811016 | tf_op jit(solution)/shard_map/ppermute | solution.py:444
  27.0 0.0 collective-permute-done.3.refs_1_
  27.0 0.9 %shard_map.86 = bf16[528,256]{1,0:T(8,128)(2,1)S(1)} custom-call(s32[1]{0:T(128)} %bitcast.place_ref, bf16[8192,1024]{1,0:T(8,128)(2,1)S(1)} %copy-done, bf16[1024,256]{1,0:T(8,128)(2,1)S(1)} %get-tuple-element.32.turned_ref, bf16[528,256]{1,0:T(8,128)(2,1)S(1)} %collective-permute-done.2.refs_0_, bf16[528,256]{1,0:T(8,128)(2,1)S(1)} %collective-permute-done.3.refs_1_), custom_call_target="tpu_custom_call" | custom-call | bytes 1024 | tf_op jit(solution)/shard_map/pallas_call | solution.py:97
  28.0 2.7 %collective-permute-start.8 = (bf16[528,256]{1,0:T(8,128)(2,1)S(1)}, bf16[528,256]{1,0:T(8,128)(2,1)S(1)}, u32[]{:S(2)}, u32[]{:S(2)}) collective-permute-start(bf16[528,256]{1,0:T(8,128)(2,1)S(1)} %shard_map.86), channel_id=1, source_target_pairs={{0,4},{1,5},{2,6},{3,7},{4,0},{5,1},{6,2},{7,3},{8,12},{9,13},{10,... | collective-permute-start | bytes 811016 | tf_op jit(solution)/shard_map/ppermute | solution.py:444
  30.6 0.1 collective-permute-done.4.refs_0_
  30.8 2.1 %collective-permute-start.9 = (bf16[528,256]{1,0:T(8,128)(2,1)S(1)}, bf16[528,256]{1,0:T(8,128)(2,1)S(1)}, u32[]{:S(2)}, u32[]{:S(2)}) collective-permute-start(bf16[528,256]{1,0:T(8,128)(2,1)S(1)} %shard_map.81), channel_id=1, source_target_pairs={{0,1},{1,0},{2,3},{3,2},{4,5},{5,4},{6,7},{7,6},{8,9},{9,8},{10,11... | collective-permute-start | bytes 811016 | tf_op jit(solution)/shard_map/ppermute | solution.py:444
  32.8 0.7 shard_map.87
  33.6 0.0 collective-permute-done.5.refs_1_
  33.6 1.6 %collective-permute-start.10 = (bf16[528,256]{1,0:T(8,128)(2,1)S(1)}, bf16[528,256]{1,0:T(8,128)(2,1)S(1)}, u32[]{:S(2)}, u32[]{:S(2)}) collective-permute-start(bf16[528,256]{1,0:T(8,128)(2,1)S(1)} %shard_map.87), channel_id=1, source_target_pairs={{0,2},{1,3},{2,0},{3,1},{4,6},{5,7},{6,4},{7,5},{8,10},{9,11},{10,... | collective-permute-start | bytes 811016 | tf_op jit(solution)/shard_map/ppermute | solution.py:444
  35.2 1.3 %shard_map.88 = bf16[528,256]{1,0:T(8,128)(2,1)} custom-call(s32[1]{0:T(128)} %bitcast.place_ref, bf16[8192,1024]{1,0:T(8,128)(2,1)S(1)} %copy-done, bf16[1024,256]{1,0:T(8,128)(2,1)S(1)} %get-tuple-element.32.turned_ref), custom_call_target="tpu_custom_call" | custom-call | bytes 1024 | tf_op jit(solution)/shard_map/pallas_call | solution.py:97
  36.6 0.0 collective-permute-done.6.refs_0_
  36.6 1.6 %shard_map.89 = bf16[528,256]{1,0:T(8,128)(2,1)} custom-call(s32[1]{0:T(128)} %bitcast.place_ref, bf16[8192,1024]{1,0:T(8,128)(2,1)S(1)} %copy-done, bf16[1024,256]{1,0:T(8,128)(2,1)S(1)} %get-tuple-element.32.turned_ref, bf16[528,256]{1,0:T(8,128)(2,1)S(1)} %collective-permute-done.6.refs_0_, bf16[528,256]{1,0:T(8,128)(2,1)S(1)} %collective-permute-done.5.refs_1_), custom_call_target="tpu_custom_call" | custom-call | bytes 1024 | tf_op jit(solution)/shard_map/pallas_call | solution.py:97
  38.2 3.1 %collective-permute-start.11 = (bf16[528,256]{1,0:T(8,128)(2,1)}, bf16[528,256]{1,0:T(8,128)(2,1)S(1)}, u32[]{:S(2)}, u32[]{:S(2)}) collective-permute-start(bf16[528,256]{1,0:T(8,128)(2,1)} %shard_map.89), channel_id=1, source_target_pairs={{0,4},{1,5},{2,6},{3,7},{4,0},{5,1},{6,2},{7,3},{8,12},{9,13},{10,... | collective-permute-start | bytes 811016 | tf_op jit(solution)/shard_map/ppermute | solution.py:444
  41.4 1.0 %collective-permute-done.7.refs_0_ = bf16[528,256]{1,0:T(8,128)(2,1)S(1)} collective-permute-done((bf16[528,256]{1,0:T(8,128)(2,1)S(1)}, bf16[528,256]{1,0:T(8,128)(2,1)S(1)}, u32[]{:S(2)}, u32[]{:S(2)}) %collective-permute-start.7) | collective-permute-done | bytes 270368 | tf_op jit(solution)/shard_map/ppermute | solution.py:444
  42.4 2.1 %collective-permute-start.12 = (bf16[528,256]{1,0:T(8,128)(2,1)}, bf16[528,256]{1,0:T(8,128)(2,1)}, u32[]{:S(2)}, u32[]{:S(2)}) collective-permute-start(bf16[528,256]{1,0:T(8,128)(2,1)} %shard_map.88), channel_id=1, source_target_pairs={{0,1},{1,0},{2,3},{3,2},{4,5},{5,4},{6,7},{7,6},{8,9},{9,8},{10,11... | collective-permute-start | bytes 811016 | tf_op jit(solution)/shard_map/ppermute | solution.py:444
  44.4 1.5 %shard_map.90 = bf16[528,256]{1,0:T(8,128)(2,1)} custom-call(s32[1]{0:T(128)} %bitcast.place_ref, bf16[8192,1024]{1,0:T(8,128)(2,1)S(1)} %copy-done, bf16[1024,256]{1,0:T(8,128)(2,1)S(1)} %get-tuple-element.32.turned_ref, bf16[528,256]{1,0:T(8,128)(2,1)S(1)} %collective-permute-done.7.refs_0_), custom_call_target="tpu_custom_call" | custom-call | bytes 1024 | tf_op jit(solution)/shard_map/pallas_call | solution.py:97
  45.9 0.0 collective-permute-done.8.refs_1_
  45.9 1.6 %collective-permute-start.13 = (bf16[528,256]{1,0:T(8,128)(2,1)}, bf16[528,256]{1,0:T(8,128)(2,1)S(1)}, u32[]{:S(2)}, u32[]{:S(2)}) collective-permute-start(bf16[528,256]{1,0:T(8,128)(2,1)} %shard_map.90), channel_id=1, source_target_pairs={{0,2},{1,3},{2,0},{3,1},{4,6},{5,7},{6,4},{7,5},{8,10},{9,11},{10,... | collective-permute-start | bytes 811016 | tf_op jit(solution)/shard_map/ppermute | solution.py:444
  47.5 0.0 copy-done.8
  47.5 0.7 collective-permute-done.9.refs_0_
  48.2 0.5 shard_map.91.acc_ref
  48.6 0.0 collective-permute-done.10.refs_0_
  48.7 0.0 copy-done.2
  48.7 2.0 %shard_map.92 = (bf16[256,1024]{1,0:T(8,128)(2,1)}, f32[1024,128]{1,0:T(8,128)S(1)}, f32[16,8,128]{2,1,0:T(8,128)S(1)}, f32[4,8,8,128]{3,2,1,0:T(8,128)}) custom-call(f32[512,256]{1,0:T(8,128)S(1)} %shard_map.91.acc_ref, bf16[528,256]{1,0:T(8,128)(2,1)S(1)} %collective-permute-done.10.refs_0_, bf16[528,256]{1,0:T(8,128)(2,1)S(1)} %collective-permute-done.8.refs_1_, ...), custom_call_target="tpu_custom_call" | custom-call | bytes 1024 | tf_op jit(solution)/shard_map/pallas_call | solution.py:243
  50.8 3.3 %all-to-all-start = ((f32[4,8,8,128]{3,2,1,0:T(8,128)}), f32[4,8,8,128]{3,2,1,0:T(8,128)S(1)}, u32[]{:S(2)}, u32[]{:S(2)}) async-start(f32[4,8,8,128]{3,2,1,0:T(8,128)} %get-tuple-element.47), calls=%async_computation | async-start | bytes 262144 | tf_op jit(solution)/shard_map/all_to_all | solution.py:424
  54.1 0.0 copy-done.9
  54.2 0.0 collective-permute-done.11.refs_1_
  54.2 0.8 %copy-done.7 = f32[16,8,128]{2,1,0:T(8,128)S(1)} copy-done((f32[16,8,128]{2,1,0:T(8,128)S(1)}, f32[16,8,128]{2,1,0:T(8,128)}, u32[]{:S(2)}) %copy-start.7) | copy-done | bytes 65560
  55.1 1.7 %shard_map.93.rows_in_ref = f32[1024,128]{1,0:T(8,128)S(1)} custom-call(f32[1024,128]{1,0:T(8,128)S(1)} %get-tuple-element.48.gc_ref, f32[16,8,128]{2,1,0:T(8,128)S(1)} %copy-done.7, f32[16,16,128]{2,1,0:T(8,128)S(1)} %bitcast.11, f32[16,16,128]{2,1,0:T(8,128)S(1)} %bitcast.16), custom_call_target="tpu_custom_call" | custom-call | bytes 1024 | tf_op jit(solution)/shard_map/pallas_call | solution.py:293
  56.8 0.0 collective-permute-done.12.refs_0_
  56.8 0.0 copy-start.1
  56.8 5.8 %copy-done.1 = bf16[8192,1024]{1,0:T(8,128)(2,1)S(1)} copy-done((bf16[8192,1024]{1,0:T(8,128)(2,1)S(1)}, bf16[8192,1024]{1,0:T(8,128)(2,1)}, u32[]{:S(2)}) %copy-start.1) | copy-done | bytes 16777240
  62.6 1.4 %shard_map.94.acc_ref = f32[512,256]{1,0:T(8,128)S(1)} custom-call(s32[1]{0:T(128)} %bitcast.place_ref, bf16[8192,1024]{1,0:T(8,128)(2,1)S(1)} %copy-done.1, bf16[1024,256]{1,0:T(8,128)(2,1)S(1)} %get-tuple-element.32.turned_ref, bf16[528,256]{1,0:T(8,128)(2,1)} %collective-permute-done.12.refs_0_), custom_call_target="tpu_custom_call" | custom-call | bytes 1024 | tf_op jit(solution)/shard_map/pallas_call | solution.py:97
  64.0 0.0 collective-permute-done.13.refs_0_
  64.1 2.0 %shard_map.95 = (bf16[256,1024]{1,0:T(8,128)(2,1)}, f32[1024,128]{1,0:T(8,128)S(1)}, f32[16,8,128]{2,1,0:T(8,128)S(1)}, f32[4,8,8,128]{3,2,1,0:T(8,128)}) custom-call(f32[512,256]{1,0:T(8,128)S(1)} %shard_map.94.acc_ref, bf16[528,256]{1,0:T(8,128)(2,1)S(1)} %collective-permute-done.13.refs_0_, ...), custom_call_target="tpu_custom_call", output_to_operand_aliasing={{0}: (6, {})} | custom-call | bytes 1024 | tf_op jit(solution)/shard_map/pallas_call | solution.py:243
  66.1 0.6 copy-done.4
  66.7 0.0 all-to-all-done.states_ref
  66.7 3.3 %all-to-all-start.1 = ((f32[4,8,8,128]{3,2,1,0:T(8,128)}), f32[4,8,8,128]{3,2,1,0:T(8,128)S(1)}, u32[]{:S(2)}, u32[]{:S(2)}) async-start(f32[4,8,8,128]{3,2,1,0:T(8,128)} %get-tuple-element.54), calls=%async_computation.1 | async-start | bytes 262144 | tf_op jit(solution)/shard_map/all_to_all | solution.py:424
  70.1 1.9 %shard_map.96.refs_0_ = bf16[256,1024]{1,0:T(8,128)(2,1)} custom-call(s32[1]{0:T(128)} %bitcast.5.group_ref, f32[1024,128]{1,0:T(8,128)S(1)} %shard_map.93.rows_in_ref, f32[4,8,8,128]{3,2,1,0:T(8,128)S(1)} %all-to-all-done.states_ref, f32[16,16,128]{2,1,0:T(8,128)S(1)} %bitcast.13, f32[16,16,128]{2,1,0:T(8,128)S(1)} %bitcast.17), custom_call_target="tpu_custom_call" | custom-call | bytes 1024 | tf_op jit(solution)/shard_map/pallas_call | solution.py:345
  71.9 0.8 %copy-done.5 = f32[16,8,128]{2,1,0:T(8,128)S(1)} copy-done((f32[16,8,128]{2,1,0:T(8,128)S(1)}, f32[16,8,128]{2,1,0:T(8,128)}, u32[]{:S(2)}) %copy-start.5) | copy-done | bytes 65560
  72.8 1.7 %shard_map.97.rows_in_ref = f32[1024,128]{1,0:T(8,128)S(1)} custom-call(f32[1024,128]{1,0:T(8,128)S(1)} %get-tuple-element.56.gc_ref, f32[16,8,128]{2,1,0:T(8,128)S(1)} %copy-done.5, f32[16,16,128]{2,1,0:T(8,128)S(1)} %bitcast.14, f32[16,16,128]{2,1,0:T(8,128)S(1)} %bitcast.18), custom_call_target="tpu_custom_call" | custom-call | bytes 1024 | tf_op jit(solution)/shard_map/pallas_call | solution.py:293
  74.5 0.2 all-to-all-done.1.states_ref
  74.7 1.9 %shard_map.98 = bf16[256,1024]{1,0:T(8,128)(2,1)} custom-call(s32[1]{0:T(128)} %bitcast.5.group_ref, f32[1024,128]{1,0:T(8,128)S(1)} %shard_map.97.rows_in_ref, f32[4,8,8,128]{3,2,1,0:T(8,128)S(1)} %all-to-all-done.1.states_ref, f32[16,16,128]{2,1,0:T(8,128)S(1)} %bitcast.15, f32[16,16,128]{2,1,0:T(8,128)S(1)} %bitcast.19, ...), custom_call_target="tpu_custom_call", output_to_operand_aliasing={{}: (5, {})} | custom-call | bytes 1024 | tf_op jit(solution)/shard_map/pallas_call | solution.py:345
  (14 shorter events, 0.1 us)
Async XLA Ops:
  0.6 6.2 %copy-start = (bf16[8192,1024]{1,0:T(8,128)(2,1)S(1)}, bf16[8192,1024]{1,0:T(8,128)(2,1)}, u32[]{:S(2)}) copy-start(bf16[8192,1024]{1,0:T(8,128)(2,1)} %w_ref.29) | copy-start | bytes 50331652
  3.1 10.3 %collective-permute-start = (bf16[528,256]{1,0:T(8,128)(2,1)S(1)}, bf16[528,256]{1,0:T(8,128)(2,1)S(1)}, u32[]{:S(2)}, u32[]{:S(2)}) collective-permute-start(bf16[528,256]{1,0:T(8,128)(2,1)S(1)} %get-tuple-element.30), channel_id=1, source_target_pairs={{0,1},{1,0},{2,3},{3,2},{4,5},{5,4},{6,7},{7,6},{8,9},{9,8},{10,11... | collective-permute-start | bytes 811016 | tf_op jit(solution)/shard_map/ppermute | solution.py:444
  7.5 11.7 %collective-permute-start.1 = (bf16[528,256]{1,0:T(8,128)(2,1)S(1)}, bf16[528,256]{1,0:T(8,128)(2,1)S(1)}, u32[]{:S(2)}, u32[]{:S(2)}) collective-permute-start(bf16[528,256]{1,0:T(8,128)(2,1)S(1)} %shard_map.78), channel_id=1, source_target_pairs={{0,1},{1,0},{2,3},{3,2},{4,5},{5,4},{6,7},{7,6},{8,9},{9,8},{10,11... | collective-permute-start | bytes 811016 | tf_op jit(solution)/shard_map/ppermute | solution.py:444
  11.2 13.8 %collective-permute-start.2 = (bf16[528,256]{1,0:T(8,128)(2,1)S(1)}, bf16[528,256]{1,0:T(8,128)(2,1)S(1)}, u32[]{:S(2)}, u32[]{:S(2)}) collective-permute-start(bf16[528,256]{1,0:T(8,128)(2,1)S(1)} %shard_map.79), channel_id=1, source_target_pairs={{0,1},{1,0},{2,3},{3,2},{4,5},{5,4},{6,7},{7,6},{8,9},{9,8},{10,11... | collective-permute-start | bytes 811016 | tf_op jit(solution)/shard_map/ppermute | solution.py:444
  14.1 12.9 %collective-permute-start.3 = (bf16[528,256]{1,0:T(8,128)(2,1)S(1)}, bf16[528,256]{1,0:T(8,128)(2,1)S(1)}, u32[]{:S(2)}, u32[]{:S(2)}) collective-permute-start(bf16[528,256]{1,0:T(8,128)(2,1)S(1)} %shard_map.82), channel_id=1, source_target_pairs={{0,2},{1,3},{2,0},{3,1},{4,6},{5,7},{6,4},{7,5},{8,10},{9,11},{10,... | collective-permute-start | bytes 811016 | tf_op jit(solution)/shard_map/ppermute | solution.py:444
  17.0 13.8 %collective-permute-start.4 = (bf16[528,256]{1,0:T(8,128)(2,1)S(1)}, bf16[528,256]{1,0:T(8,128)(2,1)S(1)}, u32[]{:S(2)}, u32[]{:S(2)}) collective-permute-start(bf16[528,256]{1,0:T(8,128)(2,1)S(1)} %shard_map.83), channel_id=1, source_target_pairs={{0,1},{1,0},{2,3},{3,2},{4,5},{5,4},{6,7},{7,6},{8,9},{9,8},{10,11... | collective-permute-start | bytes 811016 | tf_op jit(solution)/shard_map/ppermute | solution.py:444
  19.9 13.6 %collective-permute-start.5 = (bf16[528,256]{1,0:T(8,128)(2,1)S(1)}, bf16[528,256]{1,0:T(8,128)(2,1)S(1)}, u32[]{:S(2)}, u32[]{:S(2)}) collective-permute-start(bf16[528,256]{1,0:T(8,128)(2,1)S(1)} %shard_map.84), channel_id=1, source_target_pairs={{0,2},{1,3},{2,0},{3,1},{4,6},{5,7},{6,4},{7,5},{8,10},{9,11},{10,... | collective-permute-start | bytes 811016 | tf_op jit(solution)/shard_map/ppermute | solution.py:444
  22.1 14.5 %collective-permute-start.6 = (bf16[528,256]{1,0:T(8,128)(2,1)S(1)}, bf16[528,256]{1,0:T(8,128)(2,1)S(1)}, u32[]{:S(2)}, u32[]{:S(2)}) collective-permute-start(bf16[528,256]{1,0:T(8,128)(2,1)S(1)} %shard_map.80), channel_id=1, source_target_pairs={{0,1},{1,0},{2,3},{3,2},{4,5},{5,4},{6,7},{7,6},{8,9},{9,8},{10,11... | collective-permute-start | bytes 811016 | tf_op jit(solution)/shard_map/ppermute | solution.py:444
  25.0 17.4 %collective-permute-start.7 = (bf16[528,256]{1,0:T(8,128)(2,1)S(1)}, bf16[528,256]{1,0:T(8,128)(2,1)S(1)}, u32[]{:S(2)}, u32[]{:S(2)}) collective-permute-start(bf16[528,256]{1,0:T(8,128)(2,1)S(1)} %shard_map.85), channel_id=1, source_target_pairs={{0,1},{1,0},{2,3},{3,2},{4,5},{5,4},{6,7},{7,6},{8,9},{9,8},{10,11... | collective-permute-start | bytes 811016 | tf_op jit(solution)/shard_map/ppermute | solution.py:444
  28.0 17.9 %collective-permute-start.8 = (bf16[528,256]{1,0:T(8,128)(2,1)S(1)}, bf16[528,256]{1,0:T(8,128)(2,1)S(1)}, u32[]{:S(2)}, u32[]{:S(2)}) collective-permute-start(bf16[528,256]{1,0:T(8,128)(2,1)S(1)} %shard_map.86), channel_id=1, source_target_pairs={{0,4},{1,5},{2,6},{3,7},{4,0},{5,1},{6,2},{7,3},{8,12},{9,13},{10,... | collective-permute-start | bytes 811016 | tf_op jit(solution)/shard_map/ppermute | solution.py:444
  30.8 17.4 %collective-permute-start.9 = (bf16[528,256]{1,0:T(8,128)(2,1)S(1)}, bf16[528,256]{1,0:T(8,128)(2,1)S(1)}, u32[]{:S(2)}, u32[]{:S(2)}) collective-permute-start(bf16[528,256]{1,0:T(8,128)(2,1)S(1)} %shard_map.81), channel_id=1, source_target_pairs={{0,1},{1,0},{2,3},{3,2},{4,5},{5,4},{6,7},{7,6},{8,9},{9,8},{10,11... | collective-permute-start | bytes 811016 | tf_op jit(solution)/shard_map/ppermute | solution.py:444
  33.6 15.1 %collective-permute-start.10 = (bf16[528,256]{1,0:T(8,128)(2,1)S(1)}, bf16[528,256]{1,0:T(8,128)(2,1)S(1)}, u32[]{:S(2)}, u32[]{:S(2)}) collective-permute-start(bf16[528,256]{1,0:T(8,128)(2,1)S(1)} %shard_map.87), channel_id=1, source_target_pairs={{0,2},{1,3},{2,0},{3,1},{4,6},{5,7},{6,4},{7,5},{8,10},{9,11},{10,... | collective-permute-start | bytes 811016 | tf_op jit(solution)/shard_map/ppermute | solution.py:444
  36.6 10.9 %copy-start.8 = (f32[1024,16]{0,1:T(8,128)S(1)}, f32[1024,16]{0,1:T(8,128)}, u32[]{:S(2)}) copy-start(f32[1024,16]{0,1:T(8,128)} %param.11) | copy-start | bytes 196612
  38.2 10.5 %copy-start.2 = (bf16[256,1024]{1,0:T(8,128)(2,1)S(1)}, bf16[256,1024]{1,0:T(8,128)(2,1)}, u32[]{:S(2)}) copy-start(bf16[256,1024]{1,0:T(8,128)(2,1)} %refs_2_.3) | copy-start | bytes 1572868
  38.2 10.5 %copy-start.3 = (bf16[256,1024]{1,0:T(8,128)(2,1)S(1)}, bf16[256,1024]{1,0:T(8,128)(2,1)}, u32[]{:S(2)}) copy-start(bf16[256,1024]{1,0:T(8,128)(2,1)} %refs_3_.3) | copy-start | bytes 1572868
  38.2 15.9 %copy-start.9 = (f32[1024,16]{0,1:T(8,128)S(1)}, f32[1024,16]{0,1:T(8,128)}, u32[]{:S(2)}) copy-start(f32[1024,16]{0,1:T(8,128)} %param.10) | copy-start | bytes 196612
  38.2 15.9 %collective-permute-start.11 = (bf16[528,256]{1,0:T(8,128)(2,1)}, bf16[528,256]{1,0:T(8,128)(2,1)S(1)}, u32[]{:S(2)}, u32[]{:S(2)}) collective-permute-start(bf16[528,256]{1,0:T(8,128)(2,1)} %shard_map.89), channel_id=1, source_target_pairs={{0,4},{1,5},{2,6},{3,7},{4,0},{5,1},{6,2},{7,3},{8,12},{9,13},{10,... | collective-permute-start | bytes 811016 | tf_op jit(solution)/shard_map/ppermute | solution.py:444
  42.4 14.5 %collective-permute-start.12 = (bf16[528,256]{1,0:T(8,128)(2,1)}, bf16[528,256]{1,0:T(8,128)(2,1)}, u32[]{:S(2)}, u32[]{:S(2)}) collective-permute-start(bf16[528,256]{1,0:T(8,128)(2,1)} %shard_map.88), channel_id=1, source_target_pairs={{0,1},{1,0},{2,3},{3,2},{4,5},{5,4},{6,7},{7,6},{8,9},{9,8},{10,11... | collective-permute-start | bytes 811016 | tf_op jit(solution)/shard_map/ppermute | solution.py:444
  45.9 18.2 %collective-permute-start.13 = (bf16[528,256]{1,0:T(8,128)(2,1)}, bf16[528,256]{1,0:T(8,128)(2,1)S(1)}, u32[]{:S(2)}, u32[]{:S(2)}) collective-permute-start(bf16[528,256]{1,0:T(8,128)(2,1)} %shard_map.90), channel_id=1, source_target_pairs={{0,2},{1,3},{2,0},{3,1},{4,6},{5,7},{6,4},{7,5},{8,10},{9,11},{10,... | collective-permute-start | bytes 811016 | tf_op jit(solution)/shard_map/ppermute | solution.py:444
  50.8 3.4 %copy-start.6 = (f32[16,8,128]{2,1,0:T(8,128)}, f32[16,8,128]{2,1,0:T(8,128)S(1)}, u32[]{:S(2)}) copy-start(f32[16,8,128]{2,1,0:T(8,128)S(1)} %get-tuple-element.49.state_ref) | copy-start | bytes 196612
  50.8 15.9 %all-to-all-start = ((f32[4,8,8,128]{3,2,1,0:T(8,128)}), f32[4,8,8,128]{3,2,1,0:T(8,128)S(1)}, u32[]{:S(2)}, u32[]{:S(2)}) async-start(f32[4,8,8,128]{3,2,1,0:T(8,128)} %get-tuple-element.47), calls=%async_computation | async-start | bytes 262144 | tf_op jit(solution)/shard_map/all_to_all | solution.py:424
  54.2 0.8 %copy-start.7 = (f32[16,8,128]{2,1,0:T(8,128)S(1)}, f32[16,8,128]{2,1,0:T(8,128)}, u32[]{:S(2)}) copy-start(f32[16,8,128]{2,1,0:T(8,128)} %copy-done.6) | copy-start | bytes 196612
  56.8 5.8 %copy-start.1 = (bf16[8192,1024]{1,0:T(8,128)(2,1)S(1)}, bf16[8192,1024]{1,0:T(8,128)(2,1)}, u32[]{:S(2)}) copy-start(bf16[8192,1024]{1,0:T(8,128)(2,1)} %w_ref.29) | copy-start | bytes 50331652
  66.1 0.6 copy-start.4
  66.7 7.9 %all-to-all-start.1 = ((f32[4,8,8,128]{3,2,1,0:T(8,128)}), f32[4,8,8,128]{3,2,1,0:T(8,128)S(1)}, u32[]{:S(2)}, u32[]{:S(2)}) async-start(f32[4,8,8,128]{3,2,1,0:T(8,128)} %get-tuple-element.54), calls=%async_computation.1 | async-start | bytes 262144 | tf_op jit(solution)/shard_map/all_to_all | solution.py:424
  71.9 0.8 %copy-start.5 = (f32[16,8,128]{2,1,0:T(8,128)S(1)}, f32[16,8,128]{2,1,0:T(8,128)}, u32[]{:S(2)}) copy-start(f32[16,8,128]{2,1,0:T(8,128)} %copy-done.4) | copy-start | bytes 196612

commit v8 on v7

--- a/solution.py
+++ b/solution.py
@@ -12,16 +12,16 @@
 SPAN = 251 * math.log(2.0)
 SHIFT = 125 * math.log(2.0)
 STEP = 256
-VMEM = 12 * 1024 * 1024
+VMEM = 24 * 1024 * 1024
 QUICK = pl.CostEstimate(flops=0, bytes_accessed=1024, transcendentals=0)
 
 PORTIONS = (((0, 1, 2), 2, 0), ((0, 1, 2), 2, 1))
 ORDER = (
-    (0, 0, (6,)), (1, 0, (6,)), (0, 0, (4,)), (1, 0, (4,)), (0, 0, (0,)), (0, 1, (4,)), (0, 0, (2,)), (1, 1, (4,)),
-    (1, 0, (2,)), (0, 2, (0,)), (0, 1, (0,)), (1, 0, (0,)), (1, 2, (0,)), (1, 1, (0,)), (0, "sum"), (0, "gate"),
-    (0, "scan"), (1, "sum"), (1, "gate"), (0, "fix"), (1, "scan"), (1, "fix"),
+    ((1, 0, 6),), ((0, 0, 6),), ((1, 0, 4),), ((1, 0, 0),), ((0, 0, 2),), ((1, 1, 4),), ((0, 0, 4),), ((1, 0, 2),),
+    ((0, 1, 4),), ((1, 2, 0),), ((0, 0, 0),), ((0, 1, 0),), ((0, 2, 0),), ((1, 1, 0),), ("sum", 0), ("gate", 0),
+    ("sum", 1), ("gate", 1), ("scan", 1), ("fix", 1),
 )
-WAITS = {(0, "sum"): ((0, 2, 0),), (0, "scan"): ((1, 2, 0),), (1, 0, (0,)): ((1, 1, 4),)}
+WAITS = {((1, 1, 0),): ((1, 2, 0),), ((0, 0, 0),): ((0, 1, 4),)}
 
 
 def part_of(rows, blocks):
@@ -188,8 +188,10 @@
 
 def gate_kernel(half, rows, segments, pieces, near, acc_ref, *refs):
     near_refs, refs = refs[:near], refs[near:]
-    query_ref, conv_ref, decay_ref = refs[:3]
-    out_hbm, gc_ref, state_ref, pack_ref, gq_ref, sem = refs[-6:]
+    query_ref, conv_ref, decay_ref, other_ref = refs[:4]
+    out_hbm, rows_ref, state_ref, pack_ref = refs[-7:-3] if half == 0 else refs[-6:-2]
+    gq_ref, sem = refs[-2:]
+    gc_ref = refs[-3] if half == 0 else rows_ref
     toks = query_ref.shape[0]
     modes, sublanes, lanes = state_ref.shape
     mine = slice(half * sublanes, (half + 1) * sublanes)
@@ -209,8 +211,12 @@
     span = toks // segments
 
     def step(t, state):
-        row = gc_ref[pl.ds(t, sublanes, stride=span), :]
-        return tuple(decay[n] * state[n] + row for n in range(modes))
+        at = pl.ds(t, sublanes, stride=span)
+        row = gc_ref[at, :]
+        state = tuple(decay[n] * state[n] + row for n in range(modes))
+        if half == 0:
+            rows_ref[at, :] = summed([other_ref[n, mine] * state[n] for n in range(modes)])
+        return state
 
     zero = jnp.zeros((sublanes, lanes), jnp.float32)
     state = steps_back(span, step, (zero,) * modes, 8)
@@ -224,37 +230,43 @@
             for _ in range(segments - 1):
                 total = state[n] + factor * rolled(total, -1)
         whole.append(total)
-    for m in range(modes // segments):
+    packs = modes // segments
+    for m in range(packs):
         packed = whole[m * segments]
         for j in range(1, segments):
             packed = jnp.where(segment == j, rolled(whole[m * segments + j], j), packed)
-        for copy in range(pack_ref.shape[0]):
-            pack_ref[copy, m] = packed
+        if half == 0:
+            pack_ref[m] = packed
+        else:
+            pack_ref[m] = other_ref[m]
+            pack_ref[packs + m] = packed
     store.wait()
 
 
-def gate(half, rows, segments, copies, pieces, acc, nears, query_in, conv_out, decay, partial):
+def gate(half, rows, segments, pieces, acc, nears, query_in, conv_out, decay, other, partial):
     toks, width = query_in.shape
-    modes, sublanes, lanes = decay.shape
+    modes, _, lanes = decay.shape
     sublanes = rows // lanes * segments
     vmem = pl.BlockSpec(memory_space=pltpu.VMEM)
     high = pl.BlockSpec(memory_space=pltpu.HBM)
     more = [] if partial is None else [partial]
+    lines = (rows // lanes * toks, lanes)
     return pl.pallas_call(
         functools.partial(gate_kernel, half, rows, segments, pieces, len(nears)),
-        in_specs=[vmem] * (4 + len(nears)) + [high] * len(more),
+        in_specs=[vmem] * (5 + len(nears)) + [high] * len(more),
         out_specs=(high, vmem, vmem, vmem),
         out_shape=(
             jax.ShapeDtypeStruct((toks, width), jnp.bfloat16),
-            jax.ShapeDtypeStruct((rows // lanes * toks, lanes), jnp.float32),
+            jax.ShapeDtypeStruct(lines, jnp.float32),
             jax.ShapeDtypeStruct((modes, sublanes, lanes), jnp.float32),
-            jax.ShapeDtypeStruct((copies, modes // segments, sublanes, lanes), jnp.float32),
+            jax.ShapeDtypeStruct(((1 + half) * modes // segments, sublanes, lanes), jnp.float32),
         ),
-        scratch_shapes=[pltpu.VMEM((toks, rows), jnp.bfloat16), pltpu.SemaphoreType.DMA],
-        input_output_aliases={4 + len(nears): 0} if more else {},
+        scratch_shapes=([pltpu.VMEM(lines, jnp.float32)] if half == 0 else [])
+        + [pltpu.VMEM((toks, rows), jnp.bfloat16), pltpu.SemaphoreType.DMA],
+        input_output_aliases={5 + len(nears): 0} if more else {},
         compiler_params=pltpu.CompilerParams(vmem_limit_bytes=VMEM),
         cost_estimate=QUICK,
-    )(acc, *nears, query_in, conv_out, decay, *more)
+    )(acc, *nears, query_in, conv_out, decay, other, *more)
 
 
 def summed(terms):
@@ -300,62 +312,68 @@
     )(grad_conv, state, decay, residues)
 
 
-def fix_kernel(half, segments, group_ref, rows_in_ref, states_ref, decay_ref, residue_ref, *refs):
-    out_hbm, rows_ref, out_ref, sem = refs[-4:]
-    toks, rows = out_ref.shape
-    groups, _, sublanes, lanes = states_ref.shape
-    modes = decay_ref.shape[0]
-    mine = slice(half * sublanes, (half + 1) * sublanes)
+def fix_kernel(segments, hops, *refs):
+    scanned_refs, state_ref, later_refs = refs[:2], refs[2], refs[3 : 3 + hops]
+    decay_ref, residue_ref, out_hbm, rows_ref, out_ref, sems = refs[3 + hops :]
+    toks, width = out_ref.shape
+    modes, sublanes, lanes = state_ref.shape
+    packs = modes // segments
+    rows = width // 2
     span = toks // segments
     segment = segment_of((sublanes, lanes), segments)
-    decay = [decay_ref[n, mine] for n in range(modes)]
-    start = []
-    for n in range(modes):
-        lap = power(decay[n], span)
-        whole = power(lap, segments)
-        m, j = divmod(n, segments)
-        total = jnp.zeros((sublanes, lanes), jnp.float32)
-        for group in range(groups - 1, 0, -1):
-            state = rolled(states_ref[group, m], segments - 1 - j)
-            total = jnp.where(group > group_ref[0], total * whole + state, total)
-        for k in range(segments - 2, -1, -1):
-            total = jnp.where(segment == k, rolled(lap * total, -1), total)
-        start.append(residue_ref[n, mine] * total)
-
-    def step(t, state):
-        at = pl.ds(t, sublanes, stride=span)
-        state = tuple(decay[n] * state[n] for n in range(modes))
-        rows_ref[at, :] = rows_in_ref[at, :] + summed(list(state))
-        return state
-
-    steps_back(span, step, tuple(start), 8)
-    for line in range(rows // lanes):
-        out_ref[:, line * lanes : (line + 1) * lanes] = rows_ref[
-            line * toks : (line + 1) * toks, :
-        ].astype(jnp.bfloat16)
-    store = pltpu.make_async_copy(out_ref, out_hbm.at[:, pl.ds(half * rows, rows)], sem)
-    store.start()
-    store.wait()
-
-
-def fix(half, rows, segments, group, scanned, states, decay, residues, toks, width, partial):
+    stores = []
+    for half in range(2):
+        mine = slice(half * sublanes, (half + 1) * sublanes)
+        decay = [decay_ref[n, mine] for n in range(modes)]
+        start = []
+        for n in range(modes):
+            lap = power(decay[n], span)
+            whole = power(lap, segments)
+            m, j = divmod(n, segments)
+            arrived = [rolled(ref[half * packs + m], segments - 1 - j) for ref in later_refs]
+            total = arrived[-1]
+            for state in reversed(arrived[:-1]):
+                total = total * whole + state
+            for k in range(segments - 2, -1, -1):
+                brought = lap * total
+                if half == 0:
+                    brought = brought + state_ref[n]
+                total = jnp.where(segment == k, rolled(brought, -1), total)
+            start.append(residue_ref[n, mine] * total)
+
+        def step(t, state, scanned_ref=scanned_refs[half], decay=decay):
+            at = pl.ds(t, sublanes, stride=span)
+            state = tuple(decay[n] * state[n] for n in range(modes))
+            rows_ref[at, :] = scanned_ref[at, :] + summed(list(state))
+            return state
+
+        steps_back(span, step, tuple(start), 8)
+        for line in range(rows // lanes):
+            out_ref[:, half * rows + line * lanes : half * rows + (line + 1) * lanes] = rows_ref[
+                line * toks : (line + 1) * toks, :
+            ].astype(jnp.bfloat16)
+        columns = pl.ds(half * rows, rows)
+        stores.append(pltpu.make_async_copy(out_ref.at[:, columns], out_hbm.at[:, columns], sems.at[half]))
+        stores[-1].start()
+    for store in stores:
+        store.wait()
+
+
+def fix(segments, scanned, state, laters, decay, residues, toks, width):
     vmem = pl.BlockSpec(memory_space=pltpu.VMEM)
-    high = pl.BlockSpec(memory_space=pltpu.HBM)
-    more = [] if partial is None else [partial]
     return pl.pallas_call(
-        functools.partial(fix_kernel, half, segments),
-        in_specs=[pl.BlockSpec(memory_space=pltpu.SMEM)] + [vmem] * 4 + [high] * len(more),
-        out_specs=high,
+        functools.partial(fix_kernel, segments, len(laters)),
+        in_specs=[vmem] * (5 + len(laters)),
+        out_specs=pl.BlockSpec(memory_space=pltpu.HBM),
         out_shape=jax.ShapeDtypeStruct((toks, width), jnp.bfloat16),
         scratch_shapes=[
-            pltpu.VMEM(scanned.shape, jnp.float32),
-            pltpu.VMEM((toks, rows), jnp.bfloat16),
-            pltpu.SemaphoreType.DMA,
+            pltpu.VMEM(scanned[0].shape, jnp.float32),
+            pltpu.VMEM((toks, width), jnp.bfloat16),
+            pltpu.SemaphoreType.DMA((2,)),
         ],
-        input_output_aliases={5: 0} if more else {},
         compiler_params=pltpu.CompilerParams(vmem_limit_bytes=VMEM),
         cost_estimate=QUICK,
-    )(group, scanned, states, decay, residues, *more)
+    )(*scanned, state, *laters, decay, residues)
 
 
 def local(out_grad, out_weight, query_in, conv_out, residues, decay_rates):
@@ -365,7 +383,6 @@
     size, groups = lax.axis_size("ch"), lax.axis_size("ctx")
     bits = [1 << i for i in range(size.bit_length() - 1)]
     place = jnp.reshape(lax.axis_index("ch"), (1,)).astype(jnp.int32)
-    group = jnp.reshape(lax.axis_index("ctx"), (1,)).astype(jnp.int32)
     half_rows = width // 2
     lines = half_rows // lanes
     segments = 8 // lines
@@ -377,15 +394,15 @@
         waits = {}
         portions = ((tuple(range(len(bits))), 2, 0), (tuple(range(len(bits))), 2, 1))
         order = [
-            (p, s, (block,))
+            ((p, s, block),)
             for p in range(2)
             for s, bit in enumerate(bits)
             for block in sorted(range(0, size, 2 * bit), reverse=True)
-        ] + [(p, kind) for kind in ("sum", "gate", "scan", "fix") for p in range(2)]
+        ] + [("sum", 0), ("gate", 0), ("sum", 1), ("gate", 1), ("scan", 1), ("fix", 1)]
     offsets = [sum(width // part for _, part, _ in portions[:p]) for p in range(len(portions))]
 
-    received, sums, gated, scanned, states = {}, {}, {}, {}, {}
-    grad_query = grad_input = last = None
+    received, sums, scanned, states, packed = {}, {}, {}, {}, {}
+    grad_query = last = None
 
     def after(value):
         return value if last is None else lax.optimization_barrier((value, last, *awaited))[0]
@@ -400,51 +417,71 @@
             places.append((index, tuple(place)))
         return arrays, places
 
-    for p, s, *blocks in order:
-        awaited = [received[key][0] for key in waits.get((p, s, *blocks), ())]
-        inside = [q for q, (_, _, half) in enumerate(portions) if half == p]
-        if s == "sum":
-            arrays, places = collect([(q, 0, 0) for q in inside])
-            items = tuple((0, offsets[q], width // portions[q][1], (at,)) for q, at in zip(inside, places))
-            last = sums[p] = send(items, False, width, after(place), out_weight, turned, arrays)
-        elif s == "gate":
-            later = range(1, len(bits))
-            arrays, places = collect([(q, i, 0) for q in inside for i in later])
-            pieces = tuple(
-                (
-                    offsets[q] - p * half_rows,
-                    tuple(places[i * len(later) : (i + 1) * len(later)]),
-                )
-                for i, q in enumerate(inside)
-            )
-            grad_query, grad_conv, state, packed = gate(
-                p, half_rows, segments, groups, pieces, after(sums[p]), arrays, query_in, conv_out, decay, grad_query
-            )
-            last, gated[p] = packed, (grad_conv, state)
-            states[p] = lax.all_to_all(packed, "ctx", 0, 0, tiled=True)
-        elif s == "scan":
-            last = scanned[p] = scan(p, segments, after(gated[p][0]), gated[p][1], decay, residue)
-        elif s == "fix":
-            last = grad_input = fix(
-                p, half_rows, segments, group, after(scanned[p]), states[p], decay, residue, toks, width, grad_input
-            )
-        else:
-            route, part, _ = portions[p]
-            rows, (blocks,) = width // part, blocks
-            bit = bits[route[s]]
-            wanted = [(p, i, block ^ bit) for block in blocks for i in range(s)]
-            arrays, places = collect(wanted)
+    for todo in order:
+        awaited = [received[key][0] for key in waits.get(todo, ())]
+        kind, half = todo if isinstance(todo[0], str) else ("send", None)
+        inside = [q for q, (_, _, lies) in enumerate(portions) if lies == half]
+        if kind == "send":
+            arrays, items = [], []
+            wanted, rows, bits_of = [], [], []
+            for p, s, block in todo:
+                route, share, _ = portions[p]
+                bits_of.append(bits[route[s]])
+                rows.append(width // share)
+                wanted.append([(p, i, block ^ bits_of[-1]) for i in range(s)])
+            bit, count = bits_of[0], len(todo)
+            arrays, places = collect([key for keys in wanted for key in keys])
+            places = iter(places)
             items = tuple(
-                (block ^ bit, offsets[p], rows, tuple(places[i * s : (i + 1) * s])) for i, block in enumerate(blocks)
+                (block ^ bit, offsets[p], rows[i], tuple(next(places) for _ in wanted[i]))
+                for i, (p, _, block) in enumerate(todo)
             )
             if last is None:
                 last, turned = first_send(items, width, place, out_weight, out_grad)
             else:
                 last = send(items, True, width, after(place), out_weight, turned, arrays)
             arrived = lax.ppermute(last, "ch", [(i, i ^ bit) for i in range(size)])
-            each = part_of(rows, len(blocks))
-            for i, block in enumerate(blocks):
-                received[p, s, block] = (arrived, i * rows, i * (rows // each), each)
+            start = peak = 0
+            for i, key in enumerate(todo):
+                part = part_of(rows[i], count)
+                received[key] = (arrived, start, peak, part)
+                start, peak = start + rows[i], peak + rows[i] // part
+        elif kind == "sum":
+            arrays, places = collect([(q, 0, 0) for q in inside])
+            items = tuple((0, offsets[q], width // portions[q][1], (at,)) for q, at in zip(inside, places))
+            last = sums[half] = send(items, False, width, after(place), out_weight, turned, arrays)
+        elif kind == "gate":
+            later = range(1, len(bits))
+            arrays, places = collect([(q, i, 0) for q in inside for i in later])
+            pieces = tuple(
+                (offsets[q] - half * half_rows, tuple(places[i * len(later) : (i + 1) * len(later)]))
+                for i, q in enumerate(inside)
+            )
+            other = residue if half == 0 else packed[0]
+            grad_query, scanned[half], states[half], packed[half] = gate(
+                half,
+                half_rows,
+                segments,
+                pieces,
+                after(sums[half]),
+                arrays,
+                query_in,
+                conv_out,
+                decay,
+                other,
+                grad_query,
+            )
+            last = packed[half]
+        elif kind == "scan":
+            groups = lax.axis_size("ctx")
+            laters = [
+                lax.ppermute(packed[1], "ctx", [(i, i - hop) for i in range(hop, groups)]) for hop in range(1, groups)
+            ]
+            scanned[1] = scan(1, segments, after(scanned[1]), states[1], decay, residue)
+        else:
+            grad_input = fix(
+                segments, [scanned[0], scanned[1]], states[0], laters, decay, residue, toks, width
+            )
     return grad_query, grad_input
 
 

time: 77 us -> 70.5 us (0.916); the launches traced: 76.5 us -> 69.2 us
  waiting for transfers between devices: 4.23 us -> 18.4 us
  local copies, waits for them, and re-layouts: 8.99 us -> 0.94 us
  starting transfers between devices: 35.4 us -> 28 us
  Pallas kernels: 26.9 us -> 21 us
    ppermute x14, waiting for transfers between devices: 4.07 us -> 16.4 us  [local(): arrived = lax.ppermute(last, 'ch', [(i, i ^ bit) for i in range(size)])]
    unnamed x22 -> x12, local copies, waits for them, and re-layouts: 8.9 us -> 0.85 us
    all_to_all x2 -> x0, starting transfers between devices: 6.66 us -> none  [local(): states[p] = lax.all_to_all(packed, 'ctx', 0, 0, tiled=True)]
    ppermute x14, starting transfers between devices: 28.8 us -> 24.1 us  [local(): arrived = lax.ppermute(last, 'ch', [(i, i ^ bit) for i in range(size)])]
    ppermute x0 -> x3, starting transfers between devices: none -> 3.88 us  [local(): lax.ppermute(packed[1], 'ctx', [(i, i - hop) for i in range(hop, groups)])]
    pallas_call x15, Pallas kernels: 13.2 us -> 10.2 us  [send(): pl.pallas_call(functools.partial(send_kernel, items, coded, width, len(ne...]
    ppermute x0 -> x3, waiting for transfers between devices: none -> 1.95 us  [local(): lax.ppermute(packed[1], 'ctx', [(i, i - hop) for i in range(hop, groups)])]
    pallas_call x2 -> x1, Pallas kernels: 3.46 us -> 1.73 us  [scan(): pl.pallas_call(functools.partial(scan_kernel, half, segments), in_specs=[...]
  transfers between devices with their start and end apart: 16 -> 17, of which waited for: 7 -> 8; matrix products, arithmetic and copies ran while one was open for 0% -> 0% of each run, Pallas kernels for 30% -> 20%
where the time goes in v8:
time: 70.5 us; the launch traced here: 69.2 us
  starting transfers between devices  28 us (40%)
  Pallas kernels  21 us (30%)
  waiting for transfers between devices  18.4 us (26%)
  local copies, waits for them, and re-layouts  0.94 us (1%)
  between operations  0.93 us (1%)
    ppermute x14, starting transfers between devices, local(): arrived = lax.ppermute(last, 'ch', [(i, i ^ bit) for i in range(size)])  24.1 us
    ppermute x14, waiting for transfers between devices, local(): arrived = lax.ppermute(last, 'ch', [(i, i ^ bit) for i in range(size)])  16.4 us
    pallas_call x15, Pallas kernels, send(): pl.pallas_call(functools.partial(send_kernel, items, coded, width, len(ne...  10.2 us
    ppermute x3, starting transfers between devices, local(): lax.ppermute(packed[1], 'ctx', [(i, i - hop) for i in range(hop, groups)])  3.88 us
    pallas_call x2, Pallas kernels, gate(): pl.pallas_call(functools.partial(gate_kernel, half, rows, segments, piece...  3.66 us
    pallas_call x1, Pallas kernels, fix(): pl.pallas_call(functools.partial(fix_kernel, segments, len(laters)), in_s...  3.02 us
    pallas_call x1, Pallas kernels, first_send(): pl.pallas_call(functools.partial(first_kernel, items, width), in_specs=[p...  2.4 us
    ppermute x3, waiting for transfers between devices, local(): lax.ppermute(packed[1], 'ctx', [(i, i - hop) for i in range(hop, groups)])  1.95 us
  transfers between devices with their start and end apart: 17, of which 8 were waited for; matrix products, arithmetic and copies ran while one was open for 0% of the time, Pallas kernels for 20%

profile of v8, /device:TPU:0, one launch (start us, length us, event | category | flops | bytes accessed | tf_op | source)
XLA Modules:
  0.0 69.2 jit_solution(16262679338550153604)
XLA Ops:
  0.6 0.0 copy-start
  0.6 2.4 %shard_map.77 = (bf16[528,256]{1,0:T(8,128)(2,1)S(1)}, bf16[1024,256]{1,0:T(8,128)(2,1)S(1)}) custom-call(s32[1]{0:T(128)} %bitcast.place_ref, bf16[8192,1024]{1,0:T(8,128)(2,1)} %w_ref.29, bf16[256,1024]{1,0:T(8,128)(2,1)} %g_hbm.1), custom_call_target="tpu_custom_call" | custom-call | bytes 1024 | tf_op jit(solution)/shard_map/pallas_call | solution.py:143
  3.0 3.0 %collective-permute-start = (bf16[528,256]{1,0:T(8,128)(2,1)S(1)}, bf16[528,256]{1,0:T(8,128)(2,1)S(1)}, u32[]{:S(2)}, u32[]{:S(2)}) collective-permute-start(bf16[528,256]{1,0:T(8,128)(2,1)S(1)} %get-tuple-element.28), channel_id=1, source_target_pairs={{0,1},{1,0},{2,3},{3,2},{4,5},{5,4},{6,7},{7,6},{8,9},{9,8},{10,11... | collective-permute-start | bytes 811016 | tf_op jit(solution)/shard_map/ppermute | solution.py:443
  6.1 0.8 %copy-done = bf16[8192,1024]{1,0:T(8,128)(2,1)S(1)} copy-done((bf16[8192,1024]{1,0:T(8,128)(2,1)S(1)}, bf16[8192,1024]{1,0:T(8,128)(2,1)}, u32[]{:S(2)}) %copy-start) | copy-done | bytes 16777240
  6.9 0.6 shard_map.78
  7.5 3.0 %collective-permute-start.1 = (bf16[528,256]{1,0:T(8,128)(2,1)S(1)}, bf16[528,256]{1,0:T(8,128)(2,1)S(1)}, u32[]{:S(2)}, u32[]{:S(2)}) collective-permute-start(bf16[528,256]{1,0:T(8,128)(2,1)S(1)} %shard_map.78), channel_id=1, source_target_pairs={{0,1},{1,0},{2,3},{3,2},{4,5},{5,4},{6,7},{7,6},{8,9},{9,8},{10,11... | collective-permute-start | bytes 811016 | tf_op jit(solution)/shard_map/ppermute | solution.py:443
  10.5 0.6 shard_map.79
  11.2 0.1 collective-permute-start.2
  11.3 0.6 shard_map.80
  11.9 0.6 shard_map.81
  12.5 0.9 %collective-permute-done.refs_0_ = bf16[528,256]{1,0:T(8,128)(2,1)S(1)} collective-permute-done((bf16[528,256]{1,0:T(8,128)(2,1)S(1)}, bf16[528,256]{1,0:T(8,128)(2,1)S(1)}, u32[]{:S(2)}, u32[]{:S(2)}) %collective-permute-start) | collective-permute-done | bytes 270368 | tf_op jit(solution)/shard_map/ppermute | solution.py:443
  13.4 0.7 %shard_map.82 = bf16[528,256]{1,0:T(8,128)(2,1)S(1)} custom-call(s32[1]{0:T(128)} %bitcast.place_ref, bf16[8192,1024]{1,0:T(8,128)(2,1)S(1)} %copy-done, bf16[1024,256]{1,0:T(8,128)(2,1)S(1)} %get-tuple-element.30.turned_ref, bf16[528,256]{1,0:T(8,128)(2,1)S(1)} %collective-permute-done.refs_0_), custom_call_target="tpu_custom_call" | custom-call | bytes 1024 | tf_op jit(solution)/shard_map/pallas_call | solution.py:97
  14.1 2.2 %collective-permute-start.3 = (bf16[528,256]{1,0:T(8,128)(2,1)S(1)}, bf16[528,256]{1,0:T(8,128)(2,1)S(1)}, u32[]{:S(2)}, u32[]{:S(2)}) collective-permute-start(bf16[528,256]{1,0:T(8,128)(2,1)S(1)} %shard_map.82), channel_id=1, source_target_pairs={{0,2},{1,3},{2,0},{3,1},{4,6},{5,7},{6,4},{7,5},{8,10},{9,11},{10,... | collective-permute-start | bytes 811016 | tf_op jit(solution)/shard_map/ppermute | solution.py:443
  16.3 0.6 shard_map.83
  17.0 0.6 shard_map.84
  17.6 1.6 %collective-permute-done.1.refs_0_ = bf16[528,256]{1,0:T(8,128)(2,1)S(1)} collective-permute-done((bf16[528,256]{1,0:T(8,128)(2,1)S(1)}, bf16[528,256]{1,0:T(8,128)(2,1)S(1)}, u32[]{:S(2)}, u32[]{:S(2)}) %collective-permute-start.1) | collective-permute-done | bytes 270368 | tf_op jit(solution)/shard_map/ppermute | solution.py:443
  19.2 0.7 %shard_map.85 = bf16[528,256]{1,0:T(8,128)(2,1)S(1)} custom-call(s32[1]{0:T(128)} %bitcast.place_ref, bf16[8192,1024]{1,0:T(8,128)(2,1)S(1)} %copy-done, bf16[1024,256]{1,0:T(8,128)(2,1)S(1)} %get-tuple-element.30.turned_ref, bf16[528,256]{1,0:T(8,128)(2,1)S(1)} %collective-permute-done.1.refs_0_), custom_call_target="tpu_custom_call" | custom-call | bytes 1024 | tf_op jit(solution)/shard_map/pallas_call | solution.py:97
  19.9 2.2 %collective-permute-start.4 = (bf16[528,256]{1,0:T(8,128)(2,1)S(1)}, bf16[528,256]{1,0:T(8,128)(2,1)S(1)}, u32[]{:S(2)}, u32[]{:S(2)}) collective-permute-start(bf16[528,256]{1,0:T(8,128)(2,1)S(1)} %shard_map.85), channel_id=1, source_target_pairs={{0,2},{1,3},{2,0},{3,1},{4,6},{5,7},{6,4},{7,5},{8,10},{9,11},{10,... | collective-permute-start | bytes 811016 | tf_op jit(solution)/shard_map/ppermute | solution.py:443
  22.1 1.5 %collective-permute-start.5 = (bf16[528,256]{1,0:T(8,128)(2,1)S(1)}, bf16[528,256]{1,0:T(8,128)(2,1)S(1)}, u32[]{:S(2)}, u32[]{:S(2)}) collective-permute-start(bf16[528,256]{1,0:T(8,128)(2,1)S(1)} %shard_map.81), channel_id=1, source_target_pairs={{0,1},{1,0},{2,3},{3,2},{4,5},{5,4},{6,7},{7,6},{8,9},{9,8},{10,11... | collective-permute-start | bytes 811016 | tf_op jit(solution)/shard_map/ppermute | solution.py:443
  23.6 0.5 collective-permute-start.6
  24.1 0.8 %collective-permute-done.2.refs_0_ = bf16[528,256]{1,0:T(8,128)(2,1)S(1)} collective-permute-done((bf16[528,256]{1,0:T(8,128)(2,1)S(1)}, bf16[528,256]{1,0:T(8,128)(2,1)S(1)}, u32[]{:S(2)}, u32[]{:S(2)}) %collective-permute-start.2) | collective-permute-done | bytes 270368 | tf_op jit(solution)/shard_map/ppermute | solution.py:443
  25.0 0.0 collective-permute-done.3.refs_1_
  25.0 0.9 %shard_map.86 = bf16[528,256]{1,0:T(8,128)(2,1)S(1)} custom-call(s32[1]{0:T(128)} %bitcast.place_ref, bf16[8192,1024]{1,0:T(8,128)(2,1)S(1)} %copy-done, bf16[1024,256]{1,0:T(8,128)(2,1)S(1)} %get-tuple-element.30.turned_ref, bf16[528,256]{1,0:T(8,128)(2,1)S(1)} %collective-permute-done.2.refs_0_, bf16[528,256]{1,0:T(8,128)(2,1)S(1)} %collective-permute-done.3.refs_1_), custom_call_target="tpu_custom_call" | custom-call | bytes 1024 | tf_op jit(solution)/shard_map/pallas_call | solution.py:97
  25.9 3.2 %collective-permute-start.7 = (bf16[528,256]{1,0:T(8,128)(2,1)S(1)}, bf16[528,256]{1,0:T(8,128)(2,1)S(1)}, u32[]{:S(2)}, u32[]{:S(2)}) collective-permute-start(bf16[528,256]{1,0:T(8,128)(2,1)S(1)} %shard_map.86), channel_id=1, source_target_pairs={{0,4},{1,5},{2,6},{3,7},{4,0},{5,1},{6,2},{7,3},{8,12},{9,13},{10,... | collective-permute-start | bytes 811016 | tf_op jit(solution)/shard_map/ppermute | solution.py:443
  29.1 1.5 %collective-permute-start.8 = (bf16[528,256]{1,0:T(8,128)(2,1)S(1)}, bf16[528,256]{1,0:T(8,128)(2,1)S(1)}, u32[]{:S(2)}, u32[]{:S(2)}) collective-permute-start(bf16[528,256]{1,0:T(8,128)(2,1)S(1)} %shard_map.84), channel_id=1, source_target_pairs={{0,1},{1,0},{2,3},{3,2},{4,5},{5,4},{6,7},{7,6},{8,9},{9,8},{10,11... | collective-permute-start | bytes 811016 | tf_op jit(solution)/shard_map/ppermute | solution.py:443
  30.6 0.0 collective-permute-done.4.refs_1_
  30.6 0.6 shard_map.87
  31.3 0.6 collective-permute-start.9
  31.8 0.0 collective-permute-done.5.refs_0_
  31.8 0.7 %shard_map.88 = bf16[528,256]{1,0:T(8,128)(2,1)S(1)} custom-call(s32[1]{0:T(128)} %bitcast.place_ref, bf16[8192,1024]{1,0:T(8,128)(2,1)S(1)} %copy-done, bf16[1024,256]{1,0:T(8,128)(2,1)S(1)} %get-tuple-element.30.turned_ref, bf16[528,256]{1,0:T(8,128)(2,1)S(1)} %collective-permute-done.5.refs_0_), custom_call_target="tpu_custom_call" | custom-call | bytes 1024 | tf_op jit(solution)/shard_map/pallas_call | solution.py:97
  32.6 0.0 copy-start.3
  32.6 0.0 copy-start.4
  32.6 4.7 %collective-permute-done.6.refs_0_ = bf16[528,256]{1,0:T(8,128)(2,1)S(1)} collective-permute-done((bf16[528,256]{1,0:T(8,128)(2,1)S(1)}, bf16[528,256]{1,0:T(8,128)(2,1)S(1)}, u32[]{:S(2)}, u32[]{:S(2)}) %collective-permute-start.6) | collective-permute-done | bytes 270368 | tf_op jit(solution)/shard_map/ppermute | solution.py:443
  37.3 0.9 %shard_map.89 = bf16[528,256]{1,0:T(8,128)(2,1)S(1)} custom-call(s32[1]{0:T(128)} %bitcast.place_ref, bf16[8192,1024]{1,0:T(8,128)(2,1)S(1)} %copy-done, bf16[1024,256]{1,0:T(8,128)(2,1)S(1)} %get-tuple-element.30.turned_ref, bf16[528,256]{1,0:T(8,128)(2,1)S(1)} %collective-permute-done.6.refs_0_, bf16[528,256]{1,0:T(8,128)(2,1)S(1)} %collective-permute-done.4.refs_1_), custom_call_target="tpu_custom_call" | custom-call | bytes 1024 | tf_op jit(solution)/shard_map/pallas_call | solution.py:97
  38.3 0.0 copy-start.1
  38.3 0.0 copy-start.2
  38.3 2.6 %collective-permute-start.11 = (bf16[528,256]{1,0:T(8,128)(2,1)S(1)}, bf16[528,256]{1,0:T(8,128)(2,1)S(1)}, u32[]{:S(2)}, u32[]{:S(2)}) collective-permute-start(bf16[528,256]{1,0:T(8,128)(2,1)S(1)} %shard_map.89), channel_id=1, source_target_pairs={{0,4},{1,5},{2,6},{3,7},{4,0},{5,1},{6,2},{7,3},{8,12},{9,13},{10,... | collective-permute-start | bytes 811016 | tf_op jit(solution)/shard_map/ppermute | solution.py:443
  40.9 1.4 %collective-permute-start.10 = (bf16[528,256]{1,0:T(8,128)(2,1)S(1)}, bf16[528,256]{1,0:T(8,128)(2,1)S(1)}, u32[]{:S(2)}, u32[]{:S(2)}) collective-permute-start(bf16[528,256]{1,0:T(8,128)(2,1)S(1)} %shard_map.88), channel_id=1, source_target_pairs={{0,2},{1,3},{2,0},{3,1},{4,6},{5,7},{6,4},{7,5},{8,10},{9,11},{10,... | collective-permute-start | bytes 811016 | tf_op jit(solution)/shard_map/ppermute | solution.py:443
  42.3 0.0 collective-permute-done.7.refs_1_
  42.3 1.5 %collective-permute-start.12 = (bf16[528,256]{1,0:T(8,128)(2,1)S(1)}, bf16[528,256]{1,0:T(8,128)(2,1)S(1)}, u32[]{:S(2)}, u32[]{:S(2)}) collective-permute-start(bf16[528,256]{1,0:T(8,128)(2,1)S(1)} %shard_map.80), channel_id=1, source_target_pairs={{0,1},{1,0},{2,3},{3,2},{4,5},{5,4},{6,7},{7,6},{8,9},{9,8},{10,11... | collective-permute-start | bytes 811016 | tf_op jit(solution)/shard_map/ppermute | solution.py:443
  43.8 0.0 collective-permute-done.8.refs_0_
  43.8 0.7 %shard_map.90 = bf16[528,256]{1,0:T(8,128)(2,1)S(1)} custom-call(s32[1]{0:T(128)} %bitcast.place_ref, bf16[8192,1024]{1,0:T(8,128)(2,1)S(1)} %copy-done, bf16[1024,256]{1,0:T(8,128)(2,1)S(1)} %get-tuple-element.30.turned_ref, bf16[528,256]{1,0:T(8,128)(2,1)S(1)} %collective-permute-done.8.refs_0_), custom_call_target="tpu_custom_call" | custom-call | bytes 1024 | tf_op jit(solution)/shard_map/pallas_call | solution.py:97
  44.6 0.7 %collective-permute-start.13 = (bf16[528,256]{1,0:T(8,128)(2,1)S(1)}, bf16[528,256]{1,0:T(8,128)(2,1)S(1)}, u32[]{:S(2)}, u32[]{:S(2)}) collective-permute-start(bf16[528,256]{1,0:T(8,128)(2,1)S(1)} %shard_map.90), channel_id=1, source_target_pairs={{0,2},{1,3},{2,0},{3,1},{4,6},{5,7},{6,4},{7,5},{8,10},{9,11},{10,... | collective-permute-start | bytes 811016 | tf_op jit(solution)/shard_map/ppermute | solution.py:443
  45.3 0.0 copy-done.3
  45.3 0.0 copy-done.4
  45.4 3.6 %collective-permute-done.9.refs_0_ = bf16[528,256]{1,0:T(8,128)(2,1)S(1)} collective-permute-done((bf16[528,256]{1,0:T(8,128)(2,1)S(1)}, bf16[528,256]{1,0:T(8,128)(2,1)S(1)}, u32[]{:S(2)}, u32[]{:S(2)}) %collective-permute-start.9) | collective-permute-done | bytes 270368 | tf_op jit(solution)/shard_map/ppermute | solution.py:443
  48.9 0.5 shard_map.91.acc_ref
  49.4 1.7 %collective-permute-done.11.refs_1_ = bf16[528,256]{1,0:T(8,128)(2,1)S(1)} collective-permute-done((bf16[528,256]{1,0:T(8,128)(2,1)S(1)}, bf16[528,256]{1,0:T(8,128)(2,1)S(1)}, u32[]{:S(2)}, u32[]{:S(2)}) %collective-permute-start.11) | collective-permute-done | bytes 270368 | tf_op jit(solution)/shard_map/ppermute | solution.py:443
  51.2 3.1 %collective-permute-done.10.refs_0_ = bf16[528,256]{1,0:T(8,128)(2,1)S(1)} collective-permute-done((bf16[528,256]{1,0:T(8,128)(2,1)S(1)}, bf16[528,256]{1,0:T(8,128)(2,1)S(1)}, u32[]{:S(2)}, u32[]{:S(2)}) %collective-permute-start.10) | collective-permute-done | bytes 270368 | tf_op jit(solution)/shard_map/ppermute | solution.py:443
  54.4 0.0 copy-done.1
  54.4 0.0 copy-done.2
  54.4 2.3 %shard_map.92 = (bf16[256,1024]{1,0:T(8,128)(2,1)}, f32[1024,128]{1,0:T(8,128)S(1)}, f32[16,8,128]{2,1,0:T(8,128)S(1)}, f32[8,8,128]{2,1,0:T(8,128)S(1)}) custom-call(f32[512,256]{1,0:T(8,128)S(1)} %shard_map.91.acc_ref, bf16[528,256]{1,0:T(8,128)(2,1)S(1)} %collective-permute-done.10.refs_0_, bf16[528,256]{1,0:T(8,128)(2,1)S(1)} %collective-permute-done.11.refs_1_, ...), custom_call_target="tpu_custom_call" | custom-call | bytes 1024 | tf_op jit(solution)/shard_map/pallas_call | solution.py:254
  56.7 0.0 collective-permute-done.12.refs_0_
  56.7 0.5 shard_map.93.acc_ref
  57.2 0.0 collective-permute-done.13.refs_0_
  57.2 1.4 %shard_map.94 = (bf16[256,1024]{1,0:T(8,128)(2,1)}, f32[1024,128]{1,0:T(8,128)S(1)}, f32[16,8,128]{2,1,0:T(8,128)S(1)}, f32[16,8,128]{2,1,0:T(8,128)S(1)}) custom-call(f32[512,256]{1,0:T(8,128)S(1)} %shard_map.93.acc_ref, bf16[528,256]{1,0:T(8,128)(2,1)S(1)} %collective-permute-done.13.refs_0_, ...), custom_call_target="tpu_custom_call", output_to_operand_aliasing={{0}: (7, {})} | custom-call | bytes 1024 | tf_op jit(solution)/shard_map/pallas_call | solution.py:254
  58.6 1.3 %collective-permute-start.16 = (f32[16,8,128]{2,1,0:T(8,128)S(1)}, f32[16,8,128]{2,1,0:T(8,128)S(1)}, u32[]{:S(2)}, u32[]{:S(2)}) collective-permute-start(f32[16,8,128]{2,1,0:T(8,128)S(1)} %get-tuple-element.50), channel_id=1, source_target_pairs={{24,0},{25,1},{26,2},{27,3},{28,4},{29,5},{30,6},{31,7}} | collective-permute-start | bytes 196616 | tf_op jit(solution)/shard_map/ppermute | solution.py:478
  59.9 1.3 %collective-permute-start.15 = (f32[16,8,128]{2,1,0:T(8,128)S(1)}, f32[16,8,128]{2,1,0:T(8,128)S(1)}, u32[]{:S(2)}, u32[]{:S(2)}) collective-permute-start(f32[16,8,128]{2,1,0:T(8,128)S(1)} %get-tuple-element.50), channel_id=1, source_target_pairs={{16,0},{24,8},{17,1},{25,9},{18,2},{26,10},{19,3},{27,11},{20,4},{... | collective-permute-start | bytes 196616 | tf_op jit(solution)/shard_map/ppermute | solution.py:478
  61.2 1.3 %collective-permute-start.14 = (f32[16,8,128]{2,1,0:T(8,128)S(1)}, f32[16,8,128]{2,1,0:T(8,128)S(1)}, u32[]{:S(2)}, u32[]{:S(2)}) collective-permute-start(f32[16,8,128]{2,1,0:T(8,128)S(1)} %get-tuple-element.50), channel_id=1, source_target_pairs={{8,0},{16,8},{24,16},{9,1},{17,9},{25,17},{10,2},{18,10},{26,18},{... | collective-permute-start | bytes 196616 | tf_op jit(solution)/shard_map/ppermute | solution.py:478
  62.5 1.7 %shard_map.95.refs_1_ = f32[1024,128]{1,0:T(8,128)S(1)} custom-call(f32[1024,128]{1,0:T(8,128)S(1)} %get-tuple-element.51.gc_ref, f32[16,8,128]{2,1,0:T(8,128)S(1)} %get-tuple-element.52.state_ref, f32[16,16,128]{2,1,0:T(8,128)S(1)} %bitcast.11, f32[16,16,128]{2,1,0:T(8,128)S(1)} %bitcast.14), custom_call_target="tpu_custom_call" | custom-call | bytes 1024 | tf_op jit(solution)/shard_map/pallas_call | solution.py:305
  64.2 0.0 collective-permute-done.16.refs_5_
  64.2 1.9 %collective-permute-done.15.refs_4_ = f32[16,8,128]{2,1,0:T(8,128)S(1)} collective-permute-done((f32[16,8,128]{2,1,0:T(8,128)S(1)}, f32[16,8,128]{2,1,0:T(8,128)S(1)}, u32[]{:S(2)}, u32[]{:S(2)}) %collective-permute-start.15) | collective-permute-done | bytes 65568 | tf_op jit(solution)/shard_map/ppermute | solution.py:478
  66.2 0.0 collective-permute-done.14.refs_3_
  66.2 3.0 %shard_map.96 = bf16[256,1024]{1,0:T(8,128)(2,1)} custom-call(f32[1024,128]{1,0:T(8,128)S(1)} %get-tuple-element.48.refs_0_, f32[1024,128]{1,0:T(8,128)S(1)} %shard_map.95.refs_1_, f32[16,8,128]{2,1,0:T(8,128)S(1)} %get-tuple-element.53.refs_2_, f32[16,8,128]{2,1,0:T(8,128)S(1)} %collective-permute-done.14.refs_3_, ...), custom_call_target="tpu_custom_call" | custom-call | bytes 1024 | tf_op jit(solution)/shard_map/pallas_call | solution.py:364
  (4 shorter events, 0.1 us)
Async XLA Ops:
  0.6 6.2 %copy-start = (bf16[8192,1024]{1,0:T(8,128)(2,1)S(1)}, bf16[8192,1024]{1,0:T(8,128)(2,1)}, u32[]{:S(2)}) copy-start(bf16[8192,1024]{1,0:T(8,128)(2,1)} %w_ref.29) | copy-start | bytes 50331652
  3.0 10.3 %collective-permute-start = (bf16[528,256]{1,0:T(8,128)(2,1)S(1)}, bf16[528,256]{1,0:T(8,128)(2,1)S(1)}, u32[]{:S(2)}, u32[]{:S(2)}) collective-permute-start(bf16[528,256]{1,0:T(8,128)(2,1)S(1)} %get-tuple-element.28), channel_id=1, source_target_pairs={{0,1},{1,0},{2,3},{3,2},{4,5},{5,4},{6,7},{7,6},{8,9},{9,8},{10,11... | collective-permute-start | bytes 811016 | tf_op jit(solution)/shard_map/ppermute | solution.py:443
  7.5 11.7 %collective-permute-start.1 = (bf16[528,256]{1,0:T(8,128)(2,1)S(1)}, bf16[528,256]{1,0:T(8,128)(2,1)S(1)}, u32[]{:S(2)}, u32[]{:S(2)}) collective-permute-start(bf16[528,256]{1,0:T(8,128)(2,1)S(1)} %shard_map.78), channel_id=1, source_target_pairs={{0,1},{1,0},{2,3},{3,2},{4,5},{5,4},{6,7},{7,6},{8,9},{9,8},{10,11... | collective-permute-start | bytes 811016 | tf_op jit(solution)/shard_map/ppermute | solution.py:443
  11.2 13.8 %collective-permute-start.2 = (bf16[528,256]{1,0:T(8,128)(2,1)S(1)}, bf16[528,256]{1,0:T(8,128)(2,1)S(1)}, u32[]{:S(2)}, u32[]{:S(2)}) collective-permute-start(bf16[528,256]{1,0:T(8,128)(2,1)S(1)} %shard_map.79), channel_id=1, source_target_pairs={{0,1},{1,0},{2,3},{3,2},{4,5},{5,4},{6,7},{7,6},{8,9},{9,8},{10,11... | collective-permute-start | bytes 811016 | tf_op jit(solution)/shard_map/ppermute | solution.py:443
  14.1 10.8 %collective-permute-start.3 = (bf16[528,256]{1,0:T(8,128)(2,1)S(1)}, bf16[528,256]{1,0:T(8,128)(2,1)S(1)}, u32[]{:S(2)}, u32[]{:S(2)}) collective-permute-start(bf16[528,256]{1,0:T(8,128)(2,1)S(1)} %shard_map.82), channel_id=1, source_target_pairs={{0,2},{1,3},{2,0},{3,1},{4,6},{5,7},{6,4},{7,5},{8,10},{9,11},{10,... | collective-permute-start | bytes 811016 | tf_op jit(solution)/shard_map/ppermute | solution.py:443
  19.9 10.7 %collective-permute-start.4 = (bf16[528,256]{1,0:T(8,128)(2,1)S(1)}, bf16[528,256]{1,0:T(8,128)(2,1)S(1)}, u32[]{:S(2)}, u32[]{:S(2)}) collective-permute-start(bf16[528,256]{1,0:T(8,128)(2,1)S(1)} %shard_map.85), channel_id=1, source_target_pairs={{0,2},{1,3},{2,0},{3,1},{4,6},{5,7},{6,4},{7,5},{8,10},{9,11},{10,... | collective-permute-start | bytes 811016 | tf_op jit(solution)/shard_map/ppermute | solution.py:443
  22.1 9.7 %collective-permute-start.5 = (bf16[528,256]{1,0:T(8,128)(2,1)S(1)}, bf16[528,256]{1,0:T(8,128)(2,1)S(1)}, u32[]{:S(2)}, u32[]{:S(2)}) collective-permute-start(bf16[528,256]{1,0:T(8,128)(2,1)S(1)} %shard_map.81), channel_id=1, source_target_pairs={{0,1},{1,0},{2,3},{3,2},{4,5},{5,4},{6,7},{7,6},{8,9},{9,8},{10,11... | collective-permute-start | bytes 811016 | tf_op jit(solution)/shard_map/ppermute | solution.py:443
  23.6 13.7 %collective-permute-start.6 = (bf16[528,256]{1,0:T(8,128)(2,1)S(1)}, bf16[528,256]{1,0:T(8,128)(2,1)S(1)}, u32[]{:S(2)}, u32[]{:S(2)}) collective-permute-start(bf16[528,256]{1,0:T(8,128)(2,1)S(1)} %shard_map.83), channel_id=1, source_target_pairs={{0,1},{1,0},{2,3},{3,2},{4,5},{5,4},{6,7},{7,6},{8,9},{9,8},{10,11... | collective-permute-start | bytes 811016 | tf_op jit(solution)/shard_map/ppermute | solution.py:443
  25.9 16.4 %collective-permute-start.7 = (bf16[528,256]{1,0:T(8,128)(2,1)S(1)}, bf16[528,256]{1,0:T(8,128)(2,1)S(1)}, u32[]{:S(2)}, u32[]{:S(2)}) collective-permute-start(bf16[528,256]{1,0:T(8,128)(2,1)S(1)} %shard_map.86), channel_id=1, source_target_pairs={{0,4},{1,5},{2,6},{3,7},{4,0},{5,1},{6,2},{7,3},{8,12},{9,13},{10,... | collective-permute-start | bytes 811016 | tf_op jit(solution)/shard_map/ppermute | solution.py:443
  29.1 14.7 %collective-permute-start.8 = (bf16[528,256]{1,0:T(8,128)(2,1)S(1)}, bf16[528,256]{1,0:T(8,128)(2,1)S(1)}, u32[]{:S(2)}, u32[]{:S(2)}) collective-permute-start(bf16[528,256]{1,0:T(8,128)(2,1)S(1)} %shard_map.84), channel_id=1, source_target_pairs={{0,1},{1,0},{2,3},{3,2},{4,5},{5,4},{6,7},{7,6},{8,9},{9,8},{10,11... | collective-permute-start | bytes 811016 | tf_op jit(solution)/shard_map/ppermute | solution.py:443
  31.3 17.7 %collective-permute-start.9 = (bf16[528,256]{1,0:T(8,128)(2,1)S(1)}, bf16[528,256]{1,0:T(8,128)(2,1)S(1)}, u32[]{:S(2)}, u32[]{:S(2)}) collective-permute-start(bf16[528,256]{1,0:T(8,128)(2,1)S(1)} %shard_map.87), channel_id=1, source_target_pairs={{0,1},{1,0},{2,3},{3,2},{4,5},{5,4},{6,7},{7,6},{8,9},{9,8},{10,11... | collective-permute-start | bytes 811016 | tf_op jit(solution)/shard_map/ppermute | solution.py:443
  32.6 12.7 %copy-start.3 = (f32[1024,16]{0,1:T(8,128)S(1)}, f32[1024,16]{0,1:T(8,128)}, u32[]{:S(2)}) copy-start(f32[1024,16]{0,1:T(8,128)} %param.10) | copy-start | bytes 196612
  32.6 12.7 %copy-start.4 = (f32[1024,16]{0,1:T(8,128)S(1)}, f32[1024,16]{0,1:T(8,128)}, u32[]{:S(2)}) copy-start(f32[1024,16]{0,1:T(8,128)} %param.11) | copy-start | bytes 196612
  38.3 16.1 %copy-start.1 = (bf16[256,1024]{1,0:T(8,128)(2,1)S(1)}, bf16[256,1024]{1,0:T(8,128)(2,1)}, u32[]{:S(2)}) copy-start(bf16[256,1024]{1,0:T(8,128)(2,1)} %refs_2_.3) | copy-start | bytes 1572868
  38.3 16.1 %copy-start.2 = (bf16[256,1024]{1,0:T(8,128)(2,1)S(1)}, bf16[256,1024]{1,0:T(8,128)(2,1)}, u32[]{:S(2)}) copy-start(bf16[256,1024]{1,0:T(8,128)(2,1)} %refs_3_.3) | copy-start | bytes 1572868
  38.3 12.9 %collective-permute-start.11 = (bf16[528,256]{1,0:T(8,128)(2,1)S(1)}, bf16[528,256]{1,0:T(8,128)(2,1)S(1)}, u32[]{:S(2)}, u32[]{:S(2)}) collective-permute-start(bf16[528,256]{1,0:T(8,128)(2,1)S(1)} %shard_map.89), channel_id=1, source_target_pairs={{0,4},{1,5},{2,6},{3,7},{4,0},{5,1},{6,2},{7,3},{8,12},{9,13},{10,... | collective-permute-start | bytes 811016 | tf_op jit(solution)/shard_map/ppermute | solution.py:443
  40.9 13.3 %collective-permute-start.10 = (bf16[528,256]{1,0:T(8,128)(2,1)S(1)}, bf16[528,256]{1,0:T(8,128)(2,1)S(1)}, u32[]{:S(2)}, u32[]{:S(2)}) collective-permute-start(bf16[528,256]{1,0:T(8,128)(2,1)S(1)} %shard_map.88), channel_id=1, source_target_pairs={{0,2},{1,3},{2,0},{3,1},{4,6},{5,7},{6,4},{7,5},{8,10},{9,11},{10,... | collective-permute-start | bytes 811016 | tf_op jit(solution)/shard_map/ppermute | solution.py:443
  42.3 14.4 %collective-permute-start.12 = (bf16[528,256]{1,0:T(8,128)(2,1)S(1)}, bf16[528,256]{1,0:T(8,128)(2,1)S(1)}, u32[]{:S(2)}, u32[]{:S(2)}) collective-permute-start(bf16[528,256]{1,0:T(8,128)(2,1)S(1)} %shard_map.80), channel_id=1, source_target_pairs={{0,1},{1,0},{2,3},{3,2},{4,5},{5,4},{6,7},{7,6},{8,9},{9,8},{10,11... | collective-permute-start | bytes 811016 | tf_op jit(solution)/shard_map/ppermute | solution.py:443
  44.6 12.6 %collective-permute-start.13 = (bf16[528,256]{1,0:T(8,128)(2,1)S(1)}, bf16[528,256]{1,0:T(8,128)(2,1)S(1)}, u32[]{:S(2)}, u32[]{:S(2)}) collective-permute-start(bf16[528,256]{1,0:T(8,128)(2,1)S(1)} %shard_map.90), channel_id=1, source_target_pairs={{0,2},{1,3},{2,0},{3,1},{4,6},{5,7},{6,4},{7,5},{8,10},{9,11},{10,... | collective-permute-start | bytes 811016 | tf_op jit(solution)/shard_map/ppermute | solution.py:443
  58.6 5.6 %collective-permute-start.16 = (f32[16,8,128]{2,1,0:T(8,128)S(1)}, f32[16,8,128]{2,1,0:T(8,128)S(1)}, u32[]{:S(2)}, u32[]{:S(2)}) collective-permute-start(f32[16,8,128]{2,1,0:T(8,128)S(1)} %get-tuple-element.50), channel_id=1, source_target_pairs={{24,0},{25,1},{26,2},{27,3},{28,4},{29,5},{30,6},{31,7}} | collective-permute-start | bytes 196616 | tf_op jit(solution)/shard_map/ppermute | solution.py:478
  59.9 6.3 %collective-permute-start.15 = (f32[16,8,128]{2,1,0:T(8,128)S(1)}, f32[16,8,128]{2,1,0:T(8,128)S(1)}, u32[]{:S(2)}, u32[]{:S(2)}) collective-permute-start(f32[16,8,128]{2,1,0:T(8,128)S(1)} %get-tuple-element.50), channel_id=1, source_target_pairs={{16,0},{24,8},{17,1},{25,9},{18,2},{26,10},{19,3},{27,11},{20,4},{... | collective-permute-start | bytes 196616 | tf_op jit(solution)/shard_map/ppermute | solution.py:478
  61.2 5.0 %collective-permute-start.14 = (f32[16,8,128]{2,1,0:T(8,128)S(1)}, f32[16,8,128]{2,1,0:T(8,128)S(1)}, u32[]{:S(2)}, u32[]{:S(2)}) collective-permute-start(f32[16,8,128]{2,1,0:T(8,128)S(1)} %get-tuple-element.50), channel_id=1, source_target_pairs={{8,0},{16,8},{24,16},{9,1},{17,9},{25,17},{10,2},{18,10},{26,18},{... | collective-permute-start | bytes 196616 | tf_op jit(solution)/shard_map/ppermute | solution.py:478

commit v9 on v8

--- a/solution.py
+++ b/solution.py
@@ -17,11 +17,16 @@
 
 PORTIONS = (((0, 1, 2), 2, 0), ((0, 1, 2), 2, 1))
 ORDER = (
-    ((1, 0, 6),), ((0, 0, 6),), ((1, 0, 4),), ((1, 0, 0),), ((0, 0, 2),), ((1, 1, 4),), ((0, 0, 4),), ((1, 0, 2),),
-    ((0, 1, 4),), ((1, 2, 0),), ((0, 0, 0),), ((0, 1, 0),), ((0, 2, 0),), ((1, 1, 0),), ("sum", 0), ("gate", 0),
-    ("sum", 1), ("gate", 1), ("scan", 1), ("fix", 1),
+    ((0, 0, 6),), ((1, 0, 0),), ((0, 0, 4),), ((1, 0, 6),), ((1, 0, 2),), ((1, 0, 4),), ((0, 0, 2),), ((0, 1, 4),),
+    ((1, 1, 4),), ((0, 2, 0),), ((0, 0, 0),), ((0, 1, 0),), ((1, 2, 0),), ((1, 1, 0),), ("laps", None), ("sum", 0),
+    ("sum", 1), ("gate", 0), ("gate", 1), ("scan", 1), ("fix", None),
 )
-WAITS = {((1, 1, 0),): ((1, 2, 0),), ((0, 0, 0),): ((0, 1, 4),)}
+WAITS = {
+    ((1, 1, 0),): ((0, 2, 0),),
+    ("sum", 0): ((0, 1, 0), (0, 0, 0)),
+    ((1, 2, 0),): ((1, 1, 4),),
+    ("gate", 1): ((1, 2, 0),),
+}
 
 
 def part_of(rows, blocks):
@@ -188,7 +193,7 @@
 
 def gate_kernel(half, rows, segments, pieces, near, acc_ref, *refs):
     near_refs, refs = refs[:near], refs[near:]
-    query_ref, conv_ref, decay_ref, other_ref = refs[:4]
+    query_ref, conv_ref, decay_ref, lap_ref, other_ref = refs[:5]
     out_hbm, rows_ref, state_ref, pack_ref = refs[-7:-3] if half == 0 else refs[-6:-2]
     gq_ref, sem = refs[-2:]
     gc_ref = refs[-3] if half == 0 else rows_ref
@@ -226,7 +231,7 @@
         state_ref[n] = state[n]
         total = state[n]
         if segments > 1:
-            factor = jnp.where(segment < segments - 1, power(decay[n], span), 0.0)
+            factor = jnp.where(segment < segments - 1, lap_ref[n, mine], 0.0)
             for _ in range(segments - 1):
                 total = state[n] + factor * rolled(total, -1)
         whole.append(total)
@@ -243,7 +248,7 @@
     store.wait()
 
 
-def gate(half, rows, segments, pieces, acc, nears, query_in, conv_out, decay, other, partial):
+def gate(half, rows, segments, pieces, acc, nears, query_in, conv_out, decay, lap, other, partial):
     toks, width = query_in.shape
     modes, _, lanes = decay.shape
     sublanes = rows // lanes * segments
@@ -253,7 +258,7 @@
     lines = (rows // lanes * toks, lanes)
     return pl.pallas_call(
         functools.partial(gate_kernel, half, rows, segments, pieces, len(nears)),
-        in_specs=[vmem] * (5 + len(nears)) + [high] * len(more),
+        in_specs=[vmem] * (6 + len(nears)) + [high] * len(more),
         out_specs=(high, vmem, vmem, vmem),
         out_shape=(
             jax.ShapeDtypeStruct((toks, width), jnp.bfloat16),
@@ -263,10 +268,10 @@
         ),
         scratch_shapes=([pltpu.VMEM(lines, jnp.float32)] if half == 0 else [])
         + [pltpu.VMEM((toks, rows), jnp.bfloat16), pltpu.SemaphoreType.DMA],
-        input_output_aliases={5 + len(nears): 0} if more else {},
-        compiler_params=pltpu.CompilerParams(vmem_limit_bytes=VMEM),
-        cost_estimate=QUICK,
-    )(acc, *nears, query_in, conv_out, decay, other, *more)
+        input_output_aliases={6 + len(nears): 0} if more else {},
+        compiler_params=pltpu.CompilerParams(vmem_limit_bytes=VMEM),
+        cost_estimate=QUICK,
+    )(acc, *nears, query_in, conv_out, decay, lap, other, *more)
 
 
 def summed(terms):
@@ -275,7 +280,7 @@
     return terms[0]
 
 
-def scan_kernel(half, segments, gc_ref, state_ref, decay_ref, residue_ref, rows_ref):
+def scan_kernel(half, segments, gc_ref, state_ref, decay_ref, lap_ref, residue_ref, rows_ref):
     modes, sublanes, lanes = state_ref.shape
     mine = slice(half * sublanes, (half + 1) * sublanes)
     span = gc_ref.shape[0] // sublanes
@@ -285,9 +290,8 @@
     for n in range(modes):
         total = jnp.zeros((sublanes, lanes), jnp.float32)
         if segments > 1:
-            group = power(decay[n], span)
             for k in range(segments - 2, -1, -1):
-                total = jnp.where(segment == k, rolled(state_ref[n] + group * total, -1), total)
+                total = jnp.where(segment == k, rolled(state_ref[n] + lap_ref[n, mine] * total, -1), total)
         start.append(total)
 
     def step(t, state):
@@ -300,46 +304,103 @@
     steps_back(span, step, tuple(start), 8)
 
 
-def scan(half, segments, grad_conv, state, decay, residues):
+def scan(half, segments, grad_conv, state, decay, lap, residues):
     vmem = pl.BlockSpec(memory_space=pltpu.VMEM)
     return pl.pallas_call(
         functools.partial(scan_kernel, half, segments),
-        in_specs=[vmem] * 4,
+        in_specs=[vmem] * 5,
         out_specs=vmem,
         out_shape=jax.ShapeDtypeStruct(grad_conv.shape, jnp.float32),
         compiler_params=pltpu.CompilerParams(vmem_limit_bytes=VMEM),
         cost_estimate=QUICK,
-    )(grad_conv, state, decay, residues)
-
-
-def fix_kernel(segments, hops, *refs):
-    scanned_refs, state_ref, later_refs = refs[:2], refs[2], refs[3 : 3 + hops]
-    decay_ref, residue_ref, out_hbm, rows_ref, out_ref, sems = refs[3 + hops :]
+    )(grad_conv, state, decay, lap, residues)
+
+
+def laps_kernel(segments, span, decay_ref, lap_ref, wide_ref):
+    modes, sublanes, lanes = decay_ref.shape
+    sublanes //= 2
+    packs = modes // segments
+    segment = segment_of((sublanes, lanes), segments)
+    for half in range(2):
+        mine = slice(half * sublanes, (half + 1) * sublanes)
+        for m in range(packs):
+            packed = None
+            for j in range(segments):
+                lap = power(decay_ref[m * segments + j, mine], span)
+                lap_ref[m * segments + j, mine] = lap
+                wide = power(lap, segments)
+                packed = wide if packed is None else jnp.where(segment == j, wide, packed)
+            wide_ref[half * packs + m] = packed
+
+
+def laps(segments, toks, decay):
+    modes, sublanes, lanes = decay.shape
+    vmem = pl.BlockSpec(memory_space=pltpu.VMEM)
+    return pl.pallas_call(
+        functools.partial(laps_kernel, segments, toks // segments),
+        in_specs=[vmem],
+        out_specs=(vmem, vmem),
+        out_shape=(
+            jax.ShapeDtypeStruct(decay.shape, jnp.float32),
+            jax.ShapeDtypeStruct((2 * modes // segments, sublanes // 2, lanes), jnp.float32),
+        ),
+        compiler_params=pltpu.CompilerParams(vmem_limit_bytes=VMEM),
+        cost_estimate=QUICK,
+    )(decay)
+
+
+def join_kernel(round_, group_ref, state_ref, arrived_ref, wide_ref, out_ref):
+    earlier = (group_ref[0] >> round_) % 2 == 0
+    for m in range(out_ref.shape[0]):
+        wide = power(wide_ref[m], 1 << round_)
+        mine, other = state_ref[m], arrived_ref[m]
+        out_ref[m] = jnp.where(earlier, mine + wide * other, other + wide * mine)
+
+
+def join(round_, group, state, arrived, wide):
+    vmem = pl.BlockSpec(memory_space=pltpu.VMEM)
+    return pl.pallas_call(
+        functools.partial(join_kernel, round_),
+        in_specs=[pl.BlockSpec(memory_space=pltpu.SMEM)] + [vmem] * 3,
+        out_specs=vmem,
+        out_shape=jax.ShapeDtypeStruct(state.shape, jnp.float32),
+        compiler_params=pltpu.CompilerParams(vmem_limit_bytes=VMEM),
+        cost_estimate=QUICK,
+    )(group, state, arrived, wide)
+
+
+def fix_kernel(segments, rounds, group_ref, *refs):
+    scanned_refs, state_ref, arrived_refs = refs[:2], refs[2], refs[3 : 3 + rounds]
+    decay_ref, lap_ref, wide_ref, residue_ref, out_hbm, rows_ref, out_ref, sems = refs[3 + rounds :]
     toks, width = out_ref.shape
     modes, sublanes, lanes = state_ref.shape
     packs = modes // segments
     rows = width // 2
     span = toks // segments
     segment = segment_of((sublanes, lanes), segments)
+    earlier = [(group_ref[0] >> r) % 2 == 0 for r in range(rounds)]
     stores = []
     for half in range(2):
         mine = slice(half * sublanes, (half + 1) * sublanes)
         decay = [decay_ref[n, mine] for n in range(modes)]
         start = []
-        for n in range(modes):
-            lap = power(decay[n], span)
-            whole = power(lap, segments)
-            m, j = divmod(n, segments)
-            arrived = [rolled(ref[half * packs + m], segments - 1 - j) for ref in later_refs]
-            total = arrived[-1]
-            for state in reversed(arrived[:-1]):
-                total = total * whole + state
-            for k in range(segments - 2, -1, -1):
-                brought = lap * total
-                if half == 0:
-                    brought = brought + state_ref[n]
-                total = jnp.where(segment == k, rolled(brought, -1), total)
-            start.append(residue_ref[n, mine] * total)
+        for m in range(packs):
+            brought = jnp.zeros((sublanes, lanes), jnp.float32)
+            between = jnp.ones((sublanes, lanes), jnp.float32)
+            for r in range(rounds):
+                state = arrived_refs[r][half * packs + m]
+                brought = jnp.where(earlier[r], brought + between * state, brought)
+                if r + 1 < rounds:
+                    between = jnp.where(earlier[r], between * power(wide_ref[half * packs + m], 1 << r), between)
+            for j in range(segments):
+                n = m * segments + j
+                total = rolled(brought, segments - 1 - j)
+                for k in range(segments - 2, -1, -1):
+                    before = lap_ref[n, mine] * total
+                    if half == 0:
+                        before = before + state_ref[n]
+                    total = jnp.where(segment == k, rolled(before, -1), total)
+                start.append(residue_ref[n, mine] * total)
 
         def step(t, state, scanned_ref=scanned_refs[half], decay=decay):
             at = pl.ds(t, sublanes, stride=span)
@@ -359,11 +420,11 @@
         store.wait()
 
 
-def fix(segments, scanned, state, laters, decay, residues, toks, width):
-    vmem = pl.BlockSpec(memory_space=pltpu.VMEM)
-    return pl.pallas_call(
-        functools.partial(fix_kernel, segments, len(laters)),
-        in_specs=[vmem] * (5 + len(laters)),
+def fix(segments, group, scanned, state, arrived, decay, lap, wide, residues, toks, width):
+    vmem = pl.BlockSpec(memory_space=pltpu.VMEM)
+    return pl.pallas_call(
+        functools.partial(fix_kernel, segments, len(arrived)),
+        in_specs=[pl.BlockSpec(memory_space=pltpu.SMEM)] + [vmem] * (7 + len(arrived)),
         out_specs=pl.BlockSpec(memory_space=pltpu.HBM),
         out_shape=jax.ShapeDtypeStruct((toks, width), jnp.bfloat16),
         scratch_shapes=[
@@ -373,7 +434,7 @@
         ],
         compiler_params=pltpu.CompilerParams(vmem_limit_bytes=VMEM),
         cost_estimate=QUICK,
-    )(*scanned, state, *laters, decay, residues)
+    )(group, *scanned, state, *arrived, decay, lap, wide, residues)
 
 
 def local(out_grad, out_weight, query_in, conv_out, residues, decay_rates):
@@ -383,6 +444,7 @@
     size, groups = lax.axis_size("ch"), lax.axis_size("ctx")
     bits = [1 << i for i in range(size.bit_length() - 1)]
     place = jnp.reshape(lax.axis_index("ch"), (1,)).astype(jnp.int32)
+    group = jnp.reshape(lax.axis_index("ctx"), (1,)).astype(jnp.int32)
     half_rows = width // 2
     lines = half_rows // lanes
     segments = 8 // lines
@@ -398,7 +460,7 @@
             for p in range(2)
             for s, bit in enumerate(bits)
             for block in sorted(range(0, size, 2 * bit), reverse=True)
-        ] + [("sum", 0), ("gate", 0), ("sum", 1), ("gate", 1), ("scan", 1), ("fix", 1)]
+        ] + [("laps", None), ("sum", 0), ("sum", 1), ("gate", 0), ("gate", 1), ("scan", 1), ("fix", None)]
     offsets = [sum(width // part for _, part, _ in portions[:p]) for p in range(len(portions))]
 
     received, sums, scanned, states, packed = {}, {}, {}, {}, {}
@@ -446,15 +508,17 @@
                 part = part_of(rows[i], count)
                 received[key] = (arrived, start, peak, part)
                 start, peak = start + rows[i], peak + rows[i] // part
+        elif kind == "laps":
+            lap, wide = laps(segments, toks, after(decay))
+            last = wide
         elif kind == "sum":
-            arrays, places = collect([(q, 0, 0) for q in inside])
-            items = tuple((0, offsets[q], width // portions[q][1], (at,)) for q, at in zip(inside, places))
-            last = sums[half] = send(items, False, width, after(place), out_weight, turned, arrays)
+            items = tuple((0, offsets[q], width // portions[q][1], ()) for q in inside)
+            last = sums[half] = send(items, False, width, after(place), out_weight, turned, [])
         elif kind == "gate":
-            later = range(1, len(bits))
-            arrays, places = collect([(q, i, 0) for q in inside for i in later])
+            stages = range(len(bits))
+            arrays, places = collect([(q, i, 0) for q in inside for i in stages])
             pieces = tuple(
-                (offsets[q] - half * half_rows, tuple(places[i * len(later) : (i + 1) * len(later)]))
+                (offsets[q] - half * half_rows, tuple(places[i * len(stages) : (i + 1) * len(stages)]))
                 for i, q in enumerate(inside)
             )
             other = residue if half == 0 else packed[0]
@@ -468,19 +532,23 @@
                 query_in,
                 conv_out,
                 decay,
+                lap,
                 other,
                 grad_query,
             )
             last = packed[half]
         elif kind == "scan":
             groups = lax.axis_size("ctx")
-            laters = [
-                lax.ppermute(packed[1], "ctx", [(i, i - hop) for i in range(hop, groups)]) for hop in range(1, groups)
-            ]
-            scanned[1] = scan(1, segments, after(scanned[1]), states[1], decay, residue)
+            swap = lambda array, round_: lax.ppermute(array, "ctx", [(i, i ^ (1 << round_)) for i in range(groups)])
+            arrived = [swap(packed[1], 0)]
+            last = scanned[1] = scan(1, segments, after(scanned[1]), states[1], decay, lap, residue)
+            joined = packed[1]
+            for round_ in range(1, groups.bit_length() - 1):
+                joined = last = join(round_ - 1, after(group), joined, arrived[-1], wide)
+                arrived.append(swap(joined, round_))
         else:
             grad_input = fix(
-                segments, [scanned[0], scanned[1]], states[0], laters, decay, residue, toks, width
+                segments, group, [scanned[0], scanned[1]], states[0], arrived, decay, lap, wide, residue, toks, width
             )
     return grad_query, grad_input
 

time: 70.5 us -> 65.3 us (0.926); the launches traced: 69.2 us -> 64.8 us
  waiting for transfers between devices: 18.4 us -> 12.4 us
  starting transfers between devices: 28 us -> 29.1 us
    ppermute x14, waiting for transfers between devices: 16.4 us -> 8.85 us  [local(): arrived = lax.ppermute(last, 'ch', [(i, i ^ bit) for i in range(size)])]
    ppermute x14, starting transfers between devices: 24.1 us -> 28 us  [local(): arrived = lax.ppermute(last, 'ch', [(i, i ^ bit) for i in range(size)])]
    ppermute x3 -> x2, starting transfers between devices: 3.88 us -> 1.07 us  [local(): lax.ppermute(array, 'ctx', [(i, i ^ 1 << round_) for i in range(groups)])]
    ppermute x3 -> x2, waiting for transfers between devices: 1.95 us -> 3.55 us  [local(): lax.ppermute(array, 'ctx', [(i, i ^ 1 << round_) for i in range(groups)])]
    pallas_call x1 -> x3, Pallas kernels: 3.02 us -> 3.03 us  [the longest x1 2.97 us: fix(): pl.pallas_call(functools.partial(fix_kernel, segments, len(arrived)), in_...]
  transfers between devices with their start and end apart: 17 -> 16, of which waited for: 8 -> 10; matrix products, arithmetic and copies ran while one was open for 0% -> 0% of each run, Pallas kernels for 20% -> 22%
where the time goes in v9:
time: 65.3 us; the launch traced here: 64.8 us
  starting transfers between devices  29.1 us (45%)
  Pallas kernels  21.2 us (32%)
  waiting for transfers between devices  12.4 us (19%)
  local copies, waits for them, and re-layouts  1.19 us (2%)
  between operations  0.92 us (1%)
    ppermute x14, starting transfers between devices, local(): arrived = lax.ppermute(last, 'ch', [(i, i ^ bit) for i in range(size)])  28 us
    pallas_call x15, Pallas kernels, send(): pl.pallas_call(functools.partial(send_kernel, items, coded, width, len(ne...  10.1 us
    ppermute x14, waiting for transfers between devices, local(): arrived = lax.ppermute(last, 'ch', [(i, i ^ bit) for i in range(size)])  8.85 us
    pallas_call x2, Pallas kernels, gate(): pl.pallas_call(functools.partial(gate_kernel, half, rows, segments, piece...  3.98 us
    ppermute x2, waiting for transfers between devices, local(): lax.ppermute(array, 'ctx', [(i, i ^ 1 << round_) for i in range(groups)])  3.55 us
    pallas_call x1, Pallas kernels, fix(): pl.pallas_call(functools.partial(fix_kernel, segments, len(arrived)), in_...  2.97 us
    pallas_call x1, Pallas kernels, first_send(): pl.pallas_call(functools.partial(first_kernel, items, width), in_specs=[p...  2.4 us
    pallas_call x1, Pallas kernels, scan(): pl.pallas_call(functools.partial(scan_kernel, half, segments), in_specs=[...  1.72 us
  transfers between devices with their start and end apart: 16, of which 10 were waited for; matrix products, arithmetic and copies ran while one was open for 0% of the time, Pallas kernels for 22%

profile of v9, /device:TPU:0, one launch (start us, length us, event | category | flops | bytes accessed | tf_op | source)
XLA Modules:
  0.0 64.8 jit_solution(5859017394516849980)
XLA Ops:
  0.6 0.0 copy-start
  0.6 2.4 %shard_map.77 = (bf16[528,256]{1,0:T(8,128)(2,1)S(1)}, bf16[1024,256]{1,0:T(8,128)(2,1)S(1)}) custom-call(s32[1]{0:T(128)} %bitcast.place_ref, bf16[8192,1024]{1,0:T(8,128)(2,1)} %w_ref.29, bf16[256,1024]{1,0:T(8,128)(2,1)} %g_hbm.1), custom_call_target="tpu_custom_call" | custom-call | bytes 1024 | tf_op jit(solution)/shard_map/pallas_call | solution.py:148
  3.1 3.0 %collective-permute-start = (bf16[528,256]{1,0:T(8,128)(2,1)S(1)}, bf16[528,256]{1,0:T(8,128)(2,1)S(1)}, u32[]{:S(2)}, u32[]{:S(2)}) collective-permute-start(bf16[528,256]{1,0:T(8,128)(2,1)S(1)} %get-tuple-element.34), channel_id=1, source_target_pairs={{0,1},{1,0},{2,3},{3,2},{4,5},{5,4},{6,7},{7,6},{8,9},{9,8},{10,11... | collective-permute-start | bytes 811016 | tf_op jit(solution)/shard_map/ppermute | solution.py:505
  6.1 0.8 %copy-done = bf16[8192,1024]{1,0:T(8,128)(2,1)S(1)} copy-done((bf16[8192,1024]{1,0:T(8,128)(2,1)S(1)}, bf16[8192,1024]{1,0:T(8,128)(2,1)}, u32[]{:S(2)}) %copy-start) | copy-done | bytes 16777240
  6.9 0.6 shard_map.78
  7.5 0.6 shard_map.79
  8.1 0.6 shard_map.80
  8.8 3.0 %collective-permute-start.1 = (bf16[528,256]{1,0:T(8,128)(2,1)S(1)}, bf16[528,256]{1,0:T(8,128)(2,1)S(1)}, u32[]{:S(2)}, u32[]{:S(2)}) collective-permute-start(bf16[528,256]{1,0:T(8,128)(2,1)S(1)} %shard_map.80), channel_id=1, source_target_pairs={{0,1},{1,0},{2,3},{3,2},{4,5},{5,4},{6,7},{7,6},{8,9},{9,8},{10,11... | collective-permute-start | bytes 811016 | tf_op jit(solution)/shard_map/ppermute | solution.py:505
  11.8 0.1 collective-permute-start.2
  11.9 0.6 shard_map.81
  12.5 0.6 shard_map.82
  13.2 0.6 shard_map.83
  13.8 0.0 collective-permute-done.refs_0_
  13.8 0.7 %shard_map.84 = bf16[528,256]{1,0:T(8,128)(2,1)S(1)} custom-call(s32[1]{0:T(128)} %bitcast.place_ref, bf16[8192,1024]{1,0:T(8,128)(2,1)S(1)} %copy-done, bf16[1024,256]{1,0:T(8,128)(2,1)S(1)} %get-tuple-element.36.turned_ref, bf16[528,256]{1,0:T(8,128)(2,1)S(1)} %collective-permute-done.refs_0_), custom_call_target="tpu_custom_call" | custom-call | bytes 1024 | tf_op jit(solution)/shard_map/pallas_call | solution.py:102
  14.6 2.1 %collective-permute-start.3 = (bf16[528,256]{1,0:T(8,128)(2,1)S(1)}, bf16[528,256]{1,0:T(8,128)(2,1)S(1)}, u32[]{:S(2)}, u32[]{:S(2)}) collective-permute-start(bf16[528,256]{1,0:T(8,128)(2,1)S(1)} %shard_map.84), channel_id=1, source_target_pairs={{0,2},{1,3},{2,0},{3,1},{4,6},{5,7},{6,4},{7,5},{8,10},{9,11},{10,... | collective-permute-start | bytes 811016 | tf_op jit(solution)/shard_map/ppermute | solution.py:505
  16.6 1.5 %collective-permute-start.4 = (bf16[528,256]{1,0:T(8,128)(2,1)S(1)}, bf16[528,256]{1,0:T(8,128)(2,1)S(1)}, u32[]{:S(2)}, u32[]{:S(2)}) collective-permute-start(bf16[528,256]{1,0:T(8,128)(2,1)S(1)} %shard_map.83), channel_id=1, source_target_pairs={{0,1},{1,0},{2,3},{3,2},{4,5},{5,4},{6,7},{7,6},{8,9},{9,8},{10,11... | collective-permute-start | bytes 811016 | tf_op jit(solution)/shard_map/ppermute | solution.py:505
  18.1 1.0 %collective-permute-done.1.refs_0_ = bf16[528,256]{1,0:T(8,128)(2,1)S(1)} collective-permute-done((bf16[528,256]{1,0:T(8,128)(2,1)S(1)}, bf16[528,256]{1,0:T(8,128)(2,1)S(1)}, u32[]{:S(2)}, u32[]{:S(2)}) %collective-permute-start.1) | collective-permute-done | bytes 270368 | tf_op jit(solution)/shard_map/ppermute | solution.py:505
  19.1 0.7 %shard_map.85 = bf16[528,256]{1,0:T(8,128)(2,1)S(1)} custom-call(s32[1]{0:T(128)} %bitcast.place_ref, bf16[8192,1024]{1,0:T(8,128)(2,1)S(1)} %copy-done, bf16[1024,256]{1,0:T(8,128)(2,1)S(1)} %get-tuple-element.36.turned_ref, bf16[528,256]{1,0:T(8,128)(2,1)S(1)} %collective-permute-done.1.refs_0_), custom_call_target="tpu_custom_call" | custom-call | bytes 1024 | tf_op jit(solution)/shard_map/pallas_call | solution.py:102
  19.9 2.2 %collective-permute-start.5 = (bf16[528,256]{1,0:T(8,128)(2,1)S(1)}, bf16[528,256]{1,0:T(8,128)(2,1)S(1)}, u32[]{:S(2)}, u32[]{:S(2)}) collective-permute-start(bf16[528,256]{1,0:T(8,128)(2,1)S(1)} %shard_map.85), channel_id=1, source_target_pairs={{0,2},{1,3},{2,0},{3,1},{4,6},{5,7},{6,4},{7,5},{8,10},{9,11},{10,... | collective-permute-start | bytes 811016 | tf_op jit(solution)/shard_map/ppermute | solution.py:505
  22.1 1.5 %collective-permute-start.6 = (bf16[528,256]{1,0:T(8,128)(2,1)S(1)}, bf16[528,256]{1,0:T(8,128)(2,1)S(1)}, u32[]{:S(2)}, u32[]{:S(2)}) collective-permute-start(bf16[528,256]{1,0:T(8,128)(2,1)S(1)} %shard_map.82), channel_id=1, source_target_pairs={{0,1},{1,0},{2,3},{3,2},{4,5},{5,4},{6,7},{7,6},{8,9},{9,8},{10,11... | collective-permute-start | bytes 811016 | tf_op jit(solution)/shard_map/ppermute | solution.py:505
  23.6 1.3 %collective-permute-done.2.refs_0_ = bf16[528,256]{1,0:T(8,128)(2,1)S(1)} collective-permute-done((bf16[528,256]{1,0:T(8,128)(2,1)S(1)}, bf16[528,256]{1,0:T(8,128)(2,1)S(1)}, u32[]{:S(2)}, u32[]{:S(2)}) %collective-permute-start.2) | collective-permute-done | bytes 270368 | tf_op jit(solution)/shard_map/ppermute | solution.py:505
  24.9 0.0 collective-permute-done.3.refs_1_
  24.9 0.9 %shard_map.86 = bf16[528,256]{1,0:T(8,128)(2,1)S(1)} custom-call(s32[1]{0:T(128)} %bitcast.place_ref, bf16[8192,1024]{1,0:T(8,128)(2,1)S(1)} %copy-done, bf16[1024,256]{1,0:T(8,128)(2,1)S(1)} %get-tuple-element.36.turned_ref, bf16[528,256]{1,0:T(8,128)(2,1)S(1)} %collective-permute-done.2.refs_0_, bf16[528,256]{1,0:T(8,128)(2,1)S(1)} %collective-permute-done.3.refs_1_), custom_call_target="tpu_custom_call" | custom-call | bytes 1024 | tf_op jit(solution)/shard_map/pallas_call | solution.py:102
  25.8 3.2 %collective-permute-start.7 = (bf16[528,256]{1,0:T(8,128)(2,1)S(1)}, bf16[528,256]{1,0:T(8,128)(2,1)S(1)}, u32[]{:S(2)}, u32[]{:S(2)}) collective-permute-start(bf16[528,256]{1,0:T(8,128)(2,1)S(1)} %shard_map.86), channel_id=1, source_target_pairs={{0,4},{1,5},{2,6},{3,7},{4,0},{5,1},{6,2},{7,3},{8,12},{9,13},{10,... | collective-permute-start | bytes 811016 | tf_op jit(solution)/shard_map/ppermute | solution.py:505
  29.0 1.5 %collective-permute-start.8 = (bf16[528,256]{1,0:T(8,128)(2,1)S(1)}, bf16[528,256]{1,0:T(8,128)(2,1)S(1)}, u32[]{:S(2)}, u32[]{:S(2)}) collective-permute-start(bf16[528,256]{1,0:T(8,128)(2,1)S(1)} %shard_map.81), channel_id=1, source_target_pairs={{0,1},{1,0},{2,3},{3,2},{4,5},{5,4},{6,7},{7,6},{8,9},{9,8},{10,11... | collective-permute-start | bytes 811016 | tf_op jit(solution)/shard_map/ppermute | solution.py:505
  30.6 0.6 shard_map.87
  31.2 0.0 collective-permute-done.4.refs_0_
  31.2 0.7 %shard_map.88 = bf16[528,256]{1,0:T(8,128)(2,1)S(1)} custom-call(s32[1]{0:T(128)} %bitcast.place_ref, bf16[8192,1024]{1,0:T(8,128)(2,1)S(1)} %copy-done, bf16[1024,256]{1,0:T(8,128)(2,1)S(1)} %get-tuple-element.36.turned_ref, bf16[528,256]{1,0:T(8,128)(2,1)S(1)} %collective-permute-done.4.refs_0_), custom_call_target="tpu_custom_call" | custom-call | bytes 1024 | tf_op jit(solution)/shard_map/pallas_call | solution.py:102
  32.0 0.0 copy-start.3
  32.0 0.0 copy-start.4
  32.0 1.7 %collective-permute-start.9 = (bf16[528,256]{1,0:T(8,128)(2,1)S(1)}, bf16[528,256]{1,0:T(8,128)(2,1)S(1)}, u32[]{:S(2)}, u32[]{:S(2)}) collective-permute-start(bf16[528,256]{1,0:T(8,128)(2,1)S(1)} %shard_map.88), channel_id=1, source_target_pairs={{0,2},{1,3},{2,0},{3,1},{4,6},{5,7},{6,4},{7,5},{8,10},{9,11},{10,... | collective-permute-start | bytes 811016 | tf_op jit(solution)/shard_map/ppermute | solution.py:505
  33.7 0.0 collective-permute-done.5.refs_1_
  33.7 1.5 %collective-permute-start.10 = (bf16[528,256]{1,0:T(8,128)(2,1)S(1)}, bf16[528,256]{1,0:T(8,128)(2,1)S(1)}, u32[]{:S(2)}, u32[]{:S(2)}) collective-permute-start(bf16[528,256]{1,0:T(8,128)(2,1)S(1)} %shard_map.87), channel_id=1, source_target_pairs={{0,1},{1,0},{2,3},{3,2},{4,5},{5,4},{6,7},{7,6},{8,9},{9,8},{10,11... | collective-permute-start | bytes 811016 | tf_op jit(solution)/shard_map/ppermute | solution.py:505
  35.2 1.3 %collective-permute-done.6.refs_0_ = bf16[528,256]{1,0:T(8,128)(2,1)S(1)} collective-permute-done((bf16[528,256]{1,0:T(8,128)(2,1)S(1)}, bf16[528,256]{1,0:T(8,128)(2,1)S(1)}, u32[]{:S(2)}, u32[]{:S(2)}) %collective-permute-start.6) | collective-permute-done | bytes 270368 | tf_op jit(solution)/shard_map/ppermute | solution.py:505
  36.5 2.1 %collective-permute-start.12 = (bf16[528,256]{1,0:T(8,128)(2,1)S(1)}, bf16[528,256]{1,0:T(8,128)(2,1)S(1)}, u32[]{:S(2)}, u32[]{:S(2)}) collective-permute-start(bf16[528,256]{1,0:T(8,128)(2,1)S(1)} %shard_map.78), channel_id=1, source_target_pairs={{0,1},{1,0},{2,3},{3,2},{4,5},{5,4},{6,7},{7,6},{8,9},{9,8},{10,11... | collective-permute-start | bytes 811016 | tf_op jit(solution)/shard_map/ppermute | solution.py:505
  38.6 0.9 %shard_map.89 = bf16[528,256]{1,0:T(8,128)(2,1)S(1)} custom-call(s32[1]{0:T(128)} %bitcast.place_ref, bf16[8192,1024]{1,0:T(8,128)(2,1)S(1)} %copy-done, bf16[1024,256]{1,0:T(8,128)(2,1)S(1)} %get-tuple-element.36.turned_ref, bf16[528,256]{1,0:T(8,128)(2,1)S(1)} %collective-permute-done.6.refs_0_, bf16[528,256]{1,0:T(8,128)(2,1)S(1)} %collective-permute-done.5.refs_1_), custom_call_target="tpu_custom_call" | custom-call | bytes 1024 | tf_op jit(solution)/shard_map/pallas_call | solution.py:102
  39.5 0.2 collective-permute-done.7.refs_2_
  39.7 2.4 %collective-permute-start.11 = (bf16[528,256]{1,0:T(8,128)(2,1)S(1)}, bf16[528,256]{1,0:T(8,128)(2,1)S(1)}, u32[]{:S(2)}, u32[]{:S(2)}) collective-permute-start(bf16[528,256]{1,0:T(8,128)(2,1)S(1)} %shard_map.89), channel_id=1, source_target_pairs={{0,4},{1,5},{2,6},{3,7},{4,0},{5,1},{6,2},{7,3},{8,12},{9,13},{10,... | collective-permute-start | bytes 811016 | tf_op jit(solution)/shard_map/ppermute | solution.py:505
  42.2 0.1 collective-permute-done.8.refs_0_
  42.3 0.7 %shard_map.90 = bf16[528,256]{1,0:T(8,128)(2,1)S(1)} custom-call(s32[1]{0:T(128)} %bitcast.place_ref, bf16[8192,1024]{1,0:T(8,128)(2,1)S(1)} %copy-done, bf16[1024,256]{1,0:T(8,128)(2,1)S(1)} %get-tuple-element.36.turned_ref, bf16[528,256]{1,0:T(8,128)(2,1)S(1)} %collective-permute-done.8.refs_0_), custom_call_target="tpu_custom_call" | custom-call | bytes 1024 | tf_op jit(solution)/shard_map/pallas_call | solution.py:102
  43.0 2.2 %collective-permute-start.13 = (bf16[528,256]{1,0:T(8,128)(2,1)S(1)}, bf16[528,256]{1,0:T(8,128)(2,1)S(1)}, u32[]{:S(2)}, u32[]{:S(2)}) collective-permute-start(bf16[528,256]{1,0:T(8,128)(2,1)S(1)} %shard_map.90), channel_id=1, source_target_pairs={{0,2},{1,3},{2,0},{3,1},{4,6},{5,7},{6,4},{7,5},{8,10},{9,11},{10,... | collective-permute-start | bytes 811016 | tf_op jit(solution)/shard_map/ppermute | solution.py:505
  45.2 0.0 copy-done.3
  45.2 0.0 copy-done.4
  45.4 0.0 collective-permute-done.9.refs_1_
  45.4 2.7 %collective-permute-done.10.refs_0_ = bf16[528,256]{1,0:T(8,128)(2,1)S(1)} collective-permute-done((bf16[528,256]{1,0:T(8,128)(2,1)S(1)}, bf16[528,256]{1,0:T(8,128)(2,1)S(1)}, u32[]{:S(2)}, u32[]{:S(2)}) %collective-permute-start.10) | collective-permute-done | bytes 270368 | tf_op jit(solution)/shard_map/ppermute | solution.py:505
  48.1 0.0 copy-start.1
  48.1 0.0 copy-start.2
  48.1 0.4 shard_map.92.acc_ref
  48.5 0.4 shard_map.93.acc_ref
  49.0 0.1 copy-done.1
  49.1 0.2 copy-done.2
  49.3 2.4 %shard_map.94 = (bf16[256,1024]{1,0:T(8,128)(2,1)}, f32[1024,128]{1,0:T(8,128)S(1)}, f32[16,8,128]{2,1,0:T(8,128)S(1)}, f32[8,8,128]{2,1,0:T(8,128)S(1)}) custom-call(f32[512,256]{1,0:T(8,128)S(1)} %shard_map.92.acc_ref, bf16[528,256]{1,0:T(8,128)(2,1)S(1)} %collective-permute-done.10.refs_0_, bf16[528,256]{1,0:T(8,128)(2,1)S(1)} %collective-permute-done.9.refs_1_, ...), custom_call_target="tpu_custom_call" | custom-call | bytes 1024 | tf_op jit(solution)/shard_map/pallas_call | solution.py:259
  51.7 1.3 %collective-permute-done.11.refs_2_ = bf16[528,256]{1,0:T(8,128)(2,1)S(1)} collective-permute-done((bf16[528,256]{1,0:T(8,128)(2,1)S(1)}, bf16[528,256]{1,0:T(8,128)(2,1)S(1)}, u32[]{:S(2)}, u32[]{:S(2)}) %collective-permute-start.11) | collective-permute-done | bytes 270368 | tf_op jit(solution)/shard_map/ppermute | solution.py:505
  53.0 0.1 collective-permute-done.12.refs_0_
  53.1 0.8 %collective-permute-done.13.refs_1_ = bf16[528,256]{1,0:T(8,128)(2,1)S(1)} collective-permute-done((bf16[528,256]{1,0:T(8,128)(2,1)S(1)}, bf16[528,256]{1,0:T(8,128)(2,1)S(1)}, u32[]{:S(2)}, u32[]{:S(2)}) %collective-permute-start.13) | collective-permute-done | bytes 270368 | tf_op jit(solution)/shard_map/ppermute | solution.py:505
  53.9 1.5 %shard_map.95 = (bf16[256,1024]{1,0:T(8,128)(2,1)}, f32[1024,128]{1,0:T(8,128)S(1)}, f32[16,8,128]{2,1,0:T(8,128)S(1)}, f32[16,8,128]{2,1,0:T(8,128)S(1)}) custom-call(f32[512,256]{1,0:T(8,128)S(1)} %shard_map.93.acc_ref, bf16[528,256]{1,0:T(8,128)(2,1)S(1)} %collective-permute-done.12.refs_0_, ...), custom_call_target="tpu_custom_call", output_to_operand_aliasing={{0}: (9, {})} | custom-call | bytes 1024 | tf_op jit(solution)/shard_map/pallas_call | solution.py:259
  55.5 0.1 collective-permute-start.14
  55.5 1.7 %shard_map.96.refs_1_ = f32[1024,128]{1,0:T(8,128)S(1)} custom-call(f32[1024,128]{1,0:T(8,128)S(1)} %get-tuple-element.62.gc_ref, f32[16,8,128]{2,1,0:T(8,128)S(1)} %get-tuple-element.63.state_ref, f32[16,16,128]{2,1,0:T(8,128)S(1)} %bitcast.13, f32[16,16,128]{2,1,0:T(8,128)S(1)} %get-tuple-element.54.refs_6_.lap_ref, f32[16,16,128]{2,1,0:T(8,128)S(1)} %bitcast.16), custom_call_target="tpu_custom_call" | custom-call | bytes 1024 | tf_op jit(solution)/shard_map/pallas_call | solution.py:309
  57.3 0.0 collective-permute-done.14.arrived_ref.refs_3_
  57.3 1.0 %collective-permute-start.15 = (f32[16,8,128]{2,1,0:T(8,128)S(1)}, f32[16,8,128]{2,1,0:T(8,128)S(1)}, u32[]{:S(2)}, u32[]{:S(2)}) collective-permute-start(f32[16,8,128]{2,1,0:T(8,128)S(1)} %shard_map.97), channel_id=1, source_target_pairs={{0,16},{8,24},{16,0},{24,8},{1,17},{9,25},{17,1},{25,9},{2,18},{10... | collective-permute-start | bytes 196616 | tf_op jit(solution)/shard_map/ppermute | solution.py:542
  58.3 3.5 %collective-permute-done.15.refs_4_ = f32[16,8,128]{2,1,0:T(8,128)S(1)} collective-permute-done((f32[16,8,128]{2,1,0:T(8,128)S(1)}, f32[16,8,128]{2,1,0:T(8,128)S(1)}, u32[]{:S(2)}, u32[]{:S(2)}) %collective-permute-start.15) | collective-permute-done | bytes 65568 | tf_op jit(solution)/shard_map/ppermute | solution.py:542
  61.9 3.0 %shard_map.98 = bf16[256,1024]{1,0:T(8,128)(2,1)} custom-call(s32[1]{0:T(128)} %bitcast.5.group_ref, f32[1024,128]{1,0:T(8,128)S(1)} %get-tuple-element.59.refs_0_, f32[1024,128]{1,0:T(8,128)S(1)} %shard_map.96.refs_1_, f32[16,8,128]{2,1,0:T(8,128)S(1)} %get-tuple-element.64.refs_2_, f32[16,8,128]{2,1,0:T(8,128)S(1)} %collective-permute-done.14.arrived_ref.refs_3_, ...), custom_call_target="tpu_custom_call" | custom-call | bytes 1024 | tf_op jit(solution)/shard_map/pallas_call | solution.py:425
  (6 shorter events, 0.2 us)
Async XLA Ops:
  0.6 6.2 %copy-start = (bf16[8192,1024]{1,0:T(8,128)(2,1)S(1)}, bf16[8192,1024]{1,0:T(8,128)(2,1)}, u32[]{:S(2)}) copy-start(bf16[8192,1024]{1,0:T(8,128)(2,1)} %w_ref.29) | copy-start | bytes 50331652
  3.1 10.7 %collective-permute-start = (bf16[528,256]{1,0:T(8,128)(2,1)S(1)}, bf16[528,256]{1,0:T(8,128)(2,1)S(1)}, u32[]{:S(2)}, u32[]{:S(2)}) collective-permute-start(bf16[528,256]{1,0:T(8,128)(2,1)S(1)} %get-tuple-element.34), channel_id=1, source_target_pairs={{0,1},{1,0},{2,3},{3,2},{4,5},{5,4},{6,7},{7,6},{8,9},{9,8},{10,11... | collective-permute-start | bytes 811016 | tf_op jit(solution)/shard_map/ppermute | solution.py:505
  8.8 10.3 %collective-permute-start.1 = (bf16[528,256]{1,0:T(8,128)(2,1)S(1)}, bf16[528,256]{1,0:T(8,128)(2,1)S(1)}, u32[]{:S(2)}, u32[]{:S(2)}) collective-permute-start(bf16[528,256]{1,0:T(8,128)(2,1)S(1)} %shard_map.80), channel_id=1, source_target_pairs={{0,1},{1,0},{2,3},{3,2},{4,5},{5,4},{6,7},{7,6},{8,9},{9,8},{10,11... | collective-permute-start | bytes 811016 | tf_op jit(solution)/shard_map/ppermute | solution.py:505
  11.8 13.1 %collective-permute-start.2 = (bf16[528,256]{1,0:T(8,128)(2,1)S(1)}, bf16[528,256]{1,0:T(8,128)(2,1)S(1)}, u32[]{:S(2)}, u32[]{:S(2)}) collective-permute-start(bf16[528,256]{1,0:T(8,128)(2,1)S(1)} %shard_map.79), channel_id=1, source_target_pairs={{0,1},{1,0},{2,3},{3,2},{4,5},{5,4},{6,7},{7,6},{8,9},{9,8},{10,11... | collective-permute-start | bytes 811016 | tf_op jit(solution)/shard_map/ppermute | solution.py:505
  14.6 10.4 %collective-permute-start.3 = (bf16[528,256]{1,0:T(8,128)(2,1)S(1)}, bf16[528,256]{1,0:T(8,128)(2,1)S(1)}, u32[]{:S(2)}, u32[]{:S(2)}) collective-permute-start(bf16[528,256]{1,0:T(8,128)(2,1)S(1)} %shard_map.84), channel_id=1, source_target_pairs={{0,2},{1,3},{2,0},{3,1},{4,6},{5,7},{6,4},{7,5},{8,10},{9,11},{10,... | collective-permute-start | bytes 811016 | tf_op jit(solution)/shard_map/ppermute | solution.py:505
  16.6 14.6 %collective-permute-start.4 = (bf16[528,256]{1,0:T(8,128)(2,1)S(1)}, bf16[528,256]{1,0:T(8,128)(2,1)S(1)}, u32[]{:S(2)}, u32[]{:S(2)}) collective-permute-start(bf16[528,256]{1,0:T(8,128)(2,1)S(1)} %shard_map.83), channel_id=1, source_target_pairs={{0,1},{1,0},{2,3},{3,2},{4,5},{5,4},{6,7},{7,6},{8,9},{9,8},{10,11... | collective-permute-start | bytes 811016 | tf_op jit(solution)/shard_map/ppermute | solution.py:505
  19.9 13.8 %collective-permute-start.5 = (bf16[528,256]{1,0:T(8,128)(2,1)S(1)}, bf16[528,256]{1,0:T(8,128)(2,1)S(1)}, u32[]{:S(2)}, u32[]{:S(2)}) collective-permute-start(bf16[528,256]{1,0:T(8,128)(2,1)S(1)} %shard_map.85), channel_id=1, source_target_pairs={{0,2},{1,3},{2,0},{3,1},{4,6},{5,7},{6,4},{7,5},{8,10},{9,11},{10,... | collective-permute-start | bytes 811016 | tf_op jit(solution)/shard_map/ppermute | solution.py:505
  22.1 14.4 %collective-permute-start.6 = (bf16[528,256]{1,0:T(8,128)(2,1)S(1)}, bf16[528,256]{1,0:T(8,128)(2,1)S(1)}, u32[]{:S(2)}, u32[]{:S(2)}) collective-permute-start(bf16[528,256]{1,0:T(8,128)(2,1)S(1)} %shard_map.82), channel_id=1, source_target_pairs={{0,1},{1,0},{2,3},{3,2},{4,5},{5,4},{6,7},{7,6},{8,9},{9,8},{10,11... | collective-permute-start | bytes 811016 | tf_op jit(solution)/shard_map/ppermute | solution.py:505
  25.8 13.9 %collective-permute-start.7 = (bf16[528,256]{1,0:T(8,128)(2,1)S(1)}, bf16[528,256]{1,0:T(8,128)(2,1)S(1)}, u32[]{:S(2)}, u32[]{:S(2)}) collective-permute-start(bf16[528,256]{1,0:T(8,128)(2,1)S(1)} %shard_map.86), channel_id=1, source_target_pairs={{0,4},{1,5},{2,6},{3,7},{4,0},{5,1},{6,2},{7,3},{8,12},{9,13},{10,... | collective-permute-start | bytes 811016 | tf_op jit(solution)/shard_map/ppermute | solution.py:505
  29.0 13.2 %collective-permute-start.8 = (bf16[528,256]{1,0:T(8,128)(2,1)S(1)}, bf16[528,256]{1,0:T(8,128)(2,1)S(1)}, u32[]{:S(2)}, u32[]{:S(2)}) collective-permute-start(bf16[528,256]{1,0:T(8,128)(2,1)S(1)} %shard_map.81), channel_id=1, source_target_pairs={{0,1},{1,0},{2,3},{3,2},{4,5},{5,4},{6,7},{7,6},{8,9},{9,8},{10,11... | collective-permute-start | bytes 811016 | tf_op jit(solution)/shard_map/ppermute | solution.py:505
  32.0 13.3 %copy-start.3 = (f32[1024,16]{0,1:T(8,128)S(1)}, f32[1024,16]{0,1:T(8,128)}, u32[]{:S(2)}) copy-start(f32[1024,16]{0,1:T(8,128)} %param.10) | copy-start | bytes 196612
  32.0 13.3 %copy-start.4 = (f32[1024,16]{0,1:T(8,128)S(1)}, f32[1024,16]{0,1:T(8,128)}, u32[]{:S(2)}) copy-start(f32[1024,16]{0,1:T(8,128)} %param.11) | copy-start | bytes 196612
  32.0 13.4 %collective-permute-start.9 = (bf16[528,256]{1,0:T(8,128)(2,1)S(1)}, bf16[528,256]{1,0:T(8,128)(2,1)S(1)}, u32[]{:S(2)}, u32[]{:S(2)}) collective-permute-start(bf16[528,256]{1,0:T(8,128)(2,1)S(1)} %shard_map.88), channel_id=1, source_target_pairs={{0,2},{1,3},{2,0},{3,1},{4,6},{5,7},{6,4},{7,5},{8,10},{9,11},{10,... | collective-permute-start | bytes 811016 | tf_op jit(solution)/shard_map/ppermute | solution.py:505
  33.7 14.4 %collective-permute-start.10 = (bf16[528,256]{1,0:T(8,128)(2,1)S(1)}, bf16[528,256]{1,0:T(8,128)(2,1)S(1)}, u32[]{:S(2)}, u32[]{:S(2)}) collective-permute-start(bf16[528,256]{1,0:T(8,128)(2,1)S(1)} %shard_map.87), channel_id=1, source_target_pairs={{0,1},{1,0},{2,3},{3,2},{4,5},{5,4},{6,7},{7,6},{8,9},{9,8},{10,11... | collective-permute-start | bytes 811016 | tf_op jit(solution)/shard_map/ppermute | solution.py:505
  36.5 16.6 %collective-permute-start.12 = (bf16[528,256]{1,0:T(8,128)(2,1)S(1)}, bf16[528,256]{1,0:T(8,128)(2,1)S(1)}, u32[]{:S(2)}, u32[]{:S(2)}) collective-permute-start(bf16[528,256]{1,0:T(8,128)(2,1)S(1)} %shard_map.78), channel_id=1, source_target_pairs={{0,1},{1,0},{2,3},{3,2},{4,5},{5,4},{6,7},{7,6},{8,9},{9,8},{10,11... | collective-permute-start | bytes 811016 | tf_op jit(solution)/shard_map/ppermute | solution.py:505
  39.7 13.3 %collective-permute-start.11 = (bf16[528,256]{1,0:T(8,128)(2,1)S(1)}, bf16[528,256]{1,0:T(8,128)(2,1)S(1)}, u32[]{:S(2)}, u32[]{:S(2)}) collective-permute-start(bf16[528,256]{1,0:T(8,128)(2,1)S(1)} %shard_map.89), channel_id=1, source_target_pairs={{0,4},{1,5},{2,6},{3,7},{4,0},{5,1},{6,2},{7,3},{8,12},{9,13},{10,... | collective-permute-start | bytes 811016 | tf_op jit(solution)/shard_map/ppermute | solution.py:505
  43.0 10.9 %collective-permute-start.13 = (bf16[528,256]{1,0:T(8,128)(2,1)S(1)}, bf16[528,256]{1,0:T(8,128)(2,1)S(1)}, u32[]{:S(2)}, u32[]{:S(2)}) collective-permute-start(bf16[528,256]{1,0:T(8,128)(2,1)S(1)} %shard_map.90), channel_id=1, source_target_pairs={{0,2},{1,3},{2,0},{3,1},{4,6},{5,7},{6,4},{7,5},{8,10},{9,11},{10,... | collective-permute-start | bytes 811016 | tf_op jit(solution)/shard_map/ppermute | solution.py:505
  48.1 1.0 %copy-start.1 = (bf16[256,1024]{1,0:T(8,128)(2,1)S(1)}, bf16[256,1024]{1,0:T(8,128)(2,1)}, u32[]{:S(2)}) copy-start(bf16[256,1024]{1,0:T(8,128)(2,1)} %refs_3_.3) | copy-start | bytes 1572868
  48.1 1.2 %copy-start.2 = (bf16[256,1024]{1,0:T(8,128)(2,1)S(1)}, bf16[256,1024]{1,0:T(8,128)(2,1)}, u32[]{:S(2)}) copy-start(bf16[256,1024]{1,0:T(8,128)(2,1)} %refs_4_.3) | copy-start | bytes 1572868
  55.5 1.8 %collective-permute-start.14 = (f32[16,8,128]{2,1,0:T(8,128)S(1)}, f32[16,8,128]{2,1,0:T(8,128)S(1)}, u32[]{:S(2)}, u32[]{:S(2)}) collective-permute-start(f32[16,8,128]{2,1,0:T(8,128)S(1)} %get-tuple-element.61.state_ref), channel_id=1, source_target_pairs={{0,8},{8,0},{16,24},{24,16},{1,9},{9,1},{17,25},{25,17},{2,10},{10... | collective-permute-start | bytes 196616 | tf_op jit(solution)/shard_map/ppermute | solution.py:542
  57.3 4.6 %collective-permute-start.15 = (f32[16,8,128]{2,1,0:T(8,128)S(1)}, f32[16,8,128]{2,1,0:T(8,128)S(1)}, u32[]{:S(2)}, u32[]{:S(2)}) collective-permute-start(f32[16,8,128]{2,1,0:T(8,128)S(1)} %shard_map.97), channel_id=1, source_target_pairs={{0,16},{8,24},{16,0},{24,8},{1,17},{9,25},{17,1},{25,9},{2,18},{10... | collective-permute-start | bytes 196616 | tf_op jit(solution)/shard_map/ppermute | solution.py:542

commit v10 on v9

--- a/solution.py
+++ b/solution.py
@@ -12,6 +12,7 @@
 SPAN = 251 * math.log(2.0)
 SHIFT = 125 * math.log(2.0)
 STEP = 256
+PIECE = 128
 VMEM = 24 * 1024 * 1024
 QUICK = pl.CostEstimate(flops=0, bytes_accessed=1024, transcendentals=0)
 
@@ -110,10 +111,14 @@
 
 
 def first_kernel(items, width, place_ref, w_hbm, g_hbm, out_ref, turned_ref, w_ref, g_ref, sems):
-    copies = [pltpu.make_async_copy(g_hbm, g_ref, sems.at[0])]
-    base = 0
+    copies, toks = [], g_ref.shape[0]
+    piece = math.gcd(toks, PIECE)
+    for at in range(0, toks, piece):
+        lines = pl.ds(at, piece)
+        copies.append(pltpu.make_async_copy(g_hbm.at[lines, :], g_ref.at[lines, :], sems.at[len(copies)]))
+    base, grads = 0, len(copies)
     for block, offset, rows, _ in items:
-        step = step_of(rows)
+        step = math.gcd(rows, PIECE)
         first = pl.multiple_of((place_ref[0] ^ block) * width + offset, 16)
         for at in range(0, rows, step):
             copies.append(
@@ -124,13 +129,15 @@
         base += rows
     for copy in copies:
         copy.start()
-    copies[0].wait()
-    turned_ref[...] = g_ref[...].T
-    base, peaks, waits = 0, [], iter(copies[1:])
+    for i, at in enumerate(range(0, toks, piece)):
+        copies[i].wait()
+        turned_ref[:, at : at + piece] = g_ref[at : at + piece, :].T
+    base, peaks, waits = 0, [], iter(copies[grads:])
     for _, _, rows, _ in items:
         step = step_of(rows)
         for at in range(base, base + rows, step):
-            next(waits).wait()
+            for _ in range(step // math.gcd(rows, PIECE)):
+                next(waits).wait()
             total = jnp.dot(w_ref[at : at + step, :], turned_ref[...], preferred_element_type=jnp.float32)
             total, more = encode(total, part_of(rows, len(items)))
             peaks += more
@@ -144,7 +151,7 @@
     vmem = pl.BlockSpec(memory_space=pltpu.VMEM)
     high = pl.BlockSpec(memory_space=pltpu.HBM)
     count = sum(rows for _, _, rows, _ in items)
-    steps = sum(rows // step_of(rows) for _, _, rows, _ in items)
+    steps = toks // math.gcd(toks, PIECE) + sum(rows // math.gcd(rows, PIECE) for _, _, rows, _ in items)
     return pl.pallas_call(
         functools.partial(first_kernel, items, width),
         in_specs=[pl.BlockSpec(memory_space=pltpu.SMEM), high, high],
@@ -156,7 +163,7 @@
         scratch_shapes=[
             pltpu.VMEM((count, depth), jnp.bfloat16),
             pltpu.VMEM((toks, depth), jnp.bfloat16),
-            pltpu.SemaphoreType.DMA((1 + steps,)),
+            pltpu.SemaphoreType.DMA((steps,)),
         ],
         compiler_params=pltpu.CompilerParams(vmem_limit_bytes=VMEM),
         cost_estimate=QUICK,
@@ -164,6 +171,8 @@
 
 
 def steps_back(count, body, state, unroll):
+    unroll = math.gcd(count, unroll)
+
     def some(i, state):
         for j in range(unroll):
             state = body(count - 1 - (i * unroll + j), state)
@@ -224,7 +233,7 @@
         return state
 
     zero = jnp.zeros((sublanes, lanes), jnp.float32)
-    state = steps_back(span, step, (zero,) * modes, 8)
+    state = steps_back(span, step, (zero,) * modes, 16)
     segment = segment_of((sublanes, lanes), segments)
     whole = []
     for n in range(modes):
@@ -301,7 +310,7 @@
         rows_ref[at, :] = summed([residue_ref[n, mine] * state[n] for n in range(modes)])
         return state
 
-    steps_back(span, step, tuple(start), 8)
+    steps_back(span, step, tuple(start), 16)
 
 
 def scan(half, segments, grad_conv, state, decay, lap, residues):
@@ -408,7 +417,7 @@
             rows_ref[at, :] = scanned_ref[at, :] + summed(list(state))
             return state
 
-        steps_back(span, step, tuple(start), 8)
+        steps_back(span, step, tuple(start), 16)
         for line in range(rows // lanes):
             out_ref[:, half * rows + line * lanes : half * rows + (line + 1) * lanes] = rows_ref[
                 line * toks : (line + 1) * toks, :
@@ -540,12 +549,11 @@
         elif kind == "scan":
             groups = lax.axis_size("ctx")
             swap = lambda array, round_: lax.ppermute(array, "ctx", [(i, i ^ (1 << round_)) for i in range(groups)])
-            arrived = [swap(packed[1], 0)]
-            last = scanned[1] = scan(1, segments, after(scanned[1]), states[1], decay, lap, residue)
-            joined = packed[1]
+            arrived, joined = [swap(packed[1], 0)], packed[1]
             for round_ in range(1, groups.bit_length() - 1):
                 joined = last = join(round_ - 1, after(group), joined, arrived[-1], wide)
                 arrived.append(swap(joined, round_))
+            scanned[1] = scan(1, segments, after(scanned[1]), states[1], decay, lap, residue)
         else:
             grad_input = fix(
                 segments, group, [scanned[0], scanned[1]], states[0], arrived, decay, lap, wide, residue, toks, width

time: 65.3 us -> 64.6 us (0.989)
  waiting for transfers between devices: 12.4 us -> 11.6 us
    ppermute x2, waiting for transfers between devices: 3.55 us -> 2.75 us  [local(): lax.ppermute(array, 'ctx', [(i, i ^ 1 << round_) for i in range(groups)])]
  transfers between devices with their start and end apart: 16 -> 16, of which waited for: 10 -> 11; matrix products, arithmetic and copies ran while one was open for 0% -> 0% of each run, Pallas kernels for 22% -> 22%
where the time goes in v10:
time: 64.6 us; the launch traced here: 64.1 us
  starting transfers between devices  29.1 us (45%)
  Pallas kernels  21.3 us (33%)
  waiting for transfers between devices  11.6 us (18%)
  local copies, waits for them, and re-layouts  1.19 us (2%)
  between operations  0.91 us (1%)
    ppermute x14, starting transfers between devices, local(): arrived = lax.ppermute(last, 'ch', [(i, i ^ bit) for i in range(size)])  28 us
    pallas_call x15, Pallas kernels, send(): pl.pallas_call(functools.partial(send_kernel, items, coded, width, len(ne...  10.1 us
    ppermute x14, waiting for transfers between devices, local(): arrived = lax.ppermute(last, 'ch', [(i, i ^ bit) for i in range(size)])  8.83 us
    pallas_call x2, Pallas kernels, gate(): pl.pallas_call(functools.partial(gate_kernel, half, rows, segments, piece...  3.9 us
    pallas_call x1, Pallas kernels, fix(): pl.pallas_call(functools.partial(fix_kernel, segments, len(arrived)), in_...  3.09 us
    ppermute x2, waiting for transfers between devices, local(): lax.ppermute(array, 'ctx', [(i, i ^ 1 << round_) for i in range(groups)])  2.75 us
    pallas_call x1, Pallas kernels, first_send(): pl.pallas_call(functools.partial(first_kernel, items, width), in_specs=[p...  2.39 us
    pallas_call x1, Pallas kernels, scan(): pl.pallas_call(functools.partial(scan_kernel, half, segments), in_specs=[...  1.78 us
  transfers between devices with their start and end apart: 16, of which 11 were waited for; matrix products, arithmetic and copies ran while one was open for 0% of the time, Pallas kernels for 22%

profile of v10, /device:TPU:0, one launch (start us, length us, event | category | flops | bytes accessed | tf_op | source)
XLA Modules:
  0.0 64.1 jit_solution(14215409623213984720)
XLA Ops:
  0.6 0.0 copy-start
  0.6 2.4 %shard_map.77 = (bf16[528,256]{1,0:T(8,128)(2,1)S(1)}, bf16[1024,256]{1,0:T(8,128)(2,1)S(1)}) custom-call(s32[1]{0:T(128)} %bitcast.place_ref, bf16[8192,1024]{1,0:T(8,128)(2,1)} %w_ref.29, bf16[256,1024]{1,0:T(8,128)(2,1)} %g_hbm.1), custom_call_target="tpu_custom_call" | custom-call | bytes 1024 | tf_op jit(solution)/shard_map/pallas_call | solution.py:155
  3.0 3.0 %collective-permute-start = (bf16[528,256]{1,0:T(8,128)(2,1)S(1)}, bf16[528,256]{1,0:T(8,128)(2,1)S(1)}, u32[]{:S(2)}, u32[]{:S(2)}) collective-permute-start(bf16[528,256]{1,0:T(8,128)(2,1)S(1)} %get-tuple-element.34), channel_id=1, source_target_pairs={{0,1},{1,0},{2,3},{3,2},{4,5},{5,4},{6,7},{7,6},{8,9},{9,8},{10,11... | collective-permute-start | bytes 811016 | tf_op jit(solution)/shard_map/ppermute | solution.py:514
  6.1 0.8 %copy-done = bf16[8192,1024]{1,0:T(8,128)(2,1)S(1)} copy-done((bf16[8192,1024]{1,0:T(8,128)(2,1)S(1)}, bf16[8192,1024]{1,0:T(8,128)(2,1)}, u32[]{:S(2)}) %copy-start) | copy-done | bytes 16777240
  6.9 0.6 shard_map.78
  7.5 0.6 shard_map.79
  8.1 0.6 shard_map.80
  8.8 3.0 %collective-permute-start.1 = (bf16[528,256]{1,0:T(8,128)(2,1)S(1)}, bf16[528,256]{1,0:T(8,128)(2,1)S(1)}, u32[]{:S(2)}, u32[]{:S(2)}) collective-permute-start(bf16[528,256]{1,0:T(8,128)(2,1)S(1)} %shard_map.80), channel_id=1, source_target_pairs={{0,1},{1,0},{2,3},{3,2},{4,5},{5,4},{6,7},{7,6},{8,9},{9,8},{10,11... | collective-permute-start | bytes 811016 | tf_op jit(solution)/shard_map/ppermute | solution.py:514
  11.8 0.1 collective-permute-start.2
  11.9 0.6 shard_map.81
  12.5 0.6 shard_map.82
  13.2 0.6 shard_map.83
  13.8 0.0 collective-permute-done.refs_0_
  13.8 0.7 %shard_map.84 = bf16[528,256]{1,0:T(8,128)(2,1)S(1)} custom-call(s32[1]{0:T(128)} %bitcast.place_ref, bf16[8192,1024]{1,0:T(8,128)(2,1)S(1)} %copy-done, bf16[1024,256]{1,0:T(8,128)(2,1)S(1)} %get-tuple-element.36.turned_ref, bf16[528,256]{1,0:T(8,128)(2,1)S(1)} %collective-permute-done.refs_0_), custom_call_target="tpu_custom_call" | custom-call | bytes 1024 | tf_op jit(solution)/shard_map/pallas_call | solution.py:103
  14.6 2.1 %collective-permute-start.3 = (bf16[528,256]{1,0:T(8,128)(2,1)S(1)}, bf16[528,256]{1,0:T(8,128)(2,1)S(1)}, u32[]{:S(2)}, u32[]{:S(2)}) collective-permute-start(bf16[528,256]{1,0:T(8,128)(2,1)S(1)} %shard_map.84), channel_id=1, source_target_pairs={{0,2},{1,3},{2,0},{3,1},{4,6},{5,7},{6,4},{7,5},{8,10},{9,11},{10,... | collective-permute-start | bytes 811016 | tf_op jit(solution)/shard_map/ppermute | solution.py:514
  16.6 1.5 %collective-permute-start.4 = (bf16[528,256]{1,0:T(8,128)(2,1)S(1)}, bf16[528,256]{1,0:T(8,128)(2,1)S(1)}, u32[]{:S(2)}, u32[]{:S(2)}) collective-permute-start(bf16[528,256]{1,0:T(8,128)(2,1)S(1)} %shard_map.83), channel_id=1, source_target_pairs={{0,1},{1,0},{2,3},{3,2},{4,5},{5,4},{6,7},{7,6},{8,9},{9,8},{10,11... | collective-permute-start | bytes 811016 | tf_op jit(solution)/shard_map/ppermute | solution.py:514
  18.1 1.0 %collective-permute-done.1.refs_0_ = bf16[528,256]{1,0:T(8,128)(2,1)S(1)} collective-permute-done((bf16[528,256]{1,0:T(8,128)(2,1)S(1)}, bf16[528,256]{1,0:T(8,128)(2,1)S(1)}, u32[]{:S(2)}, u32[]{:S(2)}) %collective-permute-start.1) | collective-permute-done | bytes 270368 | tf_op jit(solution)/shard_map/ppermute | solution.py:514
  19.1 0.7 %shard_map.85 = bf16[528,256]{1,0:T(8,128)(2,1)S(1)} custom-call(s32[1]{0:T(128)} %bitcast.place_ref, bf16[8192,1024]{1,0:T(8,128)(2,1)S(1)} %copy-done, bf16[1024,256]{1,0:T(8,128)(2,1)S(1)} %get-tuple-element.36.turned_ref, bf16[528,256]{1,0:T(8,128)(2,1)S(1)} %collective-permute-done.1.refs_0_), custom_call_target="tpu_custom_call" | custom-call | bytes 1024 | tf_op jit(solution)/shard_map/pallas_call | solution.py:103
  19.9 2.2 %collective-permute-start.5 = (bf16[528,256]{1,0:T(8,128)(2,1)S(1)}, bf16[528,256]{1,0:T(8,128)(2,1)S(1)}, u32[]{:S(2)}, u32[]{:S(2)}) collective-permute-start(bf16[528,256]{1,0:T(8,128)(2,1)S(1)} %shard_map.85), channel_id=1, source_target_pairs={{0,2},{1,3},{2,0},{3,1},{4,6},{5,7},{6,4},{7,5},{8,10},{9,11},{10,... | collective-permute-start | bytes 811016 | tf_op jit(solution)/shard_map/ppermute | solution.py:514
  22.1 1.5 %collective-permute-start.6 = (bf16[528,256]{1,0:T(8,128)(2,1)S(1)}, bf16[528,256]{1,0:T(8,128)(2,1)S(1)}, u32[]{:S(2)}, u32[]{:S(2)}) collective-permute-start(bf16[528,256]{1,0:T(8,128)(2,1)S(1)} %shard_map.82), channel_id=1, source_target_pairs={{0,1},{1,0},{2,3},{3,2},{4,5},{5,4},{6,7},{7,6},{8,9},{9,8},{10,11... | collective-permute-start | bytes 811016 | tf_op jit(solution)/shard_map/ppermute | solution.py:514
  23.6 1.3 %collective-permute-done.2.refs_0_ = bf16[528,256]{1,0:T(8,128)(2,1)S(1)} collective-permute-done((bf16[528,256]{1,0:T(8,128)(2,1)S(1)}, bf16[528,256]{1,0:T(8,128)(2,1)S(1)}, u32[]{:S(2)}, u32[]{:S(2)}) %collective-permute-start.2) | collective-permute-done | bytes 270368 | tf_op jit(solution)/shard_map/ppermute | solution.py:514
  24.9 0.0 collective-permute-done.3.refs_1_
  24.9 0.9 %shard_map.86 = bf16[528,256]{1,0:T(8,128)(2,1)S(1)} custom-call(s32[1]{0:T(128)} %bitcast.place_ref, bf16[8192,1024]{1,0:T(8,128)(2,1)S(1)} %copy-done, bf16[1024,256]{1,0:T(8,128)(2,1)S(1)} %get-tuple-element.36.turned_ref, bf16[528,256]{1,0:T(8,128)(2,1)S(1)} %collective-permute-done.2.refs_0_, bf16[528,256]{1,0:T(8,128)(2,1)S(1)} %collective-permute-done.3.refs_1_), custom_call_target="tpu_custom_call" | custom-call | bytes 1024 | tf_op jit(solution)/shard_map/pallas_call | solution.py:103
  25.8 3.2 %collective-permute-start.7 = (bf16[528,256]{1,0:T(8,128)(2,1)S(1)}, bf16[528,256]{1,0:T(8,128)(2,1)S(1)}, u32[]{:S(2)}, u32[]{:S(2)}) collective-permute-start(bf16[528,256]{1,0:T(8,128)(2,1)S(1)} %shard_map.86), channel_id=1, source_target_pairs={{0,4},{1,5},{2,6},{3,7},{4,0},{5,1},{6,2},{7,3},{8,12},{9,13},{10,... | collective-permute-start | bytes 811016 | tf_op jit(solution)/shard_map/ppermute | solution.py:514
  29.0 1.5 %collective-permute-start.8 = (bf16[528,256]{1,0:T(8,128)(2,1)S(1)}, bf16[528,256]{1,0:T(8,128)(2,1)S(1)}, u32[]{:S(2)}, u32[]{:S(2)}) collective-permute-start(bf16[528,256]{1,0:T(8,128)(2,1)S(1)} %shard_map.81), channel_id=1, source_target_pairs={{0,1},{1,0},{2,3},{3,2},{4,5},{5,4},{6,7},{7,6},{8,9},{9,8},{10,11... | collective-permute-start | bytes 811016 | tf_op jit(solution)/shard_map/ppermute | solution.py:514
  30.6 0.6 shard_map.87
  31.2 0.0 collective-permute-done.4.refs_0_
  31.2 0.7 %shard_map.88 = bf16[528,256]{1,0:T(8,128)(2,1)S(1)} custom-call(s32[1]{0:T(128)} %bitcast.place_ref, bf16[8192,1024]{1,0:T(8,128)(2,1)S(1)} %copy-done, bf16[1024,256]{1,0:T(8,128)(2,1)S(1)} %get-tuple-element.36.turned_ref, bf16[528,256]{1,0:T(8,128)(2,1)S(1)} %collective-permute-done.4.refs_0_), custom_call_target="tpu_custom_call" | custom-call | bytes 1024 | tf_op jit(solution)/shard_map/pallas_call | solution.py:103
  32.0 0.0 copy-start.3
  32.0 0.0 copy-start.4
  32.0 1.7 %collective-permute-start.9 = (bf16[528,256]{1,0:T(8,128)(2,1)S(1)}, bf16[528,256]{1,0:T(8,128)(2,1)S(1)}, u32[]{:S(2)}, u32[]{:S(2)}) collective-permute-start(bf16[528,256]{1,0:T(8,128)(2,1)S(1)} %shard_map.88), channel_id=1, source_target_pairs={{0,2},{1,3},{2,0},{3,1},{4,6},{5,7},{6,4},{7,5},{8,10},{9,11},{10,... | collective-permute-start | bytes 811016 | tf_op jit(solution)/shard_map/ppermute | solution.py:514
  33.7 0.0 collective-permute-done.5.refs_1_
  33.7 1.5 %collective-permute-start.10 = (bf16[528,256]{1,0:T(8,128)(2,1)S(1)}, bf16[528,256]{1,0:T(8,128)(2,1)S(1)}, u32[]{:S(2)}, u32[]{:S(2)}) collective-permute-start(bf16[528,256]{1,0:T(8,128)(2,1)S(1)} %shard_map.87), channel_id=1, source_target_pairs={{0,1},{1,0},{2,3},{3,2},{4,5},{5,4},{6,7},{7,6},{8,9},{9,8},{10,11... | collective-permute-start | bytes 811016 | tf_op jit(solution)/shard_map/ppermute | solution.py:514
  35.2 1.3 %collective-permute-done.6.refs_0_ = bf16[528,256]{1,0:T(8,128)(2,1)S(1)} collective-permute-done((bf16[528,256]{1,0:T(8,128)(2,1)S(1)}, bf16[528,256]{1,0:T(8,128)(2,1)S(1)}, u32[]{:S(2)}, u32[]{:S(2)}) %collective-permute-start.6) | collective-permute-done | bytes 270368 | tf_op jit(solution)/shard_map/ppermute | solution.py:514
  36.5 2.1 %collective-permute-start.12 = (bf16[528,256]{1,0:T(8,128)(2,1)S(1)}, bf16[528,256]{1,0:T(8,128)(2,1)S(1)}, u32[]{:S(2)}, u32[]{:S(2)}) collective-permute-start(bf16[528,256]{1,0:T(8,128)(2,1)S(1)} %shard_map.78), channel_id=1, source_target_pairs={{0,1},{1,0},{2,3},{3,2},{4,5},{5,4},{6,7},{7,6},{8,9},{9,8},{10,11... | collective-permute-start | bytes 811016 | tf_op jit(solution)/shard_map/ppermute | solution.py:514
  38.6 0.9 %shard_map.89 = bf16[528,256]{1,0:T(8,128)(2,1)S(1)} custom-call(s32[1]{0:T(128)} %bitcast.place_ref, bf16[8192,1024]{1,0:T(8,128)(2,1)S(1)} %copy-done, bf16[1024,256]{1,0:T(8,128)(2,1)S(1)} %get-tuple-element.36.turned_ref, bf16[528,256]{1,0:T(8,128)(2,1)S(1)} %collective-permute-done.6.refs_0_, bf16[528,256]{1,0:T(8,128)(2,1)S(1)} %collective-permute-done.5.refs_1_), custom_call_target="tpu_custom_call" | custom-call | bytes 1024 | tf_op jit(solution)/shard_map/pallas_call | solution.py:103
  39.5 0.2 collective-permute-done.7.refs_2_
  39.7 2.4 %collective-permute-start.11 = (bf16[528,256]{1,0:T(8,128)(2,1)S(1)}, bf16[528,256]{1,0:T(8,128)(2,1)S(1)}, u32[]{:S(2)}, u32[]{:S(2)}) collective-permute-start(bf16[528,256]{1,0:T(8,128)(2,1)S(1)} %shard_map.89), channel_id=1, source_target_pairs={{0,4},{1,5},{2,6},{3,7},{4,0},{5,1},{6,2},{7,3},{8,12},{9,13},{10,... | collective-permute-start | bytes 811016 | tf_op jit(solution)/shard_map/ppermute | solution.py:514
  42.2 0.1 collective-permute-done.8.refs_0_
  42.3 0.7 %shard_map.90 = bf16[528,256]{1,0:T(8,128)(2,1)S(1)} custom-call(s32[1]{0:T(128)} %bitcast.place_ref, bf16[8192,1024]{1,0:T(8,128)(2,1)S(1)} %copy-done, bf16[1024,256]{1,0:T(8,128)(2,1)S(1)} %get-tuple-element.36.turned_ref, bf16[528,256]{1,0:T(8,128)(2,1)S(1)} %collective-permute-done.8.refs_0_), custom_call_target="tpu_custom_call" | custom-call | bytes 1024 | tf_op jit(solution)/shard_map/pallas_call | solution.py:103
  43.0 2.2 %collective-permute-start.13 = (bf16[528,256]{1,0:T(8,128)(2,1)S(1)}, bf16[528,256]{1,0:T(8,128)(2,1)S(1)}, u32[]{:S(2)}, u32[]{:S(2)}) collective-permute-start(bf16[528,256]{1,0:T(8,128)(2,1)S(1)} %shard_map.90), channel_id=1, source_target_pairs={{0,2},{1,3},{2,0},{3,1},{4,6},{5,7},{6,4},{7,5},{8,10},{9,11},{10,... | collective-permute-start | bytes 811016 | tf_op jit(solution)/shard_map/ppermute | solution.py:514
  45.2 0.0 copy-done.3
  45.2 0.0 copy-done.4
  45.4 0.0 collective-permute-done.9.refs_1_
  45.4 2.7 %collective-permute-done.10.refs_0_ = bf16[528,256]{1,0:T(8,128)(2,1)S(1)} collective-permute-done((bf16[528,256]{1,0:T(8,128)(2,1)S(1)}, bf16[528,256]{1,0:T(8,128)(2,1)S(1)}, u32[]{:S(2)}, u32[]{:S(2)}) %collective-permute-start.10) | collective-permute-done | bytes 270368 | tf_op jit(solution)/shard_map/ppermute | solution.py:514
  48.1 0.0 copy-start.1
  48.1 0.0 copy-start.2
  48.1 0.4 shard_map.92.acc_ref
  48.5 0.4 shard_map.93.acc_ref
  49.0 0.1 copy-done.1
  49.1 0.2 copy-done.2
  49.3 2.4 %shard_map.94 = (bf16[256,1024]{1,0:T(8,128)(2,1)}, f32[1024,128]{1,0:T(8,128)S(1)}, f32[16,8,128]{2,1,0:T(8,128)S(1)}, f32[8,8,128]{2,1,0:T(8,128)S(1)}) custom-call(f32[512,256]{1,0:T(8,128)S(1)} %shard_map.92.acc_ref, bf16[528,256]{1,0:T(8,128)(2,1)S(1)} %collective-permute-done.10.refs_0_, bf16[528,256]{1,0:T(8,128)(2,1)S(1)} %collective-permute-done.9.refs_1_, ...), custom_call_target="tpu_custom_call" | custom-call | bytes 1024 | tf_op jit(solution)/shard_map/pallas_call | solution.py:268
  51.7 1.2 %collective-permute-done.11.refs_2_ = bf16[528,256]{1,0:T(8,128)(2,1)S(1)} collective-permute-done((bf16[528,256]{1,0:T(8,128)(2,1)S(1)}, bf16[528,256]{1,0:T(8,128)(2,1)S(1)}, u32[]{:S(2)}, u32[]{:S(2)}) %collective-permute-start.11) | collective-permute-done | bytes 270368 | tf_op jit(solution)/shard_map/ppermute | solution.py:514
  53.0 0.1 collective-permute-done.12.refs_0_
  53.1 0.8 %collective-permute-done.13.refs_1_ = bf16[528,256]{1,0:T(8,128)(2,1)S(1)} collective-permute-done((bf16[528,256]{1,0:T(8,128)(2,1)S(1)}, bf16[528,256]{1,0:T(8,128)(2,1)S(1)}, u32[]{:S(2)}, u32[]{:S(2)}) %collective-permute-start.13) | collective-permute-done | bytes 270368 | tf_op jit(solution)/shard_map/ppermute | solution.py:514
  53.9 1.5 %shard_map.95 = (bf16[256,1024]{1,0:T(8,128)(2,1)}, f32[1024,128]{1,0:T(8,128)S(1)}, f32[16,8,128]{2,1,0:T(8,128)S(1)}, f32[16,8,128]{2,1,0:T(8,128)S(1)}) custom-call(f32[512,256]{1,0:T(8,128)S(1)} %shard_map.93.acc_ref, bf16[528,256]{1,0:T(8,128)(2,1)S(1)} %collective-permute-done.12.refs_0_, ...), custom_call_target="tpu_custom_call", output_to_operand_aliasing={{0}: (9, {})} | custom-call | bytes 1024 | tf_op jit(solution)/shard_map/pallas_call | solution.py:268
  55.3 0.1 collective-permute-start.14
  55.4 1.2 %collective-permute-done.14.arrived_ref.refs_3_ = f32[16,8,128]{2,1,0:T(8,128)S(1)} collective-permute-done((f32[16,8,128]{2,1,0:T(8,128)S(1)}, f32[16,8,128]{2,1,0:T(8,128)S(1)}, u32[]{:S(2)}, u32[]{:S(2)}) %collective-permute-start.14) | collective-permute-done | bytes 65568 | tf_op jit(solution)/shard_map/ppermute | solution.py:551
  56.7 1.0 %collective-permute-start.15 = (f32[16,8,128]{2,1,0:T(8,128)S(1)}, f32[16,8,128]{2,1,0:T(8,128)S(1)}, u32[]{:S(2)}, u32[]{:S(2)}) collective-permute-start(f32[16,8,128]{2,1,0:T(8,128)S(1)} %shard_map.96), channel_id=1, source_target_pairs={{0,16},{8,24},{16,0},{24,8},{1,17},{9,25},{17,1},{25,9},{2,18},{10... | collective-permute-start | bytes 196616 | tf_op jit(solution)/shard_map/ppermute | solution.py:551
  57.7 1.8 %shard_map.97.refs_1_ = f32[1024,128]{1,0:T(8,128)S(1)} custom-call(f32[1024,128]{1,0:T(8,128)S(1)} %get-tuple-element.63.gc_ref, f32[16,8,128]{2,1,0:T(8,128)S(1)} %get-tuple-element.64.state_ref, f32[16,16,128]{2,1,0:T(8,128)S(1)} %bitcast.13, f32[16,16,128]{2,1,0:T(8,128)S(1)} %get-tuple-element.54.refs_6_.lap_ref, f32[16,16,128]{2,1,0:T(8,128)S(1)} %bitcast.16), custom_call_target="tpu_custom_call" | custom-call | bytes 1024 | tf_op jit(solution)/shard_map/pallas_call | solution.py:318
  59.5 1.5 %collective-permute-done.15.refs_4_ = f32[16,8,128]{2,1,0:T(8,128)S(1)} collective-permute-done((f32[16,8,128]{2,1,0:T(8,128)S(1)}, f32[16,8,128]{2,1,0:T(8,128)S(1)}, u32[]{:S(2)}, u32[]{:S(2)}) %collective-permute-start.15) | collective-permute-done | bytes 65568 | tf_op jit(solution)/shard_map/ppermute | solution.py:551
  61.0 3.1 %shard_map.98 = bf16[256,1024]{1,0:T(8,128)(2,1)} custom-call(s32[1]{0:T(128)} %bitcast.5.group_ref, f32[1024,128]{1,0:T(8,128)S(1)} %get-tuple-element.59.refs_0_, f32[1024,128]{1,0:T(8,128)S(1)} %shard_map.97.refs_1_, f32[16,8,128]{2,1,0:T(8,128)S(1)} %get-tuple-element.65.refs_2_, f32[16,8,128]{2,1,0:T(8,128)S(1)} %collective-permute-done.14.arrived_ref.refs_3_, ...), custom_call_target="tpu_custom_call" | custom-call | bytes 1024 | tf_op jit(solution)/shard_map/pallas_call | solution.py:434
  (6 shorter events, 0.2 us)
Async XLA Ops:
  0.6 6.2 %copy-start = (bf16[8192,1024]{1,0:T(8,128)(2,1)S(1)}, bf16[8192,1024]{1,0:T(8,128)(2,1)}, u32[]{:S(2)}) copy-start(bf16[8192,1024]{1,0:T(8,128)(2,1)} %w_ref.29) | copy-start | bytes 50331652
  3.0 10.7 %collective-permute-start = (bf16[528,256]{1,0:T(8,128)(2,1)S(1)}, bf16[528,256]{1,0:T(8,128)(2,1)S(1)}, u32[]{:S(2)}, u32[]{:S(2)}) collective-permute-start(bf16[528,256]{1,0:T(8,128)(2,1)S(1)} %get-tuple-element.34), channel_id=1, source_target_pairs={{0,1},{1,0},{2,3},{3,2},{4,5},{5,4},{6,7},{7,6},{8,9},{9,8},{10,11... | collective-permute-start | bytes 811016 | tf_op jit(solution)/shard_map/ppermute | solution.py:514
  8.8 10.3 %collective-permute-start.1 = (bf16[528,256]{1,0:T(8,128)(2,1)S(1)}, bf16[528,256]{1,0:T(8,128)(2,1)S(1)}, u32[]{:S(2)}, u32[]{:S(2)}) collective-permute-start(bf16[528,256]{1,0:T(8,128)(2,1)S(1)} %shard_map.80), channel_id=1, source_target_pairs={{0,1},{1,0},{2,3},{3,2},{4,5},{5,4},{6,7},{7,6},{8,9},{9,8},{10,11... | collective-permute-start | bytes 811016 | tf_op jit(solution)/shard_map/ppermute | solution.py:514
  11.8 13.1 %collective-permute-start.2 = (bf16[528,256]{1,0:T(8,128)(2,1)S(1)}, bf16[528,256]{1,0:T(8,128)(2,1)S(1)}, u32[]{:S(2)}, u32[]{:S(2)}) collective-permute-start(bf16[528,256]{1,0:T(8,128)(2,1)S(1)} %shard_map.79), channel_id=1, source_target_pairs={{0,1},{1,0},{2,3},{3,2},{4,5},{5,4},{6,7},{7,6},{8,9},{9,8},{10,11... | collective-permute-start | bytes 811016 | tf_op jit(solution)/shard_map/ppermute | solution.py:514
  14.6 10.4 %collective-permute-start.3 = (bf16[528,256]{1,0:T(8,128)(2,1)S(1)}, bf16[528,256]{1,0:T(8,128)(2,1)S(1)}, u32[]{:S(2)}, u32[]{:S(2)}) collective-permute-start(bf16[528,256]{1,0:T(8,128)(2,1)S(1)} %shard_map.84), channel_id=1, source_target_pairs={{0,2},{1,3},{2,0},{3,1},{4,6},{5,7},{6,4},{7,5},{8,10},{9,11},{10,... | collective-permute-start | bytes 811016 | tf_op jit(solution)/shard_map/ppermute | solution.py:514
  16.6 14.6 %collective-permute-start.4 = (bf16[528,256]{1,0:T(8,128)(2,1)S(1)}, bf16[528,256]{1,0:T(8,128)(2,1)S(1)}, u32[]{:S(2)}, u32[]{:S(2)}) collective-permute-start(bf16[528,256]{1,0:T(8,128)(2,1)S(1)} %shard_map.83), channel_id=1, source_target_pairs={{0,1},{1,0},{2,3},{3,2},{4,5},{5,4},{6,7},{7,6},{8,9},{9,8},{10,11... | collective-permute-start | bytes 811016 | tf_op jit(solution)/shard_map/ppermute | solution.py:514
  19.9 13.8 %collective-permute-start.5 = (bf16[528,256]{1,0:T(8,128)(2,1)S(1)}, bf16[528,256]{1,0:T(8,128)(2,1)S(1)}, u32[]{:S(2)}, u32[]{:S(2)}) collective-permute-start(bf16[528,256]{1,0:T(8,128)(2,1)S(1)} %shard_map.85), channel_id=1, source_target_pairs={{0,2},{1,3},{2,0},{3,1},{4,6},{5,7},{6,4},{7,5},{8,10},{9,11},{10,... | collective-permute-start | bytes 811016 | tf_op jit(solution)/shard_map/ppermute | solution.py:514
  22.1 14.4 %collective-permute-start.6 = (bf16[528,256]{1,0:T(8,128)(2,1)S(1)}, bf16[528,256]{1,0:T(8,128)(2,1)S(1)}, u32[]{:S(2)}, u32[]{:S(2)}) collective-permute-start(bf16[528,256]{1,0:T(8,128)(2,1)S(1)} %shard_map.82), channel_id=1, source_target_pairs={{0,1},{1,0},{2,3},{3,2},{4,5},{5,4},{6,7},{7,6},{8,9},{9,8},{10,11... | collective-permute-start | bytes 811016 | tf_op jit(solution)/shard_map/ppermute | solution.py:514
  25.8 13.9 %collective-permute-start.7 = (bf16[528,256]{1,0:T(8,128)(2,1)S(1)}, bf16[528,256]{1,0:T(8,128)(2,1)S(1)}, u32[]{:S(2)}, u32[]{:S(2)}) collective-permute-start(bf16[528,256]{1,0:T(8,128)(2,1)S(1)} %shard_map.86), channel_id=1, source_target_pairs={{0,4},{1,5},{2,6},{3,7},{4,0},{5,1},{6,2},{7,3},{8,12},{9,13},{10,... | collective-permute-start | bytes 811016 | tf_op jit(solution)/shard_map/ppermute | solution.py:514
  29.0 13.3 %collective-permute-start.8 = (bf16[528,256]{1,0:T(8,128)(2,1)S(1)}, bf16[528,256]{1,0:T(8,128)(2,1)S(1)}, u32[]{:S(2)}, u32[]{:S(2)}) collective-permute-start(bf16[528,256]{1,0:T(8,128)(2,1)S(1)} %shard_map.81), channel_id=1, source_target_pairs={{0,1},{1,0},{2,3},{3,2},{4,5},{5,4},{6,7},{7,6},{8,9},{9,8},{10,11... | collective-permute-start | bytes 811016 | tf_op jit(solution)/shard_map/ppermute | solution.py:514
  32.0 13.3 %copy-start.3 = (f32[1024,16]{0,1:T(8,128)S(1)}, f32[1024,16]{0,1:T(8,128)}, u32[]{:S(2)}) copy-start(f32[1024,16]{0,1:T(8,128)} %param.10) | copy-start | bytes 196612
  32.0 13.3 %copy-start.4 = (f32[1024,16]{0,1:T(8,128)S(1)}, f32[1024,16]{0,1:T(8,128)}, u32[]{:S(2)}) copy-start(f32[1024,16]{0,1:T(8,128)} %param.11) | copy-start | bytes 196612
  32.0 13.4 %collective-permute-start.9 = (bf16[528,256]{1,0:T(8,128)(2,1)S(1)}, bf16[528,256]{1,0:T(8,128)(2,1)S(1)}, u32[]{:S(2)}, u32[]{:S(2)}) collective-permute-start(bf16[528,256]{1,0:T(8,128)(2,1)S(1)} %shard_map.88), channel_id=1, source_target_pairs={{0,2},{1,3},{2,0},{3,1},{4,6},{5,7},{6,4},{7,5},{8,10},{9,11},{10,... | collective-permute-start | bytes 811016 | tf_op jit(solution)/shard_map/ppermute | solution.py:514
  33.7 14.4 %collective-permute-start.10 = (bf16[528,256]{1,0:T(8,128)(2,1)S(1)}, bf16[528,256]{1,0:T(8,128)(2,1)S(1)}, u32[]{:S(2)}, u32[]{:S(2)}) collective-permute-start(bf16[528,256]{1,0:T(8,128)(2,1)S(1)} %shard_map.87), channel_id=1, source_target_pairs={{0,1},{1,0},{2,3},{3,2},{4,5},{5,4},{6,7},{7,6},{8,9},{9,8},{10,11... | collective-permute-start | bytes 811016 | tf_op jit(solution)/shard_map/ppermute | solution.py:514
  36.5 16.6 %collective-permute-start.12 = (bf16[528,256]{1,0:T(8,128)(2,1)S(1)}, bf16[528,256]{1,0:T(8,128)(2,1)S(1)}, u32[]{:S(2)}, u32[]{:S(2)}) collective-permute-start(bf16[528,256]{1,0:T(8,128)(2,1)S(1)} %shard_map.78), channel_id=1, source_target_pairs={{0,1},{1,0},{2,3},{3,2},{4,5},{5,4},{6,7},{7,6},{8,9},{9,8},{10,11... | collective-permute-start | bytes 811016 | tf_op jit(solution)/shard_map/ppermute | solution.py:514
  39.7 13.3 %collective-permute-start.11 = (bf16[528,256]{1,0:T(8,128)(2,1)S(1)}, bf16[528,256]{1,0:T(8,128)(2,1)S(1)}, u32[]{:S(2)}, u32[]{:S(2)}) collective-permute-start(bf16[528,256]{1,0:T(8,128)(2,1)S(1)} %shard_map.89), channel_id=1, source_target_pairs={{0,4},{1,5},{2,6},{3,7},{4,0},{5,1},{6,2},{7,3},{8,12},{9,13},{10,... | collective-permute-start | bytes 811016 | tf_op jit(solution)/shard_map/ppermute | solution.py:514
  43.0 10.8 %collective-permute-start.13 = (bf16[528,256]{1,0:T(8,128)(2,1)S(1)}, bf16[528,256]{1,0:T(8,128)(2,1)S(1)}, u32[]{:S(2)}, u32[]{:S(2)}) collective-permute-start(bf16[528,256]{1,0:T(8,128)(2,1)S(1)} %shard_map.90), channel_id=1, source_target_pairs={{0,2},{1,3},{2,0},{3,1},{4,6},{5,7},{6,4},{7,5},{8,10},{9,11},{10,... | collective-permute-start | bytes 811016 | tf_op jit(solution)/shard_map/ppermute | solution.py:514
  48.1 1.0 %copy-start.1 = (bf16[256,1024]{1,0:T(8,128)(2,1)S(1)}, bf16[256,1024]{1,0:T(8,128)(2,1)}, u32[]{:S(2)}) copy-start(bf16[256,1024]{1,0:T(8,128)(2,1)} %refs_3_.3) | copy-start | bytes 1572868
  48.1 1.2 %copy-start.2 = (bf16[256,1024]{1,0:T(8,128)(2,1)S(1)}, bf16[256,1024]{1,0:T(8,128)(2,1)}, u32[]{:S(2)}) copy-start(bf16[256,1024]{1,0:T(8,128)(2,1)} %refs_4_.3) | copy-start | bytes 1572868
  55.3 1.3 %collective-permute-start.14 = (f32[16,8,128]{2,1,0:T(8,128)S(1)}, f32[16,8,128]{2,1,0:T(8,128)S(1)}, u32[]{:S(2)}, u32[]{:S(2)}) collective-permute-start(f32[16,8,128]{2,1,0:T(8,128)S(1)} %get-tuple-element.61.state_ref), channel_id=1, source_target_pairs={{0,8},{8,0},{16,24},{24,16},{1,9},{9,1},{17,25},{25,17},{2,10},{10... | collective-permute-start | bytes 196616 | tf_op jit(solution)/shard_map/ppermute | solution.py:551
  56.7 4.3 %collective-permute-start.15 = (f32[16,8,128]{2,1,0:T(8,128)S(1)}, f32[16,8,128]{2,1,0:T(8,128)S(1)}, u32[]{:S(2)}, u32[]{:S(2)}) collective-permute-start(f32[16,8,128]{2,1,0:T(8,128)S(1)} %shard_map.96), channel_id=1, source_target_pairs={{0,16},{8,24},{16,0},{24,8},{1,17},{9,25},{17,1},{25,9},{2,18},{10... | collective-permute-start | bytes 196616 | tf_op jit(solution)/shard_map/ppermute | solution.py:551

commit v11 on v10

--- a/solution.py
+++ b/solution.py
@@ -13,6 +13,7 @@
 SHIFT = 125 * math.log(2.0)
 STEP = 256
 PIECE = 128
+GAP = 8
 VMEM = 24 * 1024 * 1024
 QUICK = pl.CostEstimate(flops=0, bytes_accessed=1024, transcendentals=0)
 
@@ -218,14 +219,17 @@
         at = slice(line * lanes, (line + 1) * lanes)
         full = slice(half * rows + line * lanes, half * rows + (line + 1) * lanes)
         gq_ref[:, at] = (mix * conv_ref[:, full].astype(jnp.float32)).astype(jnp.bfloat16)
-        gc_ref[line * toks : (line + 1) * toks, :] = mix * query_ref[:, full].astype(jnp.float32)
+        gated = mix * query_ref[:, full].astype(jnp.float32)
+        for k in range(segments):
+            start = (line * segments + k) * (toks // segments + GAP)
+            gc_ref[start : start + toks // segments, :] = gated[k * (toks // segments) : (k + 1) * (toks // segments), :]
     store = pltpu.make_async_copy(gq_ref, out_hbm.at[:, pl.ds(half * rows, rows)], sem)
     store.start()
     decay = [decay_ref[n, mine] for n in range(modes)]
     span = toks // segments
 
     def step(t, state):
-        at = pl.ds(t, sublanes, stride=span)
+        at = pl.ds(t, sublanes, stride=span + GAP)
         row = gc_ref[at, :]
         state = tuple(decay[n] * state[n] + row for n in range(modes))
         if half == 0:
@@ -264,7 +268,7 @@
     vmem = pl.BlockSpec(memory_space=pltpu.VMEM)
     high = pl.BlockSpec(memory_space=pltpu.HBM)
     more = [] if partial is None else [partial]
-    lines = (rows // lanes * toks, lanes)
+    lines = (sublanes * (toks // segments + GAP), lanes)
     return pl.pallas_call(
         functools.partial(gate_kernel, half, rows, segments, pieces, len(nears)),
         in_specs=[vmem] * (6 + len(nears)) + [high] * len(more),
@@ -292,7 +296,7 @@
 def scan_kernel(half, segments, gc_ref, state_ref, decay_ref, lap_ref, residue_ref, rows_ref):
     modes, sublanes, lanes = state_ref.shape
     mine = slice(half * sublanes, (half + 1) * sublanes)
-    span = gc_ref.shape[0] // sublanes
+    span = gc_ref.shape[0] // sublanes - GAP
     segment = segment_of((sublanes, lanes), segments)
     decay = [decay_ref[n, mine] for n in range(modes)]
     start = []
@@ -304,7 +308,7 @@
         start.append(total)
 
     def step(t, state):
-        at = pl.ds(t, sublanes, stride=span)
+        at = pl.ds(t, sublanes, stride=span + GAP)
         row = gc_ref[at, :]
         state = tuple(decay[n] * state[n] + row for n in range(modes))
         rows_ref[at, :] = summed([residue_ref[n, mine] * state[n] for n in range(modes)])
@@ -412,16 +416,17 @@
                 start.append(residue_ref[n, mine] * total)
 
         def step(t, state, scanned_ref=scanned_refs[half], decay=decay):
-            at = pl.ds(t, sublanes, stride=span)
+            at = pl.ds(t, sublanes, stride=span + GAP)
             state = tuple(decay[n] * state[n] for n in range(modes))
             rows_ref[at, :] = scanned_ref[at, :] + summed(list(state))
             return state
 
         steps_back(span, step, tuple(start), 16)
         for line in range(rows // lanes):
-            out_ref[:, half * rows + line * lanes : half * rows + (line + 1) * lanes] = rows_ref[
-                line * toks : (line + 1) * toks, :
-            ].astype(jnp.bfloat16)
+            at = slice(half * rows + line * lanes, half * rows + (line + 1) * lanes)
+            for k in range(segments):
+                start = (line * segments + k) * (span + GAP)
+                out_ref[k * span : (k + 1) * span, at] = rows_ref[start : start + span, :].astype(jnp.bfloat16)
         columns = pl.ds(half * rows, rows)
         stores.append(pltpu.make_async_copy(out_ref.at[:, columns], out_hbm.at[:, columns], sems.at[half]))
         stores[-1].start()

time: 64.6 us -> 63.6 us (0.985)
  Pallas kernels: 21.3 us -> 19.1 us
  waiting for transfers between devices: 11.6 us -> 12.8 us
    pallas_call x1, Pallas kernels: 3.09 us -> 2.22 us  [fix(): pl.pallas_call(functools.partial(fix_kernel, segments, len(arrived)), in_...]
    pallas_call x2, Pallas kernels: 3.9 us -> 3.22 us  [gate(): pl.pallas_call(functools.partial(gate_kernel, half, rows, segments, piece...]
  transfers between devices with their start and end apart: 16 -> 16, of which waited for: 11 -> 11; matrix products, arithmetic and copies ran while one was open for 0% -> 0% of each run, Pallas kernels for 22% -> 21%
where the time goes in v11:
time: 63.6 us; the launch traced here: 63.1 us
  starting transfers between devices  29.1 us (46%)
  Pallas kernels  19.1 us (30%)
  waiting for transfers between devices  12.8 us (20%)
  local copies, waits for them, and re-layouts  1.19 us (2%)
  between operations  0.9 us (1%)
    ppermute x14, starting transfers between devices, local(): arrived = lax.ppermute(last, 'ch', [(i, i ^ bit) for i in range(size)])  28 us
    pallas_call x15, Pallas kernels, send(): pl.pallas_call(functools.partial(send_kernel, items, coded, width, len(ne...  10.1 us
    ppermute x14, waiting for transfers between devices, local(): arrived = lax.ppermute(last, 'ch', [(i, i ^ bit) for i in range(size)])  9.41 us
    ppermute x2, waiting for transfers between devices, local(): lax.ppermute(array, 'ctx', [(i, i ^ 1 << round_) for i in range(groups)])  3.36 us
    pallas_call x2, Pallas kernels, gate(): pl.pallas_call(functools.partial(gate_kernel, half, rows, segments, piece...  3.22 us
    pallas_call x1, Pallas kernels, first_send(): pl.pallas_call(functools.partial(first_kernel, items, width), in_specs=[p...  2.39 us
    pallas_call x1, Pallas kernels, fix(): pl.pallas_call(functools.partial(fix_kernel, segments, len(arrived)), in_...  2.22 us
  transfers between devices with their start and end apart: 16, of which 11 were waited for; matrix products, arithmetic and copies ran while one was open for 0% of the time, Pallas kernels for 21%

profile of v11, /device:TPU:0, one launch (start us, length us, event | category | flops | bytes accessed | tf_op | source)
XLA Modules:
  0.0 63.1 jit_solution(10794075615237724377)
XLA Ops:
  0.6 0.0 copy-start
  0.6 2.4 %shard_map.77 = (bf16[528,256]{1,0:T(8,128)(2,1)S(1)}, bf16[1024,256]{1,0:T(8,128)(2,1)S(1)}) custom-call(s32[1]{0:T(128)} %bitcast.place_ref, bf16[8192,1024]{1,0:T(8,128)(2,1)} %w_ref.29, bf16[256,1024]{1,0:T(8,128)(2,1)} %g_hbm.1), custom_call_target="tpu_custom_call" | custom-call | bytes 1024 | tf_op jit(solution)/shard_map/pallas_call | solution.py:156
  3.0 3.0 %collective-permute-start = (bf16[528,256]{1,0:T(8,128)(2,1)S(1)}, bf16[528,256]{1,0:T(8,128)(2,1)S(1)}, u32[]{:S(2)}, u32[]{:S(2)}) collective-permute-start(bf16[528,256]{1,0:T(8,128)(2,1)S(1)} %get-tuple-element.34), channel_id=1, source_target_pairs={{0,1},{1,0},{2,3},{3,2},{4,5},{5,4},{6,7},{7,6},{8,9},{9,8},{10,11... | collective-permute-start | bytes 811016 | tf_op jit(solution)/shard_map/ppermute | solution.py:519
  6.1 0.8 %copy-done = bf16[8192,1024]{1,0:T(8,128)(2,1)S(1)} copy-done((bf16[8192,1024]{1,0:T(8,128)(2,1)S(1)}, bf16[8192,1024]{1,0:T(8,128)(2,1)}, u32[]{:S(2)}) %copy-start) | copy-done | bytes 16777240
  6.9 0.6 shard_map.78
  7.5 0.6 shard_map.79
  8.1 0.6 shard_map.80
  8.8 3.0 %collective-permute-start.1 = (bf16[528,256]{1,0:T(8,128)(2,1)S(1)}, bf16[528,256]{1,0:T(8,128)(2,1)S(1)}, u32[]{:S(2)}, u32[]{:S(2)}) collective-permute-start(bf16[528,256]{1,0:T(8,128)(2,1)S(1)} %shard_map.80), channel_id=1, source_target_pairs={{0,1},{1,0},{2,3},{3,2},{4,5},{5,4},{6,7},{7,6},{8,9},{9,8},{10,11... | collective-permute-start | bytes 811016 | tf_op jit(solution)/shard_map/ppermute | solution.py:519
  11.8 0.1 collective-permute-start.2
  11.9 0.6 shard_map.81
  12.5 0.6 shard_map.82
  13.2 0.6 shard_map.83
  13.8 0.0 collective-permute-done.refs_0_
  13.8 0.7 %shard_map.84 = bf16[528,256]{1,0:T(8,128)(2,1)S(1)} custom-call(s32[1]{0:T(128)} %bitcast.place_ref, bf16[8192,1024]{1,0:T(8,128)(2,1)S(1)} %copy-done, bf16[1024,256]{1,0:T(8,128)(2,1)S(1)} %get-tuple-element.36.turned_ref, bf16[528,256]{1,0:T(8,128)(2,1)S(1)} %collective-permute-done.refs_0_), custom_call_target="tpu_custom_call" | custom-call | bytes 1024 | tf_op jit(solution)/shard_map/pallas_call | solution.py:104
  14.6 2.1 %collective-permute-start.3 = (bf16[528,256]{1,0:T(8,128)(2,1)S(1)}, bf16[528,256]{1,0:T(8,128)(2,1)S(1)}, u32[]{:S(2)}, u32[]{:S(2)}) collective-permute-start(bf16[528,256]{1,0:T(8,128)(2,1)S(1)} %shard_map.84), channel_id=1, source_target_pairs={{0,2},{1,3},{2,0},{3,1},{4,6},{5,7},{6,4},{7,5},{8,10},{9,11},{10,... | collective-permute-start | bytes 811016 | tf_op jit(solution)/shard_map/ppermute | solution.py:519
  16.6 1.5 %collective-permute-start.4 = (bf16[528,256]{1,0:T(8,128)(2,1)S(1)}, bf16[528,256]{1,0:T(8,128)(2,1)S(1)}, u32[]{:S(2)}, u32[]{:S(2)}) collective-permute-start(bf16[528,256]{1,0:T(8,128)(2,1)S(1)} %shard_map.83), channel_id=1, source_target_pairs={{0,1},{1,0},{2,3},{3,2},{4,5},{5,4},{6,7},{7,6},{8,9},{9,8},{10,11... | collective-permute-start | bytes 811016 | tf_op jit(solution)/shard_map/ppermute | solution.py:519
  18.1 1.0 %collective-permute-done.1.refs_0_ = bf16[528,256]{1,0:T(8,128)(2,1)S(1)} collective-permute-done((bf16[528,256]{1,0:T(8,128)(2,1)S(1)}, bf16[528,256]{1,0:T(8,128)(2,1)S(1)}, u32[]{:S(2)}, u32[]{:S(2)}) %collective-permute-start.1) | collective-permute-done | bytes 270368 | tf_op jit(solution)/shard_map/ppermute | solution.py:519
  19.1 0.7 %shard_map.85 = bf16[528,256]{1,0:T(8,128)(2,1)S(1)} custom-call(s32[1]{0:T(128)} %bitcast.place_ref, bf16[8192,1024]{1,0:T(8,128)(2,1)S(1)} %copy-done, bf16[1024,256]{1,0:T(8,128)(2,1)S(1)} %get-tuple-element.36.turned_ref, bf16[528,256]{1,0:T(8,128)(2,1)S(1)} %collective-permute-done.1.refs_0_), custom_call_target="tpu_custom_call" | custom-call | bytes 1024 | tf_op jit(solution)/shard_map/pallas_call | solution.py:104
  19.9 2.2 %collective-permute-start.5 = (bf16[528,256]{1,0:T(8,128)(2,1)S(1)}, bf16[528,256]{1,0:T(8,128)(2,1)S(1)}, u32[]{:S(2)}, u32[]{:S(2)}) collective-permute-start(bf16[528,256]{1,0:T(8,128)(2,1)S(1)} %shard_map.85), channel_id=1, source_target_pairs={{0,2},{1,3},{2,0},{3,1},{4,6},{5,7},{6,4},{7,5},{8,10},{9,11},{10,... | collective-permute-start | bytes 811016 | tf_op jit(solution)/shard_map/ppermute | solution.py:519
  22.1 1.5 %collective-permute-start.6 = (bf16[528,256]{1,0:T(8,128)(2,1)S(1)}, bf16[528,256]{1,0:T(8,128)(2,1)S(1)}, u32[]{:S(2)}, u32[]{:S(2)}) collective-permute-start(bf16[528,256]{1,0:T(8,128)(2,1)S(1)} %shard_map.82), channel_id=1, source_target_pairs={{0,1},{1,0},{2,3},{3,2},{4,5},{5,4},{6,7},{7,6},{8,9},{9,8},{10,11... | collective-permute-start | bytes 811016 | tf_op jit(solution)/shard_map/ppermute | solution.py:519
  23.6 1.3 %collective-permute-done.2.refs_0_ = bf16[528,256]{1,0:T(8,128)(2,1)S(1)} collective-permute-done((bf16[528,256]{1,0:T(8,128)(2,1)S(1)}, bf16[528,256]{1,0:T(8,128)(2,1)S(1)}, u32[]{:S(2)}, u32[]{:S(2)}) %collective-permute-start.2) | collective-permute-done | bytes 270368 | tf_op jit(solution)/shard_map/ppermute | solution.py:519
  24.9 0.0 collective-permute-done.3.refs_1_
  24.9 0.9 %shard_map.86 = bf16[528,256]{1,0:T(8,128)(2,1)S(1)} custom-call(s32[1]{0:T(128)} %bitcast.place_ref, bf16[8192,1024]{1,0:T(8,128)(2,1)S(1)} %copy-done, bf16[1024,256]{1,0:T(8,128)(2,1)S(1)} %get-tuple-element.36.turned_ref, bf16[528,256]{1,0:T(8,128)(2,1)S(1)} %collective-permute-done.2.refs_0_, bf16[528,256]{1,0:T(8,128)(2,1)S(1)} %collective-permute-done.3.refs_1_), custom_call_target="tpu_custom_call" | custom-call | bytes 1024 | tf_op jit(solution)/shard_map/pallas_call | solution.py:104
  25.8 3.2 %collective-permute-start.7 = (bf16[528,256]{1,0:T(8,128)(2,1)S(1)}, bf16[528,256]{1,0:T(8,128)(2,1)S(1)}, u32[]{:S(2)}, u32[]{:S(2)}) collective-permute-start(bf16[528,256]{1,0:T(8,128)(2,1)S(1)} %shard_map.86), channel_id=1, source_target_pairs={{0,4},{1,5},{2,6},{3,7},{4,0},{5,1},{6,2},{7,3},{8,12},{9,13},{10,... | collective-permute-start | bytes 811016 | tf_op jit(solution)/shard_map/ppermute | solution.py:519
  29.0 1.5 %collective-permute-start.8 = (bf16[528,256]{1,0:T(8,128)(2,1)S(1)}, bf16[528,256]{1,0:T(8,128)(2,1)S(1)}, u32[]{:S(2)}, u32[]{:S(2)}) collective-permute-start(bf16[528,256]{1,0:T(8,128)(2,1)S(1)} %shard_map.81), channel_id=1, source_target_pairs={{0,1},{1,0},{2,3},{3,2},{4,5},{5,4},{6,7},{7,6},{8,9},{9,8},{10,11... | collective-permute-start | bytes 811016 | tf_op jit(solution)/shard_map/ppermute | solution.py:519
  30.6 0.6 shard_map.87
  31.2 0.0 collective-permute-done.4.refs_0_
  31.2 0.7 %shard_map.88 = bf16[528,256]{1,0:T(8,128)(2,1)S(1)} custom-call(s32[1]{0:T(128)} %bitcast.place_ref, bf16[8192,1024]{1,0:T(8,128)(2,1)S(1)} %copy-done, bf16[1024,256]{1,0:T(8,128)(2,1)S(1)} %get-tuple-element.36.turned_ref, bf16[528,256]{1,0:T(8,128)(2,1)S(1)} %collective-permute-done.4.refs_0_), custom_call_target="tpu_custom_call" | custom-call | bytes 1024 | tf_op jit(solution)/shard_map/pallas_call | solution.py:104
  32.0 0.0 copy-start.3
  32.0 0.0 copy-start.4
  32.0 1.7 %collective-permute-start.9 = (bf16[528,256]{1,0:T(8,128)(2,1)S(1)}, bf16[528,256]{1,0:T(8,128)(2,1)S(1)}, u32[]{:S(2)}, u32[]{:S(2)}) collective-permute-start(bf16[528,256]{1,0:T(8,128)(2,1)S(1)} %shard_map.88), channel_id=1, source_target_pairs={{0,2},{1,3},{2,0},{3,1},{4,6},{5,7},{6,4},{7,5},{8,10},{9,11},{10,... | collective-permute-start | bytes 811016 | tf_op jit(solution)/shard_map/ppermute | solution.py:519
  33.7 0.0 collective-permute-done.5.refs_1_
  33.7 1.5 %collective-permute-start.10 = (bf16[528,256]{1,0:T(8,128)(2,1)S(1)}, bf16[528,256]{1,0:T(8,128)(2,1)S(1)}, u32[]{:S(2)}, u32[]{:S(2)}) collective-permute-start(bf16[528,256]{1,0:T(8,128)(2,1)S(1)} %shard_map.87), channel_id=1, source_target_pairs={{0,1},{1,0},{2,3},{3,2},{4,5},{5,4},{6,7},{7,6},{8,9},{9,8},{10,11... | collective-permute-start | bytes 811016 | tf_op jit(solution)/shard_map/ppermute | solution.py:519
  35.2 1.3 %collective-permute-done.6.refs_0_ = bf16[528,256]{1,0:T(8,128)(2,1)S(1)} collective-permute-done((bf16[528,256]{1,0:T(8,128)(2,1)S(1)}, bf16[528,256]{1,0:T(8,128)(2,1)S(1)}, u32[]{:S(2)}, u32[]{:S(2)}) %collective-permute-start.6) | collective-permute-done | bytes 270368 | tf_op jit(solution)/shard_map/ppermute | solution.py:519
  36.5 2.1 %collective-permute-start.12 = (bf16[528,256]{1,0:T(8,128)(2,1)S(1)}, bf16[528,256]{1,0:T(8,128)(2,1)S(1)}, u32[]{:S(2)}, u32[]{:S(2)}) collective-permute-start(bf16[528,256]{1,0:T(8,128)(2,1)S(1)} %shard_map.78), channel_id=1, source_target_pairs={{0,1},{1,0},{2,3},{3,2},{4,5},{5,4},{6,7},{7,6},{8,9},{9,8},{10,11... | collective-permute-start | bytes 811016 | tf_op jit(solution)/shard_map/ppermute | solution.py:519
  38.6 0.9 %shard_map.89 = bf16[528,256]{1,0:T(8,128)(2,1)S(1)} custom-call(s32[1]{0:T(128)} %bitcast.place_ref, bf16[8192,1024]{1,0:T(8,128)(2,1)S(1)} %copy-done, bf16[1024,256]{1,0:T(8,128)(2,1)S(1)} %get-tuple-element.36.turned_ref, bf16[528,256]{1,0:T(8,128)(2,1)S(1)} %collective-permute-done.6.refs_0_, bf16[528,256]{1,0:T(8,128)(2,1)S(1)} %collective-permute-done.5.refs_1_), custom_call_target="tpu_custom_call" | custom-call | bytes 1024 | tf_op jit(solution)/shard_map/pallas_call | solution.py:104
  39.5 0.2 collective-permute-done.7.refs_2_
  39.7 2.4 %collective-permute-start.11 = (bf16[528,256]{1,0:T(8,128)(2,1)S(1)}, bf16[528,256]{1,0:T(8,128)(2,1)S(1)}, u32[]{:S(2)}, u32[]{:S(2)}) collective-permute-start(bf16[528,256]{1,0:T(8,128)(2,1)S(1)} %shard_map.89), channel_id=1, source_target_pairs={{0,4},{1,5},{2,6},{3,7},{4,0},{5,1},{6,2},{7,3},{8,12},{9,13},{10,... | collective-permute-start | bytes 811016 | tf_op jit(solution)/shard_map/ppermute | solution.py:519
  42.2 0.1 collective-permute-done.8.refs_0_
  42.3 0.7 %shard_map.90 = bf16[528,256]{1,0:T(8,128)(2,1)S(1)} custom-call(s32[1]{0:T(128)} %bitcast.place_ref, bf16[8192,1024]{1,0:T(8,128)(2,1)S(1)} %copy-done, bf16[1024,256]{1,0:T(8,128)(2,1)S(1)} %get-tuple-element.36.turned_ref, bf16[528,256]{1,0:T(8,128)(2,1)S(1)} %collective-permute-done.8.refs_0_), custom_call_target="tpu_custom_call" | custom-call | bytes 1024 | tf_op jit(solution)/shard_map/pallas_call | solution.py:104
  43.0 2.2 %collective-permute-start.13 = (bf16[528,256]{1,0:T(8,128)(2,1)S(1)}, bf16[528,256]{1,0:T(8,128)(2,1)S(1)}, u32[]{:S(2)}, u32[]{:S(2)}) collective-permute-start(bf16[528,256]{1,0:T(8,128)(2,1)S(1)} %shard_map.90), channel_id=1, source_target_pairs={{0,2},{1,3},{2,0},{3,1},{4,6},{5,7},{6,4},{7,5},{8,10},{9,11},{10,... | collective-permute-start | bytes 811016 | tf_op jit(solution)/shard_map/ppermute | solution.py:519
  45.2 0.0 copy-done.3
  45.2 0.0 copy-done.4
  45.4 0.0 collective-permute-done.9.refs_1_
  45.4 2.7 %collective-permute-done.10.refs_0_ = bf16[528,256]{1,0:T(8,128)(2,1)S(1)} collective-permute-done((bf16[528,256]{1,0:T(8,128)(2,1)S(1)}, bf16[528,256]{1,0:T(8,128)(2,1)S(1)}, u32[]{:S(2)}, u32[]{:S(2)}) %collective-permute-start.10) | collective-permute-done | bytes 270368 | tf_op jit(solution)/shard_map/ppermute | solution.py:519
  48.1 0.0 copy-start.1
  48.1 0.0 copy-start.2
  48.1 0.4 shard_map.92.acc_ref
  48.5 0.4 shard_map.93.acc_ref
  49.0 0.1 copy-done.1
  49.1 0.2 copy-done.2
  49.3 1.9 %shard_map.94 = (bf16[256,1024]{1,0:T(8,128)(2,1)}, f32[1088,128]{1,0:T(8,128)S(1)}, f32[16,8,128]{2,1,0:T(8,128)S(1)}, f32[8,8,128]{2,1,0:T(8,128)S(1)}) custom-call(f32[512,256]{1,0:T(8,128)S(1)} %shard_map.92.acc_ref, bf16[528,256]{1,0:T(8,128)(2,1)S(1)} %collective-permute-done.10.refs_0_, bf16[528,256]{1,0:T(8,128)(2,1)S(1)} %collective-permute-done.9.refs_1_, ...), custom_call_target="tpu_custom_call" | custom-call | bytes 1024 | tf_op jit(solution)/shard_map/pallas_call | solution.py:272
  51.2 1.8 %collective-permute-done.11.refs_2_ = bf16[528,256]{1,0:T(8,128)(2,1)S(1)} collective-permute-done((bf16[528,256]{1,0:T(8,128)(2,1)S(1)}, bf16[528,256]{1,0:T(8,128)(2,1)S(1)}, u32[]{:S(2)}, u32[]{:S(2)}) %collective-permute-start.11) | collective-permute-done | bytes 270368 | tf_op jit(solution)/shard_map/ppermute | solution.py:519
  53.0 0.1 collective-permute-done.12.refs_0_
  53.1 0.8 %collective-permute-done.13.refs_1_ = bf16[528,256]{1,0:T(8,128)(2,1)S(1)} collective-permute-done((bf16[528,256]{1,0:T(8,128)(2,1)S(1)}, bf16[528,256]{1,0:T(8,128)(2,1)S(1)}, u32[]{:S(2)}, u32[]{:S(2)}) %collective-permute-start.13) | collective-permute-done | bytes 270368 | tf_op jit(solution)/shard_map/ppermute | solution.py:519
  53.9 1.4 %shard_map.95 = (bf16[256,1024]{1,0:T(8,128)(2,1)}, f32[1088,128]{1,0:T(8,128)S(1)}, f32[16,8,128]{2,1,0:T(8,128)S(1)}, f32[16,8,128]{2,1,0:T(8,128)S(1)}) custom-call(f32[512,256]{1,0:T(8,128)S(1)} %shard_map.93.acc_ref, bf16[528,256]{1,0:T(8,128)(2,1)S(1)} %collective-permute-done.12.refs_0_, ...), custom_call_target="tpu_custom_call", output_to_operand_aliasing={{0}: (9, {})} | custom-call | bytes 1024 | tf_op jit(solution)/shard_map/pallas_call | solution.py:272
  55.2 0.1 collective-permute-start.14
  55.3 1.2 %collective-permute-done.14.arrived_ref.refs_3_ = f32[16,8,128]{2,1,0:T(8,128)S(1)} collective-permute-done((f32[16,8,128]{2,1,0:T(8,128)S(1)}, f32[16,8,128]{2,1,0:T(8,128)S(1)}, u32[]{:S(2)}, u32[]{:S(2)}) %collective-permute-start.14) | collective-permute-done | bytes 65568 | tf_op jit(solution)/shard_map/ppermute | solution.py:556
  56.6 1.0 %collective-permute-start.15 = (f32[16,8,128]{2,1,0:T(8,128)S(1)}, f32[16,8,128]{2,1,0:T(8,128)S(1)}, u32[]{:S(2)}, u32[]{:S(2)}) collective-permute-start(f32[16,8,128]{2,1,0:T(8,128)S(1)} %shard_map.96), channel_id=1, source_target_pairs={{0,16},{8,24},{16,0},{24,8},{1,17},{9,25},{17,1},{25,9},{2,18},{10... | collective-permute-start | bytes 196616 | tf_op jit(solution)/shard_map/ppermute | solution.py:556
  57.6 1.2 %shard_map.97.refs_1_ = f32[1088,128]{1,0:T(8,128)S(1)} custom-call(f32[1088,128]{1,0:T(8,128)S(1)} %get-tuple-element.63.gc_ref, f32[16,8,128]{2,1,0:T(8,128)S(1)} %get-tuple-element.64.state_ref, f32[16,16,128]{2,1,0:T(8,128)S(1)} %bitcast.13, f32[16,16,128]{2,1,0:T(8,128)S(1)} %get-tuple-element.54.refs_6_.lap_ref, f32[16,16,128]{2,1,0:T(8,128)S(1)} %bitcast.16), custom_call_target="tpu_custom_call" | custom-call | bytes 1024 | tf_op jit(solution)/shard_map/pallas_call | solution.py:322
  58.8 2.1 %collective-permute-done.15.refs_4_ = f32[16,8,128]{2,1,0:T(8,128)S(1)} collective-permute-done((f32[16,8,128]{2,1,0:T(8,128)S(1)}, f32[16,8,128]{2,1,0:T(8,128)S(1)}, u32[]{:S(2)}, u32[]{:S(2)}) %collective-permute-start.15) | collective-permute-done | bytes 65568 | tf_op jit(solution)/shard_map/ppermute | solution.py:556
  60.9 2.2 %shard_map.98 = bf16[256,1024]{1,0:T(8,128)(2,1)} custom-call(s32[1]{0:T(128)} %bitcast.5.group_ref, f32[1088,128]{1,0:T(8,128)S(1)} %get-tuple-element.59.refs_0_, f32[1088,128]{1,0:T(8,128)S(1)} %shard_map.97.refs_1_, f32[16,8,128]{2,1,0:T(8,128)S(1)} %get-tuple-element.65.refs_2_, f32[16,8,128]{2,1,0:T(8,128)S(1)} %collective-permute-done.14.arrived_ref.refs_3_, ...), custom_call_target="tpu_custom_call" | custom-call | bytes 1024 | tf_op jit(solution)/shard_map/pallas_call | solution.py:439
  (6 shorter events, 0.2 us)
Async XLA Ops:
  0.6 6.2 %copy-start = (bf16[8192,1024]{1,0:T(8,128)(2,1)S(1)}, bf16[8192,1024]{1,0:T(8,128)(2,1)}, u32[]{:S(2)}) copy-start(bf16[8192,1024]{1,0:T(8,128)(2,1)} %w_ref.29) | copy-start | bytes 50331652
  3.0 10.7 %collective-permute-start = (bf16[528,256]{1,0:T(8,128)(2,1)S(1)}, bf16[528,256]{1,0:T(8,128)(2,1)S(1)}, u32[]{:S(2)}, u32[]{:S(2)}) collective-permute-start(bf16[528,256]{1,0:T(8,128)(2,1)S(1)} %get-tuple-element.34), channel_id=1, source_target_pairs={{0,1},{1,0},{2,3},{3,2},{4,5},{5,4},{6,7},{7,6},{8,9},{9,8},{10,11... | collective-permute-start | bytes 811016 | tf_op jit(solution)/shard_map/ppermute | solution.py:519
  8.8 10.3 %collective-permute-start.1 = (bf16[528,256]{1,0:T(8,128)(2,1)S(1)}, bf16[528,256]{1,0:T(8,128)(2,1)S(1)}, u32[]{:S(2)}, u32[]{:S(2)}) collective-permute-start(bf16[528,256]{1,0:T(8,128)(2,1)S(1)} %shard_map.80), channel_id=1, source_target_pairs={{0,1},{1,0},{2,3},{3,2},{4,5},{5,4},{6,7},{7,6},{8,9},{9,8},{10,11... | collective-permute-start | bytes 811016 | tf_op jit(solution)/shard_map/ppermute | solution.py:519
  11.8 13.1 %collective-permute-start.2 = (bf16[528,256]{1,0:T(8,128)(2,1)S(1)}, bf16[528,256]{1,0:T(8,128)(2,1)S(1)}, u32[]{:S(2)}, u32[]{:S(2)}) collective-permute-start(bf16[528,256]{1,0:T(8,128)(2,1)S(1)} %shard_map.79), channel_id=1, source_target_pairs={{0,1},{1,0},{2,3},{3,2},{4,5},{5,4},{6,7},{7,6},{8,9},{9,8},{10,11... | collective-permute-start | bytes 811016 | tf_op jit(solution)/shard_map/ppermute | solution.py:519
  14.6 10.4 %collective-permute-start.3 = (bf16[528,256]{1,0:T(8,128)(2,1)S(1)}, bf16[528,256]{1,0:T(8,128)(2,1)S(1)}, u32[]{:S(2)}, u32[]{:S(2)}) collective-permute-start(bf16[528,256]{1,0:T(8,128)(2,1)S(1)} %shard_map.84), channel_id=1, source_target_pairs={{0,2},{1,3},{2,0},{3,1},{4,6},{5,7},{6,4},{7,5},{8,10},{9,11},{10,... | collective-permute-start | bytes 811016 | tf_op jit(solution)/shard_map/ppermute | solution.py:519
  16.6 14.6 %collective-permute-start.4 = (bf16[528,256]{1,0:T(8,128)(2,1)S(1)}, bf16[528,256]{1,0:T(8,128)(2,1)S(1)}, u32[]{:S(2)}, u32[]{:S(2)}) collective-permute-start(bf16[528,256]{1,0:T(8,128)(2,1)S(1)} %shard_map.83), channel_id=1, source_target_pairs={{0,1},{1,0},{2,3},{3,2},{4,5},{5,4},{6,7},{7,6},{8,9},{9,8},{10,11... | collective-permute-start | bytes 811016 | tf_op jit(solution)/shard_map/ppermute | solution.py:519
  19.9 13.8 %collective-permute-start.5 = (bf16[528,256]{1,0:T(8,128)(2,1)S(1)}, bf16[528,256]{1,0:T(8,128)(2,1)S(1)}, u32[]{:S(2)}, u32[]{:S(2)}) collective-permute-start(bf16[528,256]{1,0:T(8,128)(2,1)S(1)} %shard_map.85), channel_id=1, source_target_pairs={{0,2},{1,3},{2,0},{3,1},{4,6},{5,7},{6,4},{7,5},{8,10},{9,11},{10,... | collective-permute-start | bytes 811016 | tf_op jit(solution)/shard_map/ppermute | solution.py:519
  22.1 14.4 %collective-permute-start.6 = (bf16[528,256]{1,0:T(8,128)(2,1)S(1)}, bf16[528,256]{1,0:T(8,128)(2,1)S(1)}, u32[]{:S(2)}, u32[]{:S(2)}) collective-permute-start(bf16[528,256]{1,0:T(8,128)(2,1)S(1)} %shard_map.82), channel_id=1, source_target_pairs={{0,1},{1,0},{2,3},{3,2},{4,5},{5,4},{6,7},{7,6},{8,9},{9,8},{10,11... | collective-permute-start | bytes 811016 | tf_op jit(solution)/shard_map/ppermute | solution.py:519
  25.8 13.9 %collective-permute-start.7 = (bf16[528,256]{1,0:T(8,128)(2,1)S(1)}, bf16[528,256]{1,0:T(8,128)(2,1)S(1)}, u32[]{:S(2)}, u32[]{:S(2)}) collective-permute-start(bf16[528,256]{1,0:T(8,128)(2,1)S(1)} %shard_map.86), channel_id=1, source_target_pairs={{0,4},{1,5},{2,6},{3,7},{4,0},{5,1},{6,2},{7,3},{8,12},{9,13},{10,... | collective-permute-start | bytes 811016 | tf_op jit(solution)/shard_map/ppermute | solution.py:519
  29.0 13.3 %collective-permute-start.8 = (bf16[528,256]{1,0:T(8,128)(2,1)S(1)}, bf16[528,256]{1,0:T(8,128)(2,1)S(1)}, u32[]{:S(2)}, u32[]{:S(2)}) collective-permute-start(bf16[528,256]{1,0:T(8,128)(2,1)S(1)} %shard_map.81), channel_id=1, source_target_pairs={{0,1},{1,0},{2,3},{3,2},{4,5},{5,4},{6,7},{7,6},{8,9},{9,8},{10,11... | collective-permute-start | bytes 811016 | tf_op jit(solution)/shard_map/ppermute | solution.py:519
  32.0 13.3 %copy-start.3 = (f32[1024,16]{0,1:T(8,128)S(1)}, f32[1024,16]{0,1:T(8,128)}, u32[]{:S(2)}) copy-start(f32[1024,16]{0,1:T(8,128)} %param.10) | copy-start | bytes 196612
  32.0 13.3 %copy-start.4 = (f32[1024,16]{0,1:T(8,128)S(1)}, f32[1024,16]{0,1:T(8,128)}, u32[]{:S(2)}) copy-start(f32[1024,16]{0,1:T(8,128)} %param.11) | copy-start | bytes 196612
  32.0 13.4 %collective-permute-start.9 = (bf16[528,256]{1,0:T(8,128)(2,1)S(1)}, bf16[528,256]{1,0:T(8,128)(2,1)S(1)}, u32[]{:S(2)}, u32[]{:S(2)}) collective-permute-start(bf16[528,256]{1,0:T(8,128)(2,1)S(1)} %shard_map.88), channel_id=1, source_target_pairs={{0,2},{1,3},{2,0},{3,1},{4,6},{5,7},{6,4},{7,5},{8,10},{9,11},{10,... | collective-permute-start | bytes 811016 | tf_op jit(solution)/shard_map/ppermute | solution.py:519
  33.7 14.4 %collective-permute-start.10 = (bf16[528,256]{1,0:T(8,128)(2,1)S(1)}, bf16[528,256]{1,0:T(8,128)(2,1)S(1)}, u32[]{:S(2)}, u32[]{:S(2)}) collective-permute-start(bf16[528,256]{1,0:T(8,128)(2,1)S(1)} %shard_map.87), channel_id=1, source_target_pairs={{0,1},{1,0},{2,3},{3,2},{4,5},{5,4},{6,7},{7,6},{8,9},{9,8},{10,11... | collective-permute-start | bytes 811016 | tf_op jit(solution)/shard_map/ppermute | solution.py:519
  36.5 16.6 %collective-permute-start.12 = (bf16[528,256]{1,0:T(8,128)(2,1)S(1)}, bf16[528,256]{1,0:T(8,128)(2,1)S(1)}, u32[]{:S(2)}, u32[]{:S(2)}) collective-permute-start(bf16[528,256]{1,0:T(8,128)(2,1)S(1)} %shard_map.78), channel_id=1, source_target_pairs={{0,1},{1,0},{2,3},{3,2},{4,5},{5,4},{6,7},{7,6},{8,9},{9,8},{10,11... | collective-permute-start | bytes 811016 | tf_op jit(solution)/shard_map/ppermute | solution.py:519
  39.7 13.3 %collective-permute-start.11 = (bf16[528,256]{1,0:T(8,128)(2,1)S(1)}, bf16[528,256]{1,0:T(8,128)(2,1)S(1)}, u32[]{:S(2)}, u32[]{:S(2)}) collective-permute-start(bf16[528,256]{1,0:T(8,128)(2,1)S(1)} %shard_map.89), channel_id=1, source_target_pairs={{0,4},{1,5},{2,6},{3,7},{4,0},{5,1},{6,2},{7,3},{8,12},{9,13},{10,... | collective-permute-start | bytes 811016 | tf_op jit(solution)/shard_map/ppermute | solution.py:519
  43.0 10.8 %collective-permute-start.13 = (bf16[528,256]{1,0:T(8,128)(2,1)S(1)}, bf16[528,256]{1,0:T(8,128)(2,1)S(1)}, u32[]{:S(2)}, u32[]{:S(2)}) collective-permute-start(bf16[528,256]{1,0:T(8,128)(2,1)S(1)} %shard_map.90), channel_id=1, source_target_pairs={{0,2},{1,3},{2,0},{3,1},{4,6},{5,7},{6,4},{7,5},{8,10},{9,11},{10,... | collective-permute-start | bytes 811016 | tf_op jit(solution)/shard_map/ppermute | solution.py:519
  48.1 1.0 %copy-start.1 = (bf16[256,1024]{1,0:T(8,128)(2,1)S(1)}, bf16[256,1024]{1,0:T(8,128)(2,1)}, u32[]{:S(2)}) copy-start(bf16[256,1024]{1,0:T(8,128)(2,1)} %refs_3_.3) | copy-start | bytes 1572868
  48.1 1.2 %copy-start.2 = (bf16[256,1024]{1,0:T(8,128)(2,1)S(1)}, bf16[256,1024]{1,0:T(8,128)(2,1)}, u32[]{:S(2)}) copy-start(bf16[256,1024]{1,0:T(8,128)(2,1)} %refs_4_.3) | copy-start | bytes 1572868
  55.2 1.3 %collective-permute-start.14 = (f32[16,8,128]{2,1,0:T(8,128)S(1)}, f32[16,8,128]{2,1,0:T(8,128)S(1)}, u32[]{:S(2)}, u32[]{:S(2)}) collective-permute-start(f32[16,8,128]{2,1,0:T(8,128)S(1)} %get-tuple-element.61.state_ref), channel_id=1, source_target_pairs={{0,8},{8,0},{16,24},{24,16},{1,9},{9,1},{17,25},{25,17},{2,10},{10... | collective-permute-start | bytes 196616 | tf_op jit(solution)/shard_map/ppermute | solution.py:556
  56.6 4.3 %collective-permute-start.15 = (f32[16,8,128]{2,1,0:T(8,128)S(1)}, f32[16,8,128]{2,1,0:T(8,128)S(1)}, u32[]{:S(2)}, u32[]{:S(2)}) collective-permute-start(f32[16,8,128]{2,1,0:T(8,128)S(1)} %shard_map.96), channel_id=1, source_target_pairs={{0,16},{8,24},{16,0},{24,8},{1,17},{9,25},{17,1},{25,9},{2,18},{10... | collective-permute-start | bytes 196616 | tf_op jit(solution)/shard_map/ppermute | solution.py:556

commit v12 on v11

--- a/solution.py
+++ b/solution.py
@@ -31,8 +31,14 @@
 }
 
 
-def part_of(rows, blocks):
-    return next(part for part in range(16, rows + 1, 16) if rows % part == 0 and rows // part * blocks <= PEAKS)
+def folds_of(toks):
+    return toks // 128 if toks % 128 == 0 and PEAKS % (toks // 128) == 0 else 1
+
+
+def part_of(rows, blocks, folds):
+    return next(
+        part for part in range(16, rows + 1, 16) if rows % part == 0 and rows // part * blocks * folds <= PEAKS
+    )
 
 
 def step_of(rows):
@@ -52,22 +58,37 @@
     return jnp.concatenate(codes, axis=0).astype(jnp.bfloat16), peaks
 
 
+def put(codes, out_ref, at):
+    lanes = out_ref.shape[1]
+    folds = codes.shape[1] // lanes
+    rows = (out_ref.shape[0] - PEAKS) // folds
+    for fold in range(folds):
+        out_ref[fold * rows + at : fold * rows + at + codes.shape[0], :] = codes[:, fold * lanes : (fold + 1) * lanes]
+
+
 def put_peaks(peaks, out_ref):
+    lanes = out_ref.shape[1]
+    peaks = [peak[:, at : at + lanes] for peak in peaks for at in range(0, peak.shape[1], lanes)]
     if len(peaks) < PEAKS:
-        peaks = peaks + [jnp.zeros((PEAKS - len(peaks), peaks[0].shape[1]), jnp.float32)]
+        peaks.append(jnp.zeros((PEAKS - len(peaks), lanes), jnp.float32))
     out_ref[out_ref.shape[0] - PEAKS :, :] = jnp.concatenate(peaks, axis=0).astype(jnp.bfloat16)
 
 
-def decode(ref, place, first, count):
+def decode(ref, place, first, count, folds):
     start, peak, part = place
+    rows = (ref.shape[0] - PEAKS) // folds
     peaks = ref[ref.shape[0] - PEAKS :, :].astype(jnp.float32) * (1.0 / SPAN)
-    blocks = []
-    for i in range(first // part, -(-(first + count) // part)):
-        low, high = max(first, i * part), min(first + count, (i + 1) * part)
-        code = ref[start + low : start + high, :].astype(jnp.float32)
-        size = (jnp.log(jnp.abs(code)) + SHIFT) * peaks[peak + i : peak + i + 1, :]
-        blocks.append(jnp.where(code < 0, -size, size))
-    return jnp.concatenate(blocks, axis=0)
+    columns = []
+    for fold in range(folds):
+        blocks = []
+        for i in range(first // part, -(-(first + count) // part)):
+            low, high = max(first, i * part), min(first + count, (i + 1) * part)
+            code = ref[fold * rows + start + low : fold * rows + start + high, :].astype(jnp.float32)
+            at = (peak + i) * folds + fold
+            size = (jnp.log(jnp.abs(code)) + SHIFT) * peaks[at : at + 1, :]
+            blocks.append(jnp.where(code < 0, -size, size))
+        columns.append(jnp.concatenate(blocks, axis=0))
+    return jnp.concatenate(columns, axis=1)
 
 
 def pinned(array):
@@ -76,6 +97,7 @@
 
 def send_kernel(items, coded, width, near, place_ref, w_ref, turned_ref, *refs):
     near_refs, out_ref = refs[:near], refs[near]
+    folds = folds_of(turned_ref.shape[1])
     base, peaks = 0, []
     for block, offset, rows, sources in items:
         step = step_of(rows)
@@ -87,11 +109,13 @@
                 preferred_element_type=jnp.float32,
             )
             for source, place in sources:
-                total = total + decode(near_refs[source], place, at, step)
+                total = total + decode(near_refs[source], place, at, step, folds)
             if coded:
-                total, more = encode(total, part_of(rows, len(items)))
+                total, more = encode(total, part_of(rows, len(items), folds))
                 peaks += more
-            out_ref[base + at : base + at + step, :] = total
+                put(total, out_ref, base + at)
+            else:
+                out_ref[base + at : base + at + step, :] = total
         base += rows
     if coded:
         put_peaks(peaks, out_ref)
@@ -100,12 +124,14 @@
 def send(items, coded, width, place, weight, turned, nears):
     toks = turned.shape[1]
     vmem = pl.BlockSpec(memory_space=pltpu.VMEM)
-    count = sum(rows for _, _, rows, _ in items) + (PEAKS if coded else 0)
+    count = sum(rows for _, _, rows, _ in items)
+    folds = folds_of(toks)
+    shape = (folds * count + PEAKS, toks // folds) if coded else (count, toks)
     return pl.pallas_call(
         functools.partial(send_kernel, items, coded, width, len(nears)),
         in_specs=[pl.BlockSpec(memory_space=pltpu.SMEM)] + [vmem] * (2 + len(nears)),
         out_specs=vmem,
-        out_shape=jax.ShapeDtypeStruct((count, toks), jnp.bfloat16 if coded else jnp.float32),
+        out_shape=jax.ShapeDtypeStruct(shape, jnp.bfloat16 if coded else jnp.float32),
         compiler_params=pltpu.CompilerParams(vmem_limit_bytes=VMEM),
         cost_estimate=QUICK,
     )(place, weight, turned, *nears)
@@ -140,9 +166,9 @@
             for _ in range(step // math.gcd(rows, PIECE)):
                 next(waits).wait()
             total = jnp.dot(w_ref[at : at + step, :], turned_ref[...], preferred_element_type=jnp.float32)
-            total, more = encode(total, part_of(rows, len(items)))
+            total, more = encode(total, part_of(rows, len(items), folds_of(toks)))
             peaks += more
-            out_ref[at : at + step, :] = total
+            put(total, out_ref, at)
         base += rows
     put_peaks(peaks, out_ref)
 
@@ -152,13 +178,14 @@
     vmem = pl.BlockSpec(memory_space=pltpu.VMEM)
     high = pl.BlockSpec(memory_space=pltpu.HBM)
     count = sum(rows for _, _, rows, _ in items)
+    folds = folds_of(toks)
     steps = toks // math.gcd(toks, PIECE) + sum(rows // math.gcd(rows, PIECE) for _, _, rows, _ in items)
     return pl.pallas_call(
         functools.partial(first_kernel, items, width),
         in_specs=[pl.BlockSpec(memory_space=pltpu.SMEM), high, high],
         out_specs=(vmem, vmem),
         out_shape=(
-            jax.ShapeDtypeStruct((count + PEAKS, toks), jnp.bfloat16),
+            jax.ShapeDtypeStruct((folds * count + PEAKS, toks // folds), jnp.bfloat16),
             jax.ShapeDtypeStruct((depth, toks), jnp.bfloat16),
         ),
         scratch_shapes=[
@@ -214,7 +241,7 @@
         mix = acc_ref[line * lanes : (line + 1) * lanes, :]
         first, sources = next(piece for piece in reversed(pieces) if piece[0] <= line * lanes)
         for source, place in sources:
-            mix = mix + decode(near_refs[source], place, line * lanes - first, lanes)
+            mix = mix + decode(near_refs[source], place, line * lanes - first, lanes, folds_of(toks))
         mix = mix.T
         at = slice(line * lanes, (line + 1) * lanes)
         full = slice(half * rows + line * lanes, half * rows + (line + 1) * lanes)
@@ -362,21 +389,39 @@
     )(decay)
 
 
-def join_kernel(round_, group_ref, state_ref, arrived_ref, wide_ref, out_ref):
+def states_in(ref, shape):
+    if ref.shape == shape:
+        return [ref[m] for m in range(shape[0])]
+    packs, sublanes, _ = shape
+    rows = decode(ref, (0, 0, part_of(packs * sublanes, 1, 1)), 0, packs * sublanes, 1)
+    return [rows[m * sublanes : (m + 1) * sublanes, :] for m in range(packs)]
+
+
+def join_kernel(round_, group_ref, state_ref, arrived_ref, wide_ref, out_ref, coded_ref):
     earlier = (group_ref[0] >> round_) % 2 == 0
-    for m in range(out_ref.shape[0]):
+    packs, sublanes, _ = state_ref.shape
+    joined = []
+    for m, other in enumerate(states_in(arrived_ref, state_ref.shape)):
         wide = power(wide_ref[m], 1 << round_)
-        mine, other = state_ref[m], arrived_ref[m]
-        out_ref[m] = jnp.where(earlier, mine + wide * other, other + wide * mine)
+        mine = state_ref[m]
+        joined.append(jnp.where(earlier, mine + wide * other, other + wide * mine))
+        out_ref[m] = joined[-1]
+    codes, peaks = encode(jnp.concatenate(joined, axis=0), part_of(packs * sublanes, 1, 1))
+    put(codes, coded_ref, 0)
+    put_peaks(peaks, coded_ref)
 
 
 def join(round_, group, state, arrived, wide):
     vmem = pl.BlockSpec(memory_space=pltpu.VMEM)
+    packs, sublanes, lanes = state.shape
     return pl.pallas_call(
         functools.partial(join_kernel, round_),
         in_specs=[pl.BlockSpec(memory_space=pltpu.SMEM)] + [vmem] * 3,
-        out_specs=vmem,
-        out_shape=jax.ShapeDtypeStruct(state.shape, jnp.float32),
+        out_specs=(vmem, vmem),
+        out_shape=(
+            jax.ShapeDtypeStruct(state.shape, jnp.float32),
+            jax.ShapeDtypeStruct((packs * sublanes + PEAKS, lanes), jnp.bfloat16),
+        ),
         compiler_params=pltpu.CompilerParams(vmem_limit_bytes=VMEM),
         cost_estimate=QUICK,
     )(group, state, arrived, wide)
@@ -392,6 +437,7 @@
     span = toks // segments
     segment = segment_of((sublanes, lanes), segments)
     earlier = [(group_ref[0] >> r) % 2 == 0 for r in range(rounds)]
+    arrived = [states_in(ref, (2 * packs, sublanes, lanes)) for ref in arrived_refs]
     stores = []
     for half in range(2):
         mine = slice(half * sublanes, (half + 1) * sublanes)
@@ -401,7 +447,7 @@
             brought = jnp.zeros((sublanes, lanes), jnp.float32)
             between = jnp.ones((sublanes, lanes), jnp.float32)
             for r in range(rounds):
-                state = arrived_refs[r][half * packs + m]
+                state = arrived[r][half * packs + m]
                 brought = jnp.where(earlier[r], brought + between * state, brought)
                 if r + 1 < rounds:
                     between = jnp.where(earlier[r], between * power(wide_ref[half * packs + m], 1 << r), between)
@@ -519,7 +565,7 @@
             arrived = lax.ppermute(last, "ch", [(i, i ^ bit) for i in range(size)])
             start = peak = 0
             for i, key in enumerate(todo):
-                part = part_of(rows[i], count)
+                part = part_of(rows[i], count, folds_of(toks))
                 received[key] = (arrived, start, peak, part)
                 start, peak = start + rows[i], peak + rows[i] // part
         elif kind == "laps":
@@ -556,8 +602,8 @@
             swap = lambda array, round_: lax.ppermute(array, "ctx", [(i, i ^ (1 << round_)) for i in range(groups)])
             arrived, joined = [swap(packed[1], 0)], packed[1]
             for round_ in range(1, groups.bit_length() - 1):
-                joined = last = join(round_ - 1, after(group), joined, arrived[-1], wide)
-                arrived.append(swap(joined, round_))
+                joined, last = join(round_ - 1, after(group), joined, arrived[-1], wide)
+                arrived.append(swap(last, round_))
             scanned[1] = scan(1, segments, after(scanned[1]), states[1], decay, lap, residue)
         else:
             grad_input = fix(

time: 63.6 us -> 63 us (level)
  waiting for transfers between devices: 12.8 us -> 11.6 us
    ppermute x14, waiting for transfers between devices: 9.41 us -> 8.74 us  [local(): arrived = lax.ppermute(last, 'ch', [(i, i ^ bit) for i in range(size)])]
    pallas_call x1, Pallas kernels: 0.02 us -> 0.65 us  [join(): pl.pallas_call(functools.partial(join_kernel, round_), in_specs=[pl.Block...]
where the time goes in v12:
time: 63 us; the launch traced here: 62.4 us
  starting transfers between devices  29.4 us (47%)
  Pallas kernels  19.4 us (31%)
  waiting for transfers between devices  11.6 us (18%)
  local copies, waits for them, and re-layouts  1.22 us (2%)
  between operations  0.89 us (1%)
    ppermute x14, starting transfers between devices, local(): arrived = lax.ppermute(last, 'ch', [(i, i ^ bit) for i in range(size)])  28.1 us
    pallas_call x15, Pallas kernels, send(): pl.pallas_call(functools.partial(send_kernel, items, coded, width, len(ne...  9.74 us
    ppermute x14, waiting for transfers between devices, local(): arrived = lax.ppermute(last, 'ch', [(i, i ^ bit) for i in range(size)])  8.74 us
    pallas_call x2, Pallas kernels, gate(): pl.pallas_call(functools.partial(gate_kernel, half, rows, segments, piece...  3.2 us
    ppermute x2, waiting for transfers between devices, local(): lax.ppermute(array, 'ctx', [(i, i ^ 1 << round_) for i in range(groups)])  2.82 us
    pallas_call x1, Pallas kernels, first_send(): pl.pallas_call(functools.partial(first_kernel, items, width), in_specs=[p...  2.38 us
    pallas_call x1, Pallas kernels, fix(): pl.pallas_call(functools.partial(fix_kernel, segments, len(arrived)), in_...  2.23 us
    ppermute x2, starting transfers between devices, local(): lax.ppermute(array, 'ctx', [(i, i ^ 1 << round_) for i in range(groups)])  1.27 us
  transfers between devices with their start and end apart: 16, of which 11 were waited for; matrix products, arithmetic and copies ran while one was open for 0% of the time, Pallas kernels for 21%

profile of v12, /device:TPU:0, one launch (start us, length us, event | category | flops | bytes accessed | tf_op | source)
XLA Modules:
  0.0 62.4 jit_solution(16637284206517251700)
XLA Ops:
  0.6 0.0 copy-start
  0.6 2.4 %shard_map.77 = (bf16[1040,128]{1,0:T(8,128)(2,1)S(1)}, bf16[1024,256]{1,0:T(8,128)(2,1)S(1)}) custom-call(s32[1]{0:T(128)} %bitcast.place_ref, bf16[8192,1024]{1,0:T(8,128)(2,1)} %w_ref.29, bf16[256,1024]{1,0:T(8,128)(2,1)} %g_hbm.1), custom_call_target="tpu_custom_call" | custom-call | bytes 1024 | tf_op jit(solution)/shard_map/pallas_call | solution.py:183
  3.0 3.0 %collective-permute-start = (bf16[1040,128]{1,0:T(8,128)(2,1)S(1)}, bf16[1040,128]{1,0:T(8,128)(2,1)S(1)}, u32[]{:S(2)}, u32[]{:S(2)}) collective-permute-start(bf16[1040,128]{1,0:T(8,128)(2,1)S(1)} %get-tuple-element.35), channel_id=1, source_target_pairs={{0,1},{1,0},{2,3},{3,2},{4,5},{5,4},{6,7},{7,6},{8,9},{9,8},{10,11... | collective-permute-start | bytes 798728 | tf_op jit(solution)/shard_map/ppermute | solution.py:565
  6.1 0.8 %copy-done = bf16[8192,1024]{1,0:T(8,128)(2,1)S(1)} copy-done((bf16[8192,1024]{1,0:T(8,128)(2,1)S(1)}, bf16[8192,1024]{1,0:T(8,128)(2,1)}, u32[]{:S(2)}) %copy-start) | copy-done | bytes 16777240
  6.9 0.6 shard_map.78
  7.5 0.6 shard_map.79
  8.1 0.6 shard_map.80
  8.7 3.0 %collective-permute-start.1 = (bf16[1040,128]{1,0:T(8,128)(2,1)S(1)}, bf16[1040,128]{1,0:T(8,128)(2,1)S(1)}, u32[]{:S(2)}, u32[]{:S(2)}) collective-permute-start(bf16[1040,128]{1,0:T(8,128)(2,1)S(1)} %shard_map.80), channel_id=1, source_target_pairs={{0,1},{1,0},{2,3},{3,2},{4,5},{5,4},{6,7},{7,6},{8,9},{9,8},{10,11... | collective-permute-start | bytes 798728 | tf_op jit(solution)/shard_map/ppermute | solution.py:565
  11.7 0.1 collective-permute-start.2
  11.8 0.6 shard_map.81
  12.4 0.6 shard_map.82
  13.1 0.6 shard_map.83
  13.7 0.0 collective-permute-done.refs_0_
  13.7 0.7 %shard_map.84 = bf16[1040,128]{1,0:T(8,128)(2,1)S(1)} custom-call(s32[1]{0:T(128)} %bitcast.place_ref, bf16[8192,1024]{1,0:T(8,128)(2,1)S(1)} %copy-done, bf16[1024,256]{1,0:T(8,128)(2,1)S(1)} %get-tuple-element.37.turned_ref, bf16[1040,128]{1,0:T(8,128)(2,1)S(1)} %collective-permute-done.refs_0_), custom_call_target="tpu_custom_call" | custom-call | bytes 1024 | tf_op jit(solution)/shard_map/pallas_call | solution.py:130
  14.4 2.1 %collective-permute-start.3 = (bf16[1040,128]{1,0:T(8,128)(2,1)S(1)}, bf16[1040,128]{1,0:T(8,128)(2,1)S(1)}, u32[]{:S(2)}, u32[]{:S(2)}) collective-permute-start(bf16[1040,128]{1,0:T(8,128)(2,1)S(1)} %shard_map.84), channel_id=1, source_target_pairs={{0,2},{1,3},{2,0},{3,1},{4,6},{5,7},{6,4},{7,5},{8,10},{9,11},{10,... | collective-permute-start | bytes 798728 | tf_op jit(solution)/shard_map/ppermute | solution.py:565
  16.5 1.5 %collective-permute-start.4 = (bf16[1040,128]{1,0:T(8,128)(2,1)S(1)}, bf16[1040,128]{1,0:T(8,128)(2,1)S(1)}, u32[]{:S(2)}, u32[]{:S(2)}) collective-permute-start(bf16[1040,128]{1,0:T(8,128)(2,1)S(1)} %shard_map.83), channel_id=1, source_target_pairs={{0,1},{1,0},{2,3},{3,2},{4,5},{5,4},{6,7},{7,6},{8,9},{9,8},{10,11... | collective-permute-start | bytes 798728 | tf_op jit(solution)/shard_map/ppermute | solution.py:565
  18.0 1.0 %collective-permute-done.1.refs_0_ = bf16[1040,128]{1,0:T(8,128)(2,1)S(1)} collective-permute-done((bf16[1040,128]{1,0:T(8,128)(2,1)S(1)}, bf16[1040,128]{1,0:T(8,128)(2,1)S(1)}, u32[]{:S(2)}, u32[]{:S(2)}) %collective-permute-start.1) | collective-permute-done | bytes 266272 | tf_op jit(solution)/shard_map/ppermute | solution.py:565
  19.0 0.7 %shard_map.85 = bf16[1040,128]{1,0:T(8,128)(2,1)S(1)} custom-call(s32[1]{0:T(128)} %bitcast.place_ref, bf16[8192,1024]{1,0:T(8,128)(2,1)S(1)} %copy-done, bf16[1024,256]{1,0:T(8,128)(2,1)S(1)} %get-tuple-element.37.turned_ref, bf16[1040,128]{1,0:T(8,128)(2,1)S(1)} %collective-permute-done.1.refs_0_), custom_call_target="tpu_custom_call" | custom-call | bytes 1024 | tf_op jit(solution)/shard_map/pallas_call | solution.py:130
  19.7 2.2 %collective-permute-start.5 = (bf16[1040,128]{1,0:T(8,128)(2,1)S(1)}, bf16[1040,128]{1,0:T(8,128)(2,1)S(1)}, u32[]{:S(2)}, u32[]{:S(2)}) collective-permute-start(bf16[1040,128]{1,0:T(8,128)(2,1)S(1)} %shard_map.85), channel_id=1, source_target_pairs={{0,2},{1,3},{2,0},{3,1},{4,6},{5,7},{6,4},{7,5},{8,10},{9,11},{10,... | collective-permute-start | bytes 798728 | tf_op jit(solution)/shard_map/ppermute | solution.py:565
  21.9 1.5 %collective-permute-start.6 = (bf16[1040,128]{1,0:T(8,128)(2,1)S(1)}, bf16[1040,128]{1,0:T(8,128)(2,1)S(1)}, u32[]{:S(2)}, u32[]{:S(2)}) collective-permute-start(bf16[1040,128]{1,0:T(8,128)(2,1)S(1)} %shard_map.82), channel_id=1, source_target_pairs={{0,1},{1,0},{2,3},{3,2},{4,5},{5,4},{6,7},{7,6},{8,9},{9,8},{10,11... | collective-permute-start | bytes 798728 | tf_op jit(solution)/shard_map/ppermute | solution.py:565
  23.4 1.3 %collective-permute-done.2.refs_0_ = bf16[1040,128]{1,0:T(8,128)(2,1)S(1)} collective-permute-done((bf16[1040,128]{1,0:T(8,128)(2,1)S(1)}, bf16[1040,128]{1,0:T(8,128)(2,1)S(1)}, u32[]{:S(2)}, u32[]{:S(2)}) %collective-permute-start.2) | collective-permute-done | bytes 266272 | tf_op jit(solution)/shard_map/ppermute | solution.py:565
  24.7 0.0 collective-permute-done.3.refs_1_
  24.7 0.9 %shard_map.86 = bf16[1040,128]{1,0:T(8,128)(2,1)S(1)} custom-call(s32[1]{0:T(128)} %bitcast.place_ref, bf16[8192,1024]{1,0:T(8,128)(2,1)S(1)} %copy-done, bf16[1024,256]{1,0:T(8,128)(2,1)S(1)} %get-tuple-element.37.turned_ref, bf16[1040,128]{1,0:T(8,128)(2,1)S(1)} %collective-permute-done.2.refs_0_, bf16[1040,128]{1,0:T(8,128)(2,1)S(1)} %collective-permute-done.3.refs_1_), custom_call_target="tpu_custom_call" | custom-call | bytes 1024 | tf_op jit(solution)/shard_map/pallas_call | solution.py:130
  25.6 3.2 %collective-permute-start.7 = (bf16[1040,128]{1,0:T(8,128)(2,1)S(1)}, bf16[1040,128]{1,0:T(8,128)(2,1)S(1)}, u32[]{:S(2)}, u32[]{:S(2)}) collective-permute-start(bf16[1040,128]{1,0:T(8,128)(2,1)S(1)} %shard_map.86), channel_id=1, source_target_pairs={{0,4},{1,5},{2,6},{3,7},{4,0},{5,1},{6,2},{7,3},{8,12},{9,13},{10,... | collective-permute-start | bytes 798728 | tf_op jit(solution)/shard_map/ppermute | solution.py:565
  28.8 1.5 %collective-permute-start.8 = (bf16[1040,128]{1,0:T(8,128)(2,1)S(1)}, bf16[1040,128]{1,0:T(8,128)(2,1)S(1)}, u32[]{:S(2)}, u32[]{:S(2)}) collective-permute-start(bf16[1040,128]{1,0:T(8,128)(2,1)S(1)} %shard_map.81), channel_id=1, source_target_pairs={{0,1},{1,0},{2,3},{3,2},{4,5},{5,4},{6,7},{7,6},{8,9},{9,8},{10,11... | collective-permute-start | bytes 798728 | tf_op jit(solution)/shard_map/ppermute | solution.py:565
  30.3 0.6 shard_map.87
  30.9 0.0 collective-permute-done.4.refs_0_
  30.9 0.7 %shard_map.88 = bf16[1040,128]{1,0:T(8,128)(2,1)S(1)} custom-call(s32[1]{0:T(128)} %bitcast.place_ref, bf16[8192,1024]{1,0:T(8,128)(2,1)S(1)} %copy-done, bf16[1024,256]{1,0:T(8,128)(2,1)S(1)} %get-tuple-element.37.turned_ref, bf16[1040,128]{1,0:T(8,128)(2,1)S(1)} %collective-permute-done.4.refs_0_), custom_call_target="tpu_custom_call" | custom-call | bytes 1024 | tf_op jit(solution)/shard_map/pallas_call | solution.py:130
  31.6 0.0 copy-start.3
  31.7 0.0 copy-start.4
  31.7 1.6 %collective-permute-start.9 = (bf16[1040,128]{1,0:T(8,128)(2,1)S(1)}, bf16[1040,128]{1,0:T(8,128)(2,1)S(1)}, u32[]{:S(2)}, u32[]{:S(2)}) collective-permute-start(bf16[1040,128]{1,0:T(8,128)(2,1)S(1)} %shard_map.88), channel_id=1, source_target_pairs={{0,2},{1,3},{2,0},{3,1},{4,6},{5,7},{6,4},{7,5},{8,10},{9,11},{10,... | collective-permute-start | bytes 798728 | tf_op jit(solution)/shard_map/ppermute | solution.py:565
  33.3 0.0 collective-permute-done.5.refs_1_
  33.3 1.5 %collective-permute-start.10 = (bf16[1040,128]{1,0:T(8,128)(2,1)S(1)}, bf16[1040,128]{1,0:T(8,128)(2,1)S(1)}, u32[]{:S(2)}, u32[]{:S(2)}) collective-permute-start(bf16[1040,128]{1,0:T(8,128)(2,1)S(1)} %shard_map.87), channel_id=1, source_target_pairs={{0,1},{1,0},{2,3},{3,2},{4,5},{5,4},{6,7},{7,6},{8,9},{9,8},{10,11... | collective-permute-start | bytes 798728 | tf_op jit(solution)/shard_map/ppermute | solution.py:565
  34.8 1.3 %collective-permute-done.6.refs_0_ = bf16[1040,128]{1,0:T(8,128)(2,1)S(1)} collective-permute-done((bf16[1040,128]{1,0:T(8,128)(2,1)S(1)}, bf16[1040,128]{1,0:T(8,128)(2,1)S(1)}, u32[]{:S(2)}, u32[]{:S(2)}) %collective-permute-start.6) | collective-permute-done | bytes 266272 | tf_op jit(solution)/shard_map/ppermute | solution.py:565
  36.1 2.1 %collective-permute-start.12 = (bf16[1040,128]{1,0:T(8,128)(2,1)S(1)}, bf16[1040,128]{1,0:T(8,128)(2,1)S(1)}, u32[]{:S(2)}, u32[]{:S(2)}) collective-permute-start(bf16[1040,128]{1,0:T(8,128)(2,1)S(1)} %shard_map.78), channel_id=1, source_target_pairs={{0,1},{1,0},{2,3},{3,2},{4,5},{5,4},{6,7},{7,6},{8,9},{9,8},{10,11... | collective-permute-start | bytes 798728 | tf_op jit(solution)/shard_map/ppermute | solution.py:565
  38.1 0.9 %shard_map.89 = bf16[1040,128]{1,0:T(8,128)(2,1)S(1)} custom-call(s32[1]{0:T(128)} %bitcast.place_ref, bf16[8192,1024]{1,0:T(8,128)(2,1)S(1)} %copy-done, bf16[1024,256]{1,0:T(8,128)(2,1)S(1)} %get-tuple-element.37.turned_ref, bf16[1040,128]{1,0:T(8,128)(2,1)S(1)} %collective-permute-done.6.refs_0_, bf16[1040,128]{1,0:T(8,128)(2,1)S(1)} %collective-permute-done.5.refs_1_), custom_call_target="tpu_custom_call" | custom-call | bytes 1024 | tf_op jit(solution)/shard_map/pallas_call | solution.py:130
  39.0 0.1 collective-permute-done.7.refs_2_
  39.2 2.5 %collective-permute-start.11 = (bf16[1040,128]{1,0:T(8,128)(2,1)S(1)}, bf16[1040,128]{1,0:T(8,128)(2,1)S(1)}, u32[]{:S(2)}, u32[]{:S(2)}) collective-permute-start(bf16[1040,128]{1,0:T(8,128)(2,1)S(1)} %shard_map.89), channel_id=1, source_target_pairs={{0,4},{1,5},{2,6},{3,7},{4,0},{5,1},{6,2},{7,3},{8,12},{9,13},{10,... | collective-permute-start | bytes 798728 | tf_op jit(solution)/shard_map/ppermute | solution.py:565
  41.7 0.1 collective-permute-done.8.refs_0_
  41.8 0.7 %shard_map.90 = bf16[1040,128]{1,0:T(8,128)(2,1)S(1)} custom-call(s32[1]{0:T(128)} %bitcast.place_ref, bf16[8192,1024]{1,0:T(8,128)(2,1)S(1)} %copy-done, bf16[1024,256]{1,0:T(8,128)(2,1)S(1)} %get-tuple-element.37.turned_ref, bf16[1040,128]{1,0:T(8,128)(2,1)S(1)} %collective-permute-done.8.refs_0_), custom_call_target="tpu_custom_call" | custom-call | bytes 1024 | tf_op jit(solution)/shard_map/pallas_call | solution.py:130
  42.5 2.2 %collective-permute-start.13 = (bf16[1040,128]{1,0:T(8,128)(2,1)S(1)}, bf16[1040,128]{1,0:T(8,128)(2,1)S(1)}, u32[]{:S(2)}, u32[]{:S(2)}) collective-permute-start(bf16[1040,128]{1,0:T(8,128)(2,1)S(1)} %shard_map.90), channel_id=1, source_target_pairs={{0,2},{1,3},{2,0},{3,1},{4,6},{5,7},{6,4},{7,5},{8,10},{9,11},{10,... | collective-permute-start | bytes 798728 | tf_op jit(solution)/shard_map/ppermute | solution.py:565
  44.7 0.0 copy-done.3
  44.7 0.0 copy-done.4
  44.9 0.0 collective-permute-done.9.refs_1_
  44.9 2.6 %collective-permute-done.10.refs_0_ = bf16[1040,128]{1,0:T(8,128)(2,1)S(1)} collective-permute-done((bf16[1040,128]{1,0:T(8,128)(2,1)S(1)}, bf16[1040,128]{1,0:T(8,128)(2,1)S(1)}, u32[]{:S(2)}, u32[]{:S(2)}) %collective-permute-start.10) | collective-permute-done | bytes 266272 | tf_op jit(solution)/shard_map/ppermute | solution.py:565
  47.5 0.0 copy-start.1
  47.5 0.0 copy-start.2
  47.5 0.4 shard_map.92.acc_ref
  47.9 0.4 shard_map.93.acc_ref
  48.4 0.1 copy-done.1
  48.5 0.2 copy-done.2
  48.7 1.8 %shard_map.94 = (bf16[256,1024]{1,0:T(8,128)(2,1)}, f32[1088,128]{1,0:T(8,128)S(1)}, f32[16,8,128]{2,1,0:T(8,128)S(1)}, f32[8,8,128]{2,1,0:T(8,128)S(1)}) custom-call(f32[512,256]{1,0:T(8,128)S(1)} %shard_map.92.acc_ref, bf16[1040,128]{1,0:T(8,128)(2,1)S(1)} %collective-permute-done.10.refs_0_, bf16[1040,128]{1,0:T(8,128)(2,1)S(1)} %collective-permute-done.9.refs_1_, ...), custom_call_target="tpu_custom_call" | custom-call | bytes 1024 | tf_op jit(solution)/shard_map/pallas_call | solution.py:299
  50.6 1.5 %collective-permute-done.11.refs_2_ = bf16[1040,128]{1,0:T(8,128)(2,1)S(1)} collective-permute-done((bf16[1040,128]{1,0:T(8,128)(2,1)S(1)}, bf16[1040,128]{1,0:T(8,128)(2,1)S(1)}, u32[]{:S(2)}, u32[]{:S(2)}) %collective-permute-start.11) | collective-permute-done | bytes 266272 | tf_op jit(solution)/shard_map/ppermute | solution.py:565
  52.0 0.3 collective-permute-done.12.refs_0_
  52.4 0.5 collective-permute-done.13.refs_1_
  52.9 1.3 %shard_map.95 = (bf16[256,1024]{1,0:T(8,128)(2,1)}, f32[1088,128]{1,0:T(8,128)S(1)}, f32[16,8,128]{2,1,0:T(8,128)S(1)}, f32[16,8,128]{2,1,0:T(8,128)S(1)}) custom-call(f32[512,256]{1,0:T(8,128)S(1)} %shard_map.93.acc_ref, bf16[1040,128]{1,0:T(8,128)(2,1)S(1)} %collective-permute-done.12.refs_0_, ...), custom_call_target="tpu_custom_call", output_to_operand_aliasing={{0}: (9, {})} | custom-call | bytes 1024 | tf_op jit(solution)/shard_map/pallas_call | solution.py:299
  54.3 0.1 collective-permute-start.14
  54.4 1.2 %collective-permute-done.14.arrived_ref.refs_3_ = f32[16,8,128]{2,1,0:T(8,128)S(1)} collective-permute-done((f32[16,8,128]{2,1,0:T(8,128)S(1)}, f32[16,8,128]{2,1,0:T(8,128)S(1)}, u32[]{:S(2)}, u32[]{:S(2)}) %collective-permute-start.14) | collective-permute-done | bytes 65568 | tf_op jit(solution)/shard_map/ppermute | solution.py:602
  55.6 0.7 %shard_map.96 = (f32[16,8,128]{2,1,0:T(8,128)}, bf16[144,128]{1,0:T(8,128)(2,1)S(1)}) custom-call(s32[1]{0:T(128)} %bitcast.5.group_ref, f32[16,8,128]{2,1,0:T(8,128)S(1)} %get-tuple-element.62.state_ref, f32[16,8,128]{2,1,0:T(8,128)S(1)} %collective-permute-done.14.arrived_ref.refs_3_, f32[16,8,128]{2,1,0:T(8,128)S(1)} %get-tuple-element.51.wide_ref.refs_7_), custom_call_target="tpu_custom_call" | custom-call | bytes 1024 | tf_op jit(solution)/shard_map/pallas_call | solution.py:417
  56.2 1.2 %collective-permute-start.15 = (bf16[144,128]{1,0:T(8,128)(2,1)S(1)}, bf16[144,128]{1,0:T(8,128)(2,1)S(1)}, u32[]{:S(2)}, u32[]{:S(2)}) collective-permute-start(bf16[144,128]{1,0:T(8,128)(2,1)S(1)} %get-tuple-element.64), channel_id=1, source_target_pairs={{0,16},{8,24},{16,0},{24,8},{1,17},{9,25},{17,1},{25,9},{2,18},{10... | collective-permute-start | bytes 110600 | tf_op jit(solution)/shard_map/ppermute | solution.py:602
  57.4 1.2 %shard_map.97.refs_1_ = f32[1088,128]{1,0:T(8,128)S(1)} custom-call(f32[1088,128]{1,0:T(8,128)S(1)} %get-tuple-element.65.gc_ref, f32[16,8,128]{2,1,0:T(8,128)S(1)} %get-tuple-element.66.state_ref, f32[16,16,128]{2,1,0:T(8,128)S(1)} %bitcast.13, f32[16,16,128]{2,1,0:T(8,128)S(1)} %get-tuple-element.55.refs_6_.lap_ref, f32[16,16,128]{2,1,0:T(8,128)S(1)} %bitcast.16), custom_call_target="tpu_custom_call" | custom-call | bytes 1024 | tf_op jit(solution)/shard_map/pallas_call | solution.py:349
  58.6 1.6 %collective-permute-done.15.refs_4_ = bf16[144,128]{1,0:T(8,128)(2,1)S(1)} collective-permute-done((bf16[144,128]{1,0:T(8,128)(2,1)S(1)}, bf16[144,128]{1,0:T(8,128)(2,1)S(1)}, u32[]{:S(2)}, u32[]{:S(2)}) %collective-permute-start.15) | collective-permute-done | bytes 36896 | tf_op jit(solution)/shard_map/ppermute | solution.py:602
  60.2 2.2 %shard_map.98 = bf16[256,1024]{1,0:T(8,128)(2,1)} custom-call(s32[1]{0:T(128)} %bitcast.5.group_ref, f32[1088,128]{1,0:T(8,128)S(1)} %get-tuple-element.60.refs_0_, f32[1088,128]{1,0:T(8,128)S(1)} %shard_map.97.refs_1_, f32[16,8,128]{2,1,0:T(8,128)S(1)} %get-tuple-element.67.refs_2_, f32[16,8,128]{2,1,0:T(8,128)S(1)} %collective-permute-done.14.arrived_ref.refs_3_, ...), custom_call_target="tpu_custom_call" | custom-call | bytes 1024 | tf_op jit(solution)/shard_map/pallas_call | solution.py:485
  (5 shorter events, 0.2 us)
Async XLA Ops:
  0.6 6.2 %copy-start = (bf16[8192,1024]{1,0:T(8,128)(2,1)S(1)}, bf16[8192,1024]{1,0:T(8,128)(2,1)}, u32[]{:S(2)}) copy-start(bf16[8192,1024]{1,0:T(8,128)(2,1)} %w_ref.29) | copy-start | bytes 50331652
  3.0 10.6 %collective-permute-start = (bf16[1040,128]{1,0:T(8,128)(2,1)S(1)}, bf16[1040,128]{1,0:T(8,128)(2,1)S(1)}, u32[]{:S(2)}, u32[]{:S(2)}) collective-permute-start(bf16[1040,128]{1,0:T(8,128)(2,1)S(1)} %get-tuple-element.35), channel_id=1, source_target_pairs={{0,1},{1,0},{2,3},{3,2},{4,5},{5,4},{6,7},{7,6},{8,9},{9,8},{10,11... | collective-permute-start | bytes 798728 | tf_op jit(solution)/shard_map/ppermute | solution.py:565
  8.7 10.3 %collective-permute-start.1 = (bf16[1040,128]{1,0:T(8,128)(2,1)S(1)}, bf16[1040,128]{1,0:T(8,128)(2,1)S(1)}, u32[]{:S(2)}, u32[]{:S(2)}) collective-permute-start(bf16[1040,128]{1,0:T(8,128)(2,1)S(1)} %shard_map.80), channel_id=1, source_target_pairs={{0,1},{1,0},{2,3},{3,2},{4,5},{5,4},{6,7},{7,6},{8,9},{9,8},{10,11... | collective-permute-start | bytes 798728 | tf_op jit(solution)/shard_map/ppermute | solution.py:565
  11.7 12.9 %collective-permute-start.2 = (bf16[1040,128]{1,0:T(8,128)(2,1)S(1)}, bf16[1040,128]{1,0:T(8,128)(2,1)S(1)}, u32[]{:S(2)}, u32[]{:S(2)}) collective-permute-start(bf16[1040,128]{1,0:T(8,128)(2,1)S(1)} %shard_map.79), channel_id=1, source_target_pairs={{0,1},{1,0},{2,3},{3,2},{4,5},{5,4},{6,7},{7,6},{8,9},{9,8},{10,11... | collective-permute-start | bytes 798728 | tf_op jit(solution)/shard_map/ppermute | solution.py:565
  14.4 10.3 %collective-permute-start.3 = (bf16[1040,128]{1,0:T(8,128)(2,1)S(1)}, bf16[1040,128]{1,0:T(8,128)(2,1)S(1)}, u32[]{:S(2)}, u32[]{:S(2)}) collective-permute-start(bf16[1040,128]{1,0:T(8,128)(2,1)S(1)} %shard_map.84), channel_id=1, source_target_pairs={{0,2},{1,3},{2,0},{3,1},{4,6},{5,7},{6,4},{7,5},{8,10},{9,11},{10,... | collective-permute-start | bytes 798728 | tf_op jit(solution)/shard_map/ppermute | solution.py:565
  16.5 14.4 %collective-permute-start.4 = (bf16[1040,128]{1,0:T(8,128)(2,1)S(1)}, bf16[1040,128]{1,0:T(8,128)(2,1)S(1)}, u32[]{:S(2)}, u32[]{:S(2)}) collective-permute-start(bf16[1040,128]{1,0:T(8,128)(2,1)S(1)} %shard_map.83), channel_id=1, source_target_pairs={{0,1},{1,0},{2,3},{3,2},{4,5},{5,4},{6,7},{7,6},{8,9},{9,8},{10,11... | collective-permute-start | bytes 798728 | tf_op jit(solution)/shard_map/ppermute | solution.py:565
  19.7 13.6 %collective-permute-start.5 = (bf16[1040,128]{1,0:T(8,128)(2,1)S(1)}, bf16[1040,128]{1,0:T(8,128)(2,1)S(1)}, u32[]{:S(2)}, u32[]{:S(2)}) collective-permute-start(bf16[1040,128]{1,0:T(8,128)(2,1)S(1)} %shard_map.85), channel_id=1, source_target_pairs={{0,2},{1,3},{2,0},{3,1},{4,6},{5,7},{6,4},{7,5},{8,10},{9,11},{10,... | collective-permute-start | bytes 798728 | tf_op jit(solution)/shard_map/ppermute | solution.py:565
  21.9 14.2 %collective-permute-start.6 = (bf16[1040,128]{1,0:T(8,128)(2,1)S(1)}, bf16[1040,128]{1,0:T(8,128)(2,1)S(1)}, u32[]{:S(2)}, u32[]{:S(2)}) collective-permute-start(bf16[1040,128]{1,0:T(8,128)(2,1)S(1)} %shard_map.82), channel_id=1, source_target_pairs={{0,1},{1,0},{2,3},{3,2},{4,5},{5,4},{6,7},{7,6},{8,9},{9,8},{10,11... | collective-permute-start | bytes 798728 | tf_op jit(solution)/shard_map/ppermute | solution.py:565
  25.6 13.6 %collective-permute-start.7 = (bf16[1040,128]{1,0:T(8,128)(2,1)S(1)}, bf16[1040,128]{1,0:T(8,128)(2,1)S(1)}, u32[]{:S(2)}, u32[]{:S(2)}) collective-permute-start(bf16[1040,128]{1,0:T(8,128)(2,1)S(1)} %shard_map.86), channel_id=1, source_target_pairs={{0,4},{1,5},{2,6},{3,7},{4,0},{5,1},{6,2},{7,3},{8,12},{9,13},{10,... | collective-permute-start | bytes 798728 | tf_op jit(solution)/shard_map/ppermute | solution.py:565
  28.8 13.0 %collective-permute-start.8 = (bf16[1040,128]{1,0:T(8,128)(2,1)S(1)}, bf16[1040,128]{1,0:T(8,128)(2,1)S(1)}, u32[]{:S(2)}, u32[]{:S(2)}) collective-permute-start(bf16[1040,128]{1,0:T(8,128)(2,1)S(1)} %shard_map.81), channel_id=1, source_target_pairs={{0,1},{1,0},{2,3},{3,2},{4,5},{5,4},{6,7},{7,6},{8,9},{9,8},{10,11... | collective-permute-start | bytes 798728 | tf_op jit(solution)/shard_map/ppermute | solution.py:565
  31.6 13.1 %copy-start.3 = (f32[1024,16]{0,1:T(8,128)S(1)}, f32[1024,16]{0,1:T(8,128)}, u32[]{:S(2)}) copy-start(f32[1024,16]{0,1:T(8,128)} %param.10) | copy-start | bytes 196612
  31.7 13.1 %copy-start.4 = (f32[1024,16]{0,1:T(8,128)S(1)}, f32[1024,16]{0,1:T(8,128)}, u32[]{:S(2)}) copy-start(f32[1024,16]{0,1:T(8,128)} %param.11) | copy-start | bytes 196612
  31.7 13.2 %collective-permute-start.9 = (bf16[1040,128]{1,0:T(8,128)(2,1)S(1)}, bf16[1040,128]{1,0:T(8,128)(2,1)S(1)}, u32[]{:S(2)}, u32[]{:S(2)}) collective-permute-start(bf16[1040,128]{1,0:T(8,128)(2,1)S(1)} %shard_map.88), channel_id=1, source_target_pairs={{0,2},{1,3},{2,0},{3,1},{4,6},{5,7},{6,4},{7,5},{8,10},{9,11},{10,... | collective-permute-start | bytes 798728 | tf_op jit(solution)/shard_map/ppermute | solution.py:565
  33.3 14.2 %collective-permute-start.10 = (bf16[1040,128]{1,0:T(8,128)(2,1)S(1)}, bf16[1040,128]{1,0:T(8,128)(2,1)S(1)}, u32[]{:S(2)}, u32[]{:S(2)}) collective-permute-start(bf16[1040,128]{1,0:T(8,128)(2,1)S(1)} %shard_map.87), channel_id=1, source_target_pairs={{0,1},{1,0},{2,3},{3,2},{4,5},{5,4},{6,7},{7,6},{8,9},{9,8},{10,11... | collective-permute-start | bytes 798728 | tf_op jit(solution)/shard_map/ppermute | solution.py:565
  36.1 16.3 %collective-permute-start.12 = (bf16[1040,128]{1,0:T(8,128)(2,1)S(1)}, bf16[1040,128]{1,0:T(8,128)(2,1)S(1)}, u32[]{:S(2)}, u32[]{:S(2)}) collective-permute-start(bf16[1040,128]{1,0:T(8,128)(2,1)S(1)} %shard_map.78), channel_id=1, source_target_pairs={{0,1},{1,0},{2,3},{3,2},{4,5},{5,4},{6,7},{7,6},{8,9},{9,8},{10,11... | collective-permute-start | bytes 798728 | tf_op jit(solution)/shard_map/ppermute | solution.py:565
  39.2 12.9 %collective-permute-start.11 = (bf16[1040,128]{1,0:T(8,128)(2,1)S(1)}, bf16[1040,128]{1,0:T(8,128)(2,1)S(1)}, u32[]{:S(2)}, u32[]{:S(2)}) collective-permute-start(bf16[1040,128]{1,0:T(8,128)(2,1)S(1)} %shard_map.89), channel_id=1, source_target_pairs={{0,4},{1,5},{2,6},{3,7},{4,0},{5,1},{6,2},{7,3},{8,12},{9,13},{10,... | collective-permute-start | bytes 798728 | tf_op jit(solution)/shard_map/ppermute | solution.py:565
  42.5 10.4 %collective-permute-start.13 = (bf16[1040,128]{1,0:T(8,128)(2,1)S(1)}, bf16[1040,128]{1,0:T(8,128)(2,1)S(1)}, u32[]{:S(2)}, u32[]{:S(2)}) collective-permute-start(bf16[1040,128]{1,0:T(8,128)(2,1)S(1)} %shard_map.90), channel_id=1, source_target_pairs={{0,2},{1,3},{2,0},{3,1},{4,6},{5,7},{6,4},{7,5},{8,10},{9,11},{10,... | collective-permute-start | bytes 798728 | tf_op jit(solution)/shard_map/ppermute | solution.py:565
  47.5 1.0 %copy-start.1 = (bf16[256,1024]{1,0:T(8,128)(2,1)S(1)}, bf16[256,1024]{1,0:T(8,128)(2,1)}, u32[]{:S(2)}) copy-start(bf16[256,1024]{1,0:T(8,128)(2,1)} %refs_3_.3) | copy-start | bytes 1572868
  47.5 1.2 %copy-start.2 = (bf16[256,1024]{1,0:T(8,128)(2,1)S(1)}, bf16[256,1024]{1,0:T(8,128)(2,1)}, u32[]{:S(2)}) copy-start(bf16[256,1024]{1,0:T(8,128)(2,1)} %refs_4_.3) | copy-start | bytes 1572868
  54.3 1.3 %collective-permute-start.14 = (f32[16,8,128]{2,1,0:T(8,128)S(1)}, f32[16,8,128]{2,1,0:T(8,128)S(1)}, u32[]{:S(2)}, u32[]{:S(2)}) collective-permute-start(f32[16,8,128]{2,1,0:T(8,128)S(1)} %get-tuple-element.62.state_ref), channel_id=1, source_target_pairs={{0,8},{8,0},{16,24},{24,16},{1,9},{9,1},{17,25},{25,17},{2,10},{10... | collective-permute-start | bytes 196616 | tf_op jit(solution)/shard_map/ppermute | solution.py:602
  56.2 4.0 %collective-permute-start.15 = (bf16[144,128]{1,0:T(8,128)(2,1)S(1)}, bf16[144,128]{1,0:T(8,128)(2,1)S(1)}, u32[]{:S(2)}, u32[]{:S(2)}) collective-permute-start(bf16[144,128]{1,0:T(8,128)(2,1)S(1)} %get-tuple-element.64), channel_id=1, source_target_pairs={{0,16},{8,24},{16,0},{24,8},{1,17},{9,25},{17,1},{25,9},{2,18},{10... | collective-permute-start | bytes 110600 | tf_op jit(solution)/shard_map/ppermute | solution.py:602

commit v13 on v12

--- a/solution.py
+++ b/solution.py
@@ -17,17 +17,18 @@
 VMEM = 24 * 1024 * 1024
 QUICK = pl.CostEstimate(flops=0, bytes_accessed=1024, transcendentals=0)
 
-PORTIONS = (((0, 1, 2), 2, 0), ((0, 1, 2), 2, 1))
+PORTIONS = (((0, 1, 2), 4, 0), ((1, 0, 2), 4, 0), ((0, 1, 2), 4, 1), ((0, 1, 2), 4, 1))
 ORDER = (
-    ((0, 0, 6),), ((1, 0, 0),), ((0, 0, 4),), ((1, 0, 6),), ((1, 0, 2),), ((1, 0, 4),), ((0, 0, 2),), ((0, 1, 4),),
-    ((1, 1, 4),), ((0, 2, 0),), ((0, 0, 0),), ((0, 1, 0),), ((1, 2, 0),), ((1, 1, 0),), ("laps", None), ("sum", 0),
-    ("sum", 1), ("gate", 0), ("gate", 1), ("scan", 1), ("fix", None),
+    ((0, 0, 6), (0, 0, 2)), ((1, 0, 5), (1, 0, 1)), ((2, 0, 2), (3, 0, 2)), ("sum", 1), ((2, 0, 6), (3, 0, 6)),
+    ((2, 0, 4), (3, 0, 4)), ((1, 0, 4), (0, 1, 4)), ((1, 1, 4), (0, 0, 4)), ((2, 1, 4), (3, 1, 4)),
+    ((1, 0, 0), (0, 1, 0)), ((0, 2, 0), (1, 2, 0)), ((2, 2, 0), (3, 2, 0)), ((1, 1, 0), (0, 0, 0)),
+    ((2, 1, 0), (3, 1, 0)), ((2, 0, 0), (3, 0, 0)), ("laps", None), ("sum", 0), ("gate", 0), ("gate", 1), ("scan", 1),
+    ("fix", None),
 )
 WAITS = {
-    ((1, 1, 0),): ((0, 2, 0),),
-    ("sum", 0): ((0, 1, 0), (0, 0, 0)),
-    ((1, 2, 0),): ((1, 1, 4),),
-    ("gate", 1): ((1, 2, 0),),
+    ((1, 0, 0), (0, 1, 0)): ((1, 0, 4),),
+    ((2, 0, 0), (3, 0, 0)): ((0, 2, 0), (1, 0, 0)),
+    ("gate", 1): ((2, 2, 0), (2, 1, 0)),
 }
 
 
@@ -393,7 +394,7 @@
     if ref.shape == shape:
         return [ref[m] for m in range(shape[0])]
     packs, sublanes, _ = shape
-    rows = decode(ref, (0, 0, part_of(packs * sublanes, 1, 1)), 0, packs * sublanes, 1)
+    rows = decode(ref, (0, 0, packs * sublanes // 2), 0, packs * sublanes, 1)
     return [rows[m * sublanes : (m + 1) * sublanes, :] for m in range(packs)]
 
 
@@ -406,7 +407,7 @@
         mine = state_ref[m]
         joined.append(jnp.where(earlier, mine + wide * other, other + wide * mine))
         out_ref[m] = joined[-1]
-    codes, peaks = encode(jnp.concatenate(joined, axis=0), part_of(packs * sublanes, 1, 1))
+    codes, peaks = encode(jnp.concatenate(joined, axis=0), packs * sublanes // 2)
     put(codes, coded_ref, 0)
     put_peaks(peaks, coded_ref)
 

time: 63 us -> 61.8 us (0.981)
  transfers between devices with their start and end apart: 16 -> 16, of which waited for: 11 -> 7; matrix products, arithmetic and copies ran while one was open for 0% -> 0% of each run, Pallas kernels for 21% -> 21%
where the time goes in v13:
time: 61.8 us; the launch traced here: 61.6 us
  starting transfers between devices  29.2 us (47%)
  Pallas kernels  19.4 us (31%)
  waiting for transfers between devices  11.2 us (18%)
  local copies, waits for them, and re-layouts  0.96 us (2%)
  between operations  0.91 us (1%)
    ppermute x14, starting transfers between devices, local(): arrived = lax.ppermute(last, 'ch', [(i, i ^ bit) for i in range(size)])  27.6 us
    pallas_call x15, Pallas kernels, send(): pl.pallas_call(functools.partial(send_kernel, items, coded, width, len(ne...  9.7 us
    ppermute x14, waiting for transfers between devices, local(): arrived = lax.ppermute(last, 'ch', [(i, i ^ bit) for i in range(size)])  8.68 us
    pallas_call x2, Pallas kernels, gate(): pl.pallas_call(functools.partial(gate_kernel, half, rows, segments, piece...  3.2 us
    ppermute x2, waiting for transfers between devices, local(): lax.ppermute(array, 'ctx', [(i, i ^ 1 << round_) for i in range(groups)])  2.53 us
    pallas_call x1, Pallas kernels, first_send(): pl.pallas_call(functools.partial(first_kernel, items, width), in_specs=[p...  2.38 us
    pallas_call x1, Pallas kernels, fix(): pl.pallas_call(functools.partial(fix_kernel, segments, len(arrived)), in_...  2.23 us
    ppermute x2, starting transfers between devices, local(): lax.ppermute(array, 'ctx', [(i, i ^ 1 << round_) for i in range(groups)])  1.56 us
  transfers between devices with their start and end apart: 16, of which 7 were waited for; matrix products, arithmetic and copies ran while one was open for 0% of the time, Pallas kernels for 21%

profile of v13, /device:TPU:0, one launch (start us, length us, event | category | flops | bytes accessed | tf_op | source)
XLA Modules:
  0.0 61.6 jit_solution(4230076862708753838)
XLA Ops:
  0.6 0.0 copy-start
  0.6 2.4 %shard_map.77 = (bf16[1040,128]{1,0:T(8,128)(2,1)S(1)}, bf16[1024,256]{1,0:T(8,128)(2,1)S(1)}) custom-call(s32[1]{0:T(128)} %bitcast.place_ref, bf16[8192,1024]{1,0:T(8,128)(2,1)} %w_ref.29, bf16[256,1024]{1,0:T(8,128)(2,1)} %g_hbm.1), custom_call_target="tpu_custom_call" | custom-call | bytes 1024 | tf_op jit(solution)/shard_map/pallas_call | solution.py:184
  3.0 3.0 %collective-permute-start = (bf16[1040,128]{1,0:T(8,128)(2,1)S(1)}, bf16[1040,128]{1,0:T(8,128)(2,1)S(1)}, u32[]{:S(2)}, u32[]{:S(2)}) collective-permute-start(bf16[1040,128]{1,0:T(8,128)(2,1)S(1)} %get-tuple-element.34), channel_id=1, source_target_pairs={{0,1},{1,0},{2,3},{3,2},{4,5},{5,4},{6,7},{7,6},{8,9},{9,8},{10,11... | collective-permute-start | bytes 798728 | tf_op jit(solution)/shard_map/ppermute | solution.py:566
  6.1 0.8 %copy-done = bf16[8192,1024]{1,0:T(8,128)(2,1)S(1)} copy-done((bf16[8192,1024]{1,0:T(8,128)(2,1)S(1)}, bf16[8192,1024]{1,0:T(8,128)(2,1)}, u32[]{:S(2)}) %copy-start) | copy-done | bytes 16777240
  6.9 0.6 shard_map.78
  7.5 3.1 %collective-permute-start.1 = (bf16[1040,128]{1,0:T(8,128)(2,1)S(1)}, bf16[1040,128]{1,0:T(8,128)(2,1)S(1)}, u32[]{:S(2)}, u32[]{:S(2)}) collective-permute-start(bf16[1040,128]{1,0:T(8,128)(2,1)S(1)} %shard_map.78), channel_id=1, source_target_pairs={{0,2},{1,3},{2,0},{3,1},{4,6},{5,7},{6,4},{7,5},{8,10},{9,11},{10,... | collective-permute-start | bytes 798728 | tf_op jit(solution)/shard_map/ppermute | solution.py:566
  10.6 0.6 shard_map.79
  11.2 0.4 shard_map.80.acc_ref
  11.6 0.6 shard_map.81
  12.2 1.6 %collective-permute-start.2 = (bf16[1040,128]{1,0:T(8,128)(2,1)S(1)}, bf16[1040,128]{1,0:T(8,128)(2,1)S(1)}, u32[]{:S(2)}, u32[]{:S(2)}) collective-permute-start(bf16[1040,128]{1,0:T(8,128)(2,1)S(1)} %shard_map.81), channel_id=1, source_target_pairs={{0,1},{1,0},{2,3},{3,2},{4,5},{5,4},{6,7},{7,6},{8,9},{9,8},{10,11... | collective-permute-start | bytes 798728 | tf_op jit(solution)/shard_map/ppermute | solution.py:566
  13.8 0.6 shard_map.82
  14.4 0.0 collective-permute-done.refs_0_
  14.4 0.7 %shard_map.83 = bf16[1040,128]{1,0:T(8,128)(2,1)S(1)} custom-call(s32[1]{0:T(128)} %bitcast.place_ref, bf16[8192,1024]{1,0:T(8,128)(2,1)S(1)} %copy-done, bf16[1024,256]{1,0:T(8,128)(2,1)S(1)} %get-tuple-element.36.turned_ref, bf16[1040,128]{1,0:T(8,128)(2,1)S(1)} %collective-permute-done.refs_0_), custom_call_target="tpu_custom_call" | custom-call | bytes 1024 | tf_op jit(solution)/shard_map/pallas_call | solution.py:131
  15.1 0.5 collective-permute-start.3
  15.6 1.8 %collective-permute-done.1.refs_0_ = bf16[1040,128]{1,0:T(8,128)(2,1)S(1)} collective-permute-done((bf16[1040,128]{1,0:T(8,128)(2,1)S(1)}, bf16[1040,128]{1,0:T(8,128)(2,1)S(1)}, u32[]{:S(2)}, u32[]{:S(2)}) %collective-permute-start.1) | collective-permute-done | bytes 266272 | tf_op jit(solution)/shard_map/ppermute | solution.py:566
  17.4 0.6 %shard_map.84 = bf16[1040,128]{1,0:T(8,128)(2,1)S(1)} custom-call(s32[1]{0:T(128)} %bitcast.place_ref, bf16[8192,1024]{1,0:T(8,128)(2,1)S(1)} %copy-done, bf16[1024,256]{1,0:T(8,128)(2,1)S(1)} %get-tuple-element.36.turned_ref, bf16[1040,128]{1,0:T(8,128)(2,1)S(1)} %collective-permute-done.1.refs_0_), custom_call_target="tpu_custom_call" | custom-call | bytes 1024 | tf_op jit(solution)/shard_map/pallas_call | solution.py:131
  18.0 2.4 %collective-permute-start.4 = (bf16[1040,128]{1,0:T(8,128)(2,1)S(1)}, bf16[1040,128]{1,0:T(8,128)(2,1)S(1)}, u32[]{:S(2)}, u32[]{:S(2)}) collective-permute-start(bf16[1040,128]{1,0:T(8,128)(2,1)S(1)} %shard_map.84), channel_id=1, source_target_pairs={{0,1},{1,0},{2,3},{3,2},{4,5},{5,4},{6,7},{7,6},{8,9},{9,8},{10,11... | collective-permute-start | bytes 798728 | tf_op jit(solution)/shard_map/ppermute | solution.py:566
  20.4 0.1 collective-permute-start.5
  20.5 0.2 collective-permute-done.2.refs_0_
  20.7 0.7 %shard_map.85 = bf16[1040,128]{1,0:T(8,128)(2,1)S(1)} custom-call(s32[1]{0:T(128)} %bitcast.place_ref, bf16[8192,1024]{1,0:T(8,128)(2,1)S(1)} %copy-done, bf16[1024,256]{1,0:T(8,128)(2,1)S(1)} %get-tuple-element.36.turned_ref, bf16[1040,128]{1,0:T(8,128)(2,1)S(1)} %collective-permute-done.2.refs_0_), custom_call_target="tpu_custom_call" | custom-call | bytes 1024 | tf_op jit(solution)/shard_map/pallas_call | solution.py:131
  21.4 2.0 %collective-permute-start.6 = (bf16[1040,128]{1,0:T(8,128)(2,1)S(1)}, bf16[1040,128]{1,0:T(8,128)(2,1)S(1)}, u32[]{:S(2)}, u32[]{:S(2)}) collective-permute-start(bf16[1040,128]{1,0:T(8,128)(2,1)S(1)} %shard_map.85), channel_id=1, source_target_pairs={{0,2},{1,3},{2,0},{3,1},{4,6},{5,7},{6,4},{7,5},{8,10},{9,11},{10,... | collective-permute-start | bytes 798728 | tf_op jit(solution)/shard_map/ppermute | solution.py:566
  23.4 1.5 %collective-permute-start.7 = (bf16[1040,128]{1,0:T(8,128)(2,1)S(1)}, bf16[1040,128]{1,0:T(8,128)(2,1)S(1)}, u32[]{:S(2)}, u32[]{:S(2)}) collective-permute-start(bf16[1040,128]{1,0:T(8,128)(2,1)S(1)} %shard_map.79), channel_id=1, source_target_pairs={{0,1},{1,0},{2,3},{3,2},{4,5},{5,4},{6,7},{7,6},{8,9},{9,8},{10,11... | collective-permute-start | bytes 798728 | tf_op jit(solution)/shard_map/ppermute | solution.py:566
  24.9 0.0 collective-permute-done.3.refs_1_
  24.9 0.7 %shard_map.86 = bf16[1040,128]{1,0:T(8,128)(2,1)S(1)} custom-call(s32[1]{0:T(128)} %bitcast.place_ref, bf16[8192,1024]{1,0:T(8,128)(2,1)S(1)} %copy-done, bf16[1024,256]{1,0:T(8,128)(2,1)S(1)} %get-tuple-element.36.turned_ref, bf16[1040,128]{1,0:T(8,128)(2,1)S(1)} %collective-permute-done.refs_0_), custom_call_target="tpu_custom_call" | custom-call | bytes 1024 | tf_op jit(solution)/shard_map/pallas_call | solution.py:131
  25.6 2.1 %collective-permute-done.4.refs_0_ = bf16[1040,128]{1,0:T(8,128)(2,1)S(1)} collective-permute-done((bf16[1040,128]{1,0:T(8,128)(2,1)S(1)}, bf16[1040,128]{1,0:T(8,128)(2,1)S(1)}, u32[]{:S(2)}, u32[]{:S(2)}) %collective-permute-start.4) | collective-permute-done | bytes 266272 | tf_op jit(solution)/shard_map/ppermute | solution.py:566
  27.7 0.9 %shard_map.87 = bf16[1040,128]{1,0:T(8,128)(2,1)S(1)} custom-call(s32[1]{0:T(128)} %bitcast.place_ref, bf16[8192,1024]{1,0:T(8,128)(2,1)S(1)} %copy-done, bf16[1024,256]{1,0:T(8,128)(2,1)S(1)} %get-tuple-element.36.turned_ref, bf16[1040,128]{1,0:T(8,128)(2,1)S(1)} %collective-permute-done.4.refs_0_, bf16[1040,128]{1,0:T(8,128)(2,1)S(1)} %collective-permute-done.3.refs_1_), custom_call_target="tpu_custom_call" | custom-call | bytes 1024 | tf_op jit(solution)/shard_map/pallas_call | solution.py:131
  28.6 2.7 %collective-permute-start.8 = (bf16[1040,128]{1,0:T(8,128)(2,1)S(1)}, bf16[1040,128]{1,0:T(8,128)(2,1)S(1)}, u32[]{:S(2)}, u32[]{:S(2)}) collective-permute-start(bf16[1040,128]{1,0:T(8,128)(2,1)S(1)} %shard_map.87), channel_id=1, source_target_pairs={{0,4},{1,5},{2,6},{3,7},{4,0},{5,1},{6,2},{7,3},{8,12},{9,13},{10,... | collective-permute-start | bytes 798728 | tf_op jit(solution)/shard_map/ppermute | solution.py:566
  31.3 2.2 %collective-permute-start.9 = (bf16[1040,128]{1,0:T(8,128)(2,1)S(1)}, bf16[1040,128]{1,0:T(8,128)(2,1)S(1)}, u32[]{:S(2)}, u32[]{:S(2)}) collective-permute-start(bf16[1040,128]{1,0:T(8,128)(2,1)S(1)} %shard_map.86), channel_id=1, source_target_pairs={{0,2},{1,3},{2,0},{3,1},{4,6},{5,7},{6,4},{7,5},{8,10},{9,11},{10,... | collective-permute-start | bytes 798728 | tf_op jit(solution)/shard_map/ppermute | solution.py:566
  33.5 0.0 collective-permute-done.5.refs_0_
  33.5 0.0 collective-permute-done.6.refs_1_
  33.5 0.9 %shard_map.88 = bf16[1040,128]{1,0:T(8,128)(2,1)S(1)} custom-call(s32[1]{0:T(128)} %bitcast.place_ref, bf16[8192,1024]{1,0:T(8,128)(2,1)S(1)} %copy-done, bf16[1024,256]{1,0:T(8,128)(2,1)S(1)} %get-tuple-element.36.turned_ref, bf16[1040,128]{1,0:T(8,128)(2,1)S(1)} %collective-permute-done.5.refs_0_, bf16[1040,128]{1,0:T(8,128)(2,1)S(1)} %collective-permute-done.6.refs_1_), custom_call_target="tpu_custom_call" | custom-call | bytes 1024 | tf_op jit(solution)/shard_map/pallas_call | solution.py:131
  34.4 0.7 %shard_map.89 = bf16[1040,128]{1,0:T(8,128)(2,1)S(1)} custom-call(s32[1]{0:T(128)} %bitcast.place_ref, bf16[8192,1024]{1,0:T(8,128)(2,1)S(1)} %copy-done, bf16[1024,256]{1,0:T(8,128)(2,1)S(1)} %get-tuple-element.36.turned_ref, bf16[1040,128]{1,0:T(8,128)(2,1)S(1)} %collective-permute-done.1.refs_0_), custom_call_target="tpu_custom_call" | custom-call | bytes 1024 | tf_op jit(solution)/shard_map/pallas_call | solution.py:131
  35.0 0.0 copy-start.3
  35.0 0.0 copy-start.4
  35.1 2.0 %collective-permute-start.10 = (bf16[1040,128]{1,0:T(8,128)(2,1)S(1)}, bf16[1040,128]{1,0:T(8,128)(2,1)S(1)}, u32[]{:S(2)}, u32[]{:S(2)}) collective-permute-start(bf16[1040,128]{1,0:T(8,128)(2,1)S(1)} %shard_map.89), channel_id=1, source_target_pairs={{0,1},{1,0},{2,3},{3,2},{4,5},{5,4},{6,7},{7,6},{8,9},{9,8},{10,11... | collective-permute-start | bytes 798728 | tf_op jit(solution)/shard_map/ppermute | solution.py:566
  37.1 2.6 %collective-permute-start.11 = (bf16[1040,128]{1,0:T(8,128)(2,1)S(1)}, bf16[1040,128]{1,0:T(8,128)(2,1)S(1)}, u32[]{:S(2)}, u32[]{:S(2)}) collective-permute-start(bf16[1040,128]{1,0:T(8,128)(2,1)S(1)} %shard_map.88), channel_id=1, source_target_pairs={{0,4},{1,5},{2,6},{3,7},{4,0},{5,1},{6,2},{7,3},{8,12},{9,13},{10,... | collective-permute-start | bytes 798728 | tf_op jit(solution)/shard_map/ppermute | solution.py:566
  39.7 0.0 collective-permute-done.7.refs_0_
  39.7 0.7 %shard_map.90 = bf16[1040,128]{1,0:T(8,128)(2,1)S(1)} custom-call(s32[1]{0:T(128)} %bitcast.place_ref, bf16[8192,1024]{1,0:T(8,128)(2,1)S(1)} %copy-done, bf16[1024,256]{1,0:T(8,128)(2,1)S(1)} %get-tuple-element.36.turned_ref, bf16[1040,128]{1,0:T(8,128)(2,1)S(1)} %collective-permute-done.7.refs_0_), custom_call_target="tpu_custom_call" | custom-call | bytes 1024 | tf_op jit(solution)/shard_map/pallas_call | solution.py:131
  40.4 0.0 copy-start.1
  40.4 0.0 copy-start.2
  40.4 2.7 %collective-permute-start.12 = (bf16[1040,128]{1,0:T(8,128)(2,1)S(1)}, bf16[1040,128]{1,0:T(8,128)(2,1)S(1)}, u32[]{:S(2)}, u32[]{:S(2)}) collective-permute-start(bf16[1040,128]{1,0:T(8,128)(2,1)S(1)} %shard_map.90), channel_id=1, source_target_pairs={{0,2},{1,3},{2,0},{3,1},{4,6},{5,7},{6,4},{7,5},{8,10},{9,11},{10,... | collective-permute-start | bytes 798728 | tf_op jit(solution)/shard_map/ppermute | solution.py:566
  43.1 1.2 %collective-permute-done.8.refs_2_ = bf16[1040,128]{1,0:T(8,128)(2,1)S(1)} collective-permute-done((bf16[1040,128]{1,0:T(8,128)(2,1)S(1)}, bf16[1040,128]{1,0:T(8,128)(2,1)S(1)}, u32[]{:S(2)}, u32[]{:S(2)}) %collective-permute-start.8) | collective-permute-done | bytes 266272 | tf_op jit(solution)/shard_map/ppermute | solution.py:566
  44.3 0.0 collective-permute-done.9.refs_1_
  44.3 0.6 shard_map.91
  44.9 1.3 %collective-permute-start.13 = (bf16[1040,128]{1,0:T(8,128)(2,1)S(1)}, bf16[1040,128]{1,0:T(8,128)(2,1)S(1)}, u32[]{:S(2)}, u32[]{:S(2)}) collective-permute-start(bf16[1040,128]{1,0:T(8,128)(2,1)S(1)} %shard_map.91), channel_id=1, source_target_pairs={{0,1},{1,0},{2,3},{3,2},{4,5},{5,4},{6,7},{7,6},{8,9},{9,8},{10,11... | collective-permute-start | bytes 798728 | tf_op jit(solution)/shard_map/ppermute | solution.py:566
  46.2 0.0 copy-done.3
  46.2 0.0 copy-done.4
  46.3 0.4 shard_map.93.acc_ref
  46.8 0.0 collective-permute-done.10.refs_0_
  46.8 0.0 copy-done.1
  46.9 0.0 copy-done.2
  46.9 1.9 %shard_map.94 = (bf16[256,1024]{1,0:T(8,128)(2,1)}, f32[1088,128]{1,0:T(8,128)S(1)}, f32[16,8,128]{2,1,0:T(8,128)S(1)}, f32[8,8,128]{2,1,0:T(8,128)S(1)}) custom-call(f32[512,256]{1,0:T(8,128)S(1)} %shard_map.93.acc_ref, bf16[1040,128]{1,0:T(8,128)(2,1)S(1)} %collective-permute-done.10.refs_0_, bf16[1040,128]{1,0:T(8,128)(2,1)S(1)} %collective-permute-done.9.refs_1_, ...), custom_call_target="tpu_custom_call" | custom-call | bytes 1024 | tf_op jit(solution)/shard_map/pallas_call | solution.py:300
  48.7 3.4 %collective-permute-done.12.refs_1_ = bf16[1040,128]{1,0:T(8,128)(2,1)S(1)} collective-permute-done((bf16[1040,128]{1,0:T(8,128)(2,1)S(1)}, bf16[1040,128]{1,0:T(8,128)(2,1)S(1)}, u32[]{:S(2)}, u32[]{:S(2)}) %collective-permute-start.12) | collective-permute-done | bytes 266272 | tf_op jit(solution)/shard_map/ppermute | solution.py:566
  52.1 0.0 collective-permute-done.11.refs_2_
  52.1 0.0 collective-permute-done.13.refs_0_
  52.1 1.4 %shard_map.95 = (bf16[256,1024]{1,0:T(8,128)(2,1)}, f32[1088,128]{1,0:T(8,128)S(1)}, f32[16,8,128]{2,1,0:T(8,128)S(1)}, f32[16,8,128]{2,1,0:T(8,128)S(1)}) custom-call(f32[512,256]{1,0:T(8,128)S(1)} %shard_map.80.acc_ref, bf16[1040,128]{1,0:T(8,128)(2,1)S(1)} %collective-permute-done.13.refs_0_, ...), custom_call_target="tpu_custom_call", output_to_operand_aliasing={{0}: (9, {})} | custom-call | bytes 1024 | tf_op jit(solution)/shard_map/pallas_call | solution.py:300
  53.5 0.1 collective-permute-start.14
  53.5 1.2 %collective-permute-done.14.arrived_ref.refs_3_ = f32[16,8,128]{2,1,0:T(8,128)S(1)} collective-permute-done((f32[16,8,128]{2,1,0:T(8,128)S(1)}, f32[16,8,128]{2,1,0:T(8,128)S(1)}, u32[]{:S(2)}, u32[]{:S(2)}) %collective-permute-start.14) | collective-permute-done | bytes 65568 | tf_op jit(solution)/shard_map/ppermute | solution.py:603
  54.8 0.6 %shard_map.96 = (f32[16,8,128]{2,1,0:T(8,128)}, bf16[144,128]{1,0:T(8,128)(2,1)S(1)}) custom-call(s32[1]{0:T(128)} %bitcast.5.group_ref, f32[16,8,128]{2,1,0:T(8,128)S(1)} %get-tuple-element.60.state_ref, f32[16,8,128]{2,1,0:T(8,128)S(1)} %collective-permute-done.14.arrived_ref.refs_3_, f32[16,8,128]{2,1,0:T(8,128)S(1)} %get-tuple-element.51.wide_ref.refs_7_), custom_call_target="tpu_custom_call" | custom-call | bytes 1024 | tf_op jit(solution)/shard_map/pallas_call | solution.py:418
  55.4 1.5 %collective-permute-start.15 = (bf16[144,128]{1,0:T(8,128)(2,1)S(1)}, bf16[144,128]{1,0:T(8,128)(2,1)S(1)}, u32[]{:S(2)}, u32[]{:S(2)}) collective-permute-start(bf16[144,128]{1,0:T(8,128)(2,1)S(1)} %get-tuple-element.62), channel_id=1, source_target_pairs={{0,16},{8,24},{16,0},{24,8},{1,17},{9,25},{17,1},{25,9},{2,18},{10... | collective-permute-start | bytes 110600 | tf_op jit(solution)/shard_map/ppermute | solution.py:603
  56.9 1.2 %shard_map.97.refs_1_ = f32[1088,128]{1,0:T(8,128)S(1)} custom-call(f32[1088,128]{1,0:T(8,128)S(1)} %get-tuple-element.63.gc_ref, f32[16,8,128]{2,1,0:T(8,128)S(1)} %get-tuple-element.64.state_ref, f32[16,16,128]{2,1,0:T(8,128)S(1)} %bitcast.13, f32[16,16,128]{2,1,0:T(8,128)S(1)} %get-tuple-element.53.refs_6_.lap_ref, f32[16,16,128]{2,1,0:T(8,128)S(1)} %bitcast.16), custom_call_target="tpu_custom_call" | custom-call | bytes 1024 | tf_op jit(solution)/shard_map/pallas_call | solution.py:350
  58.1 1.3 %collective-permute-done.15.refs_4_ = bf16[144,128]{1,0:T(8,128)(2,1)S(1)} collective-permute-done((bf16[144,128]{1,0:T(8,128)(2,1)S(1)}, bf16[144,128]{1,0:T(8,128)(2,1)S(1)}, u32[]{:S(2)}, u32[]{:S(2)}) %collective-permute-start.15) | collective-permute-done | bytes 36896 | tf_op jit(solution)/shard_map/ppermute | solution.py:603
  59.4 2.2 %shard_map.98 = bf16[256,1024]{1,0:T(8,128)(2,1)} custom-call(s32[1]{0:T(128)} %bitcast.5.group_ref, f32[1088,128]{1,0:T(8,128)S(1)} %get-tuple-element.58.refs_0_, f32[1088,128]{1,0:T(8,128)S(1)} %shard_map.97.refs_1_, f32[16,8,128]{2,1,0:T(8,128)S(1)} %get-tuple-element.65.refs_2_, f32[16,8,128]{2,1,0:T(8,128)S(1)} %collective-permute-done.14.arrived_ref.refs_3_, ...), custom_call_target="tpu_custom_call" | custom-call | bytes 1024 | tf_op jit(solution)/shard_map/pallas_call | solution.py:486
  (5 shorter events, 0.2 us)
Async XLA Ops:
  0.6 6.2 %copy-start = (bf16[8192,1024]{1,0:T(8,128)(2,1)S(1)}, bf16[8192,1024]{1,0:T(8,128)(2,1)}, u32[]{:S(2)}) copy-start(bf16[8192,1024]{1,0:T(8,128)(2,1)} %w_ref.29) | copy-start | bytes 50331652
  3.0 11.4 %collective-permute-start = (bf16[1040,128]{1,0:T(8,128)(2,1)S(1)}, bf16[1040,128]{1,0:T(8,128)(2,1)S(1)}, u32[]{:S(2)}, u32[]{:S(2)}) collective-permute-start(bf16[1040,128]{1,0:T(8,128)(2,1)S(1)} %get-tuple-element.34), channel_id=1, source_target_pairs={{0,1},{1,0},{2,3},{3,2},{4,5},{5,4},{6,7},{7,6},{8,9},{9,8},{10,11... | collective-permute-start | bytes 798728 | tf_op jit(solution)/shard_map/ppermute | solution.py:566
  7.5 9.9 %collective-permute-start.1 = (bf16[1040,128]{1,0:T(8,128)(2,1)S(1)}, bf16[1040,128]{1,0:T(8,128)(2,1)S(1)}, u32[]{:S(2)}, u32[]{:S(2)}) collective-permute-start(bf16[1040,128]{1,0:T(8,128)(2,1)S(1)} %shard_map.78), channel_id=1, source_target_pairs={{0,2},{1,3},{2,0},{3,1},{4,6},{5,7},{6,4},{7,5},{8,10},{9,11},{10,... | collective-permute-start | bytes 798728 | tf_op jit(solution)/shard_map/ppermute | solution.py:566
  12.2 8.4 %collective-permute-start.2 = (bf16[1040,128]{1,0:T(8,128)(2,1)S(1)}, bf16[1040,128]{1,0:T(8,128)(2,1)S(1)}, u32[]{:S(2)}, u32[]{:S(2)}) collective-permute-start(bf16[1040,128]{1,0:T(8,128)(2,1)S(1)} %shard_map.81), channel_id=1, source_target_pairs={{0,1},{1,0},{2,3},{3,2},{4,5},{5,4},{6,7},{7,6},{8,9},{9,8},{10,11... | collective-permute-start | bytes 798728 | tf_op jit(solution)/shard_map/ppermute | solution.py:566
  15.1 9.8 %collective-permute-start.3 = (bf16[1040,128]{1,0:T(8,128)(2,1)S(1)}, bf16[1040,128]{1,0:T(8,128)(2,1)S(1)}, u32[]{:S(2)}, u32[]{:S(2)}) collective-permute-start(bf16[1040,128]{1,0:T(8,128)(2,1)S(1)} %shard_map.83), channel_id=1, source_target_pairs={{0,2},{1,3},{2,0},{3,1},{4,6},{5,7},{6,4},{7,5},{8,10},{9,11},{10,... | collective-permute-start | bytes 798728 | tf_op jit(solution)/shard_map/ppermute | solution.py:566
  18.0 9.7 %collective-permute-start.4 = (bf16[1040,128]{1,0:T(8,128)(2,1)S(1)}, bf16[1040,128]{1,0:T(8,128)(2,1)S(1)}, u32[]{:S(2)}, u32[]{:S(2)}) collective-permute-start(bf16[1040,128]{1,0:T(8,128)(2,1)S(1)} %shard_map.84), channel_id=1, source_target_pairs={{0,1},{1,0},{2,3},{3,2},{4,5},{5,4},{6,7},{7,6},{8,9},{9,8},{10,11... | collective-permute-start | bytes 798728 | tf_op jit(solution)/shard_map/ppermute | solution.py:566
  20.4 13.1 %collective-permute-start.5 = (bf16[1040,128]{1,0:T(8,128)(2,1)S(1)}, bf16[1040,128]{1,0:T(8,128)(2,1)S(1)}, u32[]{:S(2)}, u32[]{:S(2)}) collective-permute-start(bf16[1040,128]{1,0:T(8,128)(2,1)S(1)} %shard_map.82), channel_id=1, source_target_pairs={{0,1},{1,0},{2,3},{3,2},{4,5},{5,4},{6,7},{7,6},{8,9},{9,8},{10,11... | collective-permute-start | bytes 798728 | tf_op jit(solution)/shard_map/ppermute | solution.py:566
  21.4 12.1 %collective-permute-start.6 = (bf16[1040,128]{1,0:T(8,128)(2,1)S(1)}, bf16[1040,128]{1,0:T(8,128)(2,1)S(1)}, u32[]{:S(2)}, u32[]{:S(2)}) collective-permute-start(bf16[1040,128]{1,0:T(8,128)(2,1)S(1)} %shard_map.85), channel_id=1, source_target_pairs={{0,2},{1,3},{2,0},{3,1},{4,6},{5,7},{6,4},{7,5},{8,10},{9,11},{10,... | collective-permute-start | bytes 798728 | tf_op jit(solution)/shard_map/ppermute | solution.py:566
  23.4 16.3 %collective-permute-start.7 = (bf16[1040,128]{1,0:T(8,128)(2,1)S(1)}, bf16[1040,128]{1,0:T(8,128)(2,1)S(1)}, u32[]{:S(2)}, u32[]{:S(2)}) collective-permute-start(bf16[1040,128]{1,0:T(8,128)(2,1)S(1)} %shard_map.79), channel_id=1, source_target_pairs={{0,1},{1,0},{2,3},{3,2},{4,5},{5,4},{6,7},{7,6},{8,9},{9,8},{10,11... | collective-permute-start | bytes 798728 | tf_op jit(solution)/shard_map/ppermute | solution.py:566
  28.6 15.7 %collective-permute-start.8 = (bf16[1040,128]{1,0:T(8,128)(2,1)S(1)}, bf16[1040,128]{1,0:T(8,128)(2,1)S(1)}, u32[]{:S(2)}, u32[]{:S(2)}) collective-permute-start(bf16[1040,128]{1,0:T(8,128)(2,1)S(1)} %shard_map.87), channel_id=1, source_target_pairs={{0,4},{1,5},{2,6},{3,7},{4,0},{5,1},{6,2},{7,3},{8,12},{9,13},{10,... | collective-permute-start | bytes 798728 | tf_op jit(solution)/shard_map/ppermute | solution.py:566
  31.3 13.0 %collective-permute-start.9 = (bf16[1040,128]{1,0:T(8,128)(2,1)S(1)}, bf16[1040,128]{1,0:T(8,128)(2,1)S(1)}, u32[]{:S(2)}, u32[]{:S(2)}) collective-permute-start(bf16[1040,128]{1,0:T(8,128)(2,1)S(1)} %shard_map.86), channel_id=1, source_target_pairs={{0,2},{1,3},{2,0},{3,1},{4,6},{5,7},{6,4},{7,5},{8,10},{9,11},{10,... | collective-permute-start | bytes 798728 | tf_op jit(solution)/shard_map/ppermute | solution.py:566
  35.0 11.2 %copy-start.3 = (f32[1024,16]{0,1:T(8,128)S(1)}, f32[1024,16]{0,1:T(8,128)}, u32[]{:S(2)}) copy-start(f32[1024,16]{0,1:T(8,128)} %param.10) | copy-start | bytes 196612
  35.0 11.2 %copy-start.4 = (f32[1024,16]{0,1:T(8,128)S(1)}, f32[1024,16]{0,1:T(8,128)}, u32[]{:S(2)}) copy-start(f32[1024,16]{0,1:T(8,128)} %param.11) | copy-start | bytes 196612
  35.1 11.7 %collective-permute-start.10 = (bf16[1040,128]{1,0:T(8,128)(2,1)S(1)}, bf16[1040,128]{1,0:T(8,128)(2,1)S(1)}, u32[]{:S(2)}, u32[]{:S(2)}) collective-permute-start(bf16[1040,128]{1,0:T(8,128)(2,1)S(1)} %shard_map.89), channel_id=1, source_target_pairs={{0,1},{1,0},{2,3},{3,2},{4,5},{5,4},{6,7},{7,6},{8,9},{9,8},{10,11... | collective-permute-start | bytes 798728 | tf_op jit(solution)/shard_map/ppermute | solution.py:566
  37.1 15.0 %collective-permute-start.11 = (bf16[1040,128]{1,0:T(8,128)(2,1)S(1)}, bf16[1040,128]{1,0:T(8,128)(2,1)S(1)}, u32[]{:S(2)}, u32[]{:S(2)}) collective-permute-start(bf16[1040,128]{1,0:T(8,128)(2,1)S(1)} %shard_map.88), channel_id=1, source_target_pairs={{0,4},{1,5},{2,6},{3,7},{4,0},{5,1},{6,2},{7,3},{8,12},{9,13},{10,... | collective-permute-start | bytes 798728 | tf_op jit(solution)/shard_map/ppermute | solution.py:566
  40.4 6.4 %copy-start.1 = (bf16[256,1024]{1,0:T(8,128)(2,1)S(1)}, bf16[256,1024]{1,0:T(8,128)(2,1)}, u32[]{:S(2)}) copy-start(bf16[256,1024]{1,0:T(8,128)(2,1)} %refs_3_.3) | copy-start | bytes 1572868
  40.4 6.4 %copy-start.2 = (bf16[256,1024]{1,0:T(8,128)(2,1)S(1)}, bf16[256,1024]{1,0:T(8,128)(2,1)}, u32[]{:S(2)}) copy-start(bf16[256,1024]{1,0:T(8,128)(2,1)} %refs_4_.3) | copy-start | bytes 1572868
  40.4 11.7 %collective-permute-start.12 = (bf16[1040,128]{1,0:T(8,128)(2,1)S(1)}, bf16[1040,128]{1,0:T(8,128)(2,1)S(1)}, u32[]{:S(2)}, u32[]{:S(2)}) collective-permute-start(bf16[1040,128]{1,0:T(8,128)(2,1)S(1)} %shard_map.90), channel_id=1, source_target_pairs={{0,2},{1,3},{2,0},{3,1},{4,6},{5,7},{6,4},{7,5},{8,10},{9,11},{10,... | collective-permute-start | bytes 798728 | tf_op jit(solution)/shard_map/ppermute | solution.py:566
  44.9 7.2 %collective-permute-start.13 = (bf16[1040,128]{1,0:T(8,128)(2,1)S(1)}, bf16[1040,128]{1,0:T(8,128)(2,1)S(1)}, u32[]{:S(2)}, u32[]{:S(2)}) collective-permute-start(bf16[1040,128]{1,0:T(8,128)(2,1)S(1)} %shard_map.91), channel_id=1, source_target_pairs={{0,1},{1,0},{2,3},{3,2},{4,5},{5,4},{6,7},{7,6},{8,9},{9,8},{10,11... | collective-permute-start | bytes 798728 | tf_op jit(solution)/shard_map/ppermute | solution.py:566
  53.5 1.3 %collective-permute-start.14 = (f32[16,8,128]{2,1,0:T(8,128)S(1)}, f32[16,8,128]{2,1,0:T(8,128)S(1)}, u32[]{:S(2)}, u32[]{:S(2)}) collective-permute-start(f32[16,8,128]{2,1,0:T(8,128)S(1)} %get-tuple-element.60.state_ref), channel_id=1, source_target_pairs={{0,8},{8,0},{16,24},{24,16},{1,9},{9,1},{17,25},{25,17},{2,10},{10... | collective-permute-start | bytes 196616 | tf_op jit(solution)/shard_map/ppermute | solution.py:603
  55.4 4.0 %collective-permute-start.15 = (bf16[144,128]{1,0:T(8,128)(2,1)S(1)}, bf16[144,128]{1,0:T(8,128)(2,1)S(1)}, u32[]{:S(2)}, u32[]{:S(2)}) collective-permute-start(bf16[144,128]{1,0:T(8,128)(2,1)S(1)} %get-tuple-element.62), channel_id=1, source_target_pairs={{0,16},{8,24},{16,0},{24,8},{1,17},{9,25},{17,1},{25,9},{2,18},{10... | collective-permute-start | bytes 110600 | tf_op jit(solution)/shard_map/ppermute | solution.py:603

commit v14 on v13

--- a/solution.py
+++ b/solution.py
@@ -398,7 +398,7 @@
     return [rows[m * sublanes : (m + 1) * sublanes, :] for m in range(packs)]
 
 
-def join_kernel(round_, group_ref, state_ref, arrived_ref, wide_ref, out_ref, coded_ref):
+def join_kernel(round_, group_ref, state_ref, arrived_ref, wide_ref, coded_ref, *out_refs):
     earlier = (group_ref[0] >> round_) % 2 == 0
     packs, sublanes, _ = state_ref.shape
     joined = []
@@ -406,23 +406,24 @@
         wide = power(wide_ref[m], 1 << round_)
         mine = state_ref[m]
         joined.append(jnp.where(earlier, mine + wide * other, other + wide * mine))
-        out_ref[m] = joined[-1]
+        for out_ref in out_refs:
+            out_ref[m] = joined[-1]
     codes, peaks = encode(jnp.concatenate(joined, axis=0), packs * sublanes // 2)
     put(codes, coded_ref, 0)
     put_peaks(peaks, coded_ref)
 
 
-def join(round_, group, state, arrived, wide):
+def join(round_, group, state, arrived, wide, last):
     vmem = pl.BlockSpec(memory_space=pltpu.VMEM)
     packs, sublanes, lanes = state.shape
     return pl.pallas_call(
         functools.partial(join_kernel, round_),
         in_specs=[pl.BlockSpec(memory_space=pltpu.SMEM)] + [vmem] * 3,
-        out_specs=(vmem, vmem),
-        out_shape=(
+        out_specs=[vmem] * (1 if last else 2),
+        out_shape=[
+            jax.ShapeDtypeStruct((packs * sublanes + PEAKS, lanes), jnp.bfloat16),
             jax.ShapeDtypeStruct(state.shape, jnp.float32),
-            jax.ShapeDtypeStruct((packs * sublanes + PEAKS, lanes), jnp.bfloat16),
-        ),
+        ][: 1 if last else 2],
         compiler_params=pltpu.CompilerParams(vmem_limit_bytes=VMEM),
         cost_estimate=QUICK,
     )(group, state, arrived, wide)
@@ -602,8 +603,10 @@
             groups = lax.axis_size("ctx")
             swap = lambda array, round_: lax.ppermute(array, "ctx", [(i, i ^ (1 << round_)) for i in range(groups)])
             arrived, joined = [swap(packed[1], 0)], packed[1]
-            for round_ in range(1, groups.bit_length() - 1):
-                joined, last = join(round_ - 1, after(group), joined, arrived[-1], wide)
+            rounds = groups.bit_length() - 1
+            for round_ in range(1, rounds):
+                last, *joined = join(round_ - 1, after(group), joined, arrived[-1], wide, round_ + 1 == rounds)
+                joined = joined[0] if joined else None
                 arrived.append(swap(last, round_))
             scanned[1] = scan(1, segments, after(scanned[1]), states[1], decay, lap, residue)
         else:

time: 61.8 us -> 61.2 us (level)
  no operation moved by 1% of the time
where the time goes in v14:
time: 61.2 us; the launch traced here: 61.1 us
  starting transfers between devices  29.2 us (48%)
  Pallas kernels  18.8 us (31%)
  waiting for transfers between devices  11.2 us (18%)
  local copies, waits for them, and re-layouts  0.96 us (2%)
  between operations  0.92 us (2%)
    ppermute x14, starting transfers between devices, local(): arrived = lax.ppermute(last, 'ch', [(i, i ^ bit) for i in range(size)])  27.6 us
    pallas_call x15, Pallas kernels, send(): pl.pallas_call(functools.partial(send_kernel, items, coded, width, len(ne...  9.7 us
    ppermute x14, waiting for transfers between devices, local(): arrived = lax.ppermute(last, 'ch', [(i, i ^ bit) for i in range(size)])  8.68 us
    pallas_call x2, Pallas kernels, gate(): pl.pallas_call(functools.partial(gate_kernel, half, rows, segments, piece...  3.2 us
    ppermute x2, waiting for transfers between devices, local(): lax.ppermute(array, 'ctx', [(i, i ^ 1 << round_) for i in range(groups)])  2.53 us
    pallas_call x1, Pallas kernels, first_send(): pl.pallas_call(functools.partial(first_kernel, items, width), in_specs=[p...  2.38 us
    pallas_call x1, Pallas kernels, fix(): pl.pallas_call(functools.partial(fix_kernel, segments, len(arrived)), in_...  2.23 us
    ppermute x2, starting transfers between devices, local(): lax.ppermute(array, 'ctx', [(i, i ^ 1 << round_) for i in range(groups)])  1.63 us
  transfers between devices with their start and end apart: 16, of which 7 were waited for; matrix products, arithmetic and copies ran while one was open for 0% of the time, Pallas kernels for 21%

profile of v14, /device:TPU:0, one launch (start us, length us, event | category | flops | bytes accessed | tf_op | source)
XLA Modules:
  0.0 61.1 jit_solution(3840530507801165692)
XLA Ops:
  0.6 0.0 copy-start
  0.6 2.4 %shard_map.77 = (bf16[1040,128]{1,0:T(8,128)(2,1)S(1)}, bf16[1024,256]{1,0:T(8,128)(2,1)S(1)}) custom-call(s32[1]{0:T(128)} %bitcast.place_ref, bf16[8192,1024]{1,0:T(8,128)(2,1)} %w_ref.29, bf16[256,1024]{1,0:T(8,128)(2,1)} %g_hbm.1), custom_call_target="tpu_custom_call" | custom-call | bytes 1024 | tf_op jit(solution)/shard_map/pallas_call | solution.py:184
  3.0 3.0 %collective-permute-start = (bf16[1040,128]{1,0:T(8,128)(2,1)S(1)}, bf16[1040,128]{1,0:T(8,128)(2,1)S(1)}, u32[]{:S(2)}, u32[]{:S(2)}) collective-permute-start(bf16[1040,128]{1,0:T(8,128)(2,1)S(1)} %get-tuple-element.33), channel_id=1, source_target_pairs={{0,1},{1,0},{2,3},{3,2},{4,5},{5,4},{6,7},{7,6},{8,9},{9,8},{10,11... | collective-permute-start | bytes 798728 | tf_op jit(solution)/shard_map/ppermute | solution.py:567
  6.1 0.8 %copy-done = bf16[8192,1024]{1,0:T(8,128)(2,1)S(1)} copy-done((bf16[8192,1024]{1,0:T(8,128)(2,1)S(1)}, bf16[8192,1024]{1,0:T(8,128)(2,1)}, u32[]{:S(2)}) %copy-start) | copy-done | bytes 16777240
  6.9 0.6 shard_map.78
  7.5 3.1 %collective-permute-start.1 = (bf16[1040,128]{1,0:T(8,128)(2,1)S(1)}, bf16[1040,128]{1,0:T(8,128)(2,1)S(1)}, u32[]{:S(2)}, u32[]{:S(2)}) collective-permute-start(bf16[1040,128]{1,0:T(8,128)(2,1)S(1)} %shard_map.78), channel_id=1, source_target_pairs={{0,2},{1,3},{2,0},{3,1},{4,6},{5,7},{6,4},{7,5},{8,10},{9,11},{10,... | collective-permute-start | bytes 798728 | tf_op jit(solution)/shard_map/ppermute | solution.py:567
  10.6 0.6 shard_map.79
  11.2 0.4 shard_map.80.acc_ref
  11.6 0.6 shard_map.81
  12.2 1.6 %collective-permute-start.2 = (bf16[1040,128]{1,0:T(8,128)(2,1)S(1)}, bf16[1040,128]{1,0:T(8,128)(2,1)S(1)}, u32[]{:S(2)}, u32[]{:S(2)}) collective-permute-start(bf16[1040,128]{1,0:T(8,128)(2,1)S(1)} %shard_map.81), channel_id=1, source_target_pairs={{0,1},{1,0},{2,3},{3,2},{4,5},{5,4},{6,7},{7,6},{8,9},{9,8},{10,11... | collective-permute-start | bytes 798728 | tf_op jit(solution)/shard_map/ppermute | solution.py:567
  13.8 0.6 shard_map.82
  14.4 0.0 collective-permute-done.refs_0_
  14.4 0.7 %shard_map.83 = bf16[1040,128]{1,0:T(8,128)(2,1)S(1)} custom-call(s32[1]{0:T(128)} %bitcast.place_ref, bf16[8192,1024]{1,0:T(8,128)(2,1)S(1)} %copy-done, bf16[1024,256]{1,0:T(8,128)(2,1)S(1)} %get-tuple-element.35.turned_ref, bf16[1040,128]{1,0:T(8,128)(2,1)S(1)} %collective-permute-done.refs_0_), custom_call_target="tpu_custom_call" | custom-call | bytes 1024 | tf_op jit(solution)/shard_map/pallas_call | solution.py:131
  15.1 0.5 collective-permute-start.3
  15.6 1.8 %collective-permute-done.1.refs_0_ = bf16[1040,128]{1,0:T(8,128)(2,1)S(1)} collective-permute-done((bf16[1040,128]{1,0:T(8,128)(2,1)S(1)}, bf16[1040,128]{1,0:T(8,128)(2,1)S(1)}, u32[]{:S(2)}, u32[]{:S(2)}) %collective-permute-start.1) | collective-permute-done | bytes 266272 | tf_op jit(solution)/shard_map/ppermute | solution.py:567
  17.4 0.6 %shard_map.84 = bf16[1040,128]{1,0:T(8,128)(2,1)S(1)} custom-call(s32[1]{0:T(128)} %bitcast.place_ref, bf16[8192,1024]{1,0:T(8,128)(2,1)S(1)} %copy-done, bf16[1024,256]{1,0:T(8,128)(2,1)S(1)} %get-tuple-element.35.turned_ref, bf16[1040,128]{1,0:T(8,128)(2,1)S(1)} %collective-permute-done.1.refs_0_), custom_call_target="tpu_custom_call" | custom-call | bytes 1024 | tf_op jit(solution)/shard_map/pallas_call | solution.py:131
  18.0 2.4 %collective-permute-start.4 = (bf16[1040,128]{1,0:T(8,128)(2,1)S(1)}, bf16[1040,128]{1,0:T(8,128)(2,1)S(1)}, u32[]{:S(2)}, u32[]{:S(2)}) collective-permute-start(bf16[1040,128]{1,0:T(8,128)(2,1)S(1)} %shard_map.84), channel_id=1, source_target_pairs={{0,1},{1,0},{2,3},{3,2},{4,5},{5,4},{6,7},{7,6},{8,9},{9,8},{10,11... | collective-permute-start | bytes 798728 | tf_op jit(solution)/shard_map/ppermute | solution.py:567
  20.4 0.1 collective-permute-start.5
  20.5 0.2 collective-permute-done.2.refs_0_
  20.7 0.7 %shard_map.85 = bf16[1040,128]{1,0:T(8,128)(2,1)S(1)} custom-call(s32[1]{0:T(128)} %bitcast.place_ref, bf16[8192,1024]{1,0:T(8,128)(2,1)S(1)} %copy-done, bf16[1024,256]{1,0:T(8,128)(2,1)S(1)} %get-tuple-element.35.turned_ref, bf16[1040,128]{1,0:T(8,128)(2,1)S(1)} %collective-permute-done.2.refs_0_), custom_call_target="tpu_custom_call" | custom-call | bytes 1024 | tf_op jit(solution)/shard_map/pallas_call | solution.py:131
  21.4 2.0 %collective-permute-start.6 = (bf16[1040,128]{1,0:T(8,128)(2,1)S(1)}, bf16[1040,128]{1,0:T(8,128)(2,1)S(1)}, u32[]{:S(2)}, u32[]{:S(2)}) collective-permute-start(bf16[1040,128]{1,0:T(8,128)(2,1)S(1)} %shard_map.85), channel_id=1, source_target_pairs={{0,2},{1,3},{2,0},{3,1},{4,6},{5,7},{6,4},{7,5},{8,10},{9,11},{10,... | collective-permute-start | bytes 798728 | tf_op jit(solution)/shard_map/ppermute | solution.py:567
  23.4 1.5 %collective-permute-start.7 = (bf16[1040,128]{1,0:T(8,128)(2,1)S(1)}, bf16[1040,128]{1,0:T(8,128)(2,1)S(1)}, u32[]{:S(2)}, u32[]{:S(2)}) collective-permute-start(bf16[1040,128]{1,0:T(8,128)(2,1)S(1)} %shard_map.79), channel_id=1, source_target_pairs={{0,1},{1,0},{2,3},{3,2},{4,5},{5,4},{6,7},{7,6},{8,9},{9,8},{10,11... | collective-permute-start | bytes 798728 | tf_op jit(solution)/shard_map/ppermute | solution.py:567
  24.9 0.0 collective-permute-done.3.refs_1_
  24.9 0.7 %shard_map.86 = bf16[1040,128]{1,0:T(8,128)(2,1)S(1)} custom-call(s32[1]{0:T(128)} %bitcast.place_ref, bf16[8192,1024]{1,0:T(8,128)(2,1)S(1)} %copy-done, bf16[1024,256]{1,0:T(8,128)(2,1)S(1)} %get-tuple-element.35.turned_ref, bf16[1040,128]{1,0:T(8,128)(2,1)S(1)} %collective-permute-done.refs_0_), custom_call_target="tpu_custom_call" | custom-call | bytes 1024 | tf_op jit(solution)/shard_map/pallas_call | solution.py:131
  25.6 2.1 %collective-permute-done.4.refs_0_ = bf16[1040,128]{1,0:T(8,128)(2,1)S(1)} collective-permute-done((bf16[1040,128]{1,0:T(8,128)(2,1)S(1)}, bf16[1040,128]{1,0:T(8,128)(2,1)S(1)}, u32[]{:S(2)}, u32[]{:S(2)}) %collective-permute-start.4) | collective-permute-done | bytes 266272 | tf_op jit(solution)/shard_map/ppermute | solution.py:567
  27.7 0.9 %shard_map.87 = bf16[1040,128]{1,0:T(8,128)(2,1)S(1)} custom-call(s32[1]{0:T(128)} %bitcast.place_ref, bf16[8192,1024]{1,0:T(8,128)(2,1)S(1)} %copy-done, bf16[1024,256]{1,0:T(8,128)(2,1)S(1)} %get-tuple-element.35.turned_ref, bf16[1040,128]{1,0:T(8,128)(2,1)S(1)} %collective-permute-done.4.refs_0_, bf16[1040,128]{1,0:T(8,128)(2,1)S(1)} %collective-permute-done.3.refs_1_), custom_call_target="tpu_custom_call" | custom-call | bytes 1024 | tf_op jit(solution)/shard_map/pallas_call | solution.py:131
  28.6 2.7 %collective-permute-start.8 = (bf16[1040,128]{1,0:T(8,128)(2,1)S(1)}, bf16[1040,128]{1,0:T(8,128)(2,1)S(1)}, u32[]{:S(2)}, u32[]{:S(2)}) collective-permute-start(bf16[1040,128]{1,0:T(8,128)(2,1)S(1)} %shard_map.87), channel_id=1, source_target_pairs={{0,4},{1,5},{2,6},{3,7},{4,0},{5,1},{6,2},{7,3},{8,12},{9,13},{10,... | collective-permute-start | bytes 798728 | tf_op jit(solution)/shard_map/ppermute | solution.py:567
  31.3 2.2 %collective-permute-start.9 = (bf16[1040,128]{1,0:T(8,128)(2,1)S(1)}, bf16[1040,128]{1,0:T(8,128)(2,1)S(1)}, u32[]{:S(2)}, u32[]{:S(2)}) collective-permute-start(bf16[1040,128]{1,0:T(8,128)(2,1)S(1)} %shard_map.86), channel_id=1, source_target_pairs={{0,2},{1,3},{2,0},{3,1},{4,6},{5,7},{6,4},{7,5},{8,10},{9,11},{10,... | collective-permute-start | bytes 798728 | tf_op jit(solution)/shard_map/ppermute | solution.py:567
  33.5 0.0 collective-permute-done.5.refs_0_
  33.5 0.0 collective-permute-done.6.refs_1_
  33.5 0.9 %shard_map.88 = bf16[1040,128]{1,0:T(8,128)(2,1)S(1)} custom-call(s32[1]{0:T(128)} %bitcast.place_ref, bf16[8192,1024]{1,0:T(8,128)(2,1)S(1)} %copy-done, bf16[1024,256]{1,0:T(8,128)(2,1)S(1)} %get-tuple-element.35.turned_ref, bf16[1040,128]{1,0:T(8,128)(2,1)S(1)} %collective-permute-done.5.refs_0_, bf16[1040,128]{1,0:T(8,128)(2,1)S(1)} %collective-permute-done.6.refs_1_), custom_call_target="tpu_custom_call" | custom-call | bytes 1024 | tf_op jit(solution)/shard_map/pallas_call | solution.py:131
  34.4 0.7 %shard_map.89 = bf16[1040,128]{1,0:T(8,128)(2,1)S(1)} custom-call(s32[1]{0:T(128)} %bitcast.place_ref, bf16[8192,1024]{1,0:T(8,128)(2,1)S(1)} %copy-done, bf16[1024,256]{1,0:T(8,128)(2,1)S(1)} %get-tuple-element.35.turned_ref, bf16[1040,128]{1,0:T(8,128)(2,1)S(1)} %collective-permute-done.1.refs_0_), custom_call_target="tpu_custom_call" | custom-call | bytes 1024 | tf_op jit(solution)/shard_map/pallas_call | solution.py:131
  35.0 0.0 copy-start.3
  35.0 0.0 copy-start.4
  35.1 2.0 %collective-permute-start.10 = (bf16[1040,128]{1,0:T(8,128)(2,1)S(1)}, bf16[1040,128]{1,0:T(8,128)(2,1)S(1)}, u32[]{:S(2)}, u32[]{:S(2)}) collective-permute-start(bf16[1040,128]{1,0:T(8,128)(2,1)S(1)} %shard_map.89), channel_id=1, source_target_pairs={{0,1},{1,0},{2,3},{3,2},{4,5},{5,4},{6,7},{7,6},{8,9},{9,8},{10,11... | collective-permute-start | bytes 798728 | tf_op jit(solution)/shard_map/ppermute | solution.py:567
  37.1 2.6 %collective-permute-start.11 = (bf16[1040,128]{1,0:T(8,128)(2,1)S(1)}, bf16[1040,128]{1,0:T(8,128)(2,1)S(1)}, u32[]{:S(2)}, u32[]{:S(2)}) collective-permute-start(bf16[1040,128]{1,0:T(8,128)(2,1)S(1)} %shard_map.88), channel_id=1, source_target_pairs={{0,4},{1,5},{2,6},{3,7},{4,0},{5,1},{6,2},{7,3},{8,12},{9,13},{10,... | collective-permute-start | bytes 798728 | tf_op jit(solution)/shard_map/ppermute | solution.py:567
  39.7 0.0 collective-permute-done.7.refs_0_
  39.7 0.7 %shard_map.90 = bf16[1040,128]{1,0:T(8,128)(2,1)S(1)} custom-call(s32[1]{0:T(128)} %bitcast.place_ref, bf16[8192,1024]{1,0:T(8,128)(2,1)S(1)} %copy-done, bf16[1024,256]{1,0:T(8,128)(2,1)S(1)} %get-tuple-element.35.turned_ref, bf16[1040,128]{1,0:T(8,128)(2,1)S(1)} %collective-permute-done.7.refs_0_), custom_call_target="tpu_custom_call" | custom-call | bytes 1024 | tf_op jit(solution)/shard_map/pallas_call | solution.py:131
  40.4 0.0 copy-start.1
  40.4 0.0 copy-start.2
  40.4 2.7 %collective-permute-start.12 = (bf16[1040,128]{1,0:T(8,128)(2,1)S(1)}, bf16[1040,128]{1,0:T(8,128)(2,1)S(1)}, u32[]{:S(2)}, u32[]{:S(2)}) collective-permute-start(bf16[1040,128]{1,0:T(8,128)(2,1)S(1)} %shard_map.90), channel_id=1, source_target_pairs={{0,2},{1,3},{2,0},{3,1},{4,6},{5,7},{6,4},{7,5},{8,10},{9,11},{10,... | collective-permute-start | bytes 798728 | tf_op jit(solution)/shard_map/ppermute | solution.py:567
  43.1 1.2 %collective-permute-done.8.refs_2_ = bf16[1040,128]{1,0:T(8,128)(2,1)S(1)} collective-permute-done((bf16[1040,128]{1,0:T(8,128)(2,1)S(1)}, bf16[1040,128]{1,0:T(8,128)(2,1)S(1)}, u32[]{:S(2)}, u32[]{:S(2)}) %collective-permute-start.8) | collective-permute-done | bytes 266272 | tf_op jit(solution)/shard_map/ppermute | solution.py:567
  44.3 0.0 collective-permute-done.9.refs_1_
  44.3 0.6 shard_map.91
  44.9 1.3 %collective-permute-start.13 = (bf16[1040,128]{1,0:T(8,128)(2,1)S(1)}, bf16[1040,128]{1,0:T(8,128)(2,1)S(1)}, u32[]{:S(2)}, u32[]{:S(2)}) collective-permute-start(bf16[1040,128]{1,0:T(8,128)(2,1)S(1)} %shard_map.91), channel_id=1, source_target_pairs={{0,1},{1,0},{2,3},{3,2},{4,5},{5,4},{6,7},{7,6},{8,9},{9,8},{10,11... | collective-permute-start | bytes 798728 | tf_op jit(solution)/shard_map/ppermute | solution.py:567
  46.2 0.0 copy-done.3
  46.2 0.0 copy-done.4
  46.3 0.4 shard_map.93.acc_ref
  46.8 0.0 collective-permute-done.10.refs_0_
  46.8 0.0 copy-done.1
  46.9 0.0 copy-done.2
  46.9 1.9 %shard_map.94 = (bf16[256,1024]{1,0:T(8,128)(2,1)}, f32[1088,128]{1,0:T(8,128)S(1)}, f32[16,8,128]{2,1,0:T(8,128)S(1)}, f32[8,8,128]{2,1,0:T(8,128)S(1)}) custom-call(f32[512,256]{1,0:T(8,128)S(1)} %shard_map.93.acc_ref, bf16[1040,128]{1,0:T(8,128)(2,1)S(1)} %collective-permute-done.10.refs_0_, bf16[1040,128]{1,0:T(8,128)(2,1)S(1)} %collective-permute-done.9.refs_1_, ...), custom_call_target="tpu_custom_call" | custom-call | bytes 1024 | tf_op jit(solution)/shard_map/pallas_call | solution.py:300
  48.7 3.4 %collective-permute-done.12.refs_1_ = bf16[1040,128]{1,0:T(8,128)(2,1)S(1)} collective-permute-done((bf16[1040,128]{1,0:T(8,128)(2,1)S(1)}, bf16[1040,128]{1,0:T(8,128)(2,1)S(1)}, u32[]{:S(2)}, u32[]{:S(2)}) %collective-permute-start.12) | collective-permute-done | bytes 266272 | tf_op jit(solution)/shard_map/ppermute | solution.py:567
  52.1 0.0 collective-permute-done.11.refs_2_
  52.1 0.0 collective-permute-done.13.refs_0_
  52.1 1.4 %shard_map.95 = (bf16[256,1024]{1,0:T(8,128)(2,1)}, f32[1088,128]{1,0:T(8,128)S(1)}, f32[16,8,128]{2,1,0:T(8,128)S(1)}, f32[16,8,128]{2,1,0:T(8,128)S(1)}) custom-call(f32[512,256]{1,0:T(8,128)S(1)} %shard_map.80.acc_ref, bf16[1040,128]{1,0:T(8,128)(2,1)S(1)} %collective-permute-done.13.refs_0_, ...), custom_call_target="tpu_custom_call", output_to_operand_aliasing={{0}: (9, {})} | custom-call | bytes 1024 | tf_op jit(solution)/shard_map/pallas_call | solution.py:300
  53.5 0.1 collective-permute-start.14
  53.5 1.2 %collective-permute-done.14.arrived_ref.refs_3_ = f32[16,8,128]{2,1,0:T(8,128)S(1)} collective-permute-done((f32[16,8,128]{2,1,0:T(8,128)S(1)}, f32[16,8,128]{2,1,0:T(8,128)S(1)}, u32[]{:S(2)}, u32[]{:S(2)}) %collective-permute-start.14) | collective-permute-done | bytes 65568 | tf_op jit(solution)/shard_map/ppermute | solution.py:604
  54.8 0.1 shard_map.96
  54.8 1.6 %collective-permute-start.15 = (bf16[144,128]{1,0:T(8,128)(2,1)S(1)}, bf16[144,128]{1,0:T(8,128)(2,1)S(1)}, u32[]{:S(2)}, u32[]{:S(2)}) collective-permute-start(bf16[144,128]{1,0:T(8,128)(2,1)S(1)} %shard_map.96), channel_id=1, source_target_pairs={{0,16},{8,24},{16,0},{24,8},{1,17},{9,25},{17,1},{25,9},{2,18},{10... | collective-permute-start | bytes 110600 | tf_op jit(solution)/shard_map/ppermute | solution.py:604
  56.4 1.2 %shard_map.97.refs_1_ = f32[1088,128]{1,0:T(8,128)S(1)} custom-call(f32[1088,128]{1,0:T(8,128)S(1)} %get-tuple-element.61.gc_ref, f32[16,8,128]{2,1,0:T(8,128)S(1)} %get-tuple-element.62.state_ref, f32[16,16,128]{2,1,0:T(8,128)S(1)} %bitcast.13, f32[16,16,128]{2,1,0:T(8,128)S(1)} %get-tuple-element.52.refs_6_.lap_ref, f32[16,16,128]{2,1,0:T(8,128)S(1)} %bitcast.16), custom_call_target="tpu_custom_call" | custom-call | bytes 1024 | tf_op jit(solution)/shard_map/pallas_call | solution.py:350
  57.6 1.3 %collective-permute-done.15.refs_4_ = bf16[144,128]{1,0:T(8,128)(2,1)S(1)} collective-permute-done((bf16[144,128]{1,0:T(8,128)(2,1)S(1)}, bf16[144,128]{1,0:T(8,128)(2,1)S(1)}, u32[]{:S(2)}, u32[]{:S(2)}) %collective-permute-start.15) | collective-permute-done | bytes 36896 | tf_op jit(solution)/shard_map/ppermute | solution.py:604
  58.9 2.2 %shard_map.98 = bf16[256,1024]{1,0:T(8,128)(2,1)} custom-call(s32[1]{0:T(128)} %bitcast.5.group_ref, f32[1088,128]{1,0:T(8,128)S(1)} %get-tuple-element.57.refs_0_, f32[1088,128]{1,0:T(8,128)S(1)} %shard_map.97.refs_1_, f32[16,8,128]{2,1,0:T(8,128)S(1)} %get-tuple-element.63.refs_2_, f32[16,8,128]{2,1,0:T(8,128)S(1)} %collective-permute-done.14.arrived_ref.refs_3_, ...), custom_call_target="tpu_custom_call" | custom-call | bytes 1024 | tf_op jit(solution)/shard_map/pallas_call | solution.py:487
  (5 shorter events, 0.2 us)
Async XLA Ops:
  0.6 6.2 %copy-start = (bf16[8192,1024]{1,0:T(8,128)(2,1)S(1)}, bf16[8192,1024]{1,0:T(8,128)(2,1)}, u32[]{:S(2)}) copy-start(bf16[8192,1024]{1,0:T(8,128)(2,1)} %w_ref.29) | copy-start | bytes 50331652
  3.0 11.4 %collective-permute-start = (bf16[1040,128]{1,0:T(8,128)(2,1)S(1)}, bf16[1040,128]{1,0:T(8,128)(2,1)S(1)}, u32[]{:S(2)}, u32[]{:S(2)}) collective-permute-start(bf16[1040,128]{1,0:T(8,128)(2,1)S(1)} %get-tuple-element.33), channel_id=1, source_target_pairs={{0,1},{1,0},{2,3},{3,2},{4,5},{5,4},{6,7},{7,6},{8,9},{9,8},{10,11... | collective-permute-start | bytes 798728 | tf_op jit(solution)/shard_map/ppermute | solution.py:567
  7.5 9.9 %collective-permute-start.1 = (bf16[1040,128]{1,0:T(8,128)(2,1)S(1)}, bf16[1040,128]{1,0:T(8,128)(2,1)S(1)}, u32[]{:S(2)}, u32[]{:S(2)}) collective-permute-start(bf16[1040,128]{1,0:T(8,128)(2,1)S(1)} %shard_map.78), channel_id=1, source_target_pairs={{0,2},{1,3},{2,0},{3,1},{4,6},{5,7},{6,4},{7,5},{8,10},{9,11},{10,... | collective-permute-start | bytes 798728 | tf_op jit(solution)/shard_map/ppermute | solution.py:567
  12.2 8.4 %collective-permute-start.2 = (bf16[1040,128]{1,0:T(8,128)(2,1)S(1)}, bf16[1040,128]{1,0:T(8,128)(2,1)S(1)}, u32[]{:S(2)}, u32[]{:S(2)}) collective-permute-start(bf16[1040,128]{1,0:T(8,128)(2,1)S(1)} %shard_map.81), channel_id=1, source_target_pairs={{0,1},{1,0},{2,3},{3,2},{4,5},{5,4},{6,7},{7,6},{8,9},{9,8},{10,11... | collective-permute-start | bytes 798728 | tf_op jit(solution)/shard_map/ppermute | solution.py:567
  15.1 9.8 %collective-permute-start.3 = (bf16[1040,128]{1,0:T(8,128)(2,1)S(1)}, bf16[1040,128]{1,0:T(8,128)(2,1)S(1)}, u32[]{:S(2)}, u32[]{:S(2)}) collective-permute-start(bf16[1040,128]{1,0:T(8,128)(2,1)S(1)} %shard_map.83), channel_id=1, source_target_pairs={{0,2},{1,3},{2,0},{3,1},{4,6},{5,7},{6,4},{7,5},{8,10},{9,11},{10,... | collective-permute-start | bytes 798728 | tf_op jit(solution)/shard_map/ppermute | solution.py:567
  18.0 9.7 %collective-permute-start.4 = (bf16[1040,128]{1,0:T(8,128)(2,1)S(1)}, bf16[1040,128]{1,0:T(8,128)(2,1)S(1)}, u32[]{:S(2)}, u32[]{:S(2)}) collective-permute-start(bf16[1040,128]{1,0:T(8,128)(2,1)S(1)} %shard_map.84), channel_id=1, source_target_pairs={{0,1},{1,0},{2,3},{3,2},{4,5},{5,4},{6,7},{7,6},{8,9},{9,8},{10,11... | collective-permute-start | bytes 798728 | tf_op jit(solution)/shard_map/ppermute | solution.py:567
  20.4 13.1 %collective-permute-start.5 = (bf16[1040,128]{1,0:T(8,128)(2,1)S(1)}, bf16[1040,128]{1,0:T(8,128)(2,1)S(1)}, u32[]{:S(2)}, u32[]{:S(2)}) collective-permute-start(bf16[1040,128]{1,0:T(8,128)(2,1)S(1)} %shard_map.82), channel_id=1, source_target_pairs={{0,1},{1,0},{2,3},{3,2},{4,5},{5,4},{6,7},{7,6},{8,9},{9,8},{10,11... | collective-permute-start | bytes 798728 | tf_op jit(solution)/shard_map/ppermute | solution.py:567
  21.4 12.1 %collective-permute-start.6 = (bf16[1040,128]{1,0:T(8,128)(2,1)S(1)}, bf16[1040,128]{1,0:T(8,128)(2,1)S(1)}, u32[]{:S(2)}, u32[]{:S(2)}) collective-permute-start(bf16[1040,128]{1,0:T(8,128)(2,1)S(1)} %shard_map.85), channel_id=1, source_target_pairs={{0,2},{1,3},{2,0},{3,1},{4,6},{5,7},{6,4},{7,5},{8,10},{9,11},{10,... | collective-permute-start | bytes 798728 | tf_op jit(solution)/shard_map/ppermute | solution.py:567
  23.4 16.3 %collective-permute-start.7 = (bf16[1040,128]{1,0:T(8,128)(2,1)S(1)}, bf16[1040,128]{1,0:T(8,128)(2,1)S(1)}, u32[]{:S(2)}, u32[]{:S(2)}) collective-permute-start(bf16[1040,128]{1,0:T(8,128)(2,1)S(1)} %shard_map.79), channel_id=1, source_target_pairs={{0,1},{1,0},{2,3},{3,2},{4,5},{5,4},{6,7},{7,6},{8,9},{9,8},{10,11... | collective-permute-start | bytes 798728 | tf_op jit(solution)/shard_map/ppermute | solution.py:567
  28.6 15.7 %collective-permute-start.8 = (bf16[1040,128]{1,0:T(8,128)(2,1)S(1)}, bf16[1040,128]{1,0:T(8,128)(2,1)S(1)}, u32[]{:S(2)}, u32[]{:S(2)}) collective-permute-start(bf16[1040,128]{1,0:T(8,128)(2,1)S(1)} %shard_map.87), channel_id=1, source_target_pairs={{0,4},{1,5},{2,6},{3,7},{4,0},{5,1},{6,2},{7,3},{8,12},{9,13},{10,... | collective-permute-start | bytes 798728 | tf_op jit(solution)/shard_map/ppermute | solution.py:567
  31.3 13.0 %collective-permute-start.9 = (bf16[1040,128]{1,0:T(8,128)(2,1)S(1)}, bf16[1040,128]{1,0:T(8,128)(2,1)S(1)}, u32[]{:S(2)}, u32[]{:S(2)}) collective-permute-start(bf16[1040,128]{1,0:T(8,128)(2,1)S(1)} %shard_map.86), channel_id=1, source_target_pairs={{0,2},{1,3},{2,0},{3,1},{4,6},{5,7},{6,4},{7,5},{8,10},{9,11},{10,... | collective-permute-start | bytes 798728 | tf_op jit(solution)/shard_map/ppermute | solution.py:567
  35.0 11.2 %copy-start.3 = (f32[1024,16]{0,1:T(8,128)S(1)}, f32[1024,16]{0,1:T(8,128)}, u32[]{:S(2)}) copy-start(f32[1024,16]{0,1:T(8,128)} %param.10) | copy-start | bytes 196612
  35.0 11.2 %copy-start.4 = (f32[1024,16]{0,1:T(8,128)S(1)}, f32[1024,16]{0,1:T(8,128)}, u32[]{:S(2)}) copy-start(f32[1024,16]{0,1:T(8,128)} %param.11) | copy-start | bytes 196612
  35.1 11.7 %collective-permute-start.10 = (bf16[1040,128]{1,0:T(8,128)(2,1)S(1)}, bf16[1040,128]{1,0:T(8,128)(2,1)S(1)}, u32[]{:S(2)}, u32[]{:S(2)}) collective-permute-start(bf16[1040,128]{1,0:T(8,128)(2,1)S(1)} %shard_map.89), channel_id=1, source_target_pairs={{0,1},{1,0},{2,3},{3,2},{4,5},{5,4},{6,7},{7,6},{8,9},{9,8},{10,11... | collective-permute-start | bytes 798728 | tf_op jit(solution)/shard_map/ppermute | solution.py:567
  37.1 15.0 %collective-permute-start.11 = (bf16[1040,128]{1,0:T(8,128)(2,1)S(1)}, bf16[1040,128]{1,0:T(8,128)(2,1)S(1)}, u32[]{:S(2)}, u32[]{:S(2)}) collective-permute-start(bf16[1040,128]{1,0:T(8,128)(2,1)S(1)} %shard_map.88), channel_id=1, source_target_pairs={{0,4},{1,5},{2,6},{3,7},{4,0},{5,1},{6,2},{7,3},{8,12},{9,13},{10,... | collective-permute-start | bytes 798728 | tf_op jit(solution)/shard_map/ppermute | solution.py:567
  40.4 6.4 %copy-start.1 = (bf16[256,1024]{1,0:T(8,128)(2,1)S(1)}, bf16[256,1024]{1,0:T(8,128)(2,1)}, u32[]{:S(2)}) copy-start(bf16[256,1024]{1,0:T(8,128)(2,1)} %refs_3_.3) | copy-start | bytes 1572868
  40.4 6.4 %copy-start.2 = (bf16[256,1024]{1,0:T(8,128)(2,1)S(1)}, bf16[256,1024]{1,0:T(8,128)(2,1)}, u32[]{:S(2)}) copy-start(bf16[256,1024]{1,0:T(8,128)(2,1)} %refs_4_.3) | copy-start | bytes 1572868
  40.4 11.7 %collective-permute-start.12 = (bf16[1040,128]{1,0:T(8,128)(2,1)S(1)}, bf16[1040,128]{1,0:T(8,128)(2,1)S(1)}, u32[]{:S(2)}, u32[]{:S(2)}) collective-permute-start(bf16[1040,128]{1,0:T(8,128)(2,1)S(1)} %shard_map.90), channel_id=1, source_target_pairs={{0,2},{1,3},{2,0},{3,1},{4,6},{5,7},{6,4},{7,5},{8,10},{9,11},{10,... | collective-permute-start | bytes 798728 | tf_op jit(solution)/shard_map/ppermute | solution.py:567
  44.9 7.2 %collective-permute-start.13 = (bf16[1040,128]{1,0:T(8,128)(2,1)S(1)}, bf16[1040,128]{1,0:T(8,128)(2,1)S(1)}, u32[]{:S(2)}, u32[]{:S(2)}) collective-permute-start(bf16[1040,128]{1,0:T(8,128)(2,1)S(1)} %shard_map.91), channel_id=1, source_target_pairs={{0,1},{1,0},{2,3},{3,2},{4,5},{5,4},{6,7},{7,6},{8,9},{9,8},{10,11... | collective-permute-start | bytes 798728 | tf_op jit(solution)/shard_map/ppermute | solution.py:567
  53.5 1.3 %collective-permute-start.14 = (f32[16,8,128]{2,1,0:T(8,128)S(1)}, f32[16,8,128]{2,1,0:T(8,128)S(1)}, u32[]{:S(2)}, u32[]{:S(2)}) collective-permute-start(f32[16,8,128]{2,1,0:T(8,128)S(1)} %get-tuple-element.59.state_ref), channel_id=1, source_target_pairs={{0,8},{8,0},{16,24},{24,16},{1,9},{9,1},{17,25},{25,17},{2,10},{10... | collective-permute-start | bytes 196616 | tf_op jit(solution)/shard_map/ppermute | solution.py:604
  54.8 4.0 %collective-permute-start.15 = (bf16[144,128]{1,0:T(8,128)(2,1)S(1)}, bf16[144,128]{1,0:T(8,128)(2,1)S(1)}, u32[]{:S(2)}, u32[]{:S(2)}) collective-permute-start(bf16[144,128]{1,0:T(8,128)(2,1)S(1)} %shard_map.96), channel_id=1, source_target_pairs={{0,16},{8,24},{16,0},{24,8},{1,17},{9,25},{17,1},{25,9},{2,18},{10... | collective-permute-start | bytes 110600 | tf_op jit(solution)/shard_map/ppermute | solution.py:604

commit v15 on v14

--- a/solution.py
+++ b/solution.py
@@ -19,15 +19,31 @@
 
 PORTIONS = (((0, 1, 2), 4, 0), ((1, 0, 2), 4, 0), ((0, 1, 2), 4, 1), ((0, 1, 2), 4, 1))
 ORDER = (
-    ((0, 0, 6), (0, 0, 2)), ((1, 0, 5), (1, 0, 1)), ((2, 0, 2), (3, 0, 2)), ("sum", 1), ((2, 0, 6), (3, 0, 6)),
-    ((2, 0, 4), (3, 0, 4)), ((1, 0, 4), (0, 1, 4)), ((1, 1, 4), (0, 0, 4)), ((2, 1, 4), (3, 1, 4)),
-    ((1, 0, 0), (0, 1, 0)), ((0, 2, 0), (1, 2, 0)), ((2, 2, 0), (3, 2, 0)), ((1, 1, 0), (0, 0, 0)),
-    ((2, 1, 0), (3, 1, 0)), ((2, 0, 0), (3, 0, 0)), ("laps", None), ("sum", 0), ("gate", 0), ("gate", 1), ("scan", 1),
+    ((0, 0, 6), (0, 0, 2)),
+    ((1, 0, 5), (1, 0, 1)),
+    ("sum", 1),
+    ((2, 0, 2), (3, 0, 2)),
+    ((2, 0, 6), (3, 0, 6)),
+    ((2, 0, 4), (3, 0, 4)),
+    ((1, 0, 4), (0, 1, 4)),
+    ((1, 1, 4), (0, 0, 4)),
+    ((2, 1, 4), (3, 1, 4)),
+    ((1, 0, 0), (0, 1, 0)),
+    ((0, 2, 0), (1, 2, 0)),
+    ((2, 2, 0), (3, 2, 0)),
+    ((1, 1, 0), (0, 0, 0)),
+    ((2, 1, 0), (3, 1, 0)),
+    ((2, 0, 0), (3, 0, 0)),
+    ("sum", 0),
+    ("laps", None),
+    ("gate", 0),
+    ("gate", 1),
+    ("scan", 1),
     ("fix", None),
 )
 WAITS = {
     ((1, 0, 0), (0, 1, 0)): ((1, 0, 4),),
-    ((2, 0, 0), (3, 0, 0)): ((0, 2, 0), (1, 0, 0)),
+    ("gate", 0): ((0, 2, 0), (1, 0, 0)),
     ("gate", 1): ((2, 2, 0), (2, 1, 0)),
 }
 
@@ -156,7 +172,7 @@
             )
         base += rows
     for copy in copies:
-        copy.start()
+        copy.start(priority=1)
     for i, at in enumerate(range(0, toks, piece)):
         copies[i].wait()
         turned_ref[:, at : at + piece] = g_ref[at : at + piece, :].T

time: 61.2 us -> 61.3 us (level)
  transfers between devices with their start and end apart: 16 -> 16, of which waited for: 7 -> 8; matrix products, arithmetic and copies ran while one was open for 0% -> 0% of each run, Pallas kernels for 21% -> 21%
where the time goes in v15:
time: 61.3 us; the launch traced here: 61.2 us
  starting transfers between devices  29.1 us (47%)
  Pallas kernels  18.9 us (31%)
  waiting for transfers between devices  11.3 us (18%)
  local copies, waits for them, and re-layouts  0.95 us (2%)
  between operations  0.92 us (2%)
    ppermute x14, starting transfers between devices, local(): arrived = lax.ppermute(last, 'ch', [(i, i ^ bit) for i in range(size)])  27.5 us
    pallas_call x15, Pallas kernels, send(): pl.pallas_call(functools.partial(send_kernel, items, coded, width, len(ne...  9.79 us
    ppermute x14, waiting for transfers between devices, local(): arrived = lax.ppermute(last, 'ch', [(i, i ^ bit) for i in range(size)])  8.77 us
    pallas_call x2, Pallas kernels, gate(): pl.pallas_call(functools.partial(gate_kernel, half, rows, segments, piece...  3.2 us
    ppermute x2, waiting for transfers between devices, local(): lax.ppermute(array, 'ctx', [(i, i ^ 1 << round_) for i in range(groups)])  2.53 us
    pallas_call x1, Pallas kernels, first_send(): pl.pallas_call(functools.partial(first_kernel, items, width), in_specs=[p...  2.39 us
    pallas_call x1, Pallas kernels, fix(): pl.pallas_call(functools.partial(fix_kernel, segments, len(arrived)), in_...  2.23 us
    ppermute x2, starting transfers between devices, local(): lax.ppermute(array, 'ctx', [(i, i ^ 1 << round_) for i in range(groups)])  1.62 us
  transfers between devices with their start and end apart: 16, of which 8 were waited for; matrix products, arithmetic and copies ran while one was open for 0% of the time, Pallas kernels for 21%

profile of v15, /device:TPU:0, one launch (start us, length us, event | category | flops | bytes accessed | tf_op | source)
XLA Modules:
  0.0 61.2 jit_solution(4421996250824001130)
XLA Ops:
  0.6 0.0 copy-start
  0.6 2.4 %shard_map.77 = (bf16[1040,128]{1,0:T(8,128)(2,1)S(1)}, bf16[1024,256]{1,0:T(8,128)(2,1)S(1)}) custom-call(s32[1]{0:T(128)} %bitcast.place_ref, bf16[8192,1024]{1,0:T(8,128)(2,1)} %w_ref.29, bf16[256,1024]{1,0:T(8,128)(2,1)} %g_hbm.1), custom_call_target="tpu_custom_call" | custom-call | bytes 1024 | tf_op jit(solution)/shard_map/pallas_call | solution.py:200
  3.0 3.0 %collective-permute-start = (bf16[1040,128]{1,0:T(8,128)(2,1)S(1)}, bf16[1040,128]{1,0:T(8,128)(2,1)S(1)}, u32[]{:S(2)}, u32[]{:S(2)}) collective-permute-start(bf16[1040,128]{1,0:T(8,128)(2,1)S(1)} %get-tuple-element.34), channel_id=1, source_target_pairs={{0,1},{1,0},{2,3},{3,2},{4,5},{5,4},{6,7},{7,6},{8,9},{9,8},{10,11... | collective-permute-start | bytes 798728 | tf_op jit(solution)/shard_map/ppermute | solution.py:583
  6.1 0.8 %copy-done = bf16[8192,1024]{1,0:T(8,128)(2,1)S(1)} copy-done((bf16[8192,1024]{1,0:T(8,128)(2,1)S(1)}, bf16[8192,1024]{1,0:T(8,128)(2,1)}, u32[]{:S(2)}) %copy-start) | copy-done | bytes 16777240
  6.9 0.6 shard_map.78
  7.5 3.1 %collective-permute-start.1 = (bf16[1040,128]{1,0:T(8,128)(2,1)S(1)}, bf16[1040,128]{1,0:T(8,128)(2,1)S(1)}, u32[]{:S(2)}, u32[]{:S(2)}) collective-permute-start(bf16[1040,128]{1,0:T(8,128)(2,1)S(1)} %shard_map.78), channel_id=1, source_target_pairs={{0,2},{1,3},{2,0},{3,1},{4,6},{5,7},{6,4},{7,5},{8,10},{9,11},{10,... | collective-permute-start | bytes 798728 | tf_op jit(solution)/shard_map/ppermute | solution.py:583
  10.6 0.4 shard_map.79.acc_ref
  11.0 0.6 %shard_map.80 = bf16[1040,128]{1,0:T(8,128)(2,1)S(1)} custom-call(s32[1]{0:T(128)} %bitcast.place_ref, bf16[8192,1024]{1,0:T(8,128)(2,1)S(1)} %copy-done, bf16[1024,256]{1,0:T(8,128)(2,1)S(1)} %get-tuple-element.36.turned_ref), custom_call_target="tpu_custom_call" | custom-call | bytes 1024 | tf_op jit(solution)/shard_map/pallas_call | solution.py:147
  11.6 0.6 %shard_map.81 = bf16[1040,128]{1,0:T(8,128)(2,1)S(1)} custom-call(s32[1]{0:T(128)} %bitcast.place_ref, bf16[8192,1024]{1,0:T(8,128)(2,1)S(1)} %copy-done, bf16[1024,256]{1,0:T(8,128)(2,1)S(1)} %get-tuple-element.36.turned_ref), custom_call_target="tpu_custom_call" | custom-call | bytes 1024 | tf_op jit(solution)/shard_map/pallas_call | solution.py:147
  12.3 1.6 %collective-permute-start.2 = (bf16[1040,128]{1,0:T(8,128)(2,1)S(1)}, bf16[1040,128]{1,0:T(8,128)(2,1)S(1)}, u32[]{:S(2)}, u32[]{:S(2)}) collective-permute-start(bf16[1040,128]{1,0:T(8,128)(2,1)S(1)} %shard_map.81), channel_id=1, source_target_pairs={{0,1},{1,0},{2,3},{3,2},{4,5},{5,4},{6,7},{7,6},{8,9},{9,8},{10,11... | collective-permute-start | bytes 798728 | tf_op jit(solution)/shard_map/ppermute | solution.py:583
  13.9 0.6 shard_map.82
  14.5 0.0 collective-permute-done.refs_0_
  14.5 0.7 %shard_map.83 = bf16[1040,128]{1,0:T(8,128)(2,1)S(1)} custom-call(s32[1]{0:T(128)} %bitcast.place_ref, bf16[8192,1024]{1,0:T(8,128)(2,1)S(1)} %copy-done, bf16[1024,256]{1,0:T(8,128)(2,1)S(1)} %get-tuple-element.36.turned_ref, bf16[1040,128]{1,0:T(8,128)(2,1)S(1)} %collective-permute-done.refs_0_), custom_call_target="tpu_custom_call" | custom-call | bytes 1024 | tf_op jit(solution)/shard_map/pallas_call | solution.py:147
  15.1 0.5 collective-permute-start.3
  15.7 1.7 %collective-permute-done.1.refs_0_ = bf16[1040,128]{1,0:T(8,128)(2,1)S(1)} collective-permute-done((bf16[1040,128]{1,0:T(8,128)(2,1)S(1)}, bf16[1040,128]{1,0:T(8,128)(2,1)S(1)}, u32[]{:S(2)}, u32[]{:S(2)}) %collective-permute-start.1) | collective-permute-done | bytes 266272 | tf_op jit(solution)/shard_map/ppermute | solution.py:583
  17.4 0.7 %shard_map.84 = bf16[1040,128]{1,0:T(8,128)(2,1)S(1)} custom-call(s32[1]{0:T(128)} %bitcast.place_ref, bf16[8192,1024]{1,0:T(8,128)(2,1)S(1)} %copy-done, bf16[1024,256]{1,0:T(8,128)(2,1)S(1)} %get-tuple-element.36.turned_ref, bf16[1040,128]{1,0:T(8,128)(2,1)S(1)} %collective-permute-done.1.refs_0_), custom_call_target="tpu_custom_call" | custom-call | bytes 1024 | tf_op jit(solution)/shard_map/pallas_call | solution.py:147
  18.0 2.4 %collective-permute-start.4 = (bf16[1040,128]{1,0:T(8,128)(2,1)S(1)}, bf16[1040,128]{1,0:T(8,128)(2,1)S(1)}, u32[]{:S(2)}, u32[]{:S(2)}) collective-permute-start(bf16[1040,128]{1,0:T(8,128)(2,1)S(1)} %shard_map.84), channel_id=1, source_target_pairs={{0,1},{1,0},{2,3},{3,2},{4,5},{5,4},{6,7},{7,6},{8,9},{9,8},{10,11... | collective-permute-start | bytes 798728 | tf_op jit(solution)/shard_map/ppermute | solution.py:583
  20.4 0.1 collective-permute-start.5
  20.5 0.3 collective-permute-done.2.refs_0_
  20.7 0.7 %shard_map.85 = bf16[1040,128]{1,0:T(8,128)(2,1)S(1)} custom-call(s32[1]{0:T(128)} %bitcast.place_ref, bf16[8192,1024]{1,0:T(8,128)(2,1)S(1)} %copy-done, bf16[1024,256]{1,0:T(8,128)(2,1)S(1)} %get-tuple-element.36.turned_ref, bf16[1040,128]{1,0:T(8,128)(2,1)S(1)} %collective-permute-done.2.refs_0_), custom_call_target="tpu_custom_call" | custom-call | bytes 1024 | tf_op jit(solution)/shard_map/pallas_call | solution.py:147
  21.4 2.0 %collective-permute-start.6 = (bf16[1040,128]{1,0:T(8,128)(2,1)S(1)}, bf16[1040,128]{1,0:T(8,128)(2,1)S(1)}, u32[]{:S(2)}, u32[]{:S(2)}) collective-permute-start(bf16[1040,128]{1,0:T(8,128)(2,1)S(1)} %shard_map.85), channel_id=1, source_target_pairs={{0,2},{1,3},{2,0},{3,1},{4,6},{5,7},{6,4},{7,5},{8,10},{9,11},{10,... | collective-permute-start | bytes 798728 | tf_op jit(solution)/shard_map/ppermute | solution.py:583
  23.4 1.5 %collective-permute-start.7 = (bf16[1040,128]{1,0:T(8,128)(2,1)S(1)}, bf16[1040,128]{1,0:T(8,128)(2,1)S(1)}, u32[]{:S(2)}, u32[]{:S(2)}) collective-permute-start(bf16[1040,128]{1,0:T(8,128)(2,1)S(1)} %shard_map.80), channel_id=1, source_target_pairs={{0,1},{1,0},{2,3},{3,2},{4,5},{5,4},{6,7},{7,6},{8,9},{9,8},{10,11... | collective-permute-start | bytes 798728 | tf_op jit(solution)/shard_map/ppermute | solution.py:583
  24.9 0.0 collective-permute-done.3.refs_1_
  24.9 0.7 %shard_map.86 = bf16[1040,128]{1,0:T(8,128)(2,1)S(1)} custom-call(s32[1]{0:T(128)} %bitcast.place_ref, bf16[8192,1024]{1,0:T(8,128)(2,1)S(1)} %copy-done, bf16[1024,256]{1,0:T(8,128)(2,1)S(1)} %get-tuple-element.36.turned_ref, bf16[1040,128]{1,0:T(8,128)(2,1)S(1)} %collective-permute-done.refs_0_), custom_call_target="tpu_custom_call" | custom-call | bytes 1024 | tf_op jit(solution)/shard_map/pallas_call | solution.py:147
  25.6 2.1 %collective-permute-done.4.refs_0_ = bf16[1040,128]{1,0:T(8,128)(2,1)S(1)} collective-permute-done((bf16[1040,128]{1,0:T(8,128)(2,1)S(1)}, bf16[1040,128]{1,0:T(8,128)(2,1)S(1)}, u32[]{:S(2)}, u32[]{:S(2)}) %collective-permute-start.4) | collective-permute-done | bytes 266272 | tf_op jit(solution)/shard_map/ppermute | solution.py:583
  27.7 0.9 %shard_map.87 = bf16[1040,128]{1,0:T(8,128)(2,1)S(1)} custom-call(s32[1]{0:T(128)} %bitcast.place_ref, bf16[8192,1024]{1,0:T(8,128)(2,1)S(1)} %copy-done, bf16[1024,256]{1,0:T(8,128)(2,1)S(1)} %get-tuple-element.36.turned_ref, bf16[1040,128]{1,0:T(8,128)(2,1)S(1)} %collective-permute-done.4.refs_0_, bf16[1040,128]{1,0:T(8,128)(2,1)S(1)} %collective-permute-done.3.refs_1_), custom_call_target="tpu_custom_call" | custom-call | bytes 1024 | tf_op jit(solution)/shard_map/pallas_call | solution.py:147
  28.6 2.6 %collective-permute-start.8 = (bf16[1040,128]{1,0:T(8,128)(2,1)S(1)}, bf16[1040,128]{1,0:T(8,128)(2,1)S(1)}, u32[]{:S(2)}, u32[]{:S(2)}) collective-permute-start(bf16[1040,128]{1,0:T(8,128)(2,1)S(1)} %shard_map.87), channel_id=1, source_target_pairs={{0,4},{1,5},{2,6},{3,7},{4,0},{5,1},{6,2},{7,3},{8,12},{9,13},{10,... | collective-permute-start | bytes 798728 | tf_op jit(solution)/shard_map/ppermute | solution.py:583
  31.3 2.2 %collective-permute-start.9 = (bf16[1040,128]{1,0:T(8,128)(2,1)S(1)}, bf16[1040,128]{1,0:T(8,128)(2,1)S(1)}, u32[]{:S(2)}, u32[]{:S(2)}) collective-permute-start(bf16[1040,128]{1,0:T(8,128)(2,1)S(1)} %shard_map.86), channel_id=1, source_target_pairs={{0,2},{1,3},{2,0},{3,1},{4,6},{5,7},{6,4},{7,5},{8,10},{9,11},{10,... | collective-permute-start | bytes 798728 | tf_op jit(solution)/shard_map/ppermute | solution.py:583
  33.5 0.0 collective-permute-done.5.refs_0_
  33.5 0.0 collective-permute-done.6.refs_1_
  33.5 0.9 %shard_map.88 = bf16[1040,128]{1,0:T(8,128)(2,1)S(1)} custom-call(s32[1]{0:T(128)} %bitcast.place_ref, bf16[8192,1024]{1,0:T(8,128)(2,1)S(1)} %copy-done, bf16[1024,256]{1,0:T(8,128)(2,1)S(1)} %get-tuple-element.36.turned_ref, bf16[1040,128]{1,0:T(8,128)(2,1)S(1)} %collective-permute-done.5.refs_0_, bf16[1040,128]{1,0:T(8,128)(2,1)S(1)} %collective-permute-done.6.refs_1_), custom_call_target="tpu_custom_call" | custom-call | bytes 1024 | tf_op jit(solution)/shard_map/pallas_call | solution.py:147
  34.4 0.7 %shard_map.89 = bf16[1040,128]{1,0:T(8,128)(2,1)S(1)} custom-call(s32[1]{0:T(128)} %bitcast.place_ref, bf16[8192,1024]{1,0:T(8,128)(2,1)S(1)} %copy-done, bf16[1024,256]{1,0:T(8,128)(2,1)S(1)} %get-tuple-element.36.turned_ref, bf16[1040,128]{1,0:T(8,128)(2,1)S(1)} %collective-permute-done.1.refs_0_), custom_call_target="tpu_custom_call" | custom-call | bytes 1024 | tf_op jit(solution)/shard_map/pallas_call | solution.py:147
  35.1 0.0 copy-start.3
  35.1 0.0 copy-start.4
  35.1 2.0 %collective-permute-start.10 = (bf16[1040,128]{1,0:T(8,128)(2,1)S(1)}, bf16[1040,128]{1,0:T(8,128)(2,1)S(1)}, u32[]{:S(2)}, u32[]{:S(2)}) collective-permute-start(bf16[1040,128]{1,0:T(8,128)(2,1)S(1)} %shard_map.89), channel_id=1, source_target_pairs={{0,1},{1,0},{2,3},{3,2},{4,5},{5,4},{6,7},{7,6},{8,9},{9,8},{10,11... | collective-permute-start | bytes 798728 | tf_op jit(solution)/shard_map/ppermute | solution.py:583
  37.1 2.6 %collective-permute-start.11 = (bf16[1040,128]{1,0:T(8,128)(2,1)S(1)}, bf16[1040,128]{1,0:T(8,128)(2,1)S(1)}, u32[]{:S(2)}, u32[]{:S(2)}) collective-permute-start(bf16[1040,128]{1,0:T(8,128)(2,1)S(1)} %shard_map.88), channel_id=1, source_target_pairs={{0,4},{1,5},{2,6},{3,7},{4,0},{5,1},{6,2},{7,3},{8,12},{9,13},{10,... | collective-permute-start | bytes 798728 | tf_op jit(solution)/shard_map/ppermute | solution.py:583
  39.7 0.0 collective-permute-done.7.refs_0_
  39.7 0.7 %shard_map.90 = bf16[1040,128]{1,0:T(8,128)(2,1)S(1)} custom-call(s32[1]{0:T(128)} %bitcast.place_ref, bf16[8192,1024]{1,0:T(8,128)(2,1)S(1)} %copy-done, bf16[1024,256]{1,0:T(8,128)(2,1)S(1)} %get-tuple-element.36.turned_ref, bf16[1040,128]{1,0:T(8,128)(2,1)S(1)} %collective-permute-done.7.refs_0_), custom_call_target="tpu_custom_call" | custom-call | bytes 1024 | tf_op jit(solution)/shard_map/pallas_call | solution.py:147
  40.4 0.0 copy-start.1
  40.4 0.0 copy-start.2
  40.4 2.7 %collective-permute-start.12 = (bf16[1040,128]{1,0:T(8,128)(2,1)S(1)}, bf16[1040,128]{1,0:T(8,128)(2,1)S(1)}, u32[]{:S(2)}, u32[]{:S(2)}) collective-permute-start(bf16[1040,128]{1,0:T(8,128)(2,1)S(1)} %shard_map.90), channel_id=1, source_target_pairs={{0,2},{1,3},{2,0},{3,1},{4,6},{5,7},{6,4},{7,5},{8,10},{9,11},{10,... | collective-permute-start | bytes 798728 | tf_op jit(solution)/shard_map/ppermute | solution.py:583
  43.1 0.6 shard_map.91
  43.7 0.6 %collective-permute-done.8.refs_2_ = bf16[1040,128]{1,0:T(8,128)(2,1)S(1)} collective-permute-done((bf16[1040,128]{1,0:T(8,128)(2,1)S(1)}, bf16[1040,128]{1,0:T(8,128)(2,1)S(1)}, u32[]{:S(2)}, u32[]{:S(2)}) %collective-permute-start.8) | collective-permute-done | bytes 266272 | tf_op jit(solution)/shard_map/ppermute | solution.py:583
  44.3 1.2 %collective-permute-start.13 = (bf16[1040,128]{1,0:T(8,128)(2,1)S(1)}, bf16[1040,128]{1,0:T(8,128)(2,1)S(1)}, u32[]{:S(2)}, u32[]{:S(2)}) collective-permute-start(bf16[1040,128]{1,0:T(8,128)(2,1)S(1)} %shard_map.91), channel_id=1, source_target_pairs={{0,1},{1,0},{2,3},{3,2},{4,5},{5,4},{6,7},{7,6},{8,9},{9,8},{10,11... | collective-permute-start | bytes 798728 | tf_op jit(solution)/shard_map/ppermute | solution.py:583
  45.6 0.0 copy-done.3
  45.6 0.0 copy-done.4
  45.6 0.4 shard_map.92.acc_ref
  46.2 0.0 collective-permute-done.9.refs_1_
  46.2 0.0 collective-permute-done.10.refs_0_
  46.2 0.0 copy-done.1
  46.2 0.0 copy-done.2
  46.3 1.9 %shard_map.94 = (bf16[256,1024]{1,0:T(8,128)(2,1)}, f32[1088,128]{1,0:T(8,128)S(1)}, f32[16,8,128]{2,1,0:T(8,128)S(1)}, f32[8,8,128]{2,1,0:T(8,128)S(1)}) custom-call(f32[512,256]{1,0:T(8,128)S(1)} %shard_map.92.acc_ref, bf16[1040,128]{1,0:T(8,128)(2,1)S(1)} %collective-permute-done.10.refs_0_, bf16[1040,128]{1,0:T(8,128)(2,1)S(1)} %collective-permute-done.9.refs_1_, ...), custom_call_target="tpu_custom_call" | custom-call | bytes 1024 | tf_op jit(solution)/shard_map/pallas_call | solution.py:316
  48.1 3.2 %collective-permute-done.11.refs_2_ = bf16[1040,128]{1,0:T(8,128)(2,1)S(1)} collective-permute-done((bf16[1040,128]{1,0:T(8,128)(2,1)S(1)}, bf16[1040,128]{1,0:T(8,128)(2,1)S(1)}, u32[]{:S(2)}, u32[]{:S(2)}) %collective-permute-start.11) | collective-permute-done | bytes 266272 | tf_op jit(solution)/shard_map/ppermute | solution.py:583
  51.4 0.8 %collective-permute-done.12.refs_1_ = bf16[1040,128]{1,0:T(8,128)(2,1)S(1)} collective-permute-done((bf16[1040,128]{1,0:T(8,128)(2,1)S(1)}, bf16[1040,128]{1,0:T(8,128)(2,1)S(1)}, u32[]{:S(2)}, u32[]{:S(2)}) %collective-permute-start.12) | collective-permute-done | bytes 266272 | tf_op jit(solution)/shard_map/ppermute | solution.py:583
  52.2 0.0 collective-permute-done.13.refs_0_
  52.2 1.4 %shard_map.95 = (bf16[256,1024]{1,0:T(8,128)(2,1)}, f32[1088,128]{1,0:T(8,128)S(1)}, f32[16,8,128]{2,1,0:T(8,128)S(1)}, f32[16,8,128]{2,1,0:T(8,128)S(1)}) custom-call(f32[512,256]{1,0:T(8,128)S(1)} %shard_map.79.acc_ref, bf16[1040,128]{1,0:T(8,128)(2,1)S(1)} %collective-permute-done.13.refs_0_, ...), custom_call_target="tpu_custom_call", output_to_operand_aliasing={{0}: (9, {})} | custom-call | bytes 1024 | tf_op jit(solution)/shard_map/pallas_call | solution.py:316
  53.5 0.1 collective-permute-start.14
  53.6 1.2 %collective-permute-done.14.arrived_ref.refs_3_ = f32[16,8,128]{2,1,0:T(8,128)S(1)} collective-permute-done((f32[16,8,128]{2,1,0:T(8,128)S(1)}, f32[16,8,128]{2,1,0:T(8,128)S(1)}, u32[]{:S(2)}, u32[]{:S(2)}) %collective-permute-start.14) | collective-permute-done | bytes 65568 | tf_op jit(solution)/shard_map/ppermute | solution.py:620
  54.9 0.1 shard_map.96
  54.9 1.6 %collective-permute-start.15 = (bf16[144,128]{1,0:T(8,128)(2,1)S(1)}, bf16[144,128]{1,0:T(8,128)(2,1)S(1)}, u32[]{:S(2)}, u32[]{:S(2)}) collective-permute-start(bf16[144,128]{1,0:T(8,128)(2,1)S(1)} %shard_map.96), channel_id=1, source_target_pairs={{0,16},{8,24},{16,0},{24,8},{1,17},{9,25},{17,1},{25,9},{2,18},{10... | collective-permute-start | bytes 110600 | tf_op jit(solution)/shard_map/ppermute | solution.py:620
  56.5 1.2 %shard_map.97.refs_1_ = f32[1088,128]{1,0:T(8,128)S(1)} custom-call(f32[1088,128]{1,0:T(8,128)S(1)} %get-tuple-element.63.gc_ref, f32[16,8,128]{2,1,0:T(8,128)S(1)} %get-tuple-element.64.state_ref, f32[16,16,128]{2,1,0:T(8,128)S(1)} %bitcast.13, f32[16,16,128]{2,1,0:T(8,128)S(1)} %get-tuple-element.54.refs_6_.lap_ref, f32[16,16,128]{2,1,0:T(8,128)S(1)} %bitcast.16), custom_call_target="tpu_custom_call" | custom-call | bytes 1024 | tf_op jit(solution)/shard_map/pallas_call | solution.py:366
  57.6 1.3 %collective-permute-done.15.refs_4_ = bf16[144,128]{1,0:T(8,128)(2,1)S(1)} collective-permute-done((bf16[144,128]{1,0:T(8,128)(2,1)S(1)}, bf16[144,128]{1,0:T(8,128)(2,1)S(1)}, u32[]{:S(2)}, u32[]{:S(2)}) %collective-permute-start.15) | collective-permute-done | bytes 36896 | tf_op jit(solution)/shard_map/ppermute | solution.py:620
  58.9 2.2 %shard_map.98 = bf16[256,1024]{1,0:T(8,128)(2,1)} custom-call(s32[1]{0:T(128)} %bitcast.5.group_ref, f32[1088,128]{1,0:T(8,128)S(1)} %get-tuple-element.59.refs_0_, f32[1088,128]{1,0:T(8,128)S(1)} %shard_map.97.refs_1_, f32[16,8,128]{2,1,0:T(8,128)S(1)} %get-tuple-element.65.refs_2_, f32[16,8,128]{2,1,0:T(8,128)S(1)} %collective-permute-done.14.arrived_ref.refs_3_, ...), custom_call_target="tpu_custom_call" | custom-call | bytes 1024 | tf_op jit(solution)/shard_map/pallas_call | solution.py:503
  (5 shorter events, 0.2 us)
Async XLA Ops:
  0.6 6.2 %copy-start = (bf16[8192,1024]{1,0:T(8,128)(2,1)S(1)}, bf16[8192,1024]{1,0:T(8,128)(2,1)}, u32[]{:S(2)}) copy-start(bf16[8192,1024]{1,0:T(8,128)(2,1)} %w_ref.29) | copy-start | bytes 50331652
  3.0 11.4 %collective-permute-start = (bf16[1040,128]{1,0:T(8,128)(2,1)S(1)}, bf16[1040,128]{1,0:T(8,128)(2,1)S(1)}, u32[]{:S(2)}, u32[]{:S(2)}) collective-permute-start(bf16[1040,128]{1,0:T(8,128)(2,1)S(1)} %get-tuple-element.34), channel_id=1, source_target_pairs={{0,1},{1,0},{2,3},{3,2},{4,5},{5,4},{6,7},{7,6},{8,9},{9,8},{10,11... | collective-permute-start | bytes 798728 | tf_op jit(solution)/shard_map/ppermute | solution.py:583
  7.5 9.9 %collective-permute-start.1 = (bf16[1040,128]{1,0:T(8,128)(2,1)S(1)}, bf16[1040,128]{1,0:T(8,128)(2,1)S(1)}, u32[]{:S(2)}, u32[]{:S(2)}) collective-permute-start(bf16[1040,128]{1,0:T(8,128)(2,1)S(1)} %shard_map.78), channel_id=1, source_target_pairs={{0,2},{1,3},{2,0},{3,1},{4,6},{5,7},{6,4},{7,5},{8,10},{9,11},{10,... | collective-permute-start | bytes 798728 | tf_op jit(solution)/shard_map/ppermute | solution.py:583
  12.3 8.5 %collective-permute-start.2 = (bf16[1040,128]{1,0:T(8,128)(2,1)S(1)}, bf16[1040,128]{1,0:T(8,128)(2,1)S(1)}, u32[]{:S(2)}, u32[]{:S(2)}) collective-permute-start(bf16[1040,128]{1,0:T(8,128)(2,1)S(1)} %shard_map.81), channel_id=1, source_target_pairs={{0,1},{1,0},{2,3},{3,2},{4,5},{5,4},{6,7},{7,6},{8,9},{9,8},{10,11... | collective-permute-start | bytes 798728 | tf_op jit(solution)/shard_map/ppermute | solution.py:583
  15.1 9.8 %collective-permute-start.3 = (bf16[1040,128]{1,0:T(8,128)(2,1)S(1)}, bf16[1040,128]{1,0:T(8,128)(2,1)S(1)}, u32[]{:S(2)}, u32[]{:S(2)}) collective-permute-start(bf16[1040,128]{1,0:T(8,128)(2,1)S(1)} %shard_map.83), channel_id=1, source_target_pairs={{0,2},{1,3},{2,0},{3,1},{4,6},{5,7},{6,4},{7,5},{8,10},{9,11},{10,... | collective-permute-start | bytes 798728 | tf_op jit(solution)/shard_map/ppermute | solution.py:583
  18.0 9.7 %collective-permute-start.4 = (bf16[1040,128]{1,0:T(8,128)(2,1)S(1)}, bf16[1040,128]{1,0:T(8,128)(2,1)S(1)}, u32[]{:S(2)}, u32[]{:S(2)}) collective-permute-start(bf16[1040,128]{1,0:T(8,128)(2,1)S(1)} %shard_map.84), channel_id=1, source_target_pairs={{0,1},{1,0},{2,3},{3,2},{4,5},{5,4},{6,7},{7,6},{8,9},{9,8},{10,11... | collective-permute-start | bytes 798728 | tf_op jit(solution)/shard_map/ppermute | solution.py:583
  20.4 13.1 %collective-permute-start.5 = (bf16[1040,128]{1,0:T(8,128)(2,1)S(1)}, bf16[1040,128]{1,0:T(8,128)(2,1)S(1)}, u32[]{:S(2)}, u32[]{:S(2)}) collective-permute-start(bf16[1040,128]{1,0:T(8,128)(2,1)S(1)} %shard_map.82), channel_id=1, source_target_pairs={{0,1},{1,0},{2,3},{3,2},{4,5},{5,4},{6,7},{7,6},{8,9},{9,8},{10,11... | collective-permute-start | bytes 798728 | tf_op jit(solution)/shard_map/ppermute | solution.py:583
  21.4 12.0 %collective-permute-start.6 = (bf16[1040,128]{1,0:T(8,128)(2,1)S(1)}, bf16[1040,128]{1,0:T(8,128)(2,1)S(1)}, u32[]{:S(2)}, u32[]{:S(2)}) collective-permute-start(bf16[1040,128]{1,0:T(8,128)(2,1)S(1)} %shard_map.85), channel_id=1, source_target_pairs={{0,2},{1,3},{2,0},{3,1},{4,6},{5,7},{6,4},{7,5},{8,10},{9,11},{10,... | collective-permute-start | bytes 798728 | tf_op jit(solution)/shard_map/ppermute | solution.py:583
  23.4 16.3 %collective-permute-start.7 = (bf16[1040,128]{1,0:T(8,128)(2,1)S(1)}, bf16[1040,128]{1,0:T(8,128)(2,1)S(1)}, u32[]{:S(2)}, u32[]{:S(2)}) collective-permute-start(bf16[1040,128]{1,0:T(8,128)(2,1)S(1)} %shard_map.80), channel_id=1, source_target_pairs={{0,1},{1,0},{2,3},{3,2},{4,5},{5,4},{6,7},{7,6},{8,9},{9,8},{10,11... | collective-permute-start | bytes 798728 | tf_op jit(solution)/shard_map/ppermute | solution.py:583
  28.6 15.7 %collective-permute-start.8 = (bf16[1040,128]{1,0:T(8,128)(2,1)S(1)}, bf16[1040,128]{1,0:T(8,128)(2,1)S(1)}, u32[]{:S(2)}, u32[]{:S(2)}) collective-permute-start(bf16[1040,128]{1,0:T(8,128)(2,1)S(1)} %shard_map.87), channel_id=1, source_target_pairs={{0,4},{1,5},{2,6},{3,7},{4,0},{5,1},{6,2},{7,3},{8,12},{9,13},{10,... | collective-permute-start | bytes 798728 | tf_op jit(solution)/shard_map/ppermute | solution.py:583
  31.3 14.9 %collective-permute-start.9 = (bf16[1040,128]{1,0:T(8,128)(2,1)S(1)}, bf16[1040,128]{1,0:T(8,128)(2,1)S(1)}, u32[]{:S(2)}, u32[]{:S(2)}) collective-permute-start(bf16[1040,128]{1,0:T(8,128)(2,1)S(1)} %shard_map.86), channel_id=1, source_target_pairs={{0,2},{1,3},{2,0},{3,1},{4,6},{5,7},{6,4},{7,5},{8,10},{9,11},{10,... | collective-permute-start | bytes 798728 | tf_op jit(solution)/shard_map/ppermute | solution.py:583
  35.1 10.5 %copy-start.3 = (f32[1024,16]{0,1:T(8,128)S(1)}, f32[1024,16]{0,1:T(8,128)}, u32[]{:S(2)}) copy-start(f32[1024,16]{0,1:T(8,128)} %param.10) | copy-start | bytes 196612
  35.1 10.5 %copy-start.4 = (f32[1024,16]{0,1:T(8,128)S(1)}, f32[1024,16]{0,1:T(8,128)}, u32[]{:S(2)}) copy-start(f32[1024,16]{0,1:T(8,128)} %param.11) | copy-start | bytes 196612
  35.1 11.1 %collective-permute-start.10 = (bf16[1040,128]{1,0:T(8,128)(2,1)S(1)}, bf16[1040,128]{1,0:T(8,128)(2,1)S(1)}, u32[]{:S(2)}, u32[]{:S(2)}) collective-permute-start(bf16[1040,128]{1,0:T(8,128)(2,1)S(1)} %shard_map.89), channel_id=1, source_target_pairs={{0,1},{1,0},{2,3},{3,2},{4,5},{5,4},{6,7},{7,6},{8,9},{9,8},{10,11... | collective-permute-start | bytes 798728 | tf_op jit(solution)/shard_map/ppermute | solution.py:583
  37.1 14.3 %collective-permute-start.11 = (bf16[1040,128]{1,0:T(8,128)(2,1)S(1)}, bf16[1040,128]{1,0:T(8,128)(2,1)S(1)}, u32[]{:S(2)}, u32[]{:S(2)}) collective-permute-start(bf16[1040,128]{1,0:T(8,128)(2,1)S(1)} %shard_map.88), channel_id=1, source_target_pairs={{0,4},{1,5},{2,6},{3,7},{4,0},{5,1},{6,2},{7,3},{8,12},{9,13},{10,... | collective-permute-start | bytes 798728 | tf_op jit(solution)/shard_map/ppermute | solution.py:583
  40.4 5.8 %copy-start.1 = (bf16[256,1024]{1,0:T(8,128)(2,1)S(1)}, bf16[256,1024]{1,0:T(8,128)(2,1)}, u32[]{:S(2)}) copy-start(bf16[256,1024]{1,0:T(8,128)(2,1)} %refs_3_.3) | copy-start | bytes 1572868
  40.4 5.8 %copy-start.2 = (bf16[256,1024]{1,0:T(8,128)(2,1)S(1)}, bf16[256,1024]{1,0:T(8,128)(2,1)}, u32[]{:S(2)}) copy-start(bf16[256,1024]{1,0:T(8,128)(2,1)} %refs_4_.3) | copy-start | bytes 1572868
  40.4 11.7 %collective-permute-start.12 = (bf16[1040,128]{1,0:T(8,128)(2,1)S(1)}, bf16[1040,128]{1,0:T(8,128)(2,1)S(1)}, u32[]{:S(2)}, u32[]{:S(2)}) collective-permute-start(bf16[1040,128]{1,0:T(8,128)(2,1)S(1)} %shard_map.90), channel_id=1, source_target_pairs={{0,2},{1,3},{2,0},{3,1},{4,6},{5,7},{6,4},{7,5},{8,10},{9,11},{10,... | collective-permute-start | bytes 798728 | tf_op jit(solution)/shard_map/ppermute | solution.py:583
  44.3 7.9 %collective-permute-start.13 = (bf16[1040,128]{1,0:T(8,128)(2,1)S(1)}, bf16[1040,128]{1,0:T(8,128)(2,1)S(1)}, u32[]{:S(2)}, u32[]{:S(2)}) collective-permute-start(bf16[1040,128]{1,0:T(8,128)(2,1)S(1)} %shard_map.91), channel_id=1, source_target_pairs={{0,1},{1,0},{2,3},{3,2},{4,5},{5,4},{6,7},{7,6},{8,9},{9,8},{10,11... | collective-permute-start | bytes 798728 | tf_op jit(solution)/shard_map/ppermute | solution.py:583
  53.5 1.3 %collective-permute-start.14 = (f32[16,8,128]{2,1,0:T(8,128)S(1)}, f32[16,8,128]{2,1,0:T(8,128)S(1)}, u32[]{:S(2)}, u32[]{:S(2)}) collective-permute-start(f32[16,8,128]{2,1,0:T(8,128)S(1)} %get-tuple-element.61.state_ref), channel_id=1, source_target_pairs={{0,8},{8,0},{16,24},{24,16},{1,9},{9,1},{17,25},{25,17},{2,10},{10... | collective-permute-start | bytes 196616 | tf_op jit(solution)/shard_map/ppermute | solution.py:620
  54.9 4.0 %collective-permute-start.15 = (bf16[144,128]{1,0:T(8,128)(2,1)S(1)}, bf16[144,128]{1,0:T(8,128)(2,1)S(1)}, u32[]{:S(2)}, u32[]{:S(2)}) collective-permute-start(bf16[144,128]{1,0:T(8,128)(2,1)S(1)} %shard_map.96), channel_id=1, source_target_pairs={{0,16},{8,24},{16,0},{24,8},{1,17},{9,25},{17,1},{25,9},{2,18},{10... | collective-permute-start | bytes 110600 | tf_op jit(solution)/shard_map/ppermute | solution.py:620

commit v16 on v14

--- a/solution.py
+++ b/solution.py
@@ -19,15 +19,15 @@
 
 PORTIONS = (((0, 1, 2), 4, 0), ((1, 0, 2), 4, 0), ((0, 1, 2), 4, 1), ((0, 1, 2), 4, 1))
 ORDER = (
-    ((0, 0, 6), (0, 0, 2)), ((1, 0, 5), (1, 0, 1)), ((2, 0, 2), (3, 0, 2)), ("sum", 1), ((2, 0, 6), (3, 0, 6)),
+    ((0, 0, 6), (0, 0, 2)), ("both", ((1, 0, 5), (1, 0, 1)), ((2, 0, 6), (3, 0, 6))), ("sum", 1), ((2, 0, 2), (3, 0, 2)),
     ((2, 0, 4), (3, 0, 4)), ((1, 0, 4), (0, 1, 4)), ((1, 1, 4), (0, 0, 4)), ((2, 1, 4), (3, 1, 4)),
     ((1, 0, 0), (0, 1, 0)), ((0, 2, 0), (1, 2, 0)), ((2, 2, 0), (3, 2, 0)), ((1, 1, 0), (0, 0, 0)),
-    ((2, 1, 0), (3, 1, 0)), ((2, 0, 0), (3, 0, 0)), ("laps", None), ("sum", 0), ("gate", 0), ("gate", 1), ("scan", 1),
+    ((2, 1, 0), (3, 1, 0)), ((2, 0, 0), (3, 0, 0)), ("sum", 0), ("laps", None), ("gate", 0), ("gate", 1), ("scan", 1),
     ("fix", None),
 )
 WAITS = {
     ((1, 0, 0), (0, 1, 0)): ((1, 0, 4),),
-    ((2, 0, 0), (3, 0, 0)): ((0, 2, 0), (1, 0, 0)),
+    ("gate", 0): ((0, 2, 0), (1, 0, 0)),
     ("gate", 1): ((2, 2, 0), (2, 1, 0)),
 }
 
@@ -138,65 +138,69 @@
     )(place, weight, turned, *nears)
 
 
-def first_kernel(items, width, place_ref, w_hbm, g_hbm, out_ref, turned_ref, w_ref, g_ref, sems):
-    copies, toks = [], g_ref.shape[0]
-    piece = math.gcd(toks, PIECE)
-    for at in range(0, toks, piece):
-        lines = pl.ds(at, piece)
-        copies.append(pltpu.make_async_copy(g_hbm.at[lines, :], g_ref.at[lines, :], sems.at[len(copies)]))
-    base, grads = 0, len(copies)
-    for block, offset, rows, _ in items:
-        step = math.gcd(rows, PIECE)
-        first = pl.multiple_of((place_ref[0] ^ block) * width + offset, 16)
-        for at in range(0, rows, step):
-            copies.append(
-                pltpu.make_async_copy(
-                    w_hbm.at[pl.ds(first + at, step), :], w_ref.at[pl.ds(base + at, step), :], sems.at[len(copies)]
+def early_kernel(messages, width, turns, place_ref, w_hbm, g_ref, *refs):
+    out_refs, refs = refs[: len(messages)], refs[len(messages) :]
+    w_ref, sems = refs[-2:]
+    turned_ref = refs[0] if turns else g_ref
+    depth, toks = turned_ref.shape
+    copies, waits = [], []
+    if turns:
+        piece = math.gcd(toks, PIECE)
+        for at in range(0, toks, piece):
+            lines = pl.ds(at, piece)
+            copies.append(pltpu.make_async_copy(g_ref.at[lines, :], refs[1].at[lines, :], sems.at[len(copies)]))
+    grads, base = len(copies), 0
+    for items in messages:
+        for block, offset, rows, _ in items:
+            step = math.gcd(rows, PIECE)
+            first = pl.multiple_of((place_ref[0] ^ block) * width + offset, 16)
+            for at in range(0, rows, step):
+                copies.append(
+                    pltpu.make_async_copy(
+                        w_hbm.at[pl.ds(first + at, step), :], w_ref.at[pl.ds(base + at, step), :], sems.at[len(copies)]
+                    )
                 )
-            )
-        base += rows
+            base += rows
     for copy in copies:
-        copy.start()
-    for i, at in enumerate(range(0, toks, piece)):
+        copy.start(priority=1)
+    for i in range(grads):
         copies[i].wait()
-        turned_ref[:, at : at + piece] = g_ref[at : at + piece, :].T
-    base, peaks, waits = 0, [], iter(copies[grads:])
-    for _, _, rows, _ in items:
-        step = step_of(rows)
-        for at in range(base, base + rows, step):
-            for _ in range(step // math.gcd(rows, PIECE)):
-                next(waits).wait()
-            total = jnp.dot(w_ref[at : at + step, :], turned_ref[...], preferred_element_type=jnp.float32)
-            total, more = encode(total, part_of(rows, len(items), folds_of(toks)))
-            peaks += more
-            put(total, out_ref, at)
-        base += rows
-    put_peaks(peaks, out_ref)
-
-
-def first_send(items, width, place, weight, grad):
-    toks, depth = grad.shape
+        turned_ref[:, i * piece : (i + 1) * piece] = refs[1][i * piece : (i + 1) * piece, :].T
+    waits, base = iter(copies[grads:]), 0
+    for items, out_ref in zip(messages, out_refs):
+        start, peaks = base, []
+        for _, _, rows, _ in items:
+            step = step_of(rows)
+            for at in range(base, base + rows, step):
+                for _ in range(step // math.gcd(rows, PIECE)):
+                    next(waits).wait()
+                total = jnp.dot(w_ref[at : at + step, :], turned_ref[...], preferred_element_type=jnp.float32)
+                total, more = encode(total, part_of(rows, len(items), folds_of(toks)))
+                peaks += more
+                put(total, out_ref, at - start)
+            base += rows
+        put_peaks(peaks, out_ref)
+
+
+def early_send(messages, width, place, weight, grad, turns):
+    toks, depth = grad.shape if turns else grad.shape[::-1]
     vmem = pl.BlockSpec(memory_space=pltpu.VMEM)
     high = pl.BlockSpec(memory_space=pltpu.HBM)
-    count = sum(rows for _, _, rows, _ in items)
+    counts = [sum(rows for _, _, rows, _ in items) for items in messages]
     folds = folds_of(toks)
-    steps = toks // math.gcd(toks, PIECE) + sum(rows // math.gcd(rows, PIECE) for _, _, rows, _ in items)
+    steps = sum(rows // math.gcd(rows, PIECE) for items in messages for _, _, rows, _ in items)
+    steps += toks // math.gcd(toks, PIECE) if turns else 0
+    coded = [jax.ShapeDtypeStruct((folds * count + PEAKS, toks // folds), jnp.bfloat16) for count in counts]
     return pl.pallas_call(
-        functools.partial(first_kernel, items, width),
-        in_specs=[pl.BlockSpec(memory_space=pltpu.SMEM), high, high],
-        out_specs=(vmem, vmem),
-        out_shape=(
-            jax.ShapeDtypeStruct((folds * count + PEAKS, toks // folds), jnp.bfloat16),
-            jax.ShapeDtypeStruct((depth, toks), jnp.bfloat16),
-        ),
-        scratch_shapes=[
-            pltpu.VMEM((count, depth), jnp.bfloat16),
-            pltpu.VMEM((toks, depth), jnp.bfloat16),
-            pltpu.SemaphoreType.DMA((steps,)),
-        ],
+        functools.partial(early_kernel, messages, width, turns),
+        in_specs=[pl.BlockSpec(memory_space=pltpu.SMEM), high, high if turns else vmem],
+        out_specs=[vmem] * (len(messages) + turns),
+        out_shape=coded + [jax.ShapeDtypeStruct((depth, toks), jnp.bfloat16)] * turns,
+        scratch_shapes=[pltpu.VMEM((toks, depth), jnp.bfloat16)] * turns
+        + [pltpu.VMEM((sum(counts), depth), jnp.bfloat16), pltpu.SemaphoreType.DMA((steps,))],
         compiler_params=pltpu.CompilerParams(vmem_limit_bytes=VMEM),
         cost_estimate=QUICK,
-    )(place, pinned(weight), pinned(grad))
+    )(place, pinned(weight), pinned(grad) if turns else grad)
 
 
 def steps_back(count, body, state, unroll):
@@ -543,33 +547,37 @@
 
     for todo in order:
         awaited = [received[key][0] for key in waits.get(todo, ())]
-        kind, half = todo if isinstance(todo[0], str) else ("send", None)
+        kind, half = todo[:2] if isinstance(todo[0], str) else ("send", None)
         inside = [q for q, (_, _, lies) in enumerate(portions) if lies == half]
-        if kind == "send":
-            arrays, items = [], []
-            wanted, rows, bits_of = [], [], []
-            for p, s, block in todo:
-                route, share, _ = portions[p]
-                bits_of.append(bits[route[s]])
-                rows.append(width // share)
-                wanted.append([(p, i, block ^ bits_of[-1]) for i in range(s)])
-            bit, count = bits_of[0], len(todo)
-            arrays, places = collect([key for keys in wanted for key in keys])
-            places = iter(places)
-            items = tuple(
-                (block ^ bit, offsets[p], rows[i], tuple(next(places) for _ in wanted[i]))
-                for i, (p, _, block) in enumerate(todo)
-            )
+        if kind in ("send", "both"):
+            messages = todo[1:] if kind == "both" else (todo,)
+            bit_of = lambda key: bits[portions[key[0]][0][key[1]]]
+            arrays, planned = [], []
+            for message in messages:
+                wanted = [[(p, i, block ^ bit_of((p, s, block))) for i in range(s)] for p, s, block in message]
+                arrays, places = collect([key for keys in wanted for key in keys])
+                places = iter(places)
+                planned.append(
+                    tuple(
+                        (block ^ bit_of((p, s, block)), offsets[p], width // portions[p][1], tuple(next(places) for _ in keys))
+                        for (p, s, block), keys in zip(message, wanted)
+                    )
+                )
             if last is None:
-                last, turned = first_send(items, width, place, out_weight, out_grad)
+                *payloads, turned = early_send(planned, width, place, out_weight, out_grad, True)
+            elif kind == "both":
+                payloads = early_send(planned, width, after(place), out_weight, turned, False)
             else:
-                last = send(items, True, width, after(place), out_weight, turned, arrays)
-            arrived = lax.ppermute(last, "ch", [(i, i ^ bit) for i in range(size)])
-            start = peak = 0
-            for i, key in enumerate(todo):
-                part = part_of(rows[i], count, folds_of(toks))
-                received[key] = (arrived, start, peak, part)
-                start, peak = start + rows[i], peak + rows[i] // part
+                payloads = [send(planned[0], True, width, after(place), out_weight, turned, arrays)]
+            last = payloads[0]
+            for message, items, payload in zip(messages, planned, payloads):
+                bit = bit_of(message[0])
+                arrived = lax.ppermute(payload, "ch", [(i, i ^ bit) for i in range(size)])
+                start = peak = 0
+                for key, (_, _, rows, _) in zip(message, items):
+                    part = part_of(rows, len(items), folds_of(toks))
+                    received[key] = (arrived, start, peak, part)
+                    start, peak = start + rows, peak + rows // part
         elif kind == "laps":
             lap, wide = laps(segments, toks, after(decay))
             last = wide

time: 61.2 us -> 60.7 us (level)
  starting transfers between devices: 29.2 us -> 22.3 us
  waiting for transfers between devices: 11.2 us -> 16.4 us
  Pallas kernels: 18.8 us -> 20.8 us
  local copies, waits for them, and re-layouts: 0.96 us -> 0.17 us
    ppermute x14, starting transfers between devices: 27.6 us -> 20.7 us  [local(): arrived = lax.ppermute(payload, 'ch', [(i, i ^ bit) for i in range(size)])]
    ppermute x14, waiting for transfers between devices: 8.68 us -> 13.7 us  [local(): arrived = lax.ppermute(payload, 'ch', [(i, i ^ bit) for i in range(size)])]
    pallas_call x1 -> x2, Pallas kernels: 2.38 us -> 5.57 us  [early_send(): pl.pallas_call(functools.partial(early_kernel, messages, width, turns), i...]
    pallas_call x15 -> x13, Pallas kernels: 9.7 us -> 8.53 us  [send(): pl.pallas_call(functools.partial(send_kernel, items, coded, width, len(ne...]
    unnamed x12 -> x18, local copies, waits for them, and re-layouts: 0.87 us -> 0.07 us
  transfers between devices with their start and end apart: 16 -> 16, of which waited for: 7 -> 12; matrix products, arithmetic and copies ran while one was open for 0% -> 0% of each run, Pallas kernels for 21% -> 24%
where the time goes in v16:
time: 60.7 us; the launch traced here: 60.5 us
  starting transfers between devices  22.3 us (37%)
  Pallas kernels  20.8 us (34%)
  waiting for transfers between devices  16.4 us (27%)
  between operations  0.93 us (2%)
    ppermute x14, starting transfers between devices, local(): arrived = lax.ppermute(payload, 'ch', [(i, i ^ bit) for i in range(size)])  20.7 us
    ppermute x14, waiting for transfers between devices, local(): arrived = lax.ppermute(payload, 'ch', [(i, i ^ bit) for i in range(size)])  13.7 us
    pallas_call x13, Pallas kernels, send(): pl.pallas_call(functools.partial(send_kernel, items, coded, width, len(ne...  8.53 us
    pallas_call x2, Pallas kernels, early_send(): pl.pallas_call(functools.partial(early_kernel, messages, width, turns), i...  5.57 us
    pallas_call x2, Pallas kernels, gate(): pl.pallas_call(functools.partial(gate_kernel, half, rows, segments, piece...  3.2 us
    ppermute x2, waiting for transfers between devices, local(): lax.ppermute(array, 'ctx', [(i, i ^ 1 << round_) for i in range(groups)])  2.63 us
    pallas_call x1, Pallas kernels, fix(): pl.pallas_call(functools.partial(fix_kernel, segments, len(arrived)), in_...  2.23 us
    ppermute x2, starting transfers between devices, local(): lax.ppermute(array, 'ctx', [(i, i ^ 1 << round_) for i in range(groups)])  1.53 us
  transfers between devices with their start and end apart: 16, of which 12 were waited for; matrix products, arithmetic and copies ran while one was open for 0% of the time, Pallas kernels for 24%

profile of v16, /device:TPU:0, one launch (start us, length us, event | category | flops | bytes accessed | tf_op | source)
XLA Modules:
  0.0 60.5 jit_solution(11945705235551838648)
XLA Ops:
  0.6 0.0 slice-start
  0.6 0.0 slice-start.1
  0.7 2.4 %shard_map.77 = (bf16[1040,128]{1,0:T(8,128)(2,1)S(1)}, bf16[1024,256]{1,0:T(8,128)(2,1)S(1)}) custom-call(s32[1]{0:T(128)} %bitcast.place_ref, bf16[8192,1024]{1,0:T(8,128)(2,1)} %w_ref.25, bf16[256,1024]{1,0:T(8,128)(2,1)} %g_ref.1), custom_call_target="tpu_custom_call" | custom-call | bytes 1024 | tf_op jit(solution)/shard_map/pallas_call | solution.py:194
  3.0 3.0 %collective-permute-start = (bf16[1040,128]{1,0:T(8,128)(2,1)S(1)}, bf16[1040,128]{1,0:T(8,128)(2,1)S(1)}, u32[]{:S(2)}, u32[]{:S(2)}) collective-permute-start(bf16[1040,128]{1,0:T(8,128)(2,1)S(1)} %get-tuple-element.35), channel_id=1, source_target_pairs={{0,1},{1,0},{2,3},{3,2},{4,5},{5,4},{6,7},{7,6},{8,9},{9,8},{10,11... | collective-permute-start | bytes 798728 | tf_op jit(solution)/shard_map/ppermute | solution.py:575
  6.1 3.2 %shard_map.78 = (bf16[1040,128]{1,0:T(8,128)(2,1)S(1)}, bf16[1040,128]{1,0:T(8,128)(2,1)S(1)}) custom-call(s32[1]{0:T(128)} %bitcast.place_ref, bf16[8192,1024]{1,0:T(8,128)(2,1)} %w_ref.25, bf16[1024,256]{1,0:T(8,128)(2,1)S(1)} %get-tuple-element.37.g_ref.turned_ref), custom_call_target="tpu_custom_call" | custom-call | bytes 1024 | tf_op jit(solution)/shard_map/pallas_call | solution.py:194
  9.3 1.6 %collective-permute-start.1 = (bf16[1040,128]{1,0:T(8,128)(2,1)S(1)}, bf16[1040,128]{1,0:T(8,128)(2,1)S(1)}, u32[]{:S(2)}, u32[]{:S(2)}) collective-permute-start(bf16[1040,128]{1,0:T(8,128)(2,1)S(1)} %get-tuple-element.38), channel_id=1, source_target_pairs={{0,2},{1,3},{2,0},{3,1},{4,6},{5,7},{6,4},{7,5},{8,10},{9,11},{10,... | collective-permute-start | bytes 798728 | tf_op jit(solution)/shard_map/ppermute | solution.py:575
  10.9 0.5 collective-permute-start.2
  11.4 0.0 slice-done
  11.4 0.0 slice-done.1
  11.4 0.0 slice-done.2
  11.4 0.0 slice-done.3
  11.4 0.4 shard_map.79.acc_ref
  11.9 0.6 %shard_map.80 = bf16[1040,128]{1,0:T(8,128)(2,1)S(1)} custom-call(s32[1]{0:T(128)} %bitcast.place_ref, bf16[8192,1024]{1,0:T(8,128)(2,1)S(1)} %bitcast.11, bf16[1024,256]{1,0:T(8,128)(2,1)S(1)} %get-tuple-element.37.g_ref.turned_ref), custom_call_target="tpu_custom_call" | custom-call | bytes 1024 | tf_op jit(solution)/shard_map/pallas_call | solution.py:131
  12.5 0.6 %shard_map.81 = bf16[1040,128]{1,0:T(8,128)(2,1)S(1)} custom-call(s32[1]{0:T(128)} %bitcast.place_ref, bf16[8192,1024]{1,0:T(8,128)(2,1)S(1)} %bitcast.11, bf16[1024,256]{1,0:T(8,128)(2,1)S(1)} %get-tuple-element.37.g_ref.turned_ref), custom_call_target="tpu_custom_call" | custom-call | bytes 1024 | tf_op jit(solution)/shard_map/pallas_call | solution.py:131
  13.1 0.0 collective-permute-done.refs_0_
  13.1 0.7 %shard_map.82 = bf16[1040,128]{1,0:T(8,128)(2,1)S(1)} custom-call(s32[1]{0:T(128)} %bitcast.place_ref, bf16[8192,1024]{1,0:T(8,128)(2,1)S(1)} %bitcast.11, bf16[1024,256]{1,0:T(8,128)(2,1)S(1)} %get-tuple-element.37.g_ref.turned_ref, bf16[1040,128]{1,0:T(8,128)(2,1)S(1)} %collective-permute-done.refs_0_), custom_call_target="tpu_custom_call" | custom-call | bytes 1024 | tf_op jit(solution)/shard_map/pallas_call | solution.py:131
  13.8 2.1 %collective-permute-start.3 = (bf16[1040,128]{1,0:T(8,128)(2,1)S(1)}, bf16[1040,128]{1,0:T(8,128)(2,1)S(1)}, u32[]{:S(2)}, u32[]{:S(2)}) collective-permute-start(bf16[1040,128]{1,0:T(8,128)(2,1)S(1)} %shard_map.82), channel_id=1, source_target_pairs={{0,2},{1,3},{2,0},{3,1},{4,6},{5,7},{6,4},{7,5},{8,10},{9,11},{10,... | collective-permute-start | bytes 798728 | tf_op jit(solution)/shard_map/ppermute | solution.py:575
  15.9 2.7 %collective-permute-done.1.refs_0_ = bf16[1040,128]{1,0:T(8,128)(2,1)S(1)} collective-permute-done((bf16[1040,128]{1,0:T(8,128)(2,1)S(1)}, bf16[1040,128]{1,0:T(8,128)(2,1)S(1)}, u32[]{:S(2)}, u32[]{:S(2)}) %collective-permute-start.1) | collective-permute-done | bytes 266272 | tf_op jit(solution)/shard_map/ppermute | solution.py:575
  18.7 0.6 %shard_map.83 = bf16[1040,128]{1,0:T(8,128)(2,1)S(1)} custom-call(s32[1]{0:T(128)} %bitcast.place_ref, bf16[8192,1024]{1,0:T(8,128)(2,1)S(1)} %bitcast.11, bf16[1024,256]{1,0:T(8,128)(2,1)S(1)} %get-tuple-element.37.g_ref.turned_ref, bf16[1040,128]{1,0:T(8,128)(2,1)S(1)} %collective-permute-done.1.refs_0_), custom_call_target="tpu_custom_call" | custom-call | bytes 1024 | tf_op jit(solution)/shard_map/pallas_call | solution.py:131
  19.3 0.1 collective-permute-start.4
  19.4 2.0 %collective-permute-start.5 = (bf16[1040,128]{1,0:T(8,128)(2,1)S(1)}, bf16[1040,128]{1,0:T(8,128)(2,1)S(1)}, u32[]{:S(2)}, u32[]{:S(2)}) collective-permute-start(bf16[1040,128]{1,0:T(8,128)(2,1)S(1)} %shard_map.81), channel_id=1, source_target_pairs={{0,1},{1,0},{2,3},{3,2},{4,5},{5,4},{6,7},{7,6},{8,9},{9,8},{10,11... | collective-permute-start | bytes 798728 | tf_op jit(solution)/shard_map/ppermute | solution.py:575
  21.4 0.0 collective-permute-done.2.refs_0_
  21.4 0.7 %shard_map.84 = bf16[1040,128]{1,0:T(8,128)(2,1)S(1)} custom-call(s32[1]{0:T(128)} %bitcast.place_ref, bf16[8192,1024]{1,0:T(8,128)(2,1)S(1)} %bitcast.11, bf16[1024,256]{1,0:T(8,128)(2,1)S(1)} %get-tuple-element.37.g_ref.turned_ref, bf16[1040,128]{1,0:T(8,128)(2,1)S(1)} %collective-permute-done.2.refs_0_), custom_call_target="tpu_custom_call" | custom-call | bytes 1024 | tf_op jit(solution)/shard_map/pallas_call | solution.py:131
  22.1 1.6 %collective-permute-start.6 = (bf16[1040,128]{1,0:T(8,128)(2,1)S(1)}, bf16[1040,128]{1,0:T(8,128)(2,1)S(1)}, u32[]{:S(2)}, u32[]{:S(2)}) collective-permute-start(bf16[1040,128]{1,0:T(8,128)(2,1)S(1)} %shard_map.84), channel_id=1, source_target_pairs={{0,2},{1,3},{2,0},{3,1},{4,6},{5,7},{6,4},{7,5},{8,10},{9,11},{10,... | collective-permute-start | bytes 798728 | tf_op jit(solution)/shard_map/ppermute | solution.py:575
  23.8 0.3 collective-permute-start.7
  24.1 0.3 collective-permute-done.3.refs_1_
  24.4 0.7 %shard_map.85 = bf16[1040,128]{1,0:T(8,128)(2,1)S(1)} custom-call(s32[1]{0:T(128)} %bitcast.place_ref, bf16[8192,1024]{1,0:T(8,128)(2,1)S(1)} %bitcast.11, bf16[1024,256]{1,0:T(8,128)(2,1)S(1)} %get-tuple-element.37.g_ref.turned_ref, bf16[1040,128]{1,0:T(8,128)(2,1)S(1)} %collective-permute-done.refs_0_), custom_call_target="tpu_custom_call" | custom-call | bytes 1024 | tf_op jit(solution)/shard_map/pallas_call | solution.py:131
  25.0 3.7 %collective-permute-done.4.refs_0_ = bf16[1040,128]{1,0:T(8,128)(2,1)S(1)} collective-permute-done((bf16[1040,128]{1,0:T(8,128)(2,1)S(1)}, bf16[1040,128]{1,0:T(8,128)(2,1)S(1)}, u32[]{:S(2)}, u32[]{:S(2)}) %collective-permute-start.4) | collective-permute-done | bytes 266272 | tf_op jit(solution)/shard_map/ppermute | solution.py:575
  28.7 0.9 %shard_map.86 = bf16[1040,128]{1,0:T(8,128)(2,1)S(1)} custom-call(s32[1]{0:T(128)} %bitcast.place_ref, bf16[8192,1024]{1,0:T(8,128)(2,1)S(1)} %bitcast.11, bf16[1024,256]{1,0:T(8,128)(2,1)S(1)} %get-tuple-element.37.g_ref.turned_ref, bf16[1040,128]{1,0:T(8,128)(2,1)S(1)} %collective-permute-done.4.refs_0_, bf16[1040,128]{1,0:T(8,128)(2,1)S(1)} %collective-permute-done.3.refs_1_), custom_call_target="tpu_custom_call" | custom-call | bytes 1024 | tf_op jit(solution)/shard_map/pallas_call | solution.py:131
  29.6 2.7 %collective-permute-start.8 = (bf16[1040,128]{1,0:T(8,128)(2,1)S(1)}, bf16[1040,128]{1,0:T(8,128)(2,1)S(1)}, u32[]{:S(2)}, u32[]{:S(2)}) collective-permute-start(bf16[1040,128]{1,0:T(8,128)(2,1)S(1)} %shard_map.86), channel_id=1, source_target_pairs={{0,4},{1,5},{2,6},{3,7},{4,0},{5,1},{6,2},{7,3},{8,12},{9,13},{10,... | collective-permute-start | bytes 798728 | tf_op jit(solution)/shard_map/ppermute | solution.py:575
  32.3 1.6 %collective-permute-start.9 = (bf16[1040,128]{1,0:T(8,128)(2,1)S(1)}, bf16[1040,128]{1,0:T(8,128)(2,1)S(1)}, u32[]{:S(2)}, u32[]{:S(2)}) collective-permute-start(bf16[1040,128]{1,0:T(8,128)(2,1)S(1)} %shard_map.85), channel_id=1, source_target_pairs={{0,2},{1,3},{2,0},{3,1},{4,6},{5,7},{6,4},{7,5},{8,10},{9,11},{10,... | collective-permute-start | bytes 798728 | tf_op jit(solution)/shard_map/ppermute | solution.py:575
  33.8 0.6 collective-permute-done.5.refs_0_
  34.4 0.0 collective-permute-done.6.refs_1_
  34.4 0.9 %shard_map.87 = bf16[1040,128]{1,0:T(8,128)(2,1)S(1)} custom-call(s32[1]{0:T(128)} %bitcast.place_ref, bf16[8192,1024]{1,0:T(8,128)(2,1)S(1)} %bitcast.11, bf16[1024,256]{1,0:T(8,128)(2,1)S(1)} %get-tuple-element.37.g_ref.turned_ref, bf16[1040,128]{1,0:T(8,128)(2,1)S(1)} %collective-permute-done.5.refs_0_, bf16[1040,128]{1,0:T(8,128)(2,1)S(1)} %collective-permute-done.6.refs_1_), custom_call_target="tpu_custom_call" | custom-call | bytes 1024 | tf_op jit(solution)/shard_map/pallas_call | solution.py:131
  35.3 0.7 %shard_map.88 = bf16[1040,128]{1,0:T(8,128)(2,1)S(1)} custom-call(s32[1]{0:T(128)} %bitcast.place_ref, bf16[8192,1024]{1,0:T(8,128)(2,1)S(1)} %bitcast.11, bf16[1024,256]{1,0:T(8,128)(2,1)S(1)} %get-tuple-element.37.g_ref.turned_ref, bf16[1040,128]{1,0:T(8,128)(2,1)S(1)} %collective-permute-done.1.refs_0_), custom_call_target="tpu_custom_call" | custom-call | bytes 1024 | tf_op jit(solution)/shard_map/pallas_call | solution.py:131
  36.0 0.0 copy-start.2
  36.0 0.0 copy-start.3
  36.0 0.1 collective-permute-start.10
  36.1 2.9 %collective-permute-start.11 = (bf16[1040,128]{1,0:T(8,128)(2,1)S(1)}, bf16[1040,128]{1,0:T(8,128)(2,1)S(1)}, u32[]{:S(2)}, u32[]{:S(2)}) collective-permute-start(bf16[1040,128]{1,0:T(8,128)(2,1)S(1)} %shard_map.87), channel_id=1, source_target_pairs={{0,4},{1,5},{2,6},{3,7},{4,0},{5,1},{6,2},{7,3},{8,12},{9,13},{10,... | collective-permute-start | bytes 798728 | tf_op jit(solution)/shard_map/ppermute | solution.py:575
  39.0 1.1 %collective-permute-done.7.refs_0_ = bf16[1040,128]{1,0:T(8,128)(2,1)S(1)} collective-permute-done((bf16[1040,128]{1,0:T(8,128)(2,1)S(1)}, bf16[1040,128]{1,0:T(8,128)(2,1)S(1)}, u32[]{:S(2)}, u32[]{:S(2)}) %collective-permute-start.7) | collective-permute-done | bytes 266272 | tf_op jit(solution)/shard_map/ppermute | solution.py:575
  40.1 0.7 %shard_map.89 = bf16[1040,128]{1,0:T(8,128)(2,1)S(1)} custom-call(s32[1]{0:T(128)} %bitcast.place_ref, bf16[8192,1024]{1,0:T(8,128)(2,1)S(1)} %bitcast.11, bf16[1024,256]{1,0:T(8,128)(2,1)S(1)} %get-tuple-element.37.g_ref.turned_ref, bf16[1040,128]{1,0:T(8,128)(2,1)S(1)} %collective-permute-done.7.refs_0_), custom_call_target="tpu_custom_call" | custom-call | bytes 1024 | tf_op jit(solution)/shard_map/pallas_call | solution.py:131
  40.8 0.0 copy-start
  40.9 0.0 copy-start.1
  40.9 1.6 %collective-permute-start.12 = (bf16[1040,128]{1,0:T(8,128)(2,1)S(1)}, bf16[1040,128]{1,0:T(8,128)(2,1)S(1)}, u32[]{:S(2)}, u32[]{:S(2)}) collective-permute-start(bf16[1040,128]{1,0:T(8,128)(2,1)S(1)} %shard_map.89), channel_id=1, source_target_pairs={{0,2},{1,3},{2,0},{3,1},{4,6},{5,7},{6,4},{7,5},{8,10},{9,11},{10,... | collective-permute-start | bytes 798728 | tf_op jit(solution)/shard_map/ppermute | solution.py:575
  42.5 0.6 shard_map.90
  43.1 2.0 %collective-permute-done.8.refs_2_ = bf16[1040,128]{1,0:T(8,128)(2,1)S(1)} collective-permute-done((bf16[1040,128]{1,0:T(8,128)(2,1)S(1)}, bf16[1040,128]{1,0:T(8,128)(2,1)S(1)}, u32[]{:S(2)}, u32[]{:S(2)}) %collective-permute-start.8) | collective-permute-done | bytes 266272 | tf_op jit(solution)/shard_map/ppermute | solution.py:575
  45.1 0.5 collective-permute-start.13
  45.6 0.0 copy-done.2
  45.6 0.0 copy-done.3
  45.7 0.4 shard_map.91.acc_ref
  46.2 1.1 %collective-permute-done.9.refs_1_ = bf16[1040,128]{1,0:T(8,128)(2,1)S(1)} collective-permute-done((bf16[1040,128]{1,0:T(8,128)(2,1)S(1)}, bf16[1040,128]{1,0:T(8,128)(2,1)S(1)}, u32[]{:S(2)}, u32[]{:S(2)}) %collective-permute-start.9) | collective-permute-done | bytes 266272 | tf_op jit(solution)/shard_map/ppermute | solution.py:575
  47.3 0.0 collective-permute-done.10.refs_0_
  47.4 1.9 %shard_map.93 = (bf16[256,1024]{1,0:T(8,128)(2,1)}, f32[1088,128]{1,0:T(8,128)S(1)}, f32[16,8,128]{2,1,0:T(8,128)S(1)}, f32[8,8,128]{2,1,0:T(8,128)S(1)}) custom-call(f32[512,256]{1,0:T(8,128)S(1)} %shard_map.91.acc_ref, bf16[1040,128]{1,0:T(8,128)(2,1)S(1)} %collective-permute-done.10.refs_0_, bf16[1040,128]{1,0:T(8,128)(2,1)S(1)} %collective-permute-done.9.refs_1_, ...), custom_call_target="tpu_custom_call" | custom-call | bytes 1024 | tf_op jit(solution)/shard_map/pallas_call | solution.py:304
  49.3 1.6 %collective-permute-done.11.refs_2_ = bf16[1040,128]{1,0:T(8,128)(2,1)S(1)} collective-permute-done((bf16[1040,128]{1,0:T(8,128)(2,1)S(1)}, bf16[1040,128]{1,0:T(8,128)(2,1)S(1)}, u32[]{:S(2)}, u32[]{:S(2)}) %collective-permute-start.11) | collective-permute-done | bytes 266272 | tf_op jit(solution)/shard_map/ppermute | solution.py:575
  50.9 0.6 collective-permute-done.12.refs_1_
  51.4 0.1 collective-permute-done.13.refs_0_
  51.5 1.3 %shard_map.94 = (bf16[256,1024]{1,0:T(8,128)(2,1)}, f32[1088,128]{1,0:T(8,128)S(1)}, f32[16,8,128]{2,1,0:T(8,128)S(1)}, f32[16,8,128]{2,1,0:T(8,128)S(1)}) custom-call(f32[512,256]{1,0:T(8,128)S(1)} %shard_map.79.acc_ref, bf16[1040,128]{1,0:T(8,128)(2,1)S(1)} %collective-permute-done.13.refs_0_, ...), custom_call_target="tpu_custom_call", output_to_operand_aliasing={{0}: (9, {})} | custom-call | bytes 1024 | tf_op jit(solution)/shard_map/pallas_call | solution.py:304
  52.9 0.1 collective-permute-start.14
  53.0 1.2 %collective-permute-done.14.arrived_ref.refs_3_ = f32[16,8,128]{2,1,0:T(8,128)S(1)} collective-permute-done((f32[16,8,128]{2,1,0:T(8,128)S(1)}, f32[16,8,128]{2,1,0:T(8,128)S(1)}, u32[]{:S(2)}, u32[]{:S(2)}) %collective-permute-start.14) | collective-permute-done | bytes 65568 | tf_op jit(solution)/shard_map/ppermute | solution.py:612
  54.2 0.1 shard_map.95
  54.3 1.5 %collective-permute-start.15 = (bf16[144,128]{1,0:T(8,128)(2,1)S(1)}, bf16[144,128]{1,0:T(8,128)(2,1)S(1)}, u32[]{:S(2)}, u32[]{:S(2)}) collective-permute-start(bf16[144,128]{1,0:T(8,128)(2,1)S(1)} %shard_map.95), channel_id=1, source_target_pairs={{0,16},{8,24},{16,0},{24,8},{1,17},{9,25},{17,1},{25,9},{2,18},{10... | collective-permute-start | bytes 110600 | tf_op jit(solution)/shard_map/ppermute | solution.py:612
  55.7 1.2 %shard_map.96.refs_1_ = f32[1088,128]{1,0:T(8,128)S(1)} custom-call(f32[1088,128]{1,0:T(8,128)S(1)} %get-tuple-element.65.gc_ref, f32[16,8,128]{2,1,0:T(8,128)S(1)} %get-tuple-element.66.state_ref, f32[16,16,128]{2,1,0:T(8,128)S(1)} %bitcast.15, f32[16,16,128]{2,1,0:T(8,128)S(1)} %get-tuple-element.56.refs_6_.lap_ref, f32[16,16,128]{2,1,0:T(8,128)S(1)} %bitcast.18), custom_call_target="tpu_custom_call" | custom-call | bytes 1024 | tf_op jit(solution)/shard_map/pallas_call | solution.py:354
  56.9 1.4 %collective-permute-done.15.refs_4_ = bf16[144,128]{1,0:T(8,128)(2,1)S(1)} collective-permute-done((bf16[144,128]{1,0:T(8,128)(2,1)S(1)}, bf16[144,128]{1,0:T(8,128)(2,1)S(1)}, u32[]{:S(2)}, u32[]{:S(2)}) %collective-permute-start.15) | collective-permute-done | bytes 36896 | tf_op jit(solution)/shard_map/ppermute | solution.py:612
  58.3 2.2 %shard_map.97 = bf16[256,1024]{1,0:T(8,128)(2,1)} custom-call(s32[1]{0:T(128)} %bitcast.5.group_ref, f32[1088,128]{1,0:T(8,128)S(1)} %get-tuple-element.61.refs_0_, f32[1088,128]{1,0:T(8,128)S(1)} %shard_map.96.refs_1_, f32[16,8,128]{2,1,0:T(8,128)S(1)} %get-tuple-element.67.refs_2_, f32[16,8,128]{2,1,0:T(8,128)S(1)} %collective-permute-done.14.arrived_ref.refs_3_, ...), custom_call_target="tpu_custom_call" | custom-call | bytes 1024 | tf_op jit(solution)/shard_map/pallas_call | solution.py:491
  (10 shorter events, 0.2 us)
Async XLA Ops:
  0.6 10.8 %slice-start = ((s8[16777216]{0:T(1024)(128)(4,1)}), s8[4194304]{0:T(1024)(128)(4,1)S(1)}, s32[]{:S(2)}) async-start(s8[16777216]{0:T(1024)(128)(4,1)} %bitcast.10), calls=%async_computation | async-start | bytes 8388608
  0.6 10.8 %slice-start.1 = ((s8[16777216]{0:T(1024)(128)(4,1)}), s8[4194304]{0:T(1024)(128)(4,1)S(1)}, s32[]{:S(2)}) async-start(s8[16777216]{0:T(1024)(128)(4,1)} %bitcast.10), calls=%async_computation.1 | async-start | bytes 8388608
  3.0 10.1 %collective-permute-start = (bf16[1040,128]{1,0:T(8,128)(2,1)S(1)}, bf16[1040,128]{1,0:T(8,128)(2,1)S(1)}, u32[]{:S(2)}, u32[]{:S(2)}) collective-permute-start(bf16[1040,128]{1,0:T(8,128)(2,1)S(1)} %get-tuple-element.35), channel_id=1, source_target_pairs={{0,1},{1,0},{2,3},{3,2},{4,5},{5,4},{6,7},{7,6},{8,9},{9,8},{10,11... | collective-permute-start | bytes 798728 | tf_op jit(solution)/shard_map/ppermute | solution.py:575
  6.1 5.4 %slice-start.2 = ((s8[16777216]{0:T(1024)(128)(4,1)}), s8[4194304]{0:T(1024)(128)(4,1)S(1)}, s32[]{:S(2)}) async-start(s8[16777216]{0:T(1024)(128)(4,1)} %bitcast.10), calls=%async_computation.2 | async-start | bytes 8388608
  6.1 5.4 %slice-start.3 = ((s8[16777216]{0:T(1024)(128)(4,1)}), s8[4194304]{0:T(1024)(128)(4,1)S(1)}, s32[]{:S(2)}) async-start(s8[16777216]{0:T(1024)(128)(4,1)} %bitcast.10), calls=%async_computation.3 | async-start | bytes 8388608
  9.3 9.4 %collective-permute-start.1 = (bf16[1040,128]{1,0:T(8,128)(2,1)S(1)}, bf16[1040,128]{1,0:T(8,128)(2,1)S(1)}, u32[]{:S(2)}, u32[]{:S(2)}) collective-permute-start(bf16[1040,128]{1,0:T(8,128)(2,1)S(1)} %get-tuple-element.38), channel_id=1, source_target_pairs={{0,2},{1,3},{2,0},{3,1},{4,6},{5,7},{6,4},{7,5},{8,10},{9,11},{10,... | collective-permute-start | bytes 798728 | tf_op jit(solution)/shard_map/ppermute | solution.py:575
  10.9 10.5 %collective-permute-start.2 = (bf16[1040,128]{1,0:T(8,128)(2,1)S(1)}, bf16[1040,128]{1,0:T(8,128)(2,1)S(1)}, u32[]{:S(2)}, u32[]{:S(2)}) collective-permute-start(bf16[1040,128]{1,0:T(8,128)(2,1)S(1)} %get-tuple-element.45), channel_id=1, source_target_pairs={{0,1},{1,0},{2,3},{3,2},{4,5},{5,4},{6,7},{7,6},{8,9},{9,8},{10,11... | collective-permute-start | bytes 798728 | tf_op jit(solution)/shard_map/ppermute | solution.py:575
  13.8 10.6 %collective-permute-start.3 = (bf16[1040,128]{1,0:T(8,128)(2,1)S(1)}, bf16[1040,128]{1,0:T(8,128)(2,1)S(1)}, u32[]{:S(2)}, u32[]{:S(2)}) collective-permute-start(bf16[1040,128]{1,0:T(8,128)(2,1)S(1)} %shard_map.82), channel_id=1, source_target_pairs={{0,2},{1,3},{2,0},{3,1},{4,6},{5,7},{6,4},{7,5},{8,10},{9,11},{10,... | collective-permute-start | bytes 798728 | tf_op jit(solution)/shard_map/ppermute | solution.py:575
  19.3 9.4 %collective-permute-start.4 = (bf16[1040,128]{1,0:T(8,128)(2,1)S(1)}, bf16[1040,128]{1,0:T(8,128)(2,1)S(1)}, u32[]{:S(2)}, u32[]{:S(2)}) collective-permute-start(bf16[1040,128]{1,0:T(8,128)(2,1)S(1)} %shard_map.83), channel_id=1, source_target_pairs={{0,1},{1,0},{2,3},{3,2},{4,5},{5,4},{6,7},{7,6},{8,9},{9,8},{10,11... | collective-permute-start | bytes 798728 | tf_op jit(solution)/shard_map/ppermute | solution.py:575
  19.4 15.0 %collective-permute-start.5 = (bf16[1040,128]{1,0:T(8,128)(2,1)S(1)}, bf16[1040,128]{1,0:T(8,128)(2,1)S(1)}, u32[]{:S(2)}, u32[]{:S(2)}) collective-permute-start(bf16[1040,128]{1,0:T(8,128)(2,1)S(1)} %shard_map.81), channel_id=1, source_target_pairs={{0,1},{1,0},{2,3},{3,2},{4,5},{5,4},{6,7},{7,6},{8,9},{9,8},{10,11... | collective-permute-start | bytes 798728 | tf_op jit(solution)/shard_map/ppermute | solution.py:575
  22.1 12.3 %collective-permute-start.6 = (bf16[1040,128]{1,0:T(8,128)(2,1)S(1)}, bf16[1040,128]{1,0:T(8,128)(2,1)S(1)}, u32[]{:S(2)}, u32[]{:S(2)}) collective-permute-start(bf16[1040,128]{1,0:T(8,128)(2,1)S(1)} %shard_map.84), channel_id=1, source_target_pairs={{0,2},{1,3},{2,0},{3,1},{4,6},{5,7},{6,4},{7,5},{8,10},{9,11},{10,... | collective-permute-start | bytes 798728 | tf_op jit(solution)/shard_map/ppermute | solution.py:575
  23.8 16.4 %collective-permute-start.7 = (bf16[1040,128]{1,0:T(8,128)(2,1)S(1)}, bf16[1040,128]{1,0:T(8,128)(2,1)S(1)}, u32[]{:S(2)}, u32[]{:S(2)}) collective-permute-start(bf16[1040,128]{1,0:T(8,128)(2,1)S(1)} %shard_map.80), channel_id=1, source_target_pairs={{0,1},{1,0},{2,3},{3,2},{4,5},{5,4},{6,7},{7,6},{8,9},{9,8},{10,11... | collective-permute-start | bytes 798728 | tf_op jit(solution)/shard_map/ppermute | solution.py:575
  29.6 15.5 %collective-permute-start.8 = (bf16[1040,128]{1,0:T(8,128)(2,1)S(1)}, bf16[1040,128]{1,0:T(8,128)(2,1)S(1)}, u32[]{:S(2)}, u32[]{:S(2)}) collective-permute-start(bf16[1040,128]{1,0:T(8,128)(2,1)S(1)} %shard_map.86), channel_id=1, source_target_pairs={{0,4},{1,5},{2,6},{3,7},{4,0},{5,1},{6,2},{7,3},{8,12},{9,13},{10,... | collective-permute-start | bytes 798728 | tf_op jit(solution)/shard_map/ppermute | solution.py:575
  32.3 15.1 %collective-permute-start.9 = (bf16[1040,128]{1,0:T(8,128)(2,1)S(1)}, bf16[1040,128]{1,0:T(8,128)(2,1)S(1)}, u32[]{:S(2)}, u32[]{:S(2)}) collective-permute-start(bf16[1040,128]{1,0:T(8,128)(2,1)S(1)} %shard_map.85), channel_id=1, source_target_pairs={{0,2},{1,3},{2,0},{3,1},{4,6},{5,7},{6,4},{7,5},{8,10},{9,11},{10,... | collective-permute-start | bytes 798728 | tf_op jit(solution)/shard_map/ppermute | solution.py:575
  36.0 9.6 %copy-start.2 = (f32[1024,16]{0,1:T(8,128)S(1)}, f32[1024,16]{0,1:T(8,128)}, u32[]{:S(2)}) copy-start(f32[1024,16]{0,1:T(8,128)} %param.10) | copy-start | bytes 196612
  36.0 9.7 %copy-start.3 = (f32[1024,16]{0,1:T(8,128)S(1)}, f32[1024,16]{0,1:T(8,128)}, u32[]{:S(2)}) copy-start(f32[1024,16]{0,1:T(8,128)} %param.11) | copy-start | bytes 196612
  36.0 11.3 %collective-permute-start.10 = (bf16[1040,128]{1,0:T(8,128)(2,1)S(1)}, bf16[1040,128]{1,0:T(8,128)(2,1)S(1)}, u32[]{:S(2)}, u32[]{:S(2)}) collective-permute-start(bf16[1040,128]{1,0:T(8,128)(2,1)S(1)} %shard_map.88), channel_id=1, source_target_pairs={{0,1},{1,0},{2,3},{3,2},{4,5},{5,4},{6,7},{7,6},{8,9},{9,8},{10,11... | collective-permute-start | bytes 798728 | tf_op jit(solution)/shard_map/ppermute | solution.py:575
  36.1 14.8 %collective-permute-start.11 = (bf16[1040,128]{1,0:T(8,128)(2,1)S(1)}, bf16[1040,128]{1,0:T(8,128)(2,1)S(1)}, u32[]{:S(2)}, u32[]{:S(2)}) collective-permute-start(bf16[1040,128]{1,0:T(8,128)(2,1)S(1)} %shard_map.87), channel_id=1, source_target_pairs={{0,4},{1,5},{2,6},{3,7},{4,0},{5,1},{6,2},{7,3},{8,12},{9,13},{10,... | collective-permute-start | bytes 798728 | tf_op jit(solution)/shard_map/ppermute | solution.py:575
  40.8 6.5 %copy-start = (bf16[256,1024]{1,0:T(8,128)(2,1)S(1)}, bf16[256,1024]{1,0:T(8,128)(2,1)}, u32[]{:S(2)}) copy-start(bf16[256,1024]{1,0:T(8,128)(2,1)} %refs_3_.3) | copy-start | bytes 1572868
  40.9 6.5 %copy-start.1 = (bf16[256,1024]{1,0:T(8,128)(2,1)S(1)}, bf16[256,1024]{1,0:T(8,128)(2,1)}, u32[]{:S(2)}) copy-start(bf16[256,1024]{1,0:T(8,128)(2,1)} %refs_4_.3) | copy-start | bytes 1572868
  40.9 10.6 %collective-permute-start.12 = (bf16[1040,128]{1,0:T(8,128)(2,1)S(1)}, bf16[1040,128]{1,0:T(8,128)(2,1)S(1)}, u32[]{:S(2)}, u32[]{:S(2)}) collective-permute-start(bf16[1040,128]{1,0:T(8,128)(2,1)S(1)} %shard_map.89), channel_id=1, source_target_pairs={{0,2},{1,3},{2,0},{3,1},{4,6},{5,7},{6,4},{7,5},{8,10},{9,11},{10,... | collective-permute-start | bytes 798728 | tf_op jit(solution)/shard_map/ppermute | solution.py:575
  45.1 6.4 %collective-permute-start.13 = (bf16[1040,128]{1,0:T(8,128)(2,1)S(1)}, bf16[1040,128]{1,0:T(8,128)(2,1)S(1)}, u32[]{:S(2)}, u32[]{:S(2)}) collective-permute-start(bf16[1040,128]{1,0:T(8,128)(2,1)S(1)} %shard_map.90), channel_id=1, source_target_pairs={{0,1},{1,0},{2,3},{3,2},{4,5},{5,4},{6,7},{7,6},{8,9},{9,8},{10,11... | collective-permute-start | bytes 798728 | tf_op jit(solution)/shard_map/ppermute | solution.py:575
  52.9 1.3 %collective-permute-start.14 = (f32[16,8,128]{2,1,0:T(8,128)S(1)}, f32[16,8,128]{2,1,0:T(8,128)S(1)}, u32[]{:S(2)}, u32[]{:S(2)}) collective-permute-start(f32[16,8,128]{2,1,0:T(8,128)S(1)} %get-tuple-element.63.state_ref), channel_id=1, source_target_pairs={{0,8},{8,0},{16,24},{24,16},{1,9},{9,1},{17,25},{25,17},{2,10},{10... | collective-permute-start | bytes 196616 | tf_op jit(solution)/shard_map/ppermute | solution.py:612
  54.3 4.0 %collective-permute-start.15 = (bf16[144,128]{1,0:T(8,128)(2,1)S(1)}, bf16[144,128]{1,0:T(8,128)(2,1)S(1)}, u32[]{:S(2)}, u32[]{:S(2)}) collective-permute-start(bf16[144,128]{1,0:T(8,128)(2,1)S(1)} %shard_map.95), channel_id=1, source_target_pairs={{0,16},{8,24},{16,0},{24,8},{1,17},{9,25},{17,1},{25,9},{2,18},{10... | collective-permute-start | bytes 110600 | tf_op jit(solution)/shard_map/ppermute | solution.py:612

commit v17 on v16

--- a/solution.py
+++ b/solution.py
@@ -19,8 +19,8 @@
 
 PORTIONS = (((0, 1, 2), 4, 0), ((1, 0, 2), 4, 0), ((0, 1, 2), 4, 1), ((0, 1, 2), 4, 1))
 ORDER = (
-    ((0, 0, 6), (0, 0, 2)), ("both", ((1, 0, 5), (1, 0, 1)), ((2, 0, 6), (3, 0, 6))), ("sum", 1), ((2, 0, 2), (3, 0, 2)),
-    ((2, 0, 4), (3, 0, 4)), ((1, 0, 4), (0, 1, 4)), ((1, 1, 4), (0, 0, 4)), ((2, 1, 4), (3, 1, 4)),
+    ((0, 0, 6), (0, 0, 2)), ("both", ((1, 0, 5), (1, 0, 1))), ((2, 0, 6), (3, 0, 6)), ((2, 0, 4), (3, 0, 4)), ("sum", 1), ((2, 0, 2), (3, 0, 2)),
+    ((1, 0, 4), (0, 1, 4)), ((1, 1, 4), (0, 0, 4)), ((2, 1, 4), (3, 1, 4)),
     ((1, 0, 0), (0, 1, 0)), ((0, 2, 0), (1, 2, 0)), ((2, 2, 0), (3, 2, 0)), ((1, 1, 0), (0, 0, 0)),
     ((2, 1, 0), (3, 1, 0)), ((2, 0, 0), (3, 0, 0)), ("sum", 0), ("laps", None), ("gate", 0), ("gate", 1), ("scan", 1),
     ("fix", None),

time: 60.7 us -> 59.6 us (0.982)
  waiting for transfers between devices: 16.4 us -> 11.7 us
  starting transfers between devices: 22.3 us -> 26.2 us
    ppermute x14, waiting for transfers between devices: 13.7 us -> 9.17 us  [local(): arrived = lax.ppermute(payload, 'ch', [(i, i ^ bit) for i in range(size)])]
    ppermute x14, starting transfers between devices: 20.7 us -> 24.6 us  [local(): arrived = lax.ppermute(payload, 'ch', [(i, i ^ bit) for i in range(size)])]
    pallas_call x2, Pallas kernels: 5.57 us -> 4.58 us  [early_send(): pl.pallas_call(functools.partial(early_kernel, messages, width, turns), i...]
    pallas_call x13 -> x14, Pallas kernels: 8.53 us -> 9.17 us  [send(): pl.pallas_call(functools.partial(send_kernel, items, coded, width, len(ne...]
  transfers between devices with their start and end apart: 16 -> 16, of which waited for: 12 -> 9; matrix products, arithmetic and copies ran while one was open for 0% -> 0% of each run, Pallas kernels for 24% -> 24%
where the time goes in v17:
time: 59.6 us; the launch traced here: 59.4 us
  starting transfers between devices  26.2 us (44%)
  Pallas kernels  20.4 us (34%)
  waiting for transfers between devices  11.7 us (20%)
  between operations  0.95 us (2%)
    ppermute x14, starting transfers between devices, local(): arrived = lax.ppermute(payload, 'ch', [(i, i ^ bit) for i in range(size)])  24.6 us
    pallas_call x14, Pallas kernels, send(): pl.pallas_call(functools.partial(send_kernel, items, coded, width, len(ne...  9.17 us
    ppermute x14, waiting for transfers between devices, local(): arrived = lax.ppermute(payload, 'ch', [(i, i ^ bit) for i in range(size)])  9.17 us
    pallas_call x2, Pallas kernels, early_send(): pl.pallas_call(functools.partial(early_kernel, messages, width, turns), i...  4.58 us
    pallas_call x2, Pallas kernels, gate(): pl.pallas_call(functools.partial(gate_kernel, half, rows, segments, piece...  3.2 us
    ppermute x2, waiting for transfers between devices, local(): lax.ppermute(array, 'ctx', [(i, i ^ 1 << round_) for i in range(groups)])  2.53 us
    pallas_call x1, Pallas kernels, fix(): pl.pallas_call(functools.partial(fix_kernel, segments, len(arrived)), in_...  2.23 us
    ppermute x2, starting transfers between devices, local(): lax.ppermute(array, 'ctx', [(i, i ^ 1 << round_) for i in range(groups)])  1.63 us
  transfers between devices with their start and end apart: 16, of which 9 were waited for; matrix products, arithmetic and copies ran while one was open for 0% of the time, Pallas kernels for 24%

profile of v17, /device:TPU:0, one launch (start us, length us, event | category | flops | bytes accessed | tf_op | source)
XLA Modules:
  0.0 59.4 jit_solution(4617484541663871848)
XLA Ops:
  0.6 0.0 slice-start
  0.6 0.0 slice-start.1
  0.7 2.4 %shard_map.77 = (bf16[1040,128]{1,0:T(8,128)(2,1)S(1)}, bf16[1024,256]{1,0:T(8,128)(2,1)S(1)}) custom-call(s32[1]{0:T(128)} %bitcast.place_ref, bf16[8192,1024]{1,0:T(8,128)(2,1)} %w_ref.27, bf16[256,1024]{1,0:T(8,128)(2,1)} %g_ref.1), custom_call_target="tpu_custom_call" | custom-call | bytes 1024 | tf_op jit(solution)/shard_map/pallas_call | solution.py:194
  3.1 3.0 %collective-permute-start = (bf16[1040,128]{1,0:T(8,128)(2,1)S(1)}, bf16[1040,128]{1,0:T(8,128)(2,1)S(1)}, u32[]{:S(2)}, u32[]{:S(2)}) collective-permute-start(bf16[1040,128]{1,0:T(8,128)(2,1)S(1)} %get-tuple-element.34), channel_id=1, source_target_pairs={{0,1},{1,0},{2,3},{3,2},{4,5},{5,4},{6,7},{7,6},{8,9},{9,8},{10,11... | collective-permute-start | bytes 798728 | tf_op jit(solution)/shard_map/ppermute | solution.py:575
  6.1 2.2 %shard_map.78 = bf16[1040,128]{1,0:T(8,128)(2,1)S(1)} custom-call(s32[1]{0:T(128)} %bitcast.place_ref, bf16[8192,1024]{1,0:T(8,128)(2,1)} %w_ref.27, bf16[1024,256]{1,0:T(8,128)(2,1)S(1)} %get-tuple-element.36.g_ref.turned_ref), custom_call_target="tpu_custom_call" | custom-call | bytes 1024 | tf_op jit(solution)/shard_map/pallas_call | solution.py:194
  8.3 1.6 %collective-permute-start.1 = (bf16[1040,128]{1,0:T(8,128)(2,1)S(1)}, bf16[1040,128]{1,0:T(8,128)(2,1)S(1)}, u32[]{:S(2)}, u32[]{:S(2)}) collective-permute-start(bf16[1040,128]{1,0:T(8,128)(2,1)S(1)} %shard_map.78), channel_id=1, source_target_pairs={{0,2},{1,3},{2,0},{3,1},{4,6},{5,7},{6,4},{7,5},{8,10},{9,11},{10,... | collective-permute-start | bytes 798728 | tf_op jit(solution)/shard_map/ppermute | solution.py:575
  9.9 0.0 slice-done
  9.9 0.0 slice-done.1
  9.9 0.0 slice-done.2
  9.9 0.0 slice-done.3
  10.0 0.6 %shard_map.79 = bf16[1040,128]{1,0:T(8,128)(2,1)S(1)} custom-call(s32[1]{0:T(128)} %bitcast.place_ref, bf16[8192,1024]{1,0:T(8,128)(2,1)S(1)} %bitcast.11, bf16[1024,256]{1,0:T(8,128)(2,1)S(1)} %get-tuple-element.36.g_ref.turned_ref), custom_call_target="tpu_custom_call" | custom-call | bytes 1024 | tf_op jit(solution)/shard_map/pallas_call | solution.py:131
  10.6 0.6 collective-permute-start.2
  11.1 0.6 %shard_map.80 = bf16[1040,128]{1,0:T(8,128)(2,1)S(1)} custom-call(s32[1]{0:T(128)} %bitcast.place_ref, bf16[8192,1024]{1,0:T(8,128)(2,1)S(1)} %bitcast.11, bf16[1024,256]{1,0:T(8,128)(2,1)S(1)} %get-tuple-element.36.g_ref.turned_ref), custom_call_target="tpu_custom_call" | custom-call | bytes 1024 | tf_op jit(solution)/shard_map/pallas_call | solution.py:131
  11.8 0.4 shard_map.81.acc_ref
  12.2 0.6 %shard_map.82 = bf16[1040,128]{1,0:T(8,128)(2,1)S(1)} custom-call(s32[1]{0:T(128)} %bitcast.place_ref, bf16[8192,1024]{1,0:T(8,128)(2,1)S(1)} %bitcast.11, bf16[1024,256]{1,0:T(8,128)(2,1)S(1)} %get-tuple-element.36.g_ref.turned_ref), custom_call_target="tpu_custom_call" | custom-call | bytes 1024 | tf_op jit(solution)/shard_map/pallas_call | solution.py:131
  12.8 0.0 collective-permute-done.refs_0_
  12.8 0.7 %shard_map.83 = bf16[1040,128]{1,0:T(8,128)(2,1)S(1)} custom-call(s32[1]{0:T(128)} %bitcast.place_ref, bf16[8192,1024]{1,0:T(8,128)(2,1)S(1)} %bitcast.11, bf16[1024,256]{1,0:T(8,128)(2,1)S(1)} %get-tuple-element.36.g_ref.turned_ref, bf16[1040,128]{1,0:T(8,128)(2,1)S(1)} %collective-permute-done.refs_0_), custom_call_target="tpu_custom_call" | custom-call | bytes 1024 | tf_op jit(solution)/shard_map/pallas_call | solution.py:131
  13.5 1.7 %collective-permute-start.3 = (bf16[1040,128]{1,0:T(8,128)(2,1)S(1)}, bf16[1040,128]{1,0:T(8,128)(2,1)S(1)}, u32[]{:S(2)}, u32[]{:S(2)}) collective-permute-start(bf16[1040,128]{1,0:T(8,128)(2,1)S(1)} %shard_map.83), channel_id=1, source_target_pairs={{0,2},{1,3},{2,0},{3,1},{4,6},{5,7},{6,4},{7,5},{8,10},{9,11},{10,... | collective-permute-start | bytes 798728 | tf_op jit(solution)/shard_map/ppermute | solution.py:575
  15.2 1.4 %collective-permute-done.1.refs_0_ = bf16[1040,128]{1,0:T(8,128)(2,1)S(1)} collective-permute-done((bf16[1040,128]{1,0:T(8,128)(2,1)S(1)}, bf16[1040,128]{1,0:T(8,128)(2,1)S(1)}, u32[]{:S(2)}, u32[]{:S(2)}) %collective-permute-start.1) | collective-permute-done | bytes 266272 | tf_op jit(solution)/shard_map/ppermute | solution.py:575
  16.6 0.7 %shard_map.84 = bf16[1040,128]{1,0:T(8,128)(2,1)S(1)} custom-call(s32[1]{0:T(128)} %bitcast.place_ref, bf16[8192,1024]{1,0:T(8,128)(2,1)S(1)} %bitcast.11, bf16[1024,256]{1,0:T(8,128)(2,1)S(1)} %get-tuple-element.36.g_ref.turned_ref, bf16[1040,128]{1,0:T(8,128)(2,1)S(1)} %collective-permute-done.1.refs_0_), custom_call_target="tpu_custom_call" | custom-call | bytes 1024 | tf_op jit(solution)/shard_map/pallas_call | solution.py:131
  17.3 0.5 collective-permute-start.4
  17.8 1.6 %collective-permute-start.5 = (bf16[1040,128]{1,0:T(8,128)(2,1)S(1)}, bf16[1040,128]{1,0:T(8,128)(2,1)S(1)}, u32[]{:S(2)}, u32[]{:S(2)}) collective-permute-start(bf16[1040,128]{1,0:T(8,128)(2,1)S(1)} %shard_map.80), channel_id=1, source_target_pairs={{0,1},{1,0},{2,3},{3,2},{4,5},{5,4},{6,7},{7,6},{8,9},{9,8},{10,11... | collective-permute-start | bytes 798728 | tf_op jit(solution)/shard_map/ppermute | solution.py:575
  19.4 0.0 collective-permute-done.2.refs_0_
  19.4 0.7 %shard_map.85 = bf16[1040,128]{1,0:T(8,128)(2,1)S(1)} custom-call(s32[1]{0:T(128)} %bitcast.place_ref, bf16[8192,1024]{1,0:T(8,128)(2,1)S(1)} %bitcast.11, bf16[1024,256]{1,0:T(8,128)(2,1)S(1)} %get-tuple-element.36.g_ref.turned_ref, bf16[1040,128]{1,0:T(8,128)(2,1)S(1)} %collective-permute-done.2.refs_0_), custom_call_target="tpu_custom_call" | custom-call | bytes 1024 | tf_op jit(solution)/shard_map/pallas_call | solution.py:131
  20.1 1.6 %collective-permute-start.6 = (bf16[1040,128]{1,0:T(8,128)(2,1)S(1)}, bf16[1040,128]{1,0:T(8,128)(2,1)S(1)}, u32[]{:S(2)}, u32[]{:S(2)}) collective-permute-start(bf16[1040,128]{1,0:T(8,128)(2,1)S(1)} %shard_map.85), channel_id=1, source_target_pairs={{0,2},{1,3},{2,0},{3,1},{4,6},{5,7},{6,4},{7,5},{8,10},{9,11},{10,... | collective-permute-start | bytes 798728 | tf_op jit(solution)/shard_map/ppermute | solution.py:575
  21.7 1.1 %collective-permute-start.7 = (bf16[1040,128]{1,0:T(8,128)(2,1)S(1)}, bf16[1040,128]{1,0:T(8,128)(2,1)S(1)}, u32[]{:S(2)}, u32[]{:S(2)}) collective-permute-start(bf16[1040,128]{1,0:T(8,128)(2,1)S(1)} %shard_map.82), channel_id=1, source_target_pairs={{0,1},{1,0},{2,3},{3,2},{4,5},{5,4},{6,7},{7,6},{8,9},{9,8},{10,11... | collective-permute-start | bytes 798728 | tf_op jit(solution)/shard_map/ppermute | solution.py:575
  22.9 0.0 collective-permute-done.3.refs_1_
  22.9 0.7 %shard_map.86 = bf16[1040,128]{1,0:T(8,128)(2,1)S(1)} custom-call(s32[1]{0:T(128)} %bitcast.place_ref, bf16[8192,1024]{1,0:T(8,128)(2,1)S(1)} %bitcast.11, bf16[1024,256]{1,0:T(8,128)(2,1)S(1)} %get-tuple-element.36.g_ref.turned_ref, bf16[1040,128]{1,0:T(8,128)(2,1)S(1)} %collective-permute-done.refs_0_), custom_call_target="tpu_custom_call" | custom-call | bytes 1024 | tf_op jit(solution)/shard_map/pallas_call | solution.py:131
  23.6 3.1 %collective-permute-done.4.refs_0_ = bf16[1040,128]{1,0:T(8,128)(2,1)S(1)} collective-permute-done((bf16[1040,128]{1,0:T(8,128)(2,1)S(1)}, bf16[1040,128]{1,0:T(8,128)(2,1)S(1)}, u32[]{:S(2)}, u32[]{:S(2)}) %collective-permute-start.4) | collective-permute-done | bytes 266272 | tf_op jit(solution)/shard_map/ppermute | solution.py:575
  26.7 0.9 %shard_map.87 = bf16[1040,128]{1,0:T(8,128)(2,1)S(1)} custom-call(s32[1]{0:T(128)} %bitcast.place_ref, bf16[8192,1024]{1,0:T(8,128)(2,1)S(1)} %bitcast.11, bf16[1024,256]{1,0:T(8,128)(2,1)S(1)} %get-tuple-element.36.g_ref.turned_ref, bf16[1040,128]{1,0:T(8,128)(2,1)S(1)} %collective-permute-done.4.refs_0_, bf16[1040,128]{1,0:T(8,128)(2,1)S(1)} %collective-permute-done.3.refs_1_), custom_call_target="tpu_custom_call" | custom-call | bytes 1024 | tf_op jit(solution)/shard_map/pallas_call | solution.py:131
  27.6 2.6 %collective-permute-start.8 = (bf16[1040,128]{1,0:T(8,128)(2,1)S(1)}, bf16[1040,128]{1,0:T(8,128)(2,1)S(1)}, u32[]{:S(2)}, u32[]{:S(2)}) collective-permute-start(bf16[1040,128]{1,0:T(8,128)(2,1)S(1)} %shard_map.87), channel_id=1, source_target_pairs={{0,4},{1,5},{2,6},{3,7},{4,0},{5,1},{6,2},{7,3},{8,12},{9,13},{10,... | collective-permute-start | bytes 798728 | tf_op jit(solution)/shard_map/ppermute | solution.py:575
  30.2 1.6 %collective-permute-start.9 = (bf16[1040,128]{1,0:T(8,128)(2,1)S(1)}, bf16[1040,128]{1,0:T(8,128)(2,1)S(1)}, u32[]{:S(2)}, u32[]{:S(2)}) collective-permute-start(bf16[1040,128]{1,0:T(8,128)(2,1)S(1)} %shard_map.86), channel_id=1, source_target_pairs={{0,2},{1,3},{2,0},{3,1},{4,6},{5,7},{6,4},{7,5},{8,10},{9,11},{10,... | collective-permute-start | bytes 798728 | tf_op jit(solution)/shard_map/ppermute | solution.py:575
  31.8 0.6 collective-permute-done.5.refs_0_
  32.4 0.0 collective-permute-done.6.refs_1_
  32.4 0.9 %shard_map.88 = bf16[1040,128]{1,0:T(8,128)(2,1)S(1)} custom-call(s32[1]{0:T(128)} %bitcast.place_ref, bf16[8192,1024]{1,0:T(8,128)(2,1)S(1)} %bitcast.11, bf16[1024,256]{1,0:T(8,128)(2,1)S(1)} %get-tuple-element.36.g_ref.turned_ref, bf16[1040,128]{1,0:T(8,128)(2,1)S(1)} %collective-permute-done.5.refs_0_, bf16[1040,128]{1,0:T(8,128)(2,1)S(1)} %collective-permute-done.6.refs_1_), custom_call_target="tpu_custom_call" | custom-call | bytes 1024 | tf_op jit(solution)/shard_map/pallas_call | solution.py:131
  33.3 0.7 %shard_map.89 = bf16[1040,128]{1,0:T(8,128)(2,1)S(1)} custom-call(s32[1]{0:T(128)} %bitcast.place_ref, bf16[8192,1024]{1,0:T(8,128)(2,1)S(1)} %bitcast.11, bf16[1024,256]{1,0:T(8,128)(2,1)S(1)} %get-tuple-element.36.g_ref.turned_ref, bf16[1040,128]{1,0:T(8,128)(2,1)S(1)} %collective-permute-done.1.refs_0_), custom_call_target="tpu_custom_call" | custom-call | bytes 1024 | tf_op jit(solution)/shard_map/pallas_call | solution.py:131
  34.0 0.0 copy-start.2
  34.0 0.0 copy-start.3
  34.0 0.5 collective-permute-start.10
  34.5 2.6 %collective-permute-start.11 = (bf16[1040,128]{1,0:T(8,128)(2,1)S(1)}, bf16[1040,128]{1,0:T(8,128)(2,1)S(1)}, u32[]{:S(2)}, u32[]{:S(2)}) collective-permute-start(bf16[1040,128]{1,0:T(8,128)(2,1)S(1)} %shard_map.88), channel_id=1, source_target_pairs={{0,4},{1,5},{2,6},{3,7},{4,0},{5,1},{6,2},{7,3},{8,12},{9,13},{10,... | collective-permute-start | bytes 798728 | tf_op jit(solution)/shard_map/ppermute | solution.py:575
  37.1 1.0 %collective-permute-done.7.refs_0_ = bf16[1040,128]{1,0:T(8,128)(2,1)S(1)} collective-permute-done((bf16[1040,128]{1,0:T(8,128)(2,1)S(1)}, bf16[1040,128]{1,0:T(8,128)(2,1)S(1)}, u32[]{:S(2)}, u32[]{:S(2)}) %collective-permute-start.7) | collective-permute-done | bytes 266272 | tf_op jit(solution)/shard_map/ppermute | solution.py:575
  38.1 0.7 %shard_map.90 = bf16[1040,128]{1,0:T(8,128)(2,1)S(1)} custom-call(s32[1]{0:T(128)} %bitcast.place_ref, bf16[8192,1024]{1,0:T(8,128)(2,1)S(1)} %bitcast.11, bf16[1024,256]{1,0:T(8,128)(2,1)S(1)} %get-tuple-element.36.g_ref.turned_ref, bf16[1040,128]{1,0:T(8,128)(2,1)S(1)} %collective-permute-done.7.refs_0_), custom_call_target="tpu_custom_call" | custom-call | bytes 1024 | tf_op jit(solution)/shard_map/pallas_call | solution.py:131
  38.8 0.0 copy-start
  38.8 0.0 copy-start.1
  38.9 1.6 %collective-permute-start.12 = (bf16[1040,128]{1,0:T(8,128)(2,1)S(1)}, bf16[1040,128]{1,0:T(8,128)(2,1)S(1)}, u32[]{:S(2)}, u32[]{:S(2)}) collective-permute-start(bf16[1040,128]{1,0:T(8,128)(2,1)S(1)} %shard_map.90), channel_id=1, source_target_pairs={{0,2},{1,3},{2,0},{3,1},{4,6},{5,7},{6,4},{7,5},{8,10},{9,11},{10,... | collective-permute-start | bytes 798728 | tf_op jit(solution)/shard_map/ppermute | solution.py:575
  40.5 0.6 %shard_map.91 = bf16[1040,128]{1,0:T(8,128)(2,1)S(1)} custom-call(s32[1]{0:T(128)} %bitcast.place_ref, bf16[8192,1024]{1,0:T(8,128)(2,1)S(1)} %bitcast.11, bf16[1024,256]{1,0:T(8,128)(2,1)S(1)} %get-tuple-element.36.g_ref.turned_ref), custom_call_target="tpu_custom_call" | custom-call | bytes 1024 | tf_op jit(solution)/shard_map/pallas_call | solution.py:131
  41.1 0.3 collective-permute-done.8.refs_2_
  41.4 3.8 %collective-permute-start.13 = (bf16[1040,128]{1,0:T(8,128)(2,1)S(1)}, bf16[1040,128]{1,0:T(8,128)(2,1)S(1)}, u32[]{:S(2)}, u32[]{:S(2)}) collective-permute-start(bf16[1040,128]{1,0:T(8,128)(2,1)S(1)} %shard_map.91), channel_id=1, source_target_pairs={{0,1},{1,0},{2,3},{3,2},{4,5},{5,4},{6,7},{7,6},{8,9},{9,8},{10,11... | collective-permute-start | bytes 798728 | tf_op jit(solution)/shard_map/ppermute | solution.py:575
  45.2 0.0 copy-done.2
  45.3 0.4 shard_map.92.acc_ref
  45.8 0.0 collective-permute-done.9.refs_1_
  45.8 0.0 collective-permute-done.10.refs_0_
  45.9 1.9 %shard_map.94 = (bf16[256,1024]{1,0:T(8,128)(2,1)}, f32[1088,128]{1,0:T(8,128)S(1)}, f32[16,8,128]{2,1,0:T(8,128)S(1)}, f32[8,8,128]{2,1,0:T(8,128)S(1)}) custom-call(f32[512,256]{1,0:T(8,128)S(1)} %shard_map.92.acc_ref, bf16[1040,128]{1,0:T(8,128)(2,1)S(1)} %collective-permute-done.10.refs_0_, bf16[1040,128]{1,0:T(8,128)(2,1)S(1)} %collective-permute-done.9.refs_1_, ...), custom_call_target="tpu_custom_call" | custom-call | bytes 1024 | tf_op jit(solution)/shard_map/pallas_call | solution.py:304
  47.8 1.2 %collective-permute-done.11.refs_2_ = bf16[1040,128]{1,0:T(8,128)(2,1)S(1)} collective-permute-done((bf16[1040,128]{1,0:T(8,128)(2,1)S(1)}, bf16[1040,128]{1,0:T(8,128)(2,1)S(1)}, u32[]{:S(2)}, u32[]{:S(2)}) %collective-permute-start.11) | collective-permute-done | bytes 266272 | tf_op jit(solution)/shard_map/ppermute | solution.py:575
  49.0 1.5 %collective-permute-done.12.refs_1_ = bf16[1040,128]{1,0:T(8,128)(2,1)S(1)} collective-permute-done((bf16[1040,128]{1,0:T(8,128)(2,1)S(1)}, bf16[1040,128]{1,0:T(8,128)(2,1)S(1)}, u32[]{:S(2)}, u32[]{:S(2)}) %collective-permute-start.12) | collective-permute-done | bytes 266272 | tf_op jit(solution)/shard_map/ppermute | solution.py:575
  50.4 0.0 collective-permute-done.13.refs_0_
  50.4 1.4 %shard_map.95 = (bf16[256,1024]{1,0:T(8,128)(2,1)}, f32[1088,128]{1,0:T(8,128)S(1)}, f32[16,8,128]{2,1,0:T(8,128)S(1)}, f32[16,8,128]{2,1,0:T(8,128)S(1)}) custom-call(f32[512,256]{1,0:T(8,128)S(1)} %shard_map.81.acc_ref, bf16[1040,128]{1,0:T(8,128)(2,1)S(1)} %collective-permute-done.13.refs_0_, ...), custom_call_target="tpu_custom_call", output_to_operand_aliasing={{0}: (9, {})} | custom-call | bytes 1024 | tf_op jit(solution)/shard_map/pallas_call | solution.py:304
  51.8 0.1 collective-permute-start.14
  51.9 1.2 %collective-permute-done.14.arrived_ref.refs_3_ = f32[16,8,128]{2,1,0:T(8,128)S(1)} collective-permute-done((f32[16,8,128]{2,1,0:T(8,128)S(1)}, f32[16,8,128]{2,1,0:T(8,128)S(1)}, u32[]{:S(2)}, u32[]{:S(2)}) %collective-permute-start.14) | collective-permute-done | bytes 65568 | tf_op jit(solution)/shard_map/ppermute | solution.py:612
  53.1 0.1 shard_map.96
  53.2 1.6 %collective-permute-start.15 = (bf16[144,128]{1,0:T(8,128)(2,1)S(1)}, bf16[144,128]{1,0:T(8,128)(2,1)S(1)}, u32[]{:S(2)}, u32[]{:S(2)}) collective-permute-start(bf16[144,128]{1,0:T(8,128)(2,1)S(1)} %shard_map.96), channel_id=1, source_target_pairs={{0,16},{8,24},{16,0},{24,8},{1,17},{9,25},{17,1},{25,9},{2,18},{10... | collective-permute-start | bytes 110600 | tf_op jit(solution)/shard_map/ppermute | solution.py:612
  54.7 1.2 %shard_map.97.refs_1_ = f32[1088,128]{1,0:T(8,128)S(1)} custom-call(f32[1088,128]{1,0:T(8,128)S(1)} %get-tuple-element.63.gc_ref, f32[16,8,128]{2,1,0:T(8,128)S(1)} %get-tuple-element.64.state_ref, f32[16,16,128]{2,1,0:T(8,128)S(1)} %bitcast.15, f32[16,16,128]{2,1,0:T(8,128)S(1)} %get-tuple-element.54.refs_6_.lap_ref, f32[16,16,128]{2,1,0:T(8,128)S(1)} %bitcast.18), custom_call_target="tpu_custom_call" | custom-call | bytes 1024 | tf_op jit(solution)/shard_map/pallas_call | solution.py:354
  55.9 1.3 %collective-permute-done.15.refs_4_ = bf16[144,128]{1,0:T(8,128)(2,1)S(1)} collective-permute-done((bf16[144,128]{1,0:T(8,128)(2,1)S(1)}, bf16[144,128]{1,0:T(8,128)(2,1)S(1)}, u32[]{:S(2)}, u32[]{:S(2)}) %collective-permute-start.15) | collective-permute-done | bytes 36896 | tf_op jit(solution)/shard_map/ppermute | solution.py:612
  57.2 2.2 %shard_map.98 = bf16[256,1024]{1,0:T(8,128)(2,1)} custom-call(s32[1]{0:T(128)} %bitcast.5.group_ref, f32[1088,128]{1,0:T(8,128)S(1)} %get-tuple-element.59.refs_0_, f32[1088,128]{1,0:T(8,128)S(1)} %shard_map.97.refs_1_, f32[16,8,128]{2,1,0:T(8,128)S(1)} %get-tuple-element.65.refs_2_, f32[16,8,128]{2,1,0:T(8,128)S(1)} %collective-permute-done.14.arrived_ref.refs_3_, ...), custom_call_target="tpu_custom_call" | custom-call | bytes 1024 | tf_op jit(solution)/shard_map/pallas_call | solution.py:491
  (11 shorter events, 0.2 us)
Async XLA Ops:
  0.6 9.3 %slice-start = ((s8[16777216]{0:T(1024)(128)(4,1)}), s8[4194304]{0:T(1024)(128)(4,1)S(1)}, s32[]{:S(2)}) async-start(s8[16777216]{0:T(1024)(128)(4,1)} %bitcast.10), calls=%async_computation | async-start | bytes 8388608
  0.6 9.3 %slice-start.1 = ((s8[16777216]{0:T(1024)(128)(4,1)}), s8[4194304]{0:T(1024)(128)(4,1)S(1)}, s32[]{:S(2)}) async-start(s8[16777216]{0:T(1024)(128)(4,1)} %bitcast.10), calls=%async_computation.1 | async-start | bytes 8388608
  3.1 9.8 %collective-permute-start = (bf16[1040,128]{1,0:T(8,128)(2,1)S(1)}, bf16[1040,128]{1,0:T(8,128)(2,1)S(1)}, u32[]{:S(2)}, u32[]{:S(2)}) collective-permute-start(bf16[1040,128]{1,0:T(8,128)(2,1)S(1)} %get-tuple-element.34), channel_id=1, source_target_pairs={{0,1},{1,0},{2,3},{3,2},{4,5},{5,4},{6,7},{7,6},{8,9},{9,8},{10,11... | collective-permute-start | bytes 798728 | tf_op jit(solution)/shard_map/ppermute | solution.py:575
  6.1 3.9 %slice-start.2 = ((s8[16777216]{0:T(1024)(128)(4,1)}), s8[4194304]{0:T(1024)(128)(4,1)S(1)}, s32[]{:S(2)}) async-start(s8[16777216]{0:T(1024)(128)(4,1)} %bitcast.10), calls=%async_computation.2 | async-start | bytes 8388608
  6.1 3.9 %slice-start.3 = ((s8[16777216]{0:T(1024)(128)(4,1)}), s8[4194304]{0:T(1024)(128)(4,1)S(1)}, s32[]{:S(2)}) async-start(s8[16777216]{0:T(1024)(128)(4,1)} %bitcast.10), calls=%async_computation.3 | async-start | bytes 8388608
  8.3 8.3 %collective-permute-start.1 = (bf16[1040,128]{1,0:T(8,128)(2,1)S(1)}, bf16[1040,128]{1,0:T(8,128)(2,1)S(1)}, u32[]{:S(2)}, u32[]{:S(2)}) collective-permute-start(bf16[1040,128]{1,0:T(8,128)(2,1)S(1)} %shard_map.78), channel_id=1, source_target_pairs={{0,2},{1,3},{2,0},{3,1},{4,6},{5,7},{6,4},{7,5},{8,10},{9,11},{10,... | collective-permute-start | bytes 798728 | tf_op jit(solution)/shard_map/ppermute | solution.py:575
  10.6 8.8 %collective-permute-start.2 = (bf16[1040,128]{1,0:T(8,128)(2,1)S(1)}, bf16[1040,128]{1,0:T(8,128)(2,1)S(1)}, u32[]{:S(2)}, u32[]{:S(2)}) collective-permute-start(bf16[1040,128]{1,0:T(8,128)(2,1)S(1)} %shard_map.79), channel_id=1, source_target_pairs={{0,1},{1,0},{2,3},{3,2},{4,5},{5,4},{6,7},{7,6},{8,9},{9,8},{10,11... | collective-permute-start | bytes 798728 | tf_op jit(solution)/shard_map/ppermute | solution.py:575
  13.5 9.4 %collective-permute-start.3 = (bf16[1040,128]{1,0:T(8,128)(2,1)S(1)}, bf16[1040,128]{1,0:T(8,128)(2,1)S(1)}, u32[]{:S(2)}, u32[]{:S(2)}) collective-permute-start(bf16[1040,128]{1,0:T(8,128)(2,1)S(1)} %shard_map.83), channel_id=1, source_target_pairs={{0,2},{1,3},{2,0},{3,1},{4,6},{5,7},{6,4},{7,5},{8,10},{9,11},{10,... | collective-permute-start | bytes 798728 | tf_op jit(solution)/shard_map/ppermute | solution.py:575
  17.3 9.4 %collective-permute-start.4 = (bf16[1040,128]{1,0:T(8,128)(2,1)S(1)}, bf16[1040,128]{1,0:T(8,128)(2,1)S(1)}, u32[]{:S(2)}, u32[]{:S(2)}) collective-permute-start(bf16[1040,128]{1,0:T(8,128)(2,1)S(1)} %shard_map.84), channel_id=1, source_target_pairs={{0,1},{1,0},{2,3},{3,2},{4,5},{5,4},{6,7},{7,6},{8,9},{9,8},{10,11... | collective-permute-start | bytes 798728 | tf_op jit(solution)/shard_map/ppermute | solution.py:575
  17.8 14.6 %collective-permute-start.5 = (bf16[1040,128]{1,0:T(8,128)(2,1)S(1)}, bf16[1040,128]{1,0:T(8,128)(2,1)S(1)}, u32[]{:S(2)}, u32[]{:S(2)}) collective-permute-start(bf16[1040,128]{1,0:T(8,128)(2,1)S(1)} %shard_map.80), channel_id=1, source_target_pairs={{0,1},{1,0},{2,3},{3,2},{4,5},{5,4},{6,7},{7,6},{8,9},{9,8},{10,11... | collective-permute-start | bytes 798728 | tf_op jit(solution)/shard_map/ppermute | solution.py:575
  20.1 12.3 %collective-permute-start.6 = (bf16[1040,128]{1,0:T(8,128)(2,1)S(1)}, bf16[1040,128]{1,0:T(8,128)(2,1)S(1)}, u32[]{:S(2)}, u32[]{:S(2)}) collective-permute-start(bf16[1040,128]{1,0:T(8,128)(2,1)S(1)} %shard_map.85), channel_id=1, source_target_pairs={{0,2},{1,3},{2,0},{3,1},{4,6},{5,7},{6,4},{7,5},{8,10},{9,11},{10,... | collective-permute-start | bytes 798728 | tf_op jit(solution)/shard_map/ppermute | solution.py:575
  21.7 16.4 %collective-permute-start.7 = (bf16[1040,128]{1,0:T(8,128)(2,1)S(1)}, bf16[1040,128]{1,0:T(8,128)(2,1)S(1)}, u32[]{:S(2)}, u32[]{:S(2)}) collective-permute-start(bf16[1040,128]{1,0:T(8,128)(2,1)S(1)} %shard_map.82), channel_id=1, source_target_pairs={{0,1},{1,0},{2,3},{3,2},{4,5},{5,4},{6,7},{7,6},{8,9},{9,8},{10,11... | collective-permute-start | bytes 798728 | tf_op jit(solution)/shard_map/ppermute | solution.py:575
  27.6 13.8 %collective-permute-start.8 = (bf16[1040,128]{1,0:T(8,128)(2,1)S(1)}, bf16[1040,128]{1,0:T(8,128)(2,1)S(1)}, u32[]{:S(2)}, u32[]{:S(2)}) collective-permute-start(bf16[1040,128]{1,0:T(8,128)(2,1)S(1)} %shard_map.87), channel_id=1, source_target_pairs={{0,4},{1,5},{2,6},{3,7},{4,0},{5,1},{6,2},{7,3},{8,12},{9,13},{10,... | collective-permute-start | bytes 798728 | tf_op jit(solution)/shard_map/ppermute | solution.py:575
  30.2 15.6 %collective-permute-start.9 = (bf16[1040,128]{1,0:T(8,128)(2,1)S(1)}, bf16[1040,128]{1,0:T(8,128)(2,1)S(1)}, u32[]{:S(2)}, u32[]{:S(2)}) collective-permute-start(bf16[1040,128]{1,0:T(8,128)(2,1)S(1)} %shard_map.86), channel_id=1, source_target_pairs={{0,2},{1,3},{2,0},{3,1},{4,6},{5,7},{6,4},{7,5},{8,10},{9,11},{10,... | collective-permute-start | bytes 798728 | tf_op jit(solution)/shard_map/ppermute | solution.py:575
  34.0 11.3 %copy-start.2 = (f32[1024,16]{0,1:T(8,128)S(1)}, f32[1024,16]{0,1:T(8,128)}, u32[]{:S(2)}) copy-start(f32[1024,16]{0,1:T(8,128)} %param.10) | copy-start | bytes 196612
  34.0 11.3 %copy-start.3 = (f32[1024,16]{0,1:T(8,128)S(1)}, f32[1024,16]{0,1:T(8,128)}, u32[]{:S(2)}) copy-start(f32[1024,16]{0,1:T(8,128)} %param.11) | copy-start | bytes 196612
  34.0 11.9 %collective-permute-start.10 = (bf16[1040,128]{1,0:T(8,128)(2,1)S(1)}, bf16[1040,128]{1,0:T(8,128)(2,1)S(1)}, u32[]{:S(2)}, u32[]{:S(2)}) collective-permute-start(bf16[1040,128]{1,0:T(8,128)(2,1)S(1)} %shard_map.89), channel_id=1, source_target_pairs={{0,1},{1,0},{2,3},{3,2},{4,5},{5,4},{6,7},{7,6},{8,9},{9,8},{10,11... | collective-permute-start | bytes 798728 | tf_op jit(solution)/shard_map/ppermute | solution.py:575
  34.5 14.4 %collective-permute-start.11 = (bf16[1040,128]{1,0:T(8,128)(2,1)S(1)}, bf16[1040,128]{1,0:T(8,128)(2,1)S(1)}, u32[]{:S(2)}, u32[]{:S(2)}) collective-permute-start(bf16[1040,128]{1,0:T(8,128)(2,1)S(1)} %shard_map.88), channel_id=1, source_target_pairs={{0,4},{1,5},{2,6},{3,7},{4,0},{5,1},{6,2},{7,3},{8,12},{9,13},{10,... | collective-permute-start | bytes 798728 | tf_op jit(solution)/shard_map/ppermute | solution.py:575
  38.8 7.1 %copy-start = (bf16[256,1024]{1,0:T(8,128)(2,1)S(1)}, bf16[256,1024]{1,0:T(8,128)(2,1)}, u32[]{:S(2)}) copy-start(bf16[256,1024]{1,0:T(8,128)(2,1)} %refs_3_.3) | copy-start | bytes 1572868
  38.8 7.1 %copy-start.1 = (bf16[256,1024]{1,0:T(8,128)(2,1)S(1)}, bf16[256,1024]{1,0:T(8,128)(2,1)}, u32[]{:S(2)}) copy-start(bf16[256,1024]{1,0:T(8,128)(2,1)} %refs_4_.3) | copy-start | bytes 1572868
  38.9 11.6 %collective-permute-start.12 = (bf16[1040,128]{1,0:T(8,128)(2,1)S(1)}, bf16[1040,128]{1,0:T(8,128)(2,1)S(1)}, u32[]{:S(2)}, u32[]{:S(2)}) collective-permute-start(bf16[1040,128]{1,0:T(8,128)(2,1)S(1)} %shard_map.90), channel_id=1, source_target_pairs={{0,2},{1,3},{2,0},{3,1},{4,6},{5,7},{6,4},{7,5},{8,10},{9,11},{10,... | collective-permute-start | bytes 798728 | tf_op jit(solution)/shard_map/ppermute | solution.py:575
  41.4 9.0 %collective-permute-start.13 = (bf16[1040,128]{1,0:T(8,128)(2,1)S(1)}, bf16[1040,128]{1,0:T(8,128)(2,1)S(1)}, u32[]{:S(2)}, u32[]{:S(2)}) collective-permute-start(bf16[1040,128]{1,0:T(8,128)(2,1)S(1)} %shard_map.91), channel_id=1, source_target_pairs={{0,1},{1,0},{2,3},{3,2},{4,5},{5,4},{6,7},{7,6},{8,9},{9,8},{10,11... | collective-permute-start | bytes 798728 | tf_op jit(solution)/shard_map/ppermute | solution.py:575
  51.8 1.3 %collective-permute-start.14 = (f32[16,8,128]{2,1,0:T(8,128)S(1)}, f32[16,8,128]{2,1,0:T(8,128)S(1)}, u32[]{:S(2)}, u32[]{:S(2)}) collective-permute-start(f32[16,8,128]{2,1,0:T(8,128)S(1)} %get-tuple-element.61.state_ref), channel_id=1, source_target_pairs={{0,8},{8,0},{16,24},{24,16},{1,9},{9,1},{17,25},{25,17},{2,10},{10... | collective-permute-start | bytes 196616 | tf_op jit(solution)/shard_map/ppermute | solution.py:612
  53.2 4.0 %collective-permute-start.15 = (bf16[144,128]{1,0:T(8,128)(2,1)S(1)}, bf16[144,128]{1,0:T(8,128)(2,1)S(1)}, u32[]{:S(2)}, u32[]{:S(2)}) collective-permute-start(bf16[144,128]{1,0:T(8,128)(2,1)S(1)} %shard_map.96), channel_id=1, source_target_pairs={{0,16},{8,24},{16,0},{24,8},{1,17},{9,25},{17,1},{25,9},{2,18},{10... | collective-permute-start | bytes 110600 | tf_op jit(solution)/shard_map/ppermute | solution.py:612

commit v18 on v17

--- a/solution.py
+++ b/solution.py
@@ -19,16 +19,16 @@
 
 PORTIONS = (((0, 1, 2), 4, 0), ((1, 0, 2), 4, 0), ((0, 1, 2), 4, 1), ((0, 1, 2), 4, 1))
 ORDER = (
-    ((0, 0, 6), (0, 0, 2)), ("both", ((1, 0, 5), (1, 0, 1))), ((2, 0, 6), (3, 0, 6)), ((2, 0, 4), (3, 0, 4)), ("sum", 1), ((2, 0, 2), (3, 0, 2)),
-    ((1, 0, 4), (0, 1, 4)), ((1, 1, 4), (0, 0, 4)), ((2, 1, 4), (3, 1, 4)),
+    ((0, 0, 6), (0, 0, 2)), ("both", ((1, 0, 5), (1, 0, 1))), ((2, 0, 6), (3, 0, 6)), ((2, 0, 4), (3, 0, 4)),
+    ("sum", 1), ((2, 0, 2), (3, 0, 2)), ((1, 0, 4), (0, 1, 4)), ((1, 1, 4), (0, 0, 4)), ((2, 1, 4), (3, 1, 4)),
     ((1, 0, 0), (0, 1, 0)), ((0, 2, 0), (1, 2, 0)), ((2, 2, 0), (3, 2, 0)), ((1, 1, 0), (0, 0, 0)),
-    ((2, 1, 0), (3, 1, 0)), ((2, 0, 0), (3, 0, 0)), ("sum", 0), ("laps", None), ("gate", 0), ("gate", 1), ("scan", 1),
-    ("fix", None),
+    ((2, 1, 0), (3, 1, 0)), ((2, 0, 0), (3, 0, 0)), ("sum", 0), ("laps", None), ("gate", 0), ("add", 1), ("gate", 1),
+    ("scan", 1), ("fix", None),
 )
 WAITS = {
     ((1, 0, 0), (0, 1, 0)): ((1, 0, 4),),
     ("gate", 0): ((0, 2, 0), (1, 0, 0)),
-    ("gate", 1): ((2, 2, 0), (2, 1, 0)),
+    ("gate", 1): ((2, 1, 0),),
 }
 
 
@@ -203,12 +203,34 @@
     )(place, pinned(weight), pinned(grad) if turns else grad)
 
 
-def steps_back(count, body, state, unroll):
+def add_kernel(pieces, near, acc_ref, *refs):
+    near_refs, out_ref = refs[:near], refs[near]
+    toks = acc_ref.shape[1]
+    for first, rows, sources in pieces:
+        total = acc_ref[first : first + rows, :]
+        for source, place in sources:
+            total = total + decode(near_refs[source], place, 0, rows, folds_of(toks))
+        out_ref[first : first + rows, :] = total
+
+
+def add(pieces, acc, nears):
+    vmem = pl.BlockSpec(memory_space=pltpu.VMEM)
+    return pl.pallas_call(
+        functools.partial(add_kernel, pieces, len(nears)),
+        in_specs=[vmem] * (1 + len(nears)),
+        out_specs=vmem,
+        out_shape=jax.ShapeDtypeStruct(acc.shape, jnp.float32),
+        compiler_params=pltpu.CompilerParams(vmem_limit_bytes=VMEM),
+        cost_estimate=QUICK,
+    )(acc, *nears)
+
+
+def steps_back(count, body, state, unroll, base=0):
     unroll = math.gcd(count, unroll)
 
     def some(i, state):
         for j in range(unroll):
-            state = body(count - 1 - (i * unroll + j), state)
+            state = body(base + count - 1 - (i * unroll + j), state)
         return state
 
     return lax.fori_loop(0, count // unroll, some, state)
@@ -473,15 +495,23 @@
             rows_ref[at, :] = scanned_ref[at, :] + summed(list(state))
             return state
 
-        steps_back(span, step, tuple(start), 16)
-        for line in range(rows // lanes):
-            at = slice(half * rows + line * lanes, half * rows + (line + 1) * lanes)
+        state, columns = tuple(start), pl.ds(half * rows, rows)
+        for base in (span // 2, 0):
+            state = steps_back(span // 2, step, state, 16, base)
             for k in range(segments):
-                start = (line * segments + k) * (span + GAP)
-                out_ref[k * span : (k + 1) * span, at] = rows_ref[start : start + span, :].astype(jnp.bfloat16)
-        columns = pl.ds(half * rows, rows)
-        stores.append(pltpu.make_async_copy(out_ref.at[:, columns], out_hbm.at[:, columns], sems.at[half]))
-        stores[-1].start()
+                for line in range(rows // lanes):
+                    at = slice(half * rows + line * lanes, half * rows + (line + 1) * lanes)
+                    first = (line * segments + k) * (span + GAP) + base
+                    out_ref[k * span + base : k * span + base + span // 2, at] = rows_ref[
+                        first : first + span // 2, :
+                    ].astype(jnp.bfloat16)
+                lines = pl.ds(k * span + base, span // 2)
+                stores.append(
+                    pltpu.make_async_copy(
+                        out_ref.at[lines, columns], out_hbm.at[lines, columns], sems.at[len(stores)]
+                    )
+                )
+                stores[-1].start()
     for store in stores:
         store.wait()
 
@@ -496,7 +526,7 @@
         scratch_shapes=[
             pltpu.VMEM(scanned[0].shape, jnp.float32),
             pltpu.VMEM((toks, width), jnp.bfloat16),
-            pltpu.SemaphoreType.DMA((2,)),
+            pltpu.SemaphoreType.DMA((4 * segments,)),
         ],
         compiler_params=pltpu.CompilerParams(vmem_limit_bytes=VMEM),
         cost_estimate=QUICK,
@@ -531,6 +561,7 @@
 
     received, sums, scanned, states, packed = {}, {}, {}, {}, {}
     grad_query = last = None
+    added = set()
 
     def after(value):
         return value if last is None else lax.optimization_barrier((value, last, *awaited))[0]
@@ -584,8 +615,15 @@
         elif kind == "sum":
             items = tuple((0, offsets[q], width // portions[q][1], ()) for q in inside)
             last = sums[half] = send(items, False, width, after(place), out_weight, turned, [])
+        elif kind == "add":
+            arrays, places = collect([(q, len(bits) - 1, 0) for q in inside])
+            pieces = tuple(
+                (offsets[q] - half * half_rows, width // portions[q][1], (at,)) for q, at in zip(inside, places)
+            )
+            last = sums[half] = add(pieces, after(sums[half]), arrays)
+            added.add(half)
         elif kind == "gate":
-            stages = range(len(bits))
+            stages = range(len(bits) - (half in added))
             arrays, places = collect([(q, i, 0) for q in inside for i in stages])
             pieces = tuple(
                 (offsets[q] - half * half_rows, tuple(places[i * len(stages) : (i + 1) * len(stages)]))

time: 59.6 us -> 59.4 us (level)
  transfers between devices with their start and end apart: 16 -> 16, of which waited for: 9 -> 9; matrix products, arithmetic and copies ran while one was open for 0% -> 0% of each run, Pallas kernels for 24% -> 25%
where the time goes in v18:
time: 59.4 us; the launch traced here: 59.2 us
  starting transfers between devices  26.2 us (44%)
  Pallas kernels  20.4 us (34%)
  waiting for transfers between devices  11.5 us (19%)
  between operations  0.95 us (2%)
    ppermute x14, starting transfers between devices, local(): arrived = lax.ppermute(payload, 'ch', [(i, i ^ bit) for i in range(size)])  24.6 us
    pallas_call x14, Pallas kernels, send(): pl.pallas_call(functools.partial(send_kernel, items, coded, width, len(ne...  9.17 us
    ppermute x14, waiting for transfers between devices, local(): arrived = lax.ppermute(payload, 'ch', [(i, i ^ bit) for i in range(size)])  8.99 us
    pallas_call x2, Pallas kernels, early_send(): pl.pallas_call(functools.partial(early_kernel, messages, width, turns), i...  4.58 us
    pallas_call x2, Pallas kernels, gate(): pl.pallas_call(functools.partial(gate_kernel, half, rows, segments, piece...  3.03 us
    ppermute x2, waiting for transfers between devices, local(): lax.ppermute(array, 'ctx', [(i, i ^ 1 << round_) for i in range(groups)])  2.53 us
    pallas_call x1, Pallas kernels, fix(): pl.pallas_call(functools.partial(fix_kernel, segments, len(arrived)), in_...  2.17 us
    ppermute x2, starting transfers between devices, local(): lax.ppermute(array, 'ctx', [(i, i ^ 1 << round_) for i in range(groups)])  1.63 us
  transfers between devices with their start and end apart: 16, of which 9 were waited for; matrix products, arithmetic and copies ran while one was open for 0% of the time, Pallas kernels for 25%

profile of v18, /device:TPU:0, one launch (start us, length us, event | category | flops | bytes accessed | tf_op | source)
XLA Modules:
  0.0 59.2 jit_solution(9294639155100160578)
XLA Ops:
  0.6 0.0 slice-start
  0.6 0.0 slice-start.1
  0.7 2.4 %shard_map.77 = (bf16[1040,128]{1,0:T(8,128)(2,1)S(1)}, bf16[1024,256]{1,0:T(8,128)(2,1)S(1)}) custom-call(s32[1]{0:T(128)} %bitcast.place_ref, bf16[8192,1024]{1,0:T(8,128)(2,1)} %w_ref.27, bf16[256,1024]{1,0:T(8,128)(2,1)} %g_ref.1), custom_call_target="tpu_custom_call" | custom-call | bytes 1024 | tf_op jit(solution)/shard_map/pallas_call | solution.py:194
  3.1 3.0 %collective-permute-start = (bf16[1040,128]{1,0:T(8,128)(2,1)S(1)}, bf16[1040,128]{1,0:T(8,128)(2,1)S(1)}, u32[]{:S(2)}, u32[]{:S(2)}) collective-permute-start(bf16[1040,128]{1,0:T(8,128)(2,1)S(1)} %get-tuple-element.35), channel_id=1, source_target_pairs={{0,1},{1,0},{2,3},{3,2},{4,5},{5,4},{6,7},{7,6},{8,9},{9,8},{10,11... | collective-permute-start | bytes 798728 | tf_op jit(solution)/shard_map/ppermute | solution.py:606
  6.1 2.2 %shard_map.78 = bf16[1040,128]{1,0:T(8,128)(2,1)S(1)} custom-call(s32[1]{0:T(128)} %bitcast.place_ref, bf16[8192,1024]{1,0:T(8,128)(2,1)} %w_ref.27, bf16[1024,256]{1,0:T(8,128)(2,1)S(1)} %get-tuple-element.37.g_ref.turned_ref), custom_call_target="tpu_custom_call" | custom-call | bytes 1024 | tf_op jit(solution)/shard_map/pallas_call | solution.py:194
  8.3 1.6 %collective-permute-start.1 = (bf16[1040,128]{1,0:T(8,128)(2,1)S(1)}, bf16[1040,128]{1,0:T(8,128)(2,1)S(1)}, u32[]{:S(2)}, u32[]{:S(2)}) collective-permute-start(bf16[1040,128]{1,0:T(8,128)(2,1)S(1)} %shard_map.78), channel_id=1, source_target_pairs={{0,2},{1,3},{2,0},{3,1},{4,6},{5,7},{6,4},{7,5},{8,10},{9,11},{10,... | collective-permute-start | bytes 798728 | tf_op jit(solution)/shard_map/ppermute | solution.py:606
  9.9 0.0 slice-done
  9.9 0.0 slice-done.1
  9.9 0.0 slice-done.2
  9.9 0.0 slice-done.3
  10.0 0.6 %shard_map.79 = bf16[1040,128]{1,0:T(8,128)(2,1)S(1)} custom-call(s32[1]{0:T(128)} %bitcast.place_ref, bf16[8192,1024]{1,0:T(8,128)(2,1)S(1)} %bitcast.11, bf16[1024,256]{1,0:T(8,128)(2,1)S(1)} %get-tuple-element.37.g_ref.turned_ref), custom_call_target="tpu_custom_call" | custom-call | bytes 1024 | tf_op jit(solution)/shard_map/pallas_call | solution.py:131
  10.6 0.6 collective-permute-start.2
  11.1 0.6 %shard_map.80 = bf16[1040,128]{1,0:T(8,128)(2,1)S(1)} custom-call(s32[1]{0:T(128)} %bitcast.place_ref, bf16[8192,1024]{1,0:T(8,128)(2,1)S(1)} %bitcast.11, bf16[1024,256]{1,0:T(8,128)(2,1)S(1)} %get-tuple-element.37.g_ref.turned_ref), custom_call_target="tpu_custom_call" | custom-call | bytes 1024 | tf_op jit(solution)/shard_map/pallas_call | solution.py:131
  11.8 0.4 shard_map.81.acc_ref
  12.2 0.6 %shard_map.82 = bf16[1040,128]{1,0:T(8,128)(2,1)S(1)} custom-call(s32[1]{0:T(128)} %bitcast.place_ref, bf16[8192,1024]{1,0:T(8,128)(2,1)S(1)} %bitcast.11, bf16[1024,256]{1,0:T(8,128)(2,1)S(1)} %get-tuple-element.37.g_ref.turned_ref), custom_call_target="tpu_custom_call" | custom-call | bytes 1024 | tf_op jit(solution)/shard_map/pallas_call | solution.py:131
  12.8 0.0 collective-permute-done.refs_0_
  12.8 0.7 %shard_map.83 = bf16[1040,128]{1,0:T(8,128)(2,1)S(1)} custom-call(s32[1]{0:T(128)} %bitcast.place_ref, bf16[8192,1024]{1,0:T(8,128)(2,1)S(1)} %bitcast.11, bf16[1024,256]{1,0:T(8,128)(2,1)S(1)} %get-tuple-element.37.g_ref.turned_ref, bf16[1040,128]{1,0:T(8,128)(2,1)S(1)} %collective-permute-done.refs_0_), custom_call_target="tpu_custom_call" | custom-call | bytes 1024 | tf_op jit(solution)/shard_map/pallas_call | solution.py:131
  13.5 1.7 %collective-permute-start.3 = (bf16[1040,128]{1,0:T(8,128)(2,1)S(1)}, bf16[1040,128]{1,0:T(8,128)(2,1)S(1)}, u32[]{:S(2)}, u32[]{:S(2)}) collective-permute-start(bf16[1040,128]{1,0:T(8,128)(2,1)S(1)} %shard_map.83), channel_id=1, source_target_pairs={{0,2},{1,3},{2,0},{3,1},{4,6},{5,7},{6,4},{7,5},{8,10},{9,11},{10,... | collective-permute-start | bytes 798728 | tf_op jit(solution)/shard_map/ppermute | solution.py:606
  15.2 1.4 %collective-permute-done.1.refs_0_ = bf16[1040,128]{1,0:T(8,128)(2,1)S(1)} collective-permute-done((bf16[1040,128]{1,0:T(8,128)(2,1)S(1)}, bf16[1040,128]{1,0:T(8,128)(2,1)S(1)}, u32[]{:S(2)}, u32[]{:S(2)}) %collective-permute-start.1) | collective-permute-done | bytes 266272 | tf_op jit(solution)/shard_map/ppermute | solution.py:606
  16.6 0.7 %shard_map.84 = bf16[1040,128]{1,0:T(8,128)(2,1)S(1)} custom-call(s32[1]{0:T(128)} %bitcast.place_ref, bf16[8192,1024]{1,0:T(8,128)(2,1)S(1)} %bitcast.11, bf16[1024,256]{1,0:T(8,128)(2,1)S(1)} %get-tuple-element.37.g_ref.turned_ref, bf16[1040,128]{1,0:T(8,128)(2,1)S(1)} %collective-permute-done.1.refs_0_), custom_call_target="tpu_custom_call" | custom-call | bytes 1024 | tf_op jit(solution)/shard_map/pallas_call | solution.py:131
  17.3 0.5 collective-permute-start.4
  17.8 1.6 %collective-permute-start.5 = (bf16[1040,128]{1,0:T(8,128)(2,1)S(1)}, bf16[1040,128]{1,0:T(8,128)(2,1)S(1)}, u32[]{:S(2)}, u32[]{:S(2)}) collective-permute-start(bf16[1040,128]{1,0:T(8,128)(2,1)S(1)} %shard_map.80), channel_id=1, source_target_pairs={{0,1},{1,0},{2,3},{3,2},{4,5},{5,4},{6,7},{7,6},{8,9},{9,8},{10,11... | collective-permute-start | bytes 798728 | tf_op jit(solution)/shard_map/ppermute | solution.py:606
  19.4 0.0 collective-permute-done.2.refs_0_
  19.4 0.7 %shard_map.85 = bf16[1040,128]{1,0:T(8,128)(2,1)S(1)} custom-call(s32[1]{0:T(128)} %bitcast.place_ref, bf16[8192,1024]{1,0:T(8,128)(2,1)S(1)} %bitcast.11, bf16[1024,256]{1,0:T(8,128)(2,1)S(1)} %get-tuple-element.37.g_ref.turned_ref, bf16[1040,128]{1,0:T(8,128)(2,1)S(1)} %collective-permute-done.2.refs_0_), custom_call_target="tpu_custom_call" | custom-call | bytes 1024 | tf_op jit(solution)/shard_map/pallas_call | solution.py:131
  20.1 1.6 %collective-permute-start.6 = (bf16[1040,128]{1,0:T(8,128)(2,1)S(1)}, bf16[1040,128]{1,0:T(8,128)(2,1)S(1)}, u32[]{:S(2)}, u32[]{:S(2)}) collective-permute-start(bf16[1040,128]{1,0:T(8,128)(2,1)S(1)} %shard_map.85), channel_id=1, source_target_pairs={{0,2},{1,3},{2,0},{3,1},{4,6},{5,7},{6,4},{7,5},{8,10},{9,11},{10,... | collective-permute-start | bytes 798728 | tf_op jit(solution)/shard_map/ppermute | solution.py:606
  21.7 1.1 %collective-permute-start.7 = (bf16[1040,128]{1,0:T(8,128)(2,1)S(1)}, bf16[1040,128]{1,0:T(8,128)(2,1)S(1)}, u32[]{:S(2)}, u32[]{:S(2)}) collective-permute-start(bf16[1040,128]{1,0:T(8,128)(2,1)S(1)} %shard_map.82), channel_id=1, source_target_pairs={{0,1},{1,0},{2,3},{3,2},{4,5},{5,4},{6,7},{7,6},{8,9},{9,8},{10,11... | collective-permute-start | bytes 798728 | tf_op jit(solution)/shard_map/ppermute | solution.py:606
  22.9 0.0 collective-permute-done.3.refs_1_
  22.9 0.7 %shard_map.86 = bf16[1040,128]{1,0:T(8,128)(2,1)S(1)} custom-call(s32[1]{0:T(128)} %bitcast.place_ref, bf16[8192,1024]{1,0:T(8,128)(2,1)S(1)} %bitcast.11, bf16[1024,256]{1,0:T(8,128)(2,1)S(1)} %get-tuple-element.37.g_ref.turned_ref, bf16[1040,128]{1,0:T(8,128)(2,1)S(1)} %collective-permute-done.refs_0_), custom_call_target="tpu_custom_call" | custom-call | bytes 1024 | tf_op jit(solution)/shard_map/pallas_call | solution.py:131
  23.6 3.1 %collective-permute-done.4.refs_0_ = bf16[1040,128]{1,0:T(8,128)(2,1)S(1)} collective-permute-done((bf16[1040,128]{1,0:T(8,128)(2,1)S(1)}, bf16[1040,128]{1,0:T(8,128)(2,1)S(1)}, u32[]{:S(2)}, u32[]{:S(2)}) %collective-permute-start.4) | collective-permute-done | bytes 266272 | tf_op jit(solution)/shard_map/ppermute | solution.py:606
  26.7 0.9 %shard_map.87 = bf16[1040,128]{1,0:T(8,128)(2,1)S(1)} custom-call(s32[1]{0:T(128)} %bitcast.place_ref, bf16[8192,1024]{1,0:T(8,128)(2,1)S(1)} %bitcast.11, bf16[1024,256]{1,0:T(8,128)(2,1)S(1)} %get-tuple-element.37.g_ref.turned_ref, bf16[1040,128]{1,0:T(8,128)(2,1)S(1)} %collective-permute-done.4.refs_0_, bf16[1040,128]{1,0:T(8,128)(2,1)S(1)} %collective-permute-done.3.refs_1_), custom_call_target="tpu_custom_call" | custom-call | bytes 1024 | tf_op jit(solution)/shard_map/pallas_call | solution.py:131
  27.6 2.6 %collective-permute-start.8 = (bf16[1040,128]{1,0:T(8,128)(2,1)S(1)}, bf16[1040,128]{1,0:T(8,128)(2,1)S(1)}, u32[]{:S(2)}, u32[]{:S(2)}) collective-permute-start(bf16[1040,128]{1,0:T(8,128)(2,1)S(1)} %shard_map.87), channel_id=1, source_target_pairs={{0,4},{1,5},{2,6},{3,7},{4,0},{5,1},{6,2},{7,3},{8,12},{9,13},{10,... | collective-permute-start | bytes 798728 | tf_op jit(solution)/shard_map/ppermute | solution.py:606
  30.2 1.6 %collective-permute-start.9 = (bf16[1040,128]{1,0:T(8,128)(2,1)S(1)}, bf16[1040,128]{1,0:T(8,128)(2,1)S(1)}, u32[]{:S(2)}, u32[]{:S(2)}) collective-permute-start(bf16[1040,128]{1,0:T(8,128)(2,1)S(1)} %shard_map.86), channel_id=1, source_target_pairs={{0,2},{1,3},{2,0},{3,1},{4,6},{5,7},{6,4},{7,5},{8,10},{9,11},{10,... | collective-permute-start | bytes 798728 | tf_op jit(solution)/shard_map/ppermute | solution.py:606
  31.8 0.6 collective-permute-done.5.refs_0_
  32.4 0.0 collective-permute-done.6.refs_1_
  32.4 0.9 %shard_map.88 = bf16[1040,128]{1,0:T(8,128)(2,1)S(1)} custom-call(s32[1]{0:T(128)} %bitcast.place_ref, bf16[8192,1024]{1,0:T(8,128)(2,1)S(1)} %bitcast.11, bf16[1024,256]{1,0:T(8,128)(2,1)S(1)} %get-tuple-element.37.g_ref.turned_ref, bf16[1040,128]{1,0:T(8,128)(2,1)S(1)} %collective-permute-done.5.refs_0_, bf16[1040,128]{1,0:T(8,128)(2,1)S(1)} %collective-permute-done.6.refs_1_), custom_call_target="tpu_custom_call" | custom-call | bytes 1024 | tf_op jit(solution)/shard_map/pallas_call | solution.py:131
  33.3 0.7 %shard_map.89 = bf16[1040,128]{1,0:T(8,128)(2,1)S(1)} custom-call(s32[1]{0:T(128)} %bitcast.place_ref, bf16[8192,1024]{1,0:T(8,128)(2,1)S(1)} %bitcast.11, bf16[1024,256]{1,0:T(8,128)(2,1)S(1)} %get-tuple-element.37.g_ref.turned_ref, bf16[1040,128]{1,0:T(8,128)(2,1)S(1)} %collective-permute-done.1.refs_0_), custom_call_target="tpu_custom_call" | custom-call | bytes 1024 | tf_op jit(solution)/shard_map/pallas_call | solution.py:131
  34.0 0.0 copy-start.2
  34.0 0.0 copy-start.3
  34.0 0.5 collective-permute-start.10
  34.5 2.6 %collective-permute-start.11 = (bf16[1040,128]{1,0:T(8,128)(2,1)S(1)}, bf16[1040,128]{1,0:T(8,128)(2,1)S(1)}, u32[]{:S(2)}, u32[]{:S(2)}) collective-permute-start(bf16[1040,128]{1,0:T(8,128)(2,1)S(1)} %shard_map.88), channel_id=1, source_target_pairs={{0,4},{1,5},{2,6},{3,7},{4,0},{5,1},{6,2},{7,3},{8,12},{9,13},{10,... | collective-permute-start | bytes 798728 | tf_op jit(solution)/shard_map/ppermute | solution.py:606
  37.1 1.0 %collective-permute-done.7.refs_0_ = bf16[1040,128]{1,0:T(8,128)(2,1)S(1)} collective-permute-done((bf16[1040,128]{1,0:T(8,128)(2,1)S(1)}, bf16[1040,128]{1,0:T(8,128)(2,1)S(1)}, u32[]{:S(2)}, u32[]{:S(2)}) %collective-permute-start.7) | collective-permute-done | bytes 266272 | tf_op jit(solution)/shard_map/ppermute | solution.py:606
  38.1 0.7 %shard_map.90 = bf16[1040,128]{1,0:T(8,128)(2,1)S(1)} custom-call(s32[1]{0:T(128)} %bitcast.place_ref, bf16[8192,1024]{1,0:T(8,128)(2,1)S(1)} %bitcast.11, bf16[1024,256]{1,0:T(8,128)(2,1)S(1)} %get-tuple-element.37.g_ref.turned_ref, bf16[1040,128]{1,0:T(8,128)(2,1)S(1)} %collective-permute-done.7.refs_0_), custom_call_target="tpu_custom_call" | custom-call | bytes 1024 | tf_op jit(solution)/shard_map/pallas_call | solution.py:131
  38.8 0.0 copy-start
  38.8 0.0 copy-start.1
  38.9 1.6 %collective-permute-start.12 = (bf16[1040,128]{1,0:T(8,128)(2,1)S(1)}, bf16[1040,128]{1,0:T(8,128)(2,1)S(1)}, u32[]{:S(2)}, u32[]{:S(2)}) collective-permute-start(bf16[1040,128]{1,0:T(8,128)(2,1)S(1)} %shard_map.90), channel_id=1, source_target_pairs={{0,2},{1,3},{2,0},{3,1},{4,6},{5,7},{6,4},{7,5},{8,10},{9,11},{10,... | collective-permute-start | bytes 798728 | tf_op jit(solution)/shard_map/ppermute | solution.py:606
  40.5 0.6 %shard_map.91 = bf16[1040,128]{1,0:T(8,128)(2,1)S(1)} custom-call(s32[1]{0:T(128)} %bitcast.place_ref, bf16[8192,1024]{1,0:T(8,128)(2,1)S(1)} %bitcast.11, bf16[1024,256]{1,0:T(8,128)(2,1)S(1)} %get-tuple-element.37.g_ref.turned_ref), custom_call_target="tpu_custom_call" | custom-call | bytes 1024 | tf_op jit(solution)/shard_map/pallas_call | solution.py:131
  41.1 0.3 collective-permute-done.8.refs_2_
  41.4 3.8 %collective-permute-start.13 = (bf16[1040,128]{1,0:T(8,128)(2,1)S(1)}, bf16[1040,128]{1,0:T(8,128)(2,1)S(1)}, u32[]{:S(2)}, u32[]{:S(2)}) collective-permute-start(bf16[1040,128]{1,0:T(8,128)(2,1)S(1)} %shard_map.91), channel_id=1, source_target_pairs={{0,1},{1,0},{2,3},{3,2},{4,5},{5,4},{6,7},{7,6},{8,9},{9,8},{10,11... | collective-permute-start | bytes 798728 | tf_op jit(solution)/shard_map/ppermute | solution.py:606
  45.3 0.4 shard_map.92.acc_ref
  45.8 0.0 collective-permute-done.9.refs_1_
  45.8 0.0 collective-permute-done.10.refs_0_
  45.9 1.8 %shard_map.94 = (bf16[256,1024]{1,0:T(8,128)(2,1)}, f32[1088,128]{1,0:T(8,128)S(1)}, f32[16,8,128]{2,1,0:T(8,128)S(1)}, f32[8,8,128]{2,1,0:T(8,128)S(1)}) custom-call(f32[512,256]{1,0:T(8,128)S(1)} %shard_map.92.acc_ref, bf16[1040,128]{1,0:T(8,128)(2,1)S(1)} %collective-permute-done.10.refs_0_, bf16[1040,128]{1,0:T(8,128)(2,1)S(1)} %collective-permute-done.9.refs_1_, ...), custom_call_target="tpu_custom_call" | custom-call | bytes 1024 | tf_op jit(solution)/shard_map/pallas_call | solution.py:326
  47.8 1.2 %collective-permute-done.11.refs_0_ = bf16[1040,128]{1,0:T(8,128)(2,1)S(1)} collective-permute-done((bf16[1040,128]{1,0:T(8,128)(2,1)S(1)}, bf16[1040,128]{1,0:T(8,128)(2,1)S(1)}, u32[]{:S(2)}, u32[]{:S(2)}) %collective-permute-start.11) | collective-permute-done | bytes 266272 | tf_op jit(solution)/shard_map/ppermute | solution.py:606
  49.0 0.2 shard_map.95.acc_ref
  49.1 1.3 %collective-permute-done.12.refs_1_ = bf16[1040,128]{1,0:T(8,128)(2,1)S(1)} collective-permute-done((bf16[1040,128]{1,0:T(8,128)(2,1)S(1)}, bf16[1040,128]{1,0:T(8,128)(2,1)S(1)}, u32[]{:S(2)}, u32[]{:S(2)}) %collective-permute-start.12) | collective-permute-done | bytes 266272 | tf_op jit(solution)/shard_map/ppermute | solution.py:606
  50.4 0.0 collective-permute-done.13.refs_0_
  50.4 1.2 %shard_map.96 = (bf16[256,1024]{1,0:T(8,128)(2,1)}, f32[1088,128]{1,0:T(8,128)S(1)}, f32[16,8,128]{2,1,0:T(8,128)S(1)}, f32[16,8,128]{2,1,0:T(8,128)S(1)}) custom-call(f32[512,256]{1,0:T(8,128)S(1)} %shard_map.95.acc_ref, bf16[1040,128]{1,0:T(8,128)(2,1)S(1)} %collective-permute-done.13.refs_0_, ...), custom_call_target="tpu_custom_call", output_to_operand_aliasing={{0}: (8, {})} | custom-call | bytes 1024 | tf_op jit(solution)/shard_map/pallas_call | solution.py:326
  51.6 0.1 collective-permute-start.14
  51.7 1.2 %collective-permute-done.14.arrived_ref.refs_3_ = f32[16,8,128]{2,1,0:T(8,128)S(1)} collective-permute-done((f32[16,8,128]{2,1,0:T(8,128)S(1)}, f32[16,8,128]{2,1,0:T(8,128)S(1)}, u32[]{:S(2)}, u32[]{:S(2)}) %collective-permute-start.14) | collective-permute-done | bytes 65568 | tf_op jit(solution)/shard_map/ppermute | solution.py:650
  53.0 0.1 shard_map.97
  53.0 1.6 %collective-permute-start.15 = (bf16[144,128]{1,0:T(8,128)(2,1)S(1)}, bf16[144,128]{1,0:T(8,128)(2,1)S(1)}, u32[]{:S(2)}, u32[]{:S(2)}) collective-permute-start(bf16[144,128]{1,0:T(8,128)(2,1)S(1)} %shard_map.97), channel_id=1, source_target_pairs={{0,16},{8,24},{16,0},{24,8},{1,17},{9,25},{17,1},{25,9},{2,18},{10... | collective-permute-start | bytes 110600 | tf_op jit(solution)/shard_map/ppermute | solution.py:650
  54.6 1.2 %shard_map.98.refs_1_ = f32[1088,128]{1,0:T(8,128)S(1)} custom-call(f32[1088,128]{1,0:T(8,128)S(1)} %get-tuple-element.65.gc_ref, f32[16,8,128]{2,1,0:T(8,128)S(1)} %get-tuple-element.66.state_ref, f32[16,16,128]{2,1,0:T(8,128)S(1)} %bitcast.15, f32[16,16,128]{2,1,0:T(8,128)S(1)} %get-tuple-element.55.refs_6_.refs_5_.lap_ref, f32[16,16,128]{2,1,0:T(8,128)S(1)} %bitcast.18), custom_call_target="tpu_custom_call" | custom-call | bytes 1024 | tf_op jit(solution)/shard_map/pallas_call | solution.py:376
  55.7 1.3 %collective-permute-done.15.refs_4_ = bf16[144,128]{1,0:T(8,128)(2,1)S(1)} collective-permute-done((bf16[144,128]{1,0:T(8,128)(2,1)S(1)}, bf16[144,128]{1,0:T(8,128)(2,1)S(1)}, u32[]{:S(2)}, u32[]{:S(2)}) %collective-permute-start.15) | collective-permute-done | bytes 36896 | tf_op jit(solution)/shard_map/ppermute | solution.py:650
  57.0 2.2 %shard_map.99 = bf16[256,1024]{1,0:T(8,128)(2,1)} custom-call(s32[1]{0:T(128)} %bitcast.5.group_ref, f32[1088,128]{1,0:T(8,128)S(1)} %get-tuple-element.61.refs_0_, f32[1088,128]{1,0:T(8,128)S(1)} %shard_map.98.refs_1_, f32[16,8,128]{2,1,0:T(8,128)S(1)} %get-tuple-element.67.refs_2_, f32[16,8,128]{2,1,0:T(8,128)S(1)} %collective-permute-done.14.arrived_ref.refs_3_, ...), custom_call_target="tpu_custom_call" | custom-call | bytes 1024 | tf_op jit(solution)/shard_map/pallas_call | solution.py:521
  (12 shorter events, 0.2 us)
Async XLA Ops:
  0.6 9.3 %slice-start = ((s8[16777216]{0:T(1024)(128)(4,1)}), s8[4194304]{0:T(1024)(128)(4,1)S(1)}, s32[]{:S(2)}) async-start(s8[16777216]{0:T(1024)(128)(4,1)} %bitcast.10), calls=%async_computation | async-start | bytes 8388608
  0.6 9.3 %slice-start.1 = ((s8[16777216]{0:T(1024)(128)(4,1)}), s8[4194304]{0:T(1024)(128)(4,1)S(1)}, s32[]{:S(2)}) async-start(s8[16777216]{0:T(1024)(128)(4,1)} %bitcast.10), calls=%async_computation.1 | async-start | bytes 8388608
  3.1 9.8 %collective-permute-start = (bf16[1040,128]{1,0:T(8,128)(2,1)S(1)}, bf16[1040,128]{1,0:T(8,128)(2,1)S(1)}, u32[]{:S(2)}, u32[]{:S(2)}) collective-permute-start(bf16[1040,128]{1,0:T(8,128)(2,1)S(1)} %get-tuple-element.35), channel_id=1, source_target_pairs={{0,1},{1,0},{2,3},{3,2},{4,5},{5,4},{6,7},{7,6},{8,9},{9,8},{10,11... | collective-permute-start | bytes 798728 | tf_op jit(solution)/shard_map/ppermute | solution.py:606
  6.1 3.9 %slice-start.2 = ((s8[16777216]{0:T(1024)(128)(4,1)}), s8[4194304]{0:T(1024)(128)(4,1)S(1)}, s32[]{:S(2)}) async-start(s8[16777216]{0:T(1024)(128)(4,1)} %bitcast.10), calls=%async_computation.2 | async-start | bytes 8388608
  6.1 3.9 %slice-start.3 = ((s8[16777216]{0:T(1024)(128)(4,1)}), s8[4194304]{0:T(1024)(128)(4,1)S(1)}, s32[]{:S(2)}) async-start(s8[16777216]{0:T(1024)(128)(4,1)} %bitcast.10), calls=%async_computation.3 | async-start | bytes 8388608
  8.3 8.3 %collective-permute-start.1 = (bf16[1040,128]{1,0:T(8,128)(2,1)S(1)}, bf16[1040,128]{1,0:T(8,128)(2,1)S(1)}, u32[]{:S(2)}, u32[]{:S(2)}) collective-permute-start(bf16[1040,128]{1,0:T(8,128)(2,1)S(1)} %shard_map.78), channel_id=1, source_target_pairs={{0,2},{1,3},{2,0},{3,1},{4,6},{5,7},{6,4},{7,5},{8,10},{9,11},{10,... | collective-permute-start | bytes 798728 | tf_op jit(solution)/shard_map/ppermute | solution.py:606
  10.6 8.8 %collective-permute-start.2 = (bf16[1040,128]{1,0:T(8,128)(2,1)S(1)}, bf16[1040,128]{1,0:T(8,128)(2,1)S(1)}, u32[]{:S(2)}, u32[]{:S(2)}) collective-permute-start(bf16[1040,128]{1,0:T(8,128)(2,1)S(1)} %shard_map.79), channel_id=1, source_target_pairs={{0,1},{1,0},{2,3},{3,2},{4,5},{5,4},{6,7},{7,6},{8,9},{9,8},{10,11... | collective-permute-start | bytes 798728 | tf_op jit(solution)/shard_map/ppermute | solution.py:606
  13.5 9.4 %collective-permute-start.3 = (bf16[1040,128]{1,0:T(8,128)(2,1)S(1)}, bf16[1040,128]{1,0:T(8,128)(2,1)S(1)}, u32[]{:S(2)}, u32[]{:S(2)}) collective-permute-start(bf16[1040,128]{1,0:T(8,128)(2,1)S(1)} %shard_map.83), channel_id=1, source_target_pairs={{0,2},{1,3},{2,0},{3,1},{4,6},{5,7},{6,4},{7,5},{8,10},{9,11},{10,... | collective-permute-start | bytes 798728 | tf_op jit(solution)/shard_map/ppermute | solution.py:606
  17.3 9.4 %collective-permute-start.4 = (bf16[1040,128]{1,0:T(8,128)(2,1)S(1)}, bf16[1040,128]{1,0:T(8,128)(2,1)S(1)}, u32[]{:S(2)}, u32[]{:S(2)}) collective-permute-start(bf16[1040,128]{1,0:T(8,128)(2,1)S(1)} %shard_map.84), channel_id=1, source_target_pairs={{0,1},{1,0},{2,3},{3,2},{4,5},{5,4},{6,7},{7,6},{8,9},{9,8},{10,11... | collective-permute-start | bytes 798728 | tf_op jit(solution)/shard_map/ppermute | solution.py:606
  17.8 14.6 %collective-permute-start.5 = (bf16[1040,128]{1,0:T(8,128)(2,1)S(1)}, bf16[1040,128]{1,0:T(8,128)(2,1)S(1)}, u32[]{:S(2)}, u32[]{:S(2)}) collective-permute-start(bf16[1040,128]{1,0:T(8,128)(2,1)S(1)} %shard_map.80), channel_id=1, source_target_pairs={{0,1},{1,0},{2,3},{3,2},{4,5},{5,4},{6,7},{7,6},{8,9},{9,8},{10,11... | collective-permute-start | bytes 798728 | tf_op jit(solution)/shard_map/ppermute | solution.py:606
  20.1 12.3 %collective-permute-start.6 = (bf16[1040,128]{1,0:T(8,128)(2,1)S(1)}, bf16[1040,128]{1,0:T(8,128)(2,1)S(1)}, u32[]{:S(2)}, u32[]{:S(2)}) collective-permute-start(bf16[1040,128]{1,0:T(8,128)(2,1)S(1)} %shard_map.85), channel_id=1, source_target_pairs={{0,2},{1,3},{2,0},{3,1},{4,6},{5,7},{6,4},{7,5},{8,10},{9,11},{10,... | collective-permute-start | bytes 798728 | tf_op jit(solution)/shard_map/ppermute | solution.py:606
  21.7 16.4 %collective-permute-start.7 = (bf16[1040,128]{1,0:T(8,128)(2,1)S(1)}, bf16[1040,128]{1,0:T(8,128)(2,1)S(1)}, u32[]{:S(2)}, u32[]{:S(2)}) collective-permute-start(bf16[1040,128]{1,0:T(8,128)(2,1)S(1)} %shard_map.82), channel_id=1, source_target_pairs={{0,1},{1,0},{2,3},{3,2},{4,5},{5,4},{6,7},{7,6},{8,9},{9,8},{10,11... | collective-permute-start | bytes 798728 | tf_op jit(solution)/shard_map/ppermute | solution.py:606
  27.6 13.8 %collective-permute-start.8 = (bf16[1040,128]{1,0:T(8,128)(2,1)S(1)}, bf16[1040,128]{1,0:T(8,128)(2,1)S(1)}, u32[]{:S(2)}, u32[]{:S(2)}) collective-permute-start(bf16[1040,128]{1,0:T(8,128)(2,1)S(1)} %shard_map.87), channel_id=1, source_target_pairs={{0,4},{1,5},{2,6},{3,7},{4,0},{5,1},{6,2},{7,3},{8,12},{9,13},{10,... | collective-permute-start | bytes 798728 | tf_op jit(solution)/shard_map/ppermute | solution.py:606
  30.2 15.6 %collective-permute-start.9 = (bf16[1040,128]{1,0:T(8,128)(2,1)S(1)}, bf16[1040,128]{1,0:T(8,128)(2,1)S(1)}, u32[]{:S(2)}, u32[]{:S(2)}) collective-permute-start(bf16[1040,128]{1,0:T(8,128)(2,1)S(1)} %shard_map.86), channel_id=1, source_target_pairs={{0,2},{1,3},{2,0},{3,1},{4,6},{5,7},{6,4},{7,5},{8,10},{9,11},{10,... | collective-permute-start | bytes 798728 | tf_op jit(solution)/shard_map/ppermute | solution.py:606
  34.0 11.3 %copy-start.2 = (f32[1024,16]{0,1:T(8,128)S(1)}, f32[1024,16]{0,1:T(8,128)}, u32[]{:S(2)}) copy-start(f32[1024,16]{0,1:T(8,128)} %param.10) | copy-start | bytes 196612
  34.0 11.3 %copy-start.3 = (f32[1024,16]{0,1:T(8,128)S(1)}, f32[1024,16]{0,1:T(8,128)}, u32[]{:S(2)}) copy-start(f32[1024,16]{0,1:T(8,128)} %param.11) | copy-start | bytes 196612
  34.0 11.9 %collective-permute-start.10 = (bf16[1040,128]{1,0:T(8,128)(2,1)S(1)}, bf16[1040,128]{1,0:T(8,128)(2,1)S(1)}, u32[]{:S(2)}, u32[]{:S(2)}) collective-permute-start(bf16[1040,128]{1,0:T(8,128)(2,1)S(1)} %shard_map.89), channel_id=1, source_target_pairs={{0,1},{1,0},{2,3},{3,2},{4,5},{5,4},{6,7},{7,6},{8,9},{9,8},{10,11... | collective-permute-start | bytes 798728 | tf_op jit(solution)/shard_map/ppermute | solution.py:606
  34.5 14.4 %collective-permute-start.11 = (bf16[1040,128]{1,0:T(8,128)(2,1)S(1)}, bf16[1040,128]{1,0:T(8,128)(2,1)S(1)}, u32[]{:S(2)}, u32[]{:S(2)}) collective-permute-start(bf16[1040,128]{1,0:T(8,128)(2,1)S(1)} %shard_map.88), channel_id=1, source_target_pairs={{0,4},{1,5},{2,6},{3,7},{4,0},{5,1},{6,2},{7,3},{8,12},{9,13},{10,... | collective-permute-start | bytes 798728 | tf_op jit(solution)/shard_map/ppermute | solution.py:606
  38.8 7.1 %copy-start = (bf16[256,1024]{1,0:T(8,128)(2,1)S(1)}, bf16[256,1024]{1,0:T(8,128)(2,1)}, u32[]{:S(2)}) copy-start(bf16[256,1024]{1,0:T(8,128)(2,1)} %refs_2_.1) | copy-start | bytes 1572868
  38.8 7.1 %copy-start.1 = (bf16[256,1024]{1,0:T(8,128)(2,1)S(1)}, bf16[256,1024]{1,0:T(8,128)(2,1)}, u32[]{:S(2)}) copy-start(bf16[256,1024]{1,0:T(8,128)(2,1)} %refs_3_.3) | copy-start | bytes 1572868
  38.9 11.6 %collective-permute-start.12 = (bf16[1040,128]{1,0:T(8,128)(2,1)S(1)}, bf16[1040,128]{1,0:T(8,128)(2,1)S(1)}, u32[]{:S(2)}, u32[]{:S(2)}) collective-permute-start(bf16[1040,128]{1,0:T(8,128)(2,1)S(1)} %shard_map.90), channel_id=1, source_target_pairs={{0,2},{1,3},{2,0},{3,1},{4,6},{5,7},{6,4},{7,5},{8,10},{9,11},{10,... | collective-permute-start | bytes 798728 | tf_op jit(solution)/shard_map/ppermute | solution.py:606
  41.4 9.0 %collective-permute-start.13 = (bf16[1040,128]{1,0:T(8,128)(2,1)S(1)}, bf16[1040,128]{1,0:T(8,128)(2,1)S(1)}, u32[]{:S(2)}, u32[]{:S(2)}) collective-permute-start(bf16[1040,128]{1,0:T(8,128)(2,1)S(1)} %shard_map.91), channel_id=1, source_target_pairs={{0,1},{1,0},{2,3},{3,2},{4,5},{5,4},{6,7},{7,6},{8,9},{9,8},{10,11... | collective-permute-start | bytes 798728 | tf_op jit(solution)/shard_map/ppermute | solution.py:606
  51.6 1.3 %collective-permute-start.14 = (f32[16,8,128]{2,1,0:T(8,128)S(1)}, f32[16,8,128]{2,1,0:T(8,128)S(1)}, u32[]{:S(2)}, u32[]{:S(2)}) collective-permute-start(f32[16,8,128]{2,1,0:T(8,128)S(1)} %get-tuple-element.63.state_ref), channel_id=1, source_target_pairs={{0,8},{8,0},{16,24},{24,16},{1,9},{9,1},{17,25},{25,17},{2,10},{10... | collective-permute-start | bytes 196616 | tf_op jit(solution)/shard_map/ppermute | solution.py:650
  53.0 4.0 %collective-permute-start.15 = (bf16[144,128]{1,0:T(8,128)(2,1)S(1)}, bf16[144,128]{1,0:T(8,128)(2,1)S(1)}, u32[]{:S(2)}, u32[]{:S(2)}) collective-permute-start(bf16[144,128]{1,0:T(8,128)(2,1)S(1)} %shard_map.97), channel_id=1, source_target_pairs={{0,16},{8,24},{16,0},{24,8},{1,17},{9,25},{17,1},{25,9},{2,18},{10... | collective-permute-start | bytes 110600 | tf_op jit(solution)/shard_map/ppermute | solution.py:650

commit v19 on v18

--- a/solution.py
+++ b/solution.py
@@ -368,7 +368,7 @@
         rows_ref[at, :] = summed([residue_ref[n, mine] * state[n] for n in range(modes)])
         return state
 
-    steps_back(span, step, tuple(start), 16)
+    steps_back(span, step, tuple(start), 8)
 
 
 def scan(half, segments, grad_conv, state, decay, lap, residues):
@@ -497,7 +497,7 @@
 
         state, columns = tuple(start), pl.ds(half * rows, rows)
         for base in (span // 2, 0):
-            state = steps_back(span // 2, step, state, 16, base)
+            state = steps_back(span // 2, step, state, 8, base)
             for k in range(segments):
                 for line in range(rows // lanes):
                     at = slice(half * rows + line * lanes, half * rows + (line + 1) * lanes)

time: 59.4 us -> 59.4 us (level)
  no operation moved by 1% of the time
where the time goes in v19:
time: 59.4 us; the launch traced here: 59.3 us
  starting transfers between devices  26.2 us (44%)
  Pallas kernels  20.5 us (35%)
  waiting for transfers between devices  11.5 us (19%)
  between operations  0.95 us (2%)
    ppermute x14, starting transfers between devices, local(): arrived = lax.ppermute(payload, 'ch', [(i, i ^ bit) for i in range(size)])  24.6 us
    pallas_call x14, Pallas kernels, send(): pl.pallas_call(functools.partial(send_kernel, items, coded, width, len(ne...  9.17 us
    ppermute x14, waiting for transfers between devices, local(): arrived = lax.ppermute(payload, 'ch', [(i, i ^ bit) for i in range(size)])  8.99 us
    pallas_call x2, Pallas kernels, early_send(): pl.pallas_call(functools.partial(early_kernel, messages, width, turns), i...  4.58 us
    pallas_call x2, Pallas kernels, gate(): pl.pallas_call(functools.partial(gate_kernel, half, rows, segments, piece...  3.03 us
    ppermute x2, waiting for transfers between devices, local(): lax.ppermute(array, 'ctx', [(i, i ^ 1 << round_) for i in range(groups)])  2.47 us
    pallas_call x1, Pallas kernels, fix(): pl.pallas_call(functools.partial(fix_kernel, segments, len(arrived)), in_...  2.22 us
    ppermute x2, starting transfers between devices, local(): lax.ppermute(array, 'ctx', [(i, i ^ 1 << round_) for i in range(groups)])  1.63 us
  transfers between devices with their start and end apart: 16, of which 9 were waited for; matrix products, arithmetic and copies ran while one was open for 0% of the time, Pallas kernels for 25%

profile of v19, /device:TPU:0, one launch (start us, length us, event | category | flops | bytes accessed | tf_op | source)
XLA Modules:
  0.0 59.3 jit_solution(12923369573123865861)
XLA Ops:
  0.6 0.0 slice-start
  0.6 0.0 slice-start.1
  0.7 2.4 %shard_map.77 = (bf16[1040,128]{1,0:T(8,128)(2,1)S(1)}, bf16[1024,256]{1,0:T(8,128)(2,1)S(1)}) custom-call(s32[1]{0:T(128)} %bitcast.place_ref, bf16[8192,1024]{1,0:T(8,128)(2,1)} %w_ref.27, bf16[256,1024]{1,0:T(8,128)(2,1)} %g_ref.1), custom_call_target="tpu_custom_call" | custom-call | bytes 1024 | tf_op jit(solution)/shard_map/pallas_call | solution.py:194
  3.1 3.0 %collective-permute-start = (bf16[1040,128]{1,0:T(8,128)(2,1)S(1)}, bf16[1040,128]{1,0:T(8,128)(2,1)S(1)}, u32[]{:S(2)}, u32[]{:S(2)}) collective-permute-start(bf16[1040,128]{1,0:T(8,128)(2,1)S(1)} %get-tuple-element.35), channel_id=1, source_target_pairs={{0,1},{1,0},{2,3},{3,2},{4,5},{5,4},{6,7},{7,6},{8,9},{9,8},{10,11... | collective-permute-start | bytes 798728 | tf_op jit(solution)/shard_map/ppermute | solution.py:606
  6.1 2.2 %shard_map.78 = bf16[1040,128]{1,0:T(8,128)(2,1)S(1)} custom-call(s32[1]{0:T(128)} %bitcast.place_ref, bf16[8192,1024]{1,0:T(8,128)(2,1)} %w_ref.27, bf16[1024,256]{1,0:T(8,128)(2,1)S(1)} %get-tuple-element.37.g_ref.turned_ref), custom_call_target="tpu_custom_call" | custom-call | bytes 1024 | tf_op jit(solution)/shard_map/pallas_call | solution.py:194
  8.3 1.6 %collective-permute-start.1 = (bf16[1040,128]{1,0:T(8,128)(2,1)S(1)}, bf16[1040,128]{1,0:T(8,128)(2,1)S(1)}, u32[]{:S(2)}, u32[]{:S(2)}) collective-permute-start(bf16[1040,128]{1,0:T(8,128)(2,1)S(1)} %shard_map.78), channel_id=1, source_target_pairs={{0,2},{1,3},{2,0},{3,1},{4,6},{5,7},{6,4},{7,5},{8,10},{9,11},{10,... | collective-permute-start | bytes 798728 | tf_op jit(solution)/shard_map/ppermute | solution.py:606
  9.9 0.0 slice-done
  9.9 0.0 slice-done.1
  9.9 0.0 slice-done.2
  9.9 0.0 slice-done.3
  10.0 0.6 %shard_map.79 = bf16[1040,128]{1,0:T(8,128)(2,1)S(1)} custom-call(s32[1]{0:T(128)} %bitcast.place_ref, bf16[8192,1024]{1,0:T(8,128)(2,1)S(1)} %bitcast.11, bf16[1024,256]{1,0:T(8,128)(2,1)S(1)} %get-tuple-element.37.g_ref.turned_ref), custom_call_target="tpu_custom_call" | custom-call | bytes 1024 | tf_op jit(solution)/shard_map/pallas_call | solution.py:131
  10.6 0.6 collective-permute-start.2
  11.1 0.6 %shard_map.80 = bf16[1040,128]{1,0:T(8,128)(2,1)S(1)} custom-call(s32[1]{0:T(128)} %bitcast.place_ref, bf16[8192,1024]{1,0:T(8,128)(2,1)S(1)} %bitcast.11, bf16[1024,256]{1,0:T(8,128)(2,1)S(1)} %get-tuple-element.37.g_ref.turned_ref), custom_call_target="tpu_custom_call" | custom-call | bytes 1024 | tf_op jit(solution)/shard_map/pallas_call | solution.py:131
  11.8 0.4 shard_map.81.acc_ref
  12.2 0.6 %shard_map.82 = bf16[1040,128]{1,0:T(8,128)(2,1)S(1)} custom-call(s32[1]{0:T(128)} %bitcast.place_ref, bf16[8192,1024]{1,0:T(8,128)(2,1)S(1)} %bitcast.11, bf16[1024,256]{1,0:T(8,128)(2,1)S(1)} %get-tuple-element.37.g_ref.turned_ref), custom_call_target="tpu_custom_call" | custom-call | bytes 1024 | tf_op jit(solution)/shard_map/pallas_call | solution.py:131
  12.8 0.0 collective-permute-done.refs_0_
  12.8 0.7 %shard_map.83 = bf16[1040,128]{1,0:T(8,128)(2,1)S(1)} custom-call(s32[1]{0:T(128)} %bitcast.place_ref, bf16[8192,1024]{1,0:T(8,128)(2,1)S(1)} %bitcast.11, bf16[1024,256]{1,0:T(8,128)(2,1)S(1)} %get-tuple-element.37.g_ref.turned_ref, bf16[1040,128]{1,0:T(8,128)(2,1)S(1)} %collective-permute-done.refs_0_), custom_call_target="tpu_custom_call" | custom-call | bytes 1024 | tf_op jit(solution)/shard_map/pallas_call | solution.py:131
  13.5 1.7 %collective-permute-start.3 = (bf16[1040,128]{1,0:T(8,128)(2,1)S(1)}, bf16[1040,128]{1,0:T(8,128)(2,1)S(1)}, u32[]{:S(2)}, u32[]{:S(2)}) collective-permute-start(bf16[1040,128]{1,0:T(8,128)(2,1)S(1)} %shard_map.83), channel_id=1, source_target_pairs={{0,2},{1,3},{2,0},{3,1},{4,6},{5,7},{6,4},{7,5},{8,10},{9,11},{10,... | collective-permute-start | bytes 798728 | tf_op jit(solution)/shard_map/ppermute | solution.py:606
  15.2 1.4 %collective-permute-done.1.refs_0_ = bf16[1040,128]{1,0:T(8,128)(2,1)S(1)} collective-permute-done((bf16[1040,128]{1,0:T(8,128)(2,1)S(1)}, bf16[1040,128]{1,0:T(8,128)(2,1)S(1)}, u32[]{:S(2)}, u32[]{:S(2)}) %collective-permute-start.1) | collective-permute-done | bytes 266272 | tf_op jit(solution)/shard_map/ppermute | solution.py:606
  16.6 0.7 %shard_map.84 = bf16[1040,128]{1,0:T(8,128)(2,1)S(1)} custom-call(s32[1]{0:T(128)} %bitcast.place_ref, bf16[8192,1024]{1,0:T(8,128)(2,1)S(1)} %bitcast.11, bf16[1024,256]{1,0:T(8,128)(2,1)S(1)} %get-tuple-element.37.g_ref.turned_ref, bf16[1040,128]{1,0:T(8,128)(2,1)S(1)} %collective-permute-done.1.refs_0_), custom_call_target="tpu_custom_call" | custom-call | bytes 1024 | tf_op jit(solution)/shard_map/pallas_call | solution.py:131
  17.3 0.5 collective-permute-start.4
  17.8 1.6 %collective-permute-start.5 = (bf16[1040,128]{1,0:T(8,128)(2,1)S(1)}, bf16[1040,128]{1,0:T(8,128)(2,1)S(1)}, u32[]{:S(2)}, u32[]{:S(2)}) collective-permute-start(bf16[1040,128]{1,0:T(8,128)(2,1)S(1)} %shard_map.80), channel_id=1, source_target_pairs={{0,1},{1,0},{2,3},{3,2},{4,5},{5,4},{6,7},{7,6},{8,9},{9,8},{10,11... | collective-permute-start | bytes 798728 | tf_op jit(solution)/shard_map/ppermute | solution.py:606
  19.4 0.0 collective-permute-done.2.refs_0_
  19.4 0.7 %shard_map.85 = bf16[1040,128]{1,0:T(8,128)(2,1)S(1)} custom-call(s32[1]{0:T(128)} %bitcast.place_ref, bf16[8192,1024]{1,0:T(8,128)(2,1)S(1)} %bitcast.11, bf16[1024,256]{1,0:T(8,128)(2,1)S(1)} %get-tuple-element.37.g_ref.turned_ref, bf16[1040,128]{1,0:T(8,128)(2,1)S(1)} %collective-permute-done.2.refs_0_), custom_call_target="tpu_custom_call" | custom-call | bytes 1024 | tf_op jit(solution)/shard_map/pallas_call | solution.py:131
  20.1 1.6 %collective-permute-start.6 = (bf16[1040,128]{1,0:T(8,128)(2,1)S(1)}, bf16[1040,128]{1,0:T(8,128)(2,1)S(1)}, u32[]{:S(2)}, u32[]{:S(2)}) collective-permute-start(bf16[1040,128]{1,0:T(8,128)(2,1)S(1)} %shard_map.85), channel_id=1, source_target_pairs={{0,2},{1,3},{2,0},{3,1},{4,6},{5,7},{6,4},{7,5},{8,10},{9,11},{10,... | collective-permute-start | bytes 798728 | tf_op jit(solution)/shard_map/ppermute | solution.py:606
  21.7 1.1 %collective-permute-start.7 = (bf16[1040,128]{1,0:T(8,128)(2,1)S(1)}, bf16[1040,128]{1,0:T(8,128)(2,1)S(1)}, u32[]{:S(2)}, u32[]{:S(2)}) collective-permute-start(bf16[1040,128]{1,0:T(8,128)(2,1)S(1)} %shard_map.82), channel_id=1, source_target_pairs={{0,1},{1,0},{2,3},{3,2},{4,5},{5,4},{6,7},{7,6},{8,9},{9,8},{10,11... | collective-permute-start | bytes 798728 | tf_op jit(solution)/shard_map/ppermute | solution.py:606
  22.9 0.0 collective-permute-done.3.refs_1_
  22.9 0.7 %shard_map.86 = bf16[1040,128]{1,0:T(8,128)(2,1)S(1)} custom-call(s32[1]{0:T(128)} %bitcast.place_ref, bf16[8192,1024]{1,0:T(8,128)(2,1)S(1)} %bitcast.11, bf16[1024,256]{1,0:T(8,128)(2,1)S(1)} %get-tuple-element.37.g_ref.turned_ref, bf16[1040,128]{1,0:T(8,128)(2,1)S(1)} %collective-permute-done.refs_0_), custom_call_target="tpu_custom_call" | custom-call | bytes 1024 | tf_op jit(solution)/shard_map/pallas_call | solution.py:131
  23.6 3.1 %collective-permute-done.4.refs_0_ = bf16[1040,128]{1,0:T(8,128)(2,1)S(1)} collective-permute-done((bf16[1040,128]{1,0:T(8,128)(2,1)S(1)}, bf16[1040,128]{1,0:T(8,128)(2,1)S(1)}, u32[]{:S(2)}, u32[]{:S(2)}) %collective-permute-start.4) | collective-permute-done | bytes 266272 | tf_op jit(solution)/shard_map/ppermute | solution.py:606
  26.7 0.9 %shard_map.87 = bf16[1040,128]{1,0:T(8,128)(2,1)S(1)} custom-call(s32[1]{0:T(128)} %bitcast.place_ref, bf16[8192,1024]{1,0:T(8,128)(2,1)S(1)} %bitcast.11, bf16[1024,256]{1,0:T(8,128)(2,1)S(1)} %get-tuple-element.37.g_ref.turned_ref, bf16[1040,128]{1,0:T(8,128)(2,1)S(1)} %collective-permute-done.4.refs_0_, bf16[1040,128]{1,0:T(8,128)(2,1)S(1)} %collective-permute-done.3.refs_1_), custom_call_target="tpu_custom_call" | custom-call | bytes 1024 | tf_op jit(solution)/shard_map/pallas_call | solution.py:131
  27.6 2.6 %collective-permute-start.8 = (bf16[1040,128]{1,0:T(8,128)(2,1)S(1)}, bf16[1040,128]{1,0:T(8,128)(2,1)S(1)}, u32[]{:S(2)}, u32[]{:S(2)}) collective-permute-start(bf16[1040,128]{1,0:T(8,128)(2,1)S(1)} %shard_map.87), channel_id=1, source_target_pairs={{0,4},{1,5},{2,6},{3,7},{4,0},{5,1},{6,2},{7,3},{8,12},{9,13},{10,... | collective-permute-start | bytes 798728 | tf_op jit(solution)/shard_map/ppermute | solution.py:606
  30.2 1.6 %collective-permute-start.9 = (bf16[1040,128]{1,0:T(8,128)(2,1)S(1)}, bf16[1040,128]{1,0:T(8,128)(2,1)S(1)}, u32[]{:S(2)}, u32[]{:S(2)}) collective-permute-start(bf16[1040,128]{1,0:T(8,128)(2,1)S(1)} %shard_map.86), channel_id=1, source_target_pairs={{0,2},{1,3},{2,0},{3,1},{4,6},{5,7},{6,4},{7,5},{8,10},{9,11},{10,... | collective-permute-start | bytes 798728 | tf_op jit(solution)/shard_map/ppermute | solution.py:606
  31.8 0.6 collective-permute-done.5.refs_0_
  32.4 0.0 collective-permute-done.6.refs_1_
  32.4 0.9 %shard_map.88 = bf16[1040,128]{1,0:T(8,128)(2,1)S(1)} custom-call(s32[1]{0:T(128)} %bitcast.place_ref, bf16[8192,1024]{1,0:T(8,128)(2,1)S(1)} %bitcast.11, bf16[1024,256]{1,0:T(8,128)(2,1)S(1)} %get-tuple-element.37.g_ref.turned_ref, bf16[1040,128]{1,0:T(8,128)(2,1)S(1)} %collective-permute-done.5.refs_0_, bf16[1040,128]{1,0:T(8,128)(2,1)S(1)} %collective-permute-done.6.refs_1_), custom_call_target="tpu_custom_call" | custom-call | bytes 1024 | tf_op jit(solution)/shard_map/pallas_call | solution.py:131
  33.3 0.7 %shard_map.89 = bf16[1040,128]{1,0:T(8,128)(2,1)S(1)} custom-call(s32[1]{0:T(128)} %bitcast.place_ref, bf16[8192,1024]{1,0:T(8,128)(2,1)S(1)} %bitcast.11, bf16[1024,256]{1,0:T(8,128)(2,1)S(1)} %get-tuple-element.37.g_ref.turned_ref, bf16[1040,128]{1,0:T(8,128)(2,1)S(1)} %collective-permute-done.1.refs_0_), custom_call_target="tpu_custom_call" | custom-call | bytes 1024 | tf_op jit(solution)/shard_map/pallas_call | solution.py:131
  34.0 0.0 copy-start.2
  34.0 0.0 copy-start.3
  34.0 0.5 collective-permute-start.10
  34.5 2.6 %collective-permute-start.11 = (bf16[1040,128]{1,0:T(8,128)(2,1)S(1)}, bf16[1040,128]{1,0:T(8,128)(2,1)S(1)}, u32[]{:S(2)}, u32[]{:S(2)}) collective-permute-start(bf16[1040,128]{1,0:T(8,128)(2,1)S(1)} %shard_map.88), channel_id=1, source_target_pairs={{0,4},{1,5},{2,6},{3,7},{4,0},{5,1},{6,2},{7,3},{8,12},{9,13},{10,... | collective-permute-start | bytes 798728 | tf_op jit(solution)/shard_map/ppermute | solution.py:606
  37.1 1.0 %collective-permute-done.7.refs_0_ = bf16[1040,128]{1,0:T(8,128)(2,1)S(1)} collective-permute-done((bf16[1040,128]{1,0:T(8,128)(2,1)S(1)}, bf16[1040,128]{1,0:T(8,128)(2,1)S(1)}, u32[]{:S(2)}, u32[]{:S(2)}) %collective-permute-start.7) | collective-permute-done | bytes 266272 | tf_op jit(solution)/shard_map/ppermute | solution.py:606
  38.1 0.7 %shard_map.90 = bf16[1040,128]{1,0:T(8,128)(2,1)S(1)} custom-call(s32[1]{0:T(128)} %bitcast.place_ref, bf16[8192,1024]{1,0:T(8,128)(2,1)S(1)} %bitcast.11, bf16[1024,256]{1,0:T(8,128)(2,1)S(1)} %get-tuple-element.37.g_ref.turned_ref, bf16[1040,128]{1,0:T(8,128)(2,1)S(1)} %collective-permute-done.7.refs_0_), custom_call_target="tpu_custom_call" | custom-call | bytes 1024 | tf_op jit(solution)/shard_map/pallas_call | solution.py:131
  38.8 0.0 copy-start
  38.8 0.0 copy-start.1
  38.9 1.6 %collective-permute-start.12 = (bf16[1040,128]{1,0:T(8,128)(2,1)S(1)}, bf16[1040,128]{1,0:T(8,128)(2,1)S(1)}, u32[]{:S(2)}, u32[]{:S(2)}) collective-permute-start(bf16[1040,128]{1,0:T(8,128)(2,1)S(1)} %shard_map.90), channel_id=1, source_target_pairs={{0,2},{1,3},{2,0},{3,1},{4,6},{5,7},{6,4},{7,5},{8,10},{9,11},{10,... | collective-permute-start | bytes 798728 | tf_op jit(solution)/shard_map/ppermute | solution.py:606
  40.5 0.6 %shard_map.91 = bf16[1040,128]{1,0:T(8,128)(2,1)S(1)} custom-call(s32[1]{0:T(128)} %bitcast.place_ref, bf16[8192,1024]{1,0:T(8,128)(2,1)S(1)} %bitcast.11, bf16[1024,256]{1,0:T(8,128)(2,1)S(1)} %get-tuple-element.37.g_ref.turned_ref), custom_call_target="tpu_custom_call" | custom-call | bytes 1024 | tf_op jit(solution)/shard_map/pallas_call | solution.py:131
  41.1 0.3 collective-permute-done.8.refs_2_
  41.4 3.8 %collective-permute-start.13 = (bf16[1040,128]{1,0:T(8,128)(2,1)S(1)}, bf16[1040,128]{1,0:T(8,128)(2,1)S(1)}, u32[]{:S(2)}, u32[]{:S(2)}) collective-permute-start(bf16[1040,128]{1,0:T(8,128)(2,1)S(1)} %shard_map.91), channel_id=1, source_target_pairs={{0,1},{1,0},{2,3},{3,2},{4,5},{5,4},{6,7},{7,6},{8,9},{9,8},{10,11... | collective-permute-start | bytes 798728 | tf_op jit(solution)/shard_map/ppermute | solution.py:606
  45.3 0.4 shard_map.92.acc_ref
  45.8 0.0 collective-permute-done.9.refs_1_
  45.8 0.0 collective-permute-done.10.refs_0_
  45.9 1.8 %shard_map.94 = (bf16[256,1024]{1,0:T(8,128)(2,1)}, f32[1088,128]{1,0:T(8,128)S(1)}, f32[16,8,128]{2,1,0:T(8,128)S(1)}, f32[8,8,128]{2,1,0:T(8,128)S(1)}) custom-call(f32[512,256]{1,0:T(8,128)S(1)} %shard_map.92.acc_ref, bf16[1040,128]{1,0:T(8,128)(2,1)S(1)} %collective-permute-done.10.refs_0_, bf16[1040,128]{1,0:T(8,128)(2,1)S(1)} %collective-permute-done.9.refs_1_, ...), custom_call_target="tpu_custom_call" | custom-call | bytes 1024 | tf_op jit(solution)/shard_map/pallas_call | solution.py:326
  47.8 1.2 %collective-permute-done.11.refs_0_ = bf16[1040,128]{1,0:T(8,128)(2,1)S(1)} collective-permute-done((bf16[1040,128]{1,0:T(8,128)(2,1)S(1)}, bf16[1040,128]{1,0:T(8,128)(2,1)S(1)}, u32[]{:S(2)}, u32[]{:S(2)}) %collective-permute-start.11) | collective-permute-done | bytes 266272 | tf_op jit(solution)/shard_map/ppermute | solution.py:606
  49.0 0.2 shard_map.95.acc_ref
  49.1 1.3 %collective-permute-done.12.refs_1_ = bf16[1040,128]{1,0:T(8,128)(2,1)S(1)} collective-permute-done((bf16[1040,128]{1,0:T(8,128)(2,1)S(1)}, bf16[1040,128]{1,0:T(8,128)(2,1)S(1)}, u32[]{:S(2)}, u32[]{:S(2)}) %collective-permute-start.12) | collective-permute-done | bytes 266272 | tf_op jit(solution)/shard_map/ppermute | solution.py:606
  50.4 0.0 collective-permute-done.13.refs_0_
  50.4 1.2 %shard_map.96 = (bf16[256,1024]{1,0:T(8,128)(2,1)}, f32[1088,128]{1,0:T(8,128)S(1)}, f32[16,8,128]{2,1,0:T(8,128)S(1)}, f32[16,8,128]{2,1,0:T(8,128)S(1)}) custom-call(f32[512,256]{1,0:T(8,128)S(1)} %shard_map.95.acc_ref, bf16[1040,128]{1,0:T(8,128)(2,1)S(1)} %collective-permute-done.13.refs_0_, ...), custom_call_target="tpu_custom_call", output_to_operand_aliasing={{0}: (8, {})} | custom-call | bytes 1024 | tf_op jit(solution)/shard_map/pallas_call | solution.py:326
  51.6 0.1 collective-permute-start.14
  51.7 1.2 %collective-permute-done.14.arrived_ref.refs_3_ = f32[16,8,128]{2,1,0:T(8,128)S(1)} collective-permute-done((f32[16,8,128]{2,1,0:T(8,128)S(1)}, f32[16,8,128]{2,1,0:T(8,128)S(1)}, u32[]{:S(2)}, u32[]{:S(2)}) %collective-permute-start.14) | collective-permute-done | bytes 65568 | tf_op jit(solution)/shard_map/ppermute | solution.py:650
  53.0 0.1 shard_map.97
  53.0 1.6 %collective-permute-start.15 = (bf16[144,128]{1,0:T(8,128)(2,1)S(1)}, bf16[144,128]{1,0:T(8,128)(2,1)S(1)}, u32[]{:S(2)}, u32[]{:S(2)}) collective-permute-start(bf16[144,128]{1,0:T(8,128)(2,1)S(1)} %shard_map.97), channel_id=1, source_target_pairs={{0,16},{8,24},{16,0},{24,8},{1,17},{9,25},{17,1},{25,9},{2,18},{10... | collective-permute-start | bytes 110600 | tf_op jit(solution)/shard_map/ppermute | solution.py:650
  54.6 1.2 %shard_map.98.refs_1_ = f32[1088,128]{1,0:T(8,128)S(1)} custom-call(f32[1088,128]{1,0:T(8,128)S(1)} %get-tuple-element.65.gc_ref, f32[16,8,128]{2,1,0:T(8,128)S(1)} %get-tuple-element.66.state_ref, f32[16,16,128]{2,1,0:T(8,128)S(1)} %bitcast.15, f32[16,16,128]{2,1,0:T(8,128)S(1)} %get-tuple-element.55.refs_6_.refs_5_.lap_ref, f32[16,16,128]{2,1,0:T(8,128)S(1)} %bitcast.18), custom_call_target="tpu_custom_call" | custom-call | bytes 1024 | tf_op jit(solution)/shard_map/pallas_call | solution.py:376
  55.8 1.2 %collective-permute-done.15.refs_4_ = bf16[144,128]{1,0:T(8,128)(2,1)S(1)} collective-permute-done((bf16[144,128]{1,0:T(8,128)(2,1)S(1)}, bf16[144,128]{1,0:T(8,128)(2,1)S(1)}, u32[]{:S(2)}, u32[]{:S(2)}) %collective-permute-start.15) | collective-permute-done | bytes 36896 | tf_op jit(solution)/shard_map/ppermute | solution.py:650
  57.0 2.2 %shard_map.99 = bf16[256,1024]{1,0:T(8,128)(2,1)} custom-call(s32[1]{0:T(128)} %bitcast.5.group_ref, f32[1088,128]{1,0:T(8,128)S(1)} %get-tuple-element.61.refs_0_, f32[1088,128]{1,0:T(8,128)S(1)} %shard_map.98.refs_1_, f32[16,8,128]{2,1,0:T(8,128)S(1)} %get-tuple-element.67.refs_2_, f32[16,8,128]{2,1,0:T(8,128)S(1)} %collective-permute-done.14.arrived_ref.refs_3_, ...), custom_call_target="tpu_custom_call" | custom-call | bytes 1024 | tf_op jit(solution)/shard_map/pallas_call | solution.py:521
  (12 shorter events, 0.2 us)
Async XLA Ops:
  0.6 9.3 %slice-start = ((s8[16777216]{0:T(1024)(128)(4,1)}), s8[4194304]{0:T(1024)(128)(4,1)S(1)}, s32[]{:S(2)}) async-start(s8[16777216]{0:T(1024)(128)(4,1)} %bitcast.10), calls=%async_computation | async-start | bytes 8388608
  0.6 9.3 %slice-start.1 = ((s8[16777216]{0:T(1024)(128)(4,1)}), s8[4194304]{0:T(1024)(128)(4,1)S(1)}, s32[]{:S(2)}) async-start(s8[16777216]{0:T(1024)(128)(4,1)} %bitcast.10), calls=%async_computation.1 | async-start | bytes 8388608
  3.1 9.8 %collective-permute-start = (bf16[1040,128]{1,0:T(8,128)(2,1)S(1)}, bf16[1040,128]{1,0:T(8,128)(2,1)S(1)}, u32[]{:S(2)}, u32[]{:S(2)}) collective-permute-start(bf16[1040,128]{1,0:T(8,128)(2,1)S(1)} %get-tuple-element.35), channel_id=1, source_target_pairs={{0,1},{1,0},{2,3},{3,2},{4,5},{5,4},{6,7},{7,6},{8,9},{9,8},{10,11... | collective-permute-start | bytes 798728 | tf_op jit(solution)/shard_map/ppermute | solution.py:606
  6.1 3.9 %slice-start.2 = ((s8[16777216]{0:T(1024)(128)(4,1)}), s8[4194304]{0:T(1024)(128)(4,1)S(1)}, s32[]{:S(2)}) async-start(s8[16777216]{0:T(1024)(128)(4,1)} %bitcast.10), calls=%async_computation.2 | async-start | bytes 8388608
  6.1 3.9 %slice-start.3 = ((s8[16777216]{0:T(1024)(128)(4,1)}), s8[4194304]{0:T(1024)(128)(4,1)S(1)}, s32[]{:S(2)}) async-start(s8[16777216]{0:T(1024)(128)(4,1)} %bitcast.10), calls=%async_computation.3 | async-start | bytes 8388608
  8.3 8.3 %collective-permute-start.1 = (bf16[1040,128]{1,0:T(8,128)(2,1)S(1)}, bf16[1040,128]{1,0:T(8,128)(2,1)S(1)}, u32[]{:S(2)}, u32[]{:S(2)}) collective-permute-start(bf16[1040,128]{1,0:T(8,128)(2,1)S(1)} %shard_map.78), channel_id=1, source_target_pairs={{0,2},{1,3},{2,0},{3,1},{4,6},{5,7},{6,4},{7,5},{8,10},{9,11},{10,... | collective-permute-start | bytes 798728 | tf_op jit(solution)/shard_map/ppermute | solution.py:606
  10.6 8.8 %collective-permute-start.2 = (bf16[1040,128]{1,0:T(8,128)(2,1)S(1)}, bf16[1040,128]{1,0:T(8,128)(2,1)S(1)}, u32[]{:S(2)}, u32[]{:S(2)}) collective-permute-start(bf16[1040,128]{1,0:T(8,128)(2,1)S(1)} %shard_map.79), channel_id=1, source_target_pairs={{0,1},{1,0},{2,3},{3,2},{4,5},{5,4},{6,7},{7,6},{8,9},{9,8},{10,11... | collective-permute-start | bytes 798728 | tf_op jit(solution)/shard_map/ppermute | solution.py:606
  13.5 9.4 %collective-permute-start.3 = (bf16[1040,128]{1,0:T(8,128)(2,1)S(1)}, bf16[1040,128]{1,0:T(8,128)(2,1)S(1)}, u32[]{:S(2)}, u32[]{:S(2)}) collective-permute-start(bf16[1040,128]{1,0:T(8,128)(2,1)S(1)} %shard_map.83), channel_id=1, source_target_pairs={{0,2},{1,3},{2,0},{3,1},{4,6},{5,7},{6,4},{7,5},{8,10},{9,11},{10,... | collective-permute-start | bytes 798728 | tf_op jit(solution)/shard_map/ppermute | solution.py:606
  17.3 9.4 %collective-permute-start.4 = (bf16[1040,128]{1,0:T(8,128)(2,1)S(1)}, bf16[1040,128]{1,0:T(8,128)(2,1)S(1)}, u32[]{:S(2)}, u32[]{:S(2)}) collective-permute-start(bf16[1040,128]{1,0:T(8,128)(2,1)S(1)} %shard_map.84), channel_id=1, source_target_pairs={{0,1},{1,0},{2,3},{3,2},{4,5},{5,4},{6,7},{7,6},{8,9},{9,8},{10,11... | collective-permute-start | bytes 798728 | tf_op jit(solution)/shard_map/ppermute | solution.py:606
  17.8 14.6 %collective-permute-start.5 = (bf16[1040,128]{1,0:T(8,128)(2,1)S(1)}, bf16[1040,128]{1,0:T(8,128)(2,1)S(1)}, u32[]{:S(2)}, u32[]{:S(2)}) collective-permute-start(bf16[1040,128]{1,0:T(8,128)(2,1)S(1)} %shard_map.80), channel_id=1, source_target_pairs={{0,1},{1,0},{2,3},{3,2},{4,5},{5,4},{6,7},{7,6},{8,9},{9,8},{10,11... | collective-permute-start | bytes 798728 | tf_op jit(solution)/shard_map/ppermute | solution.py:606
  20.1 12.3 %collective-permute-start.6 = (bf16[1040,128]{1,0:T(8,128)(2,1)S(1)}, bf16[1040,128]{1,0:T(8,128)(2,1)S(1)}, u32[]{:S(2)}, u32[]{:S(2)}) collective-permute-start(bf16[1040,128]{1,0:T(8,128)(2,1)S(1)} %shard_map.85), channel_id=1, source_target_pairs={{0,2},{1,3},{2,0},{3,1},{4,6},{5,7},{6,4},{7,5},{8,10},{9,11},{10,... | collective-permute-start | bytes 798728 | tf_op jit(solution)/shard_map/ppermute | solution.py:606
  21.7 16.4 %collective-permute-start.7 = (bf16[1040,128]{1,0:T(8,128)(2,1)S(1)}, bf16[1040,128]{1,0:T(8,128)(2,1)S(1)}, u32[]{:S(2)}, u32[]{:S(2)}) collective-permute-start(bf16[1040,128]{1,0:T(8,128)(2,1)S(1)} %shard_map.82), channel_id=1, source_target_pairs={{0,1},{1,0},{2,3},{3,2},{4,5},{5,4},{6,7},{7,6},{8,9},{9,8},{10,11... | collective-permute-start | bytes 798728 | tf_op jit(solution)/shard_map/ppermute | solution.py:606
  27.6 13.8 %collective-permute-start.8 = (bf16[1040,128]{1,0:T(8,128)(2,1)S(1)}, bf16[1040,128]{1,0:T(8,128)(2,1)S(1)}, u32[]{:S(2)}, u32[]{:S(2)}) collective-permute-start(bf16[1040,128]{1,0:T(8,128)(2,1)S(1)} %shard_map.87), channel_id=1, source_target_pairs={{0,4},{1,5},{2,6},{3,7},{4,0},{5,1},{6,2},{7,3},{8,12},{9,13},{10,... | collective-permute-start | bytes 798728 | tf_op jit(solution)/shard_map/ppermute | solution.py:606
  30.2 15.6 %collective-permute-start.9 = (bf16[1040,128]{1,0:T(8,128)(2,1)S(1)}, bf16[1040,128]{1,0:T(8,128)(2,1)S(1)}, u32[]{:S(2)}, u32[]{:S(2)}) collective-permute-start(bf16[1040,128]{1,0:T(8,128)(2,1)S(1)} %shard_map.86), channel_id=1, source_target_pairs={{0,2},{1,3},{2,0},{3,1},{4,6},{5,7},{6,4},{7,5},{8,10},{9,11},{10,... | collective-permute-start | bytes 798728 | tf_op jit(solution)/shard_map/ppermute | solution.py:606
  34.0 11.3 %copy-start.2 = (f32[1024,16]{0,1:T(8,128)S(1)}, f32[1024,16]{0,1:T(8,128)}, u32[]{:S(2)}) copy-start(f32[1024,16]{0,1:T(8,128)} %param.10) | copy-start | bytes 196612
  34.0 11.3 %copy-start.3 = (f32[1024,16]{0,1:T(8,128)S(1)}, f32[1024,16]{0,1:T(8,128)}, u32[]{:S(2)}) copy-start(f32[1024,16]{0,1:T(8,128)} %param.11) | copy-start | bytes 196612
  34.0 11.9 %collective-permute-start.10 = (bf16[1040,128]{1,0:T(8,128)(2,1)S(1)}, bf16[1040,128]{1,0:T(8,128)(2,1)S(1)}, u32[]{:S(2)}, u32[]{:S(2)}) collective-permute-start(bf16[1040,128]{1,0:T(8,128)(2,1)S(1)} %shard_map.89), channel_id=1, source_target_pairs={{0,1},{1,0},{2,3},{3,2},{4,5},{5,4},{6,7},{7,6},{8,9},{9,8},{10,11... | collective-permute-start | bytes 798728 | tf_op jit(solution)/shard_map/ppermute | solution.py:606
  34.5 14.4 %collective-permute-start.11 = (bf16[1040,128]{1,0:T(8,128)(2,1)S(1)}, bf16[1040,128]{1,0:T(8,128)(2,1)S(1)}, u32[]{:S(2)}, u32[]{:S(2)}) collective-permute-start(bf16[1040,128]{1,0:T(8,128)(2,1)S(1)} %shard_map.88), channel_id=1, source_target_pairs={{0,4},{1,5},{2,6},{3,7},{4,0},{5,1},{6,2},{7,3},{8,12},{9,13},{10,... | collective-permute-start | bytes 798728 | tf_op jit(solution)/shard_map/ppermute | solution.py:606
  38.8 7.1 %copy-start = (bf16[256,1024]{1,0:T(8,128)(2,1)S(1)}, bf16[256,1024]{1,0:T(8,128)(2,1)}, u32[]{:S(2)}) copy-start(bf16[256,1024]{1,0:T(8,128)(2,1)} %refs_2_.1) | copy-start | bytes 1572868
  38.8 7.1 %copy-start.1 = (bf16[256,1024]{1,0:T(8,128)(2,1)S(1)}, bf16[256,1024]{1,0:T(8,128)(2,1)}, u32[]{:S(2)}) copy-start(bf16[256,1024]{1,0:T(8,128)(2,1)} %refs_3_.3) | copy-start | bytes 1572868
  38.9 11.6 %collective-permute-start.12 = (bf16[1040,128]{1,0:T(8,128)(2,1)S(1)}, bf16[1040,128]{1,0:T(8,128)(2,1)S(1)}, u32[]{:S(2)}, u32[]{:S(2)}) collective-permute-start(bf16[1040,128]{1,0:T(8,128)(2,1)S(1)} %shard_map.90), channel_id=1, source_target_pairs={{0,2},{1,3},{2,0},{3,1},{4,6},{5,7},{6,4},{7,5},{8,10},{9,11},{10,... | collective-permute-start | bytes 798728 | tf_op jit(solution)/shard_map/ppermute | solution.py:606
  41.4 9.0 %collective-permute-start.13 = (bf16[1040,128]{1,0:T(8,128)(2,1)S(1)}, bf16[1040,128]{1,0:T(8,128)(2,1)S(1)}, u32[]{:S(2)}, u32[]{:S(2)}) collective-permute-start(bf16[1040,128]{1,0:T(8,128)(2,1)S(1)} %shard_map.91), channel_id=1, source_target_pairs={{0,1},{1,0},{2,3},{3,2},{4,5},{5,4},{6,7},{7,6},{8,9},{9,8},{10,11... | collective-permute-start | bytes 798728 | tf_op jit(solution)/shard_map/ppermute | solution.py:606
  51.6 1.3 %collective-permute-start.14 = (f32[16,8,128]{2,1,0:T(8,128)S(1)}, f32[16,8,128]{2,1,0:T(8,128)S(1)}, u32[]{:S(2)}, u32[]{:S(2)}) collective-permute-start(f32[16,8,128]{2,1,0:T(8,128)S(1)} %get-tuple-element.63.state_ref), channel_id=1, source_target_pairs={{0,8},{8,0},{16,24},{24,16},{1,9},{9,1},{17,25},{25,17},{2,10},{10... | collective-permute-start | bytes 196616 | tf_op jit(solution)/shard_map/ppermute | solution.py:650
  53.0 4.0 %collective-permute-start.15 = (bf16[144,128]{1,0:T(8,128)(2,1)S(1)}, bf16[144,128]{1,0:T(8,128)(2,1)S(1)}, u32[]{:S(2)}, u32[]{:S(2)}) collective-permute-start(bf16[144,128]{1,0:T(8,128)(2,1)S(1)} %shard_map.97), channel_id=1, source_target_pairs={{0,16},{8,24},{16,0},{24,8},{1,17},{9,25},{17,1},{25,9},{2,18},{10... | collective-permute-start | bytes 110600 | tf_op jit(solution)/shard_map/ppermute | solution.py:650

commit v20 on v19

--- a/solution.py
+++ b/solution.py
@@ -322,7 +322,7 @@
     vmem = pl.BlockSpec(memory_space=pltpu.VMEM)
     high = pl.BlockSpec(memory_space=pltpu.HBM)
     more = [] if partial is None else [partial]
-    lines = (sublanes * (toks // segments + GAP), lanes)
+    lines = ((sublanes + 1) * (toks // segments + GAP), lanes)
     return pl.pallas_call(
         functools.partial(gate_kernel, half, rows, segments, pieces, len(nears)),
         in_specs=[vmem] * (6 + len(nears)) + [high] * len(more),
@@ -350,7 +350,7 @@
 def scan_kernel(half, segments, gc_ref, state_ref, decay_ref, lap_ref, residue_ref, rows_ref):
     modes, sublanes, lanes = state_ref.shape
     mine = slice(half * sublanes, (half + 1) * sublanes)
-    span = gc_ref.shape[0] // sublanes - GAP
+    span = gc_ref.shape[0] // (sublanes + 1) - GAP
     segment = segment_of((sublanes, lanes), segments)
     decay = [decay_ref[n, mine] for n in range(modes)]
     start = []

time: 59.4 us -> 59.4 us (level)
  no operation moved by 1% of the time
where the time goes in v20:
time: 59.4 us; the launch traced here: 59.3 us
  starting transfers between devices  26.2 us (44%)
  Pallas kernels  20.5 us (35%)
  waiting for transfers between devices  11.5 us (19%)
  between operations  0.95 us (2%)
    ppermute x14, starting transfers between devices, local(): arrived = lax.ppermute(payload, 'ch', [(i, i ^ bit) for i in range(size)])  24.6 us
    pallas_call x14, Pallas kernels, send(): pl.pallas_call(functools.partial(send_kernel, items, coded, width, len(ne...  9.17 us
    ppermute x14, waiting for transfers between devices, local(): arrived = lax.ppermute(payload, 'ch', [(i, i ^ bit) for i in range(size)])  8.99 us
    pallas_call x2, Pallas kernels, early_send(): pl.pallas_call(functools.partial(early_kernel, messages, width, turns), i...  4.58 us
    pallas_call x2, Pallas kernels, gate(): pl.pallas_call(functools.partial(gate_kernel, half, rows, segments, piece...  3.03 us
    ppermute x2, waiting for transfers between devices, local(): lax.ppermute(array, 'ctx', [(i, i ^ 1 << round_) for i in range(groups)])  2.47 us
    pallas_call x1, Pallas kernels, fix(): pl.pallas_call(functools.partial(fix_kernel, segments, len(arrived)), in_...  2.22 us
    ppermute x2, starting transfers between devices, local(): lax.ppermute(array, 'ctx', [(i, i ^ 1 << round_) for i in range(groups)])  1.63 us
  transfers between devices with their start and end apart: 16, of which 9 were waited for; matrix products, arithmetic and copies ran while one was open for 0% of the time, Pallas kernels for 25%

profile of v20, /device:TPU:0, one launch (start us, length us, event | category | flops | bytes accessed | tf_op | source)
XLA Modules:
  0.0 59.3 jit_solution(17789732713268107012)
XLA Ops:
  0.6 0.0 slice-start
  0.6 0.0 slice-start.1
  0.7 2.4 %shard_map.77 = (bf16[1040,128]{1,0:T(8,128)(2,1)S(1)}, bf16[1024,256]{1,0:T(8,128)(2,1)S(1)}) custom-call(s32[1]{0:T(128)} %bitcast.place_ref, bf16[8192,1024]{1,0:T(8,128)(2,1)} %w_ref.27, bf16[256,1024]{1,0:T(8,128)(2,1)} %g_ref.1), custom_call_target="tpu_custom_call" | custom-call | bytes 1024 | tf_op jit(solution)/shard_map/pallas_call | solution.py:194
  3.1 3.0 %collective-permute-start = (bf16[1040,128]{1,0:T(8,128)(2,1)S(1)}, bf16[1040,128]{1,0:T(8,128)(2,1)S(1)}, u32[]{:S(2)}, u32[]{:S(2)}) collective-permute-start(bf16[1040,128]{1,0:T(8,128)(2,1)S(1)} %get-tuple-element.35), channel_id=1, source_target_pairs={{0,1},{1,0},{2,3},{3,2},{4,5},{5,4},{6,7},{7,6},{8,9},{9,8},{10,11... | collective-permute-start | bytes 798728 | tf_op jit(solution)/shard_map/ppermute | solution.py:606
  6.1 2.2 %shard_map.78 = bf16[1040,128]{1,0:T(8,128)(2,1)S(1)} custom-call(s32[1]{0:T(128)} %bitcast.place_ref, bf16[8192,1024]{1,0:T(8,128)(2,1)} %w_ref.27, bf16[1024,256]{1,0:T(8,128)(2,1)S(1)} %get-tuple-element.37.g_ref.turned_ref), custom_call_target="tpu_custom_call" | custom-call | bytes 1024 | tf_op jit(solution)/shard_map/pallas_call | solution.py:194
  8.3 1.6 %collective-permute-start.1 = (bf16[1040,128]{1,0:T(8,128)(2,1)S(1)}, bf16[1040,128]{1,0:T(8,128)(2,1)S(1)}, u32[]{:S(2)}, u32[]{:S(2)}) collective-permute-start(bf16[1040,128]{1,0:T(8,128)(2,1)S(1)} %shard_map.78), channel_id=1, source_target_pairs={{0,2},{1,3},{2,0},{3,1},{4,6},{5,7},{6,4},{7,5},{8,10},{9,11},{10,... | collective-permute-start | bytes 798728 | tf_op jit(solution)/shard_map/ppermute | solution.py:606
  9.9 0.0 slice-done
  9.9 0.0 slice-done.1
  9.9 0.0 slice-done.2
  9.9 0.0 slice-done.3
  10.0 0.6 %shard_map.79 = bf16[1040,128]{1,0:T(8,128)(2,1)S(1)} custom-call(s32[1]{0:T(128)} %bitcast.place_ref, bf16[8192,1024]{1,0:T(8,128)(2,1)S(1)} %bitcast.11, bf16[1024,256]{1,0:T(8,128)(2,1)S(1)} %get-tuple-element.37.g_ref.turned_ref), custom_call_target="tpu_custom_call" | custom-call | bytes 1024 | tf_op jit(solution)/shard_map/pallas_call | solution.py:131
  10.6 0.6 collective-permute-start.2
  11.1 0.6 %shard_map.80 = bf16[1040,128]{1,0:T(8,128)(2,1)S(1)} custom-call(s32[1]{0:T(128)} %bitcast.place_ref, bf16[8192,1024]{1,0:T(8,128)(2,1)S(1)} %bitcast.11, bf16[1024,256]{1,0:T(8,128)(2,1)S(1)} %get-tuple-element.37.g_ref.turned_ref), custom_call_target="tpu_custom_call" | custom-call | bytes 1024 | tf_op jit(solution)/shard_map/pallas_call | solution.py:131
  11.8 0.4 shard_map.81.acc_ref
  12.2 0.6 %shard_map.82 = bf16[1040,128]{1,0:T(8,128)(2,1)S(1)} custom-call(s32[1]{0:T(128)} %bitcast.place_ref, bf16[8192,1024]{1,0:T(8,128)(2,1)S(1)} %bitcast.11, bf16[1024,256]{1,0:T(8,128)(2,1)S(1)} %get-tuple-element.37.g_ref.turned_ref), custom_call_target="tpu_custom_call" | custom-call | bytes 1024 | tf_op jit(solution)/shard_map/pallas_call | solution.py:131
  12.8 0.0 collective-permute-done.refs_0_
  12.8 0.7 %shard_map.83 = bf16[1040,128]{1,0:T(8,128)(2,1)S(1)} custom-call(s32[1]{0:T(128)} %bitcast.place_ref, bf16[8192,1024]{1,0:T(8,128)(2,1)S(1)} %bitcast.11, bf16[1024,256]{1,0:T(8,128)(2,1)S(1)} %get-tuple-element.37.g_ref.turned_ref, bf16[1040,128]{1,0:T(8,128)(2,1)S(1)} %collective-permute-done.refs_0_), custom_call_target="tpu_custom_call" | custom-call | bytes 1024 | tf_op jit(solution)/shard_map/pallas_call | solution.py:131
  13.5 1.7 %collective-permute-start.3 = (bf16[1040,128]{1,0:T(8,128)(2,1)S(1)}, bf16[1040,128]{1,0:T(8,128)(2,1)S(1)}, u32[]{:S(2)}, u32[]{:S(2)}) collective-permute-start(bf16[1040,128]{1,0:T(8,128)(2,1)S(1)} %shard_map.83), channel_id=1, source_target_pairs={{0,2},{1,3},{2,0},{3,1},{4,6},{5,7},{6,4},{7,5},{8,10},{9,11},{10,... | collective-permute-start | bytes 798728 | tf_op jit(solution)/shard_map/ppermute | solution.py:606
  15.2 1.4 %collective-permute-done.1.refs_0_ = bf16[1040,128]{1,0:T(8,128)(2,1)S(1)} collective-permute-done((bf16[1040,128]{1,0:T(8,128)(2,1)S(1)}, bf16[1040,128]{1,0:T(8,128)(2,1)S(1)}, u32[]{:S(2)}, u32[]{:S(2)}) %collective-permute-start.1) | collective-permute-done | bytes 266272 | tf_op jit(solution)/shard_map/ppermute | solution.py:606
  16.6 0.7 %shard_map.84 = bf16[1040,128]{1,0:T(8,128)(2,1)S(1)} custom-call(s32[1]{0:T(128)} %bitcast.place_ref, bf16[8192,1024]{1,0:T(8,128)(2,1)S(1)} %bitcast.11, bf16[1024,256]{1,0:T(8,128)(2,1)S(1)} %get-tuple-element.37.g_ref.turned_ref, bf16[1040,128]{1,0:T(8,128)(2,1)S(1)} %collective-permute-done.1.refs_0_), custom_call_target="tpu_custom_call" | custom-call | bytes 1024 | tf_op jit(solution)/shard_map/pallas_call | solution.py:131
  17.3 0.5 collective-permute-start.4
  17.8 1.6 %collective-permute-start.5 = (bf16[1040,128]{1,0:T(8,128)(2,1)S(1)}, bf16[1040,128]{1,0:T(8,128)(2,1)S(1)}, u32[]{:S(2)}, u32[]{:S(2)}) collective-permute-start(bf16[1040,128]{1,0:T(8,128)(2,1)S(1)} %shard_map.80), channel_id=1, source_target_pairs={{0,1},{1,0},{2,3},{3,2},{4,5},{5,4},{6,7},{7,6},{8,9},{9,8},{10,11... | collective-permute-start | bytes 798728 | tf_op jit(solution)/shard_map/ppermute | solution.py:606
  19.4 0.0 collective-permute-done.2.refs_0_
  19.4 0.7 %shard_map.85 = bf16[1040,128]{1,0:T(8,128)(2,1)S(1)} custom-call(s32[1]{0:T(128)} %bitcast.place_ref, bf16[8192,1024]{1,0:T(8,128)(2,1)S(1)} %bitcast.11, bf16[1024,256]{1,0:T(8,128)(2,1)S(1)} %get-tuple-element.37.g_ref.turned_ref, bf16[1040,128]{1,0:T(8,128)(2,1)S(1)} %collective-permute-done.2.refs_0_), custom_call_target="tpu_custom_call" | custom-call | bytes 1024 | tf_op jit(solution)/shard_map/pallas_call | solution.py:131
  20.1 1.6 %collective-permute-start.6 = (bf16[1040,128]{1,0:T(8,128)(2,1)S(1)}, bf16[1040,128]{1,0:T(8,128)(2,1)S(1)}, u32[]{:S(2)}, u32[]{:S(2)}) collective-permute-start(bf16[1040,128]{1,0:T(8,128)(2,1)S(1)} %shard_map.85), channel_id=1, source_target_pairs={{0,2},{1,3},{2,0},{3,1},{4,6},{5,7},{6,4},{7,5},{8,10},{9,11},{10,... | collective-permute-start | bytes 798728 | tf_op jit(solution)/shard_map/ppermute | solution.py:606
  21.7 1.1 %collective-permute-start.7 = (bf16[1040,128]{1,0:T(8,128)(2,1)S(1)}, bf16[1040,128]{1,0:T(8,128)(2,1)S(1)}, u32[]{:S(2)}, u32[]{:S(2)}) collective-permute-start(bf16[1040,128]{1,0:T(8,128)(2,1)S(1)} %shard_map.82), channel_id=1, source_target_pairs={{0,1},{1,0},{2,3},{3,2},{4,5},{5,4},{6,7},{7,6},{8,9},{9,8},{10,11... | collective-permute-start | bytes 798728 | tf_op jit(solution)/shard_map/ppermute | solution.py:606
  22.9 0.0 collective-permute-done.3.refs_1_
  22.9 0.7 %shard_map.86 = bf16[1040,128]{1,0:T(8,128)(2,1)S(1)} custom-call(s32[1]{0:T(128)} %bitcast.place_ref, bf16[8192,1024]{1,0:T(8,128)(2,1)S(1)} %bitcast.11, bf16[1024,256]{1,0:T(8,128)(2,1)S(1)} %get-tuple-element.37.g_ref.turned_ref, bf16[1040,128]{1,0:T(8,128)(2,1)S(1)} %collective-permute-done.refs_0_), custom_call_target="tpu_custom_call" | custom-call | bytes 1024 | tf_op jit(solution)/shard_map/pallas_call | solution.py:131
  23.6 3.1 %collective-permute-done.4.refs_0_ = bf16[1040,128]{1,0:T(8,128)(2,1)S(1)} collective-permute-done((bf16[1040,128]{1,0:T(8,128)(2,1)S(1)}, bf16[1040,128]{1,0:T(8,128)(2,1)S(1)}, u32[]{:S(2)}, u32[]{:S(2)}) %collective-permute-start.4) | collective-permute-done | bytes 266272 | tf_op jit(solution)/shard_map/ppermute | solution.py:606
  26.7 0.9 %shard_map.87 = bf16[1040,128]{1,0:T(8,128)(2,1)S(1)} custom-call(s32[1]{0:T(128)} %bitcast.place_ref, bf16[8192,1024]{1,0:T(8,128)(2,1)S(1)} %bitcast.11, bf16[1024,256]{1,0:T(8,128)(2,1)S(1)} %get-tuple-element.37.g_ref.turned_ref, bf16[1040,128]{1,0:T(8,128)(2,1)S(1)} %collective-permute-done.4.refs_0_, bf16[1040,128]{1,0:T(8,128)(2,1)S(1)} %collective-permute-done.3.refs_1_), custom_call_target="tpu_custom_call" | custom-call | bytes 1024 | tf_op jit(solution)/shard_map/pallas_call | solution.py:131
  27.6 2.6 %collective-permute-start.8 = (bf16[1040,128]{1,0:T(8,128)(2,1)S(1)}, bf16[1040,128]{1,0:T(8,128)(2,1)S(1)}, u32[]{:S(2)}, u32[]{:S(2)}) collective-permute-start(bf16[1040,128]{1,0:T(8,128)(2,1)S(1)} %shard_map.87), channel_id=1, source_target_pairs={{0,4},{1,5},{2,6},{3,7},{4,0},{5,1},{6,2},{7,3},{8,12},{9,13},{10,... | collective-permute-start | bytes 798728 | tf_op jit(solution)/shard_map/ppermute | solution.py:606
  30.2 1.6 %collective-permute-start.9 = (bf16[1040,128]{1,0:T(8,128)(2,1)S(1)}, bf16[1040,128]{1,0:T(8,128)(2,1)S(1)}, u32[]{:S(2)}, u32[]{:S(2)}) collective-permute-start(bf16[1040,128]{1,0:T(8,128)(2,1)S(1)} %shard_map.86), channel_id=1, source_target_pairs={{0,2},{1,3},{2,0},{3,1},{4,6},{5,7},{6,4},{7,5},{8,10},{9,11},{10,... | collective-permute-start | bytes 798728 | tf_op jit(solution)/shard_map/ppermute | solution.py:606
  31.8 0.6 collective-permute-done.5.refs_0_
  32.4 0.0 collective-permute-done.6.refs_1_
  32.4 0.9 %shard_map.88 = bf16[1040,128]{1,0:T(8,128)(2,1)S(1)} custom-call(s32[1]{0:T(128)} %bitcast.place_ref, bf16[8192,1024]{1,0:T(8,128)(2,1)S(1)} %bitcast.11, bf16[1024,256]{1,0:T(8,128)(2,1)S(1)} %get-tuple-element.37.g_ref.turned_ref, bf16[1040,128]{1,0:T(8,128)(2,1)S(1)} %collective-permute-done.5.refs_0_, bf16[1040,128]{1,0:T(8,128)(2,1)S(1)} %collective-permute-done.6.refs_1_), custom_call_target="tpu_custom_call" | custom-call | bytes 1024 | tf_op jit(solution)/shard_map/pallas_call | solution.py:131
  33.3 0.7 %shard_map.89 = bf16[1040,128]{1,0:T(8,128)(2,1)S(1)} custom-call(s32[1]{0:T(128)} %bitcast.place_ref, bf16[8192,1024]{1,0:T(8,128)(2,1)S(1)} %bitcast.11, bf16[1024,256]{1,0:T(8,128)(2,1)S(1)} %get-tuple-element.37.g_ref.turned_ref, bf16[1040,128]{1,0:T(8,128)(2,1)S(1)} %collective-permute-done.1.refs_0_), custom_call_target="tpu_custom_call" | custom-call | bytes 1024 | tf_op jit(solution)/shard_map/pallas_call | solution.py:131
  34.0 0.0 copy-start.2
  34.0 0.0 copy-start.3
  34.0 0.5 collective-permute-start.10
  34.5 2.6 %collective-permute-start.11 = (bf16[1040,128]{1,0:T(8,128)(2,1)S(1)}, bf16[1040,128]{1,0:T(8,128)(2,1)S(1)}, u32[]{:S(2)}, u32[]{:S(2)}) collective-permute-start(bf16[1040,128]{1,0:T(8,128)(2,1)S(1)} %shard_map.88), channel_id=1, source_target_pairs={{0,4},{1,5},{2,6},{3,7},{4,0},{5,1},{6,2},{7,3},{8,12},{9,13},{10,... | collective-permute-start | bytes 798728 | tf_op jit(solution)/shard_map/ppermute | solution.py:606
  37.1 1.0 %collective-permute-done.7.refs_0_ = bf16[1040,128]{1,0:T(8,128)(2,1)S(1)} collective-permute-done((bf16[1040,128]{1,0:T(8,128)(2,1)S(1)}, bf16[1040,128]{1,0:T(8,128)(2,1)S(1)}, u32[]{:S(2)}, u32[]{:S(2)}) %collective-permute-start.7) | collective-permute-done | bytes 266272 | tf_op jit(solution)/shard_map/ppermute | solution.py:606
  38.1 0.7 %shard_map.90 = bf16[1040,128]{1,0:T(8,128)(2,1)S(1)} custom-call(s32[1]{0:T(128)} %bitcast.place_ref, bf16[8192,1024]{1,0:T(8,128)(2,1)S(1)} %bitcast.11, bf16[1024,256]{1,0:T(8,128)(2,1)S(1)} %get-tuple-element.37.g_ref.turned_ref, bf16[1040,128]{1,0:T(8,128)(2,1)S(1)} %collective-permute-done.7.refs_0_), custom_call_target="tpu_custom_call" | custom-call | bytes 1024 | tf_op jit(solution)/shard_map/pallas_call | solution.py:131
  38.8 0.0 copy-start
  38.8 0.0 copy-start.1
  38.9 1.6 %collective-permute-start.12 = (bf16[1040,128]{1,0:T(8,128)(2,1)S(1)}, bf16[1040,128]{1,0:T(8,128)(2,1)S(1)}, u32[]{:S(2)}, u32[]{:S(2)}) collective-permute-start(bf16[1040,128]{1,0:T(8,128)(2,1)S(1)} %shard_map.90), channel_id=1, source_target_pairs={{0,2},{1,3},{2,0},{3,1},{4,6},{5,7},{6,4},{7,5},{8,10},{9,11},{10,... | collective-permute-start | bytes 798728 | tf_op jit(solution)/shard_map/ppermute | solution.py:606
  40.5 0.6 %shard_map.91 = bf16[1040,128]{1,0:T(8,128)(2,1)S(1)} custom-call(s32[1]{0:T(128)} %bitcast.place_ref, bf16[8192,1024]{1,0:T(8,128)(2,1)S(1)} %bitcast.11, bf16[1024,256]{1,0:T(8,128)(2,1)S(1)} %get-tuple-element.37.g_ref.turned_ref), custom_call_target="tpu_custom_call" | custom-call | bytes 1024 | tf_op jit(solution)/shard_map/pallas_call | solution.py:131
  41.1 0.3 collective-permute-done.8.refs_2_
  41.4 3.8 %collective-permute-start.13 = (bf16[1040,128]{1,0:T(8,128)(2,1)S(1)}, bf16[1040,128]{1,0:T(8,128)(2,1)S(1)}, u32[]{:S(2)}, u32[]{:S(2)}) collective-permute-start(bf16[1040,128]{1,0:T(8,128)(2,1)S(1)} %shard_map.91), channel_id=1, source_target_pairs={{0,1},{1,0},{2,3},{3,2},{4,5},{5,4},{6,7},{7,6},{8,9},{9,8},{10,11... | collective-permute-start | bytes 798728 | tf_op jit(solution)/shard_map/ppermute | solution.py:606
  45.3 0.4 shard_map.92.acc_ref
  45.8 0.0 collective-permute-done.9.refs_1_
  45.8 0.0 collective-permute-done.10.refs_0_
  45.9 1.8 %shard_map.94 = (bf16[256,1024]{1,0:T(8,128)(2,1)}, f32[1224,128]{1,0:T(8,128)S(1)}, f32[16,8,128]{2,1,0:T(8,128)S(1)}, f32[8,8,128]{2,1,0:T(8,128)S(1)}) custom-call(f32[512,256]{1,0:T(8,128)S(1)} %shard_map.92.acc_ref, bf16[1040,128]{1,0:T(8,128)(2,1)S(1)} %collective-permute-done.10.refs_0_, bf16[1040,128]{1,0:T(8,128)(2,1)S(1)} %collective-permute-done.9.refs_1_, ...), custom_call_target="tpu_custom_call" | custom-call | bytes 1024 | tf_op jit(solution)/shard_map/pallas_call | solution.py:326
  47.8 1.2 %collective-permute-done.11.refs_0_ = bf16[1040,128]{1,0:T(8,128)(2,1)S(1)} collective-permute-done((bf16[1040,128]{1,0:T(8,128)(2,1)S(1)}, bf16[1040,128]{1,0:T(8,128)(2,1)S(1)}, u32[]{:S(2)}, u32[]{:S(2)}) %collective-permute-start.11) | collective-permute-done | bytes 266272 | tf_op jit(solution)/shard_map/ppermute | solution.py:606
  49.0 0.2 shard_map.95.acc_ref
  49.1 1.3 %collective-permute-done.12.refs_1_ = bf16[1040,128]{1,0:T(8,128)(2,1)S(1)} collective-permute-done((bf16[1040,128]{1,0:T(8,128)(2,1)S(1)}, bf16[1040,128]{1,0:T(8,128)(2,1)S(1)}, u32[]{:S(2)}, u32[]{:S(2)}) %collective-permute-start.12) | collective-permute-done | bytes 266272 | tf_op jit(solution)/shard_map/ppermute | solution.py:606
  50.4 0.0 collective-permute-done.13.refs_0_
  50.4 1.2 %shard_map.96 = (bf16[256,1024]{1,0:T(8,128)(2,1)}, f32[1224,128]{1,0:T(8,128)S(1)}, f32[16,8,128]{2,1,0:T(8,128)S(1)}, f32[16,8,128]{2,1,0:T(8,128)S(1)}) custom-call(f32[512,256]{1,0:T(8,128)S(1)} %shard_map.95.acc_ref, bf16[1040,128]{1,0:T(8,128)(2,1)S(1)} %collective-permute-done.13.refs_0_, ...), custom_call_target="tpu_custom_call", output_to_operand_aliasing={{0}: (8, {})} | custom-call | bytes 1024 | tf_op jit(solution)/shard_map/pallas_call | solution.py:326
  51.6 0.1 collective-permute-start.14
  51.7 1.2 %collective-permute-done.14.arrived_ref.refs_3_ = f32[16,8,128]{2,1,0:T(8,128)S(1)} collective-permute-done((f32[16,8,128]{2,1,0:T(8,128)S(1)}, f32[16,8,128]{2,1,0:T(8,128)S(1)}, u32[]{:S(2)}, u32[]{:S(2)}) %collective-permute-start.14) | collective-permute-done | bytes 65568 | tf_op jit(solution)/shard_map/ppermute | solution.py:650
  53.0 0.1 shard_map.97
  53.0 1.6 %collective-permute-start.15 = (bf16[144,128]{1,0:T(8,128)(2,1)S(1)}, bf16[144,128]{1,0:T(8,128)(2,1)S(1)}, u32[]{:S(2)}, u32[]{:S(2)}) collective-permute-start(bf16[144,128]{1,0:T(8,128)(2,1)S(1)} %shard_map.97), channel_id=1, source_target_pairs={{0,16},{8,24},{16,0},{24,8},{1,17},{9,25},{17,1},{25,9},{2,18},{10... | collective-permute-start | bytes 110600 | tf_op jit(solution)/shard_map/ppermute | solution.py:650
  54.6 1.2 %shard_map.98.refs_1_ = f32[1224,128]{1,0:T(8,128)S(1)} custom-call(f32[1224,128]{1,0:T(8,128)S(1)} %get-tuple-element.65.gc_ref, f32[16,8,128]{2,1,0:T(8,128)S(1)} %get-tuple-element.66.state_ref, f32[16,16,128]{2,1,0:T(8,128)S(1)} %bitcast.15, f32[16,16,128]{2,1,0:T(8,128)S(1)} %get-tuple-element.55.refs_6_.refs_5_.lap_ref, f32[16,16,128]{2,1,0:T(8,128)S(1)} %bitcast.18), custom_call_target="tpu_custom_call" | custom-call | bytes 1024 | tf_op jit(solution)/shard_map/pallas_call | solution.py:376
  55.8 1.2 %collective-permute-done.15.refs_4_ = bf16[144,128]{1,0:T(8,128)(2,1)S(1)} collective-permute-done((bf16[144,128]{1,0:T(8,128)(2,1)S(1)}, bf16[144,128]{1,0:T(8,128)(2,1)S(1)}, u32[]{:S(2)}, u32[]{:S(2)}) %collective-permute-start.15) | collective-permute-done | bytes 36896 | tf_op jit(solution)/shard_map/ppermute | solution.py:650
  57.0 2.2 %shard_map.99 = bf16[256,1024]{1,0:T(8,128)(2,1)} custom-call(s32[1]{0:T(128)} %bitcast.5.group_ref, f32[1224,128]{1,0:T(8,128)S(1)} %get-tuple-element.61.refs_0_, f32[1224,128]{1,0:T(8,128)S(1)} %shard_map.98.refs_1_, f32[16,8,128]{2,1,0:T(8,128)S(1)} %get-tuple-element.67.refs_2_, f32[16,8,128]{2,1,0:T(8,128)S(1)} %collective-permute-done.14.arrived_ref.refs_3_, ...), custom_call_target="tpu_custom_call" | custom-call | bytes 1024 | tf_op jit(solution)/shard_map/pallas_call | solution.py:521
  (12 shorter events, 0.2 us)
Async XLA Ops:
  0.6 9.3 %slice-start = ((s8[16777216]{0:T(1024)(128)(4,1)}), s8[4194304]{0:T(1024)(128)(4,1)S(1)}, s32[]{:S(2)}) async-start(s8[16777216]{0:T(1024)(128)(4,1)} %bitcast.10), calls=%async_computation | async-start | bytes 8388608
  0.6 9.3 %slice-start.1 = ((s8[16777216]{0:T(1024)(128)(4,1)}), s8[4194304]{0:T(1024)(128)(4,1)S(1)}, s32[]{:S(2)}) async-start(s8[16777216]{0:T(1024)(128)(4,1)} %bitcast.10), calls=%async_computation.1 | async-start | bytes 8388608
  3.1 9.8 %collective-permute-start = (bf16[1040,128]{1,0:T(8,128)(2,1)S(1)}, bf16[1040,128]{1,0:T(8,128)(2,1)S(1)}, u32[]{:S(2)}, u32[]{:S(2)}) collective-permute-start(bf16[1040,128]{1,0:T(8,128)(2,1)S(1)} %get-tuple-element.35), channel_id=1, source_target_pairs={{0,1},{1,0},{2,3},{3,2},{4,5},{5,4},{6,7},{7,6},{8,9},{9,8},{10,11... | collective-permute-start | bytes 798728 | tf_op jit(solution)/shard_map/ppermute | solution.py:606
  6.1 3.9 %slice-start.2 = ((s8[16777216]{0:T(1024)(128)(4,1)}), s8[4194304]{0:T(1024)(128)(4,1)S(1)}, s32[]{:S(2)}) async-start(s8[16777216]{0:T(1024)(128)(4,1)} %bitcast.10), calls=%async_computation.2 | async-start | bytes 8388608
  6.1 3.9 %slice-start.3 = ((s8[16777216]{0:T(1024)(128)(4,1)}), s8[4194304]{0:T(1024)(128)(4,1)S(1)}, s32[]{:S(2)}) async-start(s8[16777216]{0:T(1024)(128)(4,1)} %bitcast.10), calls=%async_computation.3 | async-start | bytes 8388608
  8.3 8.3 %collective-permute-start.1 = (bf16[1040,128]{1,0:T(8,128)(2,1)S(1)}, bf16[1040,128]{1,0:T(8,128)(2,1)S(1)}, u32[]{:S(2)}, u32[]{:S(2)}) collective-permute-start(bf16[1040,128]{1,0:T(8,128)(2,1)S(1)} %shard_map.78), channel_id=1, source_target_pairs={{0,2},{1,3},{2,0},{3,1},{4,6},{5,7},{6,4},{7,5},{8,10},{9,11},{10,... | collective-permute-start | bytes 798728 | tf_op jit(solution)/shard_map/ppermute | solution.py:606
  10.6 8.8 %collective-permute-start.2 = (bf16[1040,128]{1,0:T(8,128)(2,1)S(1)}, bf16[1040,128]{1,0:T(8,128)(2,1)S(1)}, u32[]{:S(2)}, u32[]{:S(2)}) collective-permute-start(bf16[1040,128]{1,0:T(8,128)(2,1)S(1)} %shard_map.79), channel_id=1, source_target_pairs={{0,1},{1,0},{2,3},{3,2},{4,5},{5,4},{6,7},{7,6},{8,9},{9,8},{10,11... | collective-permute-start | bytes 798728 | tf_op jit(solution)/shard_map/ppermute | solution.py:606
  13.5 9.4 %collective-permute-start.3 = (bf16[1040,128]{1,0:T(8,128)(2,1)S(1)}, bf16[1040,128]{1,0:T(8,128)(2,1)S(1)}, u32[]{:S(2)}, u32[]{:S(2)}) collective-permute-start(bf16[1040,128]{1,0:T(8,128)(2,1)S(1)} %shard_map.83), channel_id=1, source_target_pairs={{0,2},{1,3},{2,0},{3,1},{4,6},{5,7},{6,4},{7,5},{8,10},{9,11},{10,... | collective-permute-start | bytes 798728 | tf_op jit(solution)/shard_map/ppermute | solution.py:606
  17.3 9.4 %collective-permute-start.4 = (bf16[1040,128]{1,0:T(8,128)(2,1)S(1)}, bf16[1040,128]{1,0:T(8,128)(2,1)S(1)}, u32[]{:S(2)}, u32[]{:S(2)}) collective-permute-start(bf16[1040,128]{1,0:T(8,128)(2,1)S(1)} %shard_map.84), channel_id=1, source_target_pairs={{0,1},{1,0},{2,3},{3,2},{4,5},{5,4},{6,7},{7,6},{8,9},{9,8},{10,11... | collective-permute-start | bytes 798728 | tf_op jit(solution)/shard_map/ppermute | solution.py:606
  17.8 14.6 %collective-permute-start.5 = (bf16[1040,128]{1,0:T(8,128)(2,1)S(1)}, bf16[1040,128]{1,0:T(8,128)(2,1)S(1)}, u32[]{:S(2)}, u32[]{:S(2)}) collective-permute-start(bf16[1040,128]{1,0:T(8,128)(2,1)S(1)} %shard_map.80), channel_id=1, source_target_pairs={{0,1},{1,0},{2,3},{3,2},{4,5},{5,4},{6,7},{7,6},{8,9},{9,8},{10,11... | collective-permute-start | bytes 798728 | tf_op jit(solution)/shard_map/ppermute | solution.py:606
  20.1 12.3 %collective-permute-start.6 = (bf16[1040,128]{1,0:T(8,128)(2,1)S(1)}, bf16[1040,128]{1,0:T(8,128)(2,1)S(1)}, u32[]{:S(2)}, u32[]{:S(2)}) collective-permute-start(bf16[1040,128]{1,0:T(8,128)(2,1)S(1)} %shard_map.85), channel_id=1, source_target_pairs={{0,2},{1,3},{2,0},{3,1},{4,6},{5,7},{6,4},{7,5},{8,10},{9,11},{10,... | collective-permute-start | bytes 798728 | tf_op jit(solution)/shard_map/ppermute | solution.py:606
  21.7 16.4 %collective-permute-start.7 = (bf16[1040,128]{1,0:T(8,128)(2,1)S(1)}, bf16[1040,128]{1,0:T(8,128)(2,1)S(1)}, u32[]{:S(2)}, u32[]{:S(2)}) collective-permute-start(bf16[1040,128]{1,0:T(8,128)(2,1)S(1)} %shard_map.82), channel_id=1, source_target_pairs={{0,1},{1,0},{2,3},{3,2},{4,5},{5,4},{6,7},{7,6},{8,9},{9,8},{10,11... | collective-permute-start | bytes 798728 | tf_op jit(solution)/shard_map/ppermute | solution.py:606
  27.6 13.8 %collective-permute-start.8 = (bf16[1040,128]{1,0:T(8,128)(2,1)S(1)}, bf16[1040,128]{1,0:T(8,128)(2,1)S(1)}, u32[]{:S(2)}, u32[]{:S(2)}) collective-permute-start(bf16[1040,128]{1,0:T(8,128)(2,1)S(1)} %shard_map.87), channel_id=1, source_target_pairs={{0,4},{1,5},{2,6},{3,7},{4,0},{5,1},{6,2},{7,3},{8,12},{9,13},{10,... | collective-permute-start | bytes 798728 | tf_op jit(solution)/shard_map/ppermute | solution.py:606
  30.2 15.6 %collective-permute-start.9 = (bf16[1040,128]{1,0:T(8,128)(2,1)S(1)}, bf16[1040,128]{1,0:T(8,128)(2,1)S(1)}, u32[]{:S(2)}, u32[]{:S(2)}) collective-permute-start(bf16[1040,128]{1,0:T(8,128)(2,1)S(1)} %shard_map.86), channel_id=1, source_target_pairs={{0,2},{1,3},{2,0},{3,1},{4,6},{5,7},{6,4},{7,5},{8,10},{9,11},{10,... | collective-permute-start | bytes 798728 | tf_op jit(solution)/shard_map/ppermute | solution.py:606
  34.0 11.3 %copy-start.2 = (f32[1024,16]{0,1:T(8,128)S(1)}, f32[1024,16]{0,1:T(8,128)}, u32[]{:S(2)}) copy-start(f32[1024,16]{0,1:T(8,128)} %param.10) | copy-start | bytes 196612
  34.0 11.3 %copy-start.3 = (f32[1024,16]{0,1:T(8,128)S(1)}, f32[1024,16]{0,1:T(8,128)}, u32[]{:S(2)}) copy-start(f32[1024,16]{0,1:T(8,128)} %param.11) | copy-start | bytes 196612
  34.0 11.9 %collective-permute-start.10 = (bf16[1040,128]{1,0:T(8,128)(2,1)S(1)}, bf16[1040,128]{1,0:T(8,128)(2,1)S(1)}, u32[]{:S(2)}, u32[]{:S(2)}) collective-permute-start(bf16[1040,128]{1,0:T(8,128)(2,1)S(1)} %shard_map.89), channel_id=1, source_target_pairs={{0,1},{1,0},{2,3},{3,2},{4,5},{5,4},{6,7},{7,6},{8,9},{9,8},{10,11... | collective-permute-start | bytes 798728 | tf_op jit(solution)/shard_map/ppermute | solution.py:606
  34.5 14.4 %collective-permute-start.11 = (bf16[1040,128]{1,0:T(8,128)(2,1)S(1)}, bf16[1040,128]{1,0:T(8,128)(2,1)S(1)}, u32[]{:S(2)}, u32[]{:S(2)}) collective-permute-start(bf16[1040,128]{1,0:T(8,128)(2,1)S(1)} %shard_map.88), channel_id=1, source_target_pairs={{0,4},{1,5},{2,6},{3,7},{4,0},{5,1},{6,2},{7,3},{8,12},{9,13},{10,... | collective-permute-start | bytes 798728 | tf_op jit(solution)/shard_map/ppermute | solution.py:606
  38.8 7.1 %copy-start = (bf16[256,1024]{1,0:T(8,128)(2,1)S(1)}, bf16[256,1024]{1,0:T(8,128)(2,1)}, u32[]{:S(2)}) copy-start(bf16[256,1024]{1,0:T(8,128)(2,1)} %refs_2_.1) | copy-start | bytes 1572868
  38.8 7.1 %copy-start.1 = (bf16[256,1024]{1,0:T(8,128)(2,1)S(1)}, bf16[256,1024]{1,0:T(8,128)(2,1)}, u32[]{:S(2)}) copy-start(bf16[256,1024]{1,0:T(8,128)(2,1)} %refs_3_.3) | copy-start | bytes 1572868
  38.9 11.6 %collective-permute-start.12 = (bf16[1040,128]{1,0:T(8,128)(2,1)S(1)}, bf16[1040,128]{1,0:T(8,128)(2,1)S(1)}, u32[]{:S(2)}, u32[]{:S(2)}) collective-permute-start(bf16[1040,128]{1,0:T(8,128)(2,1)S(1)} %shard_map.90), channel_id=1, source_target_pairs={{0,2},{1,3},{2,0},{3,1},{4,6},{5,7},{6,4},{7,5},{8,10},{9,11},{10,... | collective-permute-start | bytes 798728 | tf_op jit(solution)/shard_map/ppermute | solution.py:606
  41.4 9.0 %collective-permute-start.13 = (bf16[1040,128]{1,0:T(8,128)(2,1)S(1)}, bf16[1040,128]{1,0:T(8,128)(2,1)S(1)}, u32[]{:S(2)}, u32[]{:S(2)}) collective-permute-start(bf16[1040,128]{1,0:T(8,128)(2,1)S(1)} %shard_map.91), channel_id=1, source_target_pairs={{0,1},{1,0},{2,3},{3,2},{4,5},{5,4},{6,7},{7,6},{8,9},{9,8},{10,11... | collective-permute-start | bytes 798728 | tf_op jit(solution)/shard_map/ppermute | solution.py:606
  51.6 1.3 %collective-permute-start.14 = (f32[16,8,128]{2,1,0:T(8,128)S(1)}, f32[16,8,128]{2,1,0:T(8,128)S(1)}, u32[]{:S(2)}, u32[]{:S(2)}) collective-permute-start(f32[16,8,128]{2,1,0:T(8,128)S(1)} %get-tuple-element.63.state_ref), channel_id=1, source_target_pairs={{0,8},{8,0},{16,24},{24,16},{1,9},{9,1},{17,25},{25,17},{2,10},{10... | collective-permute-start | bytes 196616 | tf_op jit(solution)/shard_map/ppermute | solution.py:650
  53.0 4.0 %collective-permute-start.15 = (bf16[144,128]{1,0:T(8,128)(2,1)S(1)}, bf16[144,128]{1,0:T(8,128)(2,1)S(1)}, u32[]{:S(2)}, u32[]{:S(2)}) collective-permute-start(bf16[144,128]{1,0:T(8,128)(2,1)S(1)} %shard_map.97), channel_id=1, source_target_pairs={{0,16},{8,24},{16,0},{24,8},{1,17},{9,25},{17,1},{25,9},{2,18},{10... | collective-permute-start | bytes 110600 | tf_op jit(solution)/shard_map/ppermute | solution.py:650

commit v21 on v20

--- a/solution.py
+++ b/solution.py
@@ -291,7 +291,7 @@
         return state
 
     zero = jnp.zeros((sublanes, lanes), jnp.float32)
-    state = steps_back(span, step, (zero,) * modes, 16)
+    state = steps_back(span, step, (zero,) * modes, 8)
     segment = segment_of((sublanes, lanes), segments)
     whole = []
     for n in range(modes):

time: 59.4 us -> 59.4 us (level)
  no operation moved by 1% of the time
where the time goes in v21:
time: 59.4 us; the launch traced here: 59.3 us
  starting transfers between devices  26.2 us (44%)
  Pallas kernels  20.6 us (35%)
  waiting for transfers between devices  11.4 us (19%)
  between operations  0.95 us (2%)
    ppermute x14, starting transfers between devices, local(): arrived = lax.ppermute(payload, 'ch', [(i, i ^ bit) for i in range(size)])  24.6 us
    pallas_call x14, Pallas kernels, send(): pl.pallas_call(functools.partial(send_kernel, items, coded, width, len(ne...  9.17 us
    ppermute x14, waiting for transfers between devices, local(): arrived = lax.ppermute(payload, 'ch', [(i, i ^ bit) for i in range(size)])  8.94 us
    pallas_call x2, Pallas kernels, early_send(): pl.pallas_call(functools.partial(early_kernel, messages, width, turns), i...  4.58 us
    pallas_call x2, Pallas kernels, gate(): pl.pallas_call(functools.partial(gate_kernel, half, rows, segments, piece...  3.08 us
    ppermute x2, waiting for transfers between devices, local(): lax.ppermute(array, 'ctx', [(i, i ^ 1 << round_) for i in range(groups)])  2.47 us
    pallas_call x1, Pallas kernels, fix(): pl.pallas_call(functools.partial(fix_kernel, segments, len(arrived)), in_...  2.22 us
    ppermute x2, starting transfers between devices, local(): lax.ppermute(array, 'ctx', [(i, i ^ 1 << round_) for i in range(groups)])  1.63 us
  transfers between devices with their start and end apart: 16, of which 9 were waited for; matrix products, arithmetic and copies ran while one was open for 0% of the time, Pallas kernels for 25%

profile of v21, /device:TPU:0, one launch (start us, length us, event | category | flops | bytes accessed | tf_op | source)
XLA Modules:
  0.0 59.3 jit_solution(1042192748705022186)
XLA Ops:
  0.6 0.0 slice-start
  0.6 0.0 slice-start.1
  0.7 2.4 %shard_map.77 = (bf16[1040,128]{1,0:T(8,128)(2,1)S(1)}, bf16[1024,256]{1,0:T(8,128)(2,1)S(1)}) custom-call(s32[1]{0:T(128)} %bitcast.place_ref, bf16[8192,1024]{1,0:T(8,128)(2,1)} %w_ref.27, bf16[256,1024]{1,0:T(8,128)(2,1)} %g_ref.1), custom_call_target="tpu_custom_call" | custom-call | bytes 1024 | tf_op jit(solution)/shard_map/pallas_call | solution.py:194
  3.1 3.0 %collective-permute-start = (bf16[1040,128]{1,0:T(8,128)(2,1)S(1)}, bf16[1040,128]{1,0:T(8,128)(2,1)S(1)}, u32[]{:S(2)}, u32[]{:S(2)}) collective-permute-start(bf16[1040,128]{1,0:T(8,128)(2,1)S(1)} %get-tuple-element.35), channel_id=1, source_target_pairs={{0,1},{1,0},{2,3},{3,2},{4,5},{5,4},{6,7},{7,6},{8,9},{9,8},{10,11... | collective-permute-start | bytes 798728 | tf_op jit(solution)/shard_map/ppermute | solution.py:606
  6.1 2.2 %shard_map.78 = bf16[1040,128]{1,0:T(8,128)(2,1)S(1)} custom-call(s32[1]{0:T(128)} %bitcast.place_ref, bf16[8192,1024]{1,0:T(8,128)(2,1)} %w_ref.27, bf16[1024,256]{1,0:T(8,128)(2,1)S(1)} %get-tuple-element.37.g_ref.turned_ref), custom_call_target="tpu_custom_call" | custom-call | bytes 1024 | tf_op jit(solution)/shard_map/pallas_call | solution.py:194
  8.3 1.6 %collective-permute-start.1 = (bf16[1040,128]{1,0:T(8,128)(2,1)S(1)}, bf16[1040,128]{1,0:T(8,128)(2,1)S(1)}, u32[]{:S(2)}, u32[]{:S(2)}) collective-permute-start(bf16[1040,128]{1,0:T(8,128)(2,1)S(1)} %shard_map.78), channel_id=1, source_target_pairs={{0,2},{1,3},{2,0},{3,1},{4,6},{5,7},{6,4},{7,5},{8,10},{9,11},{10,... | collective-permute-start | bytes 798728 | tf_op jit(solution)/shard_map/ppermute | solution.py:606
  9.9 0.0 slice-done
  9.9 0.0 slice-done.1
  9.9 0.0 slice-done.2
  9.9 0.0 slice-done.3
  10.0 0.6 %shard_map.79 = bf16[1040,128]{1,0:T(8,128)(2,1)S(1)} custom-call(s32[1]{0:T(128)} %bitcast.place_ref, bf16[8192,1024]{1,0:T(8,128)(2,1)S(1)} %bitcast.11, bf16[1024,256]{1,0:T(8,128)(2,1)S(1)} %get-tuple-element.37.g_ref.turned_ref), custom_call_target="tpu_custom_call" | custom-call | bytes 1024 | tf_op jit(solution)/shard_map/pallas_call | solution.py:131
  10.6 0.6 collective-permute-start.2
  11.1 0.6 %shard_map.80 = bf16[1040,128]{1,0:T(8,128)(2,1)S(1)} custom-call(s32[1]{0:T(128)} %bitcast.place_ref, bf16[8192,1024]{1,0:T(8,128)(2,1)S(1)} %bitcast.11, bf16[1024,256]{1,0:T(8,128)(2,1)S(1)} %get-tuple-element.37.g_ref.turned_ref), custom_call_target="tpu_custom_call" | custom-call | bytes 1024 | tf_op jit(solution)/shard_map/pallas_call | solution.py:131
  11.8 0.4 shard_map.81.acc_ref
  12.2 0.6 %shard_map.82 = bf16[1040,128]{1,0:T(8,128)(2,1)S(1)} custom-call(s32[1]{0:T(128)} %bitcast.place_ref, bf16[8192,1024]{1,0:T(8,128)(2,1)S(1)} %bitcast.11, bf16[1024,256]{1,0:T(8,128)(2,1)S(1)} %get-tuple-element.37.g_ref.turned_ref), custom_call_target="tpu_custom_call" | custom-call | bytes 1024 | tf_op jit(solution)/shard_map/pallas_call | solution.py:131
  12.8 0.0 collective-permute-done.refs_0_
  12.8 0.7 %shard_map.83 = bf16[1040,128]{1,0:T(8,128)(2,1)S(1)} custom-call(s32[1]{0:T(128)} %bitcast.place_ref, bf16[8192,1024]{1,0:T(8,128)(2,1)S(1)} %bitcast.11, bf16[1024,256]{1,0:T(8,128)(2,1)S(1)} %get-tuple-element.37.g_ref.turned_ref, bf16[1040,128]{1,0:T(8,128)(2,1)S(1)} %collective-permute-done.refs_0_), custom_call_target="tpu_custom_call" | custom-call | bytes 1024 | tf_op jit(solution)/shard_map/pallas_call | solution.py:131
  13.5 1.7 %collective-permute-start.3 = (bf16[1040,128]{1,0:T(8,128)(2,1)S(1)}, bf16[1040,128]{1,0:T(8,128)(2,1)S(1)}, u32[]{:S(2)}, u32[]{:S(2)}) collective-permute-start(bf16[1040,128]{1,0:T(8,128)(2,1)S(1)} %shard_map.83), channel_id=1, source_target_pairs={{0,2},{1,3},{2,0},{3,1},{4,6},{5,7},{6,4},{7,5},{8,10},{9,11},{10,... | collective-permute-start | bytes 798728 | tf_op jit(solution)/shard_map/ppermute | solution.py:606
  15.2 1.4 %collective-permute-done.1.refs_0_ = bf16[1040,128]{1,0:T(8,128)(2,1)S(1)} collective-permute-done((bf16[1040,128]{1,0:T(8,128)(2,1)S(1)}, bf16[1040,128]{1,0:T(8,128)(2,1)S(1)}, u32[]{:S(2)}, u32[]{:S(2)}) %collective-permute-start.1) | collective-permute-done | bytes 266272 | tf_op jit(solution)/shard_map/ppermute | solution.py:606
  16.6 0.7 %shard_map.84 = bf16[1040,128]{1,0:T(8,128)(2,1)S(1)} custom-call(s32[1]{0:T(128)} %bitcast.place_ref, bf16[8192,1024]{1,0:T(8,128)(2,1)S(1)} %bitcast.11, bf16[1024,256]{1,0:T(8,128)(2,1)S(1)} %get-tuple-element.37.g_ref.turned_ref, bf16[1040,128]{1,0:T(8,128)(2,1)S(1)} %collective-permute-done.1.refs_0_), custom_call_target="tpu_custom_call" | custom-call | bytes 1024 | tf_op jit(solution)/shard_map/pallas_call | solution.py:131
  17.3 0.5 collective-permute-start.4
  17.8 1.6 %collective-permute-start.5 = (bf16[1040,128]{1,0:T(8,128)(2,1)S(1)}, bf16[1040,128]{1,0:T(8,128)(2,1)S(1)}, u32[]{:S(2)}, u32[]{:S(2)}) collective-permute-start(bf16[1040,128]{1,0:T(8,128)(2,1)S(1)} %shard_map.80), channel_id=1, source_target_pairs={{0,1},{1,0},{2,3},{3,2},{4,5},{5,4},{6,7},{7,6},{8,9},{9,8},{10,11... | collective-permute-start | bytes 798728 | tf_op jit(solution)/shard_map/ppermute | solution.py:606
  19.4 0.0 collective-permute-done.2.refs_0_
  19.4 0.7 %shard_map.85 = bf16[1040,128]{1,0:T(8,128)(2,1)S(1)} custom-call(s32[1]{0:T(128)} %bitcast.place_ref, bf16[8192,1024]{1,0:T(8,128)(2,1)S(1)} %bitcast.11, bf16[1024,256]{1,0:T(8,128)(2,1)S(1)} %get-tuple-element.37.g_ref.turned_ref, bf16[1040,128]{1,0:T(8,128)(2,1)S(1)} %collective-permute-done.2.refs_0_), custom_call_target="tpu_custom_call" | custom-call | bytes 1024 | tf_op jit(solution)/shard_map/pallas_call | solution.py:131
  20.1 1.6 %collective-permute-start.6 = (bf16[1040,128]{1,0:T(8,128)(2,1)S(1)}, bf16[1040,128]{1,0:T(8,128)(2,1)S(1)}, u32[]{:S(2)}, u32[]{:S(2)}) collective-permute-start(bf16[1040,128]{1,0:T(8,128)(2,1)S(1)} %shard_map.85), channel_id=1, source_target_pairs={{0,2},{1,3},{2,0},{3,1},{4,6},{5,7},{6,4},{7,5},{8,10},{9,11},{10,... | collective-permute-start | bytes 798728 | tf_op jit(solution)/shard_map/ppermute | solution.py:606
  21.7 1.1 %collective-permute-start.7 = (bf16[1040,128]{1,0:T(8,128)(2,1)S(1)}, bf16[1040,128]{1,0:T(8,128)(2,1)S(1)}, u32[]{:S(2)}, u32[]{:S(2)}) collective-permute-start(bf16[1040,128]{1,0:T(8,128)(2,1)S(1)} %shard_map.82), channel_id=1, source_target_pairs={{0,1},{1,0},{2,3},{3,2},{4,5},{5,4},{6,7},{7,6},{8,9},{9,8},{10,11... | collective-permute-start | bytes 798728 | tf_op jit(solution)/shard_map/ppermute | solution.py:606
  22.9 0.0 collective-permute-done.3.refs_1_
  22.9 0.7 %shard_map.86 = bf16[1040,128]{1,0:T(8,128)(2,1)S(1)} custom-call(s32[1]{0:T(128)} %bitcast.place_ref, bf16[8192,1024]{1,0:T(8,128)(2,1)S(1)} %bitcast.11, bf16[1024,256]{1,0:T(8,128)(2,1)S(1)} %get-tuple-element.37.g_ref.turned_ref, bf16[1040,128]{1,0:T(8,128)(2,1)S(1)} %collective-permute-done.refs_0_), custom_call_target="tpu_custom_call" | custom-call | bytes 1024 | tf_op jit(solution)/shard_map/pallas_call | solution.py:131
  23.6 3.1 %collective-permute-done.4.refs_0_ = bf16[1040,128]{1,0:T(8,128)(2,1)S(1)} collective-permute-done((bf16[1040,128]{1,0:T(8,128)(2,1)S(1)}, bf16[1040,128]{1,0:T(8,128)(2,1)S(1)}, u32[]{:S(2)}, u32[]{:S(2)}) %collective-permute-start.4) | collective-permute-done | bytes 266272 | tf_op jit(solution)/shard_map/ppermute | solution.py:606
  26.7 0.9 %shard_map.87 = bf16[1040,128]{1,0:T(8,128)(2,1)S(1)} custom-call(s32[1]{0:T(128)} %bitcast.place_ref, bf16[8192,1024]{1,0:T(8,128)(2,1)S(1)} %bitcast.11, bf16[1024,256]{1,0:T(8,128)(2,1)S(1)} %get-tuple-element.37.g_ref.turned_ref, bf16[1040,128]{1,0:T(8,128)(2,1)S(1)} %collective-permute-done.4.refs_0_, bf16[1040,128]{1,0:T(8,128)(2,1)S(1)} %collective-permute-done.3.refs_1_), custom_call_target="tpu_custom_call" | custom-call | bytes 1024 | tf_op jit(solution)/shard_map/pallas_call | solution.py:131
  27.6 2.6 %collective-permute-start.8 = (bf16[1040,128]{1,0:T(8,128)(2,1)S(1)}, bf16[1040,128]{1,0:T(8,128)(2,1)S(1)}, u32[]{:S(2)}, u32[]{:S(2)}) collective-permute-start(bf16[1040,128]{1,0:T(8,128)(2,1)S(1)} %shard_map.87), channel_id=1, source_target_pairs={{0,4},{1,5},{2,6},{3,7},{4,0},{5,1},{6,2},{7,3},{8,12},{9,13},{10,... | collective-permute-start | bytes 798728 | tf_op jit(solution)/shard_map/ppermute | solution.py:606
  30.2 1.6 %collective-permute-start.9 = (bf16[1040,128]{1,0:T(8,128)(2,1)S(1)}, bf16[1040,128]{1,0:T(8,128)(2,1)S(1)}, u32[]{:S(2)}, u32[]{:S(2)}) collective-permute-start(bf16[1040,128]{1,0:T(8,128)(2,1)S(1)} %shard_map.86), channel_id=1, source_target_pairs={{0,2},{1,3},{2,0},{3,1},{4,6},{5,7},{6,4},{7,5},{8,10},{9,11},{10,... | collective-permute-start | bytes 798728 | tf_op jit(solution)/shard_map/ppermute | solution.py:606
  31.8 0.6 collective-permute-done.5.refs_0_
  32.4 0.0 collective-permute-done.6.refs_1_
  32.4 0.9 %shard_map.88 = bf16[1040,128]{1,0:T(8,128)(2,1)S(1)} custom-call(s32[1]{0:T(128)} %bitcast.place_ref, bf16[8192,1024]{1,0:T(8,128)(2,1)S(1)} %bitcast.11, bf16[1024,256]{1,0:T(8,128)(2,1)S(1)} %get-tuple-element.37.g_ref.turned_ref, bf16[1040,128]{1,0:T(8,128)(2,1)S(1)} %collective-permute-done.5.refs_0_, bf16[1040,128]{1,0:T(8,128)(2,1)S(1)} %collective-permute-done.6.refs_1_), custom_call_target="tpu_custom_call" | custom-call | bytes 1024 | tf_op jit(solution)/shard_map/pallas_call | solution.py:131
  33.3 0.7 %shard_map.89 = bf16[1040,128]{1,0:T(8,128)(2,1)S(1)} custom-call(s32[1]{0:T(128)} %bitcast.place_ref, bf16[8192,1024]{1,0:T(8,128)(2,1)S(1)} %bitcast.11, bf16[1024,256]{1,0:T(8,128)(2,1)S(1)} %get-tuple-element.37.g_ref.turned_ref, bf16[1040,128]{1,0:T(8,128)(2,1)S(1)} %collective-permute-done.1.refs_0_), custom_call_target="tpu_custom_call" | custom-call | bytes 1024 | tf_op jit(solution)/shard_map/pallas_call | solution.py:131
  34.0 0.0 copy-start.2
  34.0 0.0 copy-start.3
  34.0 0.5 collective-permute-start.10
  34.5 2.6 %collective-permute-start.11 = (bf16[1040,128]{1,0:T(8,128)(2,1)S(1)}, bf16[1040,128]{1,0:T(8,128)(2,1)S(1)}, u32[]{:S(2)}, u32[]{:S(2)}) collective-permute-start(bf16[1040,128]{1,0:T(8,128)(2,1)S(1)} %shard_map.88), channel_id=1, source_target_pairs={{0,4},{1,5},{2,6},{3,7},{4,0},{5,1},{6,2},{7,3},{8,12},{9,13},{10,... | collective-permute-start | bytes 798728 | tf_op jit(solution)/shard_map/ppermute | solution.py:606
  37.1 1.0 %collective-permute-done.7.refs_0_ = bf16[1040,128]{1,0:T(8,128)(2,1)S(1)} collective-permute-done((bf16[1040,128]{1,0:T(8,128)(2,1)S(1)}, bf16[1040,128]{1,0:T(8,128)(2,1)S(1)}, u32[]{:S(2)}, u32[]{:S(2)}) %collective-permute-start.7) | collective-permute-done | bytes 266272 | tf_op jit(solution)/shard_map/ppermute | solution.py:606
  38.1 0.7 %shard_map.90 = bf16[1040,128]{1,0:T(8,128)(2,1)S(1)} custom-call(s32[1]{0:T(128)} %bitcast.place_ref, bf16[8192,1024]{1,0:T(8,128)(2,1)S(1)} %bitcast.11, bf16[1024,256]{1,0:T(8,128)(2,1)S(1)} %get-tuple-element.37.g_ref.turned_ref, bf16[1040,128]{1,0:T(8,128)(2,1)S(1)} %collective-permute-done.7.refs_0_), custom_call_target="tpu_custom_call" | custom-call | bytes 1024 | tf_op jit(solution)/shard_map/pallas_call | solution.py:131
  38.8 0.0 copy-start
  38.8 0.0 copy-start.1
  38.9 1.6 %collective-permute-start.12 = (bf16[1040,128]{1,0:T(8,128)(2,1)S(1)}, bf16[1040,128]{1,0:T(8,128)(2,1)S(1)}, u32[]{:S(2)}, u32[]{:S(2)}) collective-permute-start(bf16[1040,128]{1,0:T(8,128)(2,1)S(1)} %shard_map.90), channel_id=1, source_target_pairs={{0,2},{1,3},{2,0},{3,1},{4,6},{5,7},{6,4},{7,5},{8,10},{9,11},{10,... | collective-permute-start | bytes 798728 | tf_op jit(solution)/shard_map/ppermute | solution.py:606
  40.5 0.6 %shard_map.91 = bf16[1040,128]{1,0:T(8,128)(2,1)S(1)} custom-call(s32[1]{0:T(128)} %bitcast.place_ref, bf16[8192,1024]{1,0:T(8,128)(2,1)S(1)} %bitcast.11, bf16[1024,256]{1,0:T(8,128)(2,1)S(1)} %get-tuple-element.37.g_ref.turned_ref), custom_call_target="tpu_custom_call" | custom-call | bytes 1024 | tf_op jit(solution)/shard_map/pallas_call | solution.py:131
  41.1 0.3 collective-permute-done.8.refs_2_
  41.4 3.8 %collective-permute-start.13 = (bf16[1040,128]{1,0:T(8,128)(2,1)S(1)}, bf16[1040,128]{1,0:T(8,128)(2,1)S(1)}, u32[]{:S(2)}, u32[]{:S(2)}) collective-permute-start(bf16[1040,128]{1,0:T(8,128)(2,1)S(1)} %shard_map.91), channel_id=1, source_target_pairs={{0,1},{1,0},{2,3},{3,2},{4,5},{5,4},{6,7},{7,6},{8,9},{9,8},{10,11... | collective-permute-start | bytes 798728 | tf_op jit(solution)/shard_map/ppermute | solution.py:606
  45.3 0.4 shard_map.92.acc_ref
  45.8 0.0 collective-permute-done.9.refs_1_
  45.8 0.0 collective-permute-done.10.refs_0_
  45.9 1.9 %shard_map.94 = (bf16[256,1024]{1,0:T(8,128)(2,1)}, f32[1224,128]{1,0:T(8,128)S(1)}, f32[16,8,128]{2,1,0:T(8,128)S(1)}, f32[8,8,128]{2,1,0:T(8,128)S(1)}) custom-call(f32[512,256]{1,0:T(8,128)S(1)} %shard_map.92.acc_ref, bf16[1040,128]{1,0:T(8,128)(2,1)S(1)} %collective-permute-done.10.refs_0_, bf16[1040,128]{1,0:T(8,128)(2,1)S(1)} %collective-permute-done.9.refs_1_, ...), custom_call_target="tpu_custom_call" | custom-call | bytes 1024 | tf_op jit(solution)/shard_map/pallas_call | solution.py:326
  47.8 1.1 %collective-permute-done.11.refs_0_ = bf16[1040,128]{1,0:T(8,128)(2,1)S(1)} collective-permute-done((bf16[1040,128]{1,0:T(8,128)(2,1)S(1)}, bf16[1040,128]{1,0:T(8,128)(2,1)S(1)}, u32[]{:S(2)}, u32[]{:S(2)}) %collective-permute-start.11) | collective-permute-done | bytes 266272 | tf_op jit(solution)/shard_map/ppermute | solution.py:606
  49.0 0.2 shard_map.95.acc_ref
  49.1 1.3 %collective-permute-done.12.refs_1_ = bf16[1040,128]{1,0:T(8,128)(2,1)S(1)} collective-permute-done((bf16[1040,128]{1,0:T(8,128)(2,1)S(1)}, bf16[1040,128]{1,0:T(8,128)(2,1)S(1)}, u32[]{:S(2)}, u32[]{:S(2)}) %collective-permute-start.12) | collective-permute-done | bytes 266272 | tf_op jit(solution)/shard_map/ppermute | solution.py:606
  50.4 0.0 collective-permute-done.13.refs_0_
  50.4 1.2 %shard_map.96 = (bf16[256,1024]{1,0:T(8,128)(2,1)}, f32[1224,128]{1,0:T(8,128)S(1)}, f32[16,8,128]{2,1,0:T(8,128)S(1)}, f32[16,8,128]{2,1,0:T(8,128)S(1)}) custom-call(f32[512,256]{1,0:T(8,128)S(1)} %shard_map.95.acc_ref, bf16[1040,128]{1,0:T(8,128)(2,1)S(1)} %collective-permute-done.13.refs_0_, ...), custom_call_target="tpu_custom_call", output_to_operand_aliasing={{0}: (8, {})} | custom-call | bytes 1024 | tf_op jit(solution)/shard_map/pallas_call | solution.py:326
  51.6 0.1 collective-permute-start.14
  51.7 1.2 %collective-permute-done.14.arrived_ref.refs_3_ = f32[16,8,128]{2,1,0:T(8,128)S(1)} collective-permute-done((f32[16,8,128]{2,1,0:T(8,128)S(1)}, f32[16,8,128]{2,1,0:T(8,128)S(1)}, u32[]{:S(2)}, u32[]{:S(2)}) %collective-permute-start.14) | collective-permute-done | bytes 65568 | tf_op jit(solution)/shard_map/ppermute | solution.py:650
  53.0 0.1 shard_map.97
  53.0 1.6 %collective-permute-start.15 = (bf16[144,128]{1,0:T(8,128)(2,1)S(1)}, bf16[144,128]{1,0:T(8,128)(2,1)S(1)}, u32[]{:S(2)}, u32[]{:S(2)}) collective-permute-start(bf16[144,128]{1,0:T(8,128)(2,1)S(1)} %shard_map.97), channel_id=1, source_target_pairs={{0,16},{8,24},{16,0},{24,8},{1,17},{9,25},{17,1},{25,9},{2,18},{10... | collective-permute-start | bytes 110600 | tf_op jit(solution)/shard_map/ppermute | solution.py:650
  54.6 1.2 %shard_map.98.refs_1_ = f32[1224,128]{1,0:T(8,128)S(1)} custom-call(f32[1224,128]{1,0:T(8,128)S(1)} %get-tuple-element.65.gc_ref, f32[16,8,128]{2,1,0:T(8,128)S(1)} %get-tuple-element.66.state_ref, f32[16,16,128]{2,1,0:T(8,128)S(1)} %bitcast.15, f32[16,16,128]{2,1,0:T(8,128)S(1)} %get-tuple-element.55.refs_6_.refs_5_.lap_ref, f32[16,16,128]{2,1,0:T(8,128)S(1)} %bitcast.18), custom_call_target="tpu_custom_call" | custom-call | bytes 1024 | tf_op jit(solution)/shard_map/pallas_call | solution.py:376
  55.8 1.2 %collective-permute-done.15.refs_4_ = bf16[144,128]{1,0:T(8,128)(2,1)S(1)} collective-permute-done((bf16[144,128]{1,0:T(8,128)(2,1)S(1)}, bf16[144,128]{1,0:T(8,128)(2,1)S(1)}, u32[]{:S(2)}, u32[]{:S(2)}) %collective-permute-start.15) | collective-permute-done | bytes 36896 | tf_op jit(solution)/shard_map/ppermute | solution.py:650
  57.0 2.2 %shard_map.99 = bf16[256,1024]{1,0:T(8,128)(2,1)} custom-call(s32[1]{0:T(128)} %bitcast.5.group_ref, f32[1224,128]{1,0:T(8,128)S(1)} %get-tuple-element.61.refs_0_, f32[1224,128]{1,0:T(8,128)S(1)} %shard_map.98.refs_1_, f32[16,8,128]{2,1,0:T(8,128)S(1)} %get-tuple-element.67.refs_2_, f32[16,8,128]{2,1,0:T(8,128)S(1)} %collective-permute-done.14.arrived_ref.refs_3_, ...), custom_call_target="tpu_custom_call" | custom-call | bytes 1024 | tf_op jit(solution)/shard_map/pallas_call | solution.py:521
  (12 shorter events, 0.2 us)
Async XLA Ops:
  0.6 9.3 %slice-start = ((s8[16777216]{0:T(1024)(128)(4,1)}), s8[4194304]{0:T(1024)(128)(4,1)S(1)}, s32[]{:S(2)}) async-start(s8[16777216]{0:T(1024)(128)(4,1)} %bitcast.10), calls=%async_computation | async-start | bytes 8388608
  0.6 9.3 %slice-start.1 = ((s8[16777216]{0:T(1024)(128)(4,1)}), s8[4194304]{0:T(1024)(128)(4,1)S(1)}, s32[]{:S(2)}) async-start(s8[16777216]{0:T(1024)(128)(4,1)} %bitcast.10), calls=%async_computation.1 | async-start | bytes 8388608
  3.1 9.8 %collective-permute-start = (bf16[1040,128]{1,0:T(8,128)(2,1)S(1)}, bf16[1040,128]{1,0:T(8,128)(2,1)S(1)}, u32[]{:S(2)}, u32[]{:S(2)}) collective-permute-start(bf16[1040,128]{1,0:T(8,128)(2,1)S(1)} %get-tuple-element.35), channel_id=1, source_target_pairs={{0,1},{1,0},{2,3},{3,2},{4,5},{5,4},{6,7},{7,6},{8,9},{9,8},{10,11... | collective-permute-start | bytes 798728 | tf_op jit(solution)/shard_map/ppermute | solution.py:606
  6.1 3.9 %slice-start.2 = ((s8[16777216]{0:T(1024)(128)(4,1)}), s8[4194304]{0:T(1024)(128)(4,1)S(1)}, s32[]{:S(2)}) async-start(s8[16777216]{0:T(1024)(128)(4,1)} %bitcast.10), calls=%async_computation.2 | async-start | bytes 8388608
  6.1 3.9 %slice-start.3 = ((s8[16777216]{0:T(1024)(128)(4,1)}), s8[4194304]{0:T(1024)(128)(4,1)S(1)}, s32[]{:S(2)}) async-start(s8[16777216]{0:T(1024)(128)(4,1)} %bitcast.10), calls=%async_computation.3 | async-start | bytes 8388608
  8.3 8.3 %collective-permute-start.1 = (bf16[1040,128]{1,0:T(8,128)(2,1)S(1)}, bf16[1040,128]{1,0:T(8,128)(2,1)S(1)}, u32[]{:S(2)}, u32[]{:S(2)}) collective-permute-start(bf16[1040,128]{1,0:T(8,128)(2,1)S(1)} %shard_map.78), channel_id=1, source_target_pairs={{0,2},{1,3},{2,0},{3,1},{4,6},{5,7},{6,4},{7,5},{8,10},{9,11},{10,... | collective-permute-start | bytes 798728 | tf_op jit(solution)/shard_map/ppermute | solution.py:606
  10.6 8.8 %collective-permute-start.2 = (bf16[1040,128]{1,0:T(8,128)(2,1)S(1)}, bf16[1040,128]{1,0:T(8,128)(2,1)S(1)}, u32[]{:S(2)}, u32[]{:S(2)}) collective-permute-start(bf16[1040,128]{1,0:T(8,128)(2,1)S(1)} %shard_map.79), channel_id=1, source_target_pairs={{0,1},{1,0},{2,3},{3,2},{4,5},{5,4},{6,7},{7,6},{8,9},{9,8},{10,11... | collective-permute-start | bytes 798728 | tf_op jit(solution)/shard_map/ppermute | solution.py:606
  13.5 9.4 %collective-permute-start.3 = (bf16[1040,128]{1,0:T(8,128)(2,1)S(1)}, bf16[1040,128]{1,0:T(8,128)(2,1)S(1)}, u32[]{:S(2)}, u32[]{:S(2)}) collective-permute-start(bf16[1040,128]{1,0:T(8,128)(2,1)S(1)} %shard_map.83), channel_id=1, source_target_pairs={{0,2},{1,3},{2,0},{3,1},{4,6},{5,7},{6,4},{7,5},{8,10},{9,11},{10,... | collective-permute-start | bytes 798728 | tf_op jit(solution)/shard_map/ppermute | solution.py:606
  17.3 9.4 %collective-permute-start.4 = (bf16[1040,128]{1,0:T(8,128)(2,1)S(1)}, bf16[1040,128]{1,0:T(8,128)(2,1)S(1)}, u32[]{:S(2)}, u32[]{:S(2)}) collective-permute-start(bf16[1040,128]{1,0:T(8,128)(2,1)S(1)} %shard_map.84), channel_id=1, source_target_pairs={{0,1},{1,0},{2,3},{3,2},{4,5},{5,4},{6,7},{7,6},{8,9},{9,8},{10,11... | collective-permute-start | bytes 798728 | tf_op jit(solution)/shard_map/ppermute | solution.py:606
  17.8 14.6 %collective-permute-start.5 = (bf16[1040,128]{1,0:T(8,128)(2,1)S(1)}, bf16[1040,128]{1,0:T(8,128)(2,1)S(1)}, u32[]{:S(2)}, u32[]{:S(2)}) collective-permute-start(bf16[1040,128]{1,0:T(8,128)(2,1)S(1)} %shard_map.80), channel_id=1, source_target_pairs={{0,1},{1,0},{2,3},{3,2},{4,5},{5,4},{6,7},{7,6},{8,9},{9,8},{10,11... | collective-permute-start | bytes 798728 | tf_op jit(solution)/shard_map/ppermute | solution.py:606
  20.1 12.3 %collective-permute-start.6 = (bf16[1040,128]{1,0:T(8,128)(2,1)S(1)}, bf16[1040,128]{1,0:T(8,128)(2,1)S(1)}, u32[]{:S(2)}, u32[]{:S(2)}) collective-permute-start(bf16[1040,128]{1,0:T(8,128)(2,1)S(1)} %shard_map.85), channel_id=1, source_target_pairs={{0,2},{1,3},{2,0},{3,1},{4,6},{5,7},{6,4},{7,5},{8,10},{9,11},{10,... | collective-permute-start | bytes 798728 | tf_op jit(solution)/shard_map/ppermute | solution.py:606
  21.7 16.4 %collective-permute-start.7 = (bf16[1040,128]{1,0:T(8,128)(2,1)S(1)}, bf16[1040,128]{1,0:T(8,128)(2,1)S(1)}, u32[]{:S(2)}, u32[]{:S(2)}) collective-permute-start(bf16[1040,128]{1,0:T(8,128)(2,1)S(1)} %shard_map.82), channel_id=1, source_target_pairs={{0,1},{1,0},{2,3},{3,2},{4,5},{5,4},{6,7},{7,6},{8,9},{9,8},{10,11... | collective-permute-start | bytes 798728 | tf_op jit(solution)/shard_map/ppermute | solution.py:606
  27.6 13.8 %collective-permute-start.8 = (bf16[1040,128]{1,0:T(8,128)(2,1)S(1)}, bf16[1040,128]{1,0:T(8,128)(2,1)S(1)}, u32[]{:S(2)}, u32[]{:S(2)}) collective-permute-start(bf16[1040,128]{1,0:T(8,128)(2,1)S(1)} %shard_map.87), channel_id=1, source_target_pairs={{0,4},{1,5},{2,6},{3,7},{4,0},{5,1},{6,2},{7,3},{8,12},{9,13},{10,... | collective-permute-start | bytes 798728 | tf_op jit(solution)/shard_map/ppermute | solution.py:606
  30.2 15.6 %collective-permute-start.9 = (bf16[1040,128]{1,0:T(8,128)(2,1)S(1)}, bf16[1040,128]{1,0:T(8,128)(2,1)S(1)}, u32[]{:S(2)}, u32[]{:S(2)}) collective-permute-start(bf16[1040,128]{1,0:T(8,128)(2,1)S(1)} %shard_map.86), channel_id=1, source_target_pairs={{0,2},{1,3},{2,0},{3,1},{4,6},{5,7},{6,4},{7,5},{8,10},{9,11},{10,... | collective-permute-start | bytes 798728 | tf_op jit(solution)/shard_map/ppermute | solution.py:606
  34.0 11.3 %copy-start.2 = (f32[1024,16]{0,1:T(8,128)S(1)}, f32[1024,16]{0,1:T(8,128)}, u32[]{:S(2)}) copy-start(f32[1024,16]{0,1:T(8,128)} %param.10) | copy-start | bytes 196612
  34.0 11.3 %copy-start.3 = (f32[1024,16]{0,1:T(8,128)S(1)}, f32[1024,16]{0,1:T(8,128)}, u32[]{:S(2)}) copy-start(f32[1024,16]{0,1:T(8,128)} %param.11) | copy-start | bytes 196612
  34.0 11.9 %collective-permute-start.10 = (bf16[1040,128]{1,0:T(8,128)(2,1)S(1)}, bf16[1040,128]{1,0:T(8,128)(2,1)S(1)}, u32[]{:S(2)}, u32[]{:S(2)}) collective-permute-start(bf16[1040,128]{1,0:T(8,128)(2,1)S(1)} %shard_map.89), channel_id=1, source_target_pairs={{0,1},{1,0},{2,3},{3,2},{4,5},{5,4},{6,7},{7,6},{8,9},{9,8},{10,11... | collective-permute-start | bytes 798728 | tf_op jit(solution)/shard_map/ppermute | solution.py:606
  34.5 14.4 %collective-permute-start.11 = (bf16[1040,128]{1,0:T(8,128)(2,1)S(1)}, bf16[1040,128]{1,0:T(8,128)(2,1)S(1)}, u32[]{:S(2)}, u32[]{:S(2)}) collective-permute-start(bf16[1040,128]{1,0:T(8,128)(2,1)S(1)} %shard_map.88), channel_id=1, source_target_pairs={{0,4},{1,5},{2,6},{3,7},{4,0},{5,1},{6,2},{7,3},{8,12},{9,13},{10,... | collective-permute-start | bytes 798728 | tf_op jit(solution)/shard_map/ppermute | solution.py:606
  38.8 7.1 %copy-start = (bf16[256,1024]{1,0:T(8,128)(2,1)S(1)}, bf16[256,1024]{1,0:T(8,128)(2,1)}, u32[]{:S(2)}) copy-start(bf16[256,1024]{1,0:T(8,128)(2,1)} %refs_2_.1) | copy-start | bytes 1572868
  38.8 7.1 %copy-start.1 = (bf16[256,1024]{1,0:T(8,128)(2,1)S(1)}, bf16[256,1024]{1,0:T(8,128)(2,1)}, u32[]{:S(2)}) copy-start(bf16[256,1024]{1,0:T(8,128)(2,1)} %refs_3_.3) | copy-start | bytes 1572868
  38.9 11.6 %collective-permute-start.12 = (bf16[1040,128]{1,0:T(8,128)(2,1)S(1)}, bf16[1040,128]{1,0:T(8,128)(2,1)S(1)}, u32[]{:S(2)}, u32[]{:S(2)}) collective-permute-start(bf16[1040,128]{1,0:T(8,128)(2,1)S(1)} %shard_map.90), channel_id=1, source_target_pairs={{0,2},{1,3},{2,0},{3,1},{4,6},{5,7},{6,4},{7,5},{8,10},{9,11},{10,... | collective-permute-start | bytes 798728 | tf_op jit(solution)/shard_map/ppermute | solution.py:606
  41.4 9.0 %collective-permute-start.13 = (bf16[1040,128]{1,0:T(8,128)(2,1)S(1)}, bf16[1040,128]{1,0:T(8,128)(2,1)S(1)}, u32[]{:S(2)}, u32[]{:S(2)}) collective-permute-start(bf16[1040,128]{1,0:T(8,128)(2,1)S(1)} %shard_map.91), channel_id=1, source_target_pairs={{0,1},{1,0},{2,3},{3,2},{4,5},{5,4},{6,7},{7,6},{8,9},{9,8},{10,11... | collective-permute-start | bytes 798728 | tf_op jit(solution)/shard_map/ppermute | solution.py:606
  51.6 1.3 %collective-permute-start.14 = (f32[16,8,128]{2,1,0:T(8,128)S(1)}, f32[16,8,128]{2,1,0:T(8,128)S(1)}, u32[]{:S(2)}, u32[]{:S(2)}) collective-permute-start(f32[16,8,128]{2,1,0:T(8,128)S(1)} %get-tuple-element.63.state_ref), channel_id=1, source_target_pairs={{0,8},{8,0},{16,24},{24,16},{1,9},{9,1},{17,25},{25,17},{2,10},{10... | collective-permute-start | bytes 196616 | tf_op jit(solution)/shard_map/ppermute | solution.py:650
  53.0 4.0 %collective-permute-start.15 = (bf16[144,128]{1,0:T(8,128)(2,1)S(1)}, bf16[144,128]{1,0:T(8,128)(2,1)S(1)}, u32[]{:S(2)}, u32[]{:S(2)}) collective-permute-start(bf16[144,128]{1,0:T(8,128)(2,1)S(1)} %shard_map.97), channel_id=1, source_target_pairs={{0,16},{8,24},{16,0},{24,8},{1,17},{9,25},{17,1},{25,9},{2,18},{10... | collective-permute-start | bytes 110600 | tf_op jit(solution)/shard_map/ppermute | solution.py:650
